TPU v7x, 32 devices: a whole 2x2x4 slice. The times are simulated.
32 devices in a mesh: rep: 2 (over x), grp: 2 (over core), tp: 8 (over z, y).
Axes of the slice: x: 2, y: 2, z: 4, core: 2. Of those that a mesh axis runs over, the one named last changes fastest.
Arguments:
- tokens: bfloat16 [4, 128, 8192], P(('rep', 'grp'), 'tp'), parts along dimension 0, may hold values from -6 to 6
- base_projection_weight: bfloat16 [8192, 10240], P(None, 'tp'), may hold values from -0.0625 to 0.0625
- adapter_down_panels: bfloat16 [16, 8192, 64], P(('grp', 'tp')), may hold values from -0.0625 to 0.0625
- adapter_up_panels: bfloat16 [16, 64, 10240], P(('grp', 'tp')), may hold values from -0.75 to 0.75
- request_adapter_ids: int32 [4, 12], P('rep'), parts along dimension 0, may hold values from 0 to 15, all different within a row
- request_token_lengths: int32 [4, 12], P(('rep', 'grp')), parts along dimension 0, may hold values from 1 to 16, 128 in all within a row
- adapter_store_slot: int32 [16], replicated, may hold values from 0 to 15, each once
Outputs:
- projected: bfloat16 [4, 128, 10240], P(('rep', 'grp'), None, 'tp'), parts along dimension 0
There are 2 independent parts, one for each index of `rep`. A program takes and returns all parts, laid end to end along the dimension named above; an argument that names none is the same for every part. Nothing has to cross between parts.
Inputs may be any that keep to these rules, and one draw needn't show every extreme that they name: `request_adapter_ids`: each group names 12 different adapters, and every adapter is named by some group. `request_token_lengths`: each group's requests cover its 128 tokens, the longest exactly 16. `adapter_store_slot`: each slot holds one adapter.
All inputs are finite; a program needn't handle non-finite values.
Results may differ from a plain program's by a relative error of at most 0.0039.
Values may be sent and summed in bfloat16 or wider, within the bound.
No kernel may reach another device: no remote copies, remote signals or barrier semaphores. Data moves between devices by JAX's collectives and lax.ppermute only.
A program may use at most 64 MiB of HBM per device.

v0:
```python
import jax
import jax.numpy as jnp
from jax import lax
from jax.sharding import PartitionSpec as P

adapter_scale = 1.0


def on_device(
    tokens,
    base_projection_weight,
    adapter_down_panels,
    adapter_up_panels,
    request_adapter_ids,
    request_token_lengths,
    adapter_store_slot,
):
    groups = lax.axis_size("grp")
    rank_indices = lax.axis_size("tp")
    owner = lax.axis_index(("grp", "tp"))
    my_group = lax.axis_index("grp")
    feature_width = adapter_down_panels.shape[1]
    rank_index = adapter_down_panels.shape[2]
    rank_portion = rank_index // rank_indices
    column_portion = adapter_up_panels.shape[2] // rank_indices
    store_size = adapter_store_slot.shape[0]
    segs = request_adapter_ids.shape[1]
    tok_dev = tokens.shape[1]
    tok_all = tok_dev * rank_indices
    ids = jnp.arange(store_size, dtype=jnp.int32)
    req_slot = jnp.sum(
        jnp.where(
            request_adapter_ids[:, :, None] == ids[None, None, :],
            adapter_store_slot[None, None, :],
            0,
        ),
        axis=-1,
    )
    wanted = jnp.any(req_slot == owner, axis=1)
    down_portions = jnp.transpose(
        adapter_down_panels[0].reshape(feature_width, rank_indices, rank_portion), (1, 2, 0)
    )
    up_portions = jnp.transpose(
        adapter_up_panels[0].reshape(rank_index, rank_indices, column_portion), (1, 0, 2)
    )
    send_down = jnp.where(
        wanted[:, None, None, None], down_portions[None], jnp.zeros_like(down_portions[None])
    )
    send_up = jnp.where(
        wanted[:, None, None, None], up_portions[None], jnp.zeros_like(up_portions[None])
    )
    got_down, got_up = (
        lax.all_to_all(
            send_down.reshape(groups * rank_indices, rank_portion, feature_width),
            ("grp", "tp"),
            split_axis=0,
            concat_axis=0,
            tiled=True,
        ),
        lax.all_to_all(
            send_up.reshape(groups * rank_indices, rank_index, column_portion),
            ("grp", "tp"),
            split_axis=0,
            concat_axis=0,
            tiled=True,
        ),
    )
    my_slots = lax.dynamic_index_in_dim(req_slot, my_group, 0, keepdims=False)
    picker = (my_slots[:, None] == ids[None, :]).astype(jnp.bfloat16)
    down_sel = jnp.einsum(
        "sp,pkd->dsk", picker, got_down, preferred_element_type=jnp.float32
    ).astype(jnp.bfloat16)
    down_sel = down_sel.reshape(feature_width, segs * rank_portion)
    up_sel = jnp.einsum("sp,prc->src", picker, got_up, preferred_element_type=jnp.float32).astype(
        jnp.bfloat16
    )
    up_sel = up_sel.reshape(segs * rank_index, column_portion)
    request_lengths = request_token_lengths[0]
    ends = jnp.cumsum(request_lengths)
    starts = ends - request_lengths
    position = jnp.arange(tok_all, dtype=jnp.int32)[:, None]
    member = ((position >= starts[None, :]) & (position < ends[None, :])).astype(jnp.bfloat16)
    joined = jnp.concatenate([base_projection_weight, down_sel], axis=1)
    combined = jnp.dot(
        lax.all_gather(tokens[0], "tp", axis=0, tiled=True),
        joined,
        preferred_element_type=jnp.float32,
    )
    base_output = combined[:, :column_portion]
    xa = combined[:, column_portion:].reshape(tok_all, segs, rank_portion)
    low_part = jnp.sum(member.astype(jnp.float32)[:, :, None] * xa, axis=1).astype(jnp.bfloat16)
    low_cols = lax.all_gather(jnp.transpose(low_part), "tp", axis=0, tiled=True)
    low = jnp.transpose(low_cols)
    expanded = (member[:, :, None] * low[:, None, :]).reshape(tok_all, segs * rank_index)
    lifted_output = jnp.dot(expanded, up_sel, preferred_element_type=jnp.float32)
    return (base_output + adapter_scale * lifted_output).astype(jnp.bfloat16)[None]


def solution(mesh):
    return jax.shard_map(
        on_device,
        mesh=mesh,
        in_specs=(
            P(("rep", "grp"), "tp", None),
            P(None, "tp"),
            P(("grp", "tp"), None, None),
            P(("grp", "tp"), None, None),
            P("rep", None),
            P(("rep", "grp"), None),
            P(),
        ),
        out_specs=P(("rep", "grp"), None, "tp"),
        check_vma=False,
    )
```

profile of v0, /device:TPU:0, one launch (start us, length us, event | category | flops | bytes accessed | tf_op | source)
XLA Modules:
  0.0 187.5 jit_solution(10456909703878566085)
XLA Ops:
  6.5 0.8 copy.41
  7.3 1.0 fusion.20
  8.3 0.1 broadcast_in_dim.90
  8.4 0.1 broadcast_in_dim.91
  8.5 2.8 %bitcast_select_fusion.1 = bf16[16,8,8192]{2,1,0:T(8,128)(2,1)} fusion(pred[16]{0:T(512)(128)(4,1)S(1)} %broadcast_in_dim.91, bf16[8,8,8192]{2,1,0:T(8,128)(2,1)} %bitcast.57), kind=kLoop, calls=%fused_computation.15 | loop fusion | flops 1048576 | bytes 3145744 | tf_op jit(solution)/shard_map/jit(_where)/select_n | solution.py:46
  11.3 7.5 %all-to-all-start = ((bf16[16,8,8192]{2,1,0:T(8,128)(2,1)}), bf16[16,8,8192]{2,1,0:T(8,128)(2,1)S(1)}, u32[]{:S(2)}, u32[]{:S(2)}) async-start(bf16[16,8,8192]{2,1,0:T(8,128)(2,1)} %bitcast_select_fusion.1), calls=%async_computation | async-start | bytes 4194304 | tf_op jit(solution)/shard_map/all_to_all | solution.py:53
  18.9 0.7 all-gather.3.cloned.1.call-update
  19.6 0.2 copy.52
  19.8 0.2 copy.45
  20.0 1.7 bitcast_select_fusion
  21.8 69.4 %all-to-all-done = bf16[16,8,8192]{2,1,0:T(8,128)(2,1)S(1)} async-done(((bf16[16,8,8192]{2,1,0:T(8,128)(2,1)}), bf16[16,8,8192]{2,1,0:T(8,128)(2,1)S(1)}, u32[]{:S(2)}, u32[]{:S(2)}) %all-to-all-start) | async-done | bytes 2097184 | tf_op jit(solution)/shard_map/all_to_all | solution.py:53
  91.2 1.4 copy-done
  92.6 4.7 %all-to-all-start.1 = ((bf16[16,64,1280]{2,1,0:T(8,128)(2,1)}), bf16[16,64,1280]{2,1,0:T(8,128)(2,1)S(1)}, u32[]{:S(2)}, u32[]{:S(2)}) async-start(bf16[16,64,1280]{2,1,0:T(8,128)(2,1)} %bitcast_select_fusion), calls=%async_computation.1 | async-start | bytes 5242880 | tf_op jit(solution)/shard_map/all_to_all | solution.py:60
  97.4 0.2 reduce-window.4
  97.5 0.2 dynamic-slice_reduce_fusion
  97.7 0.1 fusion.25
  97.8 3.0 %fusion.4 = bf16[8192,12,8]{0,1,2:T(8,128)(2,1)S(1)} fusion(bf16[16,8,8192]{2,1,0:T(8,128)(2,1)} %copy-done, s32[12]{0:T(128)S(1)} %dynamic-slice_reduce_fusion), kind=kOutput, calls=%fused_computation.5 | convolution fusion | flops 25952448 | bytes 3670064 | tf_op jit(solution)/shard_map/sp,pkd->dsk/dot_general | solution.py:70
  100.8 2.0 %copy.60 = bf16[8192,12,8]{0,2,1:T(8,128)(2,1)} copy(bf16[8192,12,8]{0,1,2:T(8,128)(2,1)S(1)} %fusion.4) | data formatting | bytes 3145728 | tf_op jit(solution)/shard_map/convert_element_type | solution.py:72
  102.8 3.9 %copy.44 = bf16[8192,96]{1,0:T(8,128)(2,1)} copy(bf16[8192,96]{0,1:T(8,128)(2,1)} %bitcast.54) | data formatting | bytes 3145728 | tf_op jit(solution)/shard_map/reshape | solution.py:73
  106.6 15.1 %fusion.6 = f32[128,1376]{0,1:T(8,128)S(1)} fusion(bf16[8192,96]{1,0:T(8,128)(2,1)} %copy.44, bf16[8192,1280]{1,0:T(8,128)(2,1)} %param.8, bf16[1,128,8192]{2,1,0:T(8,128)(2,1)} %all-gather.3.cloned.1.call-done), kind=kOutput, calls=%fused_computation.9 | convolution fusion | flops 2930769920 | bytes 25346048 | tf_op jit(solution)/shard_map/dot_general | solution.py:84
  121.7 55.1 %all_gather.7 = bf16[64,128]{1,0:T(8,128)(2,1)S(1)} all-gather(bf16[8,128]{1,0:T(8,128)(2,1)S(1)} %bitcast.59), channel_id=1, replica_groups=mesh['rep'=2,'grp'=2,'tp'=8] {'tp'}, dimensions={0}, use_global_device_ids=true | all-gather | bytes 18432 | tf_op jit(solution)/shard_map/all_gather | solution.py:92
  176.8 1.8 convolution_convert_fusion.1
  178.6 1.1 fusion.11
  179.7 0.9 copy.49
  (11 shorter events, 0.1 us)
Async XLA Ops:
  11.3 8.3 %copy-start.1 = (bf16[1,64,10240]{2,1,0:T(8,128)(2,1)S(1)}, bf16[1,64,10240]{2,1,0:T(8,128)(2,1)}, u32[]{:S(2)}) copy-start(bf16[1,64,10240]{2,1,0:T(8,128)(2,1)} %param.10) | copy-start | bytes 3932164
  11.3 79.9 %all-to-all-start = ((bf16[16,8,8192]{2,1,0:T(8,128)(2,1)}), bf16[16,8,8192]{2,1,0:T(8,128)(2,1)S(1)}, u32[]{:S(2)}, u32[]{:S(2)}) async-start(bf16[16,8,8192]{2,1,0:T(8,128)(2,1)} %bitcast_select_fusion.1), calls=%async_computation | async-start | bytes 4194304 | tf_op jit(solution)/shard_map/all_to_all | solution.py:53
  18.8 87.8 %all-gather.3.cloned.1.call-start = ((), (), s32[]{:S(2)}) async-start(), calls=%async_computation.2 | async-start | bytes 2359296 | tf_op jit(solution)/shard_map/all_gather | solution.py:85
  21.8 75.6 %copy-start.2 = (s32[1,12]{1,0:T(1,128)S(1)}, s32[1,12]{1,0:T(1,128)}, u32[]{:S(2)}) copy-start(s32[1,12]{1,0:T(1,128)} %param.12) | copy-start | bytes 148
  91.2 1.4 copy-start
  92.6 84.2 %all-to-all-start.1 = ((bf16[16,64,1280]{2,1,0:T(8,128)(2,1)}), bf16[16,64,1280]{2,1,0:T(8,128)(2,1)S(1)}, u32[]{:S(2)}, u32[]{:S(2)}) async-start(bf16[16,64,1280]{2,1,0:T(8,128)(2,1)} %bitcast_select_fusion), calls=%async_computation.1 | async-start | bytes 5242880 | tf_op jit(solution)/shard_map/all_to_all | solution.py:60
Sparse Core Ops, SparseCore 0:
  21.8 69.9 all-gather.2
where the time goes:
time: 188 us; the launch traced here: 187 us
  waiting for transfers between devices  70.1 us (37%)
  blocking collectives  55.1 us (29%)
  matrix products  20.9 us (11%)
  between operations  13.5 us (7%)
  starting transfers between devices  12.3 us (7%)
  local copies, waits for them, and re-layouts  9.71 us (5%)
  other arithmetic  5.85 us (3%)
    all_to_all x1, waiting for transfers between devices, on_device(): lax.all_to_all(send_down.reshape(groups * rank_indices, rank_portion, fea...  69.4 us
    all_gather x1, blocking collectives, on_device(): low_cols = lax.all_gather(jnp.transpose(low_part), 'tp', axis=0, tiled=True)  55.1 us
    dot_general x1, matrix products, on_device(): jnp.dot(lax.all_gather(tokens[0], 'tp', axis=0, tiled=True), joined, pref...  15.1 us
    all_to_all x1, starting transfers between devices, on_device(): lax.all_to_all(send_down.reshape(groups * rank_indices, rank_portion, fea...  7.52 us
    all_to_all x1, starting transfers between devices, on_device(): lax.all_to_all(send_up.reshape(groups * rank_indices, rank_index, column_...  4.74 us
    reshape x1, local copies, waits for them, and re-layouts, on_device(): down_sel = down_sel.reshape(feature_width, segs * rank_portion)  3.85 us
  transfers between devices with their start and end apart: 3, of which 1 were waited for; matrix products, arithmetic and copies ran while one was open for 14% of the time, Pallas kernels for 0%

commit v1 on v0

v1 whole, which is shorter than its diff:
```python
import jax
import jax.numpy as jnp
from jax import lax
from jax.sharding import PartitionSpec as P

adapter_scale = 1.0


def swapped(x, axis):
    n = lax.axis_size(axis)
    return [x] + [
        lax.ppermute(x, axis, [((i + s) % n, i) for i in range(n)]) for s in range(1, n)
    ]


def on_device(
    tokens,
    base_projection_weight,
    adapter_down_panels,
    adapter_up_panels,
    request_adapter_ids,
    request_token_lengths,
    adapter_store_slot,
):
    groups = lax.axis_size("grp")
    tp = lax.axis_size("tp")
    reps = lax.axis_size("rep")
    my_group = lax.axis_index("grp")
    my_tp = lax.axis_index("tp")
    my_rep = lax.axis_index("rep")
    rank = adapter_down_panels.shape[2]
    rank_portion = rank // reps
    columns = base_projection_weight.shape[1]
    store_size = adapter_store_slot.shape[0]
    tok_all = tokens.shape[1] * tp

    gathered = lax.all_gather(tokens[0], "tp", axis=0, tiled=True)

    downs = swapped(jnp.transpose(adapter_down_panels[0]), "grp")

    up_mine = lax.dynamic_slice_in_dim(
        adapter_up_panels[0], my_rep * rank_portion, rank_portion, axis=0
    )
    up_send = jnp.transpose(up_mine.reshape(rank_portion, tp, columns), (1, 0, 2))
    up_got = lax.all_to_all(up_send, "tp", split_axis=0, concat_axis=0, tiled=True)
    ups = [swapped(part, "grp") for part in swapped(up_got, "rep")]

    ids = jnp.arange(store_size, dtype=jnp.int32)
    my_ids = lax.dynamic_index_in_dim(request_adapter_ids, my_group, 0, keepdims=False)
    my_slots = jnp.sum(
        jnp.where(my_ids[:, None] == ids[None, :], adapter_store_slot[None, :], 0), axis=-1
    )
    lengths = request_token_lengths[0]
    ends = jnp.cumsum(lengths)
    starts = ends - lengths
    position = jnp.arange(tok_all, dtype=jnp.int32)[:, None]
    member = (position >= starts[None, :]) & (position < ends[None, :])
    token_slot = jnp.sum(jnp.where(member, my_slots[None, :], 0), axis=1)

    low = jnp.concatenate(
        [
            jnp.where(
                (token_slot == ((my_group + s) % groups) * tp + my_tp)[:, None],
                lax.dot_general(
                    gathered, down, (((1,), (1,)), ((), ())), preferred_element_type=jnp.float32
                ),
                0.0,
            )
            for s, down in enumerate(downs)
        ],
        axis=0,
    ).astype(jnp.bfloat16)
    low = lax.dynamic_slice_in_dim(
        jnp.concatenate([low, low], axis=1), my_rep * rank_portion, rank, axis=1
    )
    low_all = lax.all_gather(low, "tp", axis=0).reshape(tp, groups, tok_all, reps, rank_portion)

    total = jnp.dot(gathered, base_projection_weight, preferred_element_type=jnp.float32)
    for r in range(reps):
        for s in range(groups):
            total = total + adapter_scale * lax.dot_general(
                low_all[:, s, :, r, :],
                ups[r][s],
                (((0, 2), (0, 1)), ((), ())),
                preferred_element_type=jnp.float32,
            )
    return total.astype(jnp.bfloat16)[None]


def solution(mesh):
    return jax.shard_map(
        on_device,
        mesh=mesh,
        in_specs=(
            P(("rep", "grp"), "tp", None),
            P(None, "tp"),
            P(("grp", "tp"), None, None),
            P(("grp", "tp"), None, None),
            P("rep", None),
            P(("rep", "grp"), None),
            P(),
        ),
        out_specs=P(("rep", "grp"), None, "tp"),
        check_vma=False,
    )
```

time: 188 us -> 132 us (0.70)
  blocking collectives: 55.1 us -> 32.8 us
  waiting for transfers between devices: 70.1 us -> 51.2 us
  other arithmetic: 5.85 us -> 0.55 us
  local copies, waits for them, and re-layouts: 9.71 us -> 5.1 us
  starting transfers between devices: 12.3 us -> 8.85 us
    all_to_all x2 -> x1, waiting for transfers between devices: 69.4 us -> 25.6 us  [on_device(): lax.all_to_all(up_send, 'tp', split_axis=0, concat_axis=0, tiled=True)]
    all_gather x1, blocking collectives: 55.1 us -> 32.8 us  [on_device(): lax.all_gather(low, 'tp', axis=0)]
    all_gather x1, waiting for transfers between devices: 0.01 us -> 14.3 us  [on_device(): gathered = lax.all_gather(tokens[0], 'tp', axis=0, tiled=True)]
    ppermute x0 -> x4, waiting for transfers between devices: none -> 10.6 us  [swapped(): lax.ppermute(x, axis, [((i + s) % n, i) for i in range(n)])]
    all_to_all x2 -> x1, starting transfers between devices: 12.3 us -> 7.28 us  [on_device(): lax.all_to_all(up_send, 'tp', split_axis=0, concat_axis=0, tiled=True)]
    select_n x2 -> x0, other arithmetic: 4.55 us -> none  [the longest x1 2.8 us: on_device(): jnp.where(wanted[:, None, None, None], down_portions[None], jnp.zeros_lik...]
    convert_element_type x1 -> x0, local copies, waits for them, and re-layouts: 2.01 us -> none  [on_device(): down_sel = jnp.einsum('sp,pkd->dsk', picker, got_down, preferred_element_...]
    dot_general x4 -> x7, matrix products: 20.9 us -> 19.7 us  [the longest x1 8.59 us: on_device(): jnp.dot(gathered, base_projection_weight, preferred_element_type=jnp.floa...]
  transfers between devices with their start and end apart: 3 -> 6, of which waited for: 1 -> 3; matrix products, arithmetic and copies ran while one was open for 14% -> 17% of each run, Pallas kernels for 0% -> 0%
where the time goes in v1:
time: 132 us
  waiting for transfers between devices  51.2 us (39%)
  blocking collectives  32.8 us (25%)
  matrix products  19.7 us (15%)
  between operations  13.6 us (10%)
  starting transfers between devices  8.85 us (7%)
  local copies, waits for them, and re-layouts  5.1 us (4%)
    all_gather x1, blocking collectives, on_device(): lax.all_gather(low, 'tp', axis=0)  32.8 us
    all_to_all x1, waiting for transfers between devices, on_device(): lax.all_to_all(up_send, 'tp', split_axis=0, concat_axis=0, tiled=True)  25.6 us
    all_gather x1, waiting for transfers between devices, on_device(): gathered = lax.all_gather(tokens[0], 'tp', axis=0, tiled=True)  14.3 us
    ppermute x4, waiting for transfers between devices, swapped(): lax.ppermute(x, axis, [((i + s) % n, i) for i in range(n)])  10.6 us
    dot_general x1, matrix products, on_device(): jnp.dot(gathered, base_projection_weight, preferred_element_type=jnp.floa...  8.59 us
    all_to_all x1, starting transfers between devices, on_device(): lax.all_to_all(up_send, 'tp', split_axis=0, concat_axis=0, tiled=True)  7.28 us
    dot_general x4, matrix products, on_device(): lax.dot_general(low_all[:, s, :, r, :], ups[r][s], (((0, 2), (0, 1)), (()...  6.18 us
    dot_general x2, matrix products, on_device(): lax.dot_general(gathered, down, (((1,), (1,)), ((), ())), preferred_eleme...  4.92 us
  transfers between devices with their start and end apart: 6, of which 3 were waited for; matrix products, arithmetic and copies ran while one was open for 17% of the time, Pallas kernels for 0%

profile of v1, /device:TPU:0, one launch (start us, length us, event | category | flops | bytes accessed | tf_op | source)
XLA Modules:
  0.0 131.7 jit_solution(11962570950600614627)
XLA Ops:
  6.5 0.7 all-gather.4.cloned.1.call-update
  7.3 0.6 copy-done
  7.9 0.1 copy.26
  8.1 0.9 copy.36
  9.0 7.3 %all-to-all-start = ((bf16[8,32,1280]{2,1,0:T(8,128)(2,1)}), bf16[8,32,1280]{2,1,0:T(8,128)(2,1)}, u32[]{:S(2)}, u32[]{:S(2)}) async-start(bf16[8,32,1280]{2,1,0:T(8,128)(2,1)} %bitcast.75), calls=%async_computation | async-start | bytes 1310720 | tf_op jit(solution)/shard_map/all_to_all | solution.py:45
  16.3 0.2 reduce-window.4
  16.5 25.6 %all-to-all-done = bf16[8,32,1280]{2,1,0:T(8,128)(2,1)} async-done(((bf16[8,32,1280]{2,1,0:T(8,128)(2,1)}), bf16[8,32,1280]{2,1,0:T(8,128)(2,1)}, u32[]{:S(2)}, u32[]{:S(2)}) %all-to-all-start) | async-done | bytes 655392 | tf_op jit(solution)/shard_map/all_to_all | solution.py:45
  42.1 1.5 %collective-permute-start.2 = (bf16[8,32,1280]{2,1,0:T(8,128)(2,1)}, bf16[8,32,1280]{2,1,0:T(8,128)(2,1)}, u32[]{:S(2)}, u32[]{:S(2)}) collective-permute-start(bf16[8,32,1280]{2,1,0:T(8,128)(2,1)} %all-to-all-done), channel_id=1, source_target_pairs={{16,0},{0,16},{17,1},{1,17},{18,2},{2,18},{19,3},{3,19},{20,4},{4,... | collective-permute-start | bytes 1966088 | tf_op jit(solution)/shard_map/ppermute | solution.py:12
  43.6 0.2 select_reduce_fusion.1
  43.8 0.1 select_reduce_fusion
  43.9 0.1 collective-permute-start.1
  44.0 10.6 %collective-permute-done.2 = bf16[8,32,1280]{2,1,0:T(8,128)(2,1)} collective-permute-done((bf16[8,32,1280]{2,1,0:T(8,128)(2,1)}, bf16[8,32,1280]{2,1,0:T(8,128)(2,1)}, u32[]{:S(2)}, u32[]{:S(2)}) %collective-permute-start.2) | collective-permute-done | bytes 655392 | tf_op jit(solution)/shard_map/ppermute | solution.py:12
  54.6 14.3 %all-gather.4.cloned.1.call-done = bf16[1,128,8192]{2,1,0:T(8,128)(2,1)} async-done(((bf16[1,16,8192]{2,1,0:T(8,128)(2,1)}), bf16[1,128,8192]{2,1,0:T(8,128)(2,1)}) %all-gather.4.cloned.1.call-update) | async-done | bytes 2097168 | tf_op jit(solution)/shard_map/all_gather | solution.py:37
  68.9 2.8 %fusion.19 = bf16[128,64]{0,1:T(8,128)(2,1)S(1)} fusion(bf16[1,128,8192]{2,1,0:T(8,128)(2,1)} %all-gather.4.cloned.1.call-done, bf16[1,8192,64]{1,2,0:T(8,128)(2,1)} %param.9, pred[128]{0:T(512)(128)(4,1)S(1)} %get-tuple-element.10), kind=kOutput, calls=%fused_computation.18 | convolution fusion | flops 134234112 | bytes 3162240 | tf_op jit(solution)/shard_map/dot_general | solution.py:64
  71.8 2.1 %fusion.16 = bf16[128,64]{0,1:T(8,128)(2,1)S(1)} fusion(bf16[64,8192]{1,0:T(8,128)(2,1)} %collective-permute-done, bf16[1,128,8192]{2,1,0:T(8,128)(2,1)S(1)} %copy-done.1, pred[128]{0:T(512)(128)(4,1)S(1)} %get-tuple-element.9), kind=kOutput, calls=%fused_computation.17 | convolution fusion | flops 134234112 | bytes 3162240 | tf_op jit(solution)/shard_map/dot_general | solution.py:64
  73.8 0.1 fusion.24
  73.9 32.8 %all-gather.1 = bf16[2048,64]{0,1:T(8,128)(2,1)} all-gather(bf16[256,64]{0,1:T(8,128)(2,1)S(1)} %fusion.24), channel_id=3, replica_groups=mesh['rep'=2,'grp'=2,'tp'=8] {'tp'}, dimensions={0}, use_global_device_ids=true | all-gather | bytes 294912 | tf_op jit(solution)/shard_map/all_gather | solution.py:76
  106.7 1.8 %reshape.30 = bf16[8,2,128,2,32]{2,1,0,4,3:T(2,128)(2,1)} reshape(bf16[2048,64]{0,1:T(8,128)(2,1)} %all-gather.1) | data formatting | bytes 524288 | tf_op jit(solution)/shard_map/reshape | solution.py:76
  108.5 1.6 %fusion.29 = (bf16[8,1,128,1,32]{2,1,0,4,3:T(2,128)(2,1)S(1)}, bf16[8,1,128,1,32]{2,1,0,4,3:T(2,128)(2,1)S(1)}, bf16[8,1,128,1,32]{2,1,0,4,3:T(2,128)(2,1)S(1)}, bf16[8,1,128,1,32]{2,1,0,4,3:T(2,128)(2,1)S(1)}) fusion(bf16[8,2,128,2,32]{2,1,0,4,3:T(2,128)(2,1)} %reshape.30), kind=kLoop, calls=%fused_computation.45 | loop fusion | bytes 524288 | tf_op jit(solution)/shard_map/slice | solution.py:82
  110.1 1.4 %convolution_bitcast_fusion.3 = f32[128,1280]{1,0:T(8,128)S(1)} fusion(bf16[8,32,1280]{2,1,0:T(8,128)(2,1)} %all-to-all-done, bf16[8,1,128,1,32]{2,1,0,4,3:T(2,128)(2,1)S(1)} %get-tuple-element.8), kind=kOutput, calls=%fused_computation.7 | convolution fusion | flops 83886080 | bytes 1376256 | tf_op jit(solution)/shard_map/dot_general | solution.py:81
  111.4 8.6 %convolution_add_fusion = f32[128,1280]{1,0:T(8,128)S(1)} fusion(f32[128,1280]{1,0:T(8,128)S(1)} %convolution_bitcast_fusion.3, bf16[8192,1280]{1,0:T(8,128)(2,1)} %param.8, bf16[1,128,8192]{2,1,0:T(8,128)(2,1)S(1)} %copy-done.1), kind=kOutput, calls=%fused_computation | convolution fusion | flops 2684518400 | bytes 24379392 | tf_op jit(solution)/shard_map/dot_general | solution.py:78
  120.0 1.4 %fusion.2 = f32[128,1280]{1,0:T(8,128)S(1)} fusion(f32[128,1280]{1,0:T(8,128)S(1)} %convolution_add_fusion, bf16[8,32,1280]{2,1,0:T(8,128)(2,1)} %collective-permute-done.1, bf16[8,1,128,1,32]{2,1,0,4,3:T(2,128)(2,1)S(1)} %get-tuple-element.7), kind=kOutput, calls=%fused_computation.6 | convolution fusion | flops 84049920 | bytes 2031616 | tf_op jit(solution)/shard_map/dot_general | solution.py:81
  121.4 1.4 %fusion.1 = f32[128,1280]{1,0:T(8,128)S(1)} fusion(f32[128,1280]{1,0:T(8,128)S(1)} %fusion.2, bf16[8,32,1280]{2,1,0:T(8,128)(2,1)} %collective-permute-done.2, bf16[8,1,128,1,32]{2,1,0,4,3:T(2,128)(2,1)S(1)} %get-tuple-element.6), kind=kOutput, calls=%fused_computation.4 | convolution fusion | flops 84049920 | bytes 2031616 | tf_op jit(solution)/shard_map/dot_general | solution.py:81
  122.8 2.1 %fusion.4 = bf16[1,128,1280]{2,1,0:T(8,128)(2,1)} fusion(f32[128,1280]{1,0:T(8,128)S(1)} %fusion.1, bf16[8,32,1280]{2,1,0:T(8,128)(2,1)} %collective-permute-done.3, bf16[8,1,128,1,32]{2,1,0,4,3:T(2,128)(2,1)S(1)} %get-tuple-element.5), kind=kOutput, calls=%fused_computation.9 | convolution fusion | flops 84213760 | bytes 1703936 | tf_op jit(solution)/shard_map/dot_general | solution.py:81
  (19 shorter events, 0.1 us)
Async XLA Ops:
  6.5 1.3 copy-start
  6.5 62.3 %all-gather.4.cloned.1.call-start = ((), (), s32[]{:S(2)}) async-start(), calls=%async_computation.1 | async-start | bytes 2359296 | tf_op jit(solution)/shard_map/all_gather | solution.py:37
  7.9 8.4 %copy-start.4 = (s32[1,12]{1,0:T(1,128)S(1)}, s32[1,12]{1,0:T(1,128)}, u32[]{:S(2)}) copy-start(s32[1,12]{1,0:T(1,128)} %param.12) | copy-start | bytes 148
  7.9 8.6 %copy-start.2 = (s32[2,12]{1,0:T(2,128)S(1)}, s32[2,12]{1,0:T(2,128)}, u32[]{:S(2)}) copy-start(s32[2,12]{1,0:T(2,128)} %param.11) | copy-start | bytes 292
  7.9 35.7 %copy-start.3 = (s32[16]{0:T(128)S(1)}, s32[16]{0:T(128)}, u32[]{:S(2)}) copy-start(s32[16]{0:T(128)} %param.13) | copy-start | bytes 196
  9.0 33.1 %all-to-all-start = ((bf16[8,32,1280]{2,1,0:T(8,128)(2,1)}), bf16[8,32,1280]{2,1,0:T(8,128)(2,1)}, u32[]{:S(2)}, u32[]{:S(2)}) async-start(bf16[8,32,1280]{2,1,0:T(8,128)(2,1)} %bitcast.75), calls=%async_computation | async-start | bytes 1310720 | tf_op jit(solution)/shard_map/all_to_all | solution.py:45
  16.3 55.5 %collective-permute-start = (bf16[64,8192]{1,0:T(8,128)(2,1)}, bf16[64,8192]{1,0:T(8,128)(2,1)}, u32[]{:S(2)}, u32[]{:S(2)}) collective-permute-start(bf16[64,8192]{1,0:T(8,128)(2,1)} %bitcast.7), channel_id=1, source_target_pairs={{8,0},{0,8},{9,1},{1,9},{10,2},{2,10},{11,3},{3,11},{12,4},{4,12},... | collective-permute-start | bytes 3145736 | tf_op jit(solution)/shard_map/ppermute | solution.py:12
  42.1 12.5 %collective-permute-start.2 = (bf16[8,32,1280]{2,1,0:T(8,128)(2,1)}, bf16[8,32,1280]{2,1,0:T(8,128)(2,1)}, u32[]{:S(2)}, u32[]{:S(2)}) collective-permute-start(bf16[8,32,1280]{2,1,0:T(8,128)(2,1)} %all-to-all-done), channel_id=1, source_target_pairs={{16,0},{0,16},{17,1},{1,17},{18,2},{2,18},{19,3},{3,19},{20,4},{4,... | collective-permute-start | bytes 1966088 | tf_op jit(solution)/shard_map/ppermute | solution.py:12
  43.9 76.1 %collective-permute-start.1 = (bf16[8,32,1280]{2,1,0:T(8,128)(2,1)}, bf16[8,32,1280]{2,1,0:T(8,128)(2,1)}, u32[]{:S(2)}, u32[]{:S(2)}) collective-permute-start(bf16[8,32,1280]{2,1,0:T(8,128)(2,1)} %all-to-all-done), channel_id=1, source_target_pairs={{8,0},{0,8},{9,1},{1,9},{10,2},{2,10},{11,3},{3,11},{12,4},{4,12},... | collective-permute-start | bytes 1966088 | tf_op jit(solution)/shard_map/ppermute | solution.py:12
  54.6 68.2 %collective-permute-start.3 = (bf16[8,32,1280]{2,1,0:T(8,128)(2,1)}, bf16[8,32,1280]{2,1,0:T(8,128)(2,1)}, u32[]{:S(2)}, u32[]{:S(2)}) collective-permute-start(bf16[8,32,1280]{2,1,0:T(8,128)(2,1)} %collective-permute-done.2), channel_id=1, source_target_pairs={{8,0},{0,8},{9,1},{1,9},{10,2},{2,10},{11,3},{3,11},{12,4},{4,12},... | collective-permute-start | bytes 1966088 | tf_op jit(solution)/shard_map/ppermute | solution.py:12
  68.9 2.9 %copy-start.1 = (bf16[1,128,8192]{2,1,0:T(8,128)(2,1)S(1)}, bf16[1,128,8192]{2,1,0:T(8,128)(2,1)}, u32[]{:S(2)}) copy-start(bf16[1,128,8192]{2,1,0:T(8,128)(2,1)} %all-gather.4.cloned.1.call-done) | copy-start | bytes 6291460
Sparse Core Ops, SparseCore 0:
  9.5 59.3 all-gather.3

commit v2 on v1

--- a/solution.py
+++ b/solution.py
@@ -11,6 +11,50 @@
     return [x] + [
         lax.ppermute(x, axis, [((i + s) % n, i) for i in range(n)]) for s in range(1, n)
     ]
+
+
+def ring_of(n):
+    return list(range(0, n, 2)) + list(range(1, n, 2))[::-1]
+
+
+def ring_gather(block, axis):
+    n = lax.axis_size(axis)
+    ring = ring_of(n)
+    rows, width = block.shape
+    me = lax.axis_index(axis)
+    place = jnp.where(me % 2 == 0, me // 2, n - 1 - me // 2)
+    up = [(ring[i], ring[(i + 1) % n]) for i in range(n)]
+    down = [(ring[(i + 1) % n], ring[i]) for i in range(n)]
+    out = jnp.zeros((n * rows, width), block.dtype)
+
+    def put(out, part, distance, column):
+        at = lax.rem(place - distance + n, n)
+        source = jnp.where(at < n // 2, 2 * at, 2 * (n - 1 - at) + 1)
+        return lax.dynamic_update_slice(out, part, (source * rows, column))
+
+    out = put(out, block, 0, 0)
+    ahead = behind = block
+    for step in range(1, n // 2):
+        ahead = lax.ppermute(ahead, axis, up)
+        behind = lax.ppermute(behind, axis, down)
+        out = put(out, ahead, step, 0)
+        out = put(out, behind, -step, 0)
+    half = width // 2
+    out = put(out, lax.ppermute(ahead[:, :half], axis, up), n // 2, 0)
+    out = put(out, lax.ppermute(behind[:, half:], axis, down), n // 2, half)
+    return out
+
+
+def direct_gather(block, axis):
+    n = lax.axis_size(axis)
+    me = lax.axis_index(axis)
+    out = jnp.zeros((n, *block.shape), block.dtype)
+    for shift in range(n):
+        part = block if shift == 0 else lax.ppermute(
+            block, axis, [(i, (i + shift) % n) for i in range(n)]
+        )
+        out = lax.dynamic_update_index_in_dim(out, part, lax.rem(me - shift + n, n), 0)
+    return out
 
 
 def on_device(
@@ -34,7 +78,7 @@
     store_size = adapter_store_slot.shape[0]
     tok_all = tokens.shape[1] * tp
 
-    gathered = lax.all_gather(tokens[0], "tp", axis=0, tiled=True)
+    gathered = ring_gather(tokens[0], "tp")
 
     downs = swapped(jnp.transpose(adapter_down_panels[0]), "grp")
 
@@ -57,29 +101,35 @@
     member = (position >= starts[None, :]) & (position < ends[None, :])
     token_slot = jnp.sum(jnp.where(member, my_slots[None, :], 0), axis=1)
 
-    low = jnp.concatenate(
-        [
-            jnp.where(
-                (token_slot == ((my_group + s) % groups) * tp + my_tp)[:, None],
-                lax.dot_general(
-                    gathered, down, (((1,), (1,)), ((), ())), preferred_element_type=jnp.float32
-                ),
-                0.0,
-            )
-            for s, down in enumerate(downs)
-        ],
-        axis=0,
+    low = sum(
+        jnp.where(
+            (token_slot == ((my_group + s) % groups) * tp + my_tp)[:, None],
+            lax.dot_general(
+                gathered, down, (((1,), (1,)), ((), ())), preferred_element_type=jnp.float32
+            ),
+            0.0,
+        )
+        for s, down in enumerate(downs)
     ).astype(jnp.bfloat16)
     low = lax.dynamic_slice_in_dim(
         jnp.concatenate([low, low], axis=1), my_rep * rank_portion, rank, axis=1
     )
-    low_all = lax.all_gather(low, "tp", axis=0).reshape(tp, groups, tok_all, reps, rank_portion)
+    low_all = direct_gather(low, "tp")
+    owners = jnp.arange(tp, dtype=jnp.int32)
+    expanded = [
+        jnp.where(
+            (token_slot[None, :] == (((my_group + s) % groups) * tp + owners)[:, None])[:, :, None],
+            low_all,
+            jnp.zeros_like(low_all),
+        )
+        for s in range(groups)
+    ]
 
     total = jnp.dot(gathered, base_projection_weight, preferred_element_type=jnp.float32)
     for r in range(reps):
         for s in range(groups):
             total = total + adapter_scale * lax.dot_general(
-                low_all[:, s, :, r, :],
+                expanded[s][:, :, r * rank_portion : (r + 1) * rank_portion],
                 ups[r][s],
                 (((0, 2), (0, 1)), ((), ())),
                 preferred_element_type=jnp.float32,

time: 132 us -> 88.3 us (0.67)
  blocking collectives: 32.8 us -> 0 us
  starting transfers between devices: 8.85 us -> 32.6 us
  waiting for transfers between devices: 51.2 us -> 29.9 us
  between operations: 13.6 us -> 0.3 us
  matrix products: 19.7 us -> 15.7 us
  other arithmetic: 0.55 us -> 2.52 us
  local copies, waits for them, and re-layouts: 5.1 us -> 6.65 us
    all_gather x1 -> x0, blocking collectives: 32.8 us -> none  [on_device(): lax.all_gather(low, 'tp', axis=0)]
    all_to_all x1, waiting for transfers between devices: 25.6 us -> 0.01 us  [on_device(): lax.all_to_all(up_send, 'tp', split_axis=0, concat_axis=0, tiled=True)]
    ppermute x0 -> x15, starting transfers between devices: none -> 24.6 us  [the longest x7 11.5 us: direct_gather(): lax.ppermute(block, axis, [(i, (i + shift) % n) for i in range(n)])]
    ppermute x0 -> x15, waiting for transfers between devices: none -> 22.1 us  [the longest x3 16.9 us: ring_gather(): ahead = lax.ppermute(ahead, axis, up)]
    all_gather x1 -> x0, waiting for transfers between devices: 14.3 us -> none  [on_device(): gathered = lax.all_gather(tokens[0], 'tp', axis=0, tiled=True)]
    dynamic_update_slice x0 -> x16, local copies, waits for them, and re-layouts: none -> 5.25 us  [the longest x9 3.03 us: put(): return lax.dynamic_update_slice(out, part, (source * rows, column))]
    dot_general x4, matrix products: 6.18 us -> 2.89 us  [on_device(): lax.dot_general(expanded[s][:, :, r * rank_portion:(r + 1) * rank_portion...]
    ppermute x4, waiting for transfers between devices: 10.6 us -> 7.84 us  [swapped(): lax.ppermute(x, axis, [((i + s) % n, i) for i in range(n)])]
  transfers between devices with their start and end apart: 6 -> 20, of which waited for: 3 -> 7; matrix products, arithmetic and copies ran while one was open for 17% -> 27% of each run, Pallas kernels for 0% -> 0%
where the time goes in v2:
time: 88.3 us; the launch traced here: 87.7 us
  starting transfers between devices  32.6 us (37%)
  waiting for transfers between devices  29.9 us (34%)
  matrix products  15.7 us (18%)
  local copies, waits for them, and re-layouts  6.65 us (8%)
  other arithmetic  2.52 us (3%)
    ppermute x3, waiting for transfers between devices, ring_gather(): ahead = lax.ppermute(ahead, axis, up)  16.9 us
    ppermute x7, starting transfers between devices, direct_gather(): lax.ppermute(block, axis, [(i, (i + shift) % n) for i in range(n)])  11.5 us
    ppermute x3, starting transfers between devices, ring_gather(): ahead = lax.ppermute(ahead, axis, up)  9.97 us
    dot_general x1, matrix products, on_device(): jnp.dot(gathered, base_projection_weight, preferred_element_type=jnp.floa...  9.92 us
    ppermute x4, waiting for transfers between devices, swapped(): lax.ppermute(x, axis, [((i + s) % n, i) for i in range(n)])  7.84 us
    all_to_all x1, starting transfers between devices, on_device(): lax.all_to_all(up_send, 'tp', split_axis=0, concat_axis=0, tiled=True)  6.4 us
    dynamic_update_slice x9, local copies, waits for them, and re-layouts, put(): return lax.dynamic_update_slice(out, part, (source * rows, column))  3.03 us
    dot_general x2, matrix products, on_device(): lax.dot_general(gathered, down, (((1,), (1,)), ((), ())), preferred_eleme...  2.91 us
  transfers between devices with their start and end apart: 20, of which 7 were waited for; matrix products, arithmetic and copies ran while one was open for 27% of the time, Pallas kernels for 0%

profile of v2, /device:TPU:0, one launch (start us, length us, event | category | flops | bytes accessed | tf_op | source)
XLA Modules:
  0.0 87.7 jit_solution(5750605069889736869)
XLA Ops:
  0.0 3.0 %collective-permute-start = (bf16[16,8192]{1,0:T(8,128)(2,1)}, bf16[16,8192]{1,0:T(8,128)(2,1)}, u32[]{:S(2)}, u32[]{:S(2)}) collective-permute-start(bf16[16,8192]{1,0:T(8,128)(2,1)} %bitcast.67), channel_id=1, source_target_pairs={{0,2},{2,4},{4,6},{6,7},{7,5},{5,3},{3,1},{1,0},{8,10},{10,12},{12... | collective-permute-start | bytes 786440 | tf_op jit(solution)/shard_map/ppermute | solution.py:38
  3.2 1.0 %copy.12 = bf16[32,8,1280]{2,0,1:T(8,128)(2,1)} copy(bf16[32,8,1280]{2,1,0:T(8,128)(2,1)S(1)} %bitcast.65) | data formatting | bytes 1310720 | tf_op jit(solution)/shard_map/reshape | solution.py:88
  4.2 6.4 %all-to-all-start = ((bf16[8,32,1280]{2,1,0:T(8,128)(2,1)}), bf16[8,32,1280]{2,1,0:T(8,128)(2,1)}, u32[]{:S(2)}, u32[]{:S(2)}) async-start(bf16[8,32,1280]{2,1,0:T(8,128)(2,1)} %bitcast.63), calls=%async_computation | async-start | bytes 1310720 | tf_op jit(solution)/shard_map/all_to_all | solution.py:89
  11.0 1.0 %constant_dynamic-update-slice_fusion.7 = bf16[128,8192]{1,0:T(8,128)(2,1)S(1)} fusion(bf16[128,8192]{1,0:T(8,128)(2,1)S(1)} %broadcast_in_dim.101, s32[]{:T(128)S(6)} %select_n.138, bf16[1,16,8192]{2,1,0:T(8,128)(2,1)} %param.7), kind=kLoop, calls=%fused_computation.48 | loop fusion | bytes 524292 | tf_op jit(solution)/shard_map/dynamic_update_slice | solution.py:33
  12.9 2.1 %collective-permute-start.2 = (bf16[16,8192]{1,0:T(8,128)(2,1)}, bf16[16,8192]{1,0:T(8,128)(2,1)S(1)}, u32[]{:S(2)}, u32[]{:S(2)}) collective-permute-start(bf16[16,8192]{1,0:T(8,128)(2,1)} %collective-permute-done), channel_id=1, source_target_pairs={{0,2},{2,4},{4,6},{6,7},{7,5},{5,3},{3,1},{1,0},{8,10},{10,12},{12... | collective-permute-start | bytes 786440 | tf_op jit(solution)/shard_map/ppermute | solution.py:38
  15.0 1.0 %constant_dynamic-update-slice_fusion.6 = bf16[128,8192]{1,0:T(8,128)(2,1)S(1)} fusion(bf16[128,8192]{1,0:T(8,128)(2,1)S(1)} %constant_dynamic-update-slice_fusion.7, bf16[16,8192]{1,0:T(8,128)(2,1)} %collective-permute-done, s32[]{:T(128)S(6)} %select_n.140), kind=kLoop, calls=%fused_computation.47 | loop fusion | bytes 524292 | tf_op jit(solution)/shard_map/dynamic_update_slice | solution.py:33
  16.0 1.0 %constant_dynamic-update-slice_fusion.5 = bf16[128,8192]{1,0:T(8,128)(2,1)S(1)} fusion(bf16[128,8192]{1,0:T(8,128)(2,1)S(1)} %constant_dynamic-update-slice_fusion.6, bf16[16,8192]{1,0:T(8,128)(2,1)} %collective-permute-done.1, s32[]{:T(128)S(6)} %select_n.142), kind=kLoop, calls=%fused_computation.46 | loop fusion | bytes 524292 | tf_op jit(solution)/shard_map/dynamic_update_slice | solution.py:33
  17.0 11.2 %collective-permute-done.2 = bf16[16,8192]{1,0:T(8,128)(2,1)S(1)} collective-permute-done((bf16[16,8192]{1,0:T(8,128)(2,1)}, bf16[16,8192]{1,0:T(8,128)(2,1)S(1)}, u32[]{:S(2)}, u32[]{:S(2)}) %collective-permute-start.2) | collective-permute-done | bytes 262176 | tf_op jit(solution)/shard_map/ppermute | solution.py:38
  28.2 4.9 %collective-permute-start.4 = (bf16[16,8192]{1,0:T(8,128)(2,1)S(1)}, bf16[16,8192]{1,0:T(8,128)(2,1)S(1)}, u32[]{:S(2)}, u32[]{:S(2)}) collective-permute-start(bf16[16,8192]{1,0:T(8,128)(2,1)S(1)} %collective-permute-done.2), channel_id=1, source_target_pairs={{0,2},{2,4},{4,6},{6,7},{7,5},{5,3},{3,1},{1,0},{8,10},{10,12},{12... | collective-permute-start | bytes 786440 | tf_op jit(solution)/shard_map/ppermute | solution.py:38
  33.1 5.7 %collective-permute-done.4 = bf16[16,8192]{1,0:T(8,128)(2,1)S(1)} collective-permute-done((bf16[16,8192]{1,0:T(8,128)(2,1)S(1)}, bf16[16,8192]{1,0:T(8,128)(2,1)S(1)}, u32[]{:S(2)}, u32[]{:S(2)}) %collective-permute-start.4) | collective-permute-done | bytes 262176 | tf_op jit(solution)/shard_map/ppermute | solution.py:38
  38.9 2.5 %collective-permute-start.6 = (bf16[16,4096]{1,0:T(8,128)(2,1)S(1)}, bf16[16,4096]{1,0:T(8,128)(2,1)S(1)}, u32[]{:S(2)}, u32[]{:S(2)}) collective-permute-start(bf16[16,4096]{1,0:T(8,128)(2,1)S(1)} %slice.24), channel_id=1, source_target_pairs={{0,2},{2,4},{4,6},{6,7},{7,5},{5,3},{3,1},{1,0},{8,10},{10,12},{12... | collective-permute-start | bytes 393224 | tf_op jit(solution)/shard_map/ppermute | solution.py:43
  42.3 2.8 %collective-permute-done.6 = bf16[16,4096]{1,0:T(8,128)(2,1)S(1)} collective-permute-done((bf16[16,4096]{1,0:T(8,128)(2,1)S(1)}, bf16[16,4096]{1,0:T(8,128)(2,1)S(1)}, u32[]{:S(2)}, u32[]{:S(2)}) %collective-permute-start.6) | collective-permute-done | bytes 131104 | tf_op jit(solution)/shard_map/ppermute | solution.py:43
  45.1 1.7 %collective-permute-done.7 = bf16[16,4096]{1,0:T(8,128)(2,1)S(1)} collective-permute-done((bf16[16,4096]{1,0:T(8,128)(2,1)S(1)}, bf16[16,4096]{1,0:T(8,128)(2,1)S(1)}, u32[]{:S(2)}, u32[]{:S(2)}) %collective-permute-start.7) | collective-permute-done | bytes 131104 | tf_op jit(solution)/shard_map/ppermute | solution.py:44
  46.8 2.1 %convolution_select_fusion = f32[128,64]{0,1:T(8,128)S(1)} fusion(bf16[128,8192]{1,0:T(8,128)(2,1)S(1)} %constant_dynamic-update-slice_fusion.8, bf16[64,8192]{1,0:T(8,128)(2,1)} %collective-permute-done.8, pred[128]{0:T(512)(128)(4,1)S(1)} %get-tuple-element.12), kind=kOutput, calls=%fused_computation.10 | convolution fusion | flops 134225920 | bytes 3178624 | tf_op jit(solution)/shard_map/dot_general | solution.py:107
  51.0 2.0 %collective-permute-start.10 = (bf16[128,64]{0,1:T(8,128)(2,1)S(1)}, bf16[128,64]{0,1:T(8,128)(2,1)S(1)}, u32[]{:S(2)}, u32[]{:S(2)}) collective-permute-start(bf16[128,64]{0,1:T(8,128)(2,1)S(1)} %get-tuple-element.6), channel_id=1, source_target_pairs={{0,2},{1,3},{2,4},{3,5},{4,6},{5,7},{6,0},{7,1},{8,10},{9,11},{10,... | collective-permute-start | bytes 49160 | tf_op jit(solution)/shard_map/ppermute | solution.py:53
  53.0 1.2 %collective-permute-start.11 = (bf16[128,64]{0,1:T(8,128)(2,1)S(1)}, bf16[128,64]{0,1:T(8,128)(2,1)S(1)}, u32[]{:S(2)}, u32[]{:S(2)}) collective-permute-start(bf16[128,64]{0,1:T(8,128)(2,1)S(1)} %get-tuple-element.6), channel_id=1, source_target_pairs={{0,3},{1,4},{2,5},{3,6},{4,7},{5,0},{6,1},{7,2},{8,11},{9,12},{10,... | collective-permute-start | bytes 49160 | tf_op jit(solution)/shard_map/ppermute | solution.py:53
  54.3 3.7 %collective-permute-start.12 = (bf16[128,64]{0,1:T(8,128)(2,1)S(1)}, bf16[128,64]{0,1:T(8,128)(2,1)S(1)}, u32[]{:S(2)}, u32[]{:S(2)}) collective-permute-start(bf16[128,64]{0,1:T(8,128)(2,1)S(1)} %get-tuple-element.6), channel_id=1, source_target_pairs={{0,4},{1,5},{2,6},{3,7},{4,0},{5,1},{6,2},{7,3},{8,12},{9,13},{10,... | collective-permute-start | bytes 49160 | tf_op jit(solution)/shard_map/ppermute | solution.py:53
  58.1 2.9 %collective-permute-start.14 = (bf16[128,64]{0,1:T(8,128)(2,1)S(1)}, bf16[128,64]{0,1:T(8,128)(2,1)}, u32[]{:S(2)}, u32[]{:S(2)}) collective-permute-start(bf16[128,64]{0,1:T(8,128)(2,1)S(1)} %get-tuple-element.6), channel_id=1, source_target_pairs={{0,6},{1,7},{2,0},{3,1},{4,2},{5,3},{6,4},{7,5},{8,14},{9,15},{10,... | collective-permute-start | bytes 49160 | tf_op jit(solution)/shard_map/ppermute | solution.py:53
  61.7 1.1 %collective-permute-start.15 = (bf16[128,64]{0,1:T(8,128)(2,1)S(1)}, bf16[128,64]{0,1:T(8,128)(2,1)}, u32[]{:S(2)}, u32[]{:S(2)}) collective-permute-start(bf16[128,64]{0,1:T(8,128)(2,1)S(1)} %get-tuple-element.6), channel_id=1, source_target_pairs={{0,7},{1,0},{2,1},{3,2},{4,3},{5,4},{6,5},{7,6},{8,15},{9,8},{10,9... | collective-permute-start | bytes 49160 | tf_op jit(solution)/shard_map/ppermute | solution.py:53
  62.8 1.6 %collective-permute-start.17 = (bf16[8,32,1280]{2,1,0:T(8,128)(2,1)}, bf16[8,32,1280]{2,1,0:T(8,128)(2,1)S(1)}, u32[]{:S(2)}, u32[]{:S(2)}) collective-permute-start(bf16[8,32,1280]{2,1,0:T(8,128)(2,1)} %all-to-all-done), channel_id=1, source_target_pairs={{16,0},{0,16},{17,1},{1,17},{18,2},{2,18},{19,3},{3,19},{20,4},{4,... | collective-permute-start | bytes 1966088 | tf_op jit(solution)/shard_map/ppermute | solution.py:12
  67.0 1.4 %convolution_bitcast_fusion.3 = f32[128,1280]{1,0:T(8,128)S(1)} fusion(bf16[8,32,1280]{2,1,0:T(8,128)(2,1)} %all-to-all-done, bf16[8,128,64]{1,2,0:T(8,128)(2,1)S(1)} %get-tuple-element.8), kind=kOutput, calls=%fused_computation.7 | convolution fusion | flops 83886080 | bytes 1376256 | tf_op jit(solution)/shard_map/dot_general | solution.py:131
  68.4 7.8 %collective-permute-done.17 = bf16[8,32,1280]{2,1,0:T(8,128)(2,1)S(1)} collective-permute-done((bf16[8,32,1280]{2,1,0:T(8,128)(2,1)}, bf16[8,32,1280]{2,1,0:T(8,128)(2,1)S(1)}, u32[]{:S(2)}, u32[]{:S(2)}) %collective-permute-start.17) | collective-permute-done | bytes 655392 | tf_op jit(solution)/shard_map/ppermute | solution.py:12
  76.7 9.9 %fusion.1 = f32[128,1280]{1,0:T(8,128)S(1)} fusion(f32[128,1280]{1,0:T(8,128)S(1)} %convolution_bitcast_fusion.1, f32[128,1280]{1,0:T(8,128)S(1)} %convolution_bitcast_fusion.2, f32[128,1280]{1,0:T(8,128)S(1)} %convolution_bitcast_fusion.3, bf16[128,8192]{1,0:T(8,128)(2,1)S(1)} %constant_dynamic-update-slice_fusion.8, bf16[8192,1280]{1,0:T(8,128)(2,1)} %param.8), kind=kOutput, calls=%fused_computation.2 | convolution fusion | flops 2684846080 | bytes 25690112 | tf_op jit(solution)/shard_map/dot_general | solution.py:128
  86.7 1.0 %fusion.4 = bf16[1,128,1280]{2,1,0:T(8,128)(2,1)} fusion(f32[128,1280]{1,0:T(8,128)S(1)} %fusion.1, bf16[8,32,1280]{2,1,0:T(8,128)(2,1)S(1)} %collective-permute-done.18, bf16[8,128,64]{1,2,0:T(8,128)(2,1)S(1)} %get-tuple-element.7), kind=kOutput, calls=%fused_computation.9 | convolution fusion | flops 84213760 | bytes 1703936 | tf_op jit(solution)/shard_map/dot_general | solution.py:131
  (74 shorter events, 8.6 us)
Async XLA Ops:
  0.0 12.9 %collective-permute-start = (bf16[16,8192]{1,0:T(8,128)(2,1)}, bf16[16,8192]{1,0:T(8,128)(2,1)}, u32[]{:S(2)}, u32[]{:S(2)}) collective-permute-start(bf16[16,8192]{1,0:T(8,128)(2,1)} %bitcast.67), channel_id=1, source_target_pairs={{0,2},{2,4},{4,6},{6,7},{7,5},{5,3},{3,1},{1,0},{8,10},{10,12},{12... | collective-permute-start | bytes 786440 | tf_op jit(solution)/shard_map/ppermute | solution.py:38
  3.0 11.9 %collective-permute-start.1 = (bf16[16,8192]{1,0:T(8,128)(2,1)}, bf16[16,8192]{1,0:T(8,128)(2,1)}, u32[]{:S(2)}, u32[]{:S(2)}) collective-permute-start(bf16[16,8192]{1,0:T(8,128)(2,1)} %bitcast.68), channel_id=1, source_target_pairs={{2,0},{4,2},{6,4},{7,6},{5,7},{3,5},{1,3},{0,1},{10,8},{12,10},{14... | collective-permute-start | bytes 786440 | tf_op jit(solution)/shard_map/ppermute | solution.py:39
  3.0 43.8 %collective-permute-start.8 = (bf16[64,8192]{1,0:T(8,128)(2,1)}, bf16[64,8192]{1,0:T(8,128)(2,1)}, u32[]{:S(2)}, u32[]{:S(2)}) collective-permute-start(bf16[64,8192]{1,0:T(8,128)(2,1)} %bitcast.66), channel_id=1, source_target_pairs={{8,0},{0,8},{9,1},{1,9},{10,2},{2,10},{11,3},{3,11},{12,4},{4,12},... | collective-permute-start | bytes 3145736 | tf_op jit(solution)/shard_map/ppermute | solution.py:12
  3.1 7.5 %copy-start.7 = (s32[1,12]{1,0:T(1,128)S(1)}, s32[1,12]{1,0:T(1,128)}, u32[]{:S(2)}) copy-start(s32[1,12]{1,0:T(1,128)} %param.12) | copy-start | bytes 148
  4.2 7.8 %copy-start.6 = (s32[2,12]{1,0:T(2,128)S(1)}, s32[2,12]{1,0:T(2,128)}, u32[]{:S(2)}) copy-start(s32[2,12]{1,0:T(2,128)} %param.11) | copy-start | bytes 292
  4.2 7.8 %copy-start.8 = (s32[16]{0:T(128)S(1)}, s32[16]{0:T(128)}, u32[]{:S(2)}) copy-start(s32[16]{0:T(128)} %param.13) | copy-start | bytes 196
  4.2 58.7 %all-to-all-start = ((bf16[8,32,1280]{2,1,0:T(8,128)(2,1)}), bf16[8,32,1280]{2,1,0:T(8,128)(2,1)}, u32[]{:S(2)}, u32[]{:S(2)}) async-start(bf16[8,32,1280]{2,1,0:T(8,128)(2,1)} %bitcast.63), calls=%async_computation | async-start | bytes 1310720 | tf_op jit(solution)/shard_map/all_to_all | solution.py:89
  12.3 32.8 %copy-start.2 = (s32[128]{0:T(128)}, s32[128]{0:T(128)S(1)}, u32[]{:S(2)}) copy-start(s32[128]{0:T(128)S(1)} %select_reduce_fusion) | copy-start | bytes 1540
  12.9 15.3 %collective-permute-start.2 = (bf16[16,8192]{1,0:T(8,128)(2,1)}, bf16[16,8192]{1,0:T(8,128)(2,1)S(1)}, u32[]{:S(2)}, u32[]{:S(2)}) collective-permute-start(bf16[16,8192]{1,0:T(8,128)(2,1)} %collective-permute-done), channel_id=1, source_target_pairs={{0,2},{2,4},{4,6},{6,7},{7,5},{5,3},{3,1},{1,0},{8,10},{10,12},{12... | collective-permute-start | bytes 786440 | tf_op jit(solution)/shard_map/ppermute | solution.py:38
  15.0 18.1 %collective-permute-start.3 = (bf16[16,8192]{1,0:T(8,128)(2,1)}, bf16[16,8192]{1,0:T(8,128)(2,1)S(1)}, u32[]{:S(2)}, u32[]{:S(2)}) collective-permute-start(bf16[16,8192]{1,0:T(8,128)(2,1)} %collective-permute-done.1), channel_id=1, source_target_pairs={{2,0},{4,2},{6,4},{7,6},{5,7},{3,5},{1,3},{0,1},{10,8},{12,10},{14... | collective-permute-start | bytes 786440 | tf_op jit(solution)/shard_map/ppermute | solution.py:39
  28.2 10.7 %collective-permute-start.4 = (bf16[16,8192]{1,0:T(8,128)(2,1)S(1)}, bf16[16,8192]{1,0:T(8,128)(2,1)S(1)}, u32[]{:S(2)}, u32[]{:S(2)}) collective-permute-start(bf16[16,8192]{1,0:T(8,128)(2,1)S(1)} %collective-permute-done.2), channel_id=1, source_target_pairs={{0,2},{2,4},{4,6},{6,7},{7,5},{5,3},{3,1},{1,0},{8,10},{10,12},{12... | collective-permute-start | bytes 786440 | tf_op jit(solution)/shard_map/ppermute | solution.py:38
  33.1 8.6 %collective-permute-start.5 = (bf16[16,8192]{1,0:T(8,128)(2,1)S(1)}, bf16[16,8192]{1,0:T(8,128)(2,1)S(1)}, u32[]{:S(2)}, u32[]{:S(2)}) collective-permute-start(bf16[16,8192]{1,0:T(8,128)(2,1)S(1)} %collective-permute-done.3), channel_id=1, source_target_pairs={{2,0},{4,2},{6,4},{7,6},{5,7},{3,5},{1,3},{0,1},{10,8},{12,10},{14... | collective-permute-start | bytes 786440 | tf_op jit(solution)/shard_map/ppermute | solution.py:39
  38.9 6.2 %collective-permute-start.6 = (bf16[16,4096]{1,0:T(8,128)(2,1)S(1)}, bf16[16,4096]{1,0:T(8,128)(2,1)S(1)}, u32[]{:S(2)}, u32[]{:S(2)}) collective-permute-start(bf16[16,4096]{1,0:T(8,128)(2,1)S(1)} %slice.24), channel_id=1, source_target_pairs={{0,2},{2,4},{4,6},{6,7},{7,5},{5,3},{3,1},{1,0},{8,10},{10,12},{12... | collective-permute-start | bytes 393224 | tf_op jit(solution)/shard_map/ppermute | solution.py:43
  41.7 5.1 %collective-permute-start.7 = (bf16[16,4096]{1,0:T(8,128)(2,1)S(1)}, bf16[16,4096]{1,0:T(8,128)(2,1)S(1)}, u32[]{:S(2)}, u32[]{:S(2)}) collective-permute-start(bf16[16,4096]{1,0:T(8,128)(2,1)S(1)} %slice.25), channel_id=1, source_target_pairs={{2,0},{4,2},{6,4},{7,6},{5,7},{3,5},{1,3},{0,1},{10,8},{12,10},{14... | collective-permute-start | bytes 393224 | tf_op jit(solution)/shard_map/ppermute | solution.py:44
  49.9 8.2 %collective-permute-start.9 = (bf16[128,64]{0,1:T(8,128)(2,1)S(1)}, bf16[128,64]{0,1:T(8,128)(2,1)}, u32[]{:S(2)}, u32[]{:S(2)}) collective-permute-start(bf16[128,64]{0,1:T(8,128)(2,1)S(1)} %get-tuple-element.6), channel_id=1, source_target_pairs={{0,1},{1,2},{2,3},{3,4},{4,5},{5,6},{6,7},{7,0},{8,9},{9,10},{10,1... | collective-permute-start | bytes 49160 | tf_op jit(solution)/shard_map/ppermute | solution.py:53
  51.0 10.7 %collective-permute-start.10 = (bf16[128,64]{0,1:T(8,128)(2,1)S(1)}, bf16[128,64]{0,1:T(8,128)(2,1)S(1)}, u32[]{:S(2)}, u32[]{:S(2)}) collective-permute-start(bf16[128,64]{0,1:T(8,128)(2,1)S(1)} %get-tuple-element.6), channel_id=1, source_target_pairs={{0,2},{1,3},{2,4},{3,5},{4,6},{5,7},{6,0},{7,1},{8,10},{9,11},{10,... | collective-permute-start | bytes 49160 | tf_op jit(solution)/shard_map/ppermute | solution.py:53
  53.0 9.7 %collective-permute-start.11 = (bf16[128,64]{0,1:T(8,128)(2,1)S(1)}, bf16[128,64]{0,1:T(8,128)(2,1)S(1)}, u32[]{:S(2)}, u32[]{:S(2)}) collective-permute-start(bf16[128,64]{0,1:T(8,128)(2,1)S(1)} %get-tuple-element.6), channel_id=1, source_target_pairs={{0,3},{1,4},{2,5},{3,6},{4,7},{5,0},{6,1},{7,2},{8,11},{9,12},{10,... | collective-permute-start | bytes 49160 | tf_op jit(solution)/shard_map/ppermute | solution.py:53
  54.3 8.5 %collective-permute-start.12 = (bf16[128,64]{0,1:T(8,128)(2,1)S(1)}, bf16[128,64]{0,1:T(8,128)(2,1)S(1)}, u32[]{:S(2)}, u32[]{:S(2)}) collective-permute-start(bf16[128,64]{0,1:T(8,128)(2,1)S(1)} %get-tuple-element.6), channel_id=1, source_target_pairs={{0,4},{1,5},{2,6},{3,7},{4,0},{5,1},{6,2},{7,3},{8,12},{9,13},{10,... | collective-permute-start | bytes 49160 | tf_op jit(solution)/shard_map/ppermute | solution.py:53
  57.9 4.9 %collective-permute-start.13 = (bf16[128,64]{0,1:T(8,128)(2,1)S(1)}, bf16[128,64]{0,1:T(8,128)(2,1)S(1)}, u32[]{:S(2)}, u32[]{:S(2)}) collective-permute-start(bf16[128,64]{0,1:T(8,128)(2,1)S(1)} %get-tuple-element.6), channel_id=1, source_target_pairs={{0,5},{1,6},{2,7},{3,0},{4,1},{5,2},{6,3},{7,4},{8,13},{9,14},{10,... | collective-permute-start | bytes 49160 | tf_op jit(solution)/shard_map/ppermute | solution.py:53
  58.1 6.4 %collective-permute-start.14 = (bf16[128,64]{0,1:T(8,128)(2,1)S(1)}, bf16[128,64]{0,1:T(8,128)(2,1)}, u32[]{:S(2)}, u32[]{:S(2)}) collective-permute-start(bf16[128,64]{0,1:T(8,128)(2,1)S(1)} %get-tuple-element.6), channel_id=1, source_target_pairs={{0,6},{1,7},{2,0},{3,1},{4,2},{5,3},{6,4},{7,5},{8,14},{9,15},{10,... | collective-permute-start | bytes 49160 | tf_op jit(solution)/shard_map/ppermute | solution.py:53
  61.7 3.8 %collective-permute-start.15 = (bf16[128,64]{0,1:T(8,128)(2,1)S(1)}, bf16[128,64]{0,1:T(8,128)(2,1)}, u32[]{:S(2)}, u32[]{:S(2)}) collective-permute-start(bf16[128,64]{0,1:T(8,128)(2,1)S(1)} %get-tuple-element.6), channel_id=1, source_target_pairs={{0,7},{1,0},{2,1},{3,2},{4,3},{5,4},{6,5},{7,6},{8,15},{9,8},{10,9... | collective-permute-start | bytes 49160 | tf_op jit(solution)/shard_map/ppermute | solution.py:53
  62.8 13.3 %collective-permute-start.17 = (bf16[8,32,1280]{2,1,0:T(8,128)(2,1)}, bf16[8,32,1280]{2,1,0:T(8,128)(2,1)S(1)}, u32[]{:S(2)}, u32[]{:S(2)}) collective-permute-start(bf16[8,32,1280]{2,1,0:T(8,128)(2,1)} %all-to-all-done), channel_id=1, source_target_pairs={{16,0},{0,16},{17,1},{1,17},{18,2},{2,18},{19,3},{3,19},{20,4},{4,... | collective-permute-start | bytes 1966088 | tf_op jit(solution)/shard_map/ppermute | solution.py:12
  65.1 11.3 %collective-permute-start.16 = (bf16[8,32,1280]{2,1,0:T(8,128)(2,1)}, bf16[8,32,1280]{2,1,0:T(8,128)(2,1)S(1)}, u32[]{:S(2)}, u32[]{:S(2)}) collective-permute-start(bf16[8,32,1280]{2,1,0:T(8,128)(2,1)} %all-to-all-done), channel_id=1, source_target_pairs={{8,0},{0,8},{9,1},{1,9},{10,2},{2,10},{11,3},{3,11},{12,4},{4,12},... | collective-permute-start | bytes 1966088 | tf_op jit(solution)/shard_map/ppermute | solution.py:12
  76.2 10.5 %collective-permute-start.18 = (bf16[8,32,1280]{2,1,0:T(8,128)(2,1)S(1)}, bf16[8,32,1280]{2,1,0:T(8,128)(2,1)S(1)}, u32[]{:S(2)}, u32[]{:S(2)}) collective-permute-start(bf16[8,32,1280]{2,1,0:T(8,128)(2,1)S(1)} %collective-permute-done.17), channel_id=1, source_target_pairs={{8,0},{0,8},{9,1},{1,9},{10,2},{2,10},{11,3},{3,11},{12,4},{4,12},... | collective-permute-start | bytes 1966088 | tf_op jit(solution)/shard_map/ppermute | solution.py:12
  (5 other events, 14.1 us)

commit v3 on v2

--- a/solution.py
+++ b/solution.py
@@ -1,6 +1,10 @@
+import functools
+
 import jax
 import jax.numpy as jnp
 from jax import lax
+from jax.experimental import pallas as pl
+from jax.experimental.pallas import tpu as pltpu
 from jax.sharding import PartitionSpec as P
 
 adapter_scale = 1.0
@@ -34,27 +38,55 @@
 
     out = put(out, block, 0, 0)
     ahead = behind = block
+    first = None
     for step in range(1, n // 2):
         ahead = lax.ppermute(ahead, axis, up)
         behind = lax.ppermute(behind, axis, down)
+        if first is None:
+            first = (ahead, behind)
         out = put(out, ahead, step, 0)
         out = put(out, behind, -step, 0)
     half = width // 2
     out = put(out, lax.ppermute(ahead[:, :half], axis, up), n // 2, 0)
     out = put(out, lax.ppermute(behind[:, half:], axis, down), n // 2, half)
-    return out
+    return out, first
 
 
-def direct_gather(block, axis):
+def sum_over(x, axis):
     n = lax.axis_size(axis)
-    me = lax.axis_index(axis)
-    out = jnp.zeros((n, *block.shape), block.dtype)
-    for shift in range(n):
-        part = block if shift == 0 else lax.ppermute(
-            block, axis, [(i, (i + shift) % n) for i in range(n)]
-        )
-        out = lax.dynamic_update_index_in_dim(out, part, lax.rem(me - shift + n, n), 0)
-    return out
+    if n & (n - 1):
+        return lax.psum(x, axis)
+    shift = 1
+    while shift < n:
+        x = x + lax.ppermute(x, axis, [(i, i ^ shift) for i in range(n)])
+        shift *= 2
+    return x
+
+
+def lift_kernel(reps, groups, pieces, at_ref, slot_ref, low_ref, *refs):
+    ups, bases, out_ref = refs[: reps * groups], refs[reps * groups : -1], refs[-1]
+    depth = ups[0].shape[0]
+    rank = low_ref.shape[1]
+    rank_portion = rank // reps
+    low = low_ref[...]
+    token_slot = slot_ref[...]
+    row = lax.broadcasted_iota(jnp.int32, (rank, depth), 0)
+    column = lax.broadcasted_iota(jnp.int32, (rank, depth), 1)
+    lane = lax.broadcasted_iota(jnp.int32, (low.shape[0], depth), 1)
+    expanded = []
+    for r in range(reps):
+        spread = (row == at_ref[r] + lax.rem(column, rank_portion)).astype(jnp.bfloat16)
+        wide = jnp.dot(low, spread, preferred_element_type=jnp.float32)
+        for s in range(groups):
+            chosen = token_slot == at_ref[reps + s] + lane // rank_portion
+            expanded.append(jnp.where(chosen, wide, 0.0).astype(jnp.bfloat16))
+    for (start, size), base in zip(pieces, bases):
+        total = base[...]
+        for part, panel in zip(expanded, ups):
+            total = total + adapter_scale * jnp.dot(
+                part, panel[:, start : start + size], preferred_element_type=jnp.float32
+            )
+        out_ref[:, start : start + size] = total.astype(out_ref.dtype)
 
 
 def on_device(
@@ -78,7 +110,7 @@
     store_size = adapter_store_slot.shape[0]
     tok_all = tokens.shape[1] * tp
 
-    gathered = ring_gather(tokens[0], "tp")
+    gathered, first = ring_gather(tokens[0], "tp")
 
     downs = swapped(jnp.transpose(adapter_down_panels[0]), "grp")
 
@@ -86,6 +118,7 @@
         adapter_up_panels[0], my_rep * rank_portion, rank_portion, axis=0
     )
     up_send = jnp.transpose(up_mine.reshape(rank_portion, tp, columns), (1, 0, 2))
+    up_send = lax.optimization_barrier((up_send, *first))[0]
     up_got = lax.all_to_all(up_send, "tp", split_axis=0, concat_axis=0, tiled=True)
     ups = [swapped(part, "grp") for part in swapped(up_got, "rep")]
 
@@ -111,30 +144,35 @@
         )
         for s, down in enumerate(downs)
     ).astype(jnp.bfloat16)
-    low = lax.dynamic_slice_in_dim(
-        jnp.concatenate([low, low], axis=1), my_rep * rank_portion, rank, axis=1
-    )
-    low_all = direct_gather(low, "tp")
-    owners = jnp.arange(tp, dtype=jnp.int32)
-    expanded = [
-        jnp.where(
-            (token_slot[None, :] == (((my_group + s) % groups) * tp + owners)[:, None])[:, :, None],
-            low_all,
-            jnp.zeros_like(low_all),
+    low = sum_over(low, "tp")
+
+    pieces = [(a, min(512, columns - a)) for a in range(0, columns, 512)]
+    bases = [
+        jnp.dot(
+            gathered, base_projection_weight[:, a : a + n], preferred_element_type=jnp.float32
         )
-        for s in range(groups)
+        for a, n in pieces
     ]
-
-    total = jnp.dot(gathered, base_projection_weight, preferred_element_type=jnp.float32)
-    for r in range(reps):
-        for s in range(groups):
-            total = total + adapter_scale * lax.dot_general(
-                expanded[s][:, :, r * rank_portion : (r + 1) * rank_portion],
-                ups[r][s],
-                (((0, 2), (0, 1)), ((), ())),
-                preferred_element_type=jnp.float32,
-            )
-    return total.astype(jnp.bfloat16)[None]
+    at = jnp.stack(
+        [lax.rem(my_rep + r, reps) * rank_portion for r in range(reps)]
+        + [lax.rem(my_group + s, groups) * tp for s in range(groups)]
+    ).astype(jnp.int32)
+    panels = [part.reshape(tp * rank_portion, columns) for row in ups for part in row]
+    in_vmem = pl.BlockSpec(memory_space=pltpu.VMEM)
+    out = pl.pallas_call(
+        functools.partial(lift_kernel, reps, groups, pieces),
+        out_shape=jax.ShapeDtypeStruct((tok_all, columns), jnp.bfloat16),
+        in_specs=[pl.BlockSpec(memory_space=pltpu.SMEM)]
+        + [in_vmem] * (2 + len(panels) + len(bases)),
+        out_specs=in_vmem,
+        cost_estimate=pl.CostEstimate(
+            flops=2 * tok_all * columns * rank * groups * tp,
+            bytes_accessed=2 * rank * groups * tp * columns + 6 * tok_all * columns,
+            transcendentals=0,
+        ),
+        name="lift",
+    )(at, token_slot[:, None], low, *panels, *bases)
+    return out[None]
 
 
 def solution(mesh):

time: 88.3 us -> 90.3 us (1.023)
  starting transfers between devices: 32.6 us -> 24.8 us
  local copies, waits for them, and re-layouts: 6.65 us -> 10.5 us
  Pallas kernels: 0 us -> 3.24 us
  matrix products: 15.7 us -> 17.1 us
  waiting for transfers between devices: 29.9 us -> 30.9 us
    ppermute x7 -> x3, starting transfers between devices: 11.5 us -> 4.86 us  [sum_over(): x = x + lax.ppermute(x, axis, [(i, i ^ shift) for i in range(n)])]
    unnamed x19 -> x17, local copies, waits for them, and re-layouts: 0.15 us -> 4.48 us
    pallas_call x0 -> x1, Pallas kernels: none -> 3.24 us  [on_device(): pl.pallas_call(functools.partial(lift_kernel, reps, groups, pieces), out_...]
    ppermute x3, waiting for transfers between devices: 16.9 us -> 19.3 us  [ring_gather(): ahead = lax.ppermute(ahead, axis, up)]
    dynamic_update_slice x7 -> x0, local copies, waits for them, and re-layouts: 2.22 us -> none  [direct_gather(): lax.dynamic_update_index_in_dim(out, part, lax.rem(me - shift + n, n), 0)]
    optimization_barrier x0 -> x1, local copies, waits for them, and re-layouts: none -> 2.03 us  [on_device(): up_send = lax.optimization_barrier((up_send, *first))[0]]
    ppermute x4, waiting for transfers between devices: 7.84 us -> 5.93 us  [swapped(): lax.ppermute(x, axis, [((i + s) % n, i) for i in range(n)])]
    dot_general x5 -> x3, matrix products: 12.8 us -> 14.5 us  [on_device(): jnp.dot(gathered, base_projection_weight[:, a:a + n], preferred_element_t...]
  transfers between devices with their start and end apart: 20 -> 16, of which waited for: 7 -> 7; matrix products, arithmetic and copies ran while one was open for 27% -> 31% of each run, Pallas kernels for 0% -> 0%
where the time goes in v3:
time: 90.3 us; the launch traced here: 89.8 us
  waiting for transfers between devices  30.9 us (34%)
  starting transfers between devices  24.8 us (27%)
  matrix products  17.1 us (19%)
  local copies, waits for them, and re-layouts  10.5 us (12%)
  Pallas kernels  3.24 us (4%)
  other arithmetic  3.06 us (3%)
    ppermute x3, waiting for transfers between devices, ring_gather(): ahead = lax.ppermute(ahead, axis, up)  19.3 us
    dot_general x3, matrix products, on_device(): jnp.dot(gathered, base_projection_weight[:, a:a + n], preferred_element_t...  14.5 us
    ppermute x3, starting transfers between devices, ring_gather(): ahead = lax.ppermute(ahead, axis, up)  9.98 us
    ppermute x4, waiting for transfers between devices, swapped(): lax.ppermute(x, axis, [((i + s) % n, i) for i in range(n)])  5.93 us
    all_to_all x1, starting transfers between devices, on_device(): lax.all_to_all(up_send, 'tp', split_axis=0, concat_axis=0, tiled=True)  5.34 us
    ppermute x3, starting transfers between devices, sum_over(): x = x + lax.ppermute(x, axis, [(i, i ^ shift) for i in range(n)])  4.86 us
    unnamed x17, local copies, waits for them, and re-layouts  4.48 us
    pallas_call x1, Pallas kernels, on_device(): pl.pallas_call(functools.partial(lift_kernel, reps, groups, pieces), out_...  3.24 us
  transfers between devices with their start and end apart: 16, of which 7 were waited for; matrix products, arithmetic and copies ran while one was open for 31% of the time, Pallas kernels for 0%

profile of v3, /device:TPU:0, one launch (start us, length us, event | category | flops | bytes accessed | tf_op | source)
XLA Modules:
  0.0 89.8 jit_solution(12877772308491807200)
XLA Ops:
  0.0 3.1 %collective-permute-start = (bf16[16,8192]{1,0:T(8,128)(2,1)}, bf16[16,8192]{1,0:T(8,128)(2,1)}, u32[]{:S(2)}, u32[]{:S(2)}) collective-permute-start(bf16[16,8192]{1,0:T(8,128)(2,1)} %bitcast.44), channel_id=1, source_target_pairs={{0,2},{2,4},{4,6},{6,7},{7,5},{5,3},{3,1},{1,0},{8,10},{10,12},{12... | collective-permute-start | bytes 786440 | tf_op jit(solution)/shard_map/ppermute | solution.py:43
  5.8 0.9 %constant_dynamic-slice_fusion = bf16[1,32,10240]{2,1,0:T(8,128)(2,1)} fusion(bf16[1,64,10240]{2,1,0:T(8,128)(2,1)S(1)} %copy-done, s32[]{:T(128)S(6)} %select_n.121), kind=kLoop, calls=%fused_computation.17 | loop fusion | bytes 1310724 | tf_op jit(solution)/shard_map/dynamic_slice | solution.py:117
  7.5 2.0 %copy.28 = bf16[4,8,8,1280]{3,2,1,0:T(8,128)(2,1)} copy(bf16[4,8,8,1280]{3,1,2,0:T(8,128)(2,1)} %bitcast.38) | data formatting | bytes 1310720
  10.2 0.9 %collective-permute-done.1 = bf16[16,8192]{1,0:T(8,128)(2,1)} collective-permute-done((bf16[16,8192]{1,0:T(8,128)(2,1)}, bf16[16,8192]{1,0:T(8,128)(2,1)}, u32[]{:S(2)}, u32[]{:S(2)}) %collective-permute-start.1) | collective-permute-done | bytes 262176 | tf_op jit(solution)/shard_map/ppermute | solution.py:44
  11.2 2.0 %copy.24 = bf16[8,32,1280]{2,1,0:T(8,128)(2,1)} copy(bf16[8,32,1280]{2,0,1:T(8,128)(2,1)} %bitcast.39) | data formatting | bytes 1310720 | tf_op jit(solution)/shard_map/optimization_barrier | solution.py:121
  13.2 5.3 %all-to-all-start = ((bf16[8,32,1280]{2,1,0:T(8,128)(2,1)}), bf16[8,32,1280]{2,1,0:T(8,128)(2,1)}, u32[]{:S(2)}, u32[]{:S(2)}) async-start(bf16[8,32,1280]{2,1,0:T(8,128)(2,1)} %copy.24), calls=%async_computation | async-start | bytes 1310720 | tf_op jit(solution)/shard_map/all_to_all | solution.py:122
  18.5 2.0 %collective-permute-start.2 = (bf16[16,8192]{1,0:T(8,128)(2,1)}, bf16[16,8192]{1,0:T(8,128)(2,1)S(1)}, u32[]{:S(2)}, u32[]{:S(2)}) collective-permute-start(bf16[16,8192]{1,0:T(8,128)(2,1)} %collective-permute-done), channel_id=1, source_target_pairs={{0,2},{2,4},{4,6},{6,7},{7,5},{5,3},{3,1},{1,0},{8,10},{10,12},{12... | collective-permute-start | bytes 786440 | tf_op jit(solution)/shard_map/ppermute | solution.py:43
  20.6 1.0 %constant_dynamic-update-slice_fusion.6 = bf16[128,8192]{1,0:T(8,128)(2,1)S(1)} fusion(bf16[128,8192]{1,0:T(8,128)(2,1)S(1)} %constant_dynamic-update-slice_fusion.7, bf16[16,8192]{1,0:T(8,128)(2,1)} %collective-permute-done, s32[]{:T(128)S(6)} %select_n.105), kind=kLoop, calls=%fused_computation.24 | loop fusion | bytes 524292 | tf_op jit(solution)/shard_map/dynamic_update_slice | solution.py:37
  21.6 1.0 %constant_dynamic-update-slice_fusion.5 = bf16[128,8192]{1,0:T(8,128)(2,1)S(1)} fusion(bf16[128,8192]{1,0:T(8,128)(2,1)S(1)} %constant_dynamic-update-slice_fusion.6, bf16[16,8192]{1,0:T(8,128)(2,1)} %collective-permute-done.1, s32[]{:T(128)S(6)} %select_n.107), kind=kLoop, calls=%fused_computation.23 | loop fusion | bytes 524292 | tf_op jit(solution)/shard_map/dynamic_update_slice | solution.py:37
  22.5 13.6 %collective-permute-done.2 = bf16[16,8192]{1,0:T(8,128)(2,1)S(1)} collective-permute-done((bf16[16,8192]{1,0:T(8,128)(2,1)}, bf16[16,8192]{1,0:T(8,128)(2,1)S(1)}, u32[]{:S(2)}, u32[]{:S(2)}) %collective-permute-start.2) | collective-permute-done | bytes 262176 | tf_op jit(solution)/shard_map/ppermute | solution.py:43
  36.1 4.9 %collective-permute-start.4 = (bf16[16,8192]{1,0:T(8,128)(2,1)S(1)}, bf16[16,8192]{1,0:T(8,128)(2,1)S(1)}, u32[]{:S(2)}, u32[]{:S(2)}) collective-permute-start(bf16[16,8192]{1,0:T(8,128)(2,1)S(1)} %collective-permute-done.2), channel_id=1, source_target_pairs={{0,2},{2,4},{4,6},{6,7},{7,5},{5,3},{3,1},{1,0},{8,10},{10,12},{12... | collective-permute-start | bytes 786440 | tf_op jit(solution)/shard_map/ppermute | solution.py:43
  41.1 5.7 %collective-permute-done.4 = bf16[16,8192]{1,0:T(8,128)(2,1)S(1)} collective-permute-done((bf16[16,8192]{1,0:T(8,128)(2,1)S(1)}, bf16[16,8192]{1,0:T(8,128)(2,1)S(1)}, u32[]{:S(2)}, u32[]{:S(2)}) %collective-permute-start.4) | collective-permute-done | bytes 262176 | tf_op jit(solution)/shard_map/ppermute | solution.py:43
  46.8 2.5 %collective-permute-start.6 = (bf16[16,4096]{1,0:T(8,128)(2,1)S(1)}, bf16[16,4096]{1,0:T(8,128)(2,1)S(1)}, u32[]{:S(2)}, u32[]{:S(2)}) collective-permute-start(bf16[16,4096]{1,0:T(8,128)(2,1)S(1)} %slice.20), channel_id=1, source_target_pairs={{0,2},{2,4},{4,6},{6,7},{7,5},{5,3},{3,1},{1,0},{8,10},{10,12},{12... | collective-permute-start | bytes 393224 | tf_op jit(solution)/shard_map/ppermute | solution.py:50
  50.3 2.8 %collective-permute-done.6 = bf16[16,4096]{1,0:T(8,128)(2,1)S(1)} collective-permute-done((bf16[16,4096]{1,0:T(8,128)(2,1)S(1)}, bf16[16,4096]{1,0:T(8,128)(2,1)S(1)}, u32[]{:S(2)}, u32[]{:S(2)}) %collective-permute-start.6) | collective-permute-done | bytes 131104 | tf_op jit(solution)/shard_map/ppermute | solution.py:50
  53.1 1.7 %collective-permute-done.7 = bf16[16,4096]{1,0:T(8,128)(2,1)S(1)} collective-permute-done((bf16[16,4096]{1,0:T(8,128)(2,1)S(1)}, bf16[16,4096]{1,0:T(8,128)(2,1)S(1)}, u32[]{:S(2)}, u32[]{:S(2)}) %collective-permute-start.7) | collective-permute-done | bytes 131104 | tf_op jit(solution)/shard_map/ppermute | solution.py:51
  54.8 1.9 %convolution_select_fusion = f32[128,64]{1,0:T(8,128)S(1)} fusion(bf16[128,8192]{1,0:T(8,128)(2,1)S(1)} %constant_dynamic-update-slice_fusion.8, bf16[64,8192]{1,0:T(8,128)(2,1)} %collective-permute-done.8, pred[128]{0:T(512)(128)(4,1)S(1)} %get-tuple-element.8), kind=kOutput, calls=%fused_computation.6 | convolution fusion | flops 134225920 | bytes 3178624 | tf_op jit(solution)/shard_map/dot_general | solution.py:140
  57.9 1.5 %collective-permute-start.13 = (bf16[8,32,1280]{2,1,0:T(8,128)(2,1)}, bf16[8,32,1280]{2,1,0:T(8,128)(2,1)S(1)}, u32[]{:S(2)}, u32[]{:S(2)}) collective-permute-start(bf16[8,32,1280]{2,1,0:T(8,128)(2,1)} %all-to-all-done), channel_id=1, source_target_pairs={{16,0},{0,16},{17,1},{1,17},{18,2},{2,18},{19,3},{3,19},{20,4},{4,... | collective-permute-start | bytes 1966088 | tf_op jit(solution)/shard_map/ppermute | solution.py:16
  59.4 5.3 %fusion.refs_5_ = f32[128,512]{1,0:T(8,128)} fusion(bf16[128,8192]{1,0:T(8,128)(2,1)S(1)} %constant_dynamic-update-slice_fusion.8, bf16[8192,1280]{1,0:T(8,128)(2,1)} %param.8), kind=kOutput, calls=%fused_computation | convolution fusion | flops 1073741824 | bytes 10747904 | tf_op jit(solution)/shard_map/dot_general | solution.py:151
  64.8 2.1 %collective-permute-start.10 = (bf16[128,64]{1,0:T(8,128)(2,1)S(1)}, bf16[128,64]{1,0:T(8,128)(2,1)S(1)}, u32[]{:S(2)}, u32[]{:S(2)}) collective-permute-start(bf16[128,64]{1,0:T(8,128)(2,1)S(1)} %add.172), channel_id=1, source_target_pairs={{0,2},{1,3},{2,0},{3,1},{4,6},{5,7},{6,4},{7,5},{8,10},{9,11},{10,... | collective-permute-start | bytes 49160 | tf_op jit(solution)/shard_map/ppermute | solution.py:61
  66.8 5.9 %collective-permute-done.13 = bf16[8,32,1280]{2,1,0:T(8,128)(2,1)S(1)} collective-permute-done((bf16[8,32,1280]{2,1,0:T(8,128)(2,1)}, bf16[8,32,1280]{2,1,0:T(8,128)(2,1)S(1)}, u32[]{:S(2)}, u32[]{:S(2)}) %collective-permute-start.13) | collective-permute-done | bytes 655392 | tf_op jit(solution)/shard_map/ppermute | solution.py:16
  72.8 5.6 %fusion.2.refs_4_ = f32[128,512]{1,0:T(8,128)} fusion(bf16[128,8192]{1,0:T(8,128)(2,1)S(1)} %constant_dynamic-update-slice_fusion.8, bf16[8192,1280]{1,0:T(8,128)(2,1)} %param.8), kind=kOutput, calls=%fused_computation.2 | convolution fusion | flops 1073741824 | bytes 10747904 | tf_op jit(solution)/shard_map/dot_general | solution.py:151
  78.4 2.3 %collective-permute-start.11 = (bf16[128,64]{1,0:T(8,128)(2,1)S(1)}, bf16[128,64]{1,0:T(8,128)(2,1)S(1)}, u32[]{:S(2)}, u32[]{:S(2)}) collective-permute-start(bf16[128,64]{1,0:T(8,128)(2,1)S(1)} %add.173), channel_id=1, source_target_pairs={{0,4},{1,5},{2,6},{3,7},{4,0},{5,1},{6,2},{7,3},{8,12},{9,13},{10,... | collective-permute-start | bytes 49160 | tf_op jit(solution)/shard_map/ppermute | solution.py:61
  80.7 3.6 %fusion.4.refs_6_ = f32[128,256]{1,0:T(8,128)} fusion(bf16[128,8192]{1,0:T(8,128)(2,1)S(1)} %constant_dynamic-update-slice_fusion.8, bf16[8192,1280]{1,0:T(8,128)(2,1)} %param.8), kind=kOutput, calls=%fused_computation.4 | convolution fusion | flops 536870912 | bytes 6422528 | tf_op jit(solution)/shard_map/dot_general | solution.py:151
  86.5 3.2 %lift.1 = bf16[128,1280]{1,0:T(8,128)(2,1)} custom-call(s32[4]{0:T(128)} %pad_add_fusion.at_ref, s32[128,1]{1,0:T(8,128)} %copy.25.slot_ref, bf16[128,64]{1,0:T(8,128)(2,1)} %add.174.low_ref, bf16[256,1280]{1,0:T(8,128)(2,1)} %bitcast.14.refs_0_, bf16[256,1280]{1,0:T(8,128)(2,1)} %bitcast.42, bf16[256,1280]{1,0:T(8,128)(2,1)} %bitcast.41, ...), custom_call_target="tpu_custom_call" | custom-call | flops 335544320 | bytes 3604480 | tf_op jit(solution)/shard_map/lift/pallas_call | solution.py:162
  (56 shorter events, 8.7 us)
Async XLA Ops:
  0.0 5.8 %copy-start = (bf16[1,64,10240]{2,1,0:T(8,128)(2,1)S(1)}, bf16[1,64,10240]{2,1,0:T(8,128)(2,1)}, u32[]{:S(2)}) copy-start(bf16[1,64,10240]{2,1,0:T(8,128)(2,1)} %param.10) | copy-start | bytes 3932164
  0.0 5.6 %copy-start.6 = (s32[2,12]{1,0:T(2,128)S(1)}, s32[2,12]{1,0:T(2,128)}, u32[]{:S(2)}) copy-start(s32[2,12]{1,0:T(2,128)} %param.11) | copy-start | bytes 292
  0.0 5.6 %copy-start.7 = (s32[16]{0:T(128)S(1)}, s32[16]{0:T(128)}, u32[]{:S(2)}) copy-start(s32[16]{0:T(128)} %param.13) | copy-start | bytes 196
  0.0 10.2 %collective-permute-start = (bf16[16,8192]{1,0:T(8,128)(2,1)}, bf16[16,8192]{1,0:T(8,128)(2,1)}, u32[]{:S(2)}, u32[]{:S(2)}) collective-permute-start(bf16[16,8192]{1,0:T(8,128)(2,1)} %bitcast.44), channel_id=1, source_target_pairs={{0,2},{2,4},{4,6},{6,7},{7,5},{5,3},{3,1},{1,0},{8,10},{10,12},{12... | collective-permute-start | bytes 786440 | tf_op jit(solution)/shard_map/ppermute | solution.py:43
  3.1 8.1 %collective-permute-start.1 = (bf16[16,8192]{1,0:T(8,128)(2,1)}, bf16[16,8192]{1,0:T(8,128)(2,1)}, u32[]{:S(2)}, u32[]{:S(2)}) collective-permute-start(bf16[16,8192]{1,0:T(8,128)(2,1)} %bitcast.45), channel_id=1, source_target_pairs={{2,0},{4,2},{6,4},{7,6},{5,7},{3,5},{1,3},{0,1},{10,8},{12,10},{14... | collective-permute-start | bytes 786440 | tf_op jit(solution)/shard_map/ppermute | solution.py:44
  3.1 51.7 %collective-permute-start.8 = (bf16[64,8192]{1,0:T(8,128)(2,1)}, bf16[64,8192]{1,0:T(8,128)(2,1)}, u32[]{:S(2)}, u32[]{:S(2)}) collective-permute-start(bf16[64,8192]{1,0:T(8,128)(2,1)} %bitcast.40), channel_id=1, source_target_pairs={{8,0},{0,8},{9,1},{1,9},{10,2},{2,10},{11,3},{3,11},{12,4},{4,12},... | collective-permute-start | bytes 3145736 | tf_op jit(solution)/shard_map/ppermute | solution.py:16
  4.6 0.9 %copy-start.5 = (bf16[1,16,8192]{2,1,0:T(8,128)(2,1)S(1)}, bf16[1,16,8192]{2,1,0:T(8,128)(2,1)}, u32[]{:S(2)}) copy-start(bf16[1,16,8192]{2,1,0:T(8,128)(2,1)} %param.7) | copy-start | bytes 786436
  13.2 44.7 %all-to-all-start = ((bf16[8,32,1280]{2,1,0:T(8,128)(2,1)}), bf16[8,32,1280]{2,1,0:T(8,128)(2,1)}, u32[]{:S(2)}, u32[]{:S(2)}) async-start(bf16[8,32,1280]{2,1,0:T(8,128)(2,1)} %copy.24), calls=%async_computation | async-start | bytes 1310720 | tf_op jit(solution)/shard_map/all_to_all | solution.py:122
  18.5 17.6 %collective-permute-start.2 = (bf16[16,8192]{1,0:T(8,128)(2,1)}, bf16[16,8192]{1,0:T(8,128)(2,1)S(1)}, u32[]{:S(2)}, u32[]{:S(2)}) collective-permute-start(bf16[16,8192]{1,0:T(8,128)(2,1)} %collective-permute-done), channel_id=1, source_target_pairs={{0,2},{2,4},{4,6},{6,7},{7,5},{5,3},{3,1},{1,0},{8,10},{10,12},{12... | collective-permute-start | bytes 786440 | tf_op jit(solution)/shard_map/ppermute | solution.py:43
  20.6 20.5 %collective-permute-start.3 = (bf16[16,8192]{1,0:T(8,128)(2,1)}, bf16[16,8192]{1,0:T(8,128)(2,1)S(1)}, u32[]{:S(2)}, u32[]{:S(2)}) collective-permute-start(bf16[16,8192]{1,0:T(8,128)(2,1)} %collective-permute-done.1), channel_id=1, source_target_pairs={{2,0},{4,2},{6,4},{7,6},{5,7},{3,5},{1,3},{0,1},{10,8},{12,10},{14... | collective-permute-start | bytes 786440 | tf_op jit(solution)/shard_map/ppermute | solution.py:44
  36.1 10.7 %collective-permute-start.4 = (bf16[16,8192]{1,0:T(8,128)(2,1)S(1)}, bf16[16,8192]{1,0:T(8,128)(2,1)S(1)}, u32[]{:S(2)}, u32[]{:S(2)}) collective-permute-start(bf16[16,8192]{1,0:T(8,128)(2,1)S(1)} %collective-permute-done.2), channel_id=1, source_target_pairs={{0,2},{2,4},{4,6},{6,7},{7,5},{5,3},{3,1},{1,0},{8,10},{10,12},{12... | collective-permute-start | bytes 786440 | tf_op jit(solution)/shard_map/ppermute | solution.py:43
  41.0 8.6 %collective-permute-start.5 = (bf16[16,8192]{1,0:T(8,128)(2,1)S(1)}, bf16[16,8192]{1,0:T(8,128)(2,1)S(1)}, u32[]{:S(2)}, u32[]{:S(2)}) collective-permute-start(bf16[16,8192]{1,0:T(8,128)(2,1)S(1)} %collective-permute-done.3), channel_id=1, source_target_pairs={{2,0},{4,2},{6,4},{7,6},{5,7},{3,5},{1,3},{0,1},{10,8},{12,10},{14... | collective-permute-start | bytes 786440 | tf_op jit(solution)/shard_map/ppermute | solution.py:44
  46.8 6.2 %collective-permute-start.6 = (bf16[16,4096]{1,0:T(8,128)(2,1)S(1)}, bf16[16,4096]{1,0:T(8,128)(2,1)S(1)}, u32[]{:S(2)}, u32[]{:S(2)}) collective-permute-start(bf16[16,4096]{1,0:T(8,128)(2,1)S(1)} %slice.20), channel_id=1, source_target_pairs={{0,2},{2,4},{4,6},{6,7},{7,5},{5,3},{3,1},{1,0},{8,10},{10,12},{12... | collective-permute-start | bytes 393224 | tf_op jit(solution)/shard_map/ppermute | solution.py:50
  49.7 5.1 %collective-permute-start.7 = (bf16[16,4096]{1,0:T(8,128)(2,1)S(1)}, bf16[16,4096]{1,0:T(8,128)(2,1)S(1)}, u32[]{:S(2)}, u32[]{:S(2)}) collective-permute-start(bf16[16,4096]{1,0:T(8,128)(2,1)S(1)} %slice.21), channel_id=1, source_target_pairs={{2,0},{4,2},{6,4},{7,6},{5,7},{3,5},{1,3},{0,1},{10,8},{12,10},{14... | collective-permute-start | bytes 393224 | tf_op jit(solution)/shard_map/ppermute | solution.py:51
  50.2 6.5 %copy-start.1 = (bf16[1,8192,64]{1,2,0:T(8,128)(2,1)S(1)}, bf16[1,8192,64]{1,2,0:T(8,128)(2,1)}, u32[]{:S(2)}) copy-start(bf16[1,8192,64]{1,2,0:T(8,128)(2,1)} %param.9) | copy-start | bytes 3145732
  57.4 7.3 %collective-permute-start.9 = (bf16[128,64]{1,0:T(8,128)(2,1)S(1)}, bf16[128,64]{1,0:T(8,128)(2,1)S(1)}, u32[]{:S(2)}, u32[]{:S(2)}) collective-permute-start(bf16[128,64]{1,0:T(8,128)(2,1)S(1)} %fusion.7), channel_id=1, source_target_pairs={{0,1},{1,0},{2,3},{3,2},{4,5},{5,4},{6,7},{7,6},{8,9},{9,8},{10,11... | collective-permute-start | bytes 49160 | tf_op jit(solution)/shard_map/ppermute | solution.py:61
  57.9 14.9 %collective-permute-start.13 = (bf16[8,32,1280]{2,1,0:T(8,128)(2,1)}, bf16[8,32,1280]{2,1,0:T(8,128)(2,1)S(1)}, u32[]{:S(2)}, u32[]{:S(2)}) collective-permute-start(bf16[8,32,1280]{2,1,0:T(8,128)(2,1)} %all-to-all-done), channel_id=1, source_target_pairs={{16,0},{0,16},{17,1},{1,17},{18,2},{2,18},{19,3},{3,19},{20,4},{4,... | collective-permute-start | bytes 1966088 | tf_op jit(solution)/shard_map/ppermute | solution.py:16
  64.8 13.6 %collective-permute-start.10 = (bf16[128,64]{1,0:T(8,128)(2,1)S(1)}, bf16[128,64]{1,0:T(8,128)(2,1)S(1)}, u32[]{:S(2)}, u32[]{:S(2)}) collective-permute-start(bf16[128,64]{1,0:T(8,128)(2,1)S(1)} %add.172), channel_id=1, source_target_pairs={{0,2},{1,3},{2,0},{3,1},{4,6},{5,7},{6,4},{7,5},{8,10},{9,11},{10,... | collective-permute-start | bytes 49160 | tf_op jit(solution)/shard_map/ppermute | solution.py:61
  66.8 18.0 %collective-permute-start.12 = (bf16[8,32,1280]{2,1,0:T(8,128)(2,1)}, bf16[8,32,1280]{2,1,0:T(8,128)(2,1)S(1)}, u32[]{:S(2)}, u32[]{:S(2)}) collective-permute-start(bf16[8,32,1280]{2,1,0:T(8,128)(2,1)} %all-to-all-done), channel_id=1, source_target_pairs={{8,0},{0,8},{9,1},{1,9},{10,2},{2,10},{11,3},{3,11},{12,4},{4,12},... | collective-permute-start | bytes 1966088 | tf_op jit(solution)/shard_map/ppermute | solution.py:16
  72.8 5.6 %copy-start.2 = (bf16[8,32,1280]{2,1,0:T(8,128)(2,1)}, bf16[8,32,1280]{2,1,0:T(8,128)(2,1)S(1)}, u32[]{:S(2)}) copy-start(bf16[8,32,1280]{2,1,0:T(8,128)(2,1)S(1)} %collective-permute-done.13) | copy-start | bytes 1966084
  72.8 12.1 %collective-permute-start.14 = (bf16[8,32,1280]{2,1,0:T(8,128)(2,1)S(1)}, bf16[8,32,1280]{2,1,0:T(8,128)(2,1)S(1)}, u32[]{:S(2)}, u32[]{:S(2)}) collective-permute-start(bf16[8,32,1280]{2,1,0:T(8,128)(2,1)S(1)} %collective-permute-done.13), channel_id=1, source_target_pairs={{8,0},{0,8},{9,1},{1,9},{10,2},{2,10},{11,3},{3,11},{12,4},{4,12},... | collective-permute-start | bytes 1966088 | tf_op jit(solution)/shard_map/ppermute | solution.py:16
  78.4 5.9 %collective-permute-start.11 = (bf16[128,64]{1,0:T(8,128)(2,1)S(1)}, bf16[128,64]{1,0:T(8,128)(2,1)S(1)}, u32[]{:S(2)}, u32[]{:S(2)}) collective-permute-start(bf16[128,64]{1,0:T(8,128)(2,1)S(1)} %add.173), channel_id=1, source_target_pairs={{0,4},{1,5},{2,6},{3,7},{4,0},{5,1},{6,2},{7,3},{8,12},{9,13},{10,... | collective-permute-start | bytes 49160 | tf_op jit(solution)/shard_map/ppermute | solution.py:61
  84.8 0.8 copy-start.3
  85.7 0.8 copy-start.4

commit v4 on v3

--- a/solution.py
+++ b/solution.py
@@ -21,7 +21,7 @@
     return list(range(0, n, 2)) + list(range(1, n, 2))[::-1]
 
 
-def ring_gather(block, axis):
+def ring_gather(block, axis, behind_which=None):
     n = lax.axis_size(axis)
     ring = ring_of(n)
     rows, width = block.shape
@@ -38,18 +38,17 @@
 
     out = put(out, block, 0, 0)
     ahead = behind = block
-    first = None
     for step in range(1, n // 2):
         ahead = lax.ppermute(ahead, axis, up)
         behind = lax.ppermute(behind, axis, down)
-        if first is None:
-            first = (ahead, behind)
         out = put(out, ahead, step, 0)
         out = put(out, behind, -step, 0)
     half = width // 2
+    if behind_which is not None:
+        ahead, behind, behind_which = lax.optimization_barrier((ahead, behind, behind_which))
     out = put(out, lax.ppermute(ahead[:, :half], axis, up), n // 2, 0)
     out = put(out, lax.ppermute(behind[:, half:], axis, down), n // 2, half)
-    return out, first
+    return out, behind_which
 
 
 def sum_over(x, axis):
@@ -63,8 +62,41 @@
     return x
 
 
-def lift_kernel(reps, groups, pieces, at_ref, slot_ref, low_ref, *refs):
-    ups, bases, out_ref = refs[: reps * groups], refs[reps * groups : -1], refs[-1]
+def cut_kernel(parts, columns, at_ref, panel_ref, out_ref):
+    rows = pl.ds(pl.multiple_of(at_ref[0], out_ref.shape[1]), out_ref.shape[1])
+    for part in range(parts):
+        out_ref[part] = panel_ref[rows, part * columns : (part + 1) * columns]
+
+
+def low_kernel(reps, groups, at_ref, slot_ref, tokens_ref, *refs):
+    downs, out_ref = refs[:-1], refs[-1]
+    total = jnp.zeros(out_ref.shape, jnp.float32)
+    for s, down in enumerate(downs):
+        mine = slot_ref[...] == at_ref[reps + s] + at_ref[reps + groups]
+        product = lax.dot_general(
+            tokens_ref[...], down[...], (((1,), (1,)), ((), ())),
+            preferred_element_type=jnp.float32,
+        )
+        total = jnp.where(mine, product, total)
+    out_ref[...] = total.astype(out_ref.dtype)
+
+
+def base_kernel(tokens_ref, weight_ref, *refs):
+    before, out_ref = refs[:-1], refs[-1]
+    product = jnp.dot(tokens_ref[...], weight_ref[...], preferred_element_type=jnp.float32)
+    first = pl.program_id(0) == 0
+
+    @pl.when(first)
+    def _():
+        out_ref[...] = product + before[0][...] if before else product
+
+    @pl.when(jnp.logical_not(first))
+    def _():
+        out_ref[...] += product
+
+
+def lift_kernel(reps, groups, at_ref, slot_ref, low_ref, base_ref, *refs):
+    ups, out_ref = refs[:-1], refs[-1]
     depth = ups[0].shape[0]
     rank = low_ref.shape[1]
     rank_portion = rank // reps
@@ -73,20 +105,17 @@
     row = lax.broadcasted_iota(jnp.int32, (rank, depth), 0)
     column = lax.broadcasted_iota(jnp.int32, (rank, depth), 1)
     lane = lax.broadcasted_iota(jnp.int32, (low.shape[0], depth), 1)
-    expanded = []
+    total = base_ref[...]
     for r in range(reps):
         spread = (row == at_ref[r] + lax.rem(column, rank_portion)).astype(jnp.bfloat16)
         wide = jnp.dot(low, spread, preferred_element_type=jnp.float32)
         for s in range(groups):
             chosen = token_slot == at_ref[reps + s] + lane // rank_portion
-            expanded.append(jnp.where(chosen, wide, 0.0).astype(jnp.bfloat16))
-    for (start, size), base in zip(pieces, bases):
-        total = base[...]
-        for part, panel in zip(expanded, ups):
+            expanded = jnp.where(chosen, wide, 0.0).astype(jnp.bfloat16)
             total = total + adapter_scale * jnp.dot(
-                part, panel[:, start : start + size], preferred_element_type=jnp.float32
+                expanded, ups[r * groups + s][...], preferred_element_type=jnp.float32
             )
-        out_ref[:, start : start + size] = total.astype(out_ref.dtype)
+    out_ref[...] = total.astype(out_ref.dtype)
 
 
 def on_device(
@@ -109,17 +138,21 @@
     columns = base_projection_weight.shape[1]
     store_size = adapter_store_slot.shape[0]
     tok_all = tokens.shape[1] * tp
-
-    gathered, first = ring_gather(tokens[0], "tp")
+    width = tokens.shape[2]
+    in_vmem = pl.BlockSpec(memory_space=pltpu.VMEM)
 
     downs = swapped(jnp.transpose(adapter_down_panels[0]), "grp")
 
-    up_mine = lax.dynamic_slice_in_dim(
-        adapter_up_panels[0], my_rep * rank_portion, rank_portion, axis=0
-    )
-    up_send = jnp.transpose(up_mine.reshape(rank_portion, tp, columns), (1, 0, 2))
-    up_send = lax.optimization_barrier((up_send, *first))[0]
+    up_send = pl.pallas_call(
+        functools.partial(cut_kernel, tp, columns),
+        out_shape=jax.ShapeDtypeStruct((tp, rank_portion, columns), jnp.bfloat16),
+        in_specs=[pl.BlockSpec(memory_space=pltpu.SMEM), in_vmem],
+        out_specs=in_vmem,
+        name="cut",
+    )((my_rep * rank_portion).astype(jnp.int32).reshape(1), adapter_up_panels[0])
     up_got = lax.all_to_all(up_send, "tp", split_axis=0, concat_axis=0, tiled=True)
+
+    gathered, up_got = ring_gather(tokens[0], "tp", up_got)
     ups = [swapped(part, "grp") for part in swapped(up_got, "rep")]
 
     ids = jnp.arange(store_size, dtype=jnp.int32)
@@ -134,36 +167,57 @@
     member = (position >= starts[None, :]) & (position < ends[None, :])
     token_slot = jnp.sum(jnp.where(member, my_slots[None, :], 0), axis=1)
 
-    low = sum(
-        jnp.where(
-            (token_slot == ((my_group + s) % groups) * tp + my_tp)[:, None],
-            lax.dot_general(
-                gathered, down, (((1,), (1,)), ((), ())), preferred_element_type=jnp.float32
-            ),
-            0.0,
-        )
-        for s, down in enumerate(downs)
-    ).astype(jnp.bfloat16)
-    low = sum_over(low, "tp")
-
-    pieces = [(a, min(512, columns - a)) for a in range(0, columns, 512)]
-    bases = [
-        jnp.dot(
-            gathered, base_projection_weight[:, a : a + n], preferred_element_type=jnp.float32
-        )
-        for a, n in pieces
-    ]
     at = jnp.stack(
         [lax.rem(my_rep + r, reps) * rank_portion for r in range(reps)]
         + [lax.rem(my_group + s, groups) * tp for s in range(groups)]
+        + [my_tp]
     ).astype(jnp.int32)
+    token_slot = token_slot[:, None]
+    low = pl.pallas_call(
+        functools.partial(low_kernel, reps, groups),
+        out_shape=jax.ShapeDtypeStruct((tok_all, rank), jnp.bfloat16),
+        in_specs=[pl.BlockSpec(memory_space=pltpu.SMEM)] + [in_vmem] * (2 + groups),
+        out_specs=in_vmem,
+        compiler_params=pltpu.CompilerParams(vmem_limit_bytes=24 * 2**20),
+        cost_estimate=pl.CostEstimate(
+            flops=2 * tok_all * width * rank * groups,
+            bytes_accessed=2 * width * (tok_all + rank * groups),
+            transcendentals=0,
+        ),
+        name="low",
+    )(at, token_slot, gathered, *downs)
+    low, gathered = lax.optimization_barrier((low, gathered))
+    low = sum_over(low, "tp")
+
+    base = None
+    parts, block = 4, 512
+    steps = width // parts // block
+    whole = pl.BlockSpec((tok_all, columns), lambda i: (0, 0))
+    for part in range(parts):
+        base = pl.pallas_call(
+            base_kernel,
+            grid=(steps,),
+            out_shape=jax.ShapeDtypeStruct((tok_all, columns), jnp.float32),
+            in_specs=[
+                pl.BlockSpec((tok_all, block), lambda i, part=part: (0, part * steps + i)),
+                pl.BlockSpec((block, columns), lambda i, part=part: (part * steps + i, 0)),
+            ]
+            + ([] if base is None else [whole]),
+            out_specs=whole,
+            compiler_params=pltpu.CompilerParams(vmem_limit_bytes=48 * 2**20),
+            cost_estimate=pl.CostEstimate(
+                flops=2 * tok_all * columns * width // parts,
+                bytes_accessed=2 * columns * width // parts,
+                transcendentals=0,
+            ),
+            name="base",
+        )(gathered, base_projection_weight, *([] if base is None else [base]))
     panels = [part.reshape(tp * rank_portion, columns) for row in ups for part in row]
-    in_vmem = pl.BlockSpec(memory_space=pltpu.VMEM)
     out = pl.pallas_call(
-        functools.partial(lift_kernel, reps, groups, pieces),
+        functools.partial(lift_kernel, reps, groups),
         out_shape=jax.ShapeDtypeStruct((tok_all, columns), jnp.bfloat16),
         in_specs=[pl.BlockSpec(memory_space=pltpu.SMEM)]
-        + [in_vmem] * (2 + len(panels) + len(bases)),
+        + [in_vmem] * (3 + len(panels)),
         out_specs=in_vmem,
         cost_estimate=pl.CostEstimate(
             flops=2 * tok_all * columns * rank * groups * tp,
@@ -171,7 +225,7 @@
             transcendentals=0,
         ),
         name="lift",
-    )(at, token_slot[:, None], low, *panels, *bases)
+    )(at, token_slot, low, base, *panels)
     return out[None]
 
 

time: 90.3 us -> 88.1 us (0.976)
  Pallas kernels: 3.24 us -> 24.3 us
  matrix products: 17.1 us -> 0 us
  local copies, waits for them, and re-layouts: 10.5 us -> 6.64 us
  other arithmetic: 3.06 us -> 1.12 us
  waiting for transfers between devices: 30.9 us -> 29.9 us
    pallas_call x1 -> x7, Pallas kernels: 3.24 us -> 24.3 us  [the longest x4 16.1 us: on_device(): pl.pallas_call(base_kernel, grid=(steps,), out_shape=jax.ShapeDtypeStruct...]
    dot_general x5 -> x0, matrix products: 17.1 us -> none  [the longest x3 14.5 us: on_device(): jnp.dot(gathered, base_projection_weight[:, a:a + n], preferred_element_t...]
    ppermute x4, waiting for transfers between devices: 5.93 us -> 11.2 us  [swapped(): lax.ppermute(x, axis, [((i + s) % n, i) for i in range(n)])]
    ppermute x3, waiting for transfers between devices: 19.3 us -> 15.4 us  [ring_gather(): ahead = lax.ppermute(ahead, axis, up)]
    optimization_barrier x1 -> x0, local copies, waits for them, and re-layouts: 2.03 us -> none  [on_device(): up_send = lax.optimization_barrier((up_send, *first))[0]]
    ppermute x1, waiting for transfers between devices: 1.68 us -> 0.01 us  [ring_gather(): out = put(out, lax.ppermute(behind[:, half:], axis, down), n // 2, half)]
    ppermute x1, waiting for transfers between devices: 2.78 us -> 1.2 us  [ring_gather(): out = put(out, lax.ppermute(ahead[:, :half], axis, up), n // 2, 0)]
    another operation x2 -> x1, other arithmetic: 1.48 us -> 0.19 us
  transfers between devices with their start and end apart: 16 -> 16, of which waited for: 7 -> 5; matrix products, arithmetic and copies ran while one was open for 31% -> 5% of each run, Pallas kernels for 0% -> 24%
where the time goes in v4:
time: 88.1 us; the launch traced here: 87.4 us
  waiting for transfers between devices  29.9 us (34%)
  starting transfers between devices  24.9 us (28%)
  Pallas kernels  24.3 us (28%)
  local copies, waits for them, and re-layouts  6.64 us (8%)
  other arithmetic  1.12 us (1%)
    pallas_call x4, Pallas kernels, on_device(): pl.pallas_call(base_kernel, grid=(steps,), out_shape=jax.ShapeDtypeStruct...  16.1 us
    ppermute x3, waiting for transfers between devices, ring_gather(): ahead = lax.ppermute(ahead, axis, up)  15.4 us
    ppermute x4, waiting for transfers between devices, swapped(): lax.ppermute(x, axis, [((i + s) % n, i) for i in range(n)])  11.2 us
    ppermute x3, starting transfers between devices, ring_gather(): ahead = lax.ppermute(ahead, axis, up)  9.95 us
    all_to_all x1, starting transfers between devices, on_device(): lax.all_to_all(up_send, 'tp', split_axis=0, concat_axis=0, tiled=True)  6.4 us
    ppermute x3, starting transfers between devices, sum_over(): x = x + lax.ppermute(x, axis, [(i, i ^ shift) for i in range(n)])  4.62 us
    pallas_call x1, Pallas kernels, on_device(): pl.pallas_call(functools.partial(lift_kernel, reps, groups), out_shape=ja...  3.43 us
    unnamed x24, local copies, waits for them, and re-layouts  3.22 us
  transfers between devices with their start and end apart: 16, of which 5 were waited for; matrix products, arithmetic and copies ran while one was open for 5% of the time, Pallas kernels for 24%

profile of v4, /device:TPU:0, one launch (start us, length us, event | category | flops | bytes accessed | tf_op | source)
XLA Modules:
  0.0 87.4 jit_solution(11147332392478752313)
XLA Ops:
  0.0 3.1 %collective-permute-start = (bf16[16,8192]{1,0:T(8,128)(2,1)}, bf16[16,8192]{1,0:T(8,128)(2,1)}, u32[]{:S(2)}, u32[]{:S(2)}) collective-permute-start(bf16[16,8192]{1,0:T(8,128)(2,1)} %bitcast.34), channel_id=1, source_target_pairs={{0,2},{2,4},{4,6},{6,7},{7,5},{5,3},{3,1},{1,0},{8,10},{10,12},{12... | collective-permute-start | bytes 786440 | tf_op jit(solution)/shard_map/ppermute | solution.py:42
  3.1 2.2 %cut.1 = bf16[8,32,1280]{2,1,0:T(8,128)(2,1)} custom-call(s32[1]{0:T(128)} %bitcast.12.at_ref, bf16[64,10240]{1,0:T(8,128)(2,1)} %bitcast.30), custom_call_target="tpu_custom_call" | custom-call | tf_op jit(solution)/shard_map/cut/pallas_call | solution.py:146
  5.3 6.4 %all-to-all-start = ((bf16[8,32,1280]{2,1,0:T(8,128)(2,1)}), bf16[8,32,1280]{2,1,0:T(8,128)(2,1)}, u32[]{:S(2)}, u32[]{:S(2)}) async-start(bf16[8,32,1280]{2,1,0:T(8,128)(2,1)} %cut.1), calls=%async_computation | async-start | bytes 1310720 | tf_op jit(solution)/shard_map/all_to_all | solution.py:153
  13.0 2.0 %collective-permute-start.2 = (bf16[16,8192]{1,0:T(8,128)(2,1)}, bf16[16,8192]{1,0:T(8,128)(2,1)S(1)}, u32[]{:S(2)}, u32[]{:S(2)}) collective-permute-start(bf16[16,8192]{1,0:T(8,128)(2,1)} %collective-permute-done), channel_id=1, source_target_pairs={{0,2},{2,4},{4,6},{6,7},{7,5},{5,3},{3,1},{1,0},{8,10},{10,12},{12... | collective-permute-start | bytes 786440 | tf_op jit(solution)/shard_map/ppermute | solution.py:42
  15.1 1.0 %constant_dynamic-update-slice_fusion.5 = bf16[128,8192]{1,0:T(8,128)(2,1)S(1)} fusion(bf16[128,8192]{1,0:T(8,128)(2,1)S(1)} %constant_dynamic-update-slice_fusion.6, bf16[16,8192]{1,0:T(8,128)(2,1)} %collective-permute-done, s32[]{:T(128)S(6)} %select_n.86), kind=kLoop, calls=%fused_computation.11 | loop fusion | bytes 524292 | tf_op jit(solution)/shard_map/dynamic_update_slice | solution.py:37
  16.0 1.0 %constant_dynamic-update-slice_fusion.4 = bf16[128,8192]{1,0:T(8,128)(2,1)S(1)} fusion(bf16[128,8192]{1,0:T(8,128)(2,1)S(1)} %constant_dynamic-update-slice_fusion.5, bf16[16,8192]{1,0:T(8,128)(2,1)} %collective-permute-done.1, s32[]{:T(128)S(6)} %select_n.88), kind=kLoop, calls=%fused_computation.10 | loop fusion | bytes 524292 | tf_op jit(solution)/shard_map/dynamic_update_slice | solution.py:37
  17.0 10.6 %collective-permute-done.2 = bf16[16,8192]{1,0:T(8,128)(2,1)S(1)} collective-permute-done((bf16[16,8192]{1,0:T(8,128)(2,1)}, bf16[16,8192]{1,0:T(8,128)(2,1)S(1)}, u32[]{:S(2)}, u32[]{:S(2)}) %collective-permute-start.2) | collective-permute-done | bytes 262176 | tf_op jit(solution)/shard_map/ppermute | solution.py:42
  27.6 4.9 %collective-permute-start.4 = (bf16[16,8192]{1,0:T(8,128)(2,1)S(1)}, bf16[16,8192]{1,0:T(8,128)(2,1)S(1)}, u32[]{:S(2)}, u32[]{:S(2)}) collective-permute-start(bf16[16,8192]{1,0:T(8,128)(2,1)S(1)} %collective-permute-done.2), channel_id=1, source_target_pairs={{0,2},{2,4},{4,6},{6,7},{7,5},{5,3},{3,1},{1,0},{8,10},{10,12},{12... | collective-permute-start | bytes 786440 | tf_op jit(solution)/shard_map/ppermute | solution.py:42
  32.6 4.7 %collective-permute-done.4 = bf16[16,8192]{1,0:T(8,128)(2,1)S(1)} collective-permute-done((bf16[16,8192]{1,0:T(8,128)(2,1)S(1)}, bf16[16,8192]{1,0:T(8,128)(2,1)S(1)}, u32[]{:S(2)}, u32[]{:S(2)}) %collective-permute-start.4) | collective-permute-done | bytes 262176 | tf_op jit(solution)/shard_map/ppermute | solution.py:42
  38.0 2.1 %collective-permute-done.5 = bf16[16,8192]{1,0:T(8,128)(2,1)S(1)} collective-permute-done((bf16[16,8192]{1,0:T(8,128)(2,1)S(1)}, bf16[16,8192]{1,0:T(8,128)(2,1)S(1)}, u32[]{:S(2)}, u32[]{:S(2)}) %collective-permute-start.5) | collective-permute-done | bytes 262176 | tf_op jit(solution)/shard_map/ppermute | solution.py:43
  40.2 0.9 %slice.6 = bf16[16,4096]{1,0:T(8,128)(2,1)S(1)} slice(bf16[16,8192]{1,0:T(8,128)(2,1)} %copy-done.8), slice={[0:16], [0:4096]} | slice | bytes 262144 | tf_op jit(solution)/shard_map/slice | solution.py:49
  41.1 1.8 %collective-permute-start.6 = (bf16[16,4096]{1,0:T(8,128)(2,1)S(1)}, bf16[16,4096]{1,0:T(8,128)(2,1)S(1)}, u32[]{:S(2)}, u32[]{:S(2)}) collective-permute-start(bf16[16,4096]{1,0:T(8,128)(2,1)S(1)} %slice.6), channel_id=1, source_target_pairs={{0,2},{2,4},{4,6},{6,7},{7,5},{5,3},{3,1},{1,0},{8,10},{10,12},{12... | collective-permute-start | bytes 393224 | tf_op jit(solution)/shard_map/ppermute | solution.py:49
  42.9 1.5 %collective-permute-start.13 = (bf16[8,32,1280]{2,1,0:T(8,128)(2,1)}, bf16[8,32,1280]{2,1,0:T(8,128)(2,1)S(1)}, u32[]{:S(2)}, u32[]{:S(2)}) collective-permute-start(bf16[8,32,1280]{2,1,0:T(8,128)(2,1)} %all-to-all-done), channel_id=1, source_target_pairs={{16,0},{0,16},{17,1},{1,17},{18,2},{2,18},{19,3},{3,19},{20,4},{4,... | collective-permute-start | bytes 1966088 | tf_op jit(solution)/shard_map/ppermute | solution.py:16
  44.9 1.2 %collective-permute-done.6 = bf16[16,4096]{1,0:T(8,128)(2,1)S(1)} collective-permute-done((bf16[16,4096]{1,0:T(8,128)(2,1)S(1)}, bf16[16,4096]{1,0:T(8,128)(2,1)S(1)}, u32[]{:S(2)}, u32[]{:S(2)}) %collective-permute-start.6) | collective-permute-done | bytes 131104 | tf_op jit(solution)/shard_map/ppermute | solution.py:49
  46.1 11.2 %collective-permute-done.13 = bf16[8,32,1280]{2,1,0:T(8,128)(2,1)S(1)} collective-permute-done((bf16[8,32,1280]{2,1,0:T(8,128)(2,1)}, bf16[8,32,1280]{2,1,0:T(8,128)(2,1)S(1)}, u32[]{:S(2)}, u32[]{:S(2)}) %collective-permute-start.13) | collective-permute-done | bytes 655392 | tf_op jit(solution)/shard_map/ppermute | solution.py:16
  57.4 2.6 %low.1 = bf16[128,64]{1,0:T(8,128)(2,1)S(1)} custom-call(s32[5]{0:T(128)S(1)} %stack.23.at_ref, s32[128,1]{1,0:T(8,128)S(1)} %copy.11.slot_ref, bf16[128,8192]{1,0:T(8,128)(2,1)S(1)} %constant_dynamic-update-slice_fusion.8.tokens_ref, bf16[64,8192]{1,0:T(8,128)(2,1)S(1)} %bitcast.29, bf16[64,8192]{1,0:T(8,128)(2,1)} %collective-permute-done.8.refs_1_), custom_call_target="tpu_custom_call" | custom-call | flops 268435456 | bytes 4194304 | tf_op jit(solution)/shard_map/low/pallas_call | solution.py:176
  60.0 1.2 %collective-permute-start.9 = (bf16[128,64]{1,0:T(8,128)(2,1)S(1)}, bf16[128,64]{1,0:T(8,128)(2,1)S(1)}, u32[]{:S(2)}, u32[]{:S(2)}) collective-permute-start(bf16[128,64]{1,0:T(8,128)(2,1)S(1)} %low.1), channel_id=1, source_target_pairs={{0,1},{1,0},{2,3},{3,2},{4,5},{5,4},{6,7},{7,6},{8,9},{9,8},{10,11... | collective-permute-start | bytes 49160 | tf_op jit(solution)/shard_map/ppermute | solution.py:60
  61.2 4.0 %base.4.refs_0_ = f32[128,1280]{1,0:T(8,128)S(1)} custom-call(bf16[128,8192]{1,0:T(8,128)(2,1)S(1)} %constant_dynamic-update-slice_fusion.8.tokens_ref, bf16[8192,1280]{1,0:T(8,128)(2,1)} %weight_ref.7), custom_call_target="tpu_custom_call" | custom-call | flops 671088640 | bytes 5242880 | tf_op jit(solution)/shard_map/base/pallas_call | solution.py:197
  65.2 4.0 %base.5.refs_0_ = f32[128,1280]{1,0:T(8,128)S(1)} custom-call(bf16[128,8192]{1,0:T(8,128)(2,1)S(1)} %constant_dynamic-update-slice_fusion.8.tokens_ref, bf16[8192,1280]{1,0:T(8,128)(2,1)} %weight_ref.7, f32[128,1280]{1,0:T(8,128)S(1)} %base.4.refs_0_), custom_call_target="tpu_custom_call" | custom-call | flops 671088640 | bytes 5242880 | tf_op jit(solution)/shard_map/base/pallas_call | solution.py:197
  69.3 1.7 %collective-permute-start.10 = (bf16[128,64]{1,0:T(8,128)(2,1)S(1)}, bf16[128,64]{1,0:T(8,128)(2,1)S(1)}, u32[]{:S(2)}, u32[]{:S(2)}) collective-permute-start(bf16[128,64]{1,0:T(8,128)(2,1)S(1)} %add.148), channel_id=1, source_target_pairs={{0,2},{1,3},{2,0},{3,1},{4,6},{5,7},{6,4},{7,5},{8,10},{9,11},{10,... | collective-permute-start | bytes 49160 | tf_op jit(solution)/shard_map/ppermute | solution.py:60
  71.0 4.0 %base.6.refs_0_ = f32[128,1280]{1,0:T(8,128)S(1)} custom-call(bf16[128,8192]{1,0:T(8,128)(2,1)S(1)} %constant_dynamic-update-slice_fusion.8.tokens_ref, bf16[8192,1280]{1,0:T(8,128)(2,1)} %weight_ref.7, f32[128,1280]{1,0:T(8,128)S(1)} %base.5.refs_0_), custom_call_target="tpu_custom_call" | custom-call | flops 671088640 | bytes 5242880 | tf_op jit(solution)/shard_map/base/pallas_call | solution.py:197
  75.1 1.7 %collective-permute-start.11 = (bf16[128,64]{1,0:T(8,128)(2,1)S(1)}, bf16[128,64]{1,0:T(8,128)(2,1)S(1)}, u32[]{:S(2)}, u32[]{:S(2)}) collective-permute-start(bf16[128,64]{1,0:T(8,128)(2,1)S(1)} %add.149), channel_id=1, source_target_pairs={{0,4},{1,5},{2,6},{3,7},{4,0},{5,1},{6,2},{7,3},{8,12},{9,13},{10,... | collective-permute-start | bytes 49160 | tf_op jit(solution)/shard_map/ppermute | solution.py:60
  76.8 4.0 %base.7.base_ref = f32[128,1280]{1,0:T(8,128)S(1)} custom-call(bf16[128,8192]{1,0:T(8,128)(2,1)S(1)} %constant_dynamic-update-slice_fusion.8.tokens_ref, bf16[8192,1280]{1,0:T(8,128)(2,1)} %weight_ref.7, f32[128,1280]{1,0:T(8,128)S(1)} %base.6.refs_0_), custom_call_target="tpu_custom_call" | custom-call | flops 671088640 | bytes 5242880 | tf_op jit(solution)/shard_map/base/pallas_call | solution.py:197
  84.0 3.4 %lift.1 = bf16[128,1280]{1,0:T(8,128)(2,1)} custom-call(s32[5]{0:T(128)} %copy-done.4, s32[128,1]{1,0:T(8,128)} %copy-done.3, bf16[128,64]{1,0:T(8,128)(2,1)} %add.150.low_ref, f32[128,1280]{1,0:T(8,128)} %copy-done.1, bf16[256,1280]{1,0:T(8,128)(2,1)} %bitcast.17.refs_0_, bf16[256,1280]{1,0:T(8,128)(2,1)} %bitcast.32, bf16[256,1280]{1,0:T(8,128)(2,1)} %bitcast.31, ...), custom_call_target="tpu_custom_call" | custom-call | flops 335544320 | bytes 3604480 | tf_op jit(solution)/shard_map/lift/pallas_call | solution.py:216
  (61 shorter events, 5.6 us)
Async XLA Ops:
  0.0 12.3 %copy-start = (s32[2,12]{1,0:T(2,128)S(1)}, s32[2,12]{1,0:T(2,128)}, u32[]{:S(2)}) copy-start(s32[2,12]{1,0:T(2,128)} %param.11) | copy-start | bytes 292
  0.0 11.7 %copy-start.2 = (bf16[1,8192,64]{1,2,0:T(8,128)(2,1)S(1)}, bf16[1,8192,64]{1,2,0:T(8,128)(2,1)}, u32[]{:S(2)}) copy-start(bf16[1,8192,64]{1,2,0:T(8,128)(2,1)} %param.9) | copy-start | bytes 3145732
  0.0 11.8 %copy-start.10 = (s32[1,12]{1,0:T(1,128)S(1)}, s32[1,12]{1,0:T(1,128)}, u32[]{:S(2)}) copy-start(s32[1,12]{1,0:T(1,128)} %param.12) | copy-start | bytes 148
  0.0 13.0 %collective-permute-start = (bf16[16,8192]{1,0:T(8,128)(2,1)}, bf16[16,8192]{1,0:T(8,128)(2,1)}, u32[]{:S(2)}, u32[]{:S(2)}) collective-permute-start(bf16[16,8192]{1,0:T(8,128)(2,1)} %bitcast.34), channel_id=1, source_target_pairs={{0,2},{2,4},{4,6},{6,7},{7,5},{5,3},{3,1},{1,0},{8,10},{10,12},{12... | collective-permute-start | bytes 786440 | tf_op jit(solution)/shard_map/ppermute | solution.py:42
  3.1 11.9 %collective-permute-start.1 = (bf16[16,8192]{1,0:T(8,128)(2,1)}, bf16[16,8192]{1,0:T(8,128)(2,1)}, u32[]{:S(2)}, u32[]{:S(2)}) collective-permute-start(bf16[16,8192]{1,0:T(8,128)(2,1)} %bitcast.35), channel_id=1, source_target_pairs={{2,0},{4,2},{6,4},{7,6},{5,7},{3,5},{1,3},{0,1},{10,8},{12,10},{14... | collective-permute-start | bytes 786440 | tf_op jit(solution)/shard_map/ppermute | solution.py:43
  5.3 6.9 %copy-start.9 = (bf16[1,16,8192]{2,1,0:T(8,128)(2,1)S(1)}, bf16[1,16,8192]{2,1,0:T(8,128)(2,1)}, u32[]{:S(2)}) copy-start(bf16[1,16,8192]{2,1,0:T(8,128)(2,1)} %param.7) | copy-start | bytes 786436
  5.3 7.2 %copy-start.11 = (s32[16]{0:T(128)S(1)}, s32[16]{0:T(128)}, u32[]{:S(2)}) copy-start(s32[16]{0:T(128)} %param.13) | copy-start | bytes 196
  5.3 34.9 %all-to-all-start = ((bf16[8,32,1280]{2,1,0:T(8,128)(2,1)}), bf16[8,32,1280]{2,1,0:T(8,128)(2,1)}, u32[]{:S(2)}, u32[]{:S(2)}) async-start(bf16[8,32,1280]{2,1,0:T(8,128)(2,1)} %cut.1), calls=%async_computation | async-start | bytes 1310720 | tf_op jit(solution)/shard_map/all_to_all | solution.py:153
  11.7 45.7 %collective-permute-start.8 = (bf16[64,8192]{1,0:T(8,128)(2,1)S(1)}, bf16[64,8192]{1,0:T(8,128)(2,1)}, u32[]{:S(2)}, u32[]{:S(2)}) collective-permute-start(bf16[64,8192]{1,0:T(8,128)(2,1)S(1)} %bitcast.28), channel_id=1, source_target_pairs={{8,0},{0,8},{9,1},{1,9},{10,2},{2,10},{11,3},{3,11},{12,4},{4,12},... | collective-permute-start | bytes 3145736 | tf_op jit(solution)/shard_map/ppermute | solution.py:16
  12.8 44.5 %copy-start.3 = (s32[128,1]{1,0:T(8,128)}, s32[128,1]{1,0:T(8,128)S(1)}, u32[]{:S(2)}) copy-start(s32[128,1]{1,0:T(8,128)S(1)} %copy.11.slot_ref) | copy-start | bytes 1540
  13.0 44.4 %copy-start.4 = (s32[5]{0:T(128)}, s32[5]{0:T(128)S(1)}, u32[]{:S(2)}) copy-start(s32[5]{0:T(128)S(1)} %stack.23.at_ref) | copy-start | bytes 64
  13.0 14.7 %collective-permute-start.2 = (bf16[16,8192]{1,0:T(8,128)(2,1)}, bf16[16,8192]{1,0:T(8,128)(2,1)S(1)}, u32[]{:S(2)}, u32[]{:S(2)}) collective-permute-start(bf16[16,8192]{1,0:T(8,128)(2,1)} %collective-permute-done), channel_id=1, source_target_pairs={{0,2},{2,4},{4,6},{6,7},{7,5},{5,3},{3,1},{1,0},{8,10},{10,12},{12... | collective-permute-start | bytes 786440 | tf_op jit(solution)/shard_map/ppermute | solution.py:42
  15.0 17.6 %collective-permute-start.3 = (bf16[16,8192]{1,0:T(8,128)(2,1)}, bf16[16,8192]{1,0:T(8,128)(2,1)S(1)}, u32[]{:S(2)}, u32[]{:S(2)}) collective-permute-start(bf16[16,8192]{1,0:T(8,128)(2,1)} %collective-permute-done.1), channel_id=1, source_target_pairs={{2,0},{4,2},{6,4},{7,6},{5,7},{3,5},{1,3},{0,1},{10,8},{12,10},{14... | collective-permute-start | bytes 786440 | tf_op jit(solution)/shard_map/ppermute | solution.py:43
  27.6 9.7 %collective-permute-start.4 = (bf16[16,8192]{1,0:T(8,128)(2,1)S(1)}, bf16[16,8192]{1,0:T(8,128)(2,1)S(1)}, u32[]{:S(2)}, u32[]{:S(2)}) collective-permute-start(bf16[16,8192]{1,0:T(8,128)(2,1)S(1)} %collective-permute-done.2), channel_id=1, source_target_pairs={{0,2},{2,4},{4,6},{6,7},{7,5},{5,3},{3,1},{1,0},{8,10},{10,12},{12... | collective-permute-start | bytes 786440 | tf_op jit(solution)/shard_map/ppermute | solution.py:42
  32.5 7.6 %collective-permute-start.5 = (bf16[16,8192]{1,0:T(8,128)(2,1)S(1)}, bf16[16,8192]{1,0:T(8,128)(2,1)S(1)}, u32[]{:S(2)}, u32[]{:S(2)}) collective-permute-start(bf16[16,8192]{1,0:T(8,128)(2,1)S(1)} %collective-permute-done.3), channel_id=1, source_target_pairs={{2,0},{4,2},{6,4},{7,6},{5,7},{3,5},{1,3},{0,1},{10,8},{12,10},{14... | collective-permute-start | bytes 786440 | tf_op jit(solution)/shard_map/ppermute | solution.py:43
  41.1 5.0 %collective-permute-start.6 = (bf16[16,4096]{1,0:T(8,128)(2,1)S(1)}, bf16[16,4096]{1,0:T(8,128)(2,1)S(1)}, u32[]{:S(2)}, u32[]{:S(2)}) collective-permute-start(bf16[16,4096]{1,0:T(8,128)(2,1)S(1)} %slice.6), channel_id=1, source_target_pairs={{0,2},{2,4},{4,6},{6,7},{7,5},{5,3},{3,1},{1,0},{8,10},{10,12},{12... | collective-permute-start | bytes 393224 | tf_op jit(solution)/shard_map/ppermute | solution.py:49
  42.9 14.4 %collective-permute-start.13 = (bf16[8,32,1280]{2,1,0:T(8,128)(2,1)}, bf16[8,32,1280]{2,1,0:T(8,128)(2,1)S(1)}, u32[]{:S(2)}, u32[]{:S(2)}) collective-permute-start(bf16[8,32,1280]{2,1,0:T(8,128)(2,1)} %all-to-all-done), channel_id=1, source_target_pairs={{16,0},{0,16},{17,1},{1,17},{18,2},{2,18},{19,3},{3,19},{20,4},{4,... | collective-permute-start | bytes 1966088 | tf_op jit(solution)/shard_map/ppermute | solution.py:16
  44.4 37.9 %collective-permute-start.12 = (bf16[8,32,1280]{2,1,0:T(8,128)(2,1)}, bf16[8,32,1280]{2,1,0:T(8,128)(2,1)S(1)}, u32[]{:S(2)}, u32[]{:S(2)}) collective-permute-start(bf16[8,32,1280]{2,1,0:T(8,128)(2,1)} %all-to-all-done), channel_id=1, source_target_pairs={{8,0},{0,8},{9,1},{1,9},{10,2},{2,10},{11,3},{3,11},{12,4},{4,12},... | collective-permute-start | bytes 1966088 | tf_op jit(solution)/shard_map/ppermute | solution.py:16
  44.5 12.8 %collective-permute-start.7 = (bf16[16,4096]{1,0:T(8,128)(2,1)S(1)}, bf16[16,4096]{1,0:T(8,128)(2,1)S(1)}, u32[]{:S(2)}, u32[]{:S(2)}) collective-permute-start(bf16[16,4096]{1,0:T(8,128)(2,1)S(1)} %slice.7), channel_id=1, source_target_pairs={{2,0},{4,2},{6,4},{7,6},{5,7},{3,5},{1,3},{0,1},{10,8},{12,10},{14... | collective-permute-start | bytes 393224 | tf_op jit(solution)/shard_map/ppermute | solution.py:50
  57.3 2.7 %copy-start.5 = (bf16[8,32,1280]{2,1,0:T(8,128)(2,1)}, bf16[8,32,1280]{2,1,0:T(8,128)(2,1)S(1)}, u32[]{:S(2)}) copy-start(bf16[8,32,1280]{2,1,0:T(8,128)(2,1)S(1)} %collective-permute-done.13) | copy-start | bytes 1966084
  57.3 25.0 %collective-permute-start.14 = (bf16[8,32,1280]{2,1,0:T(8,128)(2,1)S(1)}, bf16[8,32,1280]{2,1,0:T(8,128)(2,1)S(1)}, u32[]{:S(2)}, u32[]{:S(2)}) collective-permute-start(bf16[8,32,1280]{2,1,0:T(8,128)(2,1)S(1)} %collective-permute-done.13), channel_id=1, source_target_pairs={{8,0},{0,8},{9,1},{1,9},{10,2},{2,10},{11,3},{3,11},{12,4},{4,12},... | collective-permute-start | bytes 1966088 | tf_op jit(solution)/shard_map/ppermute | solution.py:16
  60.0 9.2 %collective-permute-start.9 = (bf16[128,64]{1,0:T(8,128)(2,1)S(1)}, bf16[128,64]{1,0:T(8,128)(2,1)S(1)}, u32[]{:S(2)}, u32[]{:S(2)}) collective-permute-start(bf16[128,64]{1,0:T(8,128)(2,1)S(1)} %low.1), channel_id=1, source_target_pairs={{0,1},{1,0},{2,3},{3,2},{4,5},{5,4},{6,7},{7,6},{8,9},{9,8},{10,11... | collective-permute-start | bytes 49160 | tf_op jit(solution)/shard_map/ppermute | solution.py:60
  69.3 5.8 %collective-permute-start.10 = (bf16[128,64]{1,0:T(8,128)(2,1)S(1)}, bf16[128,64]{1,0:T(8,128)(2,1)S(1)}, u32[]{:S(2)}, u32[]{:S(2)}) collective-permute-start(bf16[128,64]{1,0:T(8,128)(2,1)S(1)} %add.148), channel_id=1, source_target_pairs={{0,2},{1,3},{2,0},{3,1},{4,6},{5,7},{6,4},{7,5},{8,10},{9,11},{10,... | collective-permute-start | bytes 49160 | tf_op jit(solution)/shard_map/ppermute | solution.py:60
  75.1 6.6 %collective-permute-start.11 = (bf16[128,64]{1,0:T(8,128)(2,1)S(1)}, bf16[128,64]{1,0:T(8,128)(2,1)S(1)}, u32[]{:S(2)}, u32[]{:S(2)}) collective-permute-start(bf16[128,64]{1,0:T(8,128)(2,1)S(1)} %add.149), channel_id=1, source_target_pairs={{0,4},{1,5},{2,6},{3,7},{4,0},{5,1},{6,2},{7,3},{8,12},{9,13},{10,... | collective-permute-start | bytes 49160 | tf_op jit(solution)/shard_map/ppermute | solution.py:60
  (4 other events, 3.2 us)

commit v5 on v4

v5 whole, which is shorter than its diff:
```python
import functools

import jax
import jax.numpy as jnp
from jax import lax
from jax.experimental import pallas as pl
from jax.experimental.pallas import tpu as pltpu
from jax.sharding import PartitionSpec as P

adapter_scale = 1.0


def swapped(x, axis):
    n = lax.axis_size(axis)
    return [x] + [
        lax.ppermute(x, axis, [((i + s) % n, i) for i in range(n)]) for s in range(1, n)
    ]


def ring_of(n):
    return list(range(0, n, 2)) + list(range(1, n, 2))[::-1]


class Ring:
    def __init__(self, block, axis, last_from_behind):
        n = lax.axis_size(axis)
        ring = ring_of(n)
        self.n, self.axis, self.last_from_behind = n, axis, last_from_behind
        self.up = [(ring[i], ring[(i + 1) % n]) for i in range(n)]
        self.down = [(ring[(i + 1) % n], ring[i]) for i in range(n)]
        self.ahead = self.behind = block
        self.pieces = [block]

    def step(self, i):
        last = i == self.n // 2
        if not last or self.last_from_behind:
            self.ahead = lax.ppermute(self.ahead, self.axis, self.up)
            self.pieces.append(self.ahead)
        if not last or not self.last_from_behind:
            self.behind = lax.ppermute(self.behind, self.axis, self.down)
            self.pieces.append(self.behind)

    def wait_for(self, value):
        self.ahead, self.behind, value = lax.optimization_barrier(
            (self.ahead, self.behind, value)
        )
        return value


def ring_sources(axis):
    n = lax.axis_size(axis)
    me = lax.axis_index(axis)
    place = jnp.where(me % 2 == 0, me // 2, n - 1 - me // 2)
    distances = [0] + [d for i in range(1, n // 2) for d in (i, -i)] + [n // 2]
    sources = []
    for distance in distances:
        at = lax.rem(place - distance + n, n)
        sources.append(jnp.where(at < n // 2, 2 * at, 2 * (n - 1 - at) + 1))
    return sources


def sum_over(x, axis):
    n = lax.axis_size(axis)
    if n & (n - 1):
        return lax.psum(x, axis)
    shift = 1
    while shift < n:
        x = x + lax.ppermute(x, axis, [(i, i ^ shift) for i in range(n)])
        shift *= 2
    return x


def cut_kernel(parts, columns, at_ref, panel_ref, out_ref):
    rows = pl.ds(pl.multiple_of(at_ref[0], out_ref.shape[1]), out_ref.shape[1])
    for part in range(parts):
        out_ref[part] = panel_ref[rows, part * columns : (part + 1) * columns]


def halve_kernel(block_ref, *out_refs):
    width = out_refs[0].shape[1]
    for i, out_ref in enumerate(out_refs):
        out_ref[...] = block_ref[:, i * width : (i + 1) * width]


def low_kernel(reps, groups, tp, at_ref, slot_ref, *refs):
    pieces, refs = refs[:tp], refs[tp:]
    before, downs = refs[: -groups - 2], refs[-groups - 2 : -2]
    tokens_ref, out_ref = refs[-2:]
    rows = pieces[0].shape[0]
    for i, piece in enumerate(pieces):
        start = pl.multiple_of(at_ref[reps + groups + 1 + i] * rows, rows)
        tokens_ref[pl.ds(start, rows), :] = piece[...]
    last = bool(before)
    total = None
    for s, down in enumerate(downs):
        product = lax.dot_general(
            tokens_ref[...], down[...], (((1,), (1,)), ((), ())),
            preferred_element_type=jnp.float32,
        )
        if last:
            product = product + before[0][s]
            mine = slot_ref[...] == at_ref[reps + s] + at_ref[reps + groups]
            total = jnp.where(mine, product, 0.0 if total is None else total)
        else:
            out_ref[s] = product
    if last:
        out_ref[...] = total.astype(out_ref.dtype)


def lift_kernel(reps, groups, at_ref, slot_ref, low_ref, base_ref, *refs):
    ups, out_ref = refs[:-1], refs[-1]
    depth = ups[0].shape[0]
    rank = low_ref.shape[1]
    rank_portion = rank // reps
    low = low_ref[...]
    token_slot = slot_ref[...]
    row = lax.broadcasted_iota(jnp.int32, (rank, depth), 0)
    column = lax.broadcasted_iota(jnp.int32, (rank, depth), 1)
    lane = lax.broadcasted_iota(jnp.int32, (low.shape[0], depth), 1)
    total = base_ref[...]
    for r in range(reps):
        spread = (row == at_ref[r] + lax.rem(column, rank_portion)).astype(jnp.bfloat16)
        wide = jnp.dot(low, spread, preferred_element_type=jnp.float32)
        for s in range(groups):
            chosen = token_slot == at_ref[reps + s] + lane // rank_portion
            expanded = jnp.where(chosen, wide, 0.0).astype(jnp.bfloat16)
            total = total + adapter_scale * jnp.dot(
                expanded, ups[r * groups + s][...], preferred_element_type=jnp.float32
            )
    out_ref[...] = total.astype(out_ref.dtype)


def on_device(
    tokens,
    base_projection_weight,
    adapter_down_panels,
    adapter_up_panels,
    request_adapter_ids,
    request_token_lengths,
    adapter_store_slot,
):
    groups = lax.axis_size("grp")
    tp = lax.axis_size("tp")
    reps = lax.axis_size("rep")
    my_group = lax.axis_index("grp")
    my_tp = lax.axis_index("tp")
    my_rep = lax.axis_index("rep")
    rank = adapter_down_panels.shape[2]
    rank_portion = rank // reps
    columns = base_projection_weight.shape[1]
    store_size = adapter_store_slot.shape[0]
    tok_all = tokens.shape[1] * tp
    width = tokens.shape[2]
    in_vmem = pl.BlockSpec(memory_space=pltpu.VMEM)

    downs = swapped(jnp.transpose(adapter_down_panels[0]), "grp")

    up_send = pl.pallas_call(
        functools.partial(cut_kernel, tp, columns),
        out_shape=jax.ShapeDtypeStruct((tp, rank_portion, columns), jnp.bfloat16),
        in_specs=[pl.BlockSpec(memory_space=pltpu.SMEM), in_vmem],
        out_specs=in_vmem,
        compiler_params=pltpu.CompilerParams(vmem_limit_bytes=16 * 2**20),
        name="cut",
    )((my_rep * rank_portion).astype(jnp.int32).reshape(1), adapter_up_panels[0])
    up_got = lax.all_to_all(up_send, "tp", split_axis=0, concat_axis=0, tiled=True)

    half = width // 2
    steps = tp // 2
    halves = pl.pallas_call(
        halve_kernel,
        out_shape=[jax.ShapeDtypeStruct((tokens.shape[1], half), jnp.bfloat16)] * 2,
        in_specs=[in_vmem],
        out_specs=[in_vmem] * 2,
        compiler_params=pltpu.CompilerParams(vmem_limit_bytes=16 * 2**20),
        name="halve",
    )(tokens[0])
    rings = [Ring(part, "tp", k == 0) for k, part in enumerate(halves)]
    rings[0].step(1)
    rings[1].wait_for(rings[0].ahead)
    for i in range(2, steps + 1):
        rings[0].step(i)
        rings[1].step(i - 1)
    up_got = rings[1].wait_for(up_got)
    rings[1].step(steps)

    ids = jnp.arange(store_size, dtype=jnp.int32)
    my_ids = lax.dynamic_index_in_dim(request_adapter_ids, my_group, 0, keepdims=False)
    my_slots = jnp.sum(
        jnp.where(my_ids[:, None] == ids[None, :], adapter_store_slot[None, :], 0), axis=-1
    )
    lengths = request_token_lengths[0]
    ends = jnp.cumsum(lengths)
    starts = ends - lengths
    position = jnp.arange(tok_all, dtype=jnp.int32)[:, None]
    member = (position >= starts[None, :]) & (position < ends[None, :])
    token_slot = jnp.sum(jnp.where(member, my_slots[None, :], 0), axis=1)

    at = jnp.stack(
        [lax.rem(my_rep + r, reps) * rank_portion for r in range(reps)]
        + [lax.rem(my_group + s, groups) * tp for s in range(groups)]
        + [my_tp]
        + ring_sources("tp")
    ).astype(jnp.int32)
    token_slot = token_slot[:, None]
    low = base = None
    for k, ring in enumerate(rings):
        last = k == len(rings) - 1
        gathered, low = pl.pallas_call(
            functools.partial(low_kernel, reps, groups, tp),
            out_shape=[
                jax.ShapeDtypeStruct((tok_all, half), jnp.bfloat16),
                jax.ShapeDtypeStruct((tok_all, rank), jnp.bfloat16)
                if last
                else jax.ShapeDtypeStruct((groups, tok_all, rank), jnp.float32),
            ],
            in_specs=[pl.BlockSpec(memory_space=pltpu.SMEM)]
            + [in_vmem] * (1 + tp + k + groups),
            out_specs=[in_vmem] * 2,
            compiler_params=pltpu.CompilerParams(vmem_limit_bytes=16 * 2**20),
            cost_estimate=pl.CostEstimate(
                flops=2 * tok_all * half * rank * groups,
                bytes_accessed=2 * half * (tok_all + rank * groups),
                transcendentals=0,
            ),
            name="low",
        )(
            at,
            token_slot,
            *ring.pieces,
            *([low] if last else []),
            *[down[:, k * half : (k + 1) * half] for down in downs],
        )
        if last:
            across = swapped(up_got, "rep")
            own = swapped(up_got, "grp")
            low, gathered, *across = lax.optimization_barrier((low, gathered, *across))
            ups = [own] + [swapped(part, "grp") for part in across[1:]]
            low = sum_over(low, "tp")
        product = jnp.dot(
            gathered,
            base_projection_weight[k * half : (k + 1) * half],
            preferred_element_type=jnp.float32,
        )
        base = product if base is None else base + product
        if not last:
            low, base = lax.optimization_barrier((low, base))

    panels = [part.reshape(tp * rank_portion, columns) for row in ups for part in row]
    out = pl.pallas_call(
        functools.partial(lift_kernel, reps, groups),
        out_shape=jax.ShapeDtypeStruct((tok_all, columns), jnp.bfloat16),
        in_specs=[pl.BlockSpec(memory_space=pltpu.SMEM)]
        + [in_vmem] * (3 + len(panels)),
        out_specs=in_vmem,
        cost_estimate=pl.CostEstimate(
            flops=2 * tok_all * columns * rank * groups * tp,
            bytes_accessed=2 * rank * groups * tp * columns + 6 * tok_all * columns,
            transcendentals=0,
        ),
        compiler_params=pltpu.CompilerParams(vmem_limit_bytes=16 * 2**20),
        name="lift",
    )(at, token_slot, low, base, *panels)
    return out[None]


def solution(mesh):
    return jax.shard_map(
        on_device,
        mesh=mesh,
        in_specs=(
            P(("rep", "grp"), "tp", None),
            P(None, "tp"),
            P(("grp", "tp"), None, None),
            P(("grp", "tp"), None, None),
            P("rep", None),
            P(("rep", "grp"), None),
            P(),
        ),
        out_specs=P(("rep", "grp"), None, "tp"),
        check_vma=False,
    )
```

time: 88.1 us -> 84 us (0.953)
  Pallas kernels: 24.3 us -> 6.32 us
  matrix products: 0 us -> 11.4 us
  waiting for transfers between devices: 29.9 us -> 18.7 us
  starting transfers between devices: 24.9 us -> 35.1 us
  local copies, waits for them, and re-layouts: 6.64 us -> 9.15 us
  other arithmetic: 1.12 us -> 2.53 us
    pallas_call x5 -> x3, Pallas kernels: 18.7 us -> 3.39 us  [the longest x2 3.38 us: on_device(): pl.pallas_call(functools.partial(low_kernel, reps, groups, tp), out_shape...]
    dot_general x0 -> x2, matrix products: none -> 11.4 us  [on_device(): jnp.dot(gathered, base_projection_weight[k * half:(k + 1) * half], prefer...]
    ppermute x8 -> x14, starting transfers between devices: 12.3 us -> 22.7 us  [the longest x7 18.7 us: step(): self.ahead = lax.ppermute(self.ahead, self.axis, self.up)]
    ppermute x4, waiting for transfers between devices: 11.2 us -> 2.8 us  [swapped(): lax.ppermute(x, axis, [((i + s) % n, i) for i in range(n)])]
    ppermute x8 -> x14, waiting for transfers between devices: 18.7 us -> 10.8 us  [the longest x7 10.8 us: step(): self.ahead = lax.ppermute(self.ahead, self.axis, self.up)]
    ppermute x3, waiting for transfers between devices: 0.01 us -> 5.13 us  [sum_over(): x = x + lax.ppermute(x, axis, [(i, i ^ shift) for i in range(n)])]
    unnamed x24 -> x16, local copies, waits for them, and re-layouts: 3.22 us -> 6.4 us
    dynamic_update_slice x9 -> x0, local copies, waits for them, and re-layouts: 2.08 us -> none  [put(): return lax.dynamic_update_slice(out, part, (source * rows, column))]
  transfers between devices with their start and end apart: 16 -> 22, of which waited for: 5 -> 5; matrix products, arithmetic and copies ran while one was open for 5% -> 20% of each run, Pallas kernels for 24% -> 5%
where the time goes in v5:
time: 84 us; the launch traced here: 83.6 us
  starting transfers between devices  35.1 us (42%)
  waiting for transfers between devices  18.7 us (22%)
  matrix products  11.4 us (14%)
  local copies, waits for them, and re-layouts  9.15 us (11%)
  Pallas kernels  6.32 us (8%)
  other arithmetic  2.53 us (3%)
    ppermute x7, starting transfers between devices, step(): self.ahead = lax.ppermute(self.ahead, self.axis, self.up)  18.7 us
    dot_general x2, matrix products, on_device(): jnp.dot(gathered, base_projection_weight[k * half:(k + 1) * half], prefer...  11.4 us
    ppermute x7, waiting for transfers between devices, step(): self.ahead = lax.ppermute(self.ahead, self.axis, self.up)  10.8 us
    unnamed x16, local copies, waits for them, and re-layouts  6.4 us
    all_to_all x1, starting transfers between devices, on_device(): lax.all_to_all(up_send, 'tp', split_axis=0, concat_axis=0, tiled=True)  6.28 us
    ppermute x3, waiting for transfers between devices, sum_over(): x = x + lax.ppermute(x, axis, [(i, i ^ shift) for i in range(n)])  5.13 us
    ppermute x3, starting transfers between devices, sum_over(): x = x + lax.ppermute(x, axis, [(i, i ^ shift) for i in range(n)])  4.15 us
    ppermute x7, starting transfers between devices, step(): self.behind = lax.ppermute(self.behind, self.axis, self.down)  4.02 us
  transfers between devices with their start and end apart: 22, of which 5 were waited for; matrix products, arithmetic and copies ran while one was open for 20% of the time, Pallas kernels for 5%

profile of v5, /device:TPU:0, one launch (start us, length us, event | category | flops | bytes accessed | tf_op | source)
XLA Modules:
  0.0 83.6 jit_solution(2703906520696071429)
XLA Ops:
  1.0 3.1 %collective-permute-start = (bf16[16,4096]{1,0:T(8,128)(2,1)S(1)}, bf16[16,4096]{1,0:T(8,128)(2,1)S(1)}, u32[]{:S(2)}, u32[]{:S(2)}) collective-permute-start(bf16[16,4096]{1,0:T(8,128)(2,1)S(1)} %get-tuple-element.21.refs_0_), channel_id=1, source_target_pairs={{0,2},{2,4},{4,6},{6,7},{7,5},{5,3},{3,1},{1,0},{8,10},{10,12},{12... | collective-permute-start | bytes 393224 | tf_op jit(solution)/shard_map/ppermute | solution.py:37
  4.1 1.3 %copy-done.1 = bf16[1,64,10240]{2,1,0:T(8,128)(2,1)S(1)} copy-done((bf16[1,64,10240]{2,1,0:T(8,128)(2,1)S(1)}, bf16[1,64,10240]{2,1,0:T(8,128)(2,1)}, u32[]{:S(2)}) %copy-start.1) | copy-done | bytes 1310744
  6.3 6.3 %all-to-all-start = ((bf16[8,32,1280]{2,1,0:T(8,128)(2,1)}), bf16[8,32,1280]{2,1,0:T(8,128)(2,1)S(1)}, u32[]{:S(2)}, u32[]{:S(2)}) async-start(bf16[8,32,1280]{2,1,0:T(8,128)(2,1)} %cut.1), calls=%async_computation | async-start | bytes 1310720 | tf_op jit(solution)/shard_map/all_to_all | solution.py:166
  12.6 1.3 %fusion.7 = (bf16[64,4096]{1,0:T(8,128)(2,1)S(1)}, bf16[64,4096]{1,0:T(8,128)(2,1)S(1)}) fusion(bf16[64,8192]{1,0:T(8,128)(2,1)} %bitcast.44), kind=kLoop, calls=%fused_computation.14 | loop fusion | bytes 2097152 | tf_op jit(solution)/shard_map/slice | solution.py:232
  14.7 2.0 %collective-permute-start.1 = (bf16[16,4096]{1,0:T(8,128)(2,1)S(1)}, bf16[16,4096]{1,0:T(8,128)(2,1)S(1)}, u32[]{:S(2)}, u32[]{:S(2)}) collective-permute-start(bf16[16,4096]{1,0:T(8,128)(2,1)S(1)} %get-tuple-element.23.refs_0_), channel_id=1, source_target_pairs={{0,2},{2,4},{4,6},{6,7},{7,5},{5,3},{3,1},{1,0},{8,10},{10,12},{12... | collective-permute-start | bytes 393224 | tf_op jit(solution)/shard_map/ppermute | solution.py:37
  16.7 2.0 %collective-permute-start.9 = (bf16[16,4096]{1,0:T(8,128)(2,1)S(1)}, bf16[16,4096]{1,0:T(8,128)(2,1)S(1)}, u32[]{:S(2)}, u32[]{:S(2)}) collective-permute-start(bf16[16,4096]{1,0:T(8,128)(2,1)S(1)} %collective-permute-done.refs_1_), channel_id=1, source_target_pairs={{0,2},{2,4},{4,6},{6,7},{7,5},{5,3},{3,1},{1,0},{8,10},{10,12},{12... | collective-permute-start | bytes 393224 | tf_op jit(solution)/shard_map/ppermute | solution.py:37
  19.5 10.6 %collective-permute-done.9.refs_3_ = bf16[16,4096]{1,0:T(8,128)(2,1)S(1)} collective-permute-done((bf16[16,4096]{1,0:T(8,128)(2,1)S(1)}, bf16[16,4096]{1,0:T(8,128)(2,1)S(1)}, u32[]{:S(2)}, u32[]{:S(2)}) %collective-permute-start.9) | collective-permute-done | bytes 131104 | tf_op jit(solution)/shard_map/ppermute | solution.py:37
  30.0 4.9 %collective-permute-start.11 = (bf16[16,4096]{1,0:T(8,128)(2,1)S(1)}, bf16[16,4096]{1,0:T(8,128)(2,1)}, u32[]{:S(2)}, u32[]{:S(2)}) collective-permute-start(bf16[16,4096]{1,0:T(8,128)(2,1)S(1)} %collective-permute-done.9.refs_3_), channel_id=1, source_target_pairs={{0,2},{2,4},{4,6},{6,7},{7,5},{5,3},{3,1},{1,0},{8,10},{10,12},{12... | collective-permute-start | bytes 393224 | tf_op jit(solution)/shard_map/ppermute | solution.py:37
  34.9 2.5 %collective-permute-start.3 = (bf16[16,4096]{1,0:T(8,128)(2,1)S(1)}, bf16[16,4096]{1,0:T(8,128)(2,1)S(1)}, u32[]{:S(2)}, u32[]{:S(2)}) collective-permute-start(bf16[16,4096]{1,0:T(8,128)(2,1)S(1)} %collective-permute-done.1.refs_1_), channel_id=1, source_target_pairs={{0,2},{2,4},{4,6},{6,7},{7,5},{5,3},{3,1},{1,0},{8,10},{10,12},{12... | collective-permute-start | bytes 393224 | tf_op jit(solution)/shard_map/ppermute | solution.py:37
  39.6 1.7 %collective-permute-start.13 = (bf16[16,4096]{1,0:T(8,128)(2,1)}, bf16[16,4096]{1,0:T(8,128)(2,1)S(1)}, u32[]{:S(2)}, u32[]{:S(2)}) collective-permute-start(bf16[16,4096]{1,0:T(8,128)(2,1)} %collective-permute-done.11.refs_5_), channel_id=1, source_target_pairs={{0,2},{2,4},{4,6},{6,7},{7,5},{5,3},{3,1},{1,0},{8,10},{10,12},{12... | collective-permute-start | bytes 393224 | tf_op jit(solution)/shard_map/ppermute | solution.py:37
  41.3 2.6 %collective-permute-start.5 = (bf16[16,4096]{1,0:T(8,128)(2,1)S(1)}, bf16[16,4096]{1,0:T(8,128)(2,1)S(1)}, u32[]{:S(2)}, u32[]{:S(2)}) collective-permute-start(bf16[16,4096]{1,0:T(8,128)(2,1)S(1)} %collective-permute-done.3.refs_3_), channel_id=1, source_target_pairs={{0,2},{2,4},{4,6},{6,7},{7,5},{5,3},{3,1},{1,0},{8,10},{10,12},{12... | collective-permute-start | bytes 393224 | tf_op jit(solution)/shard_map/ppermute | solution.py:37
  45.0 1.3 %fusion.6 = (bf16[64,4096]{1,0:T(8,128)(2,1)S(1)}, bf16[64,4096]{1,0:T(8,128)(2,1)S(1)}) fusion(bf16[64,8192]{1,0:T(8,128)(2,1)} %collective-permute-done.14), kind=kLoop, calls=%fused_computation.13 | loop fusion | bytes 2097152 | tf_op jit(solution)/shard_map/slice | solution.py:232
  46.5 1.7 %low.2 = (bf16[128,4096]{1,0:T(8,128)(2,1)S(1)}, f32[2,128,64]{2,1,0:T(8,128)S(1)}) custom-call(s32[13]{0:T(128)S(1)} %stack.55.at_ref, s32[128,1]{1,0:T(8,128)S(1)} %copy.13.slot_ref, bf16[16,4096]{1,0:T(8,128)(2,1)S(1)} %get-tuple-element.21.refs_0_, bf16[16,4096]{1,0:T(8,128)(2,1)S(1)} %collective-permute-done.refs_1_, ...), custom_call_target="tpu_custom_call" | custom-call | flops 134217728 | bytes 2097152 | tf_op jit(solution)/shard_map/low/pallas_call | solution.py:209
  50.5 1.9 %collective-permute-start.7 = (bf16[16,4096]{1,0:T(8,128)(2,1)}, bf16[16,4096]{1,0:T(8,128)(2,1)S(1)}, u32[]{:S(2)}, u32[]{:S(2)}) collective-permute-start(bf16[16,4096]{1,0:T(8,128)(2,1)} %collective-permute-done.6.refs_6_), channel_id=1, source_target_pairs={{2,0},{4,2},{6,4},{7,6},{5,7},{3,5},{1,3},{0,1},{10,8},{12,10},{14... | collective-permute-start | bytes 393224 | tf_op jit(solution)/shard_map/ppermute | solution.py:40
  52.4 1.5 %collective-permute-start.15 = (bf16[8,32,1280]{2,1,0:T(8,128)(2,1)S(1)}, bf16[8,32,1280]{2,1,0:T(8,128)(2,1)S(1)}, u32[]{:S(2)}, u32[]{:S(2)}) collective-permute-start(bf16[8,32,1280]{2,1,0:T(8,128)(2,1)S(1)} %all-to-all-done), channel_id=1, source_target_pairs={{16,0},{0,16},{17,1},{1,17},{18,2},{2,18},{19,3},{3,19},{20,4},{4,... | collective-permute-start | bytes 1966088 | tf_op jit(solution)/shard_map/ppermute | solution.py:16
  53.9 5.8 %fusion.2 = f32[128,1280]{1,0:T(8,128)S(1)} fusion(bf16[128,4096]{1,0:T(8,128)(2,1)} %copy-done.7, bf16[8192,1280]{1,0:T(8,128)(2,1)} %param.8), kind=kOutput, calls=%fused_computation.2 | convolution fusion | flops 1342177280 | bytes 12189696 | tf_op jit(solution)/shard_map/dot_general | solution.py:240
  61.6 1.7 %low.3 = (bf16[128,4096]{1,0:T(8,128)(2,1)S(1)}, bf16[128,64]{1,0:T(8,128)(2,1)S(1)}) custom-call(s32[13]{0:T(128)S(1)} %stack.55.at_ref, s32[128,1]{1,0:T(8,128)S(1)} %copy.13.slot_ref, bf16[16,4096]{1,0:T(8,128)(2,1)S(1)} %get-tuple-element.23.refs_0_, bf16[16,4096]{1,0:T(8,128)(2,1)S(1)} %collective-permute-done.1.refs_1_, ...), custom_call_target="tpu_custom_call" | custom-call | flops 134217728 | bytes 2097152 | tf_op jit(solution)/shard_map/low/pallas_call | solution.py:209
  63.2 2.8 %collective-permute-done.15 = bf16[8,32,1280]{2,1,0:T(8,128)(2,1)S(1)} collective-permute-done((bf16[8,32,1280]{2,1,0:T(8,128)(2,1)S(1)}, bf16[8,32,1280]{2,1,0:T(8,128)(2,1)S(1)}, u32[]{:S(2)}, u32[]{:S(2)}) %collective-permute-start.15) | collective-permute-done | bytes 655392 | tf_op jit(solution)/shard_map/ppermute | solution.py:16
  66.0 1.5 %collective-permute-start.16 = (bf16[128,64]{1,0:T(8,128)(2,1)S(1)}, bf16[128,64]{1,0:T(8,128)(2,1)S(1)}, u32[]{:S(2)}, u32[]{:S(2)}) collective-permute-start(bf16[128,64]{1,0:T(8,128)(2,1)S(1)} %get-tuple-element.31), channel_id=1, source_target_pairs={{0,1},{1,0},{2,3},{3,2},{4,5},{5,4},{6,7},{7,6},{8,9},{9,8},{10,11... | collective-permute-start | bytes 49160 | tf_op jit(solution)/shard_map/ppermute | solution.py:68
  67.6 2.4 %collective-permute-done.16 = bf16[128,64]{1,0:T(8,128)(2,1)S(1)} collective-permute-done((bf16[128,64]{1,0:T(8,128)(2,1)S(1)}, bf16[128,64]{1,0:T(8,128)(2,1)S(1)}, u32[]{:S(2)}, u32[]{:S(2)}) %collective-permute-start.16) | collective-permute-done | bytes 16416 | tf_op jit(solution)/shard_map/ppermute | solution.py:68
  71.2 2.8 %collective-permute-done.17 = bf16[128,64]{1,0:T(8,128)(2,1)S(1)} collective-permute-done((bf16[128,64]{1,0:T(8,128)(2,1)S(1)}, bf16[128,64]{1,0:T(8,128)(2,1)S(1)}, u32[]{:S(2)}, u32[]{:S(2)}) %collective-permute-start.17) | collective-permute-done | bytes 16416 | tf_op jit(solution)/shard_map/ppermute | solution.py:68
  74.0 1.9 %collective-permute-start.18 = (bf16[128,64]{1,0:T(8,128)(2,1)S(1)}, bf16[128,64]{1,0:T(8,128)(2,1)S(1)}, u32[]{:S(2)}, u32[]{:S(2)}) collective-permute-start(bf16[128,64]{1,0:T(8,128)(2,1)S(1)} %add.117), channel_id=1, source_target_pairs={{0,4},{1,5},{2,6},{3,7},{4,0},{5,1},{6,2},{7,3},{8,12},{9,13},{10,... | collective-permute-start | bytes 49160 | tf_op jit(solution)/shard_map/ppermute | solution.py:68
  75.8 5.6 %fusion = f32[128,1280]{1,0:T(8,128)S(1)} fusion(bf16[128,4096]{1,0:T(8,128)(2,1)S(1)} %get-tuple-element.33, bf16[8192,1280]{1,0:T(8,128)(2,1)} %param.8), kind=kOutput, calls=%fused_computation | convolution fusion | flops 1342177280 | bytes 12189696 | tf_op jit(solution)/shard_map/dot_general | solution.py:240
  81.5 2.0 %lift.1 = bf16[128,1280]{1,0:T(8,128)(2,1)} custom-call(s32[13]{0:T(128)S(1)} %stack.55.at_ref, s32[128,1]{1,0:T(8,128)S(1)} %copy.13.slot_ref, bf16[128,64]{1,0:T(8,128)(2,1)S(1)} %add.118.low_ref, f32[128,1280]{1,0:T(8,128)S(1)} %add.119.base_ref, bf16[256,1280]{1,0:T(8,128)(2,1)S(1)} %bitcast.37, bf16[256,1280]{1,0:T(8,128)(2,1)S(1)} %bitcast.40, ...), custom_call_target="tpu_custom_call" | custom-call | flops 335544320 | bytes 3604480 | tf_op jit(solution)/shard_map/lift/pallas_call | solution.py:250
  (56 shorter events, 12.3 us)
Async XLA Ops:
  0.0 19.4 %copy-start = (s32[2,12]{1,0:T(2,128)S(1)}, s32[2,12]{1,0:T(2,128)}, u32[]{:S(2)}) copy-start(s32[2,12]{1,0:T(2,128)} %param.11) | copy-start | bytes 292
  1.0 13.7 %collective-permute-start = (bf16[16,4096]{1,0:T(8,128)(2,1)S(1)}, bf16[16,4096]{1,0:T(8,128)(2,1)S(1)}, u32[]{:S(2)}, u32[]{:S(2)}) collective-permute-start(bf16[16,4096]{1,0:T(8,128)(2,1)S(1)} %get-tuple-element.21.refs_0_), channel_id=1, source_target_pairs={{0,2},{2,4},{4,6},{6,7},{7,5},{5,3},{3,1},{1,0},{8,10},{10,12},{12... | collective-permute-start | bytes 393224 | tf_op jit(solution)/shard_map/ppermute | solution.py:37
  4.1 15.3 %collective-permute-start.8 = (bf16[16,4096]{1,0:T(8,128)(2,1)S(1)}, bf16[16,4096]{1,0:T(8,128)(2,1)S(1)}, u32[]{:S(2)}, u32[]{:S(2)}) collective-permute-start(bf16[16,4096]{1,0:T(8,128)(2,1)S(1)} %get-tuple-element.21.refs_0_), channel_id=1, source_target_pairs={{2,0},{4,2},{6,4},{7,6},{5,7},{3,5},{1,3},{0,1},{10,8},{12,10},{14... | collective-permute-start | bytes 393224 | tf_op jit(solution)/shard_map/ppermute | solution.py:40
  4.1 40.9 %collective-permute-start.14 = (bf16[64,8192]{1,0:T(8,128)(2,1)}, bf16[64,8192]{1,0:T(8,128)(2,1)}, u32[]{:S(2)}, u32[]{:S(2)}) collective-permute-start(bf16[64,8192]{1,0:T(8,128)(2,1)} %bitcast.43), channel_id=1, source_target_pairs={{8,0},{0,8},{9,1},{1,9},{10,2},{2,10},{11,3},{3,11},{12,4},{4,12},... | collective-permute-start | bytes 3145736 | tf_op jit(solution)/shard_map/ppermute | solution.py:16
  4.1 1.3 %copy-start.1 = (bf16[1,64,10240]{2,1,0:T(8,128)(2,1)S(1)}, bf16[1,64,10240]{2,1,0:T(8,128)(2,1)}, u32[]{:S(2)}) copy-start(bf16[1,64,10240]{2,1,0:T(8,128)(2,1)} %param.10) | copy-start | bytes 3932164
  6.3 44.3 %all-to-all-start = ((bf16[8,32,1280]{2,1,0:T(8,128)(2,1)}), bf16[8,32,1280]{2,1,0:T(8,128)(2,1)S(1)}, u32[]{:S(2)}, u32[]{:S(2)}) async-start(bf16[8,32,1280]{2,1,0:T(8,128)(2,1)} %cut.1), calls=%async_computation | async-start | bytes 1310720 | tf_op jit(solution)/shard_map/all_to_all | solution.py:166
  14.7 20.3 %collective-permute-start.1 = (bf16[16,4096]{1,0:T(8,128)(2,1)S(1)}, bf16[16,4096]{1,0:T(8,128)(2,1)S(1)}, u32[]{:S(2)}, u32[]{:S(2)}) collective-permute-start(bf16[16,4096]{1,0:T(8,128)(2,1)S(1)} %get-tuple-element.23.refs_0_), channel_id=1, source_target_pairs={{0,2},{2,4},{4,6},{6,7},{7,5},{5,3},{3,1},{1,0},{8,10},{10,12},{12... | collective-permute-start | bytes 393224 | tf_op jit(solution)/shard_map/ppermute | solution.py:37
  16.7 20.7 %collective-permute-start.2 = (bf16[16,4096]{1,0:T(8,128)(2,1)S(1)}, bf16[16,4096]{1,0:T(8,128)(2,1)S(1)}, u32[]{:S(2)}, u32[]{:S(2)}) collective-permute-start(bf16[16,4096]{1,0:T(8,128)(2,1)S(1)} %get-tuple-element.23.refs_0_), channel_id=1, source_target_pairs={{2,0},{4,2},{6,4},{7,6},{5,7},{3,5},{1,3},{0,1},{10,8},{12,10},{14... | collective-permute-start | bytes 393224 | tf_op jit(solution)/shard_map/ppermute | solution.py:40
  16.7 13.3 %collective-permute-start.9 = (bf16[16,4096]{1,0:T(8,128)(2,1)S(1)}, bf16[16,4096]{1,0:T(8,128)(2,1)S(1)}, u32[]{:S(2)}, u32[]{:S(2)}) collective-permute-start(bf16[16,4096]{1,0:T(8,128)(2,1)S(1)} %collective-permute-done.refs_1_), channel_id=1, source_target_pairs={{0,2},{2,4},{4,6},{6,7},{7,5},{5,3},{3,1},{1,0},{8,10},{10,12},{12... | collective-permute-start | bytes 393224 | tf_op jit(solution)/shard_map/ppermute | solution.py:37
  19.4 19.3 %collective-permute-start.10 = (bf16[16,4096]{1,0:T(8,128)(2,1)S(1)}, bf16[16,4096]{1,0:T(8,128)(2,1)}, u32[]{:S(2)}, u32[]{:S(2)}) collective-permute-start(bf16[16,4096]{1,0:T(8,128)(2,1)S(1)} %collective-permute-done.8.refs_2_), channel_id=1, source_target_pairs={{2,0},{4,2},{6,4},{7,6},{5,7},{3,5},{1,3},{0,1},{10,8},{12,10},{14... | collective-permute-start | bytes 393224 | tf_op jit(solution)/shard_map/ppermute | solution.py:40
  30.0 9.6 %collective-permute-start.11 = (bf16[16,4096]{1,0:T(8,128)(2,1)S(1)}, bf16[16,4096]{1,0:T(8,128)(2,1)}, u32[]{:S(2)}, u32[]{:S(2)}) collective-permute-start(bf16[16,4096]{1,0:T(8,128)(2,1)S(1)} %collective-permute-done.9.refs_3_), channel_id=1, source_target_pairs={{0,2},{2,4},{4,6},{6,7},{7,5},{5,3},{3,1},{1,0},{8,10},{10,12},{12... | collective-permute-start | bytes 393224 | tf_op jit(solution)/shard_map/ppermute | solution.py:37
  34.9 6.4 %collective-permute-start.3 = (bf16[16,4096]{1,0:T(8,128)(2,1)S(1)}, bf16[16,4096]{1,0:T(8,128)(2,1)S(1)}, u32[]{:S(2)}, u32[]{:S(2)}) collective-permute-start(bf16[16,4096]{1,0:T(8,128)(2,1)S(1)} %collective-permute-done.1.refs_1_), channel_id=1, source_target_pairs={{0,2},{2,4},{4,6},{6,7},{7,5},{5,3},{3,1},{1,0},{8,10},{10,12},{12... | collective-permute-start | bytes 393224 | tf_op jit(solution)/shard_map/ppermute | solution.py:37
  37.4 6.5 %collective-permute-start.4 = (bf16[16,4096]{1,0:T(8,128)(2,1)S(1)}, bf16[16,4096]{1,0:T(8,128)(2,1)S(1)}, u32[]{:S(2)}, u32[]{:S(2)}) collective-permute-start(bf16[16,4096]{1,0:T(8,128)(2,1)S(1)} %collective-permute-done.2.refs_2_), channel_id=1, source_target_pairs={{2,0},{4,2},{6,4},{7,6},{5,7},{3,5},{1,3},{0,1},{10,8},{12,10},{14... | collective-permute-start | bytes 393224 | tf_op jit(solution)/shard_map/ppermute | solution.py:40
  38.7 7.6 %collective-permute-start.12 = (bf16[16,4096]{1,0:T(8,128)(2,1)}, bf16[16,4096]{1,0:T(8,128)(2,1)S(1)}, u32[]{:S(2)}, u32[]{:S(2)}) collective-permute-start(bf16[16,4096]{1,0:T(8,128)(2,1)} %collective-permute-done.10.refs_4_), channel_id=1, source_target_pairs={{2,0},{4,2},{6,4},{7,6},{5,7},{3,5},{1,3},{0,1},{10,8},{12,10},{14... | collective-permute-start | bytes 393224 | tf_op jit(solution)/shard_map/ppermute | solution.py:40
  39.6 6.9 %collective-permute-start.13 = (bf16[16,4096]{1,0:T(8,128)(2,1)}, bf16[16,4096]{1,0:T(8,128)(2,1)S(1)}, u32[]{:S(2)}, u32[]{:S(2)}) collective-permute-start(bf16[16,4096]{1,0:T(8,128)(2,1)} %collective-permute-done.11.refs_5_), channel_id=1, source_target_pairs={{0,2},{2,4},{4,6},{6,7},{7,5},{5,3},{3,1},{1,0},{8,10},{10,12},{12... | collective-permute-start | bytes 393224 | tf_op jit(solution)/shard_map/ppermute | solution.py:37
  41.3 8.6 %collective-permute-start.5 = (bf16[16,4096]{1,0:T(8,128)(2,1)S(1)}, bf16[16,4096]{1,0:T(8,128)(2,1)S(1)}, u32[]{:S(2)}, u32[]{:S(2)}) collective-permute-start(bf16[16,4096]{1,0:T(8,128)(2,1)S(1)} %collective-permute-done.3.refs_3_), channel_id=1, source_target_pairs={{0,2},{2,4},{4,6},{6,7},{7,5},{5,3},{3,1},{1,0},{8,10},{10,12},{12... | collective-permute-start | bytes 393224 | tf_op jit(solution)/shard_map/ppermute | solution.py:37
  43.9 6.7 %collective-permute-start.6 = (bf16[16,4096]{1,0:T(8,128)(2,1)S(1)}, bf16[16,4096]{1,0:T(8,128)(2,1)}, u32[]{:S(2)}, u32[]{:S(2)}) collective-permute-start(bf16[16,4096]{1,0:T(8,128)(2,1)S(1)} %collective-permute-done.4.refs_4_), channel_id=1, source_target_pairs={{2,0},{4,2},{6,4},{7,6},{5,7},{3,5},{1,3},{0,1},{10,8},{12,10},{14... | collective-permute-start | bytes 393224 | tf_op jit(solution)/shard_map/ppermute | solution.py:40
  50.5 9.2 %collective-permute-start.7 = (bf16[16,4096]{1,0:T(8,128)(2,1)}, bf16[16,4096]{1,0:T(8,128)(2,1)S(1)}, u32[]{:S(2)}, u32[]{:S(2)}) collective-permute-start(bf16[16,4096]{1,0:T(8,128)(2,1)} %collective-permute-done.6.refs_6_), channel_id=1, source_target_pairs={{2,0},{4,2},{6,4},{7,6},{5,7},{3,5},{1,3},{0,1},{10,8},{12,10},{14... | collective-permute-start | bytes 393224 | tf_op jit(solution)/shard_map/ppermute | solution.py:40
  52.4 13.6 %collective-permute-start.15 = (bf16[8,32,1280]{2,1,0:T(8,128)(2,1)S(1)}, bf16[8,32,1280]{2,1,0:T(8,128)(2,1)S(1)}, u32[]{:S(2)}, u32[]{:S(2)}) collective-permute-start(bf16[8,32,1280]{2,1,0:T(8,128)(2,1)S(1)} %all-to-all-done), channel_id=1, source_target_pairs={{16,0},{0,16},{17,1},{1,17},{18,2},{2,18},{19,3},{3,19},{20,4},{4,... | collective-permute-start | bytes 1966088 | tf_op jit(solution)/shard_map/ppermute | solution.py:16
  66.0 3.9 %collective-permute-start.16 = (bf16[128,64]{1,0:T(8,128)(2,1)S(1)}, bf16[128,64]{1,0:T(8,128)(2,1)S(1)}, u32[]{:S(2)}, u32[]{:S(2)}) collective-permute-start(bf16[128,64]{1,0:T(8,128)(2,1)S(1)} %get-tuple-element.31), channel_id=1, source_target_pairs={{0,1},{1,0},{2,3},{3,2},{4,5},{5,4},{6,7},{7,6},{8,9},{9,8},{10,11... | collective-permute-start | bytes 49160 | tf_op jit(solution)/shard_map/ppermute | solution.py:68
  70.0 4.0 %collective-permute-start.17 = (bf16[128,64]{1,0:T(8,128)(2,1)S(1)}, bf16[128,64]{1,0:T(8,128)(2,1)S(1)}, u32[]{:S(2)}, u32[]{:S(2)}) collective-permute-start(bf16[128,64]{1,0:T(8,128)(2,1)S(1)} %add.116), channel_id=1, source_target_pairs={{0,2},{1,3},{2,0},{3,1},{4,6},{5,7},{6,4},{7,5},{8,10},{9,11},{10,... | collective-permute-start | bytes 49160 | tf_op jit(solution)/shard_map/ppermute | solution.py:68
  70.7 10.8 %collective-permute-start.19 = (bf16[8,32,1280]{2,1,0:T(8,128)(2,1)S(1)}, bf16[8,32,1280]{2,1,0:T(8,128)(2,1)S(1)}, u32[]{:S(2)}, u32[]{:S(2)}) collective-permute-start(bf16[8,32,1280]{2,1,0:T(8,128)(2,1)S(1)} %all-to-all-done), channel_id=1, source_target_pairs={{8,0},{0,8},{9,1},{1,9},{10,2},{2,10},{11,3},{3,11},{12,4},{4,12},... | collective-permute-start | bytes 1966088 | tf_op jit(solution)/shard_map/ppermute | solution.py:16
  70.7 10.9 %collective-permute-start.20 = (bf16[8,32,1280]{2,1,0:T(8,128)(2,1)S(1)}, bf16[8,32,1280]{2,1,0:T(8,128)(2,1)S(1)}, u32[]{:S(2)}, u32[]{:S(2)}) collective-permute-start(bf16[8,32,1280]{2,1,0:T(8,128)(2,1)S(1)} %collective-permute-done.15), channel_id=1, source_target_pairs={{8,0},{0,8},{9,1},{1,9},{10,2},{2,10},{11,3},{3,11},{12,4},{4,12},... | collective-permute-start | bytes 1966088 | tf_op jit(solution)/shard_map/ppermute | solution.py:16
  74.0 7.5 %collective-permute-start.18 = (bf16[128,64]{1,0:T(8,128)(2,1)S(1)}, bf16[128,64]{1,0:T(8,128)(2,1)S(1)}, u32[]{:S(2)}, u32[]{:S(2)}) collective-permute-start(bf16[128,64]{1,0:T(8,128)(2,1)S(1)} %add.117), channel_id=1, source_target_pairs={{0,4},{1,5},{2,6},{3,7},{4,0},{5,1},{6,2},{7,3},{8,12},{9,13},{10,... | collective-permute-start | bytes 49160 | tf_op jit(solution)/shard_map/ppermute | solution.py:68
  (6 other events, 5.1 us)

commit v6 on v1

v6 whole, which is shorter than its diff:
```python
import functools

import jax
import jax.numpy as jnp
from jax import lax
from jax.experimental import pallas as pl
from jax.experimental.pallas import tpu as pltpu
from jax.sharding import PartitionSpec as P

adapter_scale = 1.0


def swapped(x, axis):
    n = lax.axis_size(axis)
    return [x] + [
        lax.ppermute(x, axis, [((i + s) % n, i) for i in range(n)]) for s in range(1, n)
    ]


def ring_of(n):
    return list(range(0, n, 2)) + list(range(1, n, 2))[::-1]


class Ring:
    def __init__(self, block, axis, last_from_behind):
        n = lax.axis_size(axis)
        ring = ring_of(n)
        self.n, self.axis, self.last_from_behind = n, axis, last_from_behind
        self.up = [(ring[i], ring[(i + 1) % n]) for i in range(n)]
        self.down = [(ring[(i + 1) % n], ring[i]) for i in range(n)]
        self.ahead = self.behind = block
        self.pieces = [block]

    def step(self, i):
        last = i == self.n // 2
        if not last or self.last_from_behind:
            self.ahead = lax.ppermute(self.ahead, self.axis, self.up)
            self.pieces.append(self.ahead)
        if not last or not self.last_from_behind:
            self.behind = lax.ppermute(self.behind, self.axis, self.down)
            self.pieces.append(self.behind)

    def wait_for(self, value):
        self.ahead, self.behind, value = lax.optimization_barrier(
            (self.ahead, self.behind, value)
        )
        return value


def ring_sources(axis):
    n = lax.axis_size(axis)
    me = lax.axis_index(axis)
    place = jnp.where(me % 2 == 0, me // 2, n - 1 - me // 2)
    distances = [0] + [d for i in range(1, n // 2) for d in (i, -i)] + [n // 2]
    sources = []
    for distance in distances:
        at = lax.rem(place - distance + n, n)
        sources.append(jnp.where(at < n // 2, 2 * at, 2 * (n - 1 - at) + 1))
    return sources


def halve_kernel(block_ref, *out_refs):
    width = out_refs[0].shape[1]
    for i, out_ref in enumerate(out_refs):
        out_ref[...] = block_ref[:, i * width : (i + 1) * width]


def stack_kernel(groups, *refs):
    downs, ups, (down_ref, up_ref) = refs[:groups], refs[groups:-2], refs[-2:]
    rank = ups[0].shape[0]
    down_ref[...] = jnp.concatenate([down[...] for down in downs], axis=0).T
    for s, up in enumerate(ups):
        up_ref[s * rank : (s + 1) * rank, :] = up[...]


def lift_kernel(tp, at_ref, place_ref, down_ref, up_ref, *refs):
    pieces, (tokens_ref, out_ref) = refs[:-2], refs[-2:]
    rows, width = pieces[0].shape
    per_half = len(pieces) // 2
    for i, piece in enumerate(pieces):
        start = pl.multiple_of(at_ref[1 + i % per_half] * rows, rows)
        column = i // per_half * width
        tokens_ref[pl.ds(start, rows), column : column + width] = piece[...]
    low = jnp.dot(tokens_ref[...], down_ref[...], preferred_element_type=jnp.float32)
    low = low.astype(jnp.bfloat16)
    slots, columns = out_ref.shape[1], out_ref.shape[2]
    all_ranks = up_ref.shape[0]
    here = lax.broadcasted_iota(jnp.int32, (slots, low.shape[0]), 0) + at_ref[0]
    chosen = (here == place_ref[...]).astype(jnp.bfloat16)
    picked = jnp.dot(chosen, low, preferred_element_type=jnp.float32)
    panels = slots // (tokens_ref.shape[0] // 8)
    row_panel = lax.broadcasted_iota(jnp.int32, picked.shape, 0) // (slots // panels)
    rank_panel = lax.broadcasted_iota(jnp.int32, picked.shape, 1) // (all_ranks // panels)
    picked = jnp.where(row_panel == rank_panel, picked, 0.0).astype(jnp.bfloat16)
    for part in range(tp):
        out_ref[part] = jnp.dot(
            picked,
            up_ref[:, part * columns : (part + 1) * columns],
            preferred_element_type=jnp.float32,
        ).astype(out_ref.dtype)


def add_kernel(place_ref, base_ref, lifts_ref, out_ref):
    place = lax.broadcasted_iota(jnp.int32, (base_ref.shape[0], lifts_ref.shape[0]), 1)
    chosen = (place == place_ref[...]).astype(jnp.bfloat16)
    lift = jnp.dot(chosen, lifts_ref[...], preferred_element_type=jnp.float32)
    out_ref[...] = (base_ref[...] + adapter_scale * lift).astype(out_ref.dtype)


def on_device(
    tokens,
    base_projection_weight,
    adapter_down_panels,
    adapter_up_panels,
    request_adapter_ids,
    request_token_lengths,
    adapter_store_slot,
):
    groups = lax.axis_size("grp")
    tp = lax.axis_size("tp")
    my_group = lax.axis_index("grp")
    my_tp = lax.axis_index("tp")
    width, rank = adapter_down_panels.shape[1:]
    columns = base_projection_weight.shape[1]
    store_size = adapter_store_slot.shape[0]
    tok_all = tokens.shape[1] * tp
    longest = tok_all // 8
    here = groups * longest
    half = width // 2
    in_vmem = pl.BlockSpec(memory_space=pltpu.VMEM)
    in_smem = pl.BlockSpec(memory_space=pltpu.SMEM)
    small = pltpu.CompilerParams(vmem_limit_bytes=16 * 2**20)

    halves = pl.pallas_call(
        halve_kernel,
        out_shape=[jax.ShapeDtypeStruct((tokens.shape[1], half), jnp.bfloat16)] * 2,
        in_specs=[in_vmem],
        out_specs=[in_vmem] * 2,
        compiler_params=small,
        name="halve",
    )(tokens[0])
    rings = [Ring(part, "tp", k == 0) for k, part in enumerate(halves)]
    for i in range(1, tp // 2 + 1):
        for ring in rings:
            ring.step(i)

    down_stack, up_stack = pl.pallas_call(
        functools.partial(stack_kernel, groups),
        out_shape=[
            jax.ShapeDtypeStruct((width, groups * rank), jnp.bfloat16),
            jax.ShapeDtypeStruct((groups * rank, tp * columns), jnp.bfloat16),
        ],
        in_specs=[in_vmem] * (2 * groups),
        out_specs=[in_vmem] * 2,
        compiler_params=pltpu.CompilerParams(vmem_limit_bytes=24 * 2**20),
        name="stack",
    )(
        *swapped(jnp.transpose(adapter_down_panels[0]), "grp"),
        *swapped(adapter_up_panels[0], "grp"),
    )

    ids = jnp.arange(store_size, dtype=jnp.int32)
    my_ids = lax.dynamic_index_in_dim(request_adapter_ids, my_group, 0, keepdims=False)
    my_slots = jnp.sum(
        jnp.where(my_ids[:, None] == ids[None, :], adapter_store_slot[None, :], 0), axis=-1
    )
    lengths = request_token_lengths[0]
    ends = jnp.cumsum(lengths)
    starts = ends - lengths
    panel = lax.rem(my_slots // tp - my_group + groups, groups)
    first = lax.rem(my_slots, tp) * here + panel * longest - starts
    position = jnp.arange(tok_all, dtype=jnp.int32)[:, None]
    member = (position >= starts[None, :]) & (position < ends[None, :])
    place = jnp.sum(jnp.where(member, first[None, :] + position, 0), axis=1)

    at = jnp.stack([my_tp * here] + ring_sources("tp")).astype(jnp.int32)
    gathered, lifts = pl.pallas_call(
        functools.partial(lift_kernel, tp),
        out_shape=[
            jax.ShapeDtypeStruct((tok_all, width), jnp.bfloat16),
            jax.ShapeDtypeStruct((tp, here, columns), jnp.bfloat16),
        ],
        in_specs=[in_smem] + [in_vmem] * (3 + 2 * tp),
        out_specs=[in_vmem] * 2,
        compiler_params=pltpu.CompilerParams(vmem_limit_bytes=24 * 2**20),
        cost_estimate=pl.CostEstimate(
            flops=2 * groups * rank * (tok_all * width + here * tp * columns),
            bytes_accessed=2 * groups * rank * (width + tp * columns),
            transcendentals=0,
        ),
        name="lift",
    )(at, place[None, :], down_stack, up_stack, *rings[0].pieces, *rings[1].pieces)
    lifts = lax.all_to_all(lifts, "tp", split_axis=0, concat_axis=0, tiled=True)

    base = jnp.dot(gathered, base_projection_weight, preferred_element_type=jnp.float32)
    out = pl.pallas_call(
        add_kernel,
        out_shape=jax.ShapeDtypeStruct((tok_all, columns), jnp.bfloat16),
        in_specs=[in_vmem] * 3,
        out_specs=in_vmem,
        compiler_params=small,
        name="add",
    )(place[:, None], base, lifts.reshape(tp * here, columns))
    return out[None]


def solution(mesh):
    return jax.shard_map(
        on_device,
        mesh=mesh,
        in_specs=(
            P(("rep", "grp"), "tp", None),
            P(None, "tp"),
            P(("grp", "tp"), None, None),
            P(("grp", "tp"), None, None),
            P("rep", None),
            P(("rep", "grp"), None),
            P(),
        ),
        out_specs=P(("rep", "grp"), None, "tp"),
        check_vma=False,
    )
```

time: 132 us -> 55.5 us (0.42)
  waiting for transfers between devices: 51.2 us -> 9.43 us
  blocking collectives: 32.8 us -> 0 us
  starting transfers between devices: 8.85 us -> 25.4 us
  between operations: 13.6 us -> 0.24 us
  matrix products: 19.7 us -> 8.56 us
  Pallas kernels: 0 us -> 5.34 us
  other arithmetic: 0.55 us -> 2.44 us
  local copies, waits for them, and re-layouts: 5.1 us -> 3.7 us
    all_gather x1 -> x0, blocking collectives: 32.8 us -> none  [on_device(): lax.all_gather(low, 'tp', axis=0)]
    all_to_all x1, waiting for transfers between devices: 25.6 us -> 3.35 us  [on_device(): lifts = lax.all_to_all(lifts, 'tp', split_axis=0, concat_axis=0, tiled=True)]
    ppermute x0 -> x14, starting transfers between devices: none -> 18.6 us  [the longest x7 10.6 us: step(): self.behind = lax.ppermute(self.behind, self.axis, self.down)]
    all_gather x1 -> x0, waiting for transfers between devices: 14.3 us -> none  [on_device(): gathered = lax.all_gather(tokens[0], 'tp', axis=0, tiled=True)]
    dot_general x6 -> x0, matrix products: 11.1 us -> none  [the longest x4 6.18 us: on_device(): lax.dot_general(low_all[:, s, :, r, :], ups[r][s], (((0, 2), (0, 1)), (()...]
    ppermute x4 -> x2, waiting for transfers between devices: 10.6 us -> 0.01 us  [swapped(): lax.ppermute(x, axis, [((i + s) % n, i) for i in range(n)])]
    ppermute x0 -> x14, waiting for transfers between devices: none -> 6.07 us  [the longest x7 3.45 us: step(): self.behind = lax.ppermute(self.behind, self.axis, self.down)]
    pallas_call x0 -> x4, Pallas kernels: none -> 5.34 us  [the longest x1 3.58 us: on_device(): pl.pallas_call(functools.partial(lift_kernel, tp), out_shape=[jax.ShapeDt...]
  transfers between devices with their start and end apart: 6 -> 17, of which waited for: 3 -> 6; matrix products, arithmetic and copies ran while one was open for 17% -> 20% of each run, Pallas kernels for 0% -> 1%
where the time goes in v6:
time: 55.5 us; the launch traced here: 55.1 us
  starting transfers between devices  25.4 us (46%)
  waiting for transfers between devices  9.43 us (17%)
  matrix products  8.56 us (15%)
  Pallas kernels  5.34 us (10%)
  local copies, waits for them, and re-layouts  3.7 us (7%)
  other arithmetic  2.44 us (4%)
    ppermute x7, starting transfers between devices, step(): self.behind = lax.ppermute(self.behind, self.axis, self.down)  10.6 us
    dot_general x1, matrix products, on_device(): jnp.dot(gathered, base_projection_weight, preferred_element_type=jnp.floa...  8.56 us
    ppermute x7, starting transfers between devices, step(): self.ahead = lax.ppermute(self.ahead, self.axis, self.up)  8.01 us
    all_to_all x1, starting transfers between devices, on_device(): lifts = lax.all_to_all(lifts, 'tp', split_axis=0, concat_axis=0, tiled=True)  6.3 us
    pallas_call x1, Pallas kernels, on_device(): pl.pallas_call(functools.partial(lift_kernel, tp), out_shape=[jax.ShapeDt...  3.58 us
    unnamed x8, local copies, waits for them, and re-layouts  3.49 us
    ppermute x7, waiting for transfers between devices, step(): self.behind = lax.ppermute(self.behind, self.axis, self.down)  3.45 us
    all_to_all x1, waiting for transfers between devices, on_device(): lifts = lax.all_to_all(lifts, 'tp', split_axis=0, concat_axis=0, tiled=True)  3.35 us
  transfers between devices with their start and end apart: 17, of which 6 were waited for; matrix products, arithmetic and copies ran while one was open for 20% of the time, Pallas kernels for 1%

profile of v6, /device:TPU:0, one launch (start us, length us, event | category | flops | bytes accessed | tf_op | source)
XLA Modules:
  0.0 55.1 jit_solution(993615689993365045)
XLA Ops:
  0.5 0.9 %copy-done.3 = bf16[1,16,8192]{2,1,0:T(8,128)(2,1)S(1)} copy-done((bf16[1,16,8192]{2,1,0:T(8,128)(2,1)S(1)}, bf16[1,16,8192]{2,1,0:T(8,128)(2,1)}, u32[]{:S(2)}) %copy-start.3) | copy-done | bytes 262168
  1.5 3.0 %collective-permute-start.10 = (bf16[16,4096]{1,0:T(8,128)(2,1)S(1)}, bf16[16,4096]{1,0:T(8,128)(2,1)S(1)}, u32[]{:S(2)}, u32[]{:S(2)}) collective-permute-start(bf16[16,4096]{1,0:T(8,128)(2,1)S(1)} %get-tuple-element.14.refs_8_), channel_id=1, source_target_pairs={{2,0},{4,2},{6,4},{7,6},{5,7},{3,5},{1,3},{0,1},{10,8},{12,10},{14... | collective-permute-start | bytes 393224 | tf_op jit(solution)/shard_map/ppermute | solution.py:40
  4.6 2.0 %collective-permute-start.9 = (bf16[16,4096]{1,0:T(8,128)(2,1)S(1)}, bf16[16,4096]{1,0:T(8,128)(2,1)S(1)}, u32[]{:S(2)}, u32[]{:S(2)}) collective-permute-start(bf16[16,4096]{1,0:T(8,128)(2,1)S(1)} %get-tuple-element.14.refs_8_), channel_id=1, source_target_pairs={{0,2},{2,4},{4,6},{6,7},{7,5},{5,3},{3,1},{1,0},{8,10},{10,12},{12... | collective-permute-start | bytes 393224 | tf_op jit(solution)/shard_map/ppermute | solution.py:37
  6.6 1.7 %collective-permute-done.10.refs_10_ = bf16[16,4096]{1,0:T(8,128)(2,1)S(1)} collective-permute-done((bf16[16,4096]{1,0:T(8,128)(2,1)S(1)}, bf16[16,4096]{1,0:T(8,128)(2,1)S(1)}, u32[]{:S(2)}, u32[]{:S(2)}) %collective-permute-start.10) | collective-permute-done | bytes 131104 | tf_op jit(solution)/shard_map/ppermute | solution.py:40
  8.3 1.7 %collective-permute-start.3 = (bf16[16,4096]{1,0:T(8,128)(2,1)S(1)}, bf16[16,4096]{1,0:T(8,128)(2,1)S(1)}, u32[]{:S(2)}, u32[]{:S(2)}) collective-permute-start(bf16[16,4096]{1,0:T(8,128)(2,1)S(1)} %get-tuple-element.13.refs_0_), channel_id=1, source_target_pairs={{2,0},{4,2},{6,4},{7,6},{5,7},{3,5},{1,3},{0,1},{10,8},{12,10},{14... | collective-permute-start | bytes 393224 | tf_op jit(solution)/shard_map/ppermute | solution.py:40
  10.0 0.9 %collective-permute-done.2.refs_1_ = bf16[16,4096]{1,0:T(8,128)(2,1)S(1)} collective-permute-done((bf16[16,4096]{1,0:T(8,128)(2,1)S(1)}, bf16[16,4096]{1,0:T(8,128)(2,1)S(1)}, u32[]{:S(2)}, u32[]{:S(2)}) %collective-permute-start.2) | collective-permute-done | bytes 131104 | tf_op jit(solution)/shard_map/ppermute | solution.py:37
  10.9 1.6 %collective-permute-start.12 = (bf16[16,4096]{1,0:T(8,128)(2,1)S(1)}, bf16[16,4096]{1,0:T(8,128)(2,1)S(1)}, u32[]{:S(2)}, u32[]{:S(2)}) collective-permute-start(bf16[16,4096]{1,0:T(8,128)(2,1)S(1)} %collective-permute-done.10.refs_10_), channel_id=1, source_target_pairs={{2,0},{4,2},{6,4},{7,6},{5,7},{3,5},{1,3},{0,1},{10,8},{12,10},{14... | collective-permute-start | bytes 393224 | tf_op jit(solution)/shard_map/ppermute | solution.py:40
  12.9 1.7 %collective-permute-done.3.refs_2_ = bf16[16,4096]{1,0:T(8,128)(2,1)S(1)} collective-permute-done((bf16[16,4096]{1,0:T(8,128)(2,1)S(1)}, bf16[16,4096]{1,0:T(8,128)(2,1)S(1)}, u32[]{:S(2)}, u32[]{:S(2)}) %collective-permute-start.3) | collective-permute-done | bytes 131104 | tf_op jit(solution)/shard_map/ppermute | solution.py:40
  14.7 1.4 %collective-permute-start.11 = (bf16[16,4096]{1,0:T(8,128)(2,1)S(1)}, bf16[16,4096]{1,0:T(8,128)(2,1)}, u32[]{:S(2)}, u32[]{:S(2)}) collective-permute-start(bf16[16,4096]{1,0:T(8,128)(2,1)S(1)} %collective-permute-done.9.refs_9_), channel_id=1, source_target_pairs={{0,2},{2,4},{4,6},{6,7},{7,5},{5,3},{3,1},{1,0},{8,10},{10,12},{12... | collective-permute-start | bytes 393224 | tf_op jit(solution)/shard_map/ppermute | solution.py:37
  16.1 1.4 %collective-permute-start.5 = (bf16[16,4096]{1,0:T(8,128)(2,1)S(1)}, bf16[16,4096]{1,0:T(8,128)(2,1)}, u32[]{:S(2)}, u32[]{:S(2)}) collective-permute-start(bf16[16,4096]{1,0:T(8,128)(2,1)S(1)} %collective-permute-done.3.refs_2_), channel_id=1, source_target_pairs={{2,0},{4,2},{6,4},{7,6},{5,7},{3,5},{1,3},{0,1},{10,8},{12,10},{14... | collective-permute-start | bytes 393224 | tf_op jit(solution)/shard_map/ppermute | solution.py:40
  18.2 1.6 %collective-permute-start.14 = (bf16[16,4096]{1,0:T(8,128)(2,1)S(1)}, bf16[16,4096]{1,0:T(8,128)(2,1)}, u32[]{:S(2)}, u32[]{:S(2)}) collective-permute-start(bf16[16,4096]{1,0:T(8,128)(2,1)S(1)} %collective-permute-done.12.refs_12_), channel_id=1, source_target_pairs={{2,0},{4,2},{6,4},{7,6},{5,7},{3,5},{1,3},{0,1},{10,8},{12,10},{14... | collective-permute-start | bytes 393224 | tf_op jit(solution)/shard_map/ppermute | solution.py:40
  19.8 1.3 %collective-permute-start.6 = (bf16[16,4096]{1,0:T(8,128)(2,1)S(1)}, bf16[16,4096]{1,0:T(8,128)(2,1)}, u32[]{:S(2)}, u32[]{:S(2)}) collective-permute-start(bf16[16,4096]{1,0:T(8,128)(2,1)S(1)} %collective-permute-done.4.refs_3_), channel_id=1, source_target_pairs={{0,2},{2,4},{4,6},{6,7},{7,5},{5,3},{3,1},{1,0},{8,10},{10,12},{12... | collective-permute-start | bytes 393224 | tf_op jit(solution)/shard_map/ppermute | solution.py:37
  21.2 0.8 %reduce-window.4 = s32[12,1]{0,1:T(1,128)S(1)} reduce-window(s32[12,1]{0,1:T(1,128)} %bitcast.58, s32[]{:T(128)} %constant.91.clone.1), window={size=12x1 pad=11_0x0_0}, to_apply=%region_0.1 | reduce-window | flops 132 | bytes 100 | tf_op jit(solution)/shard_map/reduce-window
  22.0 0.8 %select_reduce_fusion.1 = s32[12]{0:T(128)S(1)} fusion(s32[16]{0:T(128)} %param.13, s32[12]{0:T(128)S(1)} %dynamic-slice_bitcast_fusion), kind=kLoop, calls=%fused_computation.1 | loop fusion | flops 564 | bytes 160 | tf_op jit(solution)/shard_map/reduce_sum | solution.py:164
  22.8 1.9 %collective-permute-start.13 = (bf16[16,4096]{1,0:T(8,128)(2,1)}, bf16[16,4096]{1,0:T(8,128)(2,1)}, u32[]{:S(2)}, u32[]{:S(2)}) collective-permute-start(bf16[16,4096]{1,0:T(8,128)(2,1)} %collective-permute-done.11.refs_11_), channel_id=1, source_target_pairs={{0,2},{2,4},{4,6},{6,7},{7,5},{5,3},{3,1},{1,0},{8,10},{10,12},{12... | collective-permute-start | bytes 393224 | tf_op jit(solution)/shard_map/ppermute | solution.py:37
  25.0 0.9 %collective-permute-done.6.refs_5_ = bf16[16,4096]{1,0:T(8,128)(2,1)} collective-permute-done((bf16[16,4096]{1,0:T(8,128)(2,1)S(1)}, bf16[16,4096]{1,0:T(8,128)(2,1)}, u32[]{:S(2)}, u32[]{:S(2)}) %collective-permute-start.6) | collective-permute-done | bytes 131104 | tf_op jit(solution)/shard_map/ppermute | solution.py:37
  25.8 1.2 %collective-permute-start.15 = (bf16[16,4096]{1,0:T(8,128)(2,1)}, bf16[16,4096]{1,0:T(8,128)(2,1)}, u32[]{:S(2)}, u32[]{:S(2)}) collective-permute-start(bf16[16,4096]{1,0:T(8,128)(2,1)} %collective-permute-done.14.refs_14_), channel_id=1, source_target_pairs={{2,0},{4,2},{6,4},{7,6},{5,7},{3,5},{1,3},{0,1},{10,8},{12,10},{14... | collective-permute-start | bytes 393224 | tf_op jit(solution)/shard_map/ppermute | solution.py:40
  29.0 1.3 %copy-done.1 = bf16[1,64,10240]{2,1,0:T(8,128)(2,1)S(1)} copy-done((bf16[1,64,10240]{2,1,0:T(8,128)(2,1)S(1)}, bf16[1,64,10240]{2,1,0:T(8,128)(2,1)}, u32[]{:S(2)}) %copy-start.1) | copy-done | bytes 1310744
  30.3 1.2 %copy-done.2 = bf16[1,8192,64]{1,2,0:T(8,128)(2,1)S(1)} copy-done((bf16[1,8192,64]{1,2,0:T(8,128)(2,1)S(1)}, bf16[1,8192,64]{1,2,0:T(8,128)(2,1)}, u32[]{:S(2)}) %copy-start.2) | copy-done | bytes 1048600
  32.3 3.6 %lift.1 = (bf16[128,8192]{1,0:T(8,128)(2,1)S(1)}, bf16[8,32,1280]{2,1,0:T(8,128)(2,1)}) custom-call(s32[9]{0:T(128)S(1)} %stack.40.at_ref, s32[1,128]{1,0:T(1,128)S(1)} %bitcast.56, bf16[8192,128]{1,0:T(8,128)(2,1)S(1)} %get-tuple-element.11.down_ref, bf16[128,10240]{1,0:T(8,128)(2,1)S(1)} %get-tuple-element.12.up_ref, ...), custom_call_target="tpu_custom_call" | custom-call | flops 352321536 | bytes 4718592 | tf_op jit(solution)/shard_map/lift/pallas_call | solution.py:177
  35.9 6.3 %all-to-all-start = ((bf16[8,32,1280]{2,1,0:T(8,128)(2,1)}), bf16[8,32,1280]{2,1,0:T(8,128)(2,1)S(1)}, u32[]{:S(2)}, u32[]{:S(2)}) async-start(bf16[8,32,1280]{2,1,0:T(8,128)(2,1)} %get-tuple-element.16), calls=%async_computation | async-start | bytes 1310720 | tf_op jit(solution)/shard_map/all_to_all | solution.py:193
  42.2 8.6 %fusion.7.base_ref = f32[128,1280]{1,0:T(8,128)S(1)} fusion(bf16[128,8192]{1,0:T(8,128)(2,1)S(1)} %get-tuple-element.15, bf16[8192,1280]{1,0:T(8,128)(2,1)} %param.8), kind=kOutput, calls=%fused_computation.21 | convolution fusion | flops 2684354560 | bytes 23724032 | tf_op jit(solution)/shard_map/dot_general | solution.py:195
  50.8 3.4 %all-to-all-done = bf16[8,32,1280]{2,1,0:T(8,128)(2,1)S(1)} async-done(((bf16[8,32,1280]{2,1,0:T(8,128)(2,1)}), bf16[8,32,1280]{2,1,0:T(8,128)(2,1)S(1)}, u32[]{:S(2)}, u32[]{:S(2)}) %all-to-all-start) | async-done | bytes 655392 | tf_op jit(solution)/shard_map/all_to_all | solution.py:193
  54.1 1.0 %add.153 = bf16[128,1280]{1,0:T(8,128)(2,1)} custom-call(s32[128,1]{1,0:T(8,128)S(1)} %copy.9.place_ref, f32[128,1280]{1,0:T(8,128)S(1)} %fusion.7.base_ref, bf16[256,1280]{1,0:T(8,128)(2,1)S(1)} %bitcast.49), custom_call_target="tpu_custom_call" | custom-call | tf_op jit(solution)/shard_map/add/pallas_call | solution.py:196
  (30 shorter events, 4.7 us)
Async XLA Ops:
  0.0 21.1 %copy-start = (s32[2,12]{1,0:T(2,128)S(1)}, s32[2,12]{1,0:T(2,128)}, u32[]{:S(2)}) copy-start(s32[2,12]{1,0:T(2,128)} %param.11) | copy-start | bytes 292
  0.0 27.0 %collective-permute-start = (bf16[64,8192]{1,0:T(8,128)(2,1)}, bf16[64,8192]{1,0:T(8,128)(2,1)S(1)}, u32[]{:S(2)}, u32[]{:S(2)}) collective-permute-start(bf16[64,8192]{1,0:T(8,128)(2,1)} %bitcast.52), channel_id=1, source_target_pairs={{8,0},{0,8},{9,1},{1,9},{10,2},{2,10},{11,3},{3,11},{12,4},{4,12},... | collective-permute-start | bytes 3145736 | tf_op jit(solution)/shard_map/ppermute | solution.py:16
  0.5 28.5 %collective-permute-start.1 = (bf16[64,10240]{1,0:T(8,128)(2,1)}, bf16[64,10240]{1,0:T(8,128)(2,1)S(1)}, u32[]{:S(2)}, u32[]{:S(2)}) collective-permute-start(bf16[64,10240]{1,0:T(8,128)(2,1)} %bitcast.50), channel_id=1, source_target_pairs={{8,0},{0,8},{9,1},{1,9},{10,2},{2,10},{11,3},{3,11},{12,4},{4,12},... | collective-permute-start | bytes 3932168 | tf_op jit(solution)/shard_map/ppermute | solution.py:16
  0.5 0.9 %copy-start.3 = (bf16[1,16,8192]{2,1,0:T(8,128)(2,1)S(1)}, bf16[1,16,8192]{2,1,0:T(8,128)(2,1)}, u32[]{:S(2)}) copy-start(bf16[1,16,8192]{2,1,0:T(8,128)(2,1)} %param.7) | copy-start | bytes 786436
  1.5 6.8 %collective-permute-start.10 = (bf16[16,4096]{1,0:T(8,128)(2,1)S(1)}, bf16[16,4096]{1,0:T(8,128)(2,1)S(1)}, u32[]{:S(2)}, u32[]{:S(2)}) collective-permute-start(bf16[16,4096]{1,0:T(8,128)(2,1)S(1)} %get-tuple-element.14.refs_8_), channel_id=1, source_target_pairs={{2,0},{4,2},{6,4},{7,6},{5,7},{3,5},{1,3},{0,1},{10,8},{12,10},{14... | collective-permute-start | bytes 393224 | tf_op jit(solution)/shard_map/ppermute | solution.py:40
  4.5 6.4 %collective-permute-start.2 = (bf16[16,4096]{1,0:T(8,128)(2,1)S(1)}, bf16[16,4096]{1,0:T(8,128)(2,1)S(1)}, u32[]{:S(2)}, u32[]{:S(2)}) collective-permute-start(bf16[16,4096]{1,0:T(8,128)(2,1)S(1)} %get-tuple-element.13.refs_0_), channel_id=1, source_target_pairs={{0,2},{2,4},{4,6},{6,7},{7,5},{5,3},{3,1},{1,0},{8,10},{10,12},{12... | collective-permute-start | bytes 393224 | tf_op jit(solution)/shard_map/ppermute | solution.py:37
  4.6 7.9 %collective-permute-start.9 = (bf16[16,4096]{1,0:T(8,128)(2,1)S(1)}, bf16[16,4096]{1,0:T(8,128)(2,1)S(1)}, u32[]{:S(2)}, u32[]{:S(2)}) collective-permute-start(bf16[16,4096]{1,0:T(8,128)(2,1)S(1)} %get-tuple-element.14.refs_8_), channel_id=1, source_target_pairs={{0,2},{2,4},{4,6},{6,7},{7,5},{5,3},{3,1},{1,0},{8,10},{10,12},{12... | collective-permute-start | bytes 393224 | tf_op jit(solution)/shard_map/ppermute | solution.py:37
  8.3 6.4 %collective-permute-start.3 = (bf16[16,4096]{1,0:T(8,128)(2,1)S(1)}, bf16[16,4096]{1,0:T(8,128)(2,1)S(1)}, u32[]{:S(2)}, u32[]{:S(2)}) collective-permute-start(bf16[16,4096]{1,0:T(8,128)(2,1)S(1)} %get-tuple-element.13.refs_0_), channel_id=1, source_target_pairs={{2,0},{4,2},{6,4},{7,6},{5,7},{3,5},{1,3},{0,1},{10,8},{12,10},{14... | collective-permute-start | bytes 393224 | tf_op jit(solution)/shard_map/ppermute | solution.py:40
  10.9 5.2 %collective-permute-start.12 = (bf16[16,4096]{1,0:T(8,128)(2,1)S(1)}, bf16[16,4096]{1,0:T(8,128)(2,1)S(1)}, u32[]{:S(2)}, u32[]{:S(2)}) collective-permute-start(bf16[16,4096]{1,0:T(8,128)(2,1)S(1)} %collective-permute-done.10.refs_10_), channel_id=1, source_target_pairs={{2,0},{4,2},{6,4},{7,6},{5,7},{3,5},{1,3},{0,1},{10,8},{12,10},{14... | collective-permute-start | bytes 393224 | tf_op jit(solution)/shard_map/ppermute | solution.py:40
  12.5 5.7 %collective-permute-start.4 = (bf16[16,4096]{1,0:T(8,128)(2,1)S(1)}, bf16[16,4096]{1,0:T(8,128)(2,1)S(1)}, u32[]{:S(2)}, u32[]{:S(2)}) collective-permute-start(bf16[16,4096]{1,0:T(8,128)(2,1)S(1)} %collective-permute-done.2.refs_1_), channel_id=1, source_target_pairs={{0,2},{2,4},{4,6},{6,7},{7,5},{5,3},{3,1},{1,0},{8,10},{10,12},{12... | collective-permute-start | bytes 393224 | tf_op jit(solution)/shard_map/ppermute | solution.py:37
  14.7 5.2 %collective-permute-start.11 = (bf16[16,4096]{1,0:T(8,128)(2,1)S(1)}, bf16[16,4096]{1,0:T(8,128)(2,1)}, u32[]{:S(2)}, u32[]{:S(2)}) collective-permute-start(bf16[16,4096]{1,0:T(8,128)(2,1)S(1)} %collective-permute-done.9.refs_9_), channel_id=1, source_target_pairs={{0,2},{2,4},{4,6},{6,7},{7,5},{5,3},{3,1},{1,0},{8,10},{10,12},{12... | collective-permute-start | bytes 393224 | tf_op jit(solution)/shard_map/ppermute | solution.py:37
  16.1 6.8 %collective-permute-start.5 = (bf16[16,4096]{1,0:T(8,128)(2,1)S(1)}, bf16[16,4096]{1,0:T(8,128)(2,1)}, u32[]{:S(2)}, u32[]{:S(2)}) collective-permute-start(bf16[16,4096]{1,0:T(8,128)(2,1)S(1)} %collective-permute-done.3.refs_2_), channel_id=1, source_target_pairs={{2,0},{4,2},{6,4},{7,6},{5,7},{3,5},{1,3},{0,1},{10,8},{12,10},{14... | collective-permute-start | bytes 393224 | tf_op jit(solution)/shard_map/ppermute | solution.py:40
  18.2 6.5 %collective-permute-start.14 = (bf16[16,4096]{1,0:T(8,128)(2,1)S(1)}, bf16[16,4096]{1,0:T(8,128)(2,1)}, u32[]{:S(2)}, u32[]{:S(2)}) collective-permute-start(bf16[16,4096]{1,0:T(8,128)(2,1)S(1)} %collective-permute-done.12.refs_12_), channel_id=1, source_target_pairs={{2,0},{4,2},{6,4},{7,6},{5,7},{3,5},{1,3},{0,1},{10,8},{12,10},{14... | collective-permute-start | bytes 393224 | tf_op jit(solution)/shard_map/ppermute | solution.py:40
  19.8 6.0 %collective-permute-start.6 = (bf16[16,4096]{1,0:T(8,128)(2,1)S(1)}, bf16[16,4096]{1,0:T(8,128)(2,1)}, u32[]{:S(2)}, u32[]{:S(2)}) collective-permute-start(bf16[16,4096]{1,0:T(8,128)(2,1)S(1)} %collective-permute-done.4.refs_3_), channel_id=1, source_target_pairs={{0,2},{2,4},{4,6},{6,7},{7,5},{5,3},{3,1},{1,0},{8,10},{10,12},{12... | collective-permute-start | bytes 393224 | tf_op jit(solution)/shard_map/ppermute | solution.py:37
  22.8 9.4 %collective-permute-start.13 = (bf16[16,4096]{1,0:T(8,128)(2,1)}, bf16[16,4096]{1,0:T(8,128)(2,1)}, u32[]{:S(2)}, u32[]{:S(2)}) collective-permute-start(bf16[16,4096]{1,0:T(8,128)(2,1)} %collective-permute-done.11.refs_11_), channel_id=1, source_target_pairs={{0,2},{2,4},{4,6},{6,7},{7,5},{5,3},{3,1},{1,0},{8,10},{10,12},{12... | collective-permute-start | bytes 393224 | tf_op jit(solution)/shard_map/ppermute | solution.py:37
  24.8 7.5 %collective-permute-start.7 = (bf16[16,4096]{1,0:T(8,128)(2,1)}, bf16[16,4096]{1,0:T(8,128)(2,1)}, u32[]{:S(2)}, u32[]{:S(2)}) collective-permute-start(bf16[16,4096]{1,0:T(8,128)(2,1)} %collective-permute-done.5.refs_4_), channel_id=1, source_target_pairs={{2,0},{4,2},{6,4},{7,6},{5,7},{3,5},{1,3},{0,1},{10,8},{12,10},{14... | collective-permute-start | bytes 393224 | tf_op jit(solution)/shard_map/ppermute | solution.py:40
  25.8 6.5 %collective-permute-start.15 = (bf16[16,4096]{1,0:T(8,128)(2,1)}, bf16[16,4096]{1,0:T(8,128)(2,1)}, u32[]{:S(2)}, u32[]{:S(2)}) collective-permute-start(bf16[16,4096]{1,0:T(8,128)(2,1)} %collective-permute-done.14.refs_14_), channel_id=1, source_target_pairs={{2,0},{4,2},{6,4},{7,6},{5,7},{3,5},{1,3},{0,1},{10,8},{12,10},{14... | collective-permute-start | bytes 393224 | tf_op jit(solution)/shard_map/ppermute | solution.py:40
  27.0 5.3 %collective-permute-start.8 = (bf16[16,4096]{1,0:T(8,128)(2,1)}, bf16[16,4096]{1,0:T(8,128)(2,1)}, u32[]{:S(2)}, u32[]{:S(2)}) collective-permute-start(bf16[16,4096]{1,0:T(8,128)(2,1)} %collective-permute-done.6.refs_5_), channel_id=1, source_target_pairs={{0,2},{2,4},{4,6},{6,7},{7,5},{5,3},{3,1},{1,0},{8,10},{10,12},{12... | collective-permute-start | bytes 393224 | tf_op jit(solution)/shard_map/ppermute | solution.py:37
  29.0 1.3 %copy-start.1 = (bf16[1,64,10240]{2,1,0:T(8,128)(2,1)S(1)}, bf16[1,64,10240]{2,1,0:T(8,128)(2,1)}, u32[]{:S(2)}) copy-start(bf16[1,64,10240]{2,1,0:T(8,128)(2,1)} %param.10) | copy-start | bytes 3932164
  30.3 1.2 %copy-start.2 = (bf16[1,8192,64]{1,2,0:T(8,128)(2,1)S(1)}, bf16[1,8192,64]{1,2,0:T(8,128)(2,1)}, u32[]{:S(2)}) copy-start(bf16[1,8192,64]{1,2,0:T(8,128)(2,1)} %param.9) | copy-start | bytes 3145732
  35.9 18.2 %all-to-all-start = ((bf16[8,32,1280]{2,1,0:T(8,128)(2,1)}), bf16[8,32,1280]{2,1,0:T(8,128)(2,1)S(1)}, u32[]{:S(2)}, u32[]{:S(2)}) async-start(bf16[8,32,1280]{2,1,0:T(8,128)(2,1)} %get-tuple-element.16), calls=%async_computation | async-start | bytes 1310720 | tf_op jit(solution)/shard_map/all_to_all | solution.py:193

commit v7 on v6

--- a/solution.py
+++ b/solution.py
@@ -22,29 +22,28 @@
 
 
 class Ring:
-    def __init__(self, block, axis, last_from_behind):
+    def __init__(self, block, axis):
         n = lax.axis_size(axis)
         ring = ring_of(n)
-        self.n, self.axis, self.last_from_behind = n, axis, last_from_behind
+        self.n, self.axis = n, axis
         self.up = [(ring[i], ring[(i + 1) % n]) for i in range(n)]
         self.down = [(ring[(i + 1) % n], ring[i]) for i in range(n)]
         self.ahead = self.behind = block
         self.pieces = [block]
 
     def step(self, i):
-        last = i == self.n // 2
-        if not last or self.last_from_behind:
-            self.ahead = lax.ppermute(self.ahead, self.axis, self.up)
-            self.pieces.append(self.ahead)
-        if not last or not self.last_from_behind:
-            self.behind = lax.ppermute(self.behind, self.axis, self.down)
-            self.pieces.append(self.behind)
-
-    def wait_for(self, value):
-        self.ahead, self.behind, value = lax.optimization_barrier(
-            (self.ahead, self.behind, value)
+        if i == self.n // 2:
+            half = self.ahead.shape[1] // 2
+            self.ahead, self.behind = self.ahead[:, :half], self.behind[:, half:]
+        self.ahead = lax.ppermute(self.ahead, self.axis, self.up)
+        self.behind = lax.ppermute(self.behind, self.axis, self.down)
+        self.pieces += [self.ahead, self.behind]
+
+    def wait_for(self, *values):
+        self.ahead, self.behind, *values = lax.optimization_barrier(
+            (self.ahead, self.behind, *values)
         )
-        return value
+        return values
 
 
 def ring_sources(axis):
@@ -59,12 +58,6 @@
     return sources
 
 
-def halve_kernel(block_ref, *out_refs):
-    width = out_refs[0].shape[1]
-    for i, out_ref in enumerate(out_refs):
-        out_ref[...] = block_ref[:, i * width : (i + 1) * width]
-
-
 def stack_kernel(groups, *refs):
     downs, ups, (down_ref, up_ref) = refs[:groups], refs[groups:-2], refs[-2:]
     rank = ups[0].shape[0]
@@ -75,12 +68,13 @@
 
 def lift_kernel(tp, at_ref, place_ref, down_ref, up_ref, *refs):
     pieces, (tokens_ref, out_ref) = refs[:-2], refs[-2:]
-    rows, width = pieces[0].shape
-    per_half = len(pieces) // 2
+    rows, half = pieces[-1].shape
     for i, piece in enumerate(pieces):
-        start = pl.multiple_of(at_ref[1 + i % per_half] * rows, rows)
-        column = i // per_half * width
-        tokens_ref[pl.ds(start, rows), column : column + width] = piece[...]
+        opposite = i >= len(pieces) - 2
+        start = pl.multiple_of(at_ref[1 + min(i, len(pieces) - 2)] * rows, rows)
+        column = half if i == len(pieces) - 1 else 0
+        size = half if opposite else 2 * half
+        tokens_ref[pl.ds(start, rows), column : column + size] = piece[...]
     low = jnp.dot(tokens_ref[...], down_ref[...], preferred_element_type=jnp.float32)
     low = low.astype(jnp.bfloat16)
     slots, columns = out_ref.shape[1], out_ref.shape[2]
@@ -126,23 +120,13 @@
     tok_all = tokens.shape[1] * tp
     longest = tok_all // 8
     here = groups * longest
-    half = width // 2
     in_vmem = pl.BlockSpec(memory_space=pltpu.VMEM)
     in_smem = pl.BlockSpec(memory_space=pltpu.SMEM)
     small = pltpu.CompilerParams(vmem_limit_bytes=16 * 2**20)
 
-    halves = pl.pallas_call(
-        halve_kernel,
-        out_shape=[jax.ShapeDtypeStruct((tokens.shape[1], half), jnp.bfloat16)] * 2,
-        in_specs=[in_vmem],
-        out_specs=[in_vmem] * 2,
-        compiler_params=small,
-        name="halve",
-    )(tokens[0])
-    rings = [Ring(part, "tp", k == 0) for k, part in enumerate(halves)]
-    for i in range(1, tp // 2 + 1):
-        for ring in rings:
-            ring.step(i)
+    ring = Ring(tokens[0], "tp")
+    ring.step(1)
+    ring.step(2)
 
     down_stack, up_stack = pl.pallas_call(
         functools.partial(stack_kernel, groups),
@@ -174,13 +158,16 @@
     place = jnp.sum(jnp.where(member, first[None, :] + position, 0), axis=1)
 
     at = jnp.stack([my_tp * here] + ring_sources("tp")).astype(jnp.int32)
+    down_stack, up_stack, place, at = ring.wait_for(down_stack, up_stack, place, at)
+    for i in range(3, tp // 2 + 1):
+        ring.step(i)
     gathered, lifts = pl.pallas_call(
         functools.partial(lift_kernel, tp),
         out_shape=[
             jax.ShapeDtypeStruct((tok_all, width), jnp.bfloat16),
             jax.ShapeDtypeStruct((tp, here, columns), jnp.bfloat16),
         ],
-        in_specs=[in_smem] + [in_vmem] * (3 + 2 * tp),
+        in_specs=[in_smem] + [in_vmem] * (3 + len(ring.pieces)),
         out_specs=[in_vmem] * 2,
         compiler_params=pltpu.CompilerParams(vmem_limit_bytes=24 * 2**20),
         cost_estimate=pl.CostEstimate(
@@ -189,7 +176,7 @@
             transcendentals=0,
         ),
         name="lift",
-    )(at, place[None, :], down_stack, up_stack, *rings[0].pieces, *rings[1].pieces)
+    )(at, place[None, :], down_stack, up_stack, *ring.pieces)
     lifts = lax.all_to_all(lifts, "tp", split_axis=0, concat_axis=0, tiled=True)
 
     base = jnp.dot(gathered, base_projection_weight, preferred_element_type=jnp.float32)

time: 55.5 us -> 64 us (1.15)
  starting transfers between devices: 25.4 us -> 14.6 us
  local copies, waits for them, and re-layouts: 3.7 us -> 14 us
  waiting for transfers between devices: 9.43 us -> 19.3 us
  Pallas kernels: 5.34 us -> 4.6 us
    unnamed x8 -> x32, local copies, waits for them, and re-layouts: 3.49 us -> 13.8 us
    ppermute x7 -> x4, waiting for transfers between devices: 2.63 us -> 12.8 us  [step(): self.ahead = lax.ppermute(self.ahead, self.axis, self.up)]
    ppermute x7 -> x4, starting transfers between devices: 10.6 us -> 1.05 us  [step(): self.behind = lax.ppermute(self.behind, self.axis, self.down)]
    ppermute x7 -> x4, waiting for transfers between devices: 3.45 us -> 0.92 us  [step(): self.behind = lax.ppermute(self.behind, self.axis, self.down)]
    all_to_all x1, waiting for transfers between devices: 3.35 us -> 5.5 us  [on_device(): lifts = lax.all_to_all(lifts, 'tp', split_axis=0, concat_axis=0, tiled=True)]
    all_to_all x1, starting transfers between devices: 6.3 us -> 4.83 us  [on_device(): lifts = lax.all_to_all(lifts, 'tp', split_axis=0, concat_axis=0, tiled=True)]
    pallas_call x1, Pallas kernels: 3.58 us -> 2.86 us  [on_device(): pl.pallas_call(functools.partial(lift_kernel, tp), out_shape=[jax.ShapeDt...]
    ppermute x7 -> x4, starting transfers between devices: 8.01 us -> 8.2 us  [step(): self.ahead = lax.ppermute(self.ahead, self.axis, self.up)]
  transfers between devices with their start and end apart: 17 -> 11, of which waited for: 6 -> 5; matrix products, arithmetic and copies ran while one was open for 20% -> 18% of each run, Pallas kernels for 1% -> 1%
where the time goes in v7:
time: 64 us; the launch traced here: 63.6 us
  waiting for transfers between devices  19.3 us (30%)
  starting transfers between devices  14.6 us (23%)
  local copies, waits for them, and re-layouts  14 us (22%)
  matrix products  8.55 us (13%)
  Pallas kernels  4.6 us (7%)
  other arithmetic  2.44 us (4%)
    unnamed x32, local copies, waits for them, and re-layouts  13.8 us
    ppermute x4, waiting for transfers between devices, step(): self.ahead = lax.ppermute(self.ahead, self.axis, self.up)  12.8 us
    dot_general x1, matrix products, on_device(): jnp.dot(gathered, base_projection_weight, preferred_element_type=jnp.floa...  8.55 us
    ppermute x4, starting transfers between devices, step(): self.ahead = lax.ppermute(self.ahead, self.axis, self.up)  8.2 us
    all_to_all x1, waiting for transfers between devices, on_device(): lifts = lax.all_to_all(lifts, 'tp', split_axis=0, concat_axis=0, tiled=True)  5.5 us
    all_to_all x1, starting transfers between devices, on_device(): lifts = lax.all_to_all(lifts, 'tp', split_axis=0, concat_axis=0, tiled=True)  4.83 us
    pallas_call x1, Pallas kernels, on_device(): pl.pallas_call(functools.partial(lift_kernel, tp), out_shape=[jax.ShapeDt...  2.86 us
  transfers between devices with their start and end apart: 11, of which 5 were waited for; matrix products, arithmetic and copies ran while one was open for 18% of the time, Pallas kernels for 1%

profile of v7, /device:TPU:0, one launch (start us, length us, event | category | flops | bytes accessed | tf_op | source)
XLA Modules:
  0.0 63.6 jit_solution(10092685372053046121)
XLA Ops:
  0.5 3.0 %collective-permute-start = (bf16[16,8192]{1,0:T(8,128)(2,1)}, bf16[16,8192]{1,0:T(8,128)(2,1)S(1)}, u32[]{:S(2)}, u32[]{:S(2)}) collective-permute-start(bf16[16,8192]{1,0:T(8,128)(2,1)} %bitcast.54), channel_id=1, source_target_pairs={{0,2},{2,4},{4,6},{6,7},{7,5},{5,3},{3,1},{1,0},{8,10},{10,12},{12... | collective-permute-start | bytes 786440 | tf_op jit(solution)/shard_map/ppermute | solution.py:38
  4.5 0.8 %select_reduce_fusion.1 = s32[12]{0:T(128)S(1)} fusion(s32[16]{0:T(128)} %param.13, s32[12]{0:T(128)S(1)} %dynamic-slice_bitcast_fusion), kind=kLoop, calls=%fused_computation.1 | loop fusion | flops 564 | bytes 160 | tf_op jit(solution)/shard_map/reduce_sum | solution.py:148
  5.3 4.9 %collective-permute-done.refs_1_ = bf16[16,8192]{1,0:T(8,128)(2,1)S(1)} collective-permute-done((bf16[16,8192]{1,0:T(8,128)(2,1)}, bf16[16,8192]{1,0:T(8,128)(2,1)S(1)}, u32[]{:S(2)}, u32[]{:S(2)}) %collective-permute-start) | collective-permute-done | bytes 262176 | tf_op jit(solution)/shard_map/ppermute | solution.py:38
  10.2 1.8 %collective-permute-start.1 = (bf16[16,8192]{1,0:T(8,128)(2,1)S(1)}, bf16[16,8192]{1,0:T(8,128)(2,1)S(1)}, u32[]{:S(2)}, u32[]{:S(2)}) collective-permute-start(bf16[16,8192]{1,0:T(8,128)(2,1)S(1)} %collective-permute-done.refs_1_), channel_id=1, source_target_pairs={{0,2},{2,4},{4,6},{6,7},{7,5},{5,3},{3,1},{1,0},{8,10},{10,12},{12... | collective-permute-start | bytes 786440 | tf_op jit(solution)/shard_map/ppermute | solution.py:38
  13.1 1.3 %copy-done.5 = bf16[1,64,10240]{2,1,0:T(8,128)(2,1)S(1)} copy-done((bf16[1,64,10240]{2,1,0:T(8,128)(2,1)S(1)}, bf16[1,64,10240]{2,1,0:T(8,128)(2,1)}, u32[]{:S(2)}) %copy-start.5) | copy-done | bytes 1310744
  14.4 1.2 %copy-done.6 = bf16[1,8192,64]{1,2,0:T(8,128)(2,1)S(1)} copy-done((bf16[1,8192,64]{1,2,0:T(8,128)(2,1)S(1)}, bf16[1,8192,64]{1,2,0:T(8,128)(2,1)}, u32[]{:S(2)}) %copy-start.6) | copy-done | bytes 1048600
  16.3 1.5 %copy-done.1 = bf16[128,10240]{1,0:T(8,128)(2,1)} copy-done((bf16[128,10240]{1,0:T(8,128)(2,1)}, bf16[128,10240]{1,0:T(8,128)(2,1)S(1)}, u32[]{:S(2)}) %copy-start.1) | copy-done | bytes 2621464
  17.8 1.4 %copy-done.3 = bf16[8192,128]{1,0:T(8,128)(2,1)} copy-done((bf16[8192,128]{1,0:T(8,128)(2,1)}, bf16[8192,128]{1,0:T(8,128)(2,1)S(1)}, u32[]{:S(2)}) %copy-start.3) | copy-done | bytes 2097176
  19.2 1.9 %collective-permute-start.6 = (bf16[16,8192]{1,0:T(8,128)(2,1)S(1)}, bf16[16,8192]{1,0:T(8,128)(2,1)S(1)}, u32[]{:S(2)}, u32[]{:S(2)}) collective-permute-start(bf16[16,8192]{1,0:T(8,128)(2,1)S(1)} %collective-permute-done.1.refs_3_), channel_id=1, source_target_pairs={{0,2},{2,4},{4,6},{6,7},{7,5},{5,3},{3,1},{1,0},{8,10},{10,12},{12... | collective-permute-start | bytes 786440 | tf_op jit(solution)/shard_map/ppermute | solution.py:38
  21.3 5.2 %collective-permute-done.6.refs_5_ = bf16[16,8192]{1,0:T(8,128)(2,1)S(1)} collective-permute-done((bf16[16,8192]{1,0:T(8,128)(2,1)S(1)}, bf16[16,8192]{1,0:T(8,128)(2,1)S(1)}, u32[]{:S(2)}, u32[]{:S(2)}) %collective-permute-start.6) | collective-permute-done | bytes 262176 | tf_op jit(solution)/shard_map/ppermute | solution.py:38
  26.5 1.5 %collective-permute-start.8 = (bf16[16,4096]{1,0:T(8,128)(2,1)S(1)}, bf16[16,4096]{1,0:T(8,128)(2,1)S(1)}, u32[]{:S(2)}, u32[]{:S(2)}) collective-permute-start(bf16[16,4096]{1,0:T(8,128)(2,1)S(1)} %slice.8), channel_id=1, source_target_pairs={{0,2},{2,4},{4,6},{6,7},{7,5},{5,3},{3,1},{1,0},{8,10},{10,12},{12... | collective-permute-start | bytes 393224 | tf_op jit(solution)/shard_map/ppermute | solution.py:38
  28.7 2.7 %collective-permute-done.8.refs_7_ = bf16[16,4096]{1,0:T(8,128)(2,1)S(1)} collective-permute-done((bf16[16,4096]{1,0:T(8,128)(2,1)S(1)}, bf16[16,4096]{1,0:T(8,128)(2,1)S(1)}, u32[]{:S(2)}, u32[]{:S(2)}) %collective-permute-start.8) | collective-permute-done | bytes 131104 | tf_op jit(solution)/shard_map/ppermute | solution.py:38
  32.1 0.9 %collective-permute-done.9.refs_8_ = bf16[16,4096]{1,0:T(8,128)(2,1)S(1)} collective-permute-done((bf16[16,4096]{1,0:T(8,128)(2,1)S(1)}, bf16[16,4096]{1,0:T(8,128)(2,1)S(1)}, u32[]{:S(2)}, u32[]{:S(2)}) %collective-permute-start.9) | collective-permute-done | bytes 131104 | tf_op jit(solution)/shard_map/ppermute | solution.py:39
  33.7 1.7 %copy-done.2 = bf16[128,10240]{1,0:T(8,128)(2,1)S(1)} copy-done((bf16[128,10240]{1,0:T(8,128)(2,1)S(1)}, bf16[128,10240]{1,0:T(8,128)(2,1)}, u32[]{:S(2)}) %copy-start.2) | copy-done | bytes 2621464
  35.5 1.6 %copy-done.4 = bf16[8192,128]{1,0:T(8,128)(2,1)S(1)} copy-done((bf16[8192,128]{1,0:T(8,128)(2,1)S(1)}, bf16[8192,128]{1,0:T(8,128)(2,1)}, u32[]{:S(2)}) %copy-start.4) | copy-done | bytes 2097176
  37.1 0.9 %copy-done.9 = bf16[16,8192]{1,0:T(8,128)(2,1)S(1)} copy-done((bf16[16,8192]{1,0:T(8,128)(2,1)S(1)}, bf16[16,8192]{1,0:T(8,128)(2,1)}, u32[]{:S(2)}) %copy-start.9) | copy-done | bytes 262168
  38.0 0.9 %copy-done.11 = bf16[16,8192]{1,0:T(8,128)(2,1)S(1)} copy-done((bf16[16,8192]{1,0:T(8,128)(2,1)S(1)}, bf16[16,8192]{1,0:T(8,128)(2,1)}, u32[]{:S(2)}) %copy-start.11) | copy-done | bytes 262168
  39.0 0.9 %copy-done.13 = bf16[16,4096]{1,0:T(8,128)(2,1)S(1)} copy-done((bf16[16,4096]{1,0:T(8,128)(2,1)S(1)}, bf16[16,4096]{1,0:T(8,128)(2,1)}, u32[]{:S(2)}) %copy-start.13) | copy-done | bytes 131096
  39.9 0.9 %copy-done.15 = bf16[16,4096]{1,0:T(8,128)(2,1)S(1)} copy-done((bf16[16,4096]{1,0:T(8,128)(2,1)S(1)}, bf16[16,4096]{1,0:T(8,128)(2,1)}, u32[]{:S(2)}) %copy-start.15) | copy-done | bytes 131096
  40.8 2.9 %lift.1 = (bf16[128,8192]{1,0:T(8,128)(2,1)S(1)}, bf16[8,32,1280]{2,1,0:T(8,128)(2,1)}) custom-call(s32[9]{0:T(128)S(1)} %stack.40.at_ref, s32[1,128]{1,0:T(1,128)S(1)} %bitcast.58, bf16[8192,128]{1,0:T(8,128)(2,1)S(1)} %copy-done.4, bf16[128,10240]{1,0:T(8,128)(2,1)S(1)} %copy-done.2, bf16[16,8192]{1,0:T(8,128)(2,1)S(1)} %bitcast.56, ...), custom_call_target="tpu_custom_call" | custom-call | flops 352321536 | bytes 4718592 | tf_op jit(solution)/shard_map/lift/pallas_call | solution.py:164
  43.6 4.8 %all-to-all-start = ((bf16[8,32,1280]{2,1,0:T(8,128)(2,1)}), bf16[8,32,1280]{2,1,0:T(8,128)(2,1)S(1)}, u32[]{:S(2)}, u32[]{:S(2)}) async-start(bf16[8,32,1280]{2,1,0:T(8,128)(2,1)} %get-tuple-element.24), calls=%async_computation | async-start | bytes 1310720 | tf_op jit(solution)/shard_map/all_to_all | solution.py:180
  48.5 8.6 %fusion.7.base_ref = f32[128,1280]{1,0:T(8,128)S(1)} fusion(bf16[128,8192]{1,0:T(8,128)(2,1)S(1)} %get-tuple-element.23, bf16[8192,1280]{1,0:T(8,128)(2,1)} %param.8), kind=kOutput, calls=%fused_computation.21 | convolution fusion | flops 2684354560 | bytes 23724032 | tf_op jit(solution)/shard_map/dot_general | solution.py:182
  57.0 5.5 %all-to-all-done = bf16[8,32,1280]{2,1,0:T(8,128)(2,1)S(1)} async-done(((bf16[8,32,1280]{2,1,0:T(8,128)(2,1)}), bf16[8,32,1280]{2,1,0:T(8,128)(2,1)S(1)}, u32[]{:S(2)}, u32[]{:S(2)}) %all-to-all-start) | async-done | bytes 655392 | tf_op jit(solution)/shard_map/all_to_all | solution.py:180
  62.5 1.0 %add.153 = bf16[128,1280]{1,0:T(8,128)(2,1)} custom-call(s32[128,1]{1,0:T(8,128)S(1)} %copy.9.place_ref, f32[128,1280]{1,0:T(8,128)S(1)} %fusion.7.base_ref, bf16[256,1280]{1,0:T(8,128)(2,1)S(1)} %bitcast.49), custom_call_target="tpu_custom_call" | custom-call | tf_op jit(solution)/shard_map/add/pallas_call | solution.py:183
  (43 shorter events, 5.5 us)
Async XLA Ops:
  0.0 4.5 %copy-start = (s32[2,12]{1,0:T(2,128)S(1)}, s32[2,12]{1,0:T(2,128)}, u32[]{:S(2)}) copy-start(s32[2,12]{1,0:T(2,128)} %param.11) | copy-start | bytes 292
  0.0 13.0 %collective-permute-start.5 = (bf16[64,10240]{1,0:T(8,128)(2,1)}, bf16[64,10240]{1,0:T(8,128)(2,1)S(1)}, u32[]{:S(2)}, u32[]{:S(2)}) collective-permute-start(bf16[64,10240]{1,0:T(8,128)(2,1)} %bitcast.50), channel_id=1, source_target_pairs={{8,0},{0,8},{9,1},{1,9},{10,2},{2,10},{11,3},{3,11},{12,4},{4,12},... | collective-permute-start | bytes 3932168 | tf_op jit(solution)/shard_map/ppermute | solution.py:16
  0.5 12.6 %collective-permute-start.4 = (bf16[64,8192]{1,0:T(8,128)(2,1)}, bf16[64,8192]{1,0:T(8,128)(2,1)S(1)}, u32[]{:S(2)}, u32[]{:S(2)}) collective-permute-start(bf16[64,8192]{1,0:T(8,128)(2,1)} %bitcast.52), channel_id=1, source_target_pairs={{8,0},{0,8},{9,1},{1,9},{10,2},{2,10},{11,3},{3,11},{12,4},{4,12},... | collective-permute-start | bytes 3145736 | tf_op jit(solution)/shard_map/ppermute | solution.py:16
  0.5 9.7 %collective-permute-start = (bf16[16,8192]{1,0:T(8,128)(2,1)}, bf16[16,8192]{1,0:T(8,128)(2,1)S(1)}, u32[]{:S(2)}, u32[]{:S(2)}) collective-permute-start(bf16[16,8192]{1,0:T(8,128)(2,1)} %bitcast.54), channel_id=1, source_target_pairs={{0,2},{2,4},{4,6},{6,7},{7,5},{5,3},{3,1},{1,0},{8,10},{10,12},{12... | collective-permute-start | bytes 786440 | tf_op jit(solution)/shard_map/ppermute | solution.py:38
  3.5 8.5 %collective-permute-start.2 = (bf16[16,8192]{1,0:T(8,128)(2,1)}, bf16[16,8192]{1,0:T(8,128)(2,1)S(1)}, u32[]{:S(2)}, u32[]{:S(2)}) collective-permute-start(bf16[16,8192]{1,0:T(8,128)(2,1)} %bitcast.55), channel_id=1, source_target_pairs={{2,0},{4,2},{6,4},{7,6},{5,7},{3,5},{1,3},{0,1},{10,8},{12,10},{14... | collective-permute-start | bytes 786440 | tf_op jit(solution)/shard_map/ppermute | solution.py:39
  10.2 9.0 %collective-permute-start.1 = (bf16[16,8192]{1,0:T(8,128)(2,1)S(1)}, bf16[16,8192]{1,0:T(8,128)(2,1)S(1)}, u32[]{:S(2)}, u32[]{:S(2)}) collective-permute-start(bf16[16,8192]{1,0:T(8,128)(2,1)S(1)} %collective-permute-done.refs_1_), channel_id=1, source_target_pairs={{0,2},{2,4},{4,6},{6,7},{7,5},{5,3},{3,1},{1,0},{8,10},{10,12},{12... | collective-permute-start | bytes 786440 | tf_op jit(solution)/shard_map/ppermute | solution.py:38
  12.0 7.2 %collective-permute-start.3 = (bf16[16,8192]{1,0:T(8,128)(2,1)S(1)}, bf16[16,8192]{1,0:T(8,128)(2,1)S(1)}, u32[]{:S(2)}, u32[]{:S(2)}) collective-permute-start(bf16[16,8192]{1,0:T(8,128)(2,1)S(1)} %collective-permute-done.2.refs_2_), channel_id=1, source_target_pairs={{2,0},{4,2},{6,4},{7,6},{5,7},{3,5},{1,3},{0,1},{10,8},{12,10},{14... | collective-permute-start | bytes 786440 | tf_op jit(solution)/shard_map/ppermute | solution.py:39
  13.0 1.3 %copy-start.5 = (bf16[1,64,10240]{2,1,0:T(8,128)(2,1)S(1)}, bf16[1,64,10240]{2,1,0:T(8,128)(2,1)}, u32[]{:S(2)}) copy-start(bf16[1,64,10240]{2,1,0:T(8,128)(2,1)} %param.10) | copy-start | bytes 3932164
  14.4 1.2 %copy-start.6 = (bf16[1,8192,64]{1,2,0:T(8,128)(2,1)S(1)}, bf16[1,8192,64]{1,2,0:T(8,128)(2,1)}, u32[]{:S(2)}) copy-start(bf16[1,8192,64]{1,2,0:T(8,128)(2,1)} %param.9) | copy-start | bytes 3145732
  15.6 18.1 %copy-start.7 = (bf16[1,16,8192]{2,1,0:T(8,128)(2,1)S(1)}, bf16[1,16,8192]{2,1,0:T(8,128)(2,1)}, u32[]{:S(2)}) copy-start(bf16[1,16,8192]{2,1,0:T(8,128)(2,1)} %param.7) | copy-start | bytes 786436
  16.3 1.5 %copy-start.1 = (bf16[128,10240]{1,0:T(8,128)(2,1)}, bf16[128,10240]{1,0:T(8,128)(2,1)S(1)}, u32[]{:S(2)}) copy-start(bf16[128,10240]{1,0:T(8,128)(2,1)S(1)} %get-tuple-element.20.up_ref) | copy-start | bytes 7864324
  17.8 1.4 %copy-start.3 = (bf16[8192,128]{1,0:T(8,128)(2,1)}, bf16[8192,128]{1,0:T(8,128)(2,1)S(1)}, u32[]{:S(2)}) copy-start(bf16[8192,128]{1,0:T(8,128)(2,1)S(1)} %get-tuple-element.19.down_ref) | copy-start | bytes 6291460
  19.2 8.8 %copy-start.8 = (bf16[16,8192]{1,0:T(8,128)(2,1)}, bf16[16,8192]{1,0:T(8,128)(2,1)S(1)}, u32[]{:S(2)}) copy-start(bf16[16,8192]{1,0:T(8,128)(2,1)S(1)} %collective-permute-done.1.refs_3_) | copy-start | bytes 786436
  19.2 8.8 %copy-start.10 = (bf16[16,8192]{1,0:T(8,128)(2,1)}, bf16[16,8192]{1,0:T(8,128)(2,1)S(1)}, u32[]{:S(2)}) copy-start(bf16[16,8192]{1,0:T(8,128)(2,1)S(1)} %collective-permute-done.3.refs_4_) | copy-start | bytes 786436
  19.2 7.3 %collective-permute-start.6 = (bf16[16,8192]{1,0:T(8,128)(2,1)S(1)}, bf16[16,8192]{1,0:T(8,128)(2,1)S(1)}, u32[]{:S(2)}, u32[]{:S(2)}) collective-permute-start(bf16[16,8192]{1,0:T(8,128)(2,1)S(1)} %collective-permute-done.1.refs_3_), channel_id=1, source_target_pairs={{0,2},{2,4},{4,6},{6,7},{7,5},{5,3},{3,1},{1,0},{8,10},{10,12},{12... | collective-permute-start | bytes 786440 | tf_op jit(solution)/shard_map/ppermute | solution.py:38
  21.1 7.0 %collective-permute-start.7 = (bf16[16,8192]{1,0:T(8,128)(2,1)S(1)}, bf16[16,8192]{1,0:T(8,128)(2,1)S(1)}, u32[]{:S(2)}, u32[]{:S(2)}) collective-permute-start(bf16[16,8192]{1,0:T(8,128)(2,1)S(1)} %collective-permute-done.3.refs_4_), channel_id=1, source_target_pairs={{2,0},{4,2},{6,4},{7,6},{5,7},{3,5},{1,3},{0,1},{10,8},{12,10},{14... | collective-permute-start | bytes 786440 | tf_op jit(solution)/shard_map/ppermute | solution.py:39
  26.5 5.0 %collective-permute-start.8 = (bf16[16,4096]{1,0:T(8,128)(2,1)S(1)}, bf16[16,4096]{1,0:T(8,128)(2,1)S(1)}, u32[]{:S(2)}, u32[]{:S(2)}) collective-permute-start(bf16[16,4096]{1,0:T(8,128)(2,1)S(1)} %slice.8), channel_id=1, source_target_pairs={{0,2},{2,4},{4,6},{6,7},{7,5},{5,3},{3,1},{1,0},{8,10},{10,12},{12... | collective-permute-start | bytes 393224 | tf_op jit(solution)/shard_map/ppermute | solution.py:38
  28.0 5.0 %collective-permute-start.9 = (bf16[16,4096]{1,0:T(8,128)(2,1)S(1)}, bf16[16,4096]{1,0:T(8,128)(2,1)S(1)}, u32[]{:S(2)}, u32[]{:S(2)}) collective-permute-start(bf16[16,4096]{1,0:T(8,128)(2,1)S(1)} %slice.9), channel_id=1, source_target_pairs={{2,0},{4,2},{6,4},{7,6},{5,7},{3,5},{1,3},{0,1},{10,8},{12,10},{14... | collective-permute-start | bytes 393224 | tf_op jit(solution)/shard_map/ppermute | solution.py:39
  33.7 1.7 %copy-start.2 = (bf16[128,10240]{1,0:T(8,128)(2,1)S(1)}, bf16[128,10240]{1,0:T(8,128)(2,1)}, u32[]{:S(2)}) copy-start(bf16[128,10240]{1,0:T(8,128)(2,1)} %copy-done.1) | copy-start | bytes 7864324
  35.5 1.6 %copy-start.4 = (bf16[8192,128]{1,0:T(8,128)(2,1)S(1)}, bf16[8192,128]{1,0:T(8,128)(2,1)}, u32[]{:S(2)}) copy-start(bf16[8192,128]{1,0:T(8,128)(2,1)} %copy-done.3) | copy-start | bytes 6291460
  37.1 0.9 %copy-start.9 = (bf16[16,8192]{1,0:T(8,128)(2,1)S(1)}, bf16[16,8192]{1,0:T(8,128)(2,1)}, u32[]{:S(2)}) copy-start(bf16[16,8192]{1,0:T(8,128)(2,1)} %copy-done.8) | copy-start | bytes 786436
  38.0 0.9 %copy-start.11 = (bf16[16,8192]{1,0:T(8,128)(2,1)S(1)}, bf16[16,8192]{1,0:T(8,128)(2,1)}, u32[]{:S(2)}) copy-start(bf16[16,8192]{1,0:T(8,128)(2,1)} %copy-done.10) | copy-start | bytes 786436
  39.0 0.9 %copy-start.13 = (bf16[16,4096]{1,0:T(8,128)(2,1)S(1)}, bf16[16,4096]{1,0:T(8,128)(2,1)}, u32[]{:S(2)}) copy-start(bf16[16,4096]{1,0:T(8,128)(2,1)} %copy-done.12) | copy-start | bytes 393220
  43.6 18.9 %all-to-all-start = ((bf16[8,32,1280]{2,1,0:T(8,128)(2,1)}), bf16[8,32,1280]{2,1,0:T(8,128)(2,1)S(1)}, u32[]{:S(2)}, u32[]{:S(2)}) async-start(bf16[8,32,1280]{2,1,0:T(8,128)(2,1)} %get-tuple-element.24), calls=%async_computation | async-start | bytes 1310720 | tf_op jit(solution)/shard_map/all_to_all | solution.py:180
  (3 other events, 2.2 us)

commit v8 on v7

v8 whole, which is shorter than its diff:
```python
import functools

import jax
import jax.numpy as jnp
from jax import lax
from jax.experimental import pallas as pl
from jax.experimental.pallas import tpu as pltpu
from jax.sharding import PartitionSpec as P

adapter_scale = 1.0


def swapped(x, axis):
    n = lax.axis_size(axis)
    return [x] + [
        lax.ppermute(x, axis, [((i + s) % n, i) for i in range(n)]) for s in range(1, n)
    ]


def ring_of(n):
    return list(range(0, n, 2)) + list(range(1, n, 2))[::-1]


def ring_gather(block, rows_axis, pair_axis):
    n = lax.axis_size(rows_axis)
    ring = ring_of(n)
    pair = lax.axis_index(pair_axis)
    me = lax.axis_index(rows_axis)
    place = jnp.where(me % 2 == 0, me // 2, n - 1 - me // 2)
    half = block.shape[1] // 2
    onward = []
    for i in range(n):
        onward.append((ring[i], ring[(i + 1) % n]))
        onward.append((n + ring[(i + 1) % n], n + ring[i]))

    def sent(x):
        return lax.ppermute(x, (pair_axis, rows_axis), onward)

    def handed(x):
        return lax.ppermute(x, pair_axis, [(0, 1), (1, 0)])

    def cut(x):
        return jnp.where(pair == 0, x[:, :half], x[:, half:])

    def source(distance):
        at = lax.rem(place - distance + 2 * n, n)
        return jnp.where(at < n // 2, 2 * at, 2 * (n - 1 - at) + 1)

    way = 1 - 2 * pair
    mine = block
    other = first = handed(block)
    pieces, sources = [block], [source(0)]
    for step in range(1, n // 2 + 1):
        if step == n // 2:
            mine, other = cut(mine), cut(other)
        mine, other = sent(mine), sent(other)
        pieces += [mine, handed(other)]
        sources += [source(way * step), source(-way * step)]
    return pieces, sources, [pair * half, (1 - pair) * half], first


def fetch_kernel(after_ref, *refs):
    n = len(refs) // 2
    copies = [
        pltpu.make_async_copy(refs[i], refs[n + i], refs[2 * n].at[i]) for i in range(n)
    ]
    for copy in copies:
        copy.start()
    for copy in copies:
        copy.wait()


def lift_kernel(groups, at_ref, place_ref, *refs):
    downs, ups, pieces = refs[:groups], refs[groups : 2 * groups], refs[2 * groups : -3]
    tokens_ref, out_ref, up_ref = refs[-3:]
    rows, half = pieces[-1].shape
    for i, piece in enumerate(pieces):
        start = pl.multiple_of(at_ref[1 + i] * rows, rows)
        last = len(pieces) - 1 - i
        if last > 1:
            tokens_ref[pl.ds(start, rows), :] = piece[...]
        else:
            column = pl.multiple_of(at_ref[2 + len(pieces) - last], half)
            tokens_ref[pl.ds(start, rows), pl.ds(column, half)] = piece[...]
    rank = ups[0].shape[0]
    for s, up in enumerate(ups):
        up_ref[s * rank : (s + 1) * rank, :] = up[...]
    down = jnp.concatenate([down[...] for down in downs], axis=0).T
    low = jnp.dot(tokens_ref[...], down, preferred_element_type=jnp.float32)
    low = low.astype(jnp.bfloat16)
    parts, slots, columns = out_ref.shape
    here = lax.broadcasted_iota(jnp.int32, (slots, low.shape[0]), 0) + at_ref[0]
    chosen = (here == place_ref[...]).astype(jnp.bfloat16)
    picked = jnp.dot(chosen, low, preferred_element_type=jnp.float32)
    row_panel = lax.broadcasted_iota(jnp.int32, picked.shape, 0) // (slots // groups)
    rank_panel = lax.broadcasted_iota(jnp.int32, picked.shape, 1) // rank
    picked = jnp.where(row_panel == rank_panel, picked, 0.0).astype(jnp.bfloat16)
    for part in range(parts):
        out_ref[part] = jnp.dot(
            picked,
            up_ref[:, part * columns : (part + 1) * columns],
            preferred_element_type=jnp.float32,
        ).astype(out_ref.dtype)


def add_kernel(place_ref, base_ref, lifts_ref, out_ref):
    place = lax.broadcasted_iota(jnp.int32, (base_ref.shape[0], lifts_ref.shape[0]), 1)
    chosen = (place == place_ref[...]).astype(jnp.bfloat16)
    lift = jnp.dot(chosen, lifts_ref[...], preferred_element_type=jnp.float32)
    out_ref[...] = (base_ref[...] + adapter_scale * lift).astype(out_ref.dtype)


def on_device(
    tokens,
    base_projection_weight,
    adapter_down_panels,
    adapter_up_panels,
    request_adapter_ids,
    request_token_lengths,
    adapter_store_slot,
):
    groups = lax.axis_size("grp")
    tp = lax.axis_size("tp")
    my_group = lax.axis_index("grp")
    my_tp = lax.axis_index("tp")
    width, rank = adapter_down_panels.shape[1:]
    columns = base_projection_weight.shape[1]
    store_size = adapter_store_slot.shape[0]
    tok_all = tokens.shape[1] * tp
    longest = tok_all // 8
    here = groups * longest
    in_vmem = pl.BlockSpec(memory_space=pltpu.VMEM)
    in_smem = pl.BlockSpec(memory_space=pltpu.SMEM)
    small = pltpu.CompilerParams(vmem_limit_bytes=16 * 2**20)

    pieces, sources, cuts, first_handed = ring_gather(tokens[0], "tp", "grp")

    down, up = adapter_down_panels[0].T, adapter_up_panels[0]
    down, up = pl.pallas_call(
        fetch_kernel,
        out_shape=[jax.ShapeDtypeStruct(x.shape, x.dtype) for x in (down, up)],
        in_specs=[pl.BlockSpec(memory_space=pl.ANY)] * 3,
        out_specs=[in_vmem] * 2,
        scratch_shapes=[pltpu.SemaphoreType.DMA((2,))],
        compiler_params=small,
        name="fetch",
    )(first_handed, down, up)
    panels = swapped(down, "grp") + swapped(up, "grp")

    ids = jnp.arange(store_size, dtype=jnp.int32)
    my_ids = lax.dynamic_index_in_dim(request_adapter_ids, my_group, 0, keepdims=False)
    my_slots = jnp.sum(
        jnp.where(my_ids[:, None] == ids[None, :], adapter_store_slot[None, :], 0), axis=-1
    )
    lengths = request_token_lengths[0]
    ends = jnp.cumsum(lengths)
    starts = ends - lengths
    panel = lax.rem(my_slots // tp - my_group + groups, groups)
    first = lax.rem(my_slots, tp) * here + panel * longest - starts
    position = jnp.arange(tok_all, dtype=jnp.int32)[:, None]
    member = (position >= starts[None, :]) & (position < ends[None, :])
    place = jnp.sum(jnp.where(member, first[None, :] + position, 0), axis=1)

    at = jnp.stack([my_tp * here] + sources + cuts).astype(jnp.int32)
    gathered, lifts = pl.pallas_call(
        functools.partial(lift_kernel, groups),
        out_shape=[
            jax.ShapeDtypeStruct((tok_all, width), jnp.bfloat16),
            jax.ShapeDtypeStruct((tp, here, columns), jnp.bfloat16),
        ],
        in_specs=[in_smem] + [in_vmem] * (1 + len(panels) + len(pieces)),
        out_specs=[in_vmem] * 2,
        scratch_shapes=[pltpu.VMEM((groups * rank, tp * columns), jnp.bfloat16)],
        compiler_params=pltpu.CompilerParams(vmem_limit_bytes=24 * 2**20),
        cost_estimate=pl.CostEstimate(
            flops=2 * groups * rank * (tok_all * width + here * tp * columns),
            bytes_accessed=2 * groups * rank * (width + tp * columns),
            transcendentals=0,
        ),
        name="lift",
    )(at, place[None, :], *panels, *pieces)
    lifts = lax.all_to_all(lifts, "tp", split_axis=0, concat_axis=0, tiled=True)

    base = jnp.dot(gathered, base_projection_weight, preferred_element_type=jnp.float32)
    out = pl.pallas_call(
        add_kernel,
        out_shape=jax.ShapeDtypeStruct((tok_all, columns), jnp.bfloat16),
        in_specs=[in_vmem] * 3,
        out_specs=in_vmem,
        compiler_params=small,
        name="add",
    )(place[:, None], base, lifts.reshape(tp * here, columns))
    return out[None]


def solution(mesh):
    return jax.shard_map(
        on_device,
        mesh=mesh,
        in_specs=(
            P(("rep", "grp"), "tp", None),
            P(None, "tp"),
            P(("grp", "tp"), None, None),
            P(("grp", "tp"), None, None),
            P("rep", None),
            P(("rep", "grp"), None),
            P(),
        ),
        out_specs=P(("rep", "grp"), None, "tp"),
        check_vma=False,
    )
```

time: 64 us -> 72.5 us (1.13)
  starting transfers between devices: 14.6 us -> 21.8 us
  Pallas kernels: 4.6 us -> 5.94 us
  other arithmetic: 2.44 us -> 3.41 us
  waiting for transfers between devices: 19.3 us -> 18.4 us
    ppermute x8 -> x13, starting transfers between devices: 9.25 us -> 16.4 us  [the longest x8 15.3 us: sent(): return lax.ppermute(x, (pair_axis, rows_axis), onward)]
    ppermute x8 -> x13, waiting for transfers between devices: 13.8 us -> 9.35 us  [the longest x8 8.19 us: sent(): return lax.ppermute(x, (pair_axis, rows_axis), onward)]
    all_to_all x1, waiting for transfers between devices: 5.5 us -> 9.04 us  [on_device(): lifts = lax.all_to_all(lifts, 'tp', split_axis=0, concat_axis=0, tiled=True)]
    select_n x0 -> x2, other arithmetic: none -> 2.36 us  [cut(): return jnp.where(pair == 0, x[:, :half], x[:, half:])]
    pallas_call x2, Pallas kernels: 3.58 us -> 4.93 us  [the longest x1 3.77 us: on_device(): pl.pallas_call(functools.partial(lift_kernel, groups), out_shape=[jax.Sha...]
    unnamed x32 -> x38, local copies, waits for them, and re-layouts: 13.8 us -> 12.8 us
  transfers between devices with their start and end apart: 11 -> 16, of which waited for: 5 -> 7; matrix products, arithmetic and copies ran while one was open for 18% -> 18% of each run, Pallas kernels for 1% -> 2%
where the time goes in v8:
time: 72.5 us; the launch traced here: 72 us
  starting transfers between devices  21.8 us (30%)
  waiting for transfers between devices  18.4 us (25%)
  local copies, waits for them, and re-layouts  13.5 us (19%)
  matrix products  8.56 us (12%)
  Pallas kernels  5.94 us (8%)
  other arithmetic  3.41 us (5%)
    ppermute x8, starting transfers between devices, sent(): return lax.ppermute(x, (pair_axis, rows_axis), onward)  15.3 us
    unnamed x38, local copies, waits for them, and re-layouts  12.8 us
    all_to_all x1, waiting for transfers between devices, on_device(): lifts = lax.all_to_all(lifts, 'tp', split_axis=0, concat_axis=0, tiled=True)  9.04 us
    dot_general x1, matrix products, on_device(): jnp.dot(gathered, base_projection_weight, preferred_element_type=jnp.floa...  8.56 us
    ppermute x8, waiting for transfers between devices, sent(): return lax.ppermute(x, (pair_axis, rows_axis), onward)  8.19 us
    all_to_all x1, starting transfers between devices, on_device(): lifts = lax.all_to_all(lifts, 'tp', split_axis=0, concat_axis=0, tiled=True)  4.82 us
    pallas_call x1, Pallas kernels, on_device(): pl.pallas_call(functools.partial(lift_kernel, groups), out_shape=[jax.Sha...  3.77 us
    select_n x2, other arithmetic, cut(): return jnp.where(pair == 0, x[:, :half], x[:, half:])  2.36 us
  transfers between devices with their start and end apart: 16, of which 7 were waited for; matrix products, arithmetic and copies ran while one was open for 18% of the time, Pallas kernels for 2%

profile of v8, /device:TPU:0, one launch (start us, length us, event | category | flops | bytes accessed | tf_op | source)
XLA Modules:
  0.0 72.0 jit_solution(6229938032553559802)
XLA Ops:
  0.5 2.6 %collective-permute-start.3 = (bf16[16,8192]{1,0:T(8,128)(2,1)}, bf16[16,8192]{1,0:T(8,128)(2,1)S(1)}, u32[]{:S(2)}, u32[]{:S(2)}) collective-permute-start(bf16[16,8192]{1,0:T(8,128)(2,1)} %bitcast.56), channel_id=1, source_target_pairs={{0,2},{10,8},{2,4},{12,10},{4,6},{14,12},{6,7},{15,14},{7,5},{13,1... | collective-permute-start | bytes 786440 | tf_op jit(solution)/shard_map/ppermute | solution.py:37
  3.2 1.7 %collective-permute-start.4 = (bf16[16,8192]{1,0:T(8,128)(2,1)S(1)}, bf16[16,8192]{1,0:T(8,128)(2,1)}, u32[]{:S(2)}, u32[]{:S(2)}) collective-permute-start(bf16[16,8192]{1,0:T(8,128)(2,1)S(1)} %collective-permute-done.after_ref), channel_id=1, source_target_pairs={{0,2},{10,8},{2,4},{12,10},{4,6},{14,12},{6,7},{15,14},{7,5},{13,1... | collective-permute-start | bytes 786440 | tf_op jit(solution)/shard_map/ppermute | solution.py:37
  4.8 2.8 %collective-permute-done.3.refs_5_ = bf16[16,8192]{1,0:T(8,128)(2,1)S(1)} collective-permute-done((bf16[16,8192]{1,0:T(8,128)(2,1)}, bf16[16,8192]{1,0:T(8,128)(2,1)S(1)}, u32[]{:S(2)}, u32[]{:S(2)}) %collective-permute-start.3) | collective-permute-done | bytes 262176 | tf_op jit(solution)/shard_map/ppermute | solution.py:37
  7.7 2.1 %collective-permute-start.6 = (bf16[16,8192]{1,0:T(8,128)(2,1)S(1)}, bf16[16,8192]{1,0:T(8,128)(2,1)S(1)}, u32[]{:S(2)}, u32[]{:S(2)}) collective-permute-start(bf16[16,8192]{1,0:T(8,128)(2,1)S(1)} %collective-permute-done.3.refs_5_), channel_id=1, source_target_pairs={{0,2},{10,8},{2,4},{12,10},{4,6},{14,12},{6,7},{15,14},{7,5},{13,1... | collective-permute-start | bytes 786440 | tf_op jit(solution)/shard_map/ppermute | solution.py:37
  10.6 2.1 %collective-permute-start.7 = (bf16[16,8192]{1,0:T(8,128)(2,1)}, bf16[16,8192]{1,0:T(8,128)(2,1)}, u32[]{:S(2)}, u32[]{:S(2)}) collective-permute-start(bf16[16,8192]{1,0:T(8,128)(2,1)} %collective-permute-done.4), channel_id=1, source_target_pairs={{0,2},{10,8},{2,4},{12,10},{4,6},{14,12},{6,7},{15,14},{7,5},{13,1... | collective-permute-start | bytes 786440 | tf_op jit(solution)/shard_map/ppermute | solution.py:37
  12.7 1.4 %collective-permute-done.6.refs_7_ = bf16[16,8192]{1,0:T(8,128)(2,1)S(1)} collective-permute-done((bf16[16,8192]{1,0:T(8,128)(2,1)S(1)}, bf16[16,8192]{1,0:T(8,128)(2,1)S(1)}, u32[]{:S(2)}, u32[]{:S(2)}) %collective-permute-start.6) | collective-permute-done | bytes 262176 | tf_op jit(solution)/shard_map/ppermute | solution.py:37
  14.1 2.1 %collective-permute-start.9 = (bf16[16,8192]{1,0:T(8,128)(2,1)S(1)}, bf16[16,8192]{1,0:T(8,128)(2,1)S(1)}, u32[]{:S(2)}, u32[]{:S(2)}) collective-permute-start(bf16[16,8192]{1,0:T(8,128)(2,1)S(1)} %collective-permute-done.6.refs_7_), channel_id=1, source_target_pairs={{0,2},{10,8},{2,4},{12,10},{4,6},{14,12},{6,7},{15,14},{7,5},{13,1... | collective-permute-start | bytes 786440 | tf_op jit(solution)/shard_map/ppermute | solution.py:37
  16.1 1.3 %copy-done.1 = bf16[1,64,10240]{2,1,0:T(8,128)(2,1)S(1)} copy-done((bf16[1,64,10240]{2,1,0:T(8,128)(2,1)S(1)}, bf16[1,64,10240]{2,1,0:T(8,128)(2,1)}, u32[]{:S(2)}) %copy-start.1) | copy-done | bytes 1310744
  17.4 1.2 %copy-done.6 = bf16[1,8192,64]{1,2,0:T(8,128)(2,1)S(1)} copy-done((bf16[1,8192,64]{1,2,0:T(8,128)(2,1)S(1)}, bf16[1,8192,64]{1,2,0:T(8,128)(2,1)}, u32[]{:S(2)}) %copy-start.6) | copy-done | bytes 1048600
  18.7 1.2 %fetch.1 = (bf16[64,8192]{1,0:T(8,128)(2,1)}, bf16[64,10240]{1,0:T(8,128)(2,1)S(1)}) custom-call(bf16[16,8192]{1,0:T(8,128)(2,1)S(1)} %collective-permute-done.after_ref, bf16[64,8192]{1,0:T(8,128)(2,1)S(1)} %bitcast.54, bf16[64,10240]{1,0:T(8,128)(2,1)S(1)} %bitcast.53), custom_call_target="tpu_custom_call" | custom-call | tf_op jit(solution)/shard_map/fetch/pallas_call | solution.py:139
  20.5 1.6 %collective-permute-start.10 = (bf16[16,8192]{1,0:T(8,128)(2,1)}, bf16[16,8192]{1,0:T(8,128)(2,1)}, u32[]{:S(2)}, u32[]{:S(2)}) collective-permute-start(bf16[16,8192]{1,0:T(8,128)(2,1)} %collective-permute-done.7), channel_id=1, source_target_pairs={{0,2},{10,8},{2,4},{12,10},{4,6},{14,12},{6,7},{15,14},{7,5},{13,1... | collective-permute-start | bytes 786440 | tf_op jit(solution)/shard_map/ppermute | solution.py:37
  22.8 1.6 %collective-permute-start.12 = (bf16[16,4096]{1,0:T(8,128)(2,1)}, bf16[16,4096]{1,0:T(8,128)(2,1)S(1)}, u32[]{:S(2)}, u32[]{:S(2)}) collective-permute-start(bf16[16,4096]{1,0:T(8,128)(2,1)} %slice_select_fusion.1), channel_id=1, source_target_pairs={{0,2},{10,8},{2,4},{12,10},{4,6},{14,12},{6,7},{15,14},{7,5},{13,1... | collective-permute-start | bytes 393224 | tf_op jit(solution)/shard_map/ppermute | solution.py:37
  24.4 2.8 %collective-permute-done.10 = bf16[16,8192]{1,0:T(8,128)(2,1)} collective-permute-done((bf16[16,8192]{1,0:T(8,128)(2,1)}, bf16[16,8192]{1,0:T(8,128)(2,1)}, u32[]{:S(2)}, u32[]{:S(2)}) %collective-permute-start.10) | collective-permute-done | bytes 262176 | tf_op jit(solution)/shard_map/ppermute | solution.py:37
  27.2 1.6 %slice_select_fusion = bf16[16,4096]{1,0:T(8,128)(2,1)} fusion(bf16[16,8192]{1,0:T(8,128)(2,1)} %collective-permute-done.10, pred[]{:T(512)S(6)} %eq.29), kind=kLoop, calls=%fused_computation | loop fusion | flops 65536 | bytes 393217 | tf_op jit(solution)/shard_map/jit(_where)/select_n | solution.py:43
  28.8 1.6 %collective-permute-start.13 = (bf16[16,4096]{1,0:T(8,128)(2,1)}, bf16[16,4096]{1,0:T(8,128)(2,1)}, u32[]{:S(2)}, u32[]{:S(2)}) collective-permute-start(bf16[16,4096]{1,0:T(8,128)(2,1)} %slice_select_fusion), channel_id=1, source_target_pairs={{0,2},{10,8},{2,4},{12,10},{4,6},{14,12},{6,7},{15,14},{7,5},{13,1... | collective-permute-start | bytes 393224 | tf_op jit(solution)/shard_map/ppermute | solution.py:37
  33.1 1.0 %collective-permute-done.13 = bf16[16,4096]{1,0:T(8,128)(2,1)} collective-permute-done((bf16[16,4096]{1,0:T(8,128)(2,1)}, bf16[16,4096]{1,0:T(8,128)(2,1)}, u32[]{:S(2)}, u32[]{:S(2)}) %collective-permute-start.13) | collective-permute-done | bytes 131104 | tf_op jit(solution)/shard_map/ppermute | solution.py:37
  34.6 1.2 %collective-permute-done.14.refs_12_ = bf16[16,4096]{1,0:T(8,128)(2,1)} collective-permute-done((bf16[16,4096]{1,0:T(8,128)(2,1)}, bf16[16,4096]{1,0:T(8,128)(2,1)}, u32[]{:S(2)}, u32[]{:S(2)}) %collective-permute-start.14) | collective-permute-done | bytes 131104 | tf_op jit(solution)/shard_map/ppermute | solution.py:40
  35.9 1.1 %copy-done.2 = bf16[64,10240]{1,0:T(8,128)(2,1)} copy-done((bf16[64,10240]{1,0:T(8,128)(2,1)}, bf16[64,10240]{1,0:T(8,128)(2,1)S(1)}, u32[]{:S(2)}) %copy-start.2) | copy-done | bytes 1310744
  36.9 1.3 %copy-done.3 = bf16[64,10240]{1,0:T(8,128)(2,1)S(1)} copy-done((bf16[64,10240]{1,0:T(8,128)(2,1)S(1)}, bf16[64,10240]{1,0:T(8,128)(2,1)}, u32[]{:S(2)}) %copy-start.3) | copy-done | bytes 1310744
  43.9 3.8 %lift.1 = (bf16[128,8192]{1,0:T(8,128)(2,1)S(1)}, bf16[8,32,1280]{2,1,0:T(8,128)(2,1)S(1)}) custom-call(s32[12]{0:T(128)S(1)} %stack.51.at_ref, s32[1,128]{1,0:T(1,128)S(1)} %bitcast.59, bf16[64,8192]{1,0:T(8,128)(2,1)} %get-tuple-element.9.refs_0_, bf16[64,8192]{1,0:T(8,128)(2,1)} %collective-permute-done.1.refs_1_, ...), custom_call_target="tpu_custom_call" | custom-call | flops 352321536 | bytes 4718592 | tf_op jit(solution)/shard_map/lift/pallas_call | solution.py:165
  48.5 4.8 %all-to-all-start = ((bf16[8,32,1280]{2,1,0:T(8,128)(2,1)}), bf16[8,32,1280]{2,1,0:T(8,128)(2,1)S(1)}, u32[]{:S(2)}, u32[]{:S(2)}) async-start(bf16[8,32,1280]{2,1,0:T(8,128)(2,1)} %copy-done.7), calls=%async_computation | async-start | bytes 1310720 | tf_op jit(solution)/shard_map/all_to_all | solution.py:182
  53.4 8.6 %fusion.7.base_ref = f32[128,1280]{1,0:T(8,128)S(1)} fusion(bf16[128,8192]{1,0:T(8,128)(2,1)S(1)} %get-tuple-element.11, bf16[8192,1280]{1,0:T(8,128)(2,1)} %param.8), kind=kOutput, calls=%fused_computation.23 | convolution fusion | flops 2684354560 | bytes 23724032 | tf_op jit(solution)/shard_map/dot_general | solution.py:184
  61.9 9.0 %all-to-all-done = bf16[8,32,1280]{2,1,0:T(8,128)(2,1)S(1)} async-done(((bf16[8,32,1280]{2,1,0:T(8,128)(2,1)}), bf16[8,32,1280]{2,1,0:T(8,128)(2,1)S(1)}, u32[]{:S(2)}, u32[]{:S(2)}) %all-to-all-start) | async-done | bytes 655392 | tf_op jit(solution)/shard_map/all_to_all | solution.py:182
  71.0 1.0 %add.140 = bf16[128,1280]{1,0:T(8,128)(2,1)} custom-call(s32[128,1]{1,0:T(8,128)S(1)} %copy.9.place_ref, f32[128,1280]{1,0:T(8,128)S(1)} %fusion.7.base_ref, bf16[256,1280]{1,0:T(8,128)(2,1)S(1)} %bitcast.52), custom_call_target="tpu_custom_call" | custom-call | tf_op jit(solution)/shard_map/add/pallas_call | solution.py:185
  (59 shorter events, 12.2 us)
Async XLA Ops:
  0.0 30.4 %copy-start = (s32[2,12]{1,0:T(2,128)S(1)}, s32[2,12]{1,0:T(2,128)}, u32[]{:S(2)}) copy-start(s32[2,12]{1,0:T(2,128)} %param.11) | copy-start | bytes 292
  0.0 30.9 %copy-start.17 = (s32[1,12]{1,0:T(1,128)S(1)}, s32[1,12]{1,0:T(1,128)}, u32[]{:S(2)}) copy-start(s32[1,12]{1,0:T(1,128)} %param.12) | copy-start | bytes 148
  0.0 31.1 %copy-start.18 = (s32[16]{0:T(128)S(1)}, s32[16]{0:T(128)}, u32[]{:S(2)}) copy-start(s32[16]{0:T(128)} %param.13) | copy-start | bytes 196
  0.0 3.2 %collective-permute-start = (bf16[16,8192]{1,0:T(8,128)(2,1)}, bf16[16,8192]{1,0:T(8,128)(2,1)S(1)}, u32[]{:S(2)}, u32[]{:S(2)}) collective-permute-start(bf16[16,8192]{1,0:T(8,128)(2,1)} %bitcast.55), channel_id=1, source_target_pairs={{0,8},{8,0},{1,9},{9,1},{2,10},{10,2},{3,11},{11,3},{4,12},{12,4},... | collective-permute-start | bytes 786440 | tf_op jit(solution)/shard_map/ppermute | solution.py:40
  0.5 7.1 %collective-permute-start.3 = (bf16[16,8192]{1,0:T(8,128)(2,1)}, bf16[16,8192]{1,0:T(8,128)(2,1)S(1)}, u32[]{:S(2)}, u32[]{:S(2)}) collective-permute-start(bf16[16,8192]{1,0:T(8,128)(2,1)} %bitcast.56), channel_id=1, source_target_pairs={{0,2},{10,8},{2,4},{12,10},{4,6},{14,12},{6,7},{15,14},{7,5},{13,1... | collective-permute-start | bytes 786440 | tf_op jit(solution)/shard_map/ppermute | solution.py:37
  3.2 7.4 %collective-permute-start.4 = (bf16[16,8192]{1,0:T(8,128)(2,1)S(1)}, bf16[16,8192]{1,0:T(8,128)(2,1)}, u32[]{:S(2)}, u32[]{:S(2)}) collective-permute-start(bf16[16,8192]{1,0:T(8,128)(2,1)S(1)} %collective-permute-done.after_ref), channel_id=1, source_target_pairs={{0,2},{10,8},{2,4},{12,10},{4,6},{14,12},{6,7},{15,14},{7,5},{13,1... | collective-permute-start | bytes 786440 | tf_op jit(solution)/shard_map/ppermute | solution.py:37
  7.7 6.4 %collective-permute-start.6 = (bf16[16,8192]{1,0:T(8,128)(2,1)S(1)}, bf16[16,8192]{1,0:T(8,128)(2,1)S(1)}, u32[]{:S(2)}, u32[]{:S(2)}) collective-permute-start(bf16[16,8192]{1,0:T(8,128)(2,1)S(1)} %collective-permute-done.3.refs_5_), channel_id=1, source_target_pairs={{0,2},{10,8},{2,4},{12,10},{4,6},{14,12},{6,7},{15,14},{7,5},{13,1... | collective-permute-start | bytes 786440 | tf_op jit(solution)/shard_map/ppermute | solution.py:37
  10.6 9.9 %collective-permute-start.7 = (bf16[16,8192]{1,0:T(8,128)(2,1)}, bf16[16,8192]{1,0:T(8,128)(2,1)}, u32[]{:S(2)}, u32[]{:S(2)}) collective-permute-start(bf16[16,8192]{1,0:T(8,128)(2,1)} %collective-permute-done.4), channel_id=1, source_target_pairs={{0,2},{10,8},{2,4},{12,10},{4,6},{14,12},{6,7},{15,14},{7,5},{13,1... | collective-permute-start | bytes 786440 | tf_op jit(solution)/shard_map/ppermute | solution.py:37
  14.0 21.8 %copy-start.11 = (bf16[16,8192]{1,0:T(8,128)(2,1)}, bf16[16,8192]{1,0:T(8,128)(2,1)S(1)}, u32[]{:S(2)}) copy-start(bf16[16,8192]{1,0:T(8,128)(2,1)S(1)} %collective-permute-done.6.refs_7_) | copy-start | bytes 786436
  14.1 8.0 %collective-permute-start.9 = (bf16[16,8192]{1,0:T(8,128)(2,1)S(1)}, bf16[16,8192]{1,0:T(8,128)(2,1)S(1)}, u32[]{:S(2)}, u32[]{:S(2)}) collective-permute-start(bf16[16,8192]{1,0:T(8,128)(2,1)S(1)} %collective-permute-done.6.refs_7_), channel_id=1, source_target_pairs={{0,2},{10,8},{2,4},{12,10},{4,6},{14,12},{6,7},{15,14},{7,5},{13,1... | collective-permute-start | bytes 786440 | tf_op jit(solution)/shard_map/ppermute | solution.py:37
  16.1 1.3 %copy-start.1 = (bf16[1,64,10240]{2,1,0:T(8,128)(2,1)S(1)}, bf16[1,64,10240]{2,1,0:T(8,128)(2,1)}, u32[]{:S(2)}) copy-start(bf16[1,64,10240]{2,1,0:T(8,128)(2,1)} %param.10) | copy-start | bytes 3932164
  19.8 16.0 %collective-permute-start.2 = (bf16[64,10240]{1,0:T(8,128)(2,1)S(1)}, bf16[64,10240]{1,0:T(8,128)(2,1)S(1)}, u32[]{:S(2)}, u32[]{:S(2)}) collective-permute-start(bf16[64,10240]{1,0:T(8,128)(2,1)S(1)} %get-tuple-element.10.refs_2_), channel_id=1, source_target_pairs={{8,0},{0,8},{9,1},{1,9},{10,2},{2,10},{11,3},{3,11},{12,4},{4,12},... | collective-permute-start | bytes 3932168 | tf_op jit(solution)/shard_map/ppermute | solution.py:16
  19.9 15.9 %collective-permute-start.1 = (bf16[64,8192]{1,0:T(8,128)(2,1)}, bf16[64,8192]{1,0:T(8,128)(2,1)}, u32[]{:S(2)}, u32[]{:S(2)}) collective-permute-start(bf16[64,8192]{1,0:T(8,128)(2,1)} %get-tuple-element.9.refs_0_), channel_id=1, source_target_pairs={{8,0},{0,8},{9,1},{1,9},{10,2},{2,10},{11,3},{3,11},{12,4},{4,12},... | collective-permute-start | bytes 3145736 | tf_op jit(solution)/shard_map/ppermute | solution.py:16
  20.4 11.4 %collective-permute-start.5 = (bf16[16,8192]{1,0:T(8,128)(2,1)}, bf16[16,8192]{1,0:T(8,128)(2,1)S(1)}, u32[]{:S(2)}, u32[]{:S(2)}) collective-permute-start(bf16[16,8192]{1,0:T(8,128)(2,1)} %collective-permute-done.4), channel_id=1, source_target_pairs={{0,8},{8,0},{1,9},{9,1},{2,10},{10,2},{3,11},{11,3},{4,12},{12,4},... | collective-permute-start | bytes 786440 | tf_op jit(solution)/shard_map/ppermute | solution.py:40
  20.5 6.7 %collective-permute-start.10 = (bf16[16,8192]{1,0:T(8,128)(2,1)}, bf16[16,8192]{1,0:T(8,128)(2,1)}, u32[]{:S(2)}, u32[]{:S(2)}) collective-permute-start(bf16[16,8192]{1,0:T(8,128)(2,1)} %collective-permute-done.7), channel_id=1, source_target_pairs={{0,2},{10,8},{2,4},{12,10},{4,6},{14,12},{6,7},{15,14},{7,5},{13,1... | collective-permute-start | bytes 786440 | tf_op jit(solution)/shard_map/ppermute | solution.py:37
  22.1 13.8 %copy-start.4 = (bf16[16,8192]{1,0:T(8,128)(2,1)}, bf16[16,8192]{1,0:T(8,128)(2,1)S(1)}, u32[]{:S(2)}) copy-start(bf16[16,8192]{1,0:T(8,128)(2,1)S(1)} %collective-permute-done.9.refs_9_) | copy-start | bytes 786436
  22.8 9.2 %collective-permute-start.12 = (bf16[16,4096]{1,0:T(8,128)(2,1)}, bf16[16,4096]{1,0:T(8,128)(2,1)S(1)}, u32[]{:S(2)}, u32[]{:S(2)}) collective-permute-start(bf16[16,4096]{1,0:T(8,128)(2,1)} %slice_select_fusion.1), channel_id=1, source_target_pairs={{0,2},{10,8},{2,4},{12,10},{4,6},{14,12},{6,7},{15,14},{7,5},{13,1... | collective-permute-start | bytes 393224 | tf_op jit(solution)/shard_map/ppermute | solution.py:37
  28.8 5.3 %collective-permute-start.13 = (bf16[16,4096]{1,0:T(8,128)(2,1)}, bf16[16,4096]{1,0:T(8,128)(2,1)}, u32[]{:S(2)}, u32[]{:S(2)}) collective-permute-start(bf16[16,4096]{1,0:T(8,128)(2,1)} %slice_select_fusion), channel_id=1, source_target_pairs={{0,2},{10,8},{2,4},{12,10},{4,6},{14,12},{6,7},{15,14},{7,5},{13,1... | collective-permute-start | bytes 393224 | tf_op jit(solution)/shard_map/ppermute | solution.py:37
  31.8 4.0 %copy-start.13 = (bf16[16,8192]{1,0:T(8,128)(2,1)}, bf16[16,8192]{1,0:T(8,128)(2,1)S(1)}, u32[]{:S(2)}) copy-start(bf16[16,8192]{1,0:T(8,128)(2,1)S(1)} %collective-permute-done.5.refs_6_) | copy-start | bytes 786436
  31.9 2.8 %collective-permute-start.8 = (bf16[16,8192]{1,0:T(8,128)(2,1)}, bf16[16,8192]{1,0:T(8,128)(2,1)}, u32[]{:S(2)}, u32[]{:S(2)}) collective-permute-start(bf16[16,8192]{1,0:T(8,128)(2,1)} %collective-permute-done.7), channel_id=1, source_target_pairs={{0,8},{8,0},{1,9},{9,1},{2,10},{10,2},{3,11},{11,3},{4,12},{12,4},... | collective-permute-start | bytes 786440 | tf_op jit(solution)/shard_map/ppermute | solution.py:40
  32.6 3.2 %collective-permute-start.11 = (bf16[16,8192]{1,0:T(8,128)(2,1)}, bf16[16,8192]{1,0:T(8,128)(2,1)}, u32[]{:S(2)}, u32[]{:S(2)}) collective-permute-start(bf16[16,8192]{1,0:T(8,128)(2,1)} %collective-permute-done.10), channel_id=1, source_target_pairs={{0,8},{8,0},{1,9},{9,1},{2,10},{10,2},{3,11},{11,3},{4,12},{12,4},... | collective-permute-start | bytes 786440 | tf_op jit(solution)/shard_map/ppermute | solution.py:40
  34.1 1.7 %collective-permute-start.14 = (bf16[16,4096]{1,0:T(8,128)(2,1)}, bf16[16,4096]{1,0:T(8,128)(2,1)}, u32[]{:S(2)}, u32[]{:S(2)}) collective-permute-start(bf16[16,4096]{1,0:T(8,128)(2,1)} %collective-permute-done.13), channel_id=1, source_target_pairs={{0,8},{8,0},{1,9},{9,1},{2,10},{10,2},{3,11},{11,3},{4,12},{12,4},... | collective-permute-start | bytes 393224 | tf_op jit(solution)/shard_map/ppermute | solution.py:40
  36.9 1.3 %copy-start.3 = (bf16[64,10240]{1,0:T(8,128)(2,1)S(1)}, bf16[64,10240]{1,0:T(8,128)(2,1)}, u32[]{:S(2)}) copy-start(bf16[64,10240]{1,0:T(8,128)(2,1)} %copy-done.2) | copy-start | bytes 3932164
  48.5 22.4 %all-to-all-start = ((bf16[8,32,1280]{2,1,0:T(8,128)(2,1)}), bf16[8,32,1280]{2,1,0:T(8,128)(2,1)S(1)}, u32[]{:S(2)}, u32[]{:S(2)}) async-start(bf16[8,32,1280]{2,1,0:T(8,128)(2,1)} %copy-done.7), calls=%async_computation | async-start | bytes 1310720 | tf_op jit(solution)/shard_map/all_to_all | solution.py:182
  (11 other events, 10.2 us)

commit v9 on v8

v9 whole, which is shorter than its diff:
```python
import functools

import jax
import jax.numpy as jnp
from jax import lax
from jax.experimental import pallas as pl
from jax.experimental.pallas import tpu as pltpu
from jax.sharding import PartitionSpec as P

adapter_scale = 1.0


def swapped(x, axis):
    n = lax.axis_size(axis)
    return [x] + [
        lax.ppermute(x, axis, [((i + s) % n, i) for i in range(n)]) for s in range(1, n)
    ]


def ring_of(n):
    return list(range(0, n, 2)) + list(range(1, n, 2))[::-1]


def ring_gather(block):
    n = lax.axis_size("tp")
    ring = ring_of(n)
    onward = []
    for i in range(n):
        onward.append((ring[i], ring[(i + 1) % n]))
        onward.append((n + ring[(i + 1) % n], n + ring[i]))

    def sent(x):
        return lax.ppermute(x, ("grp", "tp"), onward)

    def handed(x):
        return lax.ppermute(x, "grp", [(0, 1), (1, 0)])

    mine, other = block, handed(block)
    pieces = [block]
    for step in range(1, n // 2):
        mine, other = sent(mine), sent(other)
        pieces += [mine, handed(other)]
    return pieces + [sent(mine)]


def ring_sources(n):
    me = lax.axis_index("tp")
    way = 1 - 2 * lax.axis_index("grp")
    place = jnp.where(lax.rem(me, 2) == 0, me // 2, n - 1 - me // 2)
    distances = [0] + [d for i in range(1, n // 2) for d in (way * i, -way * i)] + [n // 2]
    sources = []
    for distance in distances:
        at = lax.rem(place - distance + 2 * n, n)
        sources.append(jnp.where(at < n // 2, 2 * at, 2 * (n - 1 - at) + 1))
    return sources


def places_of(position, tp, groups, longest, ids_ref, lengths_ref, slots_ref):
    group = lax.axis_index("grp")

    def add(request, carry):
        start, place = carry
        slot = slots_ref[ids_ref[group, request]]
        end = start + lengths_ref[0, request]
        panel = lax.rem(slot // tp - group + groups, groups)
        first = (lax.rem(slot, tp) * groups + panel) * longest - start
        here = (position >= start) & (position < end)
        return end, jnp.where(here, first + position, place)

    carry = (jnp.int32(0), jnp.zeros_like(position))
    return lax.fori_loop(0, ids_ref.shape[1], add, carry)[1]


def lift_kernel(groups, tp, ids_ref, lengths_ref, slots_ref, *refs):
    downs, ups, pieces = refs[:groups], refs[groups : 2 * groups], refs[2 * groups : -5]
    tokens_ref, out_ref, down_ref, up_ref, sems = refs[-5:]
    rank = ups[0].shape[0]
    rows = pieces[0].shape[0]
    parts, slots, columns = out_ref.shape
    copies = [
        pltpu.make_async_copy(down, down_ref.at[pl.ds(s * rank, rank)], sems.at[s])
        for s, down in enumerate(downs)
    ]
    for i, (piece, source) in enumerate(zip(pieces, ring_sources(tp))):
        at = pl.ds(pl.multiple_of(source * rows, rows), rows)
        copies.append(
            pltpu.make_async_copy(piece, tokens_ref.at[at], sems.at[groups + i])
        )
    up_copies = [
        pltpu.make_async_copy(
            up, up_ref.at[pl.ds(s * rank, rank)], sems.at[groups + len(pieces) + s]
        )
        for s, up in enumerate(ups)
    ]
    for copy in copies + up_copies:
        copy.start()
    tok_all = tokens_ref.shape[0]
    position = lax.broadcasted_iota(jnp.int32, (1, tok_all), 1)
    place = places_of(position, tp, groups, slots // groups, ids_ref, lengths_ref, slots_ref)
    here = lax.broadcasted_iota(jnp.int32, (slots, tok_all), 0) + lax.axis_index("tp") * slots
    chosen = (here == place).astype(jnp.bfloat16)
    for copy in copies:
        copy.wait()
    low = jnp.dot(tokens_ref[...], down_ref[...].T, preferred_element_type=jnp.float32)
    picked = jnp.dot(chosen, low.astype(jnp.bfloat16), preferred_element_type=jnp.float32)
    row_panel = lax.broadcasted_iota(jnp.int32, picked.shape, 0) // (slots // groups)
    rank_panel = lax.broadcasted_iota(jnp.int32, picked.shape, 1) // rank
    picked = jnp.where(row_panel == rank_panel, picked, 0.0).astype(jnp.bfloat16)
    for copy in up_copies:
        copy.wait()
    for part in range(parts):
        out_ref[part] = jnp.dot(
            picked,
            up_ref[:, part * columns : (part + 1) * columns],
            preferred_element_type=jnp.float32,
        ).astype(out_ref.dtype)


def add_kernel(groups, tp, ids_ref, lengths_ref, slots_ref, base_ref, lifts_ref, out_ref):
    tok_all, rows = base_ref.shape[0], lifts_ref.shape[0]
    position = lax.broadcasted_iota(jnp.int32, (tok_all, 1), 0)
    place = places_of(
        position, tp, groups, rows // tp // groups, ids_ref, lengths_ref, slots_ref
    )
    chosen = lax.broadcasted_iota(jnp.int32, (tok_all, rows), 1) == place
    lift = jnp.dot(
        chosen.astype(jnp.bfloat16), lifts_ref[...], preferred_element_type=jnp.float32
    )
    out_ref[...] = (base_ref[...] + adapter_scale * lift).astype(out_ref.dtype)


def on_device(
    tokens,
    base_projection_weight,
    adapter_down_panels,
    adapter_up_panels,
    request_adapter_ids,
    request_token_lengths,
    adapter_store_slot,
):
    groups = lax.axis_size("grp")
    tp = lax.axis_size("tp")
    width, rank = adapter_down_panels.shape[1:]
    columns = base_projection_weight.shape[1]
    tok_all = tokens.shape[1] * tp
    longest = tok_all // 8
    here = groups * longest
    in_hbm = pl.BlockSpec(memory_space=pltpu.HBM)
    in_vmem = pl.BlockSpec(memory_space=pltpu.VMEM)
    in_smem = pl.BlockSpec(memory_space=pltpu.SMEM)
    requests = (request_adapter_ids, request_token_lengths, adapter_store_slot)

    pieces = ring_gather(tokens[0])
    panels = swapped(adapter_down_panels[0].T, "grp") + swapped(adapter_up_panels[0], "grp")

    gathered, lifts = pl.pallas_call(
        functools.partial(lift_kernel, groups, tp),
        out_shape=[
            jax.ShapeDtypeStruct((tok_all, width), jnp.bfloat16),
            jax.ShapeDtypeStruct((tp, here, columns), jnp.bfloat16),
        ],
        in_specs=[in_smem] * 3 + [in_hbm] * (len(panels) + len(pieces)),
        out_specs=[in_vmem] * 2,
        scratch_shapes=[
            pltpu.VMEM((groups * rank, width), jnp.bfloat16),
            pltpu.VMEM((groups * rank, tp * columns), jnp.bfloat16),
            pltpu.SemaphoreType.DMA((len(panels) + len(pieces),)),
        ],
        compiler_params=pltpu.CompilerParams(vmem_limit_bytes=28 * 2**20),
        cost_estimate=pl.CostEstimate(
            flops=2 * groups * rank * (tok_all * width + here * tp * columns),
            bytes_accessed=2 * groups * rank * (width + tp * columns),
            transcendentals=0,
        ),
        name="lift",
    )(*requests, *panels, *pieces)
    lifts = lax.all_to_all(lifts, "tp", split_axis=0, concat_axis=0, tiled=True)

    base = jnp.dot(gathered, base_projection_weight, preferred_element_type=jnp.float32)
    out = pl.pallas_call(
        functools.partial(add_kernel, groups, tp),
        out_shape=jax.ShapeDtypeStruct((tok_all, columns), jnp.bfloat16),
        in_specs=[in_smem] * 3 + [in_vmem] * 2,
        out_specs=in_vmem,
        compiler_params=pltpu.CompilerParams(vmem_limit_bytes=16 * 2**20),
        name="add",
    )(*requests, base, lifts.reshape(tp * here, columns))
    return out[None]


def solution(mesh):
    return jax.shard_map(
        on_device,
        mesh=mesh,
        in_specs=(
            P(("rep", "grp"), "tp", None),
            P(None, "tp"),
            P(("grp", "tp"), None, None),
            P(("grp", "tp"), None, None),
            P("rep", None),
            P(("rep", "grp"), None),
            P(),
        ),
        out_specs=P(("rep", "grp"), None, "tp"),
        check_vma=False,
    )
```

time: 72.5 us -> 61.2 us (0.84)
  local copies, waits for them, and re-layouts: 13.5 us -> 5.49 us
  other arithmetic: 3.41 us -> 0 us
    unnamed x38 -> x18, local copies, waits for them, and re-layouts: 12.8 us -> 5.49 us
    select_n x2 -> x0, other arithmetic: 2.36 us -> none  [cut(): return jnp.where(pair == 0, x[:, :half], x[:, half:])]
    ppermute x13 -> x11, waiting for transfers between devices: 9.35 us -> 11.6 us  [the longest x7 11.6 us: sent(): return lax.ppermute(x, ('grp', 'tp'), onward)]
    all_to_all x1, waiting for transfers between devices: 9.04 us -> 6.98 us  [on_device(): lifts = lax.all_to_all(lifts, 'tp', split_axis=0, concat_axis=0, tiled=True)]
    all_to_all x1, starting transfers between devices: 4.82 us -> 6.35 us  [on_device(): lifts = lax.all_to_all(lifts, 'tp', split_axis=0, concat_axis=0, tiled=True)]
    ppermute x13 -> x11, starting transfers between devices: 16.4 us -> 15.5 us  [the longest x7 15 us: sent(): return lax.ppermute(x, ('grp', 'tp'), onward)]
    reduce_sum x2 -> x0, other arithmetic: 0.85 us -> none  [the longest x1 0.76 us: on_device(): jnp.sum(jnp.where(my_ids[:, None] == ids[None, :], adapter_store_slot[Non...]
    pallas_call x3 -> x2, Pallas kernels: 5.94 us -> 6.31 us  [the longest x1 4.35 us: on_device(): pl.pallas_call(functools.partial(lift_kernel, groups, tp), out_shape=[jax...]
  transfers between devices with their start and end apart: 16 -> 14, of which waited for: 7 -> 8; matrix products, arithmetic and copies ran while one was open for 18% -> 14% of each run, Pallas kernels for 2% -> 0%
where the time goes in v9:
time: 61.2 us; the launch traced here: 60.9 us
  starting transfers between devices  21.9 us (36%)
  waiting for transfers between devices  18.6 us (30%)
  matrix products  8.55 us (14%)
  Pallas kernels  6.31 us (10%)
  local copies, waits for them, and re-layouts  5.49 us (9%)
    ppermute x7, starting transfers between devices, sent(): return lax.ppermute(x, ('grp', 'tp'), onward)  15 us
    ppermute x7, waiting for transfers between devices, sent(): return lax.ppermute(x, ('grp', 'tp'), onward)  11.6 us
    dot_general x1, matrix products, on_device(): jnp.dot(gathered, base_projection_weight, preferred_element_type=jnp.floa...  8.55 us
    all_to_all x1, waiting for transfers between devices, on_device(): lifts = lax.all_to_all(lifts, 'tp', split_axis=0, concat_axis=0, tiled=True)  6.98 us
    all_to_all x1, starting transfers between devices, on_device(): lifts = lax.all_to_all(lifts, 'tp', split_axis=0, concat_axis=0, tiled=True)  6.35 us
    unnamed x18, local copies, waits for them, and re-layouts  5.49 us
    pallas_call x1, Pallas kernels, on_device(): pl.pallas_call(functools.partial(lift_kernel, groups, tp), out_shape=[jax...  4.35 us
    pallas_call x1, Pallas kernels, on_device(): pl.pallas_call(functools.partial(add_kernel, groups, tp), out_shape=jax.S...  1.96 us
  transfers between devices with their start and end apart: 14, of which 8 were waited for; matrix products, arithmetic and copies ran while one was open for 14% of the time, Pallas kernels for 0%

profile of v9, /device:TPU:0, one launch (start us, length us, event | category | flops | bytes accessed | tf_op | source)
XLA Modules:
  0.0 60.9 jit_solution(372625033929670086)
XLA Ops:
  0.5 3.0 %collective-permute-start.2 = (bf16[16,8192]{1,0:T(8,128)(2,1)}, bf16[16,8192]{1,0:T(8,128)(2,1)S(1)}, u32[]{:S(2)}, u32[]{:S(2)}) collective-permute-start(bf16[16,8192]{1,0:T(8,128)(2,1)} %bitcast.15), channel_id=1, source_target_pairs={{0,2},{10,8},{2,4},{12,10},{4,6},{14,12},{6,7},{15,14},{7,5},{13,1... | collective-permute-start | bytes 786440 | tf_op jit(solution)/shard_map/ppermute | solution.py:33
  3.5 1.6 %collective-permute-start.4 = (bf16[16,8192]{1,0:T(8,128)(2,1)S(1)}, bf16[16,8192]{1,0:T(8,128)(2,1)S(1)}, u32[]{:S(2)}, u32[]{:S(2)}) collective-permute-start(bf16[16,8192]{1,0:T(8,128)(2,1)S(1)} %collective-permute-done.3), channel_id=1, source_target_pairs={{0,2},{10,8},{2,4},{12,10},{4,6},{14,12},{6,7},{15,14},{7,5},{13,1... | collective-permute-start | bytes 786440 | tf_op jit(solution)/shard_map/ppermute | solution.py:33
  5.1 2.9 %collective-permute-done.2.refs_5_ = bf16[16,8192]{1,0:T(8,128)(2,1)S(1)} collective-permute-done((bf16[16,8192]{1,0:T(8,128)(2,1)}, bf16[16,8192]{1,0:T(8,128)(2,1)S(1)}, u32[]{:S(2)}, u32[]{:S(2)}) %collective-permute-start.2) | collective-permute-done | bytes 262176 | tf_op jit(solution)/shard_map/ppermute | solution.py:33
  8.0 2.1 %collective-permute-start.6 = (bf16[16,8192]{1,0:T(8,128)(2,1)S(1)}, bf16[16,8192]{1,0:T(8,128)(2,1)S(1)}, u32[]{:S(2)}, u32[]{:S(2)}) collective-permute-start(bf16[16,8192]{1,0:T(8,128)(2,1)S(1)} %collective-permute-done.2.refs_5_), channel_id=1, source_target_pairs={{0,2},{10,8},{2,4},{12,10},{4,6},{14,12},{6,7},{15,14},{7,5},{13,1... | collective-permute-start | bytes 786440 | tf_op jit(solution)/shard_map/ppermute | solution.py:33
  10.1 0.7 %collective-permute-done.4 = bf16[16,8192]{1,0:T(8,128)(2,1)S(1)} collective-permute-done((bf16[16,8192]{1,0:T(8,128)(2,1)S(1)}, bf16[16,8192]{1,0:T(8,128)(2,1)S(1)}, u32[]{:S(2)}, u32[]{:S(2)}) %collective-permute-start.4) | collective-permute-done | bytes 262176 | tf_op jit(solution)/shard_map/ppermute | solution.py:33
  10.8 2.1 %collective-permute-start.7 = (bf16[16,8192]{1,0:T(8,128)(2,1)S(1)}, bf16[16,8192]{1,0:T(8,128)(2,1)S(1)}, u32[]{:S(2)}, u32[]{:S(2)}) collective-permute-start(bf16[16,8192]{1,0:T(8,128)(2,1)S(1)} %collective-permute-done.4), channel_id=1, source_target_pairs={{0,2},{10,8},{2,4},{12,10},{4,6},{14,12},{6,7},{15,14},{7,5},{13,1... | collective-permute-start | bytes 786440 | tf_op jit(solution)/shard_map/ppermute | solution.py:33
  12.9 1.5 %collective-permute-done.6.refs_7_ = bf16[16,8192]{1,0:T(8,128)(2,1)S(1)} collective-permute-done((bf16[16,8192]{1,0:T(8,128)(2,1)S(1)}, bf16[16,8192]{1,0:T(8,128)(2,1)S(1)}, u32[]{:S(2)}, u32[]{:S(2)}) %collective-permute-start.6) | collective-permute-done | bytes 262176 | tf_op jit(solution)/shard_map/ppermute | solution.py:33
  14.4 2.1 %collective-permute-start.9 = (bf16[16,8192]{1,0:T(8,128)(2,1)S(1)}, bf16[16,8192]{1,0:T(8,128)(2,1)S(1)}, u32[]{:S(2)}, u32[]{:S(2)}) collective-permute-start(bf16[16,8192]{1,0:T(8,128)(2,1)S(1)} %collective-permute-done.6.refs_7_), channel_id=1, source_target_pairs={{0,2},{10,8},{2,4},{12,10},{4,6},{14,12},{6,7},{15,14},{7,5},{13,1... | collective-permute-start | bytes 786440 | tf_op jit(solution)/shard_map/ppermute | solution.py:33
  16.5 0.7 %collective-permute-done.7 = bf16[16,8192]{1,0:T(8,128)(2,1)S(1)} collective-permute-done((bf16[16,8192]{1,0:T(8,128)(2,1)S(1)}, bf16[16,8192]{1,0:T(8,128)(2,1)S(1)}, u32[]{:S(2)}, u32[]{:S(2)}) %collective-permute-start.7) | collective-permute-done | bytes 262176 | tf_op jit(solution)/shard_map/ppermute | solution.py:33
  17.2 2.1 %collective-permute-start.10 = (bf16[16,8192]{1,0:T(8,128)(2,1)S(1)}, bf16[16,8192]{1,0:T(8,128)(2,1)S(1)}, u32[]{:S(2)}, u32[]{:S(2)}) collective-permute-start(bf16[16,8192]{1,0:T(8,128)(2,1)S(1)} %collective-permute-done.7), channel_id=1, source_target_pairs={{0,2},{10,8},{2,4},{12,10},{4,6},{14,12},{6,7},{15,14},{7,5},{13,1... | collective-permute-start | bytes 786440 | tf_op jit(solution)/shard_map/ppermute | solution.py:33
  19.3 1.5 %collective-permute-done.9.refs_9_ = bf16[16,8192]{1,0:T(8,128)(2,1)S(1)} collective-permute-done((bf16[16,8192]{1,0:T(8,128)(2,1)S(1)}, bf16[16,8192]{1,0:T(8,128)(2,1)S(1)}, u32[]{:S(2)}, u32[]{:S(2)}) %collective-permute-start.9) | collective-permute-done | bytes 262176 | tf_op jit(solution)/shard_map/ppermute | solution.py:33
  20.8 2.1 %collective-permute-start.12 = (bf16[16,8192]{1,0:T(8,128)(2,1)S(1)}, bf16[16,8192]{1,0:T(8,128)(2,1)S(1)}, u32[]{:S(2)}, u32[]{:S(2)}) collective-permute-start(bf16[16,8192]{1,0:T(8,128)(2,1)S(1)} %collective-permute-done.9.refs_9_), channel_id=1, source_target_pairs={{0,2},{10,8},{2,4},{12,10},{4,6},{14,12},{6,7},{15,14},{7,5},{13,1... | collective-permute-start | bytes 786440 | tf_op jit(solution)/shard_map/ppermute | solution.py:33
  22.9 0.7 %collective-permute-done.10 = bf16[16,8192]{1,0:T(8,128)(2,1)S(1)} collective-permute-done((bf16[16,8192]{1,0:T(8,128)(2,1)S(1)}, bf16[16,8192]{1,0:T(8,128)(2,1)S(1)}, u32[]{:S(2)}, u32[]{:S(2)}) %collective-permute-start.10) | collective-permute-done | bytes 262176 | tf_op jit(solution)/shard_map/ppermute | solution.py:33
  23.6 3.6 %collective-permute-done.12.refs_11_ = bf16[16,8192]{1,0:T(8,128)(2,1)S(1)} collective-permute-done((bf16[16,8192]{1,0:T(8,128)(2,1)S(1)}, bf16[16,8192]{1,0:T(8,128)(2,1)S(1)}, u32[]{:S(2)}, u32[]{:S(2)}) %collective-permute-start.12) | collective-permute-done | bytes 262176 | tf_op jit(solution)/shard_map/ppermute | solution.py:33
  27.2 1.3 %copy-done = bf16[1,64,10240]{2,1,0:T(8,128)(2,1)S(1)} copy-done((bf16[1,64,10240]{2,1,0:T(8,128)(2,1)S(1)}, bf16[1,64,10240]{2,1,0:T(8,128)(2,1)}, u32[]{:S(2)}) %copy-start) | copy-done | bytes 1310744
  28.5 1.2 %copy-done.1 = bf16[1,8192,64]{1,2,0:T(8,128)(2,1)S(1)} copy-done((bf16[1,8192,64]{1,2,0:T(8,128)(2,1)S(1)}, bf16[1,8192,64]{1,2,0:T(8,128)(2,1)}, u32[]{:S(2)}) %copy-start.1) | copy-done | bytes 1048600
  29.7 0.9 %copy-done.2 = bf16[1,16,8192]{2,1,0:T(8,128)(2,1)S(1)} copy-done((bf16[1,16,8192]{2,1,0:T(8,128)(2,1)S(1)}, bf16[1,16,8192]{2,1,0:T(8,128)(2,1)}, u32[]{:S(2)}) %copy-start.2) | copy-done | bytes 262168
  30.7 0.7 %copy-done.3 = s32[2,12]{1,0:T(2,128)S(1)} copy-done((s32[2,12]{1,0:T(2,128)S(1)}, s32[2,12]{1,0:T(2,128)}, u32[]{:S(2)}) %copy-start.3) | copy-done | bytes 120
  31.3 0.7 %copy-done.5 = s32[1,12]{1,0:T(1,128)S(1)} copy-done((s32[1,12]{1,0:T(1,128)S(1)}, s32[1,12]{1,0:T(1,128)}, u32[]{:S(2)}) %copy-start.5) | copy-done | bytes 72
  32.7 4.3 %lift.1 = (bf16[128,8192]{1,0:T(8,128)(2,1)S(1)}, bf16[8,32,1280]{2,1,0:T(8,128)(2,1)}) custom-call(s32[2,12]{1,0:T(2,128)S(1)} %copy-done.3, s32[1,12]{1,0:T(1,128)S(1)} %copy-done.5, s32[16]{0:T(128)S(1)} %copy-done.7, bf16[64,8192]{1,0:T(8,128)(2,1)S(1)} %bitcast.13, bf16[64,8192]{1,0:T(8,128)(2,1)S(1)} %collective-permute-done.refs_1_, ...), custom_call_target="tpu_custom_call" | custom-call | flops 352321536 | bytes 4718592 | tf_op jit(solution)/shard_map/lift/pallas_call | solution.py:156
  37.0 6.3 %all-to-all-start = ((bf16[8,32,1280]{2,1,0:T(8,128)(2,1)}), bf16[8,32,1280]{2,1,0:T(8,128)(2,1)S(1)}, u32[]{:S(2)}, u32[]{:S(2)}) async-start(bf16[8,32,1280]{2,1,0:T(8,128)(2,1)} %get-tuple-element.8), calls=%async_computation | async-start | bytes 1310720 | tf_op jit(solution)/shard_map/all_to_all | solution.py:177
  43.4 8.5 %fusion.base_ref = f32[128,1280]{1,0:T(8,128)S(1)} fusion(bf16[128,8192]{1,0:T(8,128)(2,1)S(1)} %get-tuple-element.7, bf16[8192,1280]{1,0:T(8,128)(2,1)} %param.8), kind=kOutput, calls=%fused_computation | convolution fusion | flops 2684354560 | bytes 23724032 | tf_op jit(solution)/shard_map/dot_general | solution.py:179
  51.9 7.0 %all-to-all-done = bf16[8,32,1280]{2,1,0:T(8,128)(2,1)S(1)} async-done(((bf16[8,32,1280]{2,1,0:T(8,128)(2,1)}), bf16[8,32,1280]{2,1,0:T(8,128)(2,1)S(1)}, u32[]{:S(2)}, u32[]{:S(2)}) %all-to-all-start) | async-done | bytes 655392 | tf_op jit(solution)/shard_map/all_to_all | solution.py:177
  58.9 2.0 %add.1 = bf16[128,1280]{1,0:T(8,128)(2,1)} custom-call(s32[2,12]{1,0:T(2,128)S(1)} %copy-done.4, s32[1,12]{1,0:T(1,128)S(1)} %copy-done.6, s32[16]{0:T(128)S(1)} %copy-done.8, f32[128,1280]{1,0:T(8,128)S(1)} %fusion.base_ref, bf16[256,1280]{1,0:T(8,128)(2,1)S(1)} %bitcast.9), custom_call_target="tpu_custom_call" | custom-call | tf_op jit(solution)/shard_map/add/pallas_call | solution.py:180
  (25 shorter events, 1.2 us)
Async XLA Ops:
  0.0 3.5 %collective-permute-start.3 = (bf16[16,8192]{1,0:T(8,128)(2,1)}, bf16[16,8192]{1,0:T(8,128)(2,1)S(1)}, u32[]{:S(2)}, u32[]{:S(2)}) collective-permute-start(bf16[16,8192]{1,0:T(8,128)(2,1)} %bitcast.14), channel_id=1, source_target_pairs={{0,8},{8,0},{1,9},{9,1},{2,10},{10,2},{3,11},{11,3},{4,12},{12,4},... | collective-permute-start | bytes 786440 | tf_op jit(solution)/shard_map/ppermute | solution.py:36
  0.5 26.7 %collective-permute-start.1 = (bf16[64,10240]{1,0:T(8,128)(2,1)}, bf16[64,10240]{1,0:T(8,128)(2,1)S(1)}, u32[]{:S(2)}, u32[]{:S(2)}) collective-permute-start(bf16[64,10240]{1,0:T(8,128)(2,1)} %bitcast.10), channel_id=1, source_target_pairs={{8,0},{0,8},{9,1},{1,9},{10,2},{2,10},{11,3},{3,11},{12,4},{4,12},... | collective-permute-start | bytes 3932168 | tf_op jit(solution)/shard_map/ppermute | solution.py:16
  0.5 7.5 %collective-permute-start.2 = (bf16[16,8192]{1,0:T(8,128)(2,1)}, bf16[16,8192]{1,0:T(8,128)(2,1)S(1)}, u32[]{:S(2)}, u32[]{:S(2)}) collective-permute-start(bf16[16,8192]{1,0:T(8,128)(2,1)} %bitcast.15), channel_id=1, source_target_pairs={{0,2},{10,8},{2,4},{12,10},{4,6},{14,12},{6,7},{15,14},{7,5},{13,1... | collective-permute-start | bytes 786440 | tf_op jit(solution)/shard_map/ppermute | solution.py:33
  3.5 7.3 %collective-permute-start.4 = (bf16[16,8192]{1,0:T(8,128)(2,1)S(1)}, bf16[16,8192]{1,0:T(8,128)(2,1)S(1)}, u32[]{:S(2)}, u32[]{:S(2)}) collective-permute-start(bf16[16,8192]{1,0:T(8,128)(2,1)S(1)} %collective-permute-done.3), channel_id=1, source_target_pairs={{0,2},{10,8},{2,4},{12,10},{4,6},{14,12},{6,7},{15,14},{7,5},{13,1... | collective-permute-start | bytes 786440 | tf_op jit(solution)/shard_map/ppermute | solution.py:33
  5.1 22.0 %collective-permute-start = (bf16[64,8192]{1,0:T(8,128)(2,1)}, bf16[64,8192]{1,0:T(8,128)(2,1)S(1)}, u32[]{:S(2)}, u32[]{:S(2)}) collective-permute-start(bf16[64,8192]{1,0:T(8,128)(2,1)} %bitcast.12), channel_id=1, source_target_pairs={{8,0},{0,8},{9,1},{1,9},{10,2},{2,10},{11,3},{3,11},{12,4},{4,12},... | collective-permute-start | bytes 3145736 | tf_op jit(solution)/shard_map/ppermute | solution.py:16
  8.0 6.4 %collective-permute-start.6 = (bf16[16,8192]{1,0:T(8,128)(2,1)S(1)}, bf16[16,8192]{1,0:T(8,128)(2,1)S(1)}, u32[]{:S(2)}, u32[]{:S(2)}) collective-permute-start(bf16[16,8192]{1,0:T(8,128)(2,1)S(1)} %collective-permute-done.2.refs_5_), channel_id=1, source_target_pairs={{0,2},{10,8},{2,4},{12,10},{4,6},{14,12},{6,7},{15,14},{7,5},{13,1... | collective-permute-start | bytes 786440 | tf_op jit(solution)/shard_map/ppermute | solution.py:33
  10.8 6.4 %collective-permute-start.7 = (bf16[16,8192]{1,0:T(8,128)(2,1)S(1)}, bf16[16,8192]{1,0:T(8,128)(2,1)S(1)}, u32[]{:S(2)}, u32[]{:S(2)}) collective-permute-start(bf16[16,8192]{1,0:T(8,128)(2,1)S(1)} %collective-permute-done.4), channel_id=1, source_target_pairs={{0,2},{10,8},{2,4},{12,10},{4,6},{14,12},{6,7},{15,14},{7,5},{13,1... | collective-permute-start | bytes 786440 | tf_op jit(solution)/shard_map/ppermute | solution.py:33
  12.9 6.4 %collective-permute-start.5 = (bf16[16,8192]{1,0:T(8,128)(2,1)S(1)}, bf16[16,8192]{1,0:T(8,128)(2,1)S(1)}, u32[]{:S(2)}, u32[]{:S(2)}) collective-permute-start(bf16[16,8192]{1,0:T(8,128)(2,1)S(1)} %collective-permute-done.4), channel_id=1, source_target_pairs={{0,8},{8,0},{1,9},{9,1},{2,10},{10,2},{3,11},{11,3},{4,12},{12,4},... | collective-permute-start | bytes 786440 | tf_op jit(solution)/shard_map/ppermute | solution.py:36
  14.4 6.4 %collective-permute-start.9 = (bf16[16,8192]{1,0:T(8,128)(2,1)S(1)}, bf16[16,8192]{1,0:T(8,128)(2,1)S(1)}, u32[]{:S(2)}, u32[]{:S(2)}) collective-permute-start(bf16[16,8192]{1,0:T(8,128)(2,1)S(1)} %collective-permute-done.6.refs_7_), channel_id=1, source_target_pairs={{0,2},{10,8},{2,4},{12,10},{4,6},{14,12},{6,7},{15,14},{7,5},{13,1... | collective-permute-start | bytes 786440 | tf_op jit(solution)/shard_map/ppermute | solution.py:33
  17.2 6.4 %collective-permute-start.10 = (bf16[16,8192]{1,0:T(8,128)(2,1)S(1)}, bf16[16,8192]{1,0:T(8,128)(2,1)S(1)}, u32[]{:S(2)}, u32[]{:S(2)}) collective-permute-start(bf16[16,8192]{1,0:T(8,128)(2,1)S(1)} %collective-permute-done.7), channel_id=1, source_target_pairs={{0,2},{10,8},{2,4},{12,10},{4,6},{14,12},{6,7},{15,14},{7,5},{13,1... | collective-permute-start | bytes 786440 | tf_op jit(solution)/shard_map/ppermute | solution.py:33
  19.3 4.3 %collective-permute-start.8 = (bf16[16,8192]{1,0:T(8,128)(2,1)S(1)}, bf16[16,8192]{1,0:T(8,128)(2,1)S(1)}, u32[]{:S(2)}, u32[]{:S(2)}) collective-permute-start(bf16[16,8192]{1,0:T(8,128)(2,1)S(1)} %collective-permute-done.7), channel_id=1, source_target_pairs={{0,8},{8,0},{1,9},{9,1},{2,10},{10,2},{3,11},{11,3},{4,12},{12,4},... | collective-permute-start | bytes 786440 | tf_op jit(solution)/shard_map/ppermute | solution.py:36
  20.8 6.4 %collective-permute-start.12 = (bf16[16,8192]{1,0:T(8,128)(2,1)S(1)}, bf16[16,8192]{1,0:T(8,128)(2,1)S(1)}, u32[]{:S(2)}, u32[]{:S(2)}) collective-permute-start(bf16[16,8192]{1,0:T(8,128)(2,1)S(1)} %collective-permute-done.9.refs_9_), channel_id=1, source_target_pairs={{0,2},{10,8},{2,4},{12,10},{4,6},{14,12},{6,7},{15,14},{7,5},{13,1... | collective-permute-start | bytes 786440 | tf_op jit(solution)/shard_map/ppermute | solution.py:33
  23.6 3.6 %collective-permute-start.11 = (bf16[16,8192]{1,0:T(8,128)(2,1)S(1)}, bf16[16,8192]{1,0:T(8,128)(2,1)S(1)}, u32[]{:S(2)}, u32[]{:S(2)}) collective-permute-start(bf16[16,8192]{1,0:T(8,128)(2,1)S(1)} %collective-permute-done.10), channel_id=1, source_target_pairs={{0,8},{8,0},{1,9},{9,1},{2,10},{10,2},{3,11},{11,3},{4,12},{12,4},... | collective-permute-start | bytes 786440 | tf_op jit(solution)/shard_map/ppermute | solution.py:36
  27.2 1.3 %copy-start = (bf16[1,64,10240]{2,1,0:T(8,128)(2,1)S(1)}, bf16[1,64,10240]{2,1,0:T(8,128)(2,1)}, u32[]{:S(2)}) copy-start(bf16[1,64,10240]{2,1,0:T(8,128)(2,1)} %param.10) | copy-start | bytes 3932164
  28.5 1.2 %copy-start.1 = (bf16[1,8192,64]{1,2,0:T(8,128)(2,1)S(1)}, bf16[1,8192,64]{1,2,0:T(8,128)(2,1)}, u32[]{:S(2)}) copy-start(bf16[1,8192,64]{1,2,0:T(8,128)(2,1)} %param.9) | copy-start | bytes 3145732
  29.7 0.9 %copy-start.2 = (bf16[1,16,8192]{2,1,0:T(8,128)(2,1)S(1)}, bf16[1,16,8192]{2,1,0:T(8,128)(2,1)}, u32[]{:S(2)}) copy-start(bf16[1,16,8192]{2,1,0:T(8,128)(2,1)} %param.7) | copy-start | bytes 786436
  30.7 0.7 %copy-start.3 = (s32[2,12]{1,0:T(2,128)S(1)}, s32[2,12]{1,0:T(2,128)}, u32[]{:S(2)}) copy-start(s32[2,12]{1,0:T(2,128)} %ids_ref.3) | copy-start | bytes 292
  31.3 0.7 %copy-start.5 = (s32[1,12]{1,0:T(1,128)S(1)}, s32[1,12]{1,0:T(1,128)}, u32[]{:S(2)}) copy-start(s32[1,12]{1,0:T(1,128)} %lengths_ref.3) | copy-start | bytes 148
  32.0 0.7 %copy-start.7 = (s32[16]{0:T(128)S(1)}, s32[16]{0:T(128)}, u32[]{:S(2)}) copy-start(s32[16]{0:T(128)} %slots_ref.3) | copy-start | bytes 196
  37.0 21.9 %all-to-all-start = ((bf16[8,32,1280]{2,1,0:T(8,128)(2,1)}), bf16[8,32,1280]{2,1,0:T(8,128)(2,1)S(1)}, u32[]{:S(2)}, u32[]{:S(2)}) async-start(bf16[8,32,1280]{2,1,0:T(8,128)(2,1)} %get-tuple-element.8), calls=%async_computation | async-start | bytes 1310720 | tf_op jit(solution)/shard_map/all_to_all | solution.py:177
  43.4 15.6 %copy-start.4 = (s32[2,12]{1,0:T(2,128)S(1)}, s32[2,12]{1,0:T(2,128)}, u32[]{:S(2)}) copy-start(s32[2,12]{1,0:T(2,128)} %ids_ref.3) | copy-start | bytes 292
  43.4 15.6 %copy-start.6 = (s32[1,12]{1,0:T(1,128)S(1)}, s32[1,12]{1,0:T(1,128)}, u32[]{:S(2)}) copy-start(s32[1,12]{1,0:T(1,128)} %lengths_ref.3) | copy-start | bytes 148
  43.4 15.6 %copy-start.8 = (s32[16]{0:T(128)S(1)}, s32[16]{0:T(128)}, u32[]{:S(2)}) copy-start(s32[16]{0:T(128)} %slots_ref.3) | copy-start | bytes 196

commit v10 on v9

v10 whole, which is shorter than its diff:
```python
import functools

import jax
import jax.numpy as jnp
from jax import lax
from jax.experimental import pallas as pl
from jax.experimental.pallas import tpu as pltpu
from jax.sharding import PartitionSpec as P

adapter_scale = 1.0


def swapped(x, axis):
    n = lax.axis_size(axis)
    return [x] + [
        lax.ppermute(x, axis, [((i + s) % n, i) for i in range(n)]) for s in range(1, n)
    ]


def ring_of(n):
    return list(range(0, n, 2)) + list(range(1, n, 2))[::-1]


def ring_gather(block):
    n = lax.axis_size("tp")
    ring = ring_of(n)
    onward = []
    for i in range(n):
        onward.append((ring[i], ring[(i + 1) % n]))
        onward.append((n + ring[(i + 1) % n], n + ring[i]))

    def sent(x):
        return lax.ppermute(x, ("grp", "tp"), onward)

    def handed(x):
        return lax.ppermute(x, "grp", [(0, 1), (1, 0)])

    mine, other = block, handed(block)
    pieces = [block]
    for step in range(1, n // 2):
        mine, other = sent(mine), sent(other)
        pieces += [mine, handed(other)]
    return pieces + [sent(mine)]


def ring_sources(n):
    me = lax.axis_index("tp")
    way = 1 - 2 * lax.axis_index("grp")
    place = jnp.where(lax.rem(me, 2) == 0, me // 2, n - 1 - me // 2)
    distances = [0] + [d for i in range(1, n // 2) for d in (way * i, -way * i)] + [n // 2]
    sources = []
    for distance in distances:
        at = lax.rem(place - distance + 2 * n, n)
        sources.append(jnp.where(at < n // 2, 2 * at, 2 * (n - 1 - at) + 1))
    return sources


def prepare_kernel(groups, tp, ids_ref, lengths_ref, slots_ref, *refs):
    n = (len(refs) - 2) // 2
    row_ref, column_ref = refs[n : n + 2]
    for source, target in zip(refs[:n], refs[n + 2 :]):
        target[...] = source[...]
    group = lax.axis_index("grp")
    tok_all = row_ref.shape[1]
    longest = tok_all // 8
    along = lax.broadcasted_iota(jnp.int32, row_ref.shape, 1)
    down = lax.broadcasted_iota(jnp.int32, column_ref.shape, 0)

    def add(request, carry):
        start, row, column = carry
        slot = slots_ref[ids_ref[group, request]]
        end = start + lengths_ref[0, request]
        panel = lax.rem(slot // tp - group + groups, groups)
        first = (lax.rem(slot, tp) * groups + panel) * longest - start
        row = jnp.where((along >= start) & (along < end), first + along, row)
        column = jnp.where((down >= start) & (down < end), first + down, column)
        return end, row, column

    carry = (jnp.int32(0), jnp.zeros_like(along), jnp.zeros_like(down))
    _, row_ref[...], column_ref[...] = lax.fori_loop(0, ids_ref.shape[1], add, carry)


def lift_kernel(groups, tp, place_ref, *refs):
    downs, ups, pieces = refs[:groups], refs[groups : 2 * groups], refs[2 * groups : -3]
    tokens_ref, out_ref, up_ref = refs[-3:]
    rank = ups[0].shape[0]
    rows = pieces[0].shape[0]
    tok_all = tokens_ref.shape[0]
    parts, slots, columns = out_ref.shape
    for piece, source in zip(pieces, ring_sources(tp)):
        tokens_ref[pl.ds(pl.multiple_of(source * rows, rows), rows), :] = piece[...]
    for s, up in enumerate(ups):
        up_ref[s * rank : (s + 1) * rank, :] = up[...]
    down = jnp.concatenate([down[...] for down in downs], axis=0).T
    low = jnp.dot(tokens_ref[...], down, preferred_element_type=jnp.float32)
    here = lax.broadcasted_iota(jnp.int32, (slots, tok_all), 0) + lax.axis_index("tp") * slots
    chosen = (here == place_ref[...]).astype(jnp.bfloat16)
    picked = jnp.dot(chosen, low.astype(jnp.bfloat16), preferred_element_type=jnp.float32)
    row_panel = lax.broadcasted_iota(jnp.int32, picked.shape, 0) // (slots // groups)
    rank_panel = lax.broadcasted_iota(jnp.int32, picked.shape, 1) // rank
    picked = jnp.where(row_panel == rank_panel, picked, 0.0).astype(jnp.bfloat16)
    for part in range(parts):
        out_ref[part] = jnp.dot(
            picked,
            up_ref[:, part * columns : (part + 1) * columns],
            preferred_element_type=jnp.float32,
        ).astype(out_ref.dtype)


def add_kernel(place_ref, base_ref, lifts_ref, out_ref):
    place = lax.broadcasted_iota(jnp.int32, (base_ref.shape[0], lifts_ref.shape[0]), 1)
    chosen = (place == place_ref[...]).astype(jnp.bfloat16)
    lift = jnp.dot(chosen, lifts_ref[...], preferred_element_type=jnp.float32)
    out_ref[...] = (base_ref[...] + adapter_scale * lift).astype(out_ref.dtype)


def on_device(
    tokens,
    base_projection_weight,
    adapter_down_panels,
    adapter_up_panels,
    request_adapter_ids,
    request_token_lengths,
    adapter_store_slot,
):
    groups = lax.axis_size("grp")
    tp = lax.axis_size("tp")
    width, rank = adapter_down_panels.shape[1:]
    columns = base_projection_weight.shape[1]
    tok_all = tokens.shape[1] * tp
    longest = tok_all // 8
    here = groups * longest
    in_vmem = pl.BlockSpec(memory_space=pltpu.VMEM)
    in_smem = pl.BlockSpec(memory_space=pltpu.SMEM)
    small = pltpu.CompilerParams(vmem_limit_bytes=16 * 2**20)

    arrays = (tokens[0], adapter_down_panels[0].T, adapter_up_panels[0])
    pieces = ring_gather(arrays[0])
    others = [swapped(x, "grp")[1:] for x in arrays[1:]]
    row, column, own, down, up = pl.pallas_call(
        functools.partial(prepare_kernel, groups, tp),
        out_shape=[
            jax.ShapeDtypeStruct((1, tok_all), jnp.int32),
            jax.ShapeDtypeStruct((tok_all, 1), jnp.int32),
        ]
        + [jax.ShapeDtypeStruct(x.shape, x.dtype) for x in arrays],
        in_specs=[in_smem] * 3 + [in_vmem] * 3,
        out_specs=[in_vmem] * 5,
        compiler_params=small,
        name="prepare",
    )(request_adapter_ids, request_token_lengths, adapter_store_slot, *arrays)
    panels = [down, *others[0], up, *others[1]]
    pieces[0] = own

    gathered, lifts = pl.pallas_call(
        functools.partial(lift_kernel, groups, tp),
        out_shape=[
            jax.ShapeDtypeStruct((tok_all, width), jnp.bfloat16),
            jax.ShapeDtypeStruct((tp, here, columns), jnp.bfloat16),
        ],
        in_specs=[in_vmem] * (1 + len(panels) + len(pieces)),
        out_specs=[in_vmem] * 2,
        scratch_shapes=[pltpu.VMEM((groups * rank, tp * columns), jnp.bfloat16)],
        compiler_params=pltpu.CompilerParams(vmem_limit_bytes=24 * 2**20),
        cost_estimate=pl.CostEstimate(
            flops=2 * groups * rank * (tok_all * width + here * tp * columns),
            bytes_accessed=2 * groups * rank * (width + tp * columns),
            transcendentals=0,
        ),
        name="lift",
    )(row, *panels, *pieces)
    lifts = lax.all_to_all(lifts, "tp", split_axis=0, concat_axis=0, tiled=True)

    base = jnp.dot(gathered, base_projection_weight, preferred_element_type=jnp.float32)
    out = pl.pallas_call(
        add_kernel,
        out_shape=jax.ShapeDtypeStruct((tok_all, columns), jnp.bfloat16),
        in_specs=[in_vmem] * 3,
        out_specs=in_vmem,
        compiler_params=small,
        name="add",
    )(column, base, lifts.reshape(tp * here, columns))
    return out[None]


def solution(mesh):
    return jax.shard_map(
        on_device,
        mesh=mesh,
        in_specs=(
            P(("rep", "grp"), "tp", None),
            P(None, "tp"),
            P(("grp", "tp"), None, None),
            P(("grp", "tp"), None, None),
            P("rep", None),
            P(("rep", "grp"), None),
            P(),
        ),
        out_specs=P(("rep", "grp"), None, "tp"),
        check_vma=False,
    )
```

time: 61.2 us -> 59 us (0.964)
  Pallas kernels: 6.31 us -> 5.15 us
  waiting for transfers between devices: 18.6 us -> 17.6 us
    ppermute x7, waiting for transfers between devices: 11.6 us -> 8.06 us  [sent(): return lax.ppermute(x, ('grp', 'tp'), onward)]
    all_to_all x1, waiting for transfers between devices: 6.98 us -> 9.47 us  [on_device(): lifts = lax.all_to_all(lifts, 'tp', split_axis=0, concat_axis=0, tiled=True)]
    pallas_call x1, Pallas kernels: 4.35 us -> 3.01 us  [on_device(): pl.pallas_call(functools.partial(lift_kernel, groups, tp), out_shape=[jax...]
    pallas_call x1 -> x2, Pallas kernels: 1.96 us -> 2.14 us  [the longest x1 1.12 us: on_device(): pl.pallas_call(functools.partial(prepare_kernel, groups, tp), out_shape=[...]
    unnamed x18 -> x12, local copies, waits for them, and re-layouts: 5.49 us -> 5.48 us
  transfers between devices with their start and end apart: 14 -> 14, of which waited for: 8 -> 7; matrix products, arithmetic and copies ran while one was open for 14% -> 15% of each run, Pallas kernels for 0% -> 2%
where the time goes in v10:
time: 59 us; the launch traced here: 58.6 us
  starting transfers between devices  21.9 us (37%)
  waiting for transfers between devices  17.6 us (30%)
  matrix products  8.53 us (14%)
  local copies, waits for them, and re-layouts  5.48 us (9%)
  Pallas kernels  5.15 us (9%)
    ppermute x7, starting transfers between devices, sent(): return lax.ppermute(x, ('grp', 'tp'), onward)  15 us
    all_to_all x1, waiting for transfers between devices, on_device(): lifts = lax.all_to_all(lifts, 'tp', split_axis=0, concat_axis=0, tiled=True)  9.47 us
    dot_general x1, matrix products, on_device(): jnp.dot(gathered, base_projection_weight, preferred_element_type=jnp.floa...  8.53 us
    ppermute x7, waiting for transfers between devices, sent(): return lax.ppermute(x, ('grp', 'tp'), onward)  8.06 us
    all_to_all x1, starting transfers between devices, on_device(): lifts = lax.all_to_all(lifts, 'tp', split_axis=0, concat_axis=0, tiled=True)  6.34 us
    unnamed x12, local copies, waits for them, and re-layouts  5.48 us
    pallas_call x1, Pallas kernels, on_device(): pl.pallas_call(functools.partial(lift_kernel, groups, tp), out_shape=[jax...  3.01 us
  transfers between devices with their start and end apart: 14, of which 7 were waited for; matrix products, arithmetic and copies ran while one was open for 15% of the time, Pallas kernels for 2%

profile of v10, /device:TPU:0, one launch (start us, length us, event | category | flops | bytes accessed | tf_op | source)
XLA Modules:
  0.0 58.6 jit_solution(10314451532992781450)
XLA Ops:
  0.5 3.0 %collective-permute-start.2 = (bf16[16,8192]{1,0:T(8,128)(2,1)}, bf16[16,8192]{1,0:T(8,128)(2,1)S(1)}, u32[]{:S(2)}, u32[]{:S(2)}) collective-permute-start(bf16[16,8192]{1,0:T(8,128)(2,1)} %bitcast.15), channel_id=1, source_target_pairs={{0,2},{10,8},{2,4},{12,10},{4,6},{14,12},{6,7},{15,14},{7,5},{13,1... | collective-permute-start | bytes 786440 | tf_op jit(solution)/shard_map/ppermute | solution.py:33
  3.5 1.6 %collective-permute-start.4 = (bf16[16,8192]{1,0:T(8,128)(2,1)S(1)}, bf16[16,8192]{1,0:T(8,128)(2,1)S(1)}, u32[]{:S(2)}, u32[]{:S(2)}) collective-permute-start(bf16[16,8192]{1,0:T(8,128)(2,1)S(1)} %collective-permute-done.3), channel_id=1, source_target_pairs={{0,2},{10,8},{2,4},{12,10},{4,6},{14,12},{6,7},{15,14},{7,5},{13,1... | collective-permute-start | bytes 786440 | tf_op jit(solution)/shard_map/ppermute | solution.py:33
  5.1 2.9 %collective-permute-done.2.refs_5_ = bf16[16,8192]{1,0:T(8,128)(2,1)S(1)} collective-permute-done((bf16[16,8192]{1,0:T(8,128)(2,1)}, bf16[16,8192]{1,0:T(8,128)(2,1)S(1)}, u32[]{:S(2)}, u32[]{:S(2)}) %collective-permute-start.2) | collective-permute-done | bytes 262176 | tf_op jit(solution)/shard_map/ppermute | solution.py:33
  8.0 2.1 %collective-permute-start.6 = (bf16[16,8192]{1,0:T(8,128)(2,1)S(1)}, bf16[16,8192]{1,0:T(8,128)(2,1)S(1)}, u32[]{:S(2)}, u32[]{:S(2)}) collective-permute-start(bf16[16,8192]{1,0:T(8,128)(2,1)S(1)} %collective-permute-done.2.refs_5_), channel_id=1, source_target_pairs={{0,2},{10,8},{2,4},{12,10},{4,6},{14,12},{6,7},{15,14},{7,5},{13,1... | collective-permute-start | bytes 786440 | tf_op jit(solution)/shard_map/ppermute | solution.py:33
  10.1 0.7 %collective-permute-done.4 = bf16[16,8192]{1,0:T(8,128)(2,1)S(1)} collective-permute-done((bf16[16,8192]{1,0:T(8,128)(2,1)S(1)}, bf16[16,8192]{1,0:T(8,128)(2,1)S(1)}, u32[]{:S(2)}, u32[]{:S(2)}) %collective-permute-start.4) | collective-permute-done | bytes 262176 | tf_op jit(solution)/shard_map/ppermute | solution.py:33
  10.8 2.1 %collective-permute-start.7 = (bf16[16,8192]{1,0:T(8,128)(2,1)S(1)}, bf16[16,8192]{1,0:T(8,128)(2,1)S(1)}, u32[]{:S(2)}, u32[]{:S(2)}) collective-permute-start(bf16[16,8192]{1,0:T(8,128)(2,1)S(1)} %collective-permute-done.4), channel_id=1, source_target_pairs={{0,2},{10,8},{2,4},{12,10},{4,6},{14,12},{6,7},{15,14},{7,5},{13,1... | collective-permute-start | bytes 786440 | tf_op jit(solution)/shard_map/ppermute | solution.py:33
  12.9 1.5 %collective-permute-done.6.refs_7_ = bf16[16,8192]{1,0:T(8,128)(2,1)S(1)} collective-permute-done((bf16[16,8192]{1,0:T(8,128)(2,1)S(1)}, bf16[16,8192]{1,0:T(8,128)(2,1)S(1)}, u32[]{:S(2)}, u32[]{:S(2)}) %collective-permute-start.6) | collective-permute-done | bytes 262176 | tf_op jit(solution)/shard_map/ppermute | solution.py:33
  14.4 2.1 %collective-permute-start.9 = (bf16[16,8192]{1,0:T(8,128)(2,1)S(1)}, bf16[16,8192]{1,0:T(8,128)(2,1)S(1)}, u32[]{:S(2)}, u32[]{:S(2)}) collective-permute-start(bf16[16,8192]{1,0:T(8,128)(2,1)S(1)} %collective-permute-done.6.refs_7_), channel_id=1, source_target_pairs={{0,2},{10,8},{2,4},{12,10},{4,6},{14,12},{6,7},{15,14},{7,5},{13,1... | collective-permute-start | bytes 786440 | tf_op jit(solution)/shard_map/ppermute | solution.py:33
  16.5 0.7 %collective-permute-done.7 = bf16[16,8192]{1,0:T(8,128)(2,1)S(1)} collective-permute-done((bf16[16,8192]{1,0:T(8,128)(2,1)S(1)}, bf16[16,8192]{1,0:T(8,128)(2,1)S(1)}, u32[]{:S(2)}, u32[]{:S(2)}) %collective-permute-start.7) | collective-permute-done | bytes 262176 | tf_op jit(solution)/shard_map/ppermute | solution.py:33
  17.2 2.1 %collective-permute-start.10 = (bf16[16,8192]{1,0:T(8,128)(2,1)S(1)}, bf16[16,8192]{1,0:T(8,128)(2,1)S(1)}, u32[]{:S(2)}, u32[]{:S(2)}) collective-permute-start(bf16[16,8192]{1,0:T(8,128)(2,1)S(1)} %collective-permute-done.7), channel_id=1, source_target_pairs={{0,2},{10,8},{2,4},{12,10},{4,6},{14,12},{6,7},{15,14},{7,5},{13,1... | collective-permute-start | bytes 786440 | tf_op jit(solution)/shard_map/ppermute | solution.py:33
  19.3 1.5 %collective-permute-done.9.refs_9_ = bf16[16,8192]{1,0:T(8,128)(2,1)S(1)} collective-permute-done((bf16[16,8192]{1,0:T(8,128)(2,1)S(1)}, bf16[16,8192]{1,0:T(8,128)(2,1)S(1)}, u32[]{:S(2)}, u32[]{:S(2)}) %collective-permute-start.9) | collective-permute-done | bytes 262176 | tf_op jit(solution)/shard_map/ppermute | solution.py:33
  20.8 2.1 %collective-permute-start.12 = (bf16[16,8192]{1,0:T(8,128)(2,1)S(1)}, bf16[16,8192]{1,0:T(8,128)(2,1)S(1)}, u32[]{:S(2)}, u32[]{:S(2)}) collective-permute-start(bf16[16,8192]{1,0:T(8,128)(2,1)S(1)} %collective-permute-done.9.refs_9_), channel_id=1, source_target_pairs={{0,2},{10,8},{2,4},{12,10},{4,6},{14,12},{6,7},{15,14},{7,5},{13,1... | collective-permute-start | bytes 786440 | tf_op jit(solution)/shard_map/ppermute | solution.py:33
  22.9 0.7 %collective-permute-done.10 = bf16[16,8192]{1,0:T(8,128)(2,1)S(1)} collective-permute-done((bf16[16,8192]{1,0:T(8,128)(2,1)S(1)}, bf16[16,8192]{1,0:T(8,128)(2,1)S(1)}, u32[]{:S(2)}, u32[]{:S(2)}) %collective-permute-start.10) | collective-permute-done | bytes 262176 | tf_op jit(solution)/shard_map/ppermute | solution.py:33
  23.6 1.3 %copy-done = bf16[1,64,10240]{2,1,0:T(8,128)(2,1)S(1)} copy-done((bf16[1,64,10240]{2,1,0:T(8,128)(2,1)S(1)}, bf16[1,64,10240]{2,1,0:T(8,128)(2,1)}, u32[]{:S(2)}) %copy-start) | copy-done | bytes 1310744
  24.9 1.2 %copy-done.1 = bf16[1,8192,64]{1,2,0:T(8,128)(2,1)S(1)} copy-done((bf16[1,8192,64]{1,2,0:T(8,128)(2,1)S(1)}, bf16[1,8192,64]{1,2,0:T(8,128)(2,1)}, u32[]{:S(2)}) %copy-start.1) | copy-done | bytes 1048600
  26.1 0.9 %copy-done.2 = bf16[1,16,8192]{2,1,0:T(8,128)(2,1)S(1)} copy-done((bf16[1,16,8192]{2,1,0:T(8,128)(2,1)S(1)}, bf16[1,16,8192]{2,1,0:T(8,128)(2,1)}, u32[]{:S(2)}) %copy-start.2) | copy-done | bytes 262168
  27.1 0.7 %copy-done.3 = s32[2,12]{1,0:T(2,128)S(1)} copy-done((s32[2,12]{1,0:T(2,128)S(1)}, s32[2,12]{1,0:T(2,128)}, u32[]{:S(2)}) %copy-start.3) | copy-done | bytes 120
  27.8 0.7 %copy-done.4 = s32[1,12]{1,0:T(1,128)S(1)} copy-done((s32[1,12]{1,0:T(1,128)S(1)}, s32[1,12]{1,0:T(1,128)}, u32[]{:S(2)}) %copy-start.4) | copy-done | bytes 72
  29.1 1.1 %prepare.1 = (s32[1,128]{1,0:T(1,128)S(1)}, s32[128,1]{1,0:T(8,128)S(1)}, bf16[16,8192]{1,0:T(8,128)(2,1)S(1)}, bf16[64,8192]{1,0:T(8,128)(2,1)S(1)}, bf16[64,10240]{1,0:T(8,128)(2,1)S(1)}) custom-call(s32[2,12]{1,0:T(2,128)S(1)} %copy-done.3, s32[1,12]{1,0:T(1,128)S(1)} %copy-done.4, s32[16]{0:T(128)S(1)} %copy-done.5, bf16[16,8192]{1,0:T(8,128)(2,1)S(1)} %bitcast.16, ...), custom_call_target="tpu_custom_call" | custom-call | tf_op jit(solution)/shard_map/prepare/pallas_call | solution.py:140
  30.3 3.0 %lift.1 = (bf16[128,8192]{1,0:T(8,128)(2,1)S(1)}, bf16[8,32,1280]{2,1,0:T(8,128)(2,1)}) custom-call(s32[1,128]{1,0:T(1,128)S(1)} %get-tuple-element.13.place_ref, bf16[64,8192]{1,0:T(8,128)(2,1)S(1)} %get-tuple-element.14.refs_0_, bf16[64,8192]{1,0:T(8,128)(2,1)S(1)} %collective-permute-done.refs_1_, bf16[64,10240]{1,0:T(8,128)(2,1)S(1)} %get-tuple-element.15.refs_2_, ...), custom_call_target="tpu_custom_call" | custom-call | flops 352321536 | bytes 4718592 | tf_op jit(solution)/shard_map/lift/pallas_call | solution.py:155
  33.3 6.3 %all-to-all-start = ((bf16[8,32,1280]{2,1,0:T(8,128)(2,1)}), bf16[8,32,1280]{2,1,0:T(8,128)(2,1)S(1)}, u32[]{:S(2)}, u32[]{:S(2)}) async-start(bf16[8,32,1280]{2,1,0:T(8,128)(2,1)} %get-tuple-element.18), calls=%async_computation | async-start | bytes 1310720 | tf_op jit(solution)/shard_map/all_to_all | solution.py:172
  39.6 8.5 %fusion.base_ref = f32[128,1280]{1,0:T(8,128)S(1)} fusion(bf16[128,8192]{1,0:T(8,128)(2,1)S(1)} %get-tuple-element.17, bf16[8192,1280]{1,0:T(8,128)(2,1)} %param.8), kind=kOutput, calls=%fused_computation | convolution fusion | flops 2684354560 | bytes 23724032 | tf_op jit(solution)/shard_map/dot_general | solution.py:174
  48.1 9.5 %all-to-all-done = bf16[8,32,1280]{2,1,0:T(8,128)(2,1)S(1)} async-done(((bf16[8,32,1280]{2,1,0:T(8,128)(2,1)}), bf16[8,32,1280]{2,1,0:T(8,128)(2,1)S(1)}, u32[]{:S(2)}, u32[]{:S(2)}) %all-to-all-start) | async-done | bytes 655392 | tf_op jit(solution)/shard_map/all_to_all | solution.py:172
  57.6 1.0 %add.1 = bf16[128,1280]{1,0:T(8,128)(2,1)} custom-call(s32[128,1]{1,0:T(8,128)S(1)} %get-tuple-element.12.place_ref, f32[128,1280]{1,0:T(8,128)S(1)} %fusion.base_ref, bf16[256,1280]{1,0:T(8,128)(2,1)S(1)} %bitcast.9), custom_call_target="tpu_custom_call" | custom-call | tf_op jit(solution)/shard_map/add/pallas_call | solution.py:175
  (20 shorter events, 1.2 us)
Async XLA Ops:
  0.0 3.5 %collective-permute-start.3 = (bf16[16,8192]{1,0:T(8,128)(2,1)}, bf16[16,8192]{1,0:T(8,128)(2,1)S(1)}, u32[]{:S(2)}, u32[]{:S(2)}) collective-permute-start(bf16[16,8192]{1,0:T(8,128)(2,1)} %bitcast.14), channel_id=1, source_target_pairs={{0,8},{8,0},{1,9},{9,1},{2,10},{10,2},{3,11},{11,3},{4,12},{12,4},... | collective-permute-start | bytes 786440 | tf_op jit(solution)/shard_map/ppermute | solution.py:36
  0.5 29.8 %collective-permute-start.1 = (bf16[64,10240]{1,0:T(8,128)(2,1)}, bf16[64,10240]{1,0:T(8,128)(2,1)S(1)}, u32[]{:S(2)}, u32[]{:S(2)}) collective-permute-start(bf16[64,10240]{1,0:T(8,128)(2,1)} %bitcast.10), channel_id=1, source_target_pairs={{8,0},{0,8},{9,1},{1,9},{10,2},{2,10},{11,3},{3,11},{12,4},{4,12},... | collective-permute-start | bytes 3932168 | tf_op jit(solution)/shard_map/ppermute | solution.py:16
  0.5 7.5 %collective-permute-start.2 = (bf16[16,8192]{1,0:T(8,128)(2,1)}, bf16[16,8192]{1,0:T(8,128)(2,1)S(1)}, u32[]{:S(2)}, u32[]{:S(2)}) collective-permute-start(bf16[16,8192]{1,0:T(8,128)(2,1)} %bitcast.15), channel_id=1, source_target_pairs={{0,2},{10,8},{2,4},{12,10},{4,6},{14,12},{6,7},{15,14},{7,5},{13,1... | collective-permute-start | bytes 786440 | tf_op jit(solution)/shard_map/ppermute | solution.py:33
  3.5 26.7 %collective-permute-start = (bf16[64,8192]{1,0:T(8,128)(2,1)}, bf16[64,8192]{1,0:T(8,128)(2,1)S(1)}, u32[]{:S(2)}, u32[]{:S(2)}) collective-permute-start(bf16[64,8192]{1,0:T(8,128)(2,1)} %bitcast.12), channel_id=1, source_target_pairs={{8,0},{0,8},{9,1},{1,9},{10,2},{2,10},{11,3},{3,11},{12,4},{4,12},... | collective-permute-start | bytes 3145736 | tf_op jit(solution)/shard_map/ppermute | solution.py:16
  3.5 7.3 %collective-permute-start.4 = (bf16[16,8192]{1,0:T(8,128)(2,1)S(1)}, bf16[16,8192]{1,0:T(8,128)(2,1)S(1)}, u32[]{:S(2)}, u32[]{:S(2)}) collective-permute-start(bf16[16,8192]{1,0:T(8,128)(2,1)S(1)} %collective-permute-done.3), channel_id=1, source_target_pairs={{0,2},{10,8},{2,4},{12,10},{4,6},{14,12},{6,7},{15,14},{7,5},{13,1... | collective-permute-start | bytes 786440 | tf_op jit(solution)/shard_map/ppermute | solution.py:33
  8.0 6.4 %collective-permute-start.6 = (bf16[16,8192]{1,0:T(8,128)(2,1)S(1)}, bf16[16,8192]{1,0:T(8,128)(2,1)S(1)}, u32[]{:S(2)}, u32[]{:S(2)}) collective-permute-start(bf16[16,8192]{1,0:T(8,128)(2,1)S(1)} %collective-permute-done.2.refs_5_), channel_id=1, source_target_pairs={{0,2},{10,8},{2,4},{12,10},{4,6},{14,12},{6,7},{15,14},{7,5},{13,1... | collective-permute-start | bytes 786440 | tf_op jit(solution)/shard_map/ppermute | solution.py:33
  10.8 6.4 %collective-permute-start.7 = (bf16[16,8192]{1,0:T(8,128)(2,1)S(1)}, bf16[16,8192]{1,0:T(8,128)(2,1)S(1)}, u32[]{:S(2)}, u32[]{:S(2)}) collective-permute-start(bf16[16,8192]{1,0:T(8,128)(2,1)S(1)} %collective-permute-done.4), channel_id=1, source_target_pairs={{0,2},{10,8},{2,4},{12,10},{4,6},{14,12},{6,7},{15,14},{7,5},{13,1... | collective-permute-start | bytes 786440 | tf_op jit(solution)/shard_map/ppermute | solution.py:33
  12.9 6.4 %collective-permute-start.5 = (bf16[16,8192]{1,0:T(8,128)(2,1)S(1)}, bf16[16,8192]{1,0:T(8,128)(2,1)S(1)}, u32[]{:S(2)}, u32[]{:S(2)}) collective-permute-start(bf16[16,8192]{1,0:T(8,128)(2,1)S(1)} %collective-permute-done.4), channel_id=1, source_target_pairs={{0,8},{8,0},{1,9},{9,1},{2,10},{10,2},{3,11},{11,3},{4,12},{12,4},... | collective-permute-start | bytes 786440 | tf_op jit(solution)/shard_map/ppermute | solution.py:36
  14.4 6.4 %collective-permute-start.9 = (bf16[16,8192]{1,0:T(8,128)(2,1)S(1)}, bf16[16,8192]{1,0:T(8,128)(2,1)S(1)}, u32[]{:S(2)}, u32[]{:S(2)}) collective-permute-start(bf16[16,8192]{1,0:T(8,128)(2,1)S(1)} %collective-permute-done.6.refs_7_), channel_id=1, source_target_pairs={{0,2},{10,8},{2,4},{12,10},{4,6},{14,12},{6,7},{15,14},{7,5},{13,1... | collective-permute-start | bytes 786440 | tf_op jit(solution)/shard_map/ppermute | solution.py:33
  17.2 6.4 %collective-permute-start.10 = (bf16[16,8192]{1,0:T(8,128)(2,1)S(1)}, bf16[16,8192]{1,0:T(8,128)(2,1)S(1)}, u32[]{:S(2)}, u32[]{:S(2)}) collective-permute-start(bf16[16,8192]{1,0:T(8,128)(2,1)S(1)} %collective-permute-done.7), channel_id=1, source_target_pairs={{0,2},{10,8},{2,4},{12,10},{4,6},{14,12},{6,7},{15,14},{7,5},{13,1... | collective-permute-start | bytes 786440 | tf_op jit(solution)/shard_map/ppermute | solution.py:33
  19.3 10.9 %collective-permute-start.8 = (bf16[16,8192]{1,0:T(8,128)(2,1)S(1)}, bf16[16,8192]{1,0:T(8,128)(2,1)S(1)}, u32[]{:S(2)}, u32[]{:S(2)}) collective-permute-start(bf16[16,8192]{1,0:T(8,128)(2,1)S(1)} %collective-permute-done.7), channel_id=1, source_target_pairs={{0,8},{8,0},{1,9},{9,1},{2,10},{10,2},{3,11},{11,3},{4,12},{12,4},... | collective-permute-start | bytes 786440 | tf_op jit(solution)/shard_map/ppermute | solution.py:36
  20.8 9.4 %collective-permute-start.12 = (bf16[16,8192]{1,0:T(8,128)(2,1)S(1)}, bf16[16,8192]{1,0:T(8,128)(2,1)S(1)}, u32[]{:S(2)}, u32[]{:S(2)}) collective-permute-start(bf16[16,8192]{1,0:T(8,128)(2,1)S(1)} %collective-permute-done.9.refs_9_), channel_id=1, source_target_pairs={{0,2},{10,8},{2,4},{12,10},{4,6},{14,12},{6,7},{15,14},{7,5},{13,1... | collective-permute-start | bytes 786440 | tf_op jit(solution)/shard_map/ppermute | solution.py:33
  23.6 6.7 %collective-permute-start.11 = (bf16[16,8192]{1,0:T(8,128)(2,1)S(1)}, bf16[16,8192]{1,0:T(8,128)(2,1)S(1)}, u32[]{:S(2)}, u32[]{:S(2)}) collective-permute-start(bf16[16,8192]{1,0:T(8,128)(2,1)S(1)} %collective-permute-done.10), channel_id=1, source_target_pairs={{0,8},{8,0},{1,9},{9,1},{2,10},{10,2},{3,11},{11,3},{4,12},{12,4},... | collective-permute-start | bytes 786440 | tf_op jit(solution)/shard_map/ppermute | solution.py:36
  23.6 1.3 %copy-start = (bf16[1,64,10240]{2,1,0:T(8,128)(2,1)S(1)}, bf16[1,64,10240]{2,1,0:T(8,128)(2,1)}, u32[]{:S(2)}) copy-start(bf16[1,64,10240]{2,1,0:T(8,128)(2,1)} %param.10) | copy-start | bytes 3932164
  24.9 1.2 %copy-start.1 = (bf16[1,8192,64]{1,2,0:T(8,128)(2,1)S(1)}, bf16[1,8192,64]{1,2,0:T(8,128)(2,1)}, u32[]{:S(2)}) copy-start(bf16[1,8192,64]{1,2,0:T(8,128)(2,1)} %param.9) | copy-start | bytes 3145732
  26.1 0.9 %copy-start.2 = (bf16[1,16,8192]{2,1,0:T(8,128)(2,1)S(1)}, bf16[1,16,8192]{2,1,0:T(8,128)(2,1)}, u32[]{:S(2)}) copy-start(bf16[1,16,8192]{2,1,0:T(8,128)(2,1)} %param.7) | copy-start | bytes 786436
  27.1 0.7 %copy-start.3 = (s32[2,12]{1,0:T(2,128)S(1)}, s32[2,12]{1,0:T(2,128)}, u32[]{:S(2)}) copy-start(s32[2,12]{1,0:T(2,128)} %ids_ref.1) | copy-start | bytes 292
  27.8 0.7 %copy-start.4 = (s32[1,12]{1,0:T(1,128)S(1)}, s32[1,12]{1,0:T(1,128)}, u32[]{:S(2)}) copy-start(s32[1,12]{1,0:T(1,128)} %lengths_ref.1) | copy-start | bytes 148
  28.4 0.7 %copy-start.5 = (s32[16]{0:T(128)S(1)}, s32[16]{0:T(128)}, u32[]{:S(2)}) copy-start(s32[16]{0:T(128)} %slots_ref.1) | copy-start | bytes 196
  33.3 24.3 %all-to-all-start = ((bf16[8,32,1280]{2,1,0:T(8,128)(2,1)}), bf16[8,32,1280]{2,1,0:T(8,128)(2,1)S(1)}, u32[]{:S(2)}, u32[]{:S(2)}) async-start(bf16[8,32,1280]{2,1,0:T(8,128)(2,1)} %get-tuple-element.18), calls=%async_computation | async-start | bytes 1310720 | tf_op jit(solution)/shard_map/all_to_all | solution.py:172

commit v11 on v10

--- a/solution.py
+++ b/solution.py
@@ -10,15 +10,12 @@
 adapter_scale = 1.0
 
 
-def swapped(x, axis):
-    n = lax.axis_size(axis)
-    return [x] + [
-        lax.ppermute(x, axis, [((i + s) % n, i) for i in range(n)]) for s in range(1, n)
-    ]
-
-
 def ring_of(n):
     return list(range(0, n, 2)) + list(range(1, n, 2))[::-1]
+
+
+def handed(x):
+    return lax.ppermute(x, "grp", [(0, 1), (1, 0)])
 
 
 def ring_gather(block):
@@ -32,11 +29,8 @@
     def sent(x):
         return lax.ppermute(x, ("grp", "tp"), onward)
 
-    def handed(x):
-        return lax.ppermute(x, "grp", [(0, 1), (1, 0)])
-
     mine, other = block, handed(block)
-    pieces = [block]
+    pieces = [handed(other)]
     for step in range(1, n // 2):
         mine, other = sent(mine), sent(other)
         pieces += [mine, handed(other)]
@@ -55,11 +49,7 @@
     return sources
 
 
-def prepare_kernel(groups, tp, ids_ref, lengths_ref, slots_ref, *refs):
-    n = (len(refs) - 2) // 2
-    row_ref, column_ref = refs[n : n + 2]
-    for source, target in zip(refs[:n], refs[n + 2 :]):
-        target[...] = source[...]
+def prepare_kernel(groups, tp, ids_ref, lengths_ref, slots_ref, row_ref, column_ref):
     group = lax.axis_index("grp")
     tok_all = row_ref.shape[1]
     longest = tok_all // 8
@@ -80,35 +70,52 @@
     _, row_ref[...], column_ref[...] = lax.fori_loop(0, ids_ref.shape[1], add, carry)
 
 
-def lift_kernel(groups, tp, place_ref, *refs):
-    downs, ups, pieces = refs[:groups], refs[groups : 2 * groups], refs[2 * groups : -3]
-    tokens_ref, out_ref, up_ref = refs[-3:]
+def lift_kernel(groups, tp, order, place_ref, *refs):
+    downs, ups, refs = refs[:groups], refs[groups : 2 * groups], refs[2 * groups :]
+    pieces, tokens_ref, outs, up_ref = refs[:tp], refs[tp], refs[tp + 1 : -1], refs[-1]
     rank = ups[0].shape[0]
     rows = pieces[0].shape[0]
     tok_all = tokens_ref.shape[0]
-    parts, slots, columns = out_ref.shape
+    slots, columns = outs[0].shape[-2:]
     for piece, source in zip(pieces, ring_sources(tp)):
         tokens_ref[pl.ds(pl.multiple_of(source * rows, rows), rows), :] = piece[...]
     for s, up in enumerate(ups):
         up_ref[s * rank : (s + 1) * rank, :] = up[...]
     down = jnp.concatenate([down[...] for down in downs], axis=0).T
     low = jnp.dot(tokens_ref[...], down, preferred_element_type=jnp.float32)
-    here = lax.broadcasted_iota(jnp.int32, (slots, tok_all), 0) + lax.axis_index("tp") * slots
+    me = lax.axis_index("tp")
+    here = lax.broadcasted_iota(jnp.int32, (slots, tok_all), 0) + me * slots
     chosen = (here == place_ref[...]).astype(jnp.bfloat16)
     picked = jnp.dot(chosen, low.astype(jnp.bfloat16), preferred_element_type=jnp.float32)
     row_panel = lax.broadcasted_iota(jnp.int32, picked.shape, 0) // (slots // groups)
     rank_panel = lax.broadcasted_iota(jnp.int32, picked.shape, 1) // rank
     picked = jnp.where(row_panel == rank_panel, picked, 0.0).astype(jnp.bfloat16)
-    for part in range(parts):
-        out_ref[part] = jnp.dot(
-            picked,
-            up_ref[:, part * columns : (part + 1) * columns],
-            preferred_element_type=jnp.float32,
-        ).astype(out_ref.dtype)
-
-
-def add_kernel(place_ref, base_ref, lifts_ref, out_ref):
-    place = lax.broadcasted_iota(jnp.int32, (base_ref.shape[0], lifts_ref.shape[0]), 1)
+
+    def lifts(panel):
+        return jnp.dot(picked, panel, preferred_element_type=jnp.float32).astype(jnp.bfloat16)
+
+    if order is None:
+        for part in range(tp):
+            outs[0][part] = lifts(up_ref[:, part * columns : (part + 1) * columns])
+    else:
+        for out_ref, k in zip(outs, order):
+            start = pl.multiple_of(jnp.bitwise_xor(me, k) * columns, columns)
+            out_ref[...] = lifts(up_ref[:, pl.ds(start, columns)])
+
+
+def add_kernel(order, place_ref, base_ref, *refs):
+    parts, out_ref, lifts_ref = refs[:-2], refs[-2], refs[-1]
+    slots = parts[0].shape[0]
+    shape = (base_ref.shape[0], lifts_ref.shape[0])
+    place = lax.broadcasted_iota(jnp.int32, shape, 1)
+    if order is not None:
+        chip = jnp.zeros(shape, jnp.int32)
+        for i, k in enumerate(order):
+            from_chip = jnp.bitwise_xor(lax.axis_index("tp"), k)
+            chip = jnp.where(place // slots == i, from_chip, chip)
+        place = chip * slots + lax.rem(place, slots)
+    for i, part in enumerate(parts):
+        lifts_ref[i * slots : (i + 1) * slots, :] = part[...]
     chosen = (place == place_ref[...]).astype(jnp.bfloat16)
     lift = jnp.dot(chosen, lifts_ref[...], preferred_element_type=jnp.float32)
     out_ref[...] = (base_ref[...] + adapter_scale * lift).astype(out_ref.dtype)
@@ -134,32 +141,32 @@
     in_smem = pl.BlockSpec(memory_space=pltpu.SMEM)
     small = pltpu.CompilerParams(vmem_limit_bytes=16 * 2**20)
 
-    arrays = (tokens[0], adapter_down_panels[0].T, adapter_up_panels[0])
-    pieces = ring_gather(arrays[0])
-    others = [swapped(x, "grp")[1:] for x in arrays[1:]]
-    row, column, own, down, up = pl.pallas_call(
+    pieces = ring_gather(tokens[0])
+    panels = []
+    for panel in (adapter_down_panels[0].T, adapter_up_panels[0]):
+        other = handed(panel)
+        panels += [handed(other), other]
+    row, column = pl.pallas_call(
         functools.partial(prepare_kernel, groups, tp),
         out_shape=[
             jax.ShapeDtypeStruct((1, tok_all), jnp.int32),
             jax.ShapeDtypeStruct((tok_all, 1), jnp.int32),
-        ]
-        + [jax.ShapeDtypeStruct(x.shape, x.dtype) for x in arrays],
-        in_specs=[in_smem] * 3 + [in_vmem] * 3,
-        out_specs=[in_vmem] * 5,
+        ],
+        in_specs=[in_smem] * 3,
+        out_specs=[in_vmem] * 2,
         compiler_params=small,
         name="prepare",
-    )(request_adapter_ids, request_token_lengths, adapter_store_slot, *arrays)
-    panels = [down, *others[0], up, *others[1]]
-    pieces[0] = own
-
-    gathered, lifts = pl.pallas_call(
-        functools.partial(lift_kernel, groups, tp),
-        out_shape=[
-            jax.ShapeDtypeStruct((tok_all, width), jnp.bfloat16),
-            jax.ShapeDtypeStruct((tp, here, columns), jnp.bfloat16),
-        ],
+    )(request_adapter_ids, request_token_lengths, adapter_store_slot)
+
+    pairwise = columns % 128 == 0 and tp & (tp - 1) == 0
+    order = list(range(tp))[::-1] if pairwise else None
+    part = jax.ShapeDtypeStruct((here, columns), jnp.bfloat16)
+    gathered, *lifts = pl.pallas_call(
+        functools.partial(lift_kernel, groups, tp, order),
+        out_shape=[jax.ShapeDtypeStruct((tok_all, width), jnp.bfloat16)]
+        + ([part] * tp if pairwise else [jax.ShapeDtypeStruct((tp, *part.shape), part.dtype)]),
         in_specs=[in_vmem] * (1 + len(panels) + len(pieces)),
-        out_specs=[in_vmem] * 2,
+        out_specs=[in_vmem] * (1 + (tp if pairwise else 1)),
         scratch_shapes=[pltpu.VMEM((groups * rank, tp * columns), jnp.bfloat16)],
         compiler_params=pltpu.CompilerParams(vmem_limit_bytes=24 * 2**20),
         cost_estimate=pl.CostEstimate(
@@ -169,17 +176,25 @@
         ),
         name="lift",
     )(row, *panels, *pieces)
-    lifts = lax.all_to_all(lifts, "tp", split_axis=0, concat_axis=0, tiled=True)
+    if pairwise:
+        lifts = [
+            lax.ppermute(x, "tp", [(i, i ^ k) for i in range(tp)]) if k else x
+            for x, k in zip(lifts, order)
+        ]
+    else:
+        lifts = lax.all_to_all(lifts[0], "tp", split_axis=0, concat_axis=0, tiled=True)
+        lifts = [lifts.reshape(tp * here, columns)]
 
     base = jnp.dot(gathered, base_projection_weight, preferred_element_type=jnp.float32)
     out = pl.pallas_call(
-        add_kernel,
+        functools.partial(add_kernel, order),
         out_shape=jax.ShapeDtypeStruct((tok_all, columns), jnp.bfloat16),
-        in_specs=[in_vmem] * 3,
+        in_specs=[in_vmem] * (2 + len(lifts)),
         out_specs=in_vmem,
+        scratch_shapes=[pltpu.VMEM((tp * here, columns), jnp.bfloat16)],
         compiler_params=small,
         name="add",
-    )(column, base, lifts.reshape(tp * here, columns))
+    )(column, base, *lifts)
     return out[None]
 
 

time: 59 us -> 57.8 us (0.980)
  starting transfers between devices: 21.9 us -> 32.4 us
  waiting for transfers between devices: 17.6 us -> 10.5 us
  local copies, waits for them, and re-layouts: 5.48 us -> 1.99 us
  Pallas kernels: 5.15 us -> 4.13 us
    ppermute x2 -> x7, starting transfers between devices: 0.06 us -> 15.8 us  [on_device(): lax.ppermute(x, 'tp', [(i, i ^ k) for i in range(tp)])]
    all_to_all x1 -> x0, waiting for transfers between devices: 9.47 us -> none  [on_device(): lifts = lax.all_to_all(lifts, 'tp', split_axis=0, concat_axis=0, tiled=True)]
    all_to_all x1 -> x0, starting transfers between devices: 6.34 us -> none  [on_device(): lifts = lax.all_to_all(lifts, 'tp', split_axis=0, concat_axis=0, tiled=True)]
    unnamed x12 -> x6, local copies, waits for them, and re-layouts: 5.48 us -> 1.99 us
    ppermute x4 -> x9, waiting for transfers between devices: 0.01 us -> 2.38 us  [handed(): return lax.ppermute(x, 'grp', [(0, 1), (1, 0)])]
    ppermute x4 -> x9, starting transfers between devices: 0.46 us -> 1.35 us  [handed(): return lax.ppermute(x, 'grp', [(0, 1), (1, 0)])]
    pallas_call x2, Pallas kernels: 4.03 us -> 3.17 us  [the longest x1 2.14 us: on_device(): pl.pallas_call(functools.partial(lift_kernel, groups, tp, order), out_sha...]
  transfers between devices with their start and end apart: 14 -> 23, of which waited for: 7 -> 8; matrix products, arithmetic and copies ran while one was open for 15% -> 15% of each run, Pallas kernels for 2% -> 2%
where the time goes in v11:
time: 57.8 us; the launch traced here: 57.6 us
  starting transfers between devices  32.4 us (56%)
  waiting for transfers between devices  10.5 us (18%)
  matrix products  8.52 us (15%)
  Pallas kernels  4.13 us (7%)
  local copies, waits for them, and re-layouts  1.99 us (3%)
    ppermute x7, starting transfers between devices, on_device(): lax.ppermute(x, 'tp', [(i, i ^ k) for i in range(tp)])  15.8 us
    ppermute x7, starting transfers between devices, sent(): return lax.ppermute(x, ('grp', 'tp'), onward)  15.2 us
    dot_general x1, matrix products, on_device(): jnp.dot(gathered, base_projection_weight, preferred_element_type=jnp.floa...  8.52 us
    ppermute x7, waiting for transfers between devices, sent(): return lax.ppermute(x, ('grp', 'tp'), onward)  8.13 us
    ppermute x9, waiting for transfers between devices, handed(): return lax.ppermute(x, 'grp', [(0, 1), (1, 0)])  2.38 us
    pallas_call x1, Pallas kernels, on_device(): pl.pallas_call(functools.partial(lift_kernel, groups, tp, order), out_sha...  2.14 us
    unnamed x6, local copies, waits for them, and re-layouts  1.99 us
    ppermute x9, starting transfers between devices, handed(): return lax.ppermute(x, 'grp', [(0, 1), (1, 0)])  1.35 us
  transfers between devices with their start and end apart: 23, of which 8 were waited for; matrix products, arithmetic and copies ran while one was open for 15% of the time, Pallas kernels for 2%

profile of v11, /device:TPU:0, one launch (start us, length us, event | category | flops | bytes accessed | tf_op | source)
XLA Modules:
  0.0 57.6 jit_solution(12909460512652365099)
XLA Ops:
  1.0 2.4 %collective-permute-done.2.refs_3_ = bf16[64,10240]{1,0:T(8,128)(2,1)S(1)} collective-permute-done((bf16[64,10240]{1,0:T(8,128)(2,1)}, bf16[64,10240]{1,0:T(8,128)(2,1)S(1)}, u32[]{:S(2)}, u32[]{:S(2)}) %collective-permute-start.2) | collective-permute-done | bytes 1310752 | tf_op jit(solution)/shard_map/ppermute | solution.py:18
  3.7 2.7 %collective-permute-start.6 = (bf16[16,8192]{1,0:T(8,128)(2,1)}, bf16[16,8192]{1,0:T(8,128)(2,1)S(1)}, u32[]{:S(2)}, u32[]{:S(2)}) collective-permute-start(bf16[16,8192]{1,0:T(8,128)(2,1)} %bitcast.11), channel_id=1, source_target_pairs={{0,2},{10,8},{2,4},{12,10},{4,6},{14,12},{6,7},{15,14},{7,5},{13,1... | collective-permute-start | bytes 786440 | tf_op jit(solution)/shard_map/ppermute | solution.py:30
  6.4 2.1 %collective-permute-start.7 = (bf16[16,8192]{1,0:T(8,128)(2,1)S(1)}, bf16[16,8192]{1,0:T(8,128)(2,1)S(1)}, u32[]{:S(2)}, u32[]{:S(2)}) collective-permute-start(bf16[16,8192]{1,0:T(8,128)(2,1)S(1)} %collective-permute-done.4), channel_id=1, source_target_pairs={{0,2},{10,8},{2,4},{12,10},{4,6},{14,12},{6,7},{15,14},{7,5},{13,1... | collective-permute-start | bytes 786440 | tf_op jit(solution)/shard_map/ppermute | solution.py:30
  8.5 2.4 %collective-permute-done.6.refs_5_ = bf16[16,8192]{1,0:T(8,128)(2,1)S(1)} collective-permute-done((bf16[16,8192]{1,0:T(8,128)(2,1)}, bf16[16,8192]{1,0:T(8,128)(2,1)S(1)}, u32[]{:S(2)}, u32[]{:S(2)}) %collective-permute-start.6) | collective-permute-done | bytes 262176 | tf_op jit(solution)/shard_map/ppermute | solution.py:30
  10.9 2.1 %collective-permute-start.9 = (bf16[16,8192]{1,0:T(8,128)(2,1)S(1)}, bf16[16,8192]{1,0:T(8,128)(2,1)S(1)}, u32[]{:S(2)}, u32[]{:S(2)}) collective-permute-start(bf16[16,8192]{1,0:T(8,128)(2,1)S(1)} %collective-permute-done.6.refs_5_), channel_id=1, source_target_pairs={{0,2},{10,8},{2,4},{12,10},{4,6},{14,12},{6,7},{15,14},{7,5},{13,1... | collective-permute-start | bytes 786440 | tf_op jit(solution)/shard_map/ppermute | solution.py:30
  13.0 0.7 %collective-permute-done.7 = bf16[16,8192]{1,0:T(8,128)(2,1)S(1)} collective-permute-done((bf16[16,8192]{1,0:T(8,128)(2,1)S(1)}, bf16[16,8192]{1,0:T(8,128)(2,1)S(1)}, u32[]{:S(2)}, u32[]{:S(2)}) %collective-permute-start.7) | collective-permute-done | bytes 262176 | tf_op jit(solution)/shard_map/ppermute | solution.py:30
  13.7 2.1 %collective-permute-start.10 = (bf16[16,8192]{1,0:T(8,128)(2,1)S(1)}, bf16[16,8192]{1,0:T(8,128)(2,1)S(1)}, u32[]{:S(2)}, u32[]{:S(2)}) collective-permute-start(bf16[16,8192]{1,0:T(8,128)(2,1)S(1)} %collective-permute-done.7), channel_id=1, source_target_pairs={{0,2},{10,8},{2,4},{12,10},{4,6},{14,12},{6,7},{15,14},{7,5},{13,1... | collective-permute-start | bytes 786440 | tf_op jit(solution)/shard_map/ppermute | solution.py:30
  15.8 1.5 %collective-permute-done.9.refs_7_ = bf16[16,8192]{1,0:T(8,128)(2,1)S(1)} collective-permute-done((bf16[16,8192]{1,0:T(8,128)(2,1)S(1)}, bf16[16,8192]{1,0:T(8,128)(2,1)S(1)}, u32[]{:S(2)}, u32[]{:S(2)}) %collective-permute-start.9) | collective-permute-done | bytes 262176 | tf_op jit(solution)/shard_map/ppermute | solution.py:30
  17.3 2.1 %collective-permute-start.12 = (bf16[16,8192]{1,0:T(8,128)(2,1)S(1)}, bf16[16,8192]{1,0:T(8,128)(2,1)S(1)}, u32[]{:S(2)}, u32[]{:S(2)}) collective-permute-start(bf16[16,8192]{1,0:T(8,128)(2,1)S(1)} %collective-permute-done.9.refs_7_), channel_id=1, source_target_pairs={{0,2},{10,8},{2,4},{12,10},{4,6},{14,12},{6,7},{15,14},{7,5},{13,1... | collective-permute-start | bytes 786440 | tf_op jit(solution)/shard_map/ppermute | solution.py:30
  19.4 0.7 %collective-permute-done.10 = bf16[16,8192]{1,0:T(8,128)(2,1)S(1)} collective-permute-done((bf16[16,8192]{1,0:T(8,128)(2,1)S(1)}, bf16[16,8192]{1,0:T(8,128)(2,1)S(1)}, u32[]{:S(2)}, u32[]{:S(2)}) %collective-permute-start.10) | collective-permute-done | bytes 262176 | tf_op jit(solution)/shard_map/ppermute | solution.py:30
  20.1 2.1 %collective-permute-start.13 = (bf16[16,8192]{1,0:T(8,128)(2,1)S(1)}, bf16[16,8192]{1,0:T(8,128)(2,1)S(1)}, u32[]{:S(2)}, u32[]{:S(2)}) collective-permute-start(bf16[16,8192]{1,0:T(8,128)(2,1)S(1)} %collective-permute-done.10), channel_id=1, source_target_pairs={{0,2},{10,8},{2,4},{12,10},{4,6},{14,12},{6,7},{15,14},{7,5},{13,1... | collective-permute-start | bytes 786440 | tf_op jit(solution)/shard_map/ppermute | solution.py:30
  22.2 1.5 %collective-permute-done.12.refs_9_ = bf16[16,8192]{1,0:T(8,128)(2,1)S(1)} collective-permute-done((bf16[16,8192]{1,0:T(8,128)(2,1)S(1)}, bf16[16,8192]{1,0:T(8,128)(2,1)S(1)}, u32[]{:S(2)}, u32[]{:S(2)}) %collective-permute-start.12) | collective-permute-done | bytes 262176 | tf_op jit(solution)/shard_map/ppermute | solution.py:30
  23.7 2.1 %collective-permute-start.15 = (bf16[16,8192]{1,0:T(8,128)(2,1)S(1)}, bf16[16,8192]{1,0:T(8,128)(2,1)S(1)}, u32[]{:S(2)}, u32[]{:S(2)}) collective-permute-start(bf16[16,8192]{1,0:T(8,128)(2,1)S(1)} %collective-permute-done.12.refs_9_), channel_id=1, source_target_pairs={{0,2},{10,8},{2,4},{12,10},{4,6},{14,12},{6,7},{15,14},{7,5},{13,1... | collective-permute-start | bytes 786440 | tf_op jit(solution)/shard_map/ppermute | solution.py:30
  25.7 0.7 %collective-permute-done.13 = bf16[16,8192]{1,0:T(8,128)(2,1)S(1)} collective-permute-done((bf16[16,8192]{1,0:T(8,128)(2,1)S(1)}, bf16[16,8192]{1,0:T(8,128)(2,1)S(1)}, u32[]{:S(2)}, u32[]{:S(2)}) %collective-permute-start.13) | collective-permute-done | bytes 262176 | tf_op jit(solution)/shard_map/ppermute | solution.py:30
  28.5 1.0 %prepare.1 = (s32[1,128]{1,0:T(1,128)S(1)}, s32[128,1]{1,0:T(8,128)S(1)}) custom-call(s32[2,12]{1,0:T(2,128)S(1)} %copy-done, s32[1,12]{1,0:T(1,128)S(1)} %copy-done.1, s32[16]{0:T(128)S(1)} %copy-done.2), custom_call_target="tpu_custom_call" | custom-call | tf_op jit(solution)/shard_map/prepare/pallas_call | solution.py:149
  30.1 2.1 %lift.1 = (bf16[128,8192]{1,0:T(8,128)(2,1)S(1)}, bf16[32,1280]{1,0:T(8,128)(2,1)S(1)}, bf16[32,1280]{1,0:T(8,128)(2,1)S(1)}, bf16[32,1280]{1,0:T(8,128)(2,1)S(1...) custom-call(s32[1,128]{1,0:T(1,128)S(1)} %get-tuple-element.17.place, ...), custom_call_target="tpu_custom_call" | custom-call | flops 352321536 | bytes 4718592 | tf_op jit(solution)/shard_map/lift/pallas_call | solution.py:164
  32.2 5.1 %collective-permute-start.16 = (bf16[32,1280]{1,0:T(8,128)(2,1)S(1)}, bf16[32,1280]{1,0:T(8,128)(2,1)S(1)}, u32[]{:S(2)}, u32[]{:S(2)}) collective-permute-start(bf16[32,1280]{1,0:T(8,128)(2,1)S(1)} %get-tuple-element.19), channel_id=1, source_target_pairs={{0,7},{1,6},{2,5},{3,4},{4,3},{5,2},{6,1},{7,0},{8,15},{9,14},{10,... | collective-permute-start | bytes 245768 | tf_op jit(solution)/shard_map/ppermute | solution.py:181
  37.6 0.7 %collective-permute-start.18 = (bf16[32,1280]{1,0:T(8,128)(2,1)S(1)}, bf16[32,1280]{1,0:T(8,128)(2,1)S(1)}, u32[]{:S(2)}, u32[]{:S(2)}) collective-permute-start(bf16[32,1280]{1,0:T(8,128)(2,1)S(1)} %get-tuple-element.21), channel_id=1, source_target_pairs={{0,5},{1,4},{2,7},{3,6},{4,1},{5,0},{6,3},{7,2},{8,13},{9,12},{10,... | collective-permute-start | bytes 245768 | tf_op jit(solution)/shard_map/ppermute | solution.py:181
  38.3 2.0 %collective-permute-start.19 = (bf16[32,1280]{1,0:T(8,128)(2,1)S(1)}, bf16[32,1280]{1,0:T(8,128)(2,1)S(1)}, u32[]{:S(2)}, u32[]{:S(2)}) collective-permute-start(bf16[32,1280]{1,0:T(8,128)(2,1)S(1)} %get-tuple-element.22), channel_id=1, source_target_pairs={{0,4},{1,5},{2,6},{3,7},{4,0},{5,1},{6,2},{7,3},{8,12},{9,13},{10,... | collective-permute-start | bytes 245768 | tf_op jit(solution)/shard_map/ppermute | solution.py:181
  40.3 2.3 %collective-permute-start.20 = (bf16[32,1280]{1,0:T(8,128)(2,1)S(1)}, bf16[32,1280]{1,0:T(8,128)(2,1)S(1)}, u32[]{:S(2)}, u32[]{:S(2)}) collective-permute-start(bf16[32,1280]{1,0:T(8,128)(2,1)S(1)} %get-tuple-element.23), channel_id=1, source_target_pairs={{0,3},{1,2},{2,1},{3,0},{4,7},{5,6},{6,5},{7,4},{8,11},{9,10},{10,... | collective-permute-start | bytes 245768 | tf_op jit(solution)/shard_map/ppermute | solution.py:181
  42.6 3.9 %collective-permute-start.21 = (bf16[32,1280]{1,0:T(8,128)(2,1)S(1)}, bf16[32,1280]{1,0:T(8,128)(2,1)S(1)}, u32[]{:S(2)}, u32[]{:S(2)}) collective-permute-start(bf16[32,1280]{1,0:T(8,128)(2,1)S(1)} %get-tuple-element.24), channel_id=1, source_target_pairs={{0,2},{1,3},{2,0},{3,1},{4,6},{5,7},{6,4},{7,5},{8,10},{9,11},{10,... | collective-permute-start | bytes 245768 | tf_op jit(solution)/shard_map/ppermute | solution.py:181
  46.6 1.5 %collective-permute-start.22 = (bf16[32,1280]{1,0:T(8,128)(2,1)S(1)}, bf16[32,1280]{1,0:T(8,128)(2,1)S(1)}, u32[]{:S(2)}, u32[]{:S(2)}) collective-permute-start(bf16[32,1280]{1,0:T(8,128)(2,1)S(1)} %get-tuple-element.25), channel_id=1, source_target_pairs={{0,1},{1,0},{2,3},{3,2},{4,5},{5,4},{6,7},{7,6},{8,9},{9,8},{10,11... | collective-permute-start | bytes 245768 | tf_op jit(solution)/shard_map/ppermute | solution.py:181
  48.0 8.5 %fusion.base_ref = f32[128,1280]{1,0:T(8,128)S(1)} fusion(bf16[128,8192]{1,0:T(8,128)(2,1)S(1)} %get-tuple-element.18, bf16[8192,1280]{1,0:T(8,128)(2,1)} %param.8), kind=kOutput, calls=%fused_computation | convolution fusion | flops 2684354560 | bytes 23724032 | tf_op jit(solution)/shard_map/dot_general | solution.py:188
  56.6 1.0 %add.1 = bf16[128,1280]{1,0:T(8,128)(2,1)} custom-call(s32[128,1]{1,0:T(8,128)S(1)} %get-tuple-element.16.place_ref, f32[128,1280]{1,0:T(8,128)S(1)} %fusion.base_ref, bf16[32,1280]{1,0:T(8,128)(2,1)S(1)} %collective-permute-done.16.refs_0_, bf16[32,1280]{1,0:T(8,128)(2,1)S(1)} %collective-permute-done.17.refs_1_, ...), custom_call_target="tpu_custom_call" | custom-call | tf_op jit(solution)/shard_map/add/pallas_call | solution.py:189
  (32 shorter events, 4.2 us)
Async XLA Ops:
  0.0 3.3 %collective-permute-start.2 = (bf16[64,10240]{1,0:T(8,128)(2,1)}, bf16[64,10240]{1,0:T(8,128)(2,1)S(1)}, u32[]{:S(2)}, u32[]{:S(2)}) collective-permute-start(bf16[64,10240]{1,0:T(8,128)(2,1)} %bitcast.8), channel_id=1, source_target_pairs={{0,8},{8,0},{1,9},{9,1},{2,10},{10,2},{3,11},{11,3},{4,12},{12,4},... | collective-permute-start | bytes 3932168 | tf_op jit(solution)/shard_map/ppermute | solution.py:18
  0.5 8.1 %collective-permute-start = (bf16[64,8192]{1,0:T(8,128)(2,1)}, bf16[64,8192]{1,0:T(8,128)(2,1)S(1)}, u32[]{:S(2)}, u32[]{:S(2)}) collective-permute-start(bf16[64,8192]{1,0:T(8,128)(2,1)} %bitcast.9), channel_id=1, source_target_pairs={{0,8},{8,0},{1,9},{9,1},{2,10},{10,2},{3,11},{11,3},{4,12},{12,4},... | collective-permute-start | bytes 3145736 | tf_op jit(solution)/shard_map/ppermute | solution.py:18
  0.5 5.9 %collective-permute-start.4 = (bf16[16,8192]{1,0:T(8,128)(2,1)}, bf16[16,8192]{1,0:T(8,128)(2,1)S(1)}, u32[]{:S(2)}, u32[]{:S(2)}) collective-permute-start(bf16[16,8192]{1,0:T(8,128)(2,1)} %bitcast.10), channel_id=1, source_target_pairs={{0,8},{8,0},{1,9},{9,1},{2,10},{10,2},{3,11},{11,3},{4,12},{12,4},... | collective-permute-start | bytes 786440 | tf_op jit(solution)/shard_map/ppermute | solution.py:18
  3.3 26.7 %collective-permute-start.3 = (bf16[64,10240]{1,0:T(8,128)(2,1)S(1)}, bf16[64,10240]{1,0:T(8,128)(2,1)S(1)}, u32[]{:S(2)}, u32[]{:S(2)}) collective-permute-start(bf16[64,10240]{1,0:T(8,128)(2,1)S(1)} %collective-permute-done.2.refs_3_), channel_id=1, source_target_pairs={{0,8},{8,0},{1,9},{9,1},{2,10},{10,2},{3,11},{11,3},{4,12},{12,4},... | collective-permute-start | bytes 3932168 | tf_op jit(solution)/shard_map/ppermute | solution.py:18
  3.7 7.2 %collective-permute-start.6 = (bf16[16,8192]{1,0:T(8,128)(2,1)}, bf16[16,8192]{1,0:T(8,128)(2,1)S(1)}, u32[]{:S(2)}, u32[]{:S(2)}) collective-permute-start(bf16[16,8192]{1,0:T(8,128)(2,1)} %bitcast.11), channel_id=1, source_target_pairs={{0,2},{10,8},{2,4},{12,10},{4,6},{14,12},{6,7},{15,14},{7,5},{13,1... | collective-permute-start | bytes 786440 | tf_op jit(solution)/shard_map/ppermute | solution.py:30
  6.4 7.3 %collective-permute-start.7 = (bf16[16,8192]{1,0:T(8,128)(2,1)S(1)}, bf16[16,8192]{1,0:T(8,128)(2,1)S(1)}, u32[]{:S(2)}, u32[]{:S(2)}) collective-permute-start(bf16[16,8192]{1,0:T(8,128)(2,1)S(1)} %collective-permute-done.4), channel_id=1, source_target_pairs={{0,2},{10,8},{2,4},{12,10},{4,6},{14,12},{6,7},{15,14},{7,5},{13,1... | collective-permute-start | bytes 786440 | tf_op jit(solution)/shard_map/ppermute | solution.py:30
  8.5 21.5 %collective-permute-start.1 = (bf16[64,8192]{1,0:T(8,128)(2,1)S(1)}, bf16[64,8192]{1,0:T(8,128)(2,1)S(1)}, u32[]{:S(2)}, u32[]{:S(2)}) collective-permute-start(bf16[64,8192]{1,0:T(8,128)(2,1)S(1)} %collective-permute-done.refs_1_), channel_id=1, source_target_pairs={{0,8},{8,0},{1,9},{9,1},{2,10},{10,2},{3,11},{11,3},{4,12},{12,4},... | collective-permute-start | bytes 3145736 | tf_op jit(solution)/shard_map/ppermute | solution.py:18
  10.9 6.4 %collective-permute-start.9 = (bf16[16,8192]{1,0:T(8,128)(2,1)S(1)}, bf16[16,8192]{1,0:T(8,128)(2,1)S(1)}, u32[]{:S(2)}, u32[]{:S(2)}) collective-permute-start(bf16[16,8192]{1,0:T(8,128)(2,1)S(1)} %collective-permute-done.6.refs_5_), channel_id=1, source_target_pairs={{0,2},{10,8},{2,4},{12,10},{4,6},{14,12},{6,7},{15,14},{7,5},{13,1... | collective-permute-start | bytes 786440 | tf_op jit(solution)/shard_map/ppermute | solution.py:30
  13.0 6.4 %collective-permute-start.5 = (bf16[16,8192]{1,0:T(8,128)(2,1)S(1)}, bf16[16,8192]{1,0:T(8,128)(2,1)S(1)}, u32[]{:S(2)}, u32[]{:S(2)}) collective-permute-start(bf16[16,8192]{1,0:T(8,128)(2,1)S(1)} %collective-permute-done.4), channel_id=1, source_target_pairs={{0,8},{8,0},{1,9},{9,1},{2,10},{10,2},{3,11},{11,3},{4,12},{12,4},... | collective-permute-start | bytes 786440 | tf_op jit(solution)/shard_map/ppermute | solution.py:18
  13.7 6.4 %collective-permute-start.10 = (bf16[16,8192]{1,0:T(8,128)(2,1)S(1)}, bf16[16,8192]{1,0:T(8,128)(2,1)S(1)}, u32[]{:S(2)}, u32[]{:S(2)}) collective-permute-start(bf16[16,8192]{1,0:T(8,128)(2,1)S(1)} %collective-permute-done.7), channel_id=1, source_target_pairs={{0,2},{10,8},{2,4},{12,10},{4,6},{14,12},{6,7},{15,14},{7,5},{13,1... | collective-permute-start | bytes 786440 | tf_op jit(solution)/shard_map/ppermute | solution.py:30
  17.3 6.4 %collective-permute-start.12 = (bf16[16,8192]{1,0:T(8,128)(2,1)S(1)}, bf16[16,8192]{1,0:T(8,128)(2,1)S(1)}, u32[]{:S(2)}, u32[]{:S(2)}) collective-permute-start(bf16[16,8192]{1,0:T(8,128)(2,1)S(1)} %collective-permute-done.9.refs_7_), channel_id=1, source_target_pairs={{0,2},{10,8},{2,4},{12,10},{4,6},{14,12},{6,7},{15,14},{7,5},{13,1... | collective-permute-start | bytes 786440 | tf_op jit(solution)/shard_map/ppermute | solution.py:30
  19.4 4.3 %collective-permute-start.8 = (bf16[16,8192]{1,0:T(8,128)(2,1)S(1)}, bf16[16,8192]{1,0:T(8,128)(2,1)S(1)}, u32[]{:S(2)}, u32[]{:S(2)}) collective-permute-start(bf16[16,8192]{1,0:T(8,128)(2,1)S(1)} %collective-permute-done.7), channel_id=1, source_target_pairs={{0,8},{8,0},{1,9},{9,1},{2,10},{10,2},{3,11},{11,3},{4,12},{12,4},... | collective-permute-start | bytes 786440 | tf_op jit(solution)/shard_map/ppermute | solution.py:18
  20.1 6.4 %collective-permute-start.13 = (bf16[16,8192]{1,0:T(8,128)(2,1)S(1)}, bf16[16,8192]{1,0:T(8,128)(2,1)S(1)}, u32[]{:S(2)}, u32[]{:S(2)}) collective-permute-start(bf16[16,8192]{1,0:T(8,128)(2,1)S(1)} %collective-permute-done.10), channel_id=1, source_target_pairs={{0,2},{10,8},{2,4},{12,10},{4,6},{14,12},{6,7},{15,14},{7,5},{13,1... | collective-permute-start | bytes 786440 | tf_op jit(solution)/shard_map/ppermute | solution.py:30
  23.7 6.4 %collective-permute-start.11 = (bf16[16,8192]{1,0:T(8,128)(2,1)S(1)}, bf16[16,8192]{1,0:T(8,128)(2,1)S(1)}, u32[]{:S(2)}, u32[]{:S(2)}) collective-permute-start(bf16[16,8192]{1,0:T(8,128)(2,1)S(1)} %collective-permute-done.10), channel_id=1, source_target_pairs={{0,8},{8,0},{1,9},{9,1},{2,10},{10,2},{3,11},{11,3},{4,12},{12,4},... | collective-permute-start | bytes 786440 | tf_op jit(solution)/shard_map/ppermute | solution.py:18
  23.7 6.4 %collective-permute-start.15 = (bf16[16,8192]{1,0:T(8,128)(2,1)S(1)}, bf16[16,8192]{1,0:T(8,128)(2,1)S(1)}, u32[]{:S(2)}, u32[]{:S(2)}) collective-permute-start(bf16[16,8192]{1,0:T(8,128)(2,1)S(1)} %collective-permute-done.12.refs_9_), channel_id=1, source_target_pairs={{0,2},{10,8},{2,4},{12,10},{4,6},{14,12},{6,7},{15,14},{7,5},{13,1... | collective-permute-start | bytes 786440 | tf_op jit(solution)/shard_map/ppermute | solution.py:30
  26.5 3.6 %collective-permute-start.14 = (bf16[16,8192]{1,0:T(8,128)(2,1)S(1)}, bf16[16,8192]{1,0:T(8,128)(2,1)S(1)}, u32[]{:S(2)}, u32[]{:S(2)}) collective-permute-start(bf16[16,8192]{1,0:T(8,128)(2,1)S(1)} %collective-permute-done.13), channel_id=1, source_target_pairs={{0,8},{8,0},{1,9},{9,1},{2,10},{10,2},{3,11},{11,3},{4,12},{12,4},... | collective-permute-start | bytes 786440 | tf_op jit(solution)/shard_map/ppermute | solution.py:18
  26.5 0.7 %copy-start = (s32[2,12]{1,0:T(2,128)S(1)}, s32[2,12]{1,0:T(2,128)}, u32[]{:S(2)}) copy-start(s32[2,12]{1,0:T(2,128)} %ids_ref.1) | copy-start | bytes 292
  32.2 10.4 %collective-permute-start.16 = (bf16[32,1280]{1,0:T(8,128)(2,1)S(1)}, bf16[32,1280]{1,0:T(8,128)(2,1)S(1)}, u32[]{:S(2)}, u32[]{:S(2)}) collective-permute-start(bf16[32,1280]{1,0:T(8,128)(2,1)S(1)} %get-tuple-element.19), channel_id=1, source_target_pairs={{0,7},{1,6},{2,5},{3,4},{4,3},{5,2},{6,1},{7,0},{8,15},{9,14},{10,... | collective-permute-start | bytes 245768 | tf_op jit(solution)/shard_map/ppermute | solution.py:181
  37.3 9.2 %collective-permute-start.17 = (bf16[32,1280]{1,0:T(8,128)(2,1)S(1)}, bf16[32,1280]{1,0:T(8,128)(2,1)S(1)}, u32[]{:S(2)}, u32[]{:S(2)}) collective-permute-start(bf16[32,1280]{1,0:T(8,128)(2,1)S(1)} %get-tuple-element.20), channel_id=1, source_target_pairs={{0,6},{1,7},{2,4},{3,5},{4,2},{5,3},{6,0},{7,1},{8,14},{9,15},{10,... | collective-permute-start | bytes 245768 | tf_op jit(solution)/shard_map/ppermute | solution.py:181
  37.6 19.0 %collective-permute-start.18 = (bf16[32,1280]{1,0:T(8,128)(2,1)S(1)}, bf16[32,1280]{1,0:T(8,128)(2,1)S(1)}, u32[]{:S(2)}, u32[]{:S(2)}) collective-permute-start(bf16[32,1280]{1,0:T(8,128)(2,1)S(1)} %get-tuple-element.21), channel_id=1, source_target_pairs={{0,5},{1,4},{2,7},{3,6},{4,1},{5,0},{6,3},{7,2},{8,13},{9,12},{10,... | collective-permute-start | bytes 245768 | tf_op jit(solution)/shard_map/ppermute | solution.py:181
  38.3 18.3 %collective-permute-start.19 = (bf16[32,1280]{1,0:T(8,128)(2,1)S(1)}, bf16[32,1280]{1,0:T(8,128)(2,1)S(1)}, u32[]{:S(2)}, u32[]{:S(2)}) collective-permute-start(bf16[32,1280]{1,0:T(8,128)(2,1)S(1)} %get-tuple-element.22), channel_id=1, source_target_pairs={{0,4},{1,5},{2,6},{3,7},{4,0},{5,1},{6,2},{7,3},{8,12},{9,13},{10,... | collective-permute-start | bytes 245768 | tf_op jit(solution)/shard_map/ppermute | solution.py:181
  40.3 16.2 %collective-permute-start.20 = (bf16[32,1280]{1,0:T(8,128)(2,1)S(1)}, bf16[32,1280]{1,0:T(8,128)(2,1)S(1)}, u32[]{:S(2)}, u32[]{:S(2)}) collective-permute-start(bf16[32,1280]{1,0:T(8,128)(2,1)S(1)} %get-tuple-element.23), channel_id=1, source_target_pairs={{0,3},{1,2},{2,1},{3,0},{4,7},{5,6},{6,5},{7,4},{8,11},{9,10},{10,... | collective-permute-start | bytes 245768 | tf_op jit(solution)/shard_map/ppermute | solution.py:181
  42.6 14.0 %collective-permute-start.21 = (bf16[32,1280]{1,0:T(8,128)(2,1)S(1)}, bf16[32,1280]{1,0:T(8,128)(2,1)S(1)}, u32[]{:S(2)}, u32[]{:S(2)}) collective-permute-start(bf16[32,1280]{1,0:T(8,128)(2,1)S(1)} %get-tuple-element.24), channel_id=1, source_target_pairs={{0,2},{1,3},{2,0},{3,1},{4,6},{5,7},{6,4},{7,5},{8,10},{9,11},{10,... | collective-permute-start | bytes 245768 | tf_op jit(solution)/shard_map/ppermute | solution.py:181
  46.6 10.0 %collective-permute-start.22 = (bf16[32,1280]{1,0:T(8,128)(2,1)S(1)}, bf16[32,1280]{1,0:T(8,128)(2,1)S(1)}, u32[]{:S(2)}, u32[]{:S(2)}) collective-permute-start(bf16[32,1280]{1,0:T(8,128)(2,1)S(1)} %get-tuple-element.25), channel_id=1, source_target_pairs={{0,1},{1,0},{2,3},{3,2},{4,5},{5,4},{6,7},{7,6},{8,9},{9,8},{10,11... | collective-permute-start | bytes 245768 | tf_op jit(solution)/shard_map/ppermute | solution.py:181
  (2 other events, 1.3 us)

commit v12 on v11

--- a/solution.py
+++ b/solution.py
@@ -18,7 +18,7 @@
     return lax.ppermute(x, "grp", [(0, 1), (1, 0)])
 
 
-def ring_gather(block):
+def ring_gather(block, copied):
     n = lax.axis_size("tp")
     ring = ring_of(n)
     onward = []
@@ -29,19 +29,21 @@
     def sent(x):
         return lax.ppermute(x, ("grp", "tp"), onward)
 
-    mine, other = block, handed(block)
-    pieces = [handed(other)]
-    for step in range(1, n // 2):
+    mine, other = sent(block), handed(copied)
+    pieces = [copied, mine]
+    for step in range(2, n // 2 + 1):
         mine, other = sent(mine), sent(other)
-        pieces += [mine, handed(other)]
-    return pieces + [sent(mine)]
+        pieces += [handed(other), mine]
+    return pieces
 
 
 def ring_sources(n):
     me = lax.axis_index("tp")
     way = 1 - 2 * lax.axis_index("grp")
     place = jnp.where(lax.rem(me, 2) == 0, me // 2, n - 1 - me // 2)
-    distances = [0] + [d for i in range(1, n // 2) for d in (way * i, -way * i)] + [n // 2]
+    distances = [0, way]
+    for i in range(2, n // 2 + 1):
+        distances += [-way * (i - 1), way * i]
     sources = []
     for distance in distances:
         at = lax.rem(place - distance + 2 * n, n)
@@ -49,7 +51,11 @@
     return sources
 
 
-def prepare_kernel(groups, tp, ids_ref, lengths_ref, slots_ref, row_ref, column_ref):
+def prepare_kernel(groups, tp, ids_ref, lengths_ref, slots_ref, *refs):
+    n = (len(refs) - 2) // 2
+    row_ref, column_ref = refs[n : n + 2]
+    for source, target in zip(refs[:n], refs[n + 2 :]):
+        target[...] = source[...]
     group = lax.axis_index("grp")
     tok_all = row_ref.shape[1]
     longest = tok_all // 8
@@ -103,6 +109,12 @@
             out_ref[...] = lifts(up_ref[:, pl.ds(start, columns)])
 
 
+def pass_kernel(after_ref, *refs):
+    n = len(refs) // 2
+    for source, target in zip(refs[:n], refs[n:]):
+        target[...] = source[...]
+
+
 def add_kernel(order, place_ref, base_ref, *refs):
     parts, out_ref, lifts_ref = refs[:-2], refs[-2], refs[-1]
     slots = parts[0].shape[0]
@@ -141,22 +153,21 @@
     in_smem = pl.BlockSpec(memory_space=pltpu.SMEM)
     small = pltpu.CompilerParams(vmem_limit_bytes=16 * 2**20)
 
-    pieces = ring_gather(tokens[0])
-    panels = []
-    for panel in (adapter_down_panels[0].T, adapter_up_panels[0]):
-        other = handed(panel)
-        panels += [handed(other), other]
-    row, column = pl.pallas_call(
+    arrays = (tokens[0], adapter_down_panels[0].T, adapter_up_panels[0])
+    row, column, copied, down, up = pl.pallas_call(
         functools.partial(prepare_kernel, groups, tp),
         out_shape=[
             jax.ShapeDtypeStruct((1, tok_all), jnp.int32),
             jax.ShapeDtypeStruct((tok_all, 1), jnp.int32),
-        ],
-        in_specs=[in_smem] * 3,
-        out_specs=[in_vmem] * 2,
+        ]
+        + [jax.ShapeDtypeStruct(x.shape, x.dtype) for x in arrays],
+        in_specs=[in_smem] * 3 + [in_vmem] * 3,
+        out_specs=[in_vmem] * 5,
         compiler_params=small,
         name="prepare",
-    )(request_adapter_ids, request_token_lengths, adapter_store_slot)
+    )(request_adapter_ids, request_token_lengths, adapter_store_slot, *arrays)
+    pieces = ring_gather(arrays[0], copied)
+    panels = [down, handed(down), up, handed(up)]
 
     pairwise = columns % 128 == 0 and tp & (tp - 1) == 0
     order = list(range(tp))[::-1] if pairwise else None
@@ -176,16 +187,25 @@
         ),
         name="lift",
     )(row, *panels, *pieces)
+    base = jnp.dot(gathered, base_projection_weight, preferred_element_type=jnp.float32)
     if pairwise:
+        far = tp // 2
+        near = pl.pallas_call(
+            pass_kernel,
+            out_shape=[part] * (tp - far - 1),
+            in_specs=[pl.BlockSpec(memory_space=pl.ANY)] + [in_vmem] * (tp - far - 1),
+            out_specs=[in_vmem] * (tp - far - 1),
+            compiler_params=small,
+            name="near",
+        )(base, *lifts[far:-1])
         lifts = [
             lax.ppermute(x, "tp", [(i, i ^ k) for i in range(tp)]) if k else x
-            for x, k in zip(lifts, order)
+            for x, k in zip([*lifts[:far], *near, lifts[-1]], order)
         ]
     else:
         lifts = lax.all_to_all(lifts[0], "tp", split_axis=0, concat_axis=0, tiled=True)
         lifts = [lifts.reshape(tp * here, columns)]
 
-    base = jnp.dot(gathered, base_projection_weight, preferred_element_type=jnp.float32)
     out = pl.pallas_call(
         functools.partial(add_kernel, order),
         out_shape=jax.ShapeDtypeStruct((tok_all, columns), jnp.bfloat16),

time: 57.8 us -> 66.1 us (1.14)
  waiting for transfers between devices: 10.5 us -> 20.4 us
  starting transfers between devices: 32.4 us -> 27.1 us
  local copies, waits for them, and re-layouts: 1.99 us -> 5.48 us
    ppermute x7, waiting for transfers between devices: 0.02 us -> 8.93 us  [on_device(): lax.ppermute(x, 'tp', [(i, i ^ k) for i in range(tp)])]
    ppermute x7, starting transfers between devices: 15.8 us -> 11.5 us  [on_device(): lax.ppermute(x, 'tp', [(i, i ^ k) for i in range(tp)])]
    unnamed x6 -> x12, local copies, waits for them, and re-layouts: 1.99 us -> 5.48 us
    ppermute x7, waiting for transfers between devices: 8.13 us -> 11.4 us  [sent(): return lax.ppermute(x, ('grp', 'tp'), onward)]
    ppermute x9 -> x6, waiting for transfers between devices: 2.38 us -> 0.02 us  [handed(): return lax.ppermute(x, 'grp', [(0, 1), (1, 0)])]
    ppermute x9 -> x6, starting transfers between devices: 1.35 us -> 0.61 us  [handed(): return lax.ppermute(x, 'grp', [(0, 1), (1, 0)])]
  transfers between devices with their start and end apart: 23 -> 20, of which waited for: 8 -> 11; matrix products, arithmetic and copies ran while one was open for 15% -> 0% of each run, Pallas kernels for 2% -> 0%
where the time goes in v12:
time: 66.1 us; the launch traced here: 65.9 us
  starting transfers between devices  27.1 us (41%)
  waiting for transfers between devices  20.4 us (31%)
  matrix products  8.54 us (13%)
  local copies, waits for them, and re-layouts  5.48 us (8%)
  Pallas kernels  4.31 us (7%)
    ppermute x7, starting transfers between devices, sent(): return lax.ppermute(x, ('grp', 'tp'), onward)  15 us
    ppermute x7, starting transfers between devices, on_device(): lax.ppermute(x, 'tp', [(i, i ^ k) for i in range(tp)])  11.5 us
    ppermute x7, waiting for transfers between devices, sent(): return lax.ppermute(x, ('grp', 'tp'), onward)  11.4 us
    ppermute x7, waiting for transfers between devices, on_device(): lax.ppermute(x, 'tp', [(i, i ^ k) for i in range(tp)])  8.93 us
    dot_general x1, matrix products, on_device(): jnp.dot(gathered, base_projection_weight, preferred_element_type=jnp.floa...  8.54 us
    unnamed x12, local copies, waits for them, and re-layouts  5.48 us
    pallas_call x1, Pallas kernels, on_device(): pl.pallas_call(functools.partial(lift_kernel, groups, tp, order), out_sha...  2.15 us
  transfers between devices with their start and end apart: 20, of which 11 were waited for; matrix products, arithmetic and copies ran while one was open for 0% of the time, Pallas kernels for 0%

profile of v12, /device:TPU:0, one launch (start us, length us, event | category | flops | bytes accessed | tf_op | source)
XLA Modules:
  0.0 65.9 jit_solution(90790225440840114)
XLA Ops:
  0.0 1.3 %copy-done = bf16[1,64,10240]{2,1,0:T(8,128)(2,1)S(1)} copy-done((bf16[1,64,10240]{2,1,0:T(8,128)(2,1)S(1)}, bf16[1,64,10240]{2,1,0:T(8,128)(2,1)}, u32[]{:S(2)}) %copy-start) | copy-done | bytes 1310744
  1.3 1.2 %copy-done.1 = bf16[1,8192,64]{1,2,0:T(8,128)(2,1)S(1)} copy-done((bf16[1,8192,64]{1,2,0:T(8,128)(2,1)S(1)}, bf16[1,8192,64]{1,2,0:T(8,128)(2,1)}, u32[]{:S(2)}) %copy-start.1) | copy-done | bytes 1048600
  2.5 0.9 %copy-done.2 = bf16[1,16,8192]{2,1,0:T(8,128)(2,1)S(1)} copy-done((bf16[1,16,8192]{2,1,0:T(8,128)(2,1)S(1)}, bf16[1,16,8192]{2,1,0:T(8,128)(2,1)}, u32[]{:S(2)}) %copy-start.2) | copy-done | bytes 262168
  5.5 1.1 %prepare.1 = (s32[1,128]{1,0:T(1,128)S(1)}, s32[128,1]{1,0:T(8,128)S(1)}, bf16[16,8192]{1,0:T(8,128)(2,1)S(1)}, bf16[64,8192]{1,0:T(8,128)(2,1)S(1)}, bf16[64,10240]{1,0:T(8,128)(2,1)S(1)}) custom-call(s32[2,12]{1,0:T(2,128)S(1)} %copy-done.3, s32[1,12]{1,0:T(1,128)S(1)} %copy-done.4, s32[16]{0:T(128)S(1)} %copy-done.5, bf16[16,8192]{1,0:T(8,128)(2,1)S(1)} %bitcast.10, ...), custom_call_target="tpu_custom_call" | custom-call | tf_op jit(solution)/shard_map/prepare/pallas_call | solution.py:157
  7.2 3.0 %collective-permute-start.2 = (bf16[16,8192]{1,0:T(8,128)(2,1)S(1)}, bf16[16,8192]{1,0:T(8,128)(2,1)S(1)}, u32[]{:S(2)}, u32[]{:S(2)}) collective-permute-start(bf16[16,8192]{1,0:T(8,128)(2,1)S(1)} %bitcast.11), channel_id=1, source_target_pairs={{0,2},{10,8},{2,4},{12,10},{4,6},{14,12},{6,7},{15,14},{7,5},{13,1... | collective-permute-start | bytes 786440 | tf_op jit(solution)/shard_map/ppermute | solution.py:30
  10.2 1.6 %collective-permute-start.4 = (bf16[16,8192]{1,0:T(8,128)(2,1)S(1)}, bf16[16,8192]{1,0:T(8,128)(2,1)S(1)}, u32[]{:S(2)}, u32[]{:S(2)}) collective-permute-start(bf16[16,8192]{1,0:T(8,128)(2,1)S(1)} %collective-permute-done.3), channel_id=1, source_target_pairs={{0,2},{10,8},{2,4},{12,10},{4,6},{14,12},{6,7},{15,14},{7,5},{13,1... | collective-permute-start | bytes 786440 | tf_op jit(solution)/shard_map/ppermute | solution.py:30
  11.8 2.7 %collective-permute-done.2.refs_5_ = bf16[16,8192]{1,0:T(8,128)(2,1)S(1)} collective-permute-done((bf16[16,8192]{1,0:T(8,128)(2,1)S(1)}, bf16[16,8192]{1,0:T(8,128)(2,1)S(1)}, u32[]{:S(2)}, u32[]{:S(2)}) %collective-permute-start.2) | collective-permute-done | bytes 262176 | tf_op jit(solution)/shard_map/ppermute | solution.py:30
  14.5 2.1 %collective-permute-start.6 = (bf16[16,8192]{1,0:T(8,128)(2,1)S(1)}, bf16[16,8192]{1,0:T(8,128)(2,1)S(1)}, u32[]{:S(2)}, u32[]{:S(2)}) collective-permute-start(bf16[16,8192]{1,0:T(8,128)(2,1)S(1)} %collective-permute-done.2.refs_5_), channel_id=1, source_target_pairs={{0,2},{10,8},{2,4},{12,10},{4,6},{14,12},{6,7},{15,14},{7,5},{13,1... | collective-permute-start | bytes 786440 | tf_op jit(solution)/shard_map/ppermute | solution.py:30
  17.3 2.1 %collective-permute-start.7 = (bf16[16,8192]{1,0:T(8,128)(2,1)S(1)}, bf16[16,8192]{1,0:T(8,128)(2,1)S(1)}, u32[]{:S(2)}, u32[]{:S(2)}) collective-permute-start(bf16[16,8192]{1,0:T(8,128)(2,1)S(1)} %collective-permute-done.4), channel_id=1, source_target_pairs={{0,2},{10,8},{2,4},{12,10},{4,6},{14,12},{6,7},{15,14},{7,5},{13,1... | collective-permute-start | bytes 786440 | tf_op jit(solution)/shard_map/ppermute | solution.py:30
  19.4 1.5 %collective-permute-done.6.refs_7_ = bf16[16,8192]{1,0:T(8,128)(2,1)S(1)} collective-permute-done((bf16[16,8192]{1,0:T(8,128)(2,1)S(1)}, bf16[16,8192]{1,0:T(8,128)(2,1)S(1)}, u32[]{:S(2)}, u32[]{:S(2)}) %collective-permute-start.6) | collective-permute-done | bytes 262176 | tf_op jit(solution)/shard_map/ppermute | solution.py:30
  20.9 2.1 %collective-permute-start.9 = (bf16[16,8192]{1,0:T(8,128)(2,1)S(1)}, bf16[16,8192]{1,0:T(8,128)(2,1)S(1)}, u32[]{:S(2)}, u32[]{:S(2)}) collective-permute-start(bf16[16,8192]{1,0:T(8,128)(2,1)S(1)} %collective-permute-done.6.refs_7_), channel_id=1, source_target_pairs={{0,2},{10,8},{2,4},{12,10},{4,6},{14,12},{6,7},{15,14},{7,5},{13,1... | collective-permute-start | bytes 786440 | tf_op jit(solution)/shard_map/ppermute | solution.py:30
  23.7 2.1 %collective-permute-start.10 = (bf16[16,8192]{1,0:T(8,128)(2,1)S(1)}, bf16[16,8192]{1,0:T(8,128)(2,1)S(1)}, u32[]{:S(2)}, u32[]{:S(2)}) collective-permute-start(bf16[16,8192]{1,0:T(8,128)(2,1)S(1)} %collective-permute-done.7), channel_id=1, source_target_pairs={{0,2},{10,8},{2,4},{12,10},{4,6},{14,12},{6,7},{15,14},{7,5},{13,1... | collective-permute-start | bytes 786440 | tf_op jit(solution)/shard_map/ppermute | solution.py:30
  25.8 1.5 %collective-permute-done.9.refs_9_ = bf16[16,8192]{1,0:T(8,128)(2,1)S(1)} collective-permute-done((bf16[16,8192]{1,0:T(8,128)(2,1)S(1)}, bf16[16,8192]{1,0:T(8,128)(2,1)S(1)}, u32[]{:S(2)}, u32[]{:S(2)}) %collective-permute-start.9) | collective-permute-done | bytes 262176 | tf_op jit(solution)/shard_map/ppermute | solution.py:30
  27.2 2.1 %collective-permute-start.12 = (bf16[16,8192]{1,0:T(8,128)(2,1)S(1)}, bf16[16,8192]{1,0:T(8,128)(2,1)S(1)}, u32[]{:S(2)}, u32[]{:S(2)}) collective-permute-start(bf16[16,8192]{1,0:T(8,128)(2,1)S(1)} %collective-permute-done.9.refs_9_), channel_id=1, source_target_pairs={{0,2},{10,8},{2,4},{12,10},{4,6},{14,12},{6,7},{15,14},{7,5},{13,1... | collective-permute-start | bytes 786440 | tf_op jit(solution)/shard_map/ppermute | solution.py:30
  30.1 3.6 %collective-permute-done.12.refs_11_ = bf16[16,8192]{1,0:T(8,128)(2,1)S(1)} collective-permute-done((bf16[16,8192]{1,0:T(8,128)(2,1)S(1)}, bf16[16,8192]{1,0:T(8,128)(2,1)S(1)}, u32[]{:S(2)}, u32[]{:S(2)}) %collective-permute-start.12) | collective-permute-done | bytes 262176 | tf_op jit(solution)/shard_map/ppermute | solution.py:30
  33.6 2.1 %lift.1 = (bf16[128,8192]{1,0:T(8,128)(2,1)S(1)}, bf16[32,1280]{1,0:T(8,128)(2,1)S(1)}, bf16[32,1280]{1,0:T(8,128)(2,1)S(1)}, bf16[32,1280]{1,0:T(8,128)(2,1)S(1...) custom-call(s32[1,128]{1,0:T(1,128)S(1)} %get-tuple-element.23.place, ...), custom_call_target="tpu_custom_call" | custom-call | flops 352321536 | bytes 4718592 | tf_op jit(solution)/shard_map/lift/pallas_call | solution.py:175
  35.8 8.5 %fusion.after_ref.base_ref = f32[128,1280]{1,0:T(8,128)S(1)} fusion(bf16[128,8192]{1,0:T(8,128)(2,1)S(1)} %get-tuple-element.27, bf16[8192,1280]{1,0:T(8,128)(2,1)} %param.8), kind=kOutput, calls=%fused_computation | convolution fusion | flops 2684354560 | bytes 23724032 | tf_op jit(solution)/shard_map/dot_general | solution.py:190
  44.4 3.1 %collective-permute-start.17 = (bf16[32,1280]{1,0:T(8,128)(2,1)S(1)}, bf16[32,1280]{1,0:T(8,128)(2,1)S(1)}, u32[]{:S(2)}, u32[]{:S(2)}) collective-permute-start(bf16[32,1280]{1,0:T(8,128)(2,1)S(1)} %get-tuple-element.35), channel_id=1, source_target_pairs={{0,3},{1,2},{2,1},{3,0},{4,7},{5,6},{6,5},{7,4},{8,11},{9,10},{10,... | collective-permute-start | bytes 245768 | tf_op jit(solution)/shard_map/ppermute | solution.py:202
  48.1 4.9 %collective-permute-start.13 = (bf16[32,1280]{1,0:T(8,128)(2,1)S(1)}, bf16[32,1280]{1,0:T(8,128)(2,1)S(1)}, u32[]{:S(2)}, u32[]{:S(2)}) collective-permute-start(bf16[32,1280]{1,0:T(8,128)(2,1)S(1)} %get-tuple-element.28), channel_id=1, source_target_pairs={{0,7},{1,6},{2,5},{3,4},{4,3},{5,2},{6,1},{7,0},{8,15},{9,14},{10,... | collective-permute-start | bytes 245768 | tf_op jit(solution)/shard_map/ppermute | solution.py:202
  53.2 1.3 %collective-permute-start.15 = (bf16[32,1280]{1,0:T(8,128)(2,1)S(1)}, bf16[32,1280]{1,0:T(8,128)(2,1)S(1)}, u32[]{:S(2)}, u32[]{:S(2)}) collective-permute-start(bf16[32,1280]{1,0:T(8,128)(2,1)S(1)} %get-tuple-element.30), channel_id=1, source_target_pairs={{0,5},{1,4},{2,7},{3,6},{4,1},{5,0},{6,3},{7,2},{8,13},{9,12},{10,... | collective-permute-start | bytes 245768 | tf_op jit(solution)/shard_map/ppermute | solution.py:202
  54.5 1.4 %collective-permute-start.16 = (bf16[32,1280]{1,0:T(8,128)(2,1)S(1)}, bf16[32,1280]{1,0:T(8,128)(2,1)S(1)}, u32[]{:S(2)}, u32[]{:S(2)}) collective-permute-start(bf16[32,1280]{1,0:T(8,128)(2,1)S(1)} %get-tuple-element.31), channel_id=1, source_target_pairs={{0,4},{1,5},{2,6},{3,7},{4,0},{5,1},{6,2},{7,3},{8,12},{9,13},{10,... | collective-permute-start | bytes 245768 | tf_op jit(solution)/shard_map/ppermute | solution.py:202
  56.4 2.9 %collective-permute-done.14.refs_1_ = bf16[32,1280]{1,0:T(8,128)(2,1)S(1)} collective-permute-done((bf16[32,1280]{1,0:T(8,128)(2,1)S(1)}, bf16[32,1280]{1,0:T(8,128)(2,1)S(1)}, u32[]{:S(2)}, u32[]{:S(2)}) %collective-permute-start.14) | collective-permute-done | bytes 81952 | tf_op jit(solution)/shard_map/ppermute | solution.py:202
  59.2 5.2 %collective-permute-done.15.refs_2_ = bf16[32,1280]{1,0:T(8,128)(2,1)S(1)} collective-permute-done((bf16[32,1280]{1,0:T(8,128)(2,1)S(1)}, bf16[32,1280]{1,0:T(8,128)(2,1)S(1)}, u32[]{:S(2)}, u32[]{:S(2)}) %collective-permute-start.15) | collective-permute-done | bytes 81952 | tf_op jit(solution)/shard_map/ppermute | solution.py:202
  64.9 1.0 %add.1 = bf16[128,1280]{1,0:T(8,128)(2,1)} custom-call(s32[128,1]{1,0:T(8,128)S(1)} %get-tuple-element.22.place_ref, f32[128,1280]{1,0:T(8,128)S(1)} %fusion.after_ref.base_ref, bf16[32,1280]{1,0:T(8,128)(2,1)S(1)} %collective-permute-done.13.refs_0_, bf16[32,1280]{1,0:T(8,128)(2,1)S(1)} %collective-permute-done.14.refs_1_, ...), custom_call_target="tpu_custom_call" | custom-call | tf_op jit(solution)/shard_map/add/pallas_call | solution.py:209
  (33 shorter events, 6.6 us)
Async XLA Ops:
  0.0 1.3 %copy-start = (bf16[1,64,10240]{2,1,0:T(8,128)(2,1)S(1)}, bf16[1,64,10240]{2,1,0:T(8,128)(2,1)}, u32[]{:S(2)}) copy-start(bf16[1,64,10240]{2,1,0:T(8,128)(2,1)} %param.10) | copy-start | bytes 3932164
  1.3 1.2 %copy-start.1 = (bf16[1,8192,64]{1,2,0:T(8,128)(2,1)S(1)}, bf16[1,8192,64]{1,2,0:T(8,128)(2,1)}, u32[]{:S(2)}) copy-start(bf16[1,8192,64]{1,2,0:T(8,128)(2,1)} %param.9) | copy-start | bytes 3145732
  2.5 0.9 %copy-start.2 = (bf16[1,16,8192]{2,1,0:T(8,128)(2,1)S(1)}, bf16[1,16,8192]{2,1,0:T(8,128)(2,1)}, u32[]{:S(2)}) copy-start(bf16[1,16,8192]{2,1,0:T(8,128)(2,1)} %param.7) | copy-start | bytes 786436
  3.5 0.7 %copy-start.3 = (s32[2,12]{1,0:T(2,128)S(1)}, s32[2,12]{1,0:T(2,128)}, u32[]{:S(2)}) copy-start(s32[2,12]{1,0:T(2,128)} %ids_ref.1) | copy-start | bytes 292
  6.6 3.6 %collective-permute-start.3 = (bf16[16,8192]{1,0:T(8,128)(2,1)S(1)}, bf16[16,8192]{1,0:T(8,128)(2,1)S(1)}, u32[]{:S(2)}, u32[]{:S(2)}) collective-permute-start(bf16[16,8192]{1,0:T(8,128)(2,1)S(1)} %get-tuple-element.26.refs_4_), channel_id=1, source_target_pairs={{0,8},{8,0},{1,9},{9,1},{2,10},{10,2},{3,11},{11,3},{4,12},{12,4},... | collective-permute-start | bytes 786440 | tf_op jit(solution)/shard_map/ppermute | solution.py:18
  7.1 26.5 %collective-permute-start.1 = (bf16[64,10240]{1,0:T(8,128)(2,1)S(1)}, bf16[64,10240]{1,0:T(8,128)(2,1)S(1)}, u32[]{:S(2)}, u32[]{:S(2)}) collective-permute-start(bf16[64,10240]{1,0:T(8,128)(2,1)S(1)} %get-tuple-element.25.refs_2_), channel_id=1, source_target_pairs={{0,8},{8,0},{1,9},{9,1},{2,10},{10,2},{3,11},{11,3},{4,12},{12,4},... | collective-permute-start | bytes 3932168 | tf_op jit(solution)/shard_map/ppermute | solution.py:18
  7.2 7.3 %collective-permute-start.2 = (bf16[16,8192]{1,0:T(8,128)(2,1)S(1)}, bf16[16,8192]{1,0:T(8,128)(2,1)S(1)}, u32[]{:S(2)}, u32[]{:S(2)}) collective-permute-start(bf16[16,8192]{1,0:T(8,128)(2,1)S(1)} %bitcast.11), channel_id=1, source_target_pairs={{0,2},{10,8},{2,4},{12,10},{4,6},{14,12},{6,7},{15,14},{7,5},{13,1... | collective-permute-start | bytes 786440 | tf_op jit(solution)/shard_map/ppermute | solution.py:30
  10.2 7.1 %collective-permute-start.4 = (bf16[16,8192]{1,0:T(8,128)(2,1)S(1)}, bf16[16,8192]{1,0:T(8,128)(2,1)S(1)}, u32[]{:S(2)}, u32[]{:S(2)}) collective-permute-start(bf16[16,8192]{1,0:T(8,128)(2,1)S(1)} %collective-permute-done.3), channel_id=1, source_target_pairs={{0,2},{10,8},{2,4},{12,10},{4,6},{14,12},{6,7},{15,14},{7,5},{13,1... | collective-permute-start | bytes 786440 | tf_op jit(solution)/shard_map/ppermute | solution.py:30
  11.8 21.8 %collective-permute-start = (bf16[64,8192]{1,0:T(8,128)(2,1)S(1)}, bf16[64,8192]{1,0:T(8,128)(2,1)S(1)}, u32[]{:S(2)}, u32[]{:S(2)}) collective-permute-start(bf16[64,8192]{1,0:T(8,128)(2,1)S(1)} %get-tuple-element.24.refs_0_), channel_id=1, source_target_pairs={{0,8},{8,0},{1,9},{9,1},{2,10},{10,2},{3,11},{11,3},{4,12},{12,4},... | collective-permute-start | bytes 3145736 | tf_op jit(solution)/shard_map/ppermute | solution.py:18
  14.5 6.4 %collective-permute-start.6 = (bf16[16,8192]{1,0:T(8,128)(2,1)S(1)}, bf16[16,8192]{1,0:T(8,128)(2,1)S(1)}, u32[]{:S(2)}, u32[]{:S(2)}) collective-permute-start(bf16[16,8192]{1,0:T(8,128)(2,1)S(1)} %collective-permute-done.2.refs_5_), channel_id=1, source_target_pairs={{0,2},{10,8},{2,4},{12,10},{4,6},{14,12},{6,7},{15,14},{7,5},{13,1... | collective-permute-start | bytes 786440 | tf_op jit(solution)/shard_map/ppermute | solution.py:30
  17.3 6.4 %collective-permute-start.7 = (bf16[16,8192]{1,0:T(8,128)(2,1)S(1)}, bf16[16,8192]{1,0:T(8,128)(2,1)S(1)}, u32[]{:S(2)}, u32[]{:S(2)}) collective-permute-start(bf16[16,8192]{1,0:T(8,128)(2,1)S(1)} %collective-permute-done.4), channel_id=1, source_target_pairs={{0,2},{10,8},{2,4},{12,10},{4,6},{14,12},{6,7},{15,14},{7,5},{13,1... | collective-permute-start | bytes 786440 | tf_op jit(solution)/shard_map/ppermute | solution.py:30
  20.9 6.4 %collective-permute-start.9 = (bf16[16,8192]{1,0:T(8,128)(2,1)S(1)}, bf16[16,8192]{1,0:T(8,128)(2,1)S(1)}, u32[]{:S(2)}, u32[]{:S(2)}) collective-permute-start(bf16[16,8192]{1,0:T(8,128)(2,1)S(1)} %collective-permute-done.6.refs_7_), channel_id=1, source_target_pairs={{0,2},{10,8},{2,4},{12,10},{4,6},{14,12},{6,7},{15,14},{7,5},{13,1... | collective-permute-start | bytes 786440 | tf_op jit(solution)/shard_map/ppermute | solution.py:30
  23.0 6.4 %collective-permute-start.5 = (bf16[16,8192]{1,0:T(8,128)(2,1)S(1)}, bf16[16,8192]{1,0:T(8,128)(2,1)S(1)}, u32[]{:S(2)}, u32[]{:S(2)}) collective-permute-start(bf16[16,8192]{1,0:T(8,128)(2,1)S(1)} %collective-permute-done.4), channel_id=1, source_target_pairs={{0,8},{8,0},{1,9},{9,1},{2,10},{10,2},{3,11},{11,3},{4,12},{12,4},... | collective-permute-start | bytes 786440 | tf_op jit(solution)/shard_map/ppermute | solution.py:18
  23.7 6.4 %collective-permute-start.10 = (bf16[16,8192]{1,0:T(8,128)(2,1)S(1)}, bf16[16,8192]{1,0:T(8,128)(2,1)S(1)}, u32[]{:S(2)}, u32[]{:S(2)}) collective-permute-start(bf16[16,8192]{1,0:T(8,128)(2,1)S(1)} %collective-permute-done.7), channel_id=1, source_target_pairs={{0,2},{10,8},{2,4},{12,10},{4,6},{14,12},{6,7},{15,14},{7,5},{13,1... | collective-permute-start | bytes 786440 | tf_op jit(solution)/shard_map/ppermute | solution.py:30
  27.2 6.4 %collective-permute-start.12 = (bf16[16,8192]{1,0:T(8,128)(2,1)S(1)}, bf16[16,8192]{1,0:T(8,128)(2,1)S(1)}, u32[]{:S(2)}, u32[]{:S(2)}) collective-permute-start(bf16[16,8192]{1,0:T(8,128)(2,1)S(1)} %collective-permute-done.9.refs_9_), channel_id=1, source_target_pairs={{0,2},{10,8},{2,4},{12,10},{4,6},{14,12},{6,7},{15,14},{7,5},{13,1... | collective-permute-start | bytes 786440 | tf_op jit(solution)/shard_map/ppermute | solution.py:30
  29.3 4.3 %collective-permute-start.8 = (bf16[16,8192]{1,0:T(8,128)(2,1)S(1)}, bf16[16,8192]{1,0:T(8,128)(2,1)S(1)}, u32[]{:S(2)}, u32[]{:S(2)}) collective-permute-start(bf16[16,8192]{1,0:T(8,128)(2,1)S(1)} %collective-permute-done.7), channel_id=1, source_target_pairs={{0,8},{8,0},{1,9},{9,1},{2,10},{10,2},{3,11},{11,3},{4,12},{12,4},... | collective-permute-start | bytes 786440 | tf_op jit(solution)/shard_map/ppermute | solution.py:18
  30.1 3.6 %collective-permute-start.11 = (bf16[16,8192]{1,0:T(8,128)(2,1)S(1)}, bf16[16,8192]{1,0:T(8,128)(2,1)S(1)}, u32[]{:S(2)}, u32[]{:S(2)}) collective-permute-start(bf16[16,8192]{1,0:T(8,128)(2,1)S(1)} %collective-permute-done.10), channel_id=1, source_target_pairs={{0,8},{8,0},{1,9},{9,1},{2,10},{10,2},{3,11},{11,3},{4,12},{12,4},... | collective-permute-start | bytes 786440 | tf_op jit(solution)/shard_map/ppermute | solution.py:18
  44.4 8.8 %collective-permute-start.17 = (bf16[32,1280]{1,0:T(8,128)(2,1)S(1)}, bf16[32,1280]{1,0:T(8,128)(2,1)S(1)}, u32[]{:S(2)}, u32[]{:S(2)}) collective-permute-start(bf16[32,1280]{1,0:T(8,128)(2,1)S(1)} %get-tuple-element.35), channel_id=1, source_target_pairs={{0,3},{1,2},{2,1},{3,0},{4,7},{5,6},{6,5},{7,4},{8,11},{9,10},{10,... | collective-permute-start | bytes 245768 | tf_op jit(solution)/shard_map/ppermute | solution.py:202
  47.5 7.0 %collective-permute-start.18 = (bf16[32,1280]{1,0:T(8,128)(2,1)S(1)}, bf16[32,1280]{1,0:T(8,128)(2,1)S(1)}, u32[]{:S(2)}, u32[]{:S(2)}) collective-permute-start(bf16[32,1280]{1,0:T(8,128)(2,1)S(1)} %get-tuple-element.36), channel_id=1, source_target_pairs={{0,2},{1,3},{2,0},{3,1},{4,6},{5,7},{6,4},{7,5},{8,10},{9,11},{10,... | collective-permute-start | bytes 245768 | tf_op jit(solution)/shard_map/ppermute | solution.py:202
  47.9 8.0 %collective-permute-start.19 = (bf16[32,1280]{1,0:T(8,128)(2,1)S(1)}, bf16[32,1280]{1,0:T(8,128)(2,1)S(1)}, u32[]{:S(2)}, u32[]{:S(2)}) collective-permute-start(bf16[32,1280]{1,0:T(8,128)(2,1)S(1)} %get-tuple-element.37), channel_id=1, source_target_pairs={{0,1},{1,0},{2,3},{3,2},{4,5},{5,4},{6,7},{7,6},{8,9},{9,8},{10,11... | collective-permute-start | bytes 245768 | tf_op jit(solution)/shard_map/ppermute | solution.py:202
  48.1 8.3 %collective-permute-start.13 = (bf16[32,1280]{1,0:T(8,128)(2,1)S(1)}, bf16[32,1280]{1,0:T(8,128)(2,1)S(1)}, u32[]{:S(2)}, u32[]{:S(2)}) collective-permute-start(bf16[32,1280]{1,0:T(8,128)(2,1)S(1)} %get-tuple-element.28), channel_id=1, source_target_pairs={{0,7},{1,6},{2,5},{3,4},{4,3},{5,2},{6,1},{7,0},{8,15},{9,14},{10,... | collective-permute-start | bytes 245768 | tf_op jit(solution)/shard_map/ppermute | solution.py:202
  53.0 6.2 %collective-permute-start.14 = (bf16[32,1280]{1,0:T(8,128)(2,1)S(1)}, bf16[32,1280]{1,0:T(8,128)(2,1)S(1)}, u32[]{:S(2)}, u32[]{:S(2)}) collective-permute-start(bf16[32,1280]{1,0:T(8,128)(2,1)S(1)} %get-tuple-element.29), channel_id=1, source_target_pairs={{0,6},{1,7},{2,4},{3,5},{4,2},{5,3},{6,0},{7,1},{8,14},{9,15},{10,... | collective-permute-start | bytes 245768 | tf_op jit(solution)/shard_map/ppermute | solution.py:202
  53.2 11.2 %collective-permute-start.15 = (bf16[32,1280]{1,0:T(8,128)(2,1)S(1)}, bf16[32,1280]{1,0:T(8,128)(2,1)S(1)}, u32[]{:S(2)}, u32[]{:S(2)}) collective-permute-start(bf16[32,1280]{1,0:T(8,128)(2,1)S(1)} %get-tuple-element.30), channel_id=1, source_target_pairs={{0,5},{1,4},{2,7},{3,6},{4,1},{5,0},{6,3},{7,2},{8,13},{9,12},{10,... | collective-permute-start | bytes 245768 | tf_op jit(solution)/shard_map/ppermute | solution.py:202
  54.5 10.3 %collective-permute-start.16 = (bf16[32,1280]{1,0:T(8,128)(2,1)S(1)}, bf16[32,1280]{1,0:T(8,128)(2,1)S(1)}, u32[]{:S(2)}, u32[]{:S(2)}) collective-permute-start(bf16[32,1280]{1,0:T(8,128)(2,1)S(1)} %get-tuple-element.31), channel_id=1, source_target_pairs={{0,4},{1,5},{2,6},{3,7},{4,0},{5,1},{6,2},{7,3},{8,12},{9,13},{10,... | collective-permute-start | bytes 245768 | tf_op jit(solution)/shard_map/ppermute | solution.py:202
  (2 other events, 1.3 us)

commit v13 on v10

--- a/solution.py
+++ b/solution.py
@@ -10,59 +10,56 @@
 adapter_scale = 1.0
 
 
-def swapped(x, axis):
+def fetched(x, axis="grp", shift=0):
     n = lax.axis_size(axis)
-    return [x] + [
-        lax.ppermute(x, axis, [((i + s) % n, i) for i in range(n)]) for s in range(1, n)
-    ]
+    return lax.ppermute(x, axis, [((i + shift) % n, i) for i in range(n)])
 
 
 def ring_of(n):
     return list(range(0, n, 2)) + list(range(1, n, 2))[::-1]
 
 
-def ring_gather(block):
-    n = lax.axis_size("tp")
-    ring = ring_of(n)
-    onward = []
-    for i in range(n):
-        onward.append((ring[i], ring[(i + 1) % n]))
-        onward.append((n + ring[(i + 1) % n], n + ring[i]))
-
-    def sent(x):
-        return lax.ppermute(x, ("grp", "tp"), onward)
-
-    def handed(x):
-        return lax.ppermute(x, "grp", [(0, 1), (1, 0)])
-
-    mine, other = block, handed(block)
-    pieces = [block]
-    for step in range(1, n // 2):
-        mine, other = sent(mine), sent(other)
-        pieces += [mine, handed(other)]
-    return pieces + [sent(mine)]
-
-
-def ring_sources(n):
-    me = lax.axis_index("tp")
-    way = 1 - 2 * lax.axis_index("grp")
+class Ring:
+    def __init__(self, block, axis, last_from_behind):
+        n = lax.axis_size(axis)
+        ring = ring_of(n)
+        self.n, self.axis, self.last_from_behind = n, axis, last_from_behind
+        self.up = [(ring[i], ring[(i + 1) % n]) for i in range(n)]
+        self.down = [(ring[(i + 1) % n], ring[i]) for i in range(n)]
+        self.ahead = self.behind = block
+        self.pieces = [block]
+
+    def step(self, i):
+        last = i == self.n // 2
+        if not last or self.last_from_behind:
+            self.ahead = lax.ppermute(self.ahead, self.axis, self.up)
+            self.pieces.append(self.ahead)
+        if not last or not self.last_from_behind:
+            self.behind = lax.ppermute(self.behind, self.axis, self.down)
+            self.pieces.append(self.behind)
+
+
+def ring_sources(axis):
+    n = lax.axis_size(axis)
+    me = lax.axis_index(axis)
     place = jnp.where(lax.rem(me, 2) == 0, me // 2, n - 1 - me // 2)
-    distances = [0] + [d for i in range(1, n // 2) for d in (way * i, -way * i)] + [n // 2]
+    distances = [0] + [d for i in range(1, n // 2) for d in (i, -i)] + [n // 2]
     sources = []
     for distance in distances:
-        at = lax.rem(place - distance + 2 * n, n)
+        at = lax.rem(place - distance + n, n)
         sources.append(jnp.where(at < n // 2, 2 * at, 2 * (n - 1 - at) + 1))
     return sources
 
 
-def prepare_kernel(groups, tp, ids_ref, lengths_ref, slots_ref, *refs):
-    n = (len(refs) - 2) // 2
-    row_ref, column_ref = refs[n : n + 2]
-    for source, target in zip(refs[:n], refs[n + 2 :]):
-        target[...] = source[...]
+def halve_kernel(block_ref, *out_refs):
+    width = out_refs[0].shape[1]
+    for i, out_ref in enumerate(out_refs):
+        out_ref[...] = block_ref[:, i * width : (i + 1) * width]
+
+
+def place_kernel(groups, tp, ids_ref, lengths_ref, slots_ref, row_ref, column_ref):
     group = lax.axis_index("grp")
-    tok_all = row_ref.shape[1]
-    longest = tok_all // 8
+    longest = row_ref.shape[1] // 8
     along = lax.broadcasted_iota(jnp.int32, row_ref.shape, 1)
     down = lax.broadcasted_iota(jnp.int32, column_ref.shape, 0)
 
@@ -80,15 +77,18 @@
     _, row_ref[...], column_ref[...] = lax.fori_loop(0, ids_ref.shape[1], add, carry)
 
 
-def lift_kernel(groups, tp, place_ref, *refs):
+def lift_kernel(groups, place_ref, *refs):
     downs, ups, pieces = refs[:groups], refs[groups : 2 * groups], refs[2 * groups : -3]
     tokens_ref, out_ref, up_ref = refs[-3:]
     rank = ups[0].shape[0]
-    rows = pieces[0].shape[0]
+    rows, width = pieces[0].shape
     tok_all = tokens_ref.shape[0]
     parts, slots, columns = out_ref.shape
-    for piece, source in zip(pieces, ring_sources(tp)):
-        tokens_ref[pl.ds(pl.multiple_of(source * rows, rows), rows), :] = piece[...]
+    sources = ring_sources("tp")
+    for i, piece in enumerate(pieces):
+        start = pl.multiple_of(sources[i % len(sources)] * rows, rows)
+        column = i // len(sources) * width
+        tokens_ref[pl.ds(start, rows), column : column + width] = piece[...]
     for s, up in enumerate(ups):
         up_ref[s * rank : (s + 1) * rank, :] = up[...]
     down = jnp.concatenate([down[...] for down in downs], axis=0).T
@@ -130,30 +130,48 @@
     tok_all = tokens.shape[1] * tp
     longest = tok_all // 8
     here = groups * longest
+    half = width // 2
     in_vmem = pl.BlockSpec(memory_space=pltpu.VMEM)
     in_smem = pl.BlockSpec(memory_space=pltpu.SMEM)
     small = pltpu.CompilerParams(vmem_limit_bytes=16 * 2**20)
 
-    arrays = (tokens[0], adapter_down_panels[0].T, adapter_up_panels[0])
-    pieces = ring_gather(arrays[0])
-    others = [swapped(x, "grp")[1:] for x in arrays[1:]]
-    row, column, own, down, up = pl.pallas_call(
-        functools.partial(prepare_kernel, groups, tp),
+    halves = pl.pallas_call(
+        halve_kernel,
+        out_shape=[jax.ShapeDtypeStruct((tokens.shape[1], half), jnp.bfloat16)] * 2,
+        in_specs=[in_vmem],
+        out_specs=[in_vmem] * 2,
+        compiler_params=small,
+        name="halve",
+    )(tokens[0])
+    rings = [Ring(part, "tp", k == 0) for k, part in enumerate(halves)]
+    for i in range(1, tp // 2 + 1):
+        for ring in rings:
+            ring.step(i)
+
+    pieces = rings[0].pieces + rings[1].pieces
+
+    panels = [
+        fetched(panel, shift=s)
+        for panel in (adapter_down_panels[0].T, adapter_up_panels[0])
+        for s in range(groups)
+    ]
+    requests = [
+        fetched(x) for x in (request_adapter_ids, request_token_lengths, adapter_store_slot)
+    ]
+    row, column = pl.pallas_call(
+        functools.partial(place_kernel, groups, tp),
         out_shape=[
             jax.ShapeDtypeStruct((1, tok_all), jnp.int32),
             jax.ShapeDtypeStruct((tok_all, 1), jnp.int32),
-        ]
-        + [jax.ShapeDtypeStruct(x.shape, x.dtype) for x in arrays],
-        in_specs=[in_smem] * 3 + [in_vmem] * 3,
-        out_specs=[in_vmem] * 5,
+        ],
+        in_specs=[in_smem] * 3,
+        out_specs=[in_vmem] * 2,
         compiler_params=small,
-        name="prepare",
-    )(request_adapter_ids, request_token_lengths, adapter_store_slot, *arrays)
-    panels = [down, *others[0], up, *others[1]]
-    pieces[0] = own
+        name="place",
+    )(*requests)
 
     gathered, lifts = pl.pallas_call(
-        functools.partial(lift_kernel, groups, tp),
+        functools.partial(lift_kernel, groups),
         out_shape=[
             jax.ShapeDtypeStruct((tok_all, width), jnp.bfloat16),
             jax.ShapeDtypeStruct((tp, here, columns), jnp.bfloat16),

time: 59 us -> 76.3 us (1.29)
  waiting for transfers between devices: 17.6 us -> 36.1 us
  local copies, waits for them, and re-layouts: 5.48 us -> 0.95 us
  starting transfers between devices: 21.9 us -> 25.3 us
    ppermute x13 -> x21, waiting for transfers between devices: 8.08 us -> 33 us  [the longest x7 22.4 us: step(): self.ahead = lax.ppermute(self.ahead, self.axis, self.up)]
    all_to_all x1, waiting for transfers between devices: 9.47 us -> 3.15 us  [on_device(): lifts = lax.all_to_all(lifts, 'tp', split_axis=0, concat_axis=0, tiled=True)]
    ppermute x13 -> x21, starting transfers between devices: 15.5 us -> 20.5 us  [the longest x7 13.1 us: step(): self.behind = lax.ppermute(self.behind, self.axis, self.down)]
    unnamed x12 -> x2, local copies, waits for them, and re-layouts: 5.48 us -> 0.95 us
    all_to_all x1, starting transfers between devices: 6.34 us -> 4.88 us  [on_device(): lifts = lax.all_to_all(lifts, 'tp', split_axis=0, concat_axis=0, tiled=True)]
    pallas_call x2 -> x3, Pallas kernels: 4.13 us -> 3.98 us  [the longest x1 3 us: on_device(): pl.pallas_call(functools.partial(lift_kernel, groups), out_shape=[jax.Sha...]
  transfers between devices with their start and end apart: 14 -> 22, of which waited for: 7 -> 11; matrix products, arithmetic and copies ran while one was open for 15% -> 11% of each run, Pallas kernels for 2% -> 1%
where the time goes in v13:
time: 76.3 us; the launch traced here: 76 us
  waiting for transfers between devices  36.1 us (47%)
  starting transfers between devices  25.3 us (33%)
  matrix products  8.53 us (11%)
  Pallas kernels  5 us (7%)
  local copies, waits for them, and re-layouts  0.95 us (1%)
    ppermute x7, waiting for transfers between devices, step(): self.ahead = lax.ppermute(self.ahead, self.axis, self.up)  22.4 us
    ppermute x7, starting transfers between devices, step(): self.behind = lax.ppermute(self.behind, self.axis, self.down)  13.1 us
    ppermute x7, waiting for transfers between devices, step(): self.behind = lax.ppermute(self.behind, self.axis, self.down)  10.5 us
    dot_general x1, matrix products, on_device(): jnp.dot(gathered, base_projection_weight, preferred_element_type=jnp.floa...  8.53 us
    all_to_all x1, starting transfers between devices, on_device(): lifts = lax.all_to_all(lifts, 'tp', split_axis=0, concat_axis=0, tiled=True)  4.88 us
    ppermute x7, starting transfers between devices, fetched(): return lax.ppermute(x, axis, [((i + shift) % n, i) for i in range(n)])  4.54 us
    all_to_all x1, waiting for transfers between devices, on_device(): lifts = lax.all_to_all(lifts, 'tp', split_axis=0, concat_axis=0, tiled=True)  3.15 us
    pallas_call x1, Pallas kernels, on_device(): pl.pallas_call(functools.partial(lift_kernel, groups), out_shape=[jax.Sha...  3 us
  transfers between devices with their start and end apart: 22, of which 11 were waited for; matrix products, arithmetic and copies ran while one was open for 11% of the time, Pallas kernels for 1%

profile of v13, /device:TPU:0, one launch (start us, length us, event | category | flops | bytes accessed | tf_op | source)
XLA Modules:
  0.0 76.0 jit_solution(4880941970343737964)
XLA Ops:
  1.0 3.0 %collective-permute-start.8 = (bf16[16,4096]{1,0:T(8,128)(2,1)S(1)}, bf16[16,4096]{1,0:T(8,128)(2,1)S(1)}, u32[]{:S(2)}, u32[]{:S(2)}) collective-permute-start(bf16[16,4096]{1,0:T(8,128)(2,1)S(1)} %get-tuple-element.13.refs_4_), channel_id=1, source_target_pairs={{2,0},{4,2},{6,4},{7,6},{5,7},{3,5},{1,3},{0,1},{10,8},{12,10},{14... | collective-permute-start | bytes 393224 | tf_op jit(solution)/shard_map/ppermute | solution.py:38
  6.1 1.9 %collective-permute-start.15 = (bf16[16,4096]{1,0:T(8,128)(2,1)S(1)}, bf16[16,4096]{1,0:T(8,128)(2,1)S(1)}, u32[]{:S(2)}, u32[]{:S(2)}) collective-permute-start(bf16[16,4096]{1,0:T(8,128)(2,1)S(1)} %get-tuple-element.14.refs_12_), channel_id=1, source_target_pairs={{2,0},{4,2},{6,4},{7,6},{5,7},{3,5},{1,3},{0,1},{10,8},{12,10},{14... | collective-permute-start | bytes 393224 | tf_op jit(solution)/shard_map/ppermute | solution.py:38
  8.0 1.3 %collective-permute-start.5 = (bf16[64,10240]{1,0:T(8,128)(2,1)}, bf16[64,10240]{1,0:T(8,128)(2,1)S(1)}, u32[]{:S(2)}, u32[]{:S(2)}) collective-permute-start(bf16[64,10240]{1,0:T(8,128)(2,1)} %bitcast.12), channel_id=1, source_target_pairs={{0,0},{8,8},{1,1},{9,9},{2,2},{10,10},{3,3},{11,11},{4,4},{12,12},... | collective-permute-start | bytes 3932168 | tf_op jit(solution)/shard_map/ppermute | solution.py:15
  9.5 1.9 %collective-permute-start.10 = (bf16[16,4096]{1,0:T(8,128)(2,1)S(1)}, bf16[16,4096]{1,0:T(8,128)(2,1)S(1)}, u32[]{:S(2)}, u32[]{:S(2)}) collective-permute-start(bf16[16,4096]{1,0:T(8,128)(2,1)S(1)} %collective-permute-done.8.refs_6_), channel_id=1, source_target_pairs={{2,0},{4,2},{6,4},{7,6},{5,7},{3,5},{1,3},{0,1},{10,8},{12,10},{14... | collective-permute-start | bytes 393224 | tf_op jit(solution)/shard_map/ppermute | solution.py:38
  11.4 1.7 %collective-permute-start.9 = (bf16[16,4096]{1,0:T(8,128)(2,1)S(1)}, bf16[16,4096]{1,0:T(8,128)(2,1)S(1)}, u32[]{:S(2)}, u32[]{:S(2)}) collective-permute-start(bf16[16,4096]{1,0:T(8,128)(2,1)S(1)} %collective-permute-done.7.refs_5_), channel_id=1, source_target_pairs={{0,2},{2,4},{4,6},{6,7},{7,5},{5,3},{3,1},{1,0},{8,10},{10,12},{12... | collective-permute-start | bytes 393224 | tf_op jit(solution)/shard_map/ppermute | solution.py:35
  13.0 2.6 %collective-permute-done.14.refs_13_ = bf16[16,4096]{1,0:T(8,128)(2,1)S(1)} collective-permute-done((bf16[16,4096]{1,0:T(8,128)(2,1)S(1)}, bf16[16,4096]{1,0:T(8,128)(2,1)S(1)}, u32[]{:S(2)}, u32[]{:S(2)}) %collective-permute-start.14) | collective-permute-done | bytes 131104 | tf_op jit(solution)/shard_map/ppermute | solution.py:35
  15.6 1.6 %collective-permute-start.17 = (bf16[16,4096]{1,0:T(8,128)(2,1)S(1)}, bf16[16,4096]{1,0:T(8,128)(2,1)S(1)}, u32[]{:S(2)}, u32[]{:S(2)}) collective-permute-start(bf16[16,4096]{1,0:T(8,128)(2,1)S(1)} %collective-permute-done.15.refs_14_), channel_id=1, source_target_pairs={{2,0},{4,2},{6,4},{7,6},{5,7},{3,5},{1,3},{0,1},{10,8},{12,10},{14... | collective-permute-start | bytes 393224 | tf_op jit(solution)/shard_map/ppermute | solution.py:38
  18.1 1.2 %collective-permute-start.3 = (bf16[64,8192]{1,0:T(8,128)(2,1)}, bf16[64,8192]{1,0:T(8,128)(2,1)S(1)}, u32[]{:S(2)}, u32[]{:S(2)}) collective-permute-start(bf16[64,8192]{1,0:T(8,128)(2,1)} %bitcast.14), channel_id=1, source_target_pairs={{0,0},{8,8},{1,1},{9,9},{2,2},{10,10},{3,3},{11,11},{4,4},{12,12},... | collective-permute-start | bytes 3145736 | tf_op jit(solution)/shard_map/ppermute | solution.py:15
  19.3 1.3 %collective-permute-done.17.refs_16_ = bf16[16,4096]{1,0:T(8,128)(2,1)S(1)} collective-permute-done((bf16[16,4096]{1,0:T(8,128)(2,1)S(1)}, bf16[16,4096]{1,0:T(8,128)(2,1)S(1)}, u32[]{:S(2)}, u32[]{:S(2)}) %collective-permute-start.17) | collective-permute-done | bytes 131104 | tf_op jit(solution)/shard_map/ppermute | solution.py:38
  20.8 4.7 %collective-permute-done.16.refs_15_ = bf16[16,4096]{1,0:T(8,128)(2,1)S(1)} collective-permute-done((bf16[16,4096]{1,0:T(8,128)(2,1)S(1)}, bf16[16,4096]{1,0:T(8,128)(2,1)S(1)}, u32[]{:S(2)}, u32[]{:S(2)}) %collective-permute-start.16) | collective-permute-done | bytes 131104 | tf_op jit(solution)/shard_map/ppermute | solution.py:35
  25.6 1.6 %collective-permute-start.12 = (bf16[16,4096]{1,0:T(8,128)(2,1)S(1)}, bf16[16,4096]{1,0:T(8,128)(2,1)S(1)}, u32[]{:S(2)}, u32[]{:S(2)}) collective-permute-start(bf16[16,4096]{1,0:T(8,128)(2,1)S(1)} %collective-permute-done.10.refs_8_), channel_id=1, source_target_pairs={{2,0},{4,2},{6,4},{7,6},{5,7},{3,5},{1,3},{0,1},{10,8},{12,10},{14... | collective-permute-start | bytes 393224 | tf_op jit(solution)/shard_map/ppermute | solution.py:38
  27.2 3.4 %collective-permute-done.12.refs_10_ = bf16[16,4096]{1,0:T(8,128)(2,1)S(1)} collective-permute-done((bf16[16,4096]{1,0:T(8,128)(2,1)S(1)}, bf16[16,4096]{1,0:T(8,128)(2,1)S(1)}, u32[]{:S(2)}, u32[]{:S(2)}) %collective-permute-start.12) | collective-permute-done | bytes 131104 | tf_op jit(solution)/shard_map/ppermute | solution.py:38
  30.8 4.7 %collective-permute-done.11.refs_9_ = bf16[16,4096]{1,0:T(8,128)(2,1)S(1)} collective-permute-done((bf16[16,4096]{1,0:T(8,128)(2,1)S(1)}, bf16[16,4096]{1,0:T(8,128)(2,1)S(1)}, u32[]{:S(2)}, u32[]{:S(2)}) %collective-permute-start.11) | collective-permute-done | bytes 131104 | tf_op jit(solution)/shard_map/ppermute | solution.py:35
  35.5 1.6 %collective-permute-start.19 = (bf16[16,4096]{1,0:T(8,128)(2,1)S(1)}, bf16[16,4096]{1,0:T(8,128)(2,1)S(1)}, u32[]{:S(2)}, u32[]{:S(2)}) collective-permute-start(bf16[16,4096]{1,0:T(8,128)(2,1)S(1)} %collective-permute-done.17.refs_16_), channel_id=1, source_target_pairs={{2,0},{4,2},{6,4},{7,6},{5,7},{3,5},{1,3},{0,1},{10,8},{12,10},{14... | collective-permute-start | bytes 393224 | tf_op jit(solution)/shard_map/ppermute | solution.py:38
  37.1 3.4 %collective-permute-done.19.refs_18_ = bf16[16,4096]{1,0:T(8,128)(2,1)S(1)} collective-permute-done((bf16[16,4096]{1,0:T(8,128)(2,1)S(1)}, bf16[16,4096]{1,0:T(8,128)(2,1)S(1)}, u32[]{:S(2)}, u32[]{:S(2)}) %collective-permute-start.19) | collective-permute-done | bytes 131104 | tf_op jit(solution)/shard_map/ppermute | solution.py:38
  40.7 4.7 %collective-permute-done.18.refs_17_ = bf16[16,4096]{1,0:T(8,128)(2,1)S(1)} collective-permute-done((bf16[16,4096]{1,0:T(8,128)(2,1)S(1)}, bf16[16,4096]{1,0:T(8,128)(2,1)S(1)}, u32[]{:S(2)}, u32[]{:S(2)}) %collective-permute-start.18) | collective-permute-done | bytes 131104 | tf_op jit(solution)/shard_map/ppermute | solution.py:35
  45.7 4.7 %collective-permute-done.13.refs_11_ = bf16[16,4096]{1,0:T(8,128)(2,1)S(1)} collective-permute-done((bf16[16,4096]{1,0:T(8,128)(2,1)S(1)}, bf16[16,4096]{1,0:T(8,128)(2,1)S(1)}, u32[]{:S(2)}, u32[]{:S(2)}) %collective-permute-start.13) | collective-permute-done | bytes 131104 | tf_op jit(solution)/shard_map/ppermute | solution.py:35
  50.4 1.6 %collective-permute-start.20 = (bf16[16,4096]{1,0:T(8,128)(2,1)S(1)}, bf16[16,4096]{1,0:T(8,128)(2,1)S(1)}, u32[]{:S(2)}, u32[]{:S(2)}) collective-permute-start(bf16[16,4096]{1,0:T(8,128)(2,1)S(1)} %collective-permute-done.19.refs_18_), channel_id=1, source_target_pairs={{2,0},{4,2},{6,4},{7,6},{5,7},{3,5},{1,3},{0,1},{10,8},{12,10},{14... | collective-permute-start | bytes 393224 | tf_op jit(solution)/shard_map/ppermute | solution.py:38
  53.0 2.4 %collective-permute-done.20.refs_19_ = bf16[16,4096]{1,0:T(8,128)(2,1)S(1)} collective-permute-done((bf16[16,4096]{1,0:T(8,128)(2,1)S(1)}, bf16[16,4096]{1,0:T(8,128)(2,1)S(1)}, u32[]{:S(2)}, u32[]{:S(2)}) %collective-permute-start.20) | collective-permute-done | bytes 131104 | tf_op jit(solution)/shard_map/ppermute | solution.py:38
  55.4 3.0 %lift.1 = (bf16[128,8192]{1,0:T(8,128)(2,1)S(1)}, bf16[8,32,1280]{2,1,0:T(8,128)(2,1)}) custom-call(s32[1,128]{1,0:T(1,128)S(1)} %get-tuple-element.12.place_ref, bf16[64,8192]{1,0:T(8,128)(2,1)S(1)} %collective-permute-done.3.refs_0_, bf16[64,8192]{1,0:T(8,128)(2,1)S(1)} %collective-permute-done.4.refs_1_, ...), custom_call_target="tpu_custom_call" | custom-call | flops 352321536 | bytes 4718592 | tf_op jit(solution)/shard_map/lift/pallas_call | solution.py:173
  58.4 4.9 %all-to-all-start = ((bf16[8,32,1280]{2,1,0:T(8,128)(2,1)}), bf16[8,32,1280]{2,1,0:T(8,128)(2,1)S(1)}, u32[]{:S(2)}, u32[]{:S(2)}) async-start(bf16[8,32,1280]{2,1,0:T(8,128)(2,1)} %get-tuple-element.16), calls=%async_computation | async-start | bytes 1310720 | tf_op jit(solution)/shard_map/all_to_all | solution.py:190
  63.3 8.5 %fusion.base_ref = f32[128,1280]{1,0:T(8,128)S(1)} fusion(bf16[128,8192]{1,0:T(8,128)(2,1)S(1)} %get-tuple-element.15, bf16[8192,1280]{1,0:T(8,128)(2,1)} %param.8), kind=kOutput, calls=%fused_computation | convolution fusion | flops 2684354560 | bytes 23724032 | tf_op jit(solution)/shard_map/dot_general | solution.py:192
  71.8 3.1 %all-to-all-done = bf16[8,32,1280]{2,1,0:T(8,128)(2,1)S(1)} async-done(((bf16[8,32,1280]{2,1,0:T(8,128)(2,1)}), bf16[8,32,1280]{2,1,0:T(8,128)(2,1)S(1)}, u32[]{:S(2)}, u32[]{:S(2)}) %all-to-all-start) | async-done | bytes 655392 | tf_op jit(solution)/shard_map/all_to_all | solution.py:190
  75.0 1.0 %add.1 = bf16[128,1280]{1,0:T(8,128)(2,1)} custom-call(s32[128,1]{1,0:T(8,128)S(1)} %get-tuple-element.11.place_ref, f32[128,1280]{1,0:T(8,128)S(1)} %fusion.base_ref, bf16[256,1280]{1,0:T(8,128)(2,1)S(1)} %bitcast.9), custom_call_target="tpu_custom_call" | custom-call | tf_op jit(solution)/shard_map/add/pallas_call | solution.py:193
  (27 shorter events, 6.0 us)
Async XLA Ops:
  0.0 0.9 %copy-start = (bf16[1,16,8192]{2,1,0:T(8,128)(2,1)S(1)}, bf16[1,16,8192]{2,1,0:T(8,128)(2,1)}, u32[]{:S(2)}) copy-start(bf16[1,16,8192]{2,1,0:T(8,128)(2,1)} %param.7) | copy-start | bytes 786436
  1.0 8.4 %collective-permute-start.8 = (bf16[16,4096]{1,0:T(8,128)(2,1)S(1)}, bf16[16,4096]{1,0:T(8,128)(2,1)S(1)}, u32[]{:S(2)}, u32[]{:S(2)}) collective-permute-start(bf16[16,4096]{1,0:T(8,128)(2,1)S(1)} %get-tuple-element.13.refs_4_), channel_id=1, source_target_pairs={{2,0},{4,2},{6,4},{7,6},{5,7},{3,5},{1,3},{0,1},{10,8},{12,10},{14... | collective-permute-start | bytes 393224 | tf_op jit(solution)/shard_map/ppermute | solution.py:38
  4.0 5.5 %collective-permute-start.7 = (bf16[16,4096]{1,0:T(8,128)(2,1)S(1)}, bf16[16,4096]{1,0:T(8,128)(2,1)S(1)}, u32[]{:S(2)}, u32[]{:S(2)}) collective-permute-start(bf16[16,4096]{1,0:T(8,128)(2,1)S(1)} %get-tuple-element.13.refs_4_), channel_id=1, source_target_pairs={{0,2},{2,4},{4,6},{6,7},{7,5},{5,3},{3,1},{1,0},{8,10},{10,12},{12... | collective-permute-start | bytes 393224 | tf_op jit(solution)/shard_map/ppermute | solution.py:35
  4.1 2.0 %collective-permute-start.1 = (s32[1,12]{1,0:T(1,128)}, s32[1,12]{1,0:T(1,128)S(1)}, u32[]{:S(2)}, u32[]{:S(2)}) collective-permute-start(s32[1,12]{1,0:T(1,128)} %param.12), channel_id=1, source_target_pairs={{0,0},{8,8},{1,1},{9,9},{2,2},{10,10},{3,3},{11,11},{4,4},{12,12},... | collective-permute-start | bytes 152 | tf_op jit(solution)/shard_map/ppermute | solution.py:15
  4.8 3.2 %collective-permute-start.2 = (s32[16]{0:T(128)}, s32[16]{0:T(128)S(1)}, u32[]{:S(2)}, u32[]{:S(2)}) collective-permute-start(s32[16]{0:T(128)} %param.13), channel_id=1, source_target_pairs={{0,0},{8,8},{1,1},{9,9},{2,2},{10,10},{3,3},{11,11},{4,4},{12,12},... | collective-permute-start | bytes 200 | tf_op jit(solution)/shard_map/ppermute | solution.py:15
  5.4 2.6 %collective-permute-start = (s32[2,12]{1,0:T(2,128)}, s32[2,12]{1,0:T(2,128)S(1)}, u32[]{:S(2)}, u32[]{:S(2)}) collective-permute-start(s32[2,12]{1,0:T(2,128)} %param.11), channel_id=1, source_target_pairs={{0,0},{8,8},{1,1},{9,9},{2,2},{10,10},{3,3},{11,11},{4,4},{12,12},... | collective-permute-start | bytes 296 | tf_op jit(solution)/shard_map/ppermute | solution.py:15
  6.1 5.3 %collective-permute-start.15 = (bf16[16,4096]{1,0:T(8,128)(2,1)S(1)}, bf16[16,4096]{1,0:T(8,128)(2,1)S(1)}, u32[]{:S(2)}, u32[]{:S(2)}) collective-permute-start(bf16[16,4096]{1,0:T(8,128)(2,1)S(1)} %get-tuple-element.14.refs_12_), channel_id=1, source_target_pairs={{2,0},{4,2},{6,4},{7,6},{5,7},{3,5},{1,3},{0,1},{10,8},{12,10},{14... | collective-permute-start | bytes 393224 | tf_op jit(solution)/shard_map/ppermute | solution.py:38
  8.0 47.4 %collective-permute-start.6 = (bf16[64,10240]{1,0:T(8,128)(2,1)}, bf16[64,10240]{1,0:T(8,128)(2,1)S(1)}, u32[]{:S(2)}, u32[]{:S(2)}) collective-permute-start(bf16[64,10240]{1,0:T(8,128)(2,1)} %bitcast.11), channel_id=1, source_target_pairs={{8,0},{0,8},{9,1},{1,9},{10,2},{2,10},{11,3},{3,11},{12,4},{4,12},... | collective-permute-start | bytes 3932168 | tf_op jit(solution)/shard_map/ppermute | solution.py:15
  8.0 47.4 %collective-permute-start.5 = (bf16[64,10240]{1,0:T(8,128)(2,1)}, bf16[64,10240]{1,0:T(8,128)(2,1)S(1)}, u32[]{:S(2)}, u32[]{:S(2)}) collective-permute-start(bf16[64,10240]{1,0:T(8,128)(2,1)} %bitcast.12), channel_id=1, source_target_pairs={{0,0},{8,8},{1,1},{9,9},{2,2},{10,10},{3,3},{11,11},{4,4},{12,12},... | collective-permute-start | bytes 3932168 | tf_op jit(solution)/shard_map/ppermute | solution.py:15
  9.4 6.3 %collective-permute-start.14 = (bf16[16,4096]{1,0:T(8,128)(2,1)S(1)}, bf16[16,4096]{1,0:T(8,128)(2,1)S(1)}, u32[]{:S(2)}, u32[]{:S(2)}) collective-permute-start(bf16[16,4096]{1,0:T(8,128)(2,1)S(1)} %get-tuple-element.14.refs_12_), channel_id=1, source_target_pairs={{0,2},{2,4},{4,6},{6,7},{7,5},{5,3},{3,1},{1,0},{8,10},{10,12},{12... | collective-permute-start | bytes 393224 | tf_op jit(solution)/shard_map/ppermute | solution.py:35
  9.5 7.7 %collective-permute-start.10 = (bf16[16,4096]{1,0:T(8,128)(2,1)S(1)}, bf16[16,4096]{1,0:T(8,128)(2,1)S(1)}, u32[]{:S(2)}, u32[]{:S(2)}) collective-permute-start(bf16[16,4096]{1,0:T(8,128)(2,1)S(1)} %collective-permute-done.8.refs_6_), channel_id=1, source_target_pairs={{2,0},{4,2},{6,4},{7,6},{5,7},{3,5},{1,3},{0,1},{10,8},{12,10},{14... | collective-permute-start | bytes 393224 | tf_op jit(solution)/shard_map/ppermute | solution.py:38
  11.4 6.7 %collective-permute-start.9 = (bf16[16,4096]{1,0:T(8,128)(2,1)S(1)}, bf16[16,4096]{1,0:T(8,128)(2,1)S(1)}, u32[]{:S(2)}, u32[]{:S(2)}) collective-permute-start(bf16[16,4096]{1,0:T(8,128)(2,1)S(1)} %collective-permute-done.7.refs_5_), channel_id=1, source_target_pairs={{0,2},{2,4},{4,6},{6,7},{7,5},{5,3},{3,1},{1,0},{8,10},{10,12},{12... | collective-permute-start | bytes 393224 | tf_op jit(solution)/shard_map/ppermute | solution.py:35
  15.6 5.0 %collective-permute-start.17 = (bf16[16,4096]{1,0:T(8,128)(2,1)S(1)}, bf16[16,4096]{1,0:T(8,128)(2,1)S(1)}, u32[]{:S(2)}, u32[]{:S(2)}) collective-permute-start(bf16[16,4096]{1,0:T(8,128)(2,1)S(1)} %collective-permute-done.15.refs_14_), channel_id=1, source_target_pairs={{2,0},{4,2},{6,4},{7,6},{5,7},{3,5},{1,3},{0,1},{10,8},{12,10},{14... | collective-permute-start | bytes 393224 | tf_op jit(solution)/shard_map/ppermute | solution.py:38
  17.2 38.2 %collective-permute-start.4 = (bf16[64,8192]{1,0:T(8,128)(2,1)}, bf16[64,8192]{1,0:T(8,128)(2,1)S(1)}, u32[]{:S(2)}, u32[]{:S(2)}) collective-permute-start(bf16[64,8192]{1,0:T(8,128)(2,1)} %bitcast.13), channel_id=1, source_target_pairs={{8,0},{0,8},{9,1},{1,9},{10,2},{2,10},{11,3},{3,11},{12,4},{4,12},... | collective-permute-start | bytes 3145736 | tf_op jit(solution)/shard_map/ppermute | solution.py:15
  18.1 37.3 %collective-permute-start.3 = (bf16[64,8192]{1,0:T(8,128)(2,1)}, bf16[64,8192]{1,0:T(8,128)(2,1)S(1)}, u32[]{:S(2)}, u32[]{:S(2)}) collective-permute-start(bf16[64,8192]{1,0:T(8,128)(2,1)} %bitcast.14), channel_id=1, source_target_pairs={{0,0},{8,8},{1,1},{9,9},{2,2},{10,10},{3,3},{11,11},{4,4},{12,12},... | collective-permute-start | bytes 3145736 | tf_op jit(solution)/shard_map/ppermute | solution.py:15
  20.6 5.0 %collective-permute-start.16 = (bf16[16,4096]{1,0:T(8,128)(2,1)S(1)}, bf16[16,4096]{1,0:T(8,128)(2,1)S(1)}, u32[]{:S(2)}, u32[]{:S(2)}) collective-permute-start(bf16[16,4096]{1,0:T(8,128)(2,1)S(1)} %collective-permute-done.14.refs_13_), channel_id=1, source_target_pairs={{0,2},{2,4},{4,6},{6,7},{7,5},{5,3},{3,1},{1,0},{8,10},{10,12},{12... | collective-permute-start | bytes 393224 | tf_op jit(solution)/shard_map/ppermute | solution.py:35
  25.6 5.0 %collective-permute-start.12 = (bf16[16,4096]{1,0:T(8,128)(2,1)S(1)}, bf16[16,4096]{1,0:T(8,128)(2,1)S(1)}, u32[]{:S(2)}, u32[]{:S(2)}) collective-permute-start(bf16[16,4096]{1,0:T(8,128)(2,1)S(1)} %collective-permute-done.10.refs_8_), channel_id=1, source_target_pairs={{2,0},{4,2},{6,4},{7,6},{5,7},{3,5},{1,3},{0,1},{10,8},{12,10},{14... | collective-permute-start | bytes 393224 | tf_op jit(solution)/shard_map/ppermute | solution.py:38
  30.5 5.0 %collective-permute-start.11 = (bf16[16,4096]{1,0:T(8,128)(2,1)S(1)}, bf16[16,4096]{1,0:T(8,128)(2,1)S(1)}, u32[]{:S(2)}, u32[]{:S(2)}) collective-permute-start(bf16[16,4096]{1,0:T(8,128)(2,1)S(1)} %collective-permute-done.9.refs_7_), channel_id=1, source_target_pairs={{0,2},{2,4},{4,6},{6,7},{7,5},{5,3},{3,1},{1,0},{8,10},{10,12},{12... | collective-permute-start | bytes 393224 | tf_op jit(solution)/shard_map/ppermute | solution.py:35
  35.5 5.0 %collective-permute-start.19 = (bf16[16,4096]{1,0:T(8,128)(2,1)S(1)}, bf16[16,4096]{1,0:T(8,128)(2,1)S(1)}, u32[]{:S(2)}, u32[]{:S(2)}) collective-permute-start(bf16[16,4096]{1,0:T(8,128)(2,1)S(1)} %collective-permute-done.17.refs_16_), channel_id=1, source_target_pairs={{2,0},{4,2},{6,4},{7,6},{5,7},{3,5},{1,3},{0,1},{10,8},{12,10},{14... | collective-permute-start | bytes 393224 | tf_op jit(solution)/shard_map/ppermute | solution.py:38
  40.5 5.0 %collective-permute-start.18 = (bf16[16,4096]{1,0:T(8,128)(2,1)S(1)}, bf16[16,4096]{1,0:T(8,128)(2,1)S(1)}, u32[]{:S(2)}, u32[]{:S(2)}) collective-permute-start(bf16[16,4096]{1,0:T(8,128)(2,1)S(1)} %collective-permute-done.16.refs_15_), channel_id=1, source_target_pairs={{0,2},{2,4},{4,6},{6,7},{7,5},{5,3},{3,1},{1,0},{8,10},{10,12},{12... | collective-permute-start | bytes 393224 | tf_op jit(solution)/shard_map/ppermute | solution.py:35
  45.5 5.0 %collective-permute-start.13 = (bf16[16,4096]{1,0:T(8,128)(2,1)S(1)}, bf16[16,4096]{1,0:T(8,128)(2,1)S(1)}, u32[]{:S(2)}, u32[]{:S(2)}) collective-permute-start(bf16[16,4096]{1,0:T(8,128)(2,1)S(1)} %collective-permute-done.11.refs_9_), channel_id=1, source_target_pairs={{0,2},{2,4},{4,6},{6,7},{7,5},{5,3},{3,1},{1,0},{8,10},{10,12},{12... | collective-permute-start | bytes 393224 | tf_op jit(solution)/shard_map/ppermute | solution.py:35
  50.4 5.0 %collective-permute-start.20 = (bf16[16,4096]{1,0:T(8,128)(2,1)S(1)}, bf16[16,4096]{1,0:T(8,128)(2,1)S(1)}, u32[]{:S(2)}, u32[]{:S(2)}) collective-permute-start(bf16[16,4096]{1,0:T(8,128)(2,1)S(1)} %collective-permute-done.19.refs_18_), channel_id=1, source_target_pairs={{2,0},{4,2},{6,4},{7,6},{5,7},{3,5},{1,3},{0,1},{10,8},{12,10},{14... | collective-permute-start | bytes 393224 | tf_op jit(solution)/shard_map/ppermute | solution.py:38
  58.4 16.6 %all-to-all-start = ((bf16[8,32,1280]{2,1,0:T(8,128)(2,1)}), bf16[8,32,1280]{2,1,0:T(8,128)(2,1)S(1)}, u32[]{:S(2)}, u32[]{:S(2)}) async-start(bf16[8,32,1280]{2,1,0:T(8,128)(2,1)} %get-tuple-element.16), calls=%async_computation | async-start | bytes 1310720 | tf_op jit(solution)/shard_map/all_to_all | solution.py:190

commit v14 on v13

--- a/solution.py
+++ b/solution.py
@@ -10,9 +10,11 @@
 adapter_scale = 1.0
 
 
-def fetched(x, axis="grp", shift=0):
+def swapped(x, axis):
     n = lax.axis_size(axis)
-    return lax.ppermute(x, axis, [((i + shift) % n, i) for i in range(n)])
+    return [x] + [
+        lax.ppermute(x, axis, [((i + s) % n, i) for i in range(n)]) for s in range(1, n)
+    ]
 
 
 def ring_of(n):
@@ -57,7 +59,17 @@
         out_ref[...] = block_ref[:, i * width : (i + 1) * width]
 
 
-def place_kernel(groups, tp, ids_ref, lengths_ref, slots_ref, row_ref, column_ref):
+def stack_kernel(groups, passed_ref, *refs):
+    downs, ups, (pass_ref, down_ref, up_ref) = refs[:groups], refs[groups:-3], refs[-3:]
+    pass_ref[...] = passed_ref[...]
+    rank = ups[0].shape[0]
+    down_ref[...] = jnp.concatenate([down[...] for down in downs], axis=0).T
+    for s, up in enumerate(ups):
+        up_ref[s * rank : (s + 1) * rank, :] = up[...]
+
+
+def place_kernel(groups, tp, ids_ref, lengths_ref, slots_ref, passed_ref, pass_ref, row_ref, column_ref):
+    pass_ref[...] = passed_ref[...]
     group = lax.axis_index("grp")
     longest = row_ref.shape[1] // 8
     along = lax.broadcasted_iota(jnp.int32, row_ref.shape, 1)
@@ -77,10 +89,9 @@
     _, row_ref[...], column_ref[...] = lax.fori_loop(0, ids_ref.shape[1], add, carry)
 
 
-def lift_kernel(groups, place_ref, *refs):
-    downs, ups, pieces = refs[:groups], refs[groups : 2 * groups], refs[2 * groups : -3]
-    tokens_ref, out_ref, up_ref = refs[-3:]
-    rank = ups[0].shape[0]
+def lift_kernel(groups, place_ref, down_ref, up_ref, *refs):
+    pieces, (tokens_ref, out_ref) = refs[:-2], refs[-2:]
+    rank = up_ref.shape[0] // groups
     rows, width = pieces[0].shape
     tok_all = tokens_ref.shape[0]
     parts, slots, columns = out_ref.shape
@@ -89,10 +100,7 @@
         start = pl.multiple_of(sources[i % len(sources)] * rows, rows)
         column = i // len(sources) * width
         tokens_ref[pl.ds(start, rows), column : column + width] = piece[...]
-    for s, up in enumerate(ups):
-        up_ref[s * rank : (s + 1) * rank, :] = up[...]
-    down = jnp.concatenate([down[...] for down in downs], axis=0).T
-    low = jnp.dot(tokens_ref[...], down, preferred_element_type=jnp.float32)
+    low = jnp.dot(tokens_ref[...], down_ref[...], preferred_element_type=jnp.float32)
     here = lax.broadcasted_iota(jnp.int32, (slots, tok_all), 0) + lax.axis_index("tp") * slots
     chosen = (here == place_ref[...]).astype(jnp.bfloat16)
     picked = jnp.dot(chosen, low.astype(jnp.bfloat16), preferred_element_type=jnp.float32)
@@ -144,31 +152,42 @@
         name="halve",
     )(tokens[0])
     rings = [Ring(part, "tp", k == 0) for k, part in enumerate(halves)]
-    for i in range(1, tp // 2 + 1):
-        for ring in rings:
-            ring.step(i)
-
-    pieces = rings[0].pieces + rings[1].pieces
-
-    panels = [
-        fetched(panel, shift=s)
-        for panel in (adapter_down_panels[0].T, adapter_up_panels[0])
-        for s in range(groups)
-    ]
-    requests = [
-        fetched(x) for x in (request_adapter_ids, request_token_lengths, adapter_store_slot)
-    ]
-    row, column = pl.pallas_call(
+    rings[0].step(1)
+    rings[1].step(1)
+    piece = jax.ShapeDtypeStruct(halves[0].shape, jnp.bfloat16)
+
+    panels = swapped(adapter_down_panels[0].T, "grp") + swapped(adapter_up_panels[0], "grp")
+    rings[1].ahead, down, up = pl.pallas_call(
+        functools.partial(stack_kernel, groups),
+        out_shape=[
+            piece,
+            jax.ShapeDtypeStruct((width, groups * rank), jnp.bfloat16),
+            jax.ShapeDtypeStruct((groups * rank, tp * columns), jnp.bfloat16),
+        ],
+        in_specs=[in_vmem] * (1 + len(panels)),
+        out_specs=[in_vmem] * 3,
+        compiler_params=small,
+        name="stack",
+    )(rings[1].ahead, *panels)
+    rings[0].step(2)
+    rings[1].step(2)
+
+    rings[0].ahead, row, column = pl.pallas_call(
         functools.partial(place_kernel, groups, tp),
         out_shape=[
+            piece,
             jax.ShapeDtypeStruct((1, tok_all), jnp.int32),
             jax.ShapeDtypeStruct((tok_all, 1), jnp.int32),
         ],
-        in_specs=[in_smem] * 3,
-        out_specs=[in_vmem] * 2,
+        in_specs=[in_smem] * 3 + [in_vmem],
+        out_specs=[in_vmem] * 3,
         compiler_params=small,
         name="place",
-    )(*requests)
+    )(request_adapter_ids, request_token_lengths, adapter_store_slot, rings[0].ahead)
+    for i in range(3, tp // 2 + 1):
+        for ring in rings:
+            ring.step(i)
+    pieces = rings[0].pieces + rings[1].pieces
 
     gathered, lifts = pl.pallas_call(
         functools.partial(lift_kernel, groups),
@@ -176,9 +195,8 @@
             jax.ShapeDtypeStruct((tok_all, width), jnp.bfloat16),
             jax.ShapeDtypeStruct((tp, here, columns), jnp.bfloat16),
         ],
-        in_specs=[in_vmem] * (1 + len(panels) + len(pieces)),
+        in_specs=[in_vmem] * (3 + len(pieces)),
         out_specs=[in_vmem] * 2,
-        scratch_shapes=[pltpu.VMEM((groups * rank, tp * columns), jnp.bfloat16)],
         compiler_params=pltpu.CompilerParams(vmem_limit_bytes=24 * 2**20),
         cost_estimate=pl.CostEstimate(
             flops=2 * groups * rank * (tok_all * width + here * tp * columns),
@@ -186,7 +204,7 @@
             transcendentals=0,
         ),
         name="lift",
-    )(row, *panels, *pieces)
+    )(row, down, up, *pieces)
     lifts = lax.all_to_all(lifts, "tp", split_axis=0, concat_axis=0, tiled=True)
 
     base = jnp.dot(gathered, base_projection_weight, preferred_element_type=jnp.float32)

time: 76.3 us -> 56.9 us (0.75)
  waiting for transfers between devices: 36.1 us -> 14.9 us
  local copies, waits for them, and re-layouts: 0.95 us -> 5.48 us
  starting transfers between devices: 25.3 us -> 22.5 us
    ppermute x7, waiting for transfers between devices: 22.4 us -> 9.43 us  [step(): self.ahead = lax.ppermute(self.ahead, self.axis, self.up)]
    ppermute x7, waiting for transfers between devices: 10.5 us -> 1.19 us  [step(): self.behind = lax.ppermute(self.behind, self.axis, self.down)]
    ppermute x7, starting transfers between devices: 2.81 us -> 8.81 us  [step(): self.ahead = lax.ppermute(self.ahead, self.axis, self.up)]
    ppermute x7, starting transfers between devices: 13.1 us -> 8.26 us  [step(): self.behind = lax.ppermute(self.behind, self.axis, self.down)]
    unnamed x2 -> x12, local copies, waits for them, and re-layouts: 0.95 us -> 5.48 us
    ppermute x7 -> x2, starting transfers between devices: 4.54 us -> 0.51 us  [swapped(): lax.ppermute(x, axis, [((i + s) % n, i) for i in range(n)])]
    all_to_all x1, waiting for transfers between devices: 3.15 us -> 4.32 us  [on_device(): lifts = lax.all_to_all(lifts, 'tp', split_axis=0, concat_axis=0, tiled=True)]
    pallas_call x1 -> x2, Pallas kernels: 0.96 us -> 1.69 us  [the longest x1 0.96 us: on_device(): pl.pallas_call(functools.partial(place_kernel, groups, tp), out_shape=[pi...]
  transfers between devices with their start and end apart: 22 -> 17, of which waited for: 11 -> 8; matrix products, arithmetic and copies ran while one was open for 11% -> 15% of each run, Pallas kernels for 1% -> 3%
where the time goes in v14:
time: 56.9 us; the launch traced here: 56.6 us
  starting transfers between devices  22.5 us (40%)
  waiting for transfers between devices  14.9 us (26%)
  matrix products  8.53 us (15%)
  local copies, waits for them, and re-layouts  5.48 us (10%)
  Pallas kernels  5.08 us (9%)
    ppermute x7, waiting for transfers between devices, step(): self.ahead = lax.ppermute(self.ahead, self.axis, self.up)  9.43 us
    ppermute x7, starting transfers between devices, step(): self.ahead = lax.ppermute(self.ahead, self.axis, self.up)  8.81 us
    dot_general x1, matrix products, on_device(): jnp.dot(gathered, base_projection_weight, preferred_element_type=jnp.floa...  8.53 us
    ppermute x7, starting transfers between devices, step(): self.behind = lax.ppermute(self.behind, self.axis, self.down)  8.26 us
    unnamed x12, local copies, waits for them, and re-layouts  5.48 us
    all_to_all x1, starting transfers between devices, on_device(): lifts = lax.all_to_all(lifts, 'tp', split_axis=0, concat_axis=0, tiled=True)  4.88 us
    all_to_all x1, waiting for transfers between devices, on_device(): lifts = lax.all_to_all(lifts, 'tp', split_axis=0, concat_axis=0, tiled=True)  4.32 us
    pallas_call x1, Pallas kernels, on_device(): pl.pallas_call(functools.partial(lift_kernel, groups), out_shape=[jax.Sha...  2.36 us
  transfers between devices with their start and end apart: 17, of which 8 were waited for; matrix products, arithmetic and copies ran while one was open for 15% of the time, Pallas kernels for 3%

profile of v14, /device:TPU:0, one launch (start us, length us, event | category | flops | bytes accessed | tf_op | source)
XLA Modules:
  0.0 56.6 jit_solution(5601403010105083556)
XLA Ops:
  0.5 0.9 %copy-done.2 = bf16[1,16,8192]{2,1,0:T(8,128)(2,1)S(1)} copy-done((bf16[1,16,8192]{2,1,0:T(8,128)(2,1)S(1)}, bf16[1,16,8192]{2,1,0:T(8,128)(2,1)}, u32[]{:S(2)}) %copy-start.2) | copy-done | bytes 262168
  1.5 3.1 %collective-permute-start = (bf16[16,4096]{1,0:T(8,128)(2,1)S(1)}, bf16[16,4096]{1,0:T(8,128)(2,1)S(1)}, u32[]{:S(2)}, u32[]{:S(2)}) collective-permute-start(bf16[16,4096]{1,0:T(8,128)(2,1)S(1)} %get-tuple-element.15.refs_0_), channel_id=1, source_target_pairs={{0,2},{2,4},{4,6},{6,7},{7,5},{5,3},{3,1},{1,0},{8,10},{10,12},{12... | collective-permute-start | bytes 393224 | tf_op jit(solution)/shard_map/ppermute | solution.py:37
  4.6 2.0 %collective-permute-start.10 = (bf16[16,4096]{1,0:T(8,128)(2,1)S(1)}, bf16[16,4096]{1,0:T(8,128)(2,1)S(1)}, u32[]{:S(2)}, u32[]{:S(2)}) collective-permute-start(bf16[16,4096]{1,0:T(8,128)(2,1)S(1)} %get-tuple-element.18.refs_8_), channel_id=1, source_target_pairs={{2,0},{4,2},{6,4},{7,6},{5,7},{3,5},{1,3},{0,1},{10,8},{12,10},{14... | collective-permute-start | bytes 393224 | tf_op jit(solution)/shard_map/ppermute | solution.py:40
  6.5 1.6 %collective-permute-done.refs_1_ = bf16[16,4096]{1,0:T(8,128)(2,1)S(1)} collective-permute-done((bf16[16,4096]{1,0:T(8,128)(2,1)S(1)}, bf16[16,4096]{1,0:T(8,128)(2,1)S(1)}, u32[]{:S(2)}, u32[]{:S(2)}) %collective-permute-start) | collective-permute-done | bytes 131104 | tf_op jit(solution)/shard_map/ppermute | solution.py:37
  8.2 1.8 %collective-permute-start.1 = (bf16[16,4096]{1,0:T(8,128)(2,1)S(1)}, bf16[16,4096]{1,0:T(8,128)(2,1)S(1)}, u32[]{:S(2)}, u32[]{:S(2)}) collective-permute-start(bf16[16,4096]{1,0:T(8,128)(2,1)S(1)} %collective-permute-done.refs_1_), channel_id=1, source_target_pairs={{0,2},{2,4},{4,6},{6,7},{7,5},{5,3},{3,1},{1,0},{8,10},{10,12},{12... | collective-permute-start | bytes 393224 | tf_op jit(solution)/shard_map/ppermute | solution.py:37
  10.0 1.0 %collective-permute-done.5.refs_2_ = bf16[16,4096]{1,0:T(8,128)(2,1)S(1)} collective-permute-done((bf16[16,4096]{1,0:T(8,128)(2,1)S(1)}, bf16[16,4096]{1,0:T(8,128)(2,1)S(1)}, u32[]{:S(2)}, u32[]{:S(2)}) %collective-permute-start.5) | collective-permute-done | bytes 131104 | tf_op jit(solution)/shard_map/ppermute | solution.py:40
  11.0 1.6 %collective-permute-start.2 = (bf16[16,4096]{1,0:T(8,128)(2,1)S(1)}, bf16[16,4096]{1,0:T(8,128)(2,1)S(1)}, u32[]{:S(2)}, u32[]{:S(2)}) collective-permute-start(bf16[16,4096]{1,0:T(8,128)(2,1)S(1)} %get-tuple-element.18.refs_8_), channel_id=1, source_target_pairs={{0,2},{2,4},{4,6},{6,7},{7,5},{5,3},{3,1},{1,0},{8,10},{10,12},{12... | collective-permute-start | bytes 393224 | tf_op jit(solution)/shard_map/ppermute | solution.py:37
  13.0 1.4 %collective-permute-done.1.passed_ref.refs_3_ = bf16[16,4096]{1,0:T(8,128)(2,1)S(1)} collective-permute-done((bf16[16,4096]{1,0:T(8,128)(2,1)S(1)}, bf16[16,4096]{1,0:T(8,128)(2,1)S(1)}, u32[]{:S(2)}, u32[]{:S(2)}) %collective-permute-start.1) | collective-permute-done | bytes 131104 | tf_op jit(solution)/shard_map/ppermute | solution.py:37
  14.4 1.4 %collective-permute-start.6 = (bf16[16,4096]{1,0:T(8,128)(2,1)S(1)}, bf16[16,4096]{1,0:T(8,128)(2,1)S(1)}, u32[]{:S(2)}, u32[]{:S(2)}) collective-permute-start(bf16[16,4096]{1,0:T(8,128)(2,1)S(1)} %collective-permute-done.5.refs_2_), channel_id=1, source_target_pairs={{2,0},{4,2},{6,4},{7,6},{5,7},{3,5},{1,3},{0,1},{10,8},{12,10},{14... | collective-permute-start | bytes 393224 | tf_op jit(solution)/shard_map/ppermute | solution.py:40
  17.9 1.0 %place.1 = (bf16[16,4096]{1,0:T(8,128)(2,1)S(1)}, s32[1,128]{1,0:T(1,128)S(1)}, s32[128,1]{1,0:T(8,128)S(1)}) custom-call(s32[2,12]{1,0:T(2,128)S(1)} %copy-done.3, s32[1,12]{1,0:T(1,128)S(1)} %copy-done.4, s32[16]{0:T(128)S(1)} %copy-done.5, bf16[16,4096]{1,0:T(8,128)(2,1)S(1)} %collective-permute-done.1.passed_ref.refs_3_), custom_call_target="tpu_custom_call" | custom-call | tf_op jit(solution)/shard_map/place/pallas_call | solution.py:175
  19.5 1.4 %collective-permute-start.14 = (bf16[16,4096]{1,0:T(8,128)(2,1)S(1)}, bf16[16,4096]{1,0:T(8,128)(2,1)S(1)}, u32[]{:S(2)}, u32[]{:S(2)}) collective-permute-start(bf16[16,4096]{1,0:T(8,128)(2,1)S(1)} %collective-permute-done.12.refs_12_), channel_id=1, source_target_pairs={{2,0},{4,2},{6,4},{7,6},{5,7},{3,5},{1,3},{0,1},{10,8},{12,10},{14... | collective-permute-start | bytes 393224 | tf_op jit(solution)/shard_map/ppermute | solution.py:40
  20.9 1.3 %copy-done = bf16[1,64,10240]{2,1,0:T(8,128)(2,1)S(1)} copy-done((bf16[1,64,10240]{2,1,0:T(8,128)(2,1)S(1)}, bf16[1,64,10240]{2,1,0:T(8,128)(2,1)}, u32[]{:S(2)}) %copy-start) | copy-done | bytes 1310744
  22.2 1.2 %copy-done.1 = bf16[1,8192,64]{1,2,0:T(8,128)(2,1)S(1)} copy-done((bf16[1,8192,64]{1,2,0:T(8,128)(2,1)S(1)}, bf16[1,8192,64]{1,2,0:T(8,128)(2,1)}, u32[]{:S(2)}) %copy-start.1) | copy-done | bytes 1048600
  23.5 0.7 %stack.1 = (bf16[16,4096]{1,0:T(8,128)(2,1)S(1)}, bf16[8192,128]{1,0:T(8,128)(2,1)S(1)}, bf16[128,10240]{1,0:T(8,128)(2,1)S(1)}) custom-call(bf16[16,4096]{1,0:T(8,128)(2,1)S(1)} %collective-permute-done.2.passed_ref.refs_9_, bf16[64,8192]{1,0:T(8,128)(2,1)S(1)} %bitcast.13, bf16[64,8192]{1,0:T(8,128)(2,1)S(1)} %collective-permute-done.3.refs_1_, ...), custom_call_target="tpu_custom_call" | custom-call | tf_op jit(solution)/shard_map/stack/pallas_call | solution.py:160
  24.9 1.4 %collective-permute-start.8 = (bf16[16,4096]{1,0:T(8,128)(2,1)S(1)}, bf16[16,4096]{1,0:T(8,128)(2,1)S(1)}, u32[]{:S(2)}, u32[]{:S(2)}) collective-permute-start(bf16[16,4096]{1,0:T(8,128)(2,1)S(1)} %collective-permute-done.6.refs_4_), channel_id=1, source_target_pairs={{2,0},{4,2},{6,4},{7,6},{5,7},{3,5},{1,3},{0,1},{10,8},{12,10},{14... | collective-permute-start | bytes 393224 | tf_op jit(solution)/shard_map/ppermute | solution.py:40
  26.3 1.6 %collective-permute-start.15 = (bf16[16,4096]{1,0:T(8,128)(2,1)S(1)}, bf16[16,4096]{1,0:T(8,128)(2,1)S(1)}, u32[]{:S(2)}, u32[]{:S(2)}) collective-permute-start(bf16[16,4096]{1,0:T(8,128)(2,1)S(1)} %collective-permute-done.14.refs_14_), channel_id=1, source_target_pairs={{2,0},{4,2},{6,4},{7,6},{5,7},{3,5},{1,3},{0,1},{10,8},{12,10},{14... | collective-permute-start | bytes 393224 | tf_op jit(solution)/shard_map/ppermute | solution.py:40
  28.3 2.2 %collective-permute-done.11.refs_11_ = bf16[16,4096]{1,0:T(8,128)(2,1)S(1)} collective-permute-done((bf16[16,4096]{1,0:T(8,128)(2,1)S(1)}, bf16[16,4096]{1,0:T(8,128)(2,1)S(1)}, u32[]{:S(2)}, u32[]{:S(2)}) %collective-permute-start.11) | collective-permute-done | bytes 131104 | tf_op jit(solution)/shard_map/ppermute | solution.py:37
  31.3 1.6 %collective-permute-done.9.refs_7_ = bf16[16,4096]{1,0:T(8,128)(2,1)S(1)} collective-permute-done((bf16[16,4096]{1,0:T(8,128)(2,1)S(1)}, bf16[16,4096]{1,0:T(8,128)(2,1)S(1)}, u32[]{:S(2)}, u32[]{:S(2)}) %collective-permute-start.9) | collective-permute-done | bytes 131104 | tf_op jit(solution)/shard_map/ppermute | solution.py:37
  32.8 2.6 %collective-permute-done.13.refs_13_ = bf16[16,4096]{1,0:T(8,128)(2,1)S(1)} collective-permute-done((bf16[16,4096]{1,0:T(8,128)(2,1)S(1)}, bf16[16,4096]{1,0:T(8,128)(2,1)S(1)}, u32[]{:S(2)}, u32[]{:S(2)}) %collective-permute-start.13) | collective-permute-done | bytes 131104 | tf_op jit(solution)/shard_map/ppermute | solution.py:37
  35.4 2.4 %lift.1 = (bf16[128,8192]{1,0:T(8,128)(2,1)S(1)}, bf16[8,32,1280]{2,1,0:T(8,128)(2,1)}) custom-call(s32[1,128]{1,0:T(1,128)S(1)} %get-tuple-element.17.place_ref, bf16[8192,128]{1,0:T(8,128)(2,1)S(1)} %get-tuple-element.19.down_ref, bf16[128,10240]{1,0:T(8,128)(2,1)S(1)} %get-tuple-element.20.up_ref, bf16[16,4096]{1,0:T(8,128)(2,1)S(1)} %get-tuple-element.15.refs_0_, ...), custom_call_target="tpu_custom_call" | custom-call | flops 352321536 | bytes 4718592 | tf_op jit(solution)/shard_map/lift/pallas_call | solution.py:192
  37.8 4.9 %all-to-all-start = ((bf16[8,32,1280]{2,1,0:T(8,128)(2,1)}), bf16[8,32,1280]{2,1,0:T(8,128)(2,1)S(1)}, u32[]{:S(2)}, u32[]{:S(2)}) async-start(bf16[8,32,1280]{2,1,0:T(8,128)(2,1)} %get-tuple-element.24), calls=%async_computation | async-start | bytes 1310720 | tf_op jit(solution)/shard_map/all_to_all | solution.py:208
  42.7 8.5 %fusion.base_ref = f32[128,1280]{1,0:T(8,128)S(1)} fusion(bf16[128,8192]{1,0:T(8,128)(2,1)S(1)} %get-tuple-element.23, bf16[8192,1280]{1,0:T(8,128)(2,1)} %param.8), kind=kOutput, calls=%fused_computation | convolution fusion | flops 2684354560 | bytes 23724032 | tf_op jit(solution)/shard_map/dot_general | solution.py:210
  51.2 4.3 %all-to-all-done = bf16[8,32,1280]{2,1,0:T(8,128)(2,1)S(1)} async-done(((bf16[8,32,1280]{2,1,0:T(8,128)(2,1)}), bf16[8,32,1280]{2,1,0:T(8,128)(2,1)S(1)}, u32[]{:S(2)}, u32[]{:S(2)}) %all-to-all-start) | async-done | bytes 655392 | tf_op jit(solution)/shard_map/all_to_all | solution.py:208
  55.5 1.0 %add.1 = bf16[128,1280]{1,0:T(8,128)(2,1)} custom-call(s32[128,1]{1,0:T(8,128)S(1)} %get-tuple-element.16.place_ref, f32[128,1280]{1,0:T(8,128)S(1)} %fusion.base_ref, bf16[256,1280]{1,0:T(8,128)(2,1)S(1)} %bitcast.9), custom_call_target="tpu_custom_call" | custom-call | tf_op jit(solution)/shard_map/add/pallas_call | solution.py:211
  (28 shorter events, 5.5 us)
Async XLA Ops:
  0.0 20.9 %collective-permute-start.4 = (bf16[64,10240]{1,0:T(8,128)(2,1)}, bf16[64,10240]{1,0:T(8,128)(2,1)S(1)}, u32[]{:S(2)}, u32[]{:S(2)}) collective-permute-start(bf16[64,10240]{1,0:T(8,128)(2,1)} %bitcast.10), channel_id=1, source_target_pairs={{8,0},{0,8},{9,1},{1,9},{10,2},{2,10},{11,3},{3,11},{12,4},{4,12},... | collective-permute-start | bytes 3932168 | tf_op jit(solution)/shard_map/ppermute | solution.py:16
  0.5 20.5 %collective-permute-start.3 = (bf16[64,8192]{1,0:T(8,128)(2,1)}, bf16[64,8192]{1,0:T(8,128)(2,1)S(1)}, u32[]{:S(2)}, u32[]{:S(2)}) collective-permute-start(bf16[64,8192]{1,0:T(8,128)(2,1)} %bitcast.12), channel_id=1, source_target_pairs={{8,0},{0,8},{9,1},{1,9},{10,2},{2,10},{11,3},{3,11},{12,4},{4,12},... | collective-permute-start | bytes 3145736 | tf_op jit(solution)/shard_map/ppermute | solution.py:16
  0.5 0.9 %copy-start.2 = (bf16[1,16,8192]{2,1,0:T(8,128)(2,1)S(1)}, bf16[1,16,8192]{2,1,0:T(8,128)(2,1)}, u32[]{:S(2)}) copy-start(bf16[1,16,8192]{2,1,0:T(8,128)(2,1)} %param.7) | copy-start | bytes 786436
  1.5 6.7 %collective-permute-start = (bf16[16,4096]{1,0:T(8,128)(2,1)S(1)}, bf16[16,4096]{1,0:T(8,128)(2,1)S(1)}, u32[]{:S(2)}, u32[]{:S(2)}) collective-permute-start(bf16[16,4096]{1,0:T(8,128)(2,1)S(1)} %get-tuple-element.15.refs_0_), channel_id=1, source_target_pairs={{0,2},{2,4},{4,6},{6,7},{7,5},{5,3},{3,1},{1,0},{8,10},{10,12},{12... | collective-permute-start | bytes 393224 | tf_op jit(solution)/shard_map/ppermute | solution.py:37
  4.6 6.4 %collective-permute-start.5 = (bf16[16,4096]{1,0:T(8,128)(2,1)S(1)}, bf16[16,4096]{1,0:T(8,128)(2,1)S(1)}, u32[]{:S(2)}, u32[]{:S(2)}) collective-permute-start(bf16[16,4096]{1,0:T(8,128)(2,1)S(1)} %get-tuple-element.15.refs_0_), channel_id=1, source_target_pairs={{2,0},{4,2},{6,4},{7,6},{5,7},{3,5},{1,3},{0,1},{10,8},{12,10},{14... | collective-permute-start | bytes 393224 | tf_op jit(solution)/shard_map/ppermute | solution.py:40
  4.6 8.0 %collective-permute-start.10 = (bf16[16,4096]{1,0:T(8,128)(2,1)S(1)}, bf16[16,4096]{1,0:T(8,128)(2,1)S(1)}, u32[]{:S(2)}, u32[]{:S(2)}) collective-permute-start(bf16[16,4096]{1,0:T(8,128)(2,1)S(1)} %get-tuple-element.18.refs_8_), channel_id=1, source_target_pairs={{2,0},{4,2},{6,4},{7,6},{5,7},{3,5},{1,3},{0,1},{10,8},{12,10},{14... | collective-permute-start | bytes 393224 | tf_op jit(solution)/shard_map/ppermute | solution.py:40
  8.2 6.3 %collective-permute-start.1 = (bf16[16,4096]{1,0:T(8,128)(2,1)S(1)}, bf16[16,4096]{1,0:T(8,128)(2,1)S(1)}, u32[]{:S(2)}, u32[]{:S(2)}) collective-permute-start(bf16[16,4096]{1,0:T(8,128)(2,1)S(1)} %collective-permute-done.refs_1_), channel_id=1, source_target_pairs={{0,2},{2,4},{4,6},{6,7},{7,5},{5,3},{3,1},{1,0},{8,10},{10,12},{12... | collective-permute-start | bytes 393224 | tf_op jit(solution)/shard_map/ppermute | solution.py:37
  11.0 7.9 %collective-permute-start.2 = (bf16[16,4096]{1,0:T(8,128)(2,1)S(1)}, bf16[16,4096]{1,0:T(8,128)(2,1)S(1)}, u32[]{:S(2)}, u32[]{:S(2)}) collective-permute-start(bf16[16,4096]{1,0:T(8,128)(2,1)S(1)} %get-tuple-element.18.refs_8_), channel_id=1, source_target_pairs={{0,2},{2,4},{4,6},{6,7},{7,5},{5,3},{3,1},{1,0},{8,10},{10,12},{12... | collective-permute-start | bytes 393224 | tf_op jit(solution)/shard_map/ppermute | solution.py:37
  12.5 6.9 %collective-permute-start.12 = (bf16[16,4096]{1,0:T(8,128)(2,1)S(1)}, bf16[16,4096]{1,0:T(8,128)(2,1)S(1)}, u32[]{:S(2)}, u32[]{:S(2)}) collective-permute-start(bf16[16,4096]{1,0:T(8,128)(2,1)S(1)} %collective-permute-done.10.refs_10_), channel_id=1, source_target_pairs={{2,0},{4,2},{6,4},{7,6},{5,7},{3,5},{1,3},{0,1},{10,8},{12,10},{14... | collective-permute-start | bytes 393224 | tf_op jit(solution)/shard_map/ppermute | solution.py:40
  14.4 10.4 %collective-permute-start.6 = (bf16[16,4096]{1,0:T(8,128)(2,1)S(1)}, bf16[16,4096]{1,0:T(8,128)(2,1)S(1)}, u32[]{:S(2)}, u32[]{:S(2)}) collective-permute-start(bf16[16,4096]{1,0:T(8,128)(2,1)S(1)} %collective-permute-done.5.refs_2_), channel_id=1, source_target_pairs={{2,0},{4,2},{6,4},{7,6},{5,7},{3,5},{1,3},{0,1},{10,8},{12,10},{14... | collective-permute-start | bytes 393224 | tf_op jit(solution)/shard_map/ppermute | solution.py:40
  15.9 0.7 %copy-start.3 = (s32[2,12]{1,0:T(2,128)S(1)}, s32[2,12]{1,0:T(2,128)}, u32[]{:S(2)}) copy-start(s32[2,12]{1,0:T(2,128)} %ids_ref.1) | copy-start | bytes 292
  16.5 0.7 %copy-start.4 = (s32[1,12]{1,0:T(1,128)S(1)}, s32[1,12]{1,0:T(1,128)}, u32[]{:S(2)}) copy-start(s32[1,12]{1,0:T(1,128)} %lengths_ref.1) | copy-start | bytes 148
  17.2 0.7 %copy-start.5 = (s32[16]{0:T(128)S(1)}, s32[16]{0:T(128)}, u32[]{:S(2)}) copy-start(s32[16]{0:T(128)} %slots_ref.1) | copy-start | bytes 196
  18.8 9.0 %collective-permute-start.7 = (bf16[16,4096]{1,0:T(8,128)(2,1)S(1)}, bf16[16,4096]{1,0:T(8,128)(2,1)S(1)}, u32[]{:S(2)}, u32[]{:S(2)}) collective-permute-start(bf16[16,4096]{1,0:T(8,128)(2,1)S(1)} %get-tuple-element.21), channel_id=1, source_target_pairs={{0,2},{2,4},{4,6},{6,7},{7,5},{5,3},{3,1},{1,0},{8,10},{10,12},{12... | collective-permute-start | bytes 393224 | tf_op jit(solution)/shard_map/ppermute | solution.py:37
  19.5 6.8 %collective-permute-start.14 = (bf16[16,4096]{1,0:T(8,128)(2,1)S(1)}, bf16[16,4096]{1,0:T(8,128)(2,1)S(1)}, u32[]{:S(2)}, u32[]{:S(2)}) collective-permute-start(bf16[16,4096]{1,0:T(8,128)(2,1)S(1)} %collective-permute-done.12.refs_12_), channel_id=1, source_target_pairs={{2,0},{4,2},{6,4},{7,6},{5,7},{3,5},{1,3},{0,1},{10,8},{12,10},{14... | collective-permute-start | bytes 393224 | tf_op jit(solution)/shard_map/ppermute | solution.py:40
  20.9 1.3 %copy-start = (bf16[1,64,10240]{2,1,0:T(8,128)(2,1)S(1)}, bf16[1,64,10240]{2,1,0:T(8,128)(2,1)}, u32[]{:S(2)}) copy-start(bf16[1,64,10240]{2,1,0:T(8,128)(2,1)} %param.10) | copy-start | bytes 3932164
  22.2 1.2 %copy-start.1 = (bf16[1,8192,64]{1,2,0:T(8,128)(2,1)S(1)}, bf16[1,8192,64]{1,2,0:T(8,128)(2,1)}, u32[]{:S(2)}) copy-start(bf16[1,8192,64]{1,2,0:T(8,128)(2,1)} %param.9) | copy-start | bytes 3145732
  24.2 6.3 %collective-permute-start.11 = (bf16[16,4096]{1,0:T(8,128)(2,1)S(1)}, bf16[16,4096]{1,0:T(8,128)(2,1)S(1)}, u32[]{:S(2)}, u32[]{:S(2)}) collective-permute-start(bf16[16,4096]{1,0:T(8,128)(2,1)S(1)} %get-tuple-element.22), channel_id=1, source_target_pairs={{0,2},{2,4},{4,6},{6,7},{7,5},{5,3},{3,1},{1,0},{8,10},{10,12},{12... | collective-permute-start | bytes 393224 | tf_op jit(solution)/shard_map/ppermute | solution.py:37
  24.9 6.2 %collective-permute-start.8 = (bf16[16,4096]{1,0:T(8,128)(2,1)S(1)}, bf16[16,4096]{1,0:T(8,128)(2,1)S(1)}, u32[]{:S(2)}, u32[]{:S(2)}) collective-permute-start(bf16[16,4096]{1,0:T(8,128)(2,1)S(1)} %collective-permute-done.6.refs_4_), channel_id=1, source_target_pairs={{2,0},{4,2},{6,4},{7,6},{5,7},{3,5},{1,3},{0,1},{10,8},{12,10},{14... | collective-permute-start | bytes 393224 | tf_op jit(solution)/shard_map/ppermute | solution.py:40
  26.3 5.0 %collective-permute-start.15 = (bf16[16,4096]{1,0:T(8,128)(2,1)S(1)}, bf16[16,4096]{1,0:T(8,128)(2,1)S(1)}, u32[]{:S(2)}, u32[]{:S(2)}) collective-permute-start(bf16[16,4096]{1,0:T(8,128)(2,1)S(1)} %collective-permute-done.14.refs_14_), channel_id=1, source_target_pairs={{2,0},{4,2},{6,4},{7,6},{5,7},{3,5},{1,3},{0,1},{10,8},{12,10},{14... | collective-permute-start | bytes 393224 | tf_op jit(solution)/shard_map/ppermute | solution.py:40
  27.9 5.0 %collective-permute-start.9 = (bf16[16,4096]{1,0:T(8,128)(2,1)S(1)}, bf16[16,4096]{1,0:T(8,128)(2,1)S(1)}, u32[]{:S(2)}, u32[]{:S(2)}) collective-permute-start(bf16[16,4096]{1,0:T(8,128)(2,1)S(1)} %collective-permute-done.7.refs_5_), channel_id=1, source_target_pairs={{0,2},{2,4},{4,6},{6,7},{7,5},{5,3},{3,1},{1,0},{8,10},{10,12},{12... | collective-permute-start | bytes 393224 | tf_op jit(solution)/shard_map/ppermute | solution.py:37
  30.5 5.0 %collective-permute-start.13 = (bf16[16,4096]{1,0:T(8,128)(2,1)S(1)}, bf16[16,4096]{1,0:T(8,128)(2,1)S(1)}, u32[]{:S(2)}, u32[]{:S(2)}) collective-permute-start(bf16[16,4096]{1,0:T(8,128)(2,1)S(1)} %collective-permute-done.11.refs_11_), channel_id=1, source_target_pairs={{0,2},{2,4},{4,6},{6,7},{7,5},{5,3},{3,1},{1,0},{8,10},{10,12},{12... | collective-permute-start | bytes 393224 | tf_op jit(solution)/shard_map/ppermute | solution.py:37
  37.8 17.7 %all-to-all-start = ((bf16[8,32,1280]{2,1,0:T(8,128)(2,1)}), bf16[8,32,1280]{2,1,0:T(8,128)(2,1)S(1)}, u32[]{:S(2)}, u32[]{:S(2)}) async-start(bf16[8,32,1280]{2,1,0:T(8,128)(2,1)} %get-tuple-element.24), calls=%async_computation | async-start | bytes 1310720 | tf_op jit(solution)/shard_map/all_to_all | solution.py:208

commit v15 on v14

--- a/solution.py
+++ b/solution.py
@@ -21,31 +21,48 @@
     return list(range(0, n, 2)) + list(range(1, n, 2))[::-1]
 
 
-class Ring:
-    def __init__(self, block, axis, last_from_behind):
-        n = lax.axis_size(axis)
-        ring = ring_of(n)
-        self.n, self.axis, self.last_from_behind = n, axis, last_from_behind
-        self.up = [(ring[i], ring[(i + 1) % n]) for i in range(n)]
-        self.down = [(ring[(i + 1) % n], ring[i]) for i in range(n)]
-        self.ahead = self.behind = block
-        self.pieces = [block]
-
-    def step(self, i):
-        last = i == self.n // 2
-        if not last or self.last_from_behind:
-            self.ahead = lax.ppermute(self.ahead, self.axis, self.up)
-            self.pieces.append(self.ahead)
-        if not last or not self.last_from_behind:
-            self.behind = lax.ppermute(self.behind, self.axis, self.down)
-            self.pieces.append(self.behind)
+def ring_gather(block, axis, ahead_of_third, ahead_of_last):
+    n = lax.axis_size(axis)
+    ring = ring_of(n)
+    up = [(ring[i], ring[(i + 1) % n]) for i in range(n)]
+    down = [(ring[(i + 1) % n], ring[i]) for i in range(n)]
+    ahead = behind = block
+    pieces = [block]
+    for step in range(1, n // 2 + 1):
+        if step == n // 2:
+            ahead, behind = handed_on((ahead, behind), ahead_of_last, block.shape[1] // 2)
+        elif step == 3:
+            ahead, behind = handed_on((ahead, behind), ahead_of_third, block.shape[1])
+        ahead, behind = lax.ppermute(ahead, axis, up), lax.ppermute(behind, axis, down)
+        pieces += [ahead, behind]
+    return pieces
+
+
+def pass_kernel(waits, *refs):
+    n = (len(refs) - waits) // 2
+    for source, target in zip(refs[:n], refs[-n:]):
+        width = target.shape[1]
+        start = 0 if source is refs[0] else source.shape[1] - width
+        target[...] = source[:, start : start + width]
+
+
+def handed_on(arrays, values, width):
+    in_vmem = pl.BlockSpec(memory_space=pltpu.VMEM)
+    return pl.pallas_call(
+        functools.partial(pass_kernel, len(values)),
+        out_shape=[jax.ShapeDtypeStruct((x.shape[0], width), x.dtype) for x in arrays],
+        in_specs=[in_vmem] * len(arrays) + [pl.BlockSpec(memory_space=pl.ANY)] * len(values),
+        out_specs=[in_vmem] * len(arrays),
+        compiler_params=pltpu.CompilerParams(vmem_limit_bytes=16 * 2**20),
+        name="pass",
+    )(*arrays, *values)
 
 
 def ring_sources(axis):
     n = lax.axis_size(axis)
     me = lax.axis_index(axis)
     place = jnp.where(lax.rem(me, 2) == 0, me // 2, n - 1 - me // 2)
-    distances = [0] + [d for i in range(1, n // 2) for d in (i, -i)] + [n // 2]
+    distances = [0] + [d for i in range(1, n // 2) for d in (i, -i)] + [n // 2] * 2
     sources = []
     for distance in distances:
         at = lax.rem(place - distance + n, n)
@@ -53,23 +70,15 @@
     return sources
 
 
-def halve_kernel(block_ref, *out_refs):
-    width = out_refs[0].shape[1]
-    for i, out_ref in enumerate(out_refs):
-        out_ref[...] = block_ref[:, i * width : (i + 1) * width]
-
-
-def stack_kernel(groups, passed_ref, *refs):
-    downs, ups, (pass_ref, down_ref, up_ref) = refs[:groups], refs[groups:-3], refs[-3:]
-    pass_ref[...] = passed_ref[...]
+def stack_kernel(groups, *refs):
+    downs, ups, (down_ref, up_ref) = refs[:groups], refs[groups:-2], refs[-2:]
     rank = ups[0].shape[0]
     down_ref[...] = jnp.concatenate([down[...] for down in downs], axis=0).T
     for s, up in enumerate(ups):
         up_ref[s * rank : (s + 1) * rank, :] = up[...]
 
 
-def place_kernel(groups, tp, ids_ref, lengths_ref, slots_ref, passed_ref, pass_ref, row_ref, column_ref):
-    pass_ref[...] = passed_ref[...]
+def place_kernel(groups, tp, ids_ref, lengths_ref, slots_ref, row_ref, column_ref):
     group = lax.axis_index("grp")
     longest = row_ref.shape[1] // 8
     along = lax.broadcasted_iota(jnp.int32, row_ref.shape, 1)
@@ -92,14 +101,14 @@
 def lift_kernel(groups, place_ref, down_ref, up_ref, *refs):
     pieces, (tokens_ref, out_ref) = refs[:-2], refs[-2:]
     rank = up_ref.shape[0] // groups
-    rows, width = pieces[0].shape
+    rows = pieces[0].shape[0]
     tok_all = tokens_ref.shape[0]
     parts, slots, columns = out_ref.shape
-    sources = ring_sources("tp")
-    for i, piece in enumerate(pieces):
-        start = pl.multiple_of(sources[i % len(sources)] * rows, rows)
-        column = i // len(sources) * width
-        tokens_ref[pl.ds(start, rows), column : column + width] = piece[...]
+    for i, (piece, source) in enumerate(zip(pieces, ring_sources("tp"))):
+        start = pl.multiple_of(source * rows, rows)
+        size = piece.shape[1]
+        column = tokens_ref.shape[1] - size if i == len(pieces) - 1 else 0
+        tokens_ref[pl.ds(start, rows), column : column + size] = piece[...]
     low = jnp.dot(tokens_ref[...], down_ref[...], preferred_element_type=jnp.float32)
     here = lax.broadcasted_iota(jnp.int32, (slots, tok_all), 0) + lax.axis_index("tp") * slots
     chosen = (here == place_ref[...]).astype(jnp.bfloat16)
@@ -138,56 +147,34 @@
     tok_all = tokens.shape[1] * tp
     longest = tok_all // 8
     here = groups * longest
-    half = width // 2
     in_vmem = pl.BlockSpec(memory_space=pltpu.VMEM)
     in_smem = pl.BlockSpec(memory_space=pltpu.SMEM)
     small = pltpu.CompilerParams(vmem_limit_bytes=16 * 2**20)
 
-    halves = pl.pallas_call(
-        halve_kernel,
-        out_shape=[jax.ShapeDtypeStruct((tokens.shape[1], half), jnp.bfloat16)] * 2,
-        in_specs=[in_vmem],
-        out_specs=[in_vmem] * 2,
-        compiler_params=small,
-        name="halve",
-    )(tokens[0])
-    rings = [Ring(part, "tp", k == 0) for k, part in enumerate(halves)]
-    rings[0].step(1)
-    rings[1].step(1)
-    piece = jax.ShapeDtypeStruct(halves[0].shape, jnp.bfloat16)
-
     panels = swapped(adapter_down_panels[0].T, "grp") + swapped(adapter_up_panels[0], "grp")
-    rings[1].ahead, down, up = pl.pallas_call(
+    down, up = pl.pallas_call(
         functools.partial(stack_kernel, groups),
         out_shape=[
-            piece,
             jax.ShapeDtypeStruct((width, groups * rank), jnp.bfloat16),
             jax.ShapeDtypeStruct((groups * rank, tp * columns), jnp.bfloat16),
         ],
-        in_specs=[in_vmem] * (1 + len(panels)),
-        out_specs=[in_vmem] * 3,
+        in_specs=[in_vmem] * len(panels),
+        out_specs=[in_vmem] * 2,
         compiler_params=small,
         name="stack",
-    )(rings[1].ahead, *panels)
-    rings[0].step(2)
-    rings[1].step(2)
-
-    rings[0].ahead, row, column = pl.pallas_call(
+    )(*panels)
+    row, column = pl.pallas_call(
         functools.partial(place_kernel, groups, tp),
         out_shape=[
-            piece,
             jax.ShapeDtypeStruct((1, tok_all), jnp.int32),
             jax.ShapeDtypeStruct((tok_all, 1), jnp.int32),
         ],
-        in_specs=[in_smem] * 3 + [in_vmem],
-        out_specs=[in_vmem] * 3,
+        in_specs=[in_smem] * 3,
+        out_specs=[in_vmem] * 2,
         compiler_params=small,
         name="place",
-    )(request_adapter_ids, request_token_lengths, adapter_store_slot, rings[0].ahead)
-    for i in range(3, tp // 2 + 1):
-        for ring in rings:
-            ring.step(i)
-    pieces = rings[0].pieces + rings[1].pieces
+    )(request_adapter_ids, request_token_lengths, adapter_store_slot)
+    pieces = ring_gather(tokens[0], "tp", (down, up), (row, column))
 
     gathered, lifts = pl.pallas_call(
         functools.partial(lift_kernel, groups),

time: 56.9 us -> 54.1 us (0.951)
  waiting for transfers between devices: 14.9 us -> 22.6 us
  starting transfers between devices: 22.5 us -> 15 us
  local copies, waits for them, and re-layouts: 5.48 us -> 2.55 us
    ppermute x14 -> x8, waiting for transfers between devices: 10.6 us -> 18.5 us  [the longest x4 11.1 us: ring_gather(): lax.ppermute(behind, axis, down)]
    ppermute x14 -> x8, starting transfers between devices: 17.1 us -> 9.21 us  [the longest x4 6.62 us: ring_gather(): lax.ppermute(behind, axis, down)]
    unnamed x12, local copies, waits for them, and re-layouts: 5.48 us -> 2.55 us
    pallas_call x3 -> x4, Pallas kernels: 1.7 us -> 1.74 us  [the longest x1 0.96 us: on_device(): pl.pallas_call(functools.partial(place_kernel, groups, tp), out_shape=[ja...]
  transfers between devices with their start and end apart: 17 -> 11, of which waited for: 8 -> 8; matrix products, arithmetic and copies ran while one was open for 15% -> 16% of each run, Pallas kernels for 3% -> 3%
where the time goes in v15:
time: 54.1 us; the launch traced here: 53.9 us
  waiting for transfers between devices  22.6 us (42%)
  starting transfers between devices  15 us (28%)
  matrix products  8.53 us (16%)
  Pallas kernels  5.13 us (9%)
  local copies, waits for them, and re-layouts  2.55 us (5%)
    ppermute x4, waiting for transfers between devices, ring_gather(): lax.ppermute(behind, axis, down)  11.1 us
    dot_general x1, matrix products, on_device(): jnp.dot(gathered, base_projection_weight, preferred_element_type=jnp.floa...  8.53 us
    ppermute x4, waiting for transfers between devices, ring_gather(): lax.ppermute(ahead, axis, up)  7.41 us
    ppermute x4, starting transfers between devices, ring_gather(): lax.ppermute(behind, axis, down)  6.62 us
    all_to_all x1, starting transfers between devices, on_device(): lifts = lax.all_to_all(lifts, 'tp', split_axis=0, concat_axis=0, tiled=True)  5.29 us
    all_to_all x1, waiting for transfers between devices, on_device(): lifts = lax.all_to_all(lifts, 'tp', split_axis=0, concat_axis=0, tiled=True)  4.08 us
    ppermute x4, starting transfers between devices, ring_gather(): lax.ppermute(ahead, axis, up)  2.59 us
    unnamed x12, local copies, waits for them, and re-layouts  2.55 us
  transfers between devices with their start and end apart: 11, of which 8 were waited for; matrix products, arithmetic and copies ran while one was open for 16% of the time, Pallas kernels for 3%

profile of v15, /device:TPU:0, one launch (start us, length us, event | category | flops | bytes accessed | tf_op | source)
XLA Modules:
  0.0 53.9 jit_solution(16012077643126319043)
XLA Ops:
  0.0 0.5 collective-permute-start.1
  0.5 3.0 %collective-permute-start.3 = (bf16[16,8192]{1,0:T(8,128)(2,1)}, bf16[16,8192]{1,0:T(8,128)(2,1)S(1)}, u32[]{:S(2)}, u32[]{:S(2)}) collective-permute-start(bf16[16,8192]{1,0:T(8,128)(2,1)} %bitcast.14), channel_id=1, source_target_pairs={{2,0},{4,2},{6,4},{7,6},{5,7},{3,5},{1,3},{0,1},{10,8},{12,10},{14... | collective-permute-start | bytes 786440 | tf_op jit(solution)/shard_map/ppermute | solution.py:36
  3.5 6.7 %collective-permute-done.3.refs_2_ = bf16[16,8192]{1,0:T(8,128)(2,1)S(1)} collective-permute-done((bf16[16,8192]{1,0:T(8,128)(2,1)}, bf16[16,8192]{1,0:T(8,128)(2,1)S(1)}, u32[]{:S(2)}, u32[]{:S(2)}) %collective-permute-start.3) | collective-permute-done | bytes 262176 | tf_op jit(solution)/shard_map/ppermute | solution.py:36
  10.2 1.7 %collective-permute-start.5 = (bf16[16,8192]{1,0:T(8,128)(2,1)S(1)}, bf16[16,8192]{1,0:T(8,128)(2,1)S(1)}, u32[]{:S(2)}, u32[]{:S(2)}) collective-permute-start(bf16[16,8192]{1,0:T(8,128)(2,1)S(1)} %collective-permute-done.3.refs_2_), channel_id=1, source_target_pairs={{2,0},{4,2},{6,4},{7,6},{5,7},{3,5},{1,3},{0,1},{10,8},{12,10},{14... | collective-permute-start | bytes 786440 | tf_op jit(solution)/shard_map/ppermute | solution.py:36
  11.9 0.3 collective-permute-start.4
  12.3 1.3 %copy-done = bf16[1,64,10240]{2,1,0:T(8,128)(2,1)S(1)} copy-done((bf16[1,64,10240]{2,1,0:T(8,128)(2,1)S(1)}, bf16[1,64,10240]{2,1,0:T(8,128)(2,1)}, u32[]{:S(2)}) %copy-start) | copy-done | bytes 1310744
  13.6 1.2 %copy-done.1 = bf16[1,8192,64]{1,2,0:T(8,128)(2,1)S(1)} copy-done((bf16[1,8192,64]{1,2,0:T(8,128)(2,1)S(1)}, bf16[1,8192,64]{1,2,0:T(8,128)(2,1)}, u32[]{:S(2)}) %copy-start.1) | copy-done | bytes 1048600
  14.8 0.7 %stack.1 = (bf16[8192,128]{1,0:T(8,128)(2,1)S(1)}, bf16[128,10240]{1,0:T(8,128)(2,1)S(1)}) custom-call(bf16[64,8192]{1,0:T(8,128)(2,1)S(1)} %bitcast.13, bf16[64,8192]{1,0:T(8,128)(2,1)S(1)} %collective-permute-done.refs_1_, bf16[64,10240]{1,0:T(8,128)(2,1)S(1)} %bitcast.11, bf16[64,10240]{1,0:T(8,128)(2,1)S(1)} %collective-permute-done.1.refs_3_), custom_call_target="tpu_custom_call" | custom-call | tf_op jit(solution)/shard_map/stack/pallas_call | solution.py:155
  15.5 2.4 %collective-permute-done.5.refs_1_.refs_4_ = bf16[16,8192]{1,0:T(8,128)(2,1)S(1)} collective-permute-done((bf16[16,8192]{1,0:T(8,128)(2,1)S(1)}, bf16[16,8192]{1,0:T(8,128)(2,1)S(1)}, u32[]{:S(2)}, u32[]{:S(2)}) %collective-permute-start.5) | collective-permute-done | bytes 262176 | tf_op jit(solution)/shard_map/ppermute | solution.py:36
  17.9 1.1 %collective-permute-done.4.refs_0_.refs_3_ = bf16[16,8192]{1,0:T(8,128)(2,1)S(1)} collective-permute-done((bf16[16,8192]{1,0:T(8,128)(2,1)S(1)}, bf16[16,8192]{1,0:T(8,128)(2,1)S(1)}, u32[]{:S(2)}, u32[]{:S(2)}) %collective-permute-start.4) | collective-permute-done | bytes 262176 | tf_op jit(solution)/shard_map/ppermute | solution.py:36
  19.0 0.7 %collective-permute-start.6 = (bf16[16,8192]{1,0:T(8,128)(2,1)S(1)}, bf16[16,8192]{1,0:T(8,128)(2,1)S(1)}, u32[]{:S(2)}, u32[]{:S(2)}) collective-permute-start(bf16[16,8192]{1,0:T(8,128)(2,1)S(1)} %get-tuple-element.19), channel_id=1, source_target_pairs={{0,2},{2,4},{4,6},{6,7},{7,5},{5,3},{3,1},{1,0},{8,10},{10,12},{12... | collective-permute-start | bytes 786440 | tf_op jit(solution)/shard_map/ppermute | solution.py:36
  19.8 1.4 %collective-permute-start.7 = (bf16[16,8192]{1,0:T(8,128)(2,1)S(1)}, bf16[16,8192]{1,0:T(8,128)(2,1)S(1)}, u32[]{:S(2)}, u32[]{:S(2)}) collective-permute-start(bf16[16,8192]{1,0:T(8,128)(2,1)S(1)} %get-tuple-element.20), channel_id=1, source_target_pairs={{2,0},{4,2},{6,4},{7,6},{5,7},{3,5},{1,3},{0,1},{10,8},{12,10},{14... | collective-permute-start | bytes 786440 | tf_op jit(solution)/shard_map/ppermute | solution.py:36
  21.1 1.0 %place.1 = (s32[1,128]{1,0:T(1,128)S(1)}, s32[128,1]{1,0:T(8,128)S(1)}) custom-call(s32[2,12]{1,0:T(2,128)S(1)} %copy-done.3, s32[1,12]{1,0:T(1,128)S(1)} %copy-done.4, s32[16]{0:T(128)S(1)} %copy-done.5), custom_call_target="tpu_custom_call" | custom-call | tf_op jit(solution)/shard_map/place/pallas_call | solution.py:166
  22.1 3.4 %collective-permute-done.6.refs_0_.refs_5_ = bf16[16,8192]{1,0:T(8,128)(2,1)S(1)} collective-permute-done((bf16[16,8192]{1,0:T(8,128)(2,1)S(1)}, bf16[16,8192]{1,0:T(8,128)(2,1)S(1)}, u32[]{:S(2)}, u32[]{:S(2)}) %collective-permute-start.6) | collective-permute-done | bytes 262176 | tf_op jit(solution)/shard_map/ppermute | solution.py:36
  25.5 0.7 %collective-permute-done.7.refs_1_.refs_6_ = bf16[16,8192]{1,0:T(8,128)(2,1)S(1)} collective-permute-done((bf16[16,8192]{1,0:T(8,128)(2,1)S(1)}, bf16[16,8192]{1,0:T(8,128)(2,1)S(1)}, u32[]{:S(2)}, u32[]{:S(2)}) %collective-permute-start.7) | collective-permute-done | bytes 262176 | tf_op jit(solution)/shard_map/ppermute | solution.py:36
  26.1 1.5 %collective-permute-start.8 = (bf16[16,4096]{1,0:T(8,128)(2,1)S(1)}, bf16[16,4096]{1,0:T(8,128)(2,1)S(1)}, u32[]{:S(2)}, u32[]{:S(2)}) collective-permute-start(bf16[16,4096]{1,0:T(8,128)(2,1)S(1)} %get-tuple-element.21), channel_id=1, source_target_pairs={{0,2},{2,4},{4,6},{6,7},{7,5},{5,3},{3,1},{1,0},{8,10},{10,12},{12... | collective-permute-start | bytes 393224 | tf_op jit(solution)/shard_map/ppermute | solution.py:36
  27.6 0.6 %collective-permute-start.9 = (bf16[16,4096]{1,0:T(8,128)(2,1)S(1)}, bf16[16,4096]{1,0:T(8,128)(2,1)S(1)}, u32[]{:S(2)}, u32[]{:S(2)}) collective-permute-start(bf16[16,4096]{1,0:T(8,128)(2,1)S(1)} %get-tuple-element.22), channel_id=1, source_target_pairs={{2,0},{4,2},{6,4},{7,6},{5,7},{3,5},{1,3},{0,1},{10,8},{12,10},{14... | collective-permute-start | bytes 393224 | tf_op jit(solution)/shard_map/ppermute | solution.py:36
  28.2 2.9 %collective-permute-done.8.refs_7_ = bf16[16,4096]{1,0:T(8,128)(2,1)S(1)} collective-permute-done((bf16[16,4096]{1,0:T(8,128)(2,1)S(1)}, bf16[16,4096]{1,0:T(8,128)(2,1)S(1)}, u32[]{:S(2)}, u32[]{:S(2)}) %collective-permute-start.8) | collective-permute-done | bytes 131104 | tf_op jit(solution)/shard_map/ppermute | solution.py:36
  31.2 1.4 %collective-permute-done.9.refs_8_ = bf16[16,4096]{1,0:T(8,128)(2,1)S(1)} collective-permute-done((bf16[16,4096]{1,0:T(8,128)(2,1)S(1)}, bf16[16,4096]{1,0:T(8,128)(2,1)S(1)}, u32[]{:S(2)}, u32[]{:S(2)}) %collective-permute-start.9) | collective-permute-done | bytes 131104 | tf_op jit(solution)/shard_map/ppermute | solution.py:36
  32.6 2.4 %lift.1 = (bf16[128,8192]{1,0:T(8,128)(2,1)S(1)}, bf16[8,32,1280]{2,1,0:T(8,128)(2,1)}) custom-call(s32[1,128]{1,0:T(1,128)S(1)} %get-tuple-element.16.refs_2_.place_ref, bf16[8192,128]{1,0:T(8,128)(2,1)S(1)} %get-tuple-element.17.refs_2_.down_ref, bf16[128,10240]{1,0:T(8,128)(2,1)S(1)} %get-tuple-element.18.refs_3_.up_ref, bf16[16,8192]{1,0:T(8,128)(2,1)S(1)} %bitcast.16, ...), custom_call_target="tpu_custom_call" | custom-call | flops 352321536 | bytes 4718592 | tf_op jit(solution)/shard_map/lift/pallas_call | solution.py:179
  35.0 5.3 %all-to-all-start = ((bf16[8,32,1280]{2,1,0:T(8,128)(2,1)}), bf16[8,32,1280]{2,1,0:T(8,128)(2,1)S(1)}, u32[]{:S(2)}, u32[]{:S(2)}) async-start(bf16[8,32,1280]{2,1,0:T(8,128)(2,1)} %get-tuple-element.24), calls=%async_computation | async-start | bytes 1310720 | tf_op jit(solution)/shard_map/all_to_all | solution.py:195
  40.3 8.5 %fusion.base_ref = f32[128,1280]{1,0:T(8,128)S(1)} fusion(bf16[128,8192]{1,0:T(8,128)(2,1)S(1)} %get-tuple-element.23, bf16[8192,1280]{1,0:T(8,128)(2,1)} %param.8), kind=kOutput, calls=%fused_computation | convolution fusion | flops 2684354560 | bytes 23724032 | tf_op jit(solution)/shard_map/dot_general | solution.py:197
  48.8 4.1 %all-to-all-done = bf16[8,32,1280]{2,1,0:T(8,128)(2,1)S(1)} async-done(((bf16[8,32,1280]{2,1,0:T(8,128)(2,1)}), bf16[8,32,1280]{2,1,0:T(8,128)(2,1)S(1)}, u32[]{:S(2)}, u32[]{:S(2)}) %all-to-all-start) | async-done | bytes 655392 | tf_op jit(solution)/shard_map/all_to_all | solution.py:195
  52.9 1.0 %add.1 = bf16[128,1280]{1,0:T(8,128)(2,1)} custom-call(s32[128,1]{1,0:T(8,128)S(1)} %get-tuple-element.15.refs_3_.place_ref, f32[128,1280]{1,0:T(8,128)S(1)} %fusion.base_ref, bf16[256,1280]{1,0:T(8,128)(2,1)S(1)} %bitcast.9), custom_call_target="tpu_custom_call" | custom-call | tf_op jit(solution)/shard_map/add/pallas_call | solution.py:198
  (17 shorter events, 0.2 us)
Async XLA Ops:
  0.0 12.3 %collective-permute-start.1 = (bf16[64,10240]{1,0:T(8,128)(2,1)}, bf16[64,10240]{1,0:T(8,128)(2,1)S(1)}, u32[]{:S(2)}, u32[]{:S(2)}) collective-permute-start(bf16[64,10240]{1,0:T(8,128)(2,1)} %bitcast.10), channel_id=1, source_target_pairs={{8,0},{0,8},{9,1},{1,9},{10,2},{2,10},{11,3},{3,11},{12,4},{4,12},... | collective-permute-start | bytes 3932168 | tf_op jit(solution)/shard_map/ppermute | solution.py:16
  0.5 11.8 %collective-permute-start = (bf16[64,8192]{1,0:T(8,128)(2,1)}, bf16[64,8192]{1,0:T(8,128)(2,1)S(1)}, u32[]{:S(2)}, u32[]{:S(2)}) collective-permute-start(bf16[64,8192]{1,0:T(8,128)(2,1)} %bitcast.12), channel_id=1, source_target_pairs={{8,0},{0,8},{9,1},{1,9},{10,2},{2,10},{11,3},{3,11},{12,4},{4,12},... | collective-permute-start | bytes 3145736 | tf_op jit(solution)/shard_map/ppermute | solution.py:16
  0.5 9.7 %collective-permute-start.3 = (bf16[16,8192]{1,0:T(8,128)(2,1)}, bf16[16,8192]{1,0:T(8,128)(2,1)S(1)}, u32[]{:S(2)}, u32[]{:S(2)}) collective-permute-start(bf16[16,8192]{1,0:T(8,128)(2,1)} %bitcast.14), channel_id=1, source_target_pairs={{2,0},{4,2},{6,4},{7,6},{5,7},{3,5},{1,3},{0,1},{10,8},{12,10},{14... | collective-permute-start | bytes 786440 | tf_op jit(solution)/shard_map/ppermute | solution.py:36
  3.5 8.4 %collective-permute-start.2 = (bf16[16,8192]{1,0:T(8,128)(2,1)}, bf16[16,8192]{1,0:T(8,128)(2,1)S(1)}, u32[]{:S(2)}, u32[]{:S(2)}) collective-permute-start(bf16[16,8192]{1,0:T(8,128)(2,1)} %bitcast.15), channel_id=1, source_target_pairs={{0,2},{2,4},{4,6},{6,7},{7,5},{5,3},{3,1},{1,0},{8,10},{10,12},{12... | collective-permute-start | bytes 786440 | tf_op jit(solution)/shard_map/ppermute | solution.py:36
  10.2 7.7 %collective-permute-start.5 = (bf16[16,8192]{1,0:T(8,128)(2,1)S(1)}, bf16[16,8192]{1,0:T(8,128)(2,1)S(1)}, u32[]{:S(2)}, u32[]{:S(2)}) collective-permute-start(bf16[16,8192]{1,0:T(8,128)(2,1)S(1)} %collective-permute-done.3.refs_2_), channel_id=1, source_target_pairs={{2,0},{4,2},{6,4},{7,6},{5,7},{3,5},{1,3},{0,1},{10,8},{12,10},{14... | collective-permute-start | bytes 786440 | tf_op jit(solution)/shard_map/ppermute | solution.py:36
  11.9 7.1 %collective-permute-start.4 = (bf16[16,8192]{1,0:T(8,128)(2,1)S(1)}, bf16[16,8192]{1,0:T(8,128)(2,1)S(1)}, u32[]{:S(2)}, u32[]{:S(2)}) collective-permute-start(bf16[16,8192]{1,0:T(8,128)(2,1)S(1)} %collective-permute-done.2.refs_1_), channel_id=1, source_target_pairs={{0,2},{2,4},{4,6},{6,7},{7,5},{5,3},{3,1},{1,0},{8,10},{10,12},{12... | collective-permute-start | bytes 786440 | tf_op jit(solution)/shard_map/ppermute | solution.py:36
  12.3 1.3 %copy-start = (bf16[1,64,10240]{2,1,0:T(8,128)(2,1)S(1)}, bf16[1,64,10240]{2,1,0:T(8,128)(2,1)}, u32[]{:S(2)}) copy-start(bf16[1,64,10240]{2,1,0:T(8,128)(2,1)} %param.10) | copy-start | bytes 3932164
  13.6 1.2 %copy-start.1 = (bf16[1,8192,64]{1,2,0:T(8,128)(2,1)S(1)}, bf16[1,8192,64]{1,2,0:T(8,128)(2,1)}, u32[]{:S(2)}) copy-start(bf16[1,8192,64]{1,2,0:T(8,128)(2,1)} %param.9) | copy-start | bytes 3145732
  19.0 2.1 %copy-start.3 = (s32[2,12]{1,0:T(2,128)S(1)}, s32[2,12]{1,0:T(2,128)}, u32[]{:S(2)}) copy-start(s32[2,12]{1,0:T(2,128)} %ids_ref.1) | copy-start | bytes 292
  19.0 2.1 %copy-start.4 = (s32[1,12]{1,0:T(1,128)S(1)}, s32[1,12]{1,0:T(1,128)}, u32[]{:S(2)}) copy-start(s32[1,12]{1,0:T(1,128)} %lengths_ref.1) | copy-start | bytes 148
  19.0 2.1 %copy-start.5 = (s32[16]{0:T(128)S(1)}, s32[16]{0:T(128)}, u32[]{:S(2)}) copy-start(s32[16]{0:T(128)} %slots_ref.1) | copy-start | bytes 196
  19.0 13.6 %copy-start.2 = (bf16[1,16,8192]{2,1,0:T(8,128)(2,1)S(1)}, bf16[1,16,8192]{2,1,0:T(8,128)(2,1)}, u32[]{:S(2)}) copy-start(bf16[1,16,8192]{2,1,0:T(8,128)(2,1)} %param.7) | copy-start | bytes 786436
  19.0 6.4 %collective-permute-start.6 = (bf16[16,8192]{1,0:T(8,128)(2,1)S(1)}, bf16[16,8192]{1,0:T(8,128)(2,1)S(1)}, u32[]{:S(2)}, u32[]{:S(2)}) collective-permute-start(bf16[16,8192]{1,0:T(8,128)(2,1)S(1)} %get-tuple-element.19), channel_id=1, source_target_pairs={{0,2},{2,4},{4,6},{6,7},{7,5},{5,3},{3,1},{1,0},{8,10},{10,12},{12... | collective-permute-start | bytes 786440 | tf_op jit(solution)/shard_map/ppermute | solution.py:36
  19.8 6.4 %collective-permute-start.7 = (bf16[16,8192]{1,0:T(8,128)(2,1)S(1)}, bf16[16,8192]{1,0:T(8,128)(2,1)S(1)}, u32[]{:S(2)}, u32[]{:S(2)}) collective-permute-start(bf16[16,8192]{1,0:T(8,128)(2,1)S(1)} %get-tuple-element.20), channel_id=1, source_target_pairs={{2,0},{4,2},{6,4},{7,6},{5,7},{3,5},{1,3},{0,1},{10,8},{12,10},{14... | collective-permute-start | bytes 786440 | tf_op jit(solution)/shard_map/ppermute | solution.py:36
  26.1 5.0 %collective-permute-start.8 = (bf16[16,4096]{1,0:T(8,128)(2,1)S(1)}, bf16[16,4096]{1,0:T(8,128)(2,1)S(1)}, u32[]{:S(2)}, u32[]{:S(2)}) collective-permute-start(bf16[16,4096]{1,0:T(8,128)(2,1)S(1)} %get-tuple-element.21), channel_id=1, source_target_pairs={{0,2},{2,4},{4,6},{6,7},{7,5},{5,3},{3,1},{1,0},{8,10},{10,12},{12... | collective-permute-start | bytes 393224 | tf_op jit(solution)/shard_map/ppermute | solution.py:36
  27.6 5.0 %collective-permute-start.9 = (bf16[16,4096]{1,0:T(8,128)(2,1)S(1)}, bf16[16,4096]{1,0:T(8,128)(2,1)S(1)}, u32[]{:S(2)}, u32[]{:S(2)}) collective-permute-start(bf16[16,4096]{1,0:T(8,128)(2,1)S(1)} %get-tuple-element.22), channel_id=1, source_target_pairs={{2,0},{4,2},{6,4},{7,6},{5,7},{3,5},{1,3},{0,1},{10,8},{12,10},{14... | collective-permute-start | bytes 393224 | tf_op jit(solution)/shard_map/ppermute | solution.py:36
  35.0 17.9 %all-to-all-start = ((bf16[8,32,1280]{2,1,0:T(8,128)(2,1)}), bf16[8,32,1280]{2,1,0:T(8,128)(2,1)S(1)}, u32[]{:S(2)}, u32[]{:S(2)}) async-start(bf16[8,32,1280]{2,1,0:T(8,128)(2,1)} %get-tuple-element.24), calls=%async_computation | async-start | bytes 1310720 | tf_op jit(solution)/shard_map/all_to_all | solution.py:195

commit v16 on v15

--- a/solution.py
+++ b/solution.py
@@ -21,52 +21,51 @@
     return list(range(0, n, 2)) + list(range(1, n, 2))[::-1]
 
 
-def ring_gather(block, axis, ahead_of_third, ahead_of_last):
+def ring_gather(block, axis, first):
     n = lax.axis_size(axis)
     ring = ring_of(n)
     up = [(ring[i], ring[(i + 1) % n]) for i in range(n)]
     down = [(ring[(i + 1) % n], ring[i]) for i in range(n)]
-    ahead = behind = block
-    pieces = [block]
-    for step in range(1, n // 2 + 1):
-        if step == n // 2:
-            ahead, behind = handed_on((ahead, behind), ahead_of_last, block.shape[1] // 2)
-        elif step == 3:
-            ahead, behind = handed_on((ahead, behind), ahead_of_third, block.shape[1])
-        ahead, behind = lax.ppermute(ahead, axis, up), lax.ppermute(behind, axis, down)
-        pieces += [ahead, behind]
-    return pieces
-
-
-def pass_kernel(waits, *refs):
-    n = (len(refs) - waits) // 2
-    for source, target in zip(refs[:n], refs[-n:]):
-        width = target.shape[1]
-        start = 0 if source is refs[0] else source.shape[1] - width
-        target[...] = source[:, start : start + width]
-
-
-def handed_on(arrays, values, width):
+    half = block.shape[1] // 2
+    neighbours = lax.ppermute(block, axis, up), lax.ppermute(block, axis, down)
+    cuts = [(0, 0), (1, 0), (0, half), (1, half)]
+    streams = handed_on(neighbours, first, cuts, half)
+    pieces = [block, *neighbours]
+    for step in range(2, n // 2):
+        streams = [lax.ppermute(x, axis, way) for x, way in zip(streams, (up, down) * 2)]
+        pieces += streams
+    return pieces + [lax.ppermute(streams[0], axis, up), lax.ppermute(streams[3], axis, down)]
+
+
+def pass_kernel(cuts, *refs):
+    for (i, start), target in zip(cuts, refs[-len(cuts) :]):
+        target[...] = refs[i][:, start : start + target.shape[1]]
+
+
+def handed_on(arrays, values, cuts, width):
     in_vmem = pl.BlockSpec(memory_space=pltpu.VMEM)
     return pl.pallas_call(
-        functools.partial(pass_kernel, len(values)),
-        out_shape=[jax.ShapeDtypeStruct((x.shape[0], width), x.dtype) for x in arrays],
+        functools.partial(pass_kernel, cuts),
+        out_shape=[jax.ShapeDtypeStruct((arrays[0].shape[0], width), arrays[0].dtype)] * len(cuts),
         in_specs=[in_vmem] * len(arrays) + [pl.BlockSpec(memory_space=pl.ANY)] * len(values),
-        out_specs=[in_vmem] * len(arrays),
+        out_specs=[in_vmem] * len(cuts),
         compiler_params=pltpu.CompilerParams(vmem_limit_bytes=16 * 2**20),
         name="pass",
     )(*arrays, *values)
 
 
-def ring_sources(axis):
+def ring_sources(axis, half):
     n = lax.axis_size(axis)
     me = lax.axis_index(axis)
     place = jnp.where(lax.rem(me, 2) == 0, me // 2, n - 1 - me // 2)
-    distances = [0] + [d for i in range(1, n // 2) for d in (i, -i)] + [n // 2] * 2
+    found = [(0, 0), (1, 0), (-1, 0)]
+    for i in range(2, n // 2):
+        found += [(i, 0), (-i, 0), (i, half), (-i, half)]
+    found += [(n // 2, 0), (n // 2, half)]
     sources = []
-    for distance in distances:
+    for distance, column in found:
         at = lax.rem(place - distance + n, n)
-        sources.append(jnp.where(at < n // 2, 2 * at, 2 * (n - 1 - at) + 1))
+        sources.append((jnp.where(at < n // 2, 2 * at, 2 * (n - 1 - at) + 1), column))
     return sources
 
 
@@ -104,11 +103,9 @@
     rows = pieces[0].shape[0]
     tok_all = tokens_ref.shape[0]
     parts, slots, columns = out_ref.shape
-    for i, (piece, source) in enumerate(zip(pieces, ring_sources("tp"))):
+    for piece, (source, column) in zip(pieces, ring_sources("tp", pieces[-1].shape[1])):
         start = pl.multiple_of(source * rows, rows)
-        size = piece.shape[1]
-        column = tokens_ref.shape[1] - size if i == len(pieces) - 1 else 0
-        tokens_ref[pl.ds(start, rows), column : column + size] = piece[...]
+        tokens_ref[pl.ds(start, rows), column : column + piece.shape[1]] = piece[...]
     low = jnp.dot(tokens_ref[...], down_ref[...], preferred_element_type=jnp.float32)
     here = lax.broadcasted_iota(jnp.int32, (slots, tok_all), 0) + lax.axis_index("tp") * slots
     chosen = (here == place_ref[...]).astype(jnp.bfloat16)
@@ -174,7 +171,7 @@
         compiler_params=small,
         name="place",
     )(request_adapter_ids, request_token_lengths, adapter_store_slot)
-    pieces = ring_gather(tokens[0], "tp", (down, up), (row, column))
+    pieces = ring_gather(tokens[0], "tp", (down, up, row, column))
 
     gathered, lifts = pl.pallas_call(
         functools.partial(lift_kernel, groups),

time: 54.1 us -> 53.1 us (0.982)
  waiting for transfers between devices: 22.6 us -> 15.6 us
  starting transfers between devices: 15 us -> 19 us
  local copies, waits for them, and re-layouts: 2.55 us -> 4.53 us
    ppermute x8 -> x12, waiting for transfers between devices: 18.5 us -> 9.74 us  [the longest x8 5.71 us: ring_gather(): lax.ppermute(x, axis, way)]
    ppermute x8 -> x12, starting transfers between devices: 9.21 us -> 12.9 us  [the longest x8 7.81 us: ring_gather(): lax.ppermute(x, axis, way)]
    unnamed x12, local copies, waits for them, and re-layouts: 2.55 us -> 4.53 us
    all_to_all x1, waiting for transfers between devices: 4.08 us -> 5.83 us  [on_device(): lifts = lax.all_to_all(lifts, 'tp', split_axis=0, concat_axis=0, tiled=True)]
  transfers between devices with their start and end apart: 11 -> 15, of which waited for: 8 -> 11; matrix products, arithmetic and copies ran while one was open for 16% -> 16% of each run, Pallas kernels for 3% -> 3%
where the time goes in v16:
time: 53.1 us; the launch traced here: 52.8 us
  starting transfers between devices  19 us (36%)
  waiting for transfers between devices  15.6 us (29%)
  matrix products  8.53 us (16%)
  Pallas kernels  5.08 us (10%)
  local copies, waits for them, and re-layouts  4.53 us (9%)
    dot_general x1, matrix products, on_device(): jnp.dot(gathered, base_projection_weight, preferred_element_type=jnp.floa...  8.53 us
    ppermute x8, starting transfers between devices, ring_gather(): lax.ppermute(x, axis, way)  7.81 us
    all_to_all x1, waiting for transfers between devices, on_device(): lifts = lax.all_to_all(lifts, 'tp', split_axis=0, concat_axis=0, tiled=True)  5.83 us
    ppermute x8, waiting for transfers between devices, ring_gather(): lax.ppermute(x, axis, way)  5.71 us
    all_to_all x1, starting transfers between devices, on_device(): lifts = lax.all_to_all(lifts, 'tp', split_axis=0, concat_axis=0, tiled=True)  5.64 us
    unnamed x12, local copies, waits for them, and re-layouts  4.53 us
    ppermute x1, starting transfers between devices, ring_gather(): lax.ppermute(block, axis, down)  2.97 us
    pallas_call x1, Pallas kernels, on_device(): pl.pallas_call(functools.partial(lift_kernel, groups), out_shape=[jax.Sha...  2.35 us
  transfers between devices with their start and end apart: 15, of which 11 were waited for; matrix products, arithmetic and copies ran while one was open for 16% of the time, Pallas kernels for 3%

profile of v16, /device:TPU:0, one launch (start us, length us, event | category | flops | bytes accessed | tf_op | source)
XLA Modules:
  0.0 52.8 jit_solution(9156924598264791370)
XLA Ops:
  0.5 3.0 %collective-permute-start.3 = (bf16[16,8192]{1,0:T(8,128)(2,1)}, bf16[16,8192]{1,0:T(8,128)(2,1)S(1)}, u32[]{:S(2)}, u32[]{:S(2)}) collective-permute-start(bf16[16,8192]{1,0:T(8,128)(2,1)} %bitcast.14), channel_id=1, source_target_pairs={{2,0},{4,2},{6,4},{7,6},{5,7},{3,5},{1,3},{0,1},{10,8},{12,10},{14... | collective-permute-start | bytes 786440 | tf_op jit(solution)/shard_map/ppermute | solution.py:30
  3.5 0.7 %copy-done.3 = s32[2,12]{1,0:T(2,128)S(1)} copy-done((s32[2,12]{1,0:T(2,128)S(1)}, s32[2,12]{1,0:T(2,128)}, u32[]{:S(2)}) %copy-start.3) | copy-done | bytes 120
  4.2 0.7 %copy-done.4 = s32[1,12]{1,0:T(1,128)S(1)} copy-done((s32[1,12]{1,0:T(1,128)S(1)}, s32[1,12]{1,0:T(1,128)}, u32[]{:S(2)}) %copy-start.4) | copy-done | bytes 72
  5.5 1.0 %place.1 = (s32[1,128]{1,0:T(1,128)S(1)}, s32[128,1]{1,0:T(8,128)S(1)}) custom-call(s32[2,12]{1,0:T(2,128)S(1)} %copy-done.3, s32[1,12]{1,0:T(1,128)S(1)} %copy-done.4, s32[16]{0:T(128)S(1)} %copy-done.5), custom_call_target="tpu_custom_call" | custom-call | tf_op jit(solution)/shard_map/place/pallas_call | solution.py:163
  6.5 1.3 %copy-done = bf16[1,64,10240]{2,1,0:T(8,128)(2,1)S(1)} copy-done((bf16[1,64,10240]{2,1,0:T(8,128)(2,1)S(1)}, bf16[1,64,10240]{2,1,0:T(8,128)(2,1)}, u32[]{:S(2)}) %copy-start) | copy-done | bytes 1310744
  7.8 1.2 %copy-done.1 = bf16[1,8192,64]{1,2,0:T(8,128)(2,1)S(1)} copy-done((bf16[1,8192,64]{1,2,0:T(8,128)(2,1)S(1)}, bf16[1,8192,64]{1,2,0:T(8,128)(2,1)}, u32[]{:S(2)}) %copy-start.1) | copy-done | bytes 1048600
  9.1 0.7 %stack.1 = (bf16[8192,128]{1,0:T(8,128)(2,1)S(1)}, bf16[128,10240]{1,0:T(8,128)(2,1)S(1)}) custom-call(bf16[64,8192]{1,0:T(8,128)(2,1)S(1)} %bitcast.13, bf16[64,8192]{1,0:T(8,128)(2,1)S(1)} %collective-permute-done.refs_1_, bf16[64,10240]{1,0:T(8,128)(2,1)S(1)} %bitcast.11, bf16[64,10240]{1,0:T(8,128)(2,1)S(1)} %collective-permute-done.1.refs_3_), custom_call_target="tpu_custom_call" | custom-call | tf_op jit(solution)/shard_map/stack/pallas_call | solution.py:152
  10.2 1.4 %collective-permute-done.2.refs_0_.refs_1_ = bf16[16,8192]{1,0:T(8,128)(2,1)S(1)} collective-permute-done((bf16[16,8192]{1,0:T(8,128)(2,1)}, bf16[16,8192]{1,0:T(8,128)(2,1)S(1)}, u32[]{:S(2)}, u32[]{:S(2)}) %collective-permute-start.2) | collective-permute-done | bytes 262176 | tf_op jit(solution)/shard_map/ppermute | solution.py:30
  12.1 1.7 %collective-permute-start.7 = (bf16[16,4096]{1,0:T(8,128)(2,1)S(1)}, bf16[16,4096]{1,0:T(8,128)(2,1)S(1)}, u32[]{:S(2)}, u32[]{:S(2)}) collective-permute-start(bf16[16,4096]{1,0:T(8,128)(2,1)S(1)} %get-tuple-element.22), channel_id=1, source_target_pairs={{2,0},{4,2},{6,4},{7,6},{5,7},{3,5},{1,3},{0,1},{10,8},{12,10},{14... | collective-permute-start | bytes 393224 | tf_op jit(solution)/shard_map/ppermute | solution.py:35
  13.7 1.6 %collective-permute-start.5 = (bf16[16,4096]{1,0:T(8,128)(2,1)S(1)}, bf16[16,4096]{1,0:T(8,128)(2,1)S(1)}, u32[]{:S(2)}, u32[]{:S(2)}) collective-permute-start(bf16[16,4096]{1,0:T(8,128)(2,1)S(1)} %get-tuple-element.20), channel_id=1, source_target_pairs={{2,0},{4,2},{6,4},{7,6},{5,7},{3,5},{1,3},{0,1},{10,8},{12,10},{14... | collective-permute-start | bytes 393224 | tf_op jit(solution)/shard_map/ppermute | solution.py:35
  15.8 1.7 %collective-permute-done.4.refs_3_ = bf16[16,4096]{1,0:T(8,128)(2,1)S(1)} collective-permute-done((bf16[16,4096]{1,0:T(8,128)(2,1)S(1)}, bf16[16,4096]{1,0:T(8,128)(2,1)S(1)}, u32[]{:S(2)}, u32[]{:S(2)}) %collective-permute-start.4) | collective-permute-done | bytes 131104 | tf_op jit(solution)/shard_map/ppermute | solution.py:35
  18.1 1.4 %collective-permute-start.11 = (bf16[16,4096]{1,0:T(8,128)(2,1)S(1)}, bf16[16,4096]{1,0:T(8,128)(2,1)S(1)}, u32[]{:S(2)}, u32[]{:S(2)}) collective-permute-start(bf16[16,4096]{1,0:T(8,128)(2,1)S(1)} %collective-permute-done.7.refs_6_), channel_id=1, source_target_pairs={{2,0},{4,2},{6,4},{7,6},{5,7},{3,5},{1,3},{0,1},{10,8},{12,10},{14... | collective-permute-start | bytes 393224 | tf_op jit(solution)/shard_map/ppermute | solution.py:35
  19.5 1.4 %collective-permute-done.5.refs_4_ = bf16[16,4096]{1,0:T(8,128)(2,1)S(1)} collective-permute-done((bf16[16,4096]{1,0:T(8,128)(2,1)S(1)}, bf16[16,4096]{1,0:T(8,128)(2,1)S(1)}, u32[]{:S(2)}, u32[]{:S(2)}) %collective-permute-start.5) | collective-permute-done | bytes 131104 | tf_op jit(solution)/shard_map/ppermute | solution.py:35
  20.9 1.3 %collective-permute-start.9 = (bf16[16,4096]{1,0:T(8,128)(2,1)S(1)}, bf16[16,4096]{1,0:T(8,128)(2,1)S(1)}, u32[]{:S(2)}, u32[]{:S(2)}) collective-permute-start(bf16[16,4096]{1,0:T(8,128)(2,1)S(1)} %collective-permute-done.5.refs_4_), channel_id=1, source_target_pairs={{2,0},{4,2},{6,4},{7,6},{5,7},{3,5},{1,3},{0,1},{10,8},{12,10},{14... | collective-permute-start | bytes 393224 | tf_op jit(solution)/shard_map/ppermute | solution.py:35
  22.2 0.7 %collective-permute-start.10 = (bf16[16,4096]{1,0:T(8,128)(2,1)S(1)}, bf16[16,4096]{1,0:T(8,128)(2,1)S(1)}, u32[]{:S(2)}, u32[]{:S(2)}) collective-permute-start(bf16[16,4096]{1,0:T(8,128)(2,1)S(1)} %collective-permute-done.6.refs_5_), channel_id=1, source_target_pairs={{0,2},{2,4},{4,6},{6,7},{7,5},{5,3},{3,1},{1,0},{8,10},{10,12},{12... | collective-permute-start | bytes 393224 | tf_op jit(solution)/shard_map/ppermute | solution.py:35
  23.0 0.9 %collective-permute-done.8.refs_7_ = bf16[16,4096]{1,0:T(8,128)(2,1)S(1)} collective-permute-done((bf16[16,4096]{1,0:T(8,128)(2,1)S(1)}, bf16[16,4096]{1,0:T(8,128)(2,1)S(1)}, u32[]{:S(2)}, u32[]{:S(2)}) %collective-permute-start.8) | collective-permute-done | bytes 131104 | tf_op jit(solution)/shard_map/ppermute | solution.py:35
  24.4 1.5 %collective-permute-start.13 = (bf16[16,4096]{1,0:T(8,128)(2,1)S(1)}, bf16[16,4096]{1,0:T(8,128)(2,1)S(1)}, u32[]{:S(2)}, u32[]{:S(2)}) collective-permute-start(bf16[16,4096]{1,0:T(8,128)(2,1)S(1)} %collective-permute-done.11.refs_10_), channel_id=1, source_target_pairs={{2,0},{4,2},{6,4},{7,6},{5,7},{3,5},{1,3},{0,1},{10,8},{12,10},{14... | collective-permute-start | bytes 393224 | tf_op jit(solution)/shard_map/ppermute | solution.py:37
  26.3 0.9 %collective-permute-done.10.refs_9_ = bf16[16,4096]{1,0:T(8,128)(2,1)S(1)} collective-permute-done((bf16[16,4096]{1,0:T(8,128)(2,1)S(1)}, bf16[16,4096]{1,0:T(8,128)(2,1)S(1)}, u32[]{:S(2)}, u32[]{:S(2)}) %collective-permute-start.10) | collective-permute-done | bytes 131104 | tf_op jit(solution)/shard_map/ppermute | solution.py:35
  27.2 1.6 %collective-permute-done.12.refs_11_ = bf16[16,4096]{1,0:T(8,128)(2,1)S(1)} collective-permute-done((bf16[16,4096]{1,0:T(8,128)(2,1)S(1)}, bf16[16,4096]{1,0:T(8,128)(2,1)S(1)}, u32[]{:S(2)}, u32[]{:S(2)}) %collective-permute-start.12) | collective-permute-done | bytes 131104 | tf_op jit(solution)/shard_map/ppermute | solution.py:37
  29.4 2.3 %lift.1 = (bf16[128,8192]{1,0:T(8,128)(2,1)S(1)}, bf16[8,32,1280]{2,1,0:T(8,128)(2,1)}) custom-call(s32[1,128]{1,0:T(1,128)S(1)} %get-tuple-element.16.refs_4_.place_ref, bf16[8192,128]{1,0:T(8,128)(2,1)S(1)} %get-tuple-element.17.refs_2_.down_ref, bf16[128,10240]{1,0:T(8,128)(2,1)S(1)} %get-tuple-element.18.refs_3_.up_ref, bf16[16,8192]{1,0:T(8,128)(2,1)S(1)} %bitcast.16, ...), custom_call_target="tpu_custom_call" | custom-call | flops 352321536 | bytes 4718592 | tf_op jit(solution)/shard_map/lift/pallas_call | solution.py:176
  31.8 5.6 %all-to-all-start = ((bf16[8,32,1280]{2,1,0:T(8,128)(2,1)}), bf16[8,32,1280]{2,1,0:T(8,128)(2,1)S(1)}, u32[]{:S(2)}, u32[]{:S(2)}) async-start(bf16[8,32,1280]{2,1,0:T(8,128)(2,1)} %get-tuple-element.24), calls=%async_computation | async-start | bytes 1310720 | tf_op jit(solution)/shard_map/all_to_all | solution.py:192
  37.4 8.5 %fusion.base_ref = f32[128,1280]{1,0:T(8,128)S(1)} fusion(bf16[128,8192]{1,0:T(8,128)(2,1)S(1)} %get-tuple-element.23, bf16[8192,1280]{1,0:T(8,128)(2,1)} %param.8), kind=kOutput, calls=%fused_computation | convolution fusion | flops 2684354560 | bytes 23724032 | tf_op jit(solution)/shard_map/dot_general | solution.py:194
  45.9 5.8 %all-to-all-done = bf16[8,32,1280]{2,1,0:T(8,128)(2,1)S(1)} async-done(((bf16[8,32,1280]{2,1,0:T(8,128)(2,1)}), bf16[8,32,1280]{2,1,0:T(8,128)(2,1)S(1)}, u32[]{:S(2)}, u32[]{:S(2)}) %all-to-all-start) | async-done | bytes 655392 | tf_op jit(solution)/shard_map/all_to_all | solution.py:192
  51.8 1.0 %add.1 = bf16[128,1280]{1,0:T(8,128)(2,1)} custom-call(s32[128,1]{1,0:T(8,128)S(1)} %get-tuple-element.15.refs_5_.place_ref, f32[128,1280]{1,0:T(8,128)S(1)} %fusion.base_ref, bf16[256,1280]{1,0:T(8,128)(2,1)S(1)} %bitcast.9), custom_call_target="tpu_custom_call" | custom-call | tf_op jit(solution)/shard_map/add/pallas_call | solution.py:195
  (24 shorter events, 4.6 us)
Async XLA Ops:
  0.0 6.5 %collective-permute-start.1 = (bf16[64,10240]{1,0:T(8,128)(2,1)}, bf16[64,10240]{1,0:T(8,128)(2,1)S(1)}, u32[]{:S(2)}, u32[]{:S(2)}) collective-permute-start(bf16[64,10240]{1,0:T(8,128)(2,1)} %bitcast.10), channel_id=1, source_target_pairs={{8,0},{0,8},{9,1},{1,9},{10,2},{2,10},{11,3},{3,11},{12,4},{4,12},... | collective-permute-start | bytes 3932168 | tf_op jit(solution)/shard_map/ppermute | solution.py:16
  0.5 6.0 %collective-permute-start = (bf16[64,8192]{1,0:T(8,128)(2,1)}, bf16[64,8192]{1,0:T(8,128)(2,1)S(1)}, u32[]{:S(2)}, u32[]{:S(2)}) collective-permute-start(bf16[64,8192]{1,0:T(8,128)(2,1)} %bitcast.12), channel_id=1, source_target_pairs={{8,0},{0,8},{9,1},{1,9},{10,2},{2,10},{11,3},{3,11},{12,4},{4,12},... | collective-permute-start | bytes 3145736 | tf_op jit(solution)/shard_map/ppermute | solution.py:16
  0.5 9.7 %collective-permute-start.3 = (bf16[16,8192]{1,0:T(8,128)(2,1)}, bf16[16,8192]{1,0:T(8,128)(2,1)S(1)}, u32[]{:S(2)}, u32[]{:S(2)}) collective-permute-start(bf16[16,8192]{1,0:T(8,128)(2,1)} %bitcast.14), channel_id=1, source_target_pairs={{2,0},{4,2},{6,4},{7,6},{5,7},{3,5},{1,3},{0,1},{10,8},{12,10},{14... | collective-permute-start | bytes 786440 | tf_op jit(solution)/shard_map/ppermute | solution.py:30
  3.5 8.1 %collective-permute-start.2 = (bf16[16,8192]{1,0:T(8,128)(2,1)}, bf16[16,8192]{1,0:T(8,128)(2,1)S(1)}, u32[]{:S(2)}, u32[]{:S(2)}) collective-permute-start(bf16[16,8192]{1,0:T(8,128)(2,1)} %bitcast.15), channel_id=1, source_target_pairs={{0,2},{2,4},{4,6},{6,7},{7,5},{5,3},{3,1},{1,0},{8,10},{10,12},{12... | collective-permute-start | bytes 786440 | tf_op jit(solution)/shard_map/ppermute | solution.py:30
  3.5 0.7 %copy-start.3 = (s32[2,12]{1,0:T(2,128)S(1)}, s32[2,12]{1,0:T(2,128)}, u32[]{:S(2)}) copy-start(s32[2,12]{1,0:T(2,128)} %ids_ref.1) | copy-start | bytes 292
  4.2 0.7 %copy-start.4 = (s32[1,12]{1,0:T(1,128)S(1)}, s32[1,12]{1,0:T(1,128)}, u32[]{:S(2)}) copy-start(s32[1,12]{1,0:T(1,128)} %lengths_ref.1) | copy-start | bytes 148
  4.9 0.7 %copy-start.5 = (s32[16]{0:T(128)S(1)}, s32[16]{0:T(128)}, u32[]{:S(2)}) copy-start(s32[16]{0:T(128)} %slots_ref.1) | copy-start | bytes 196
  6.5 1.3 %copy-start = (bf16[1,64,10240]{2,1,0:T(8,128)(2,1)S(1)}, bf16[1,64,10240]{2,1,0:T(8,128)(2,1)}, u32[]{:S(2)}) copy-start(bf16[1,64,10240]{2,1,0:T(8,128)(2,1)} %param.10) | copy-start | bytes 3932164
  7.8 1.2 %copy-start.1 = (bf16[1,8192,64]{1,2,0:T(8,128)(2,1)S(1)}, bf16[1,8192,64]{1,2,0:T(8,128)(2,1)}, u32[]{:S(2)}) copy-start(bf16[1,8192,64]{1,2,0:T(8,128)(2,1)} %param.9) | copy-start | bytes 3145732
  11.6 17.8 %copy-start.2 = (bf16[1,16,8192]{2,1,0:T(8,128)(2,1)S(1)}, bf16[1,16,8192]{2,1,0:T(8,128)(2,1)}, u32[]{:S(2)}) copy-start(bf16[1,16,8192]{2,1,0:T(8,128)(2,1)} %param.7) | copy-start | bytes 786436
  11.7 5.9 %collective-permute-start.4 = (bf16[16,4096]{1,0:T(8,128)(2,1)S(1)}, bf16[16,4096]{1,0:T(8,128)(2,1)S(1)}, u32[]{:S(2)}, u32[]{:S(2)}) collective-permute-start(bf16[16,4096]{1,0:T(8,128)(2,1)S(1)} %get-tuple-element.19), channel_id=1, source_target_pairs={{0,2},{2,4},{4,6},{6,7},{7,5},{5,3},{3,1},{1,0},{8,10},{10,12},{12... | collective-permute-start | bytes 393224 | tf_op jit(solution)/shard_map/ppermute | solution.py:35
  12.1 6.0 %collective-permute-start.7 = (bf16[16,4096]{1,0:T(8,128)(2,1)S(1)}, bf16[16,4096]{1,0:T(8,128)(2,1)S(1)}, u32[]{:S(2)}, u32[]{:S(2)}) collective-permute-start(bf16[16,4096]{1,0:T(8,128)(2,1)S(1)} %get-tuple-element.22), channel_id=1, source_target_pairs={{2,0},{4,2},{6,4},{7,6},{5,7},{3,5},{1,3},{0,1},{10,8},{12,10},{14... | collective-permute-start | bytes 393224 | tf_op jit(solution)/shard_map/ppermute | solution.py:35
  13.7 7.2 %collective-permute-start.5 = (bf16[16,4096]{1,0:T(8,128)(2,1)S(1)}, bf16[16,4096]{1,0:T(8,128)(2,1)S(1)}, u32[]{:S(2)}, u32[]{:S(2)}) collective-permute-start(bf16[16,4096]{1,0:T(8,128)(2,1)S(1)} %get-tuple-element.20), channel_id=1, source_target_pairs={{2,0},{4,2},{6,4},{7,6},{5,7},{3,5},{1,3},{0,1},{10,8},{12,10},{14... | collective-permute-start | bytes 393224 | tf_op jit(solution)/shard_map/ppermute | solution.py:35
  15.3 6.9 %collective-permute-start.6 = (bf16[16,4096]{1,0:T(8,128)(2,1)S(1)}, bf16[16,4096]{1,0:T(8,128)(2,1)S(1)}, u32[]{:S(2)}, u32[]{:S(2)}) collective-permute-start(bf16[16,4096]{1,0:T(8,128)(2,1)S(1)} %get-tuple-element.21), channel_id=1, source_target_pairs={{0,2},{2,4},{4,6},{6,7},{7,5},{5,3},{3,1},{1,0},{8,10},{10,12},{12... | collective-permute-start | bytes 393224 | tf_op jit(solution)/shard_map/ppermute | solution.py:35
  17.5 6.4 %collective-permute-start.8 = (bf16[16,4096]{1,0:T(8,128)(2,1)S(1)}, bf16[16,4096]{1,0:T(8,128)(2,1)S(1)}, u32[]{:S(2)}, u32[]{:S(2)}) collective-permute-start(bf16[16,4096]{1,0:T(8,128)(2,1)S(1)} %collective-permute-done.4.refs_3_), channel_id=1, source_target_pairs={{0,2},{2,4},{4,6},{6,7},{7,5},{5,3},{3,1},{1,0},{8,10},{10,12},{12... | collective-permute-start | bytes 393224 | tf_op jit(solution)/shard_map/ppermute | solution.py:35
  18.1 6.3 %collective-permute-start.11 = (bf16[16,4096]{1,0:T(8,128)(2,1)S(1)}, bf16[16,4096]{1,0:T(8,128)(2,1)S(1)}, u32[]{:S(2)}, u32[]{:S(2)}) collective-permute-start(bf16[16,4096]{1,0:T(8,128)(2,1)S(1)} %collective-permute-done.7.refs_6_), channel_id=1, source_target_pairs={{2,0},{4,2},{6,4},{7,6},{5,7},{3,5},{1,3},{0,1},{10,8},{12,10},{14... | collective-permute-start | bytes 393224 | tf_op jit(solution)/shard_map/ppermute | solution.py:35
  20.9 5.4 %collective-permute-start.9 = (bf16[16,4096]{1,0:T(8,128)(2,1)S(1)}, bf16[16,4096]{1,0:T(8,128)(2,1)S(1)}, u32[]{:S(2)}, u32[]{:S(2)}) collective-permute-start(bf16[16,4096]{1,0:T(8,128)(2,1)S(1)} %collective-permute-done.5.refs_4_), channel_id=1, source_target_pairs={{2,0},{4,2},{6,4},{7,6},{5,7},{3,5},{1,3},{0,1},{10,8},{12,10},{14... | collective-permute-start | bytes 393224 | tf_op jit(solution)/shard_map/ppermute | solution.py:35
  22.2 5.0 %collective-permute-start.10 = (bf16[16,4096]{1,0:T(8,128)(2,1)S(1)}, bf16[16,4096]{1,0:T(8,128)(2,1)S(1)}, u32[]{:S(2)}, u32[]{:S(2)}) collective-permute-start(bf16[16,4096]{1,0:T(8,128)(2,1)S(1)} %collective-permute-done.6.refs_5_), channel_id=1, source_target_pairs={{0,2},{2,4},{4,6},{6,7},{7,5},{5,3},{3,1},{1,0},{8,10},{10,12},{12... | collective-permute-start | bytes 393224 | tf_op jit(solution)/shard_map/ppermute | solution.py:35
  23.9 5.0 %collective-permute-start.12 = (bf16[16,4096]{1,0:T(8,128)(2,1)S(1)}, bf16[16,4096]{1,0:T(8,128)(2,1)S(1)}, u32[]{:S(2)}, u32[]{:S(2)}) collective-permute-start(bf16[16,4096]{1,0:T(8,128)(2,1)S(1)} %collective-permute-done.8.refs_7_), channel_id=1, source_target_pairs={{0,2},{2,4},{4,6},{6,7},{7,5},{5,3},{3,1},{1,0},{8,10},{10,12},{12... | collective-permute-start | bytes 393224 | tf_op jit(solution)/shard_map/ppermute | solution.py:37
  24.4 5.0 %collective-permute-start.13 = (bf16[16,4096]{1,0:T(8,128)(2,1)S(1)}, bf16[16,4096]{1,0:T(8,128)(2,1)S(1)}, u32[]{:S(2)}, u32[]{:S(2)}) collective-permute-start(bf16[16,4096]{1,0:T(8,128)(2,1)S(1)} %collective-permute-done.11.refs_10_), channel_id=1, source_target_pairs={{2,0},{4,2},{6,4},{7,6},{5,7},{3,5},{1,3},{0,1},{10,8},{12,10},{14... | collective-permute-start | bytes 393224 | tf_op jit(solution)/shard_map/ppermute | solution.py:37
  31.8 20.0 %all-to-all-start = ((bf16[8,32,1280]{2,1,0:T(8,128)(2,1)}), bf16[8,32,1280]{2,1,0:T(8,128)(2,1)S(1)}, u32[]{:S(2)}, u32[]{:S(2)}) async-start(bf16[8,32,1280]{2,1,0:T(8,128)(2,1)} %get-tuple-element.24), calls=%async_computation | async-start | bytes 1310720 | tf_op jit(solution)/shard_map/all_to_all | solution.py:192

commit v17 on v16

--- a/solution.py
+++ b/solution.py
@@ -54,10 +54,13 @@
     )(*arrays, *values)
 
 
+def ring_place(i, n):
+    return jnp.where(lax.rem(i, 2) == 0, i // 2, n - 1 - i // 2)
+
+
 def ring_sources(axis, half):
     n = lax.axis_size(axis)
-    me = lax.axis_index(axis)
-    place = jnp.where(lax.rem(me, 2) == 0, me // 2, n - 1 - me // 2)
+    place = ring_place(lax.axis_index(axis), n)
     found = [(0, 0), (1, 0), (-1, 0)]
     for i in range(2, n // 2):
         found += [(i, 0), (-i, 0), (i, half), (-i, half)]
@@ -88,7 +91,7 @@
         slot = slots_ref[ids_ref[group, request]]
         end = start + lengths_ref[0, request]
         panel = lax.rem(slot // tp - group + groups, groups)
-        first = (lax.rem(slot, tp) * groups + panel) * longest - start
+        first = (ring_place(lax.rem(slot, tp), tp) * groups + panel) * longest - start
         row = jnp.where((along >= start) & (along < end), first + along, row)
         column = jnp.where((down >= start) & (down < end), first + down, column)
         return end, row, column
@@ -107,16 +110,17 @@
         start = pl.multiple_of(source * rows, rows)
         tokens_ref[pl.ds(start, rows), column : column + piece.shape[1]] = piece[...]
     low = jnp.dot(tokens_ref[...], down_ref[...], preferred_element_type=jnp.float32)
-    here = lax.broadcasted_iota(jnp.int32, (slots, tok_all), 0) + lax.axis_index("tp") * slots
+    place = ring_place(lax.axis_index("tp"), parts)
+    here = lax.broadcasted_iota(jnp.int32, (slots, tok_all), 0) + place * slots
     chosen = (here == place_ref[...]).astype(jnp.bfloat16)
     picked = jnp.dot(chosen, low.astype(jnp.bfloat16), preferred_element_type=jnp.float32)
     row_panel = lax.broadcasted_iota(jnp.int32, picked.shape, 0) // (slots // groups)
     rank_panel = lax.broadcasted_iota(jnp.int32, picked.shape, 1) // rank
     picked = jnp.where(row_panel == rank_panel, picked, 0.0).astype(jnp.bfloat16)
-    for part in range(parts):
+    for part, owner in enumerate(ring_of(parts)):
         out_ref[part] = jnp.dot(
             picked,
-            up_ref[:, part * columns : (part + 1) * columns],
+            up_ref[:, owner * columns : (owner + 1) * columns],
             preferred_element_type=jnp.float32,
         ).astype(out_ref.dtype)
 
@@ -189,7 +193,9 @@
         ),
         name="lift",
     )(row, down, up, *pieces)
-    lifts = lax.all_to_all(lifts, "tp", split_axis=0, concat_axis=0, tiled=True)
+    lifts = lax.all_to_all(
+        lifts, "tp", split_axis=0, concat_axis=0, axis_index_groups=[ring_of(tp)], tiled=True
+    )
 
     base = jnp.dot(gathered, base_projection_weight, preferred_element_type=jnp.float32)
     out = pl.pallas_call(

time: 53.1 us -> 51.7 us (0.974)
  waiting for transfers between devices: 15.6 us -> 14.2 us
    all_to_all x1, waiting for transfers between devices: 5.83 us -> 4.42 us  [on_device(): lax.all_to_all(lifts, 'tp', split_axis=0, concat_axis=0, axis_index_group...]
  transfers between devices with their start and end apart: 15 -> 15, of which waited for: 11 -> 11; matrix products, arithmetic and copies ran while one was open for 16% -> 17% of each run, Pallas kernels for 3% -> 3%
where the time goes in v17:
time: 51.7 us; the launch traced here: 51.4 us
  starting transfers between devices  19 us (37%)
  waiting for transfers between devices  14.2 us (27%)
  matrix products  8.53 us (16%)
  Pallas kernels  5.13 us (10%)
  local copies, waits for them, and re-layouts  4.53 us (9%)
    dot_general x1, matrix products, on_device(): jnp.dot(gathered, base_projection_weight, preferred_element_type=jnp.floa...  8.53 us
    ppermute x8, starting transfers between devices, ring_gather(): lax.ppermute(x, axis, way)  7.77 us
    ppermute x8, waiting for transfers between devices, ring_gather(): lax.ppermute(x, axis, way)  5.75 us
    all_to_all x1, starting transfers between devices, on_device(): lax.all_to_all(lifts, 'tp', split_axis=0, concat_axis=0, axis_index_group...  5.64 us
    unnamed x12, local copies, waits for them, and re-layouts  4.53 us
    all_to_all x1, waiting for transfers between devices, on_device(): lax.all_to_all(lifts, 'tp', split_axis=0, concat_axis=0, axis_index_group...  4.42 us
    ppermute x1, starting transfers between devices, ring_gather(): lax.ppermute(block, axis, down)  2.97 us
    pallas_call x1, Pallas kernels, on_device(): pl.pallas_call(functools.partial(lift_kernel, groups), out_shape=[jax.Sha...  2.35 us
  transfers between devices with their start and end apart: 15, of which 11 were waited for; matrix products, arithmetic and copies ran while one was open for 17% of the time, Pallas kernels for 3%

profile of v17, /device:TPU:0, one launch (start us, length us, event | category | flops | bytes accessed | tf_op | source)
XLA Modules:
  0.0 51.4 jit_solution(7111371887702360090)
XLA Ops:
  0.5 3.0 %collective-permute-start.3 = (bf16[16,8192]{1,0:T(8,128)(2,1)}, bf16[16,8192]{1,0:T(8,128)(2,1)S(1)}, u32[]{:S(2)}, u32[]{:S(2)}) collective-permute-start(bf16[16,8192]{1,0:T(8,128)(2,1)} %bitcast.14), channel_id=1, source_target_pairs={{2,0},{4,2},{6,4},{7,6},{5,7},{3,5},{1,3},{0,1},{10,8},{12,10},{14... | collective-permute-start | bytes 786440 | tf_op jit(solution)/shard_map/ppermute | solution.py:30
  3.5 0.7 %copy-done.3 = s32[2,12]{1,0:T(2,128)S(1)} copy-done((s32[2,12]{1,0:T(2,128)S(1)}, s32[2,12]{1,0:T(2,128)}, u32[]{:S(2)}) %copy-start.3) | copy-done | bytes 120
  4.2 0.7 %copy-done.4 = s32[1,12]{1,0:T(1,128)S(1)} copy-done((s32[1,12]{1,0:T(1,128)S(1)}, s32[1,12]{1,0:T(1,128)}, u32[]{:S(2)}) %copy-start.4) | copy-done | bytes 72
  5.5 1.0 %place.1 = (s32[1,128]{1,0:T(1,128)S(1)}, s32[128,1]{1,0:T(8,128)S(1)}) custom-call(s32[2,12]{1,0:T(2,128)S(1)} %copy-done.3, s32[1,12]{1,0:T(1,128)S(1)} %copy-done.4, s32[16]{0:T(128)S(1)} %copy-done.5), custom_call_target="tpu_custom_call" | custom-call | tf_op jit(solution)/shard_map/place/pallas_call | solution.py:167
  6.6 1.3 %copy-done = bf16[1,64,10240]{2,1,0:T(8,128)(2,1)S(1)} copy-done((bf16[1,64,10240]{2,1,0:T(8,128)(2,1)S(1)}, bf16[1,64,10240]{2,1,0:T(8,128)(2,1)}, u32[]{:S(2)}) %copy-start) | copy-done | bytes 1310744
  7.9 1.2 %copy-done.1 = bf16[1,8192,64]{1,2,0:T(8,128)(2,1)S(1)} copy-done((bf16[1,8192,64]{1,2,0:T(8,128)(2,1)S(1)}, bf16[1,8192,64]{1,2,0:T(8,128)(2,1)}, u32[]{:S(2)}) %copy-start.1) | copy-done | bytes 1048600
  9.1 0.7 %stack.1 = (bf16[8192,128]{1,0:T(8,128)(2,1)S(1)}, bf16[128,10240]{1,0:T(8,128)(2,1)S(1)}) custom-call(bf16[64,8192]{1,0:T(8,128)(2,1)S(1)} %bitcast.13, bf16[64,8192]{1,0:T(8,128)(2,1)S(1)} %collective-permute-done.refs_1_, bf16[64,10240]{1,0:T(8,128)(2,1)S(1)} %bitcast.11, bf16[64,10240]{1,0:T(8,128)(2,1)S(1)} %collective-permute-done.1.refs_3_), custom_call_target="tpu_custom_call" | custom-call | tf_op jit(solution)/shard_map/stack/pallas_call | solution.py:156
  10.2 1.4 %collective-permute-done.2.refs_0_.refs_1_ = bf16[16,8192]{1,0:T(8,128)(2,1)S(1)} collective-permute-done((bf16[16,8192]{1,0:T(8,128)(2,1)}, bf16[16,8192]{1,0:T(8,128)(2,1)S(1)}, u32[]{:S(2)}, u32[]{:S(2)}) %collective-permute-start.2) | collective-permute-done | bytes 262176 | tf_op jit(solution)/shard_map/ppermute | solution.py:30
  12.1 1.7 %collective-permute-start.7 = (bf16[16,4096]{1,0:T(8,128)(2,1)S(1)}, bf16[16,4096]{1,0:T(8,128)(2,1)S(1)}, u32[]{:S(2)}, u32[]{:S(2)}) collective-permute-start(bf16[16,4096]{1,0:T(8,128)(2,1)S(1)} %get-tuple-element.22), channel_id=1, source_target_pairs={{2,0},{4,2},{6,4},{7,6},{5,7},{3,5},{1,3},{0,1},{10,8},{12,10},{14... | collective-permute-start | bytes 393224 | tf_op jit(solution)/shard_map/ppermute | solution.py:35
  13.7 1.6 %collective-permute-start.5 = (bf16[16,4096]{1,0:T(8,128)(2,1)S(1)}, bf16[16,4096]{1,0:T(8,128)(2,1)S(1)}, u32[]{:S(2)}, u32[]{:S(2)}) collective-permute-start(bf16[16,4096]{1,0:T(8,128)(2,1)S(1)} %get-tuple-element.20), channel_id=1, source_target_pairs={{2,0},{4,2},{6,4},{7,6},{5,7},{3,5},{1,3},{0,1},{10,8},{12,10},{14... | collective-permute-start | bytes 393224 | tf_op jit(solution)/shard_map/ppermute | solution.py:35
  15.8 1.7 %collective-permute-done.4.refs_3_ = bf16[16,4096]{1,0:T(8,128)(2,1)S(1)} collective-permute-done((bf16[16,4096]{1,0:T(8,128)(2,1)S(1)}, bf16[16,4096]{1,0:T(8,128)(2,1)S(1)}, u32[]{:S(2)}, u32[]{:S(2)}) %collective-permute-start.4) | collective-permute-done | bytes 131104 | tf_op jit(solution)/shard_map/ppermute | solution.py:35
  18.2 1.4 %collective-permute-start.11 = (bf16[16,4096]{1,0:T(8,128)(2,1)S(1)}, bf16[16,4096]{1,0:T(8,128)(2,1)S(1)}, u32[]{:S(2)}, u32[]{:S(2)}) collective-permute-start(bf16[16,4096]{1,0:T(8,128)(2,1)S(1)} %collective-permute-done.7.refs_6_), channel_id=1, source_target_pairs={{2,0},{4,2},{6,4},{7,6},{5,7},{3,5},{1,3},{0,1},{10,8},{12,10},{14... | collective-permute-start | bytes 393224 | tf_op jit(solution)/shard_map/ppermute | solution.py:35
  19.5 1.4 %collective-permute-done.5.refs_4_ = bf16[16,4096]{1,0:T(8,128)(2,1)S(1)} collective-permute-done((bf16[16,4096]{1,0:T(8,128)(2,1)S(1)}, bf16[16,4096]{1,0:T(8,128)(2,1)S(1)}, u32[]{:S(2)}, u32[]{:S(2)}) %collective-permute-start.5) | collective-permute-done | bytes 131104 | tf_op jit(solution)/shard_map/ppermute | solution.py:35
  21.0 1.3 %collective-permute-start.9 = (bf16[16,4096]{1,0:T(8,128)(2,1)S(1)}, bf16[16,4096]{1,0:T(8,128)(2,1)S(1)}, u32[]{:S(2)}, u32[]{:S(2)}) collective-permute-start(bf16[16,4096]{1,0:T(8,128)(2,1)S(1)} %collective-permute-done.5.refs_4_), channel_id=1, source_target_pairs={{2,0},{4,2},{6,4},{7,6},{5,7},{3,5},{1,3},{0,1},{10,8},{12,10},{14... | collective-permute-start | bytes 393224 | tf_op jit(solution)/shard_map/ppermute | solution.py:35
  22.2 0.7 %collective-permute-start.10 = (bf16[16,4096]{1,0:T(8,128)(2,1)S(1)}, bf16[16,4096]{1,0:T(8,128)(2,1)S(1)}, u32[]{:S(2)}, u32[]{:S(2)}) collective-permute-start(bf16[16,4096]{1,0:T(8,128)(2,1)S(1)} %collective-permute-done.6.refs_5_), channel_id=1, source_target_pairs={{0,2},{2,4},{4,6},{6,7},{7,5},{5,3},{3,1},{1,0},{8,10},{10,12},{12... | collective-permute-start | bytes 393224 | tf_op jit(solution)/shard_map/ppermute | solution.py:35
  23.0 0.9 %collective-permute-done.8.refs_7_ = bf16[16,4096]{1,0:T(8,128)(2,1)S(1)} collective-permute-done((bf16[16,4096]{1,0:T(8,128)(2,1)S(1)}, bf16[16,4096]{1,0:T(8,128)(2,1)S(1)}, u32[]{:S(2)}, u32[]{:S(2)}) %collective-permute-start.8) | collective-permute-done | bytes 131104 | tf_op jit(solution)/shard_map/ppermute | solution.py:35
  24.4 1.5 %collective-permute-start.13 = (bf16[16,4096]{1,0:T(8,128)(2,1)S(1)}, bf16[16,4096]{1,0:T(8,128)(2,1)S(1)}, u32[]{:S(2)}, u32[]{:S(2)}) collective-permute-start(bf16[16,4096]{1,0:T(8,128)(2,1)S(1)} %collective-permute-done.11.refs_10_), channel_id=1, source_target_pairs={{2,0},{4,2},{6,4},{7,6},{5,7},{3,5},{1,3},{0,1},{10,8},{12,10},{14... | collective-permute-start | bytes 393224 | tf_op jit(solution)/shard_map/ppermute | solution.py:37
  26.4 0.8 %collective-permute-done.10.refs_9_ = bf16[16,4096]{1,0:T(8,128)(2,1)S(1)} collective-permute-done((bf16[16,4096]{1,0:T(8,128)(2,1)S(1)}, bf16[16,4096]{1,0:T(8,128)(2,1)S(1)}, u32[]{:S(2)}, u32[]{:S(2)}) %collective-permute-start.10) | collective-permute-done | bytes 131104 | tf_op jit(solution)/shard_map/ppermute | solution.py:35
  27.2 1.6 %collective-permute-done.12.refs_11_ = bf16[16,4096]{1,0:T(8,128)(2,1)S(1)} collective-permute-done((bf16[16,4096]{1,0:T(8,128)(2,1)S(1)}, bf16[16,4096]{1,0:T(8,128)(2,1)S(1)}, u32[]{:S(2)}, u32[]{:S(2)}) %collective-permute-start.12) | collective-permute-done | bytes 131104 | tf_op jit(solution)/shard_map/ppermute | solution.py:37
  29.4 2.4 %lift.1 = (bf16[128,8192]{1,0:T(8,128)(2,1)S(1)}, bf16[8,32,1280]{2,1,0:T(8,128)(2,1)}) custom-call(s32[1,128]{1,0:T(1,128)S(1)} %get-tuple-element.16.refs_4_.place_ref, bf16[8192,128]{1,0:T(8,128)(2,1)S(1)} %get-tuple-element.17.refs_2_.down_ref, bf16[128,10240]{1,0:T(8,128)(2,1)S(1)} %get-tuple-element.18.refs_3_.up_ref, bf16[16,8192]{1,0:T(8,128)(2,1)S(1)} %bitcast.16, ...), custom_call_target="tpu_custom_call" | custom-call | flops 352321536 | bytes 4718592 | tf_op jit(solution)/shard_map/lift/pallas_call | solution.py:180
  31.8 5.6 %all-to-all-start = ((bf16[8,32,1280]{2,1,0:T(8,128)(2,1)}), bf16[8,32,1280]{2,1,0:T(8,128)(2,1)S(1)}, u32[]{:S(2)}, u32[]{:S(2)}) async-start(bf16[8,32,1280]{2,1,0:T(8,128)(2,1)} %get-tuple-element.24), calls=%async_computation | async-start | bytes 1310720 | tf_op jit(solution)/shard_map/all_to_all | solution.py:196
  37.4 8.5 %fusion.base_ref = f32[128,1280]{1,0:T(8,128)S(1)} fusion(bf16[128,8192]{1,0:T(8,128)(2,1)S(1)} %get-tuple-element.23, bf16[8192,1280]{1,0:T(8,128)(2,1)} %param.8), kind=kOutput, calls=%fused_computation | convolution fusion | flops 2684354560 | bytes 23724032 | tf_op jit(solution)/shard_map/dot_general | solution.py:200
  45.9 4.4 %all-to-all-done = bf16[8,32,1280]{2,1,0:T(8,128)(2,1)S(1)} async-done(((bf16[8,32,1280]{2,1,0:T(8,128)(2,1)}), bf16[8,32,1280]{2,1,0:T(8,128)(2,1)S(1)}, u32[]{:S(2)}, u32[]{:S(2)}) %all-to-all-start) | async-done | bytes 655392 | tf_op jit(solution)/shard_map/all_to_all | solution.py:196
  50.4 1.0 %add.1 = bf16[128,1280]{1,0:T(8,128)(2,1)} custom-call(s32[128,1]{1,0:T(8,128)S(1)} %get-tuple-element.15.refs_5_.place_ref, f32[128,1280]{1,0:T(8,128)S(1)} %fusion.base_ref, bf16[256,1280]{1,0:T(8,128)(2,1)S(1)} %bitcast.9), custom_call_target="tpu_custom_call" | custom-call | tf_op jit(solution)/shard_map/add/pallas_call | solution.py:201
  (24 shorter events, 4.7 us)
Async XLA Ops:
  0.0 6.6 %collective-permute-start.1 = (bf16[64,10240]{1,0:T(8,128)(2,1)}, bf16[64,10240]{1,0:T(8,128)(2,1)S(1)}, u32[]{:S(2)}, u32[]{:S(2)}) collective-permute-start(bf16[64,10240]{1,0:T(8,128)(2,1)} %bitcast.10), channel_id=1, source_target_pairs={{8,0},{0,8},{9,1},{1,9},{10,2},{2,10},{11,3},{3,11},{12,4},{4,12},... | collective-permute-start | bytes 3932168 | tf_op jit(solution)/shard_map/ppermute | solution.py:16
  0.5 6.1 %collective-permute-start = (bf16[64,8192]{1,0:T(8,128)(2,1)}, bf16[64,8192]{1,0:T(8,128)(2,1)S(1)}, u32[]{:S(2)}, u32[]{:S(2)}) collective-permute-start(bf16[64,8192]{1,0:T(8,128)(2,1)} %bitcast.12), channel_id=1, source_target_pairs={{8,0},{0,8},{9,1},{1,9},{10,2},{2,10},{11,3},{3,11},{12,4},{4,12},... | collective-permute-start | bytes 3145736 | tf_op jit(solution)/shard_map/ppermute | solution.py:16
  0.5 9.7 %collective-permute-start.3 = (bf16[16,8192]{1,0:T(8,128)(2,1)}, bf16[16,8192]{1,0:T(8,128)(2,1)S(1)}, u32[]{:S(2)}, u32[]{:S(2)}) collective-permute-start(bf16[16,8192]{1,0:T(8,128)(2,1)} %bitcast.14), channel_id=1, source_target_pairs={{2,0},{4,2},{6,4},{7,6},{5,7},{3,5},{1,3},{0,1},{10,8},{12,10},{14... | collective-permute-start | bytes 786440 | tf_op jit(solution)/shard_map/ppermute | solution.py:30
  3.5 8.1 %collective-permute-start.2 = (bf16[16,8192]{1,0:T(8,128)(2,1)}, bf16[16,8192]{1,0:T(8,128)(2,1)S(1)}, u32[]{:S(2)}, u32[]{:S(2)}) collective-permute-start(bf16[16,8192]{1,0:T(8,128)(2,1)} %bitcast.15), channel_id=1, source_target_pairs={{0,2},{2,4},{4,6},{6,7},{7,5},{5,3},{3,1},{1,0},{8,10},{10,12},{12... | collective-permute-start | bytes 786440 | tf_op jit(solution)/shard_map/ppermute | solution.py:30
  3.5 0.7 %copy-start.3 = (s32[2,12]{1,0:T(2,128)S(1)}, s32[2,12]{1,0:T(2,128)}, u32[]{:S(2)}) copy-start(s32[2,12]{1,0:T(2,128)} %ids_ref.1) | copy-start | bytes 292
  4.2 0.7 %copy-start.4 = (s32[1,12]{1,0:T(1,128)S(1)}, s32[1,12]{1,0:T(1,128)}, u32[]{:S(2)}) copy-start(s32[1,12]{1,0:T(1,128)} %lengths_ref.1) | copy-start | bytes 148
  4.9 0.7 %copy-start.5 = (s32[16]{0:T(128)S(1)}, s32[16]{0:T(128)}, u32[]{:S(2)}) copy-start(s32[16]{0:T(128)} %slots_ref.1) | copy-start | bytes 196
  6.6 1.3 %copy-start = (bf16[1,64,10240]{2,1,0:T(8,128)(2,1)S(1)}, bf16[1,64,10240]{2,1,0:T(8,128)(2,1)}, u32[]{:S(2)}) copy-start(bf16[1,64,10240]{2,1,0:T(8,128)(2,1)} %param.10) | copy-start | bytes 3932164
  7.9 1.2 %copy-start.1 = (bf16[1,8192,64]{1,2,0:T(8,128)(2,1)S(1)}, bf16[1,8192,64]{1,2,0:T(8,128)(2,1)}, u32[]{:S(2)}) copy-start(bf16[1,8192,64]{1,2,0:T(8,128)(2,1)} %param.9) | copy-start | bytes 3145732
  11.6 17.8 %copy-start.2 = (bf16[1,16,8192]{2,1,0:T(8,128)(2,1)S(1)}, bf16[1,16,8192]{2,1,0:T(8,128)(2,1)}, u32[]{:S(2)}) copy-start(bf16[1,16,8192]{2,1,0:T(8,128)(2,1)} %param.7) | copy-start | bytes 786436
  11.7 5.9 %collective-permute-start.4 = (bf16[16,4096]{1,0:T(8,128)(2,1)S(1)}, bf16[16,4096]{1,0:T(8,128)(2,1)S(1)}, u32[]{:S(2)}, u32[]{:S(2)}) collective-permute-start(bf16[16,4096]{1,0:T(8,128)(2,1)S(1)} %get-tuple-element.19), channel_id=1, source_target_pairs={{0,2},{2,4},{4,6},{6,7},{7,5},{5,3},{3,1},{1,0},{8,10},{10,12},{12... | collective-permute-start | bytes 393224 | tf_op jit(solution)/shard_map/ppermute | solution.py:35
  12.1 6.1 %collective-permute-start.7 = (bf16[16,4096]{1,0:T(8,128)(2,1)S(1)}, bf16[16,4096]{1,0:T(8,128)(2,1)S(1)}, u32[]{:S(2)}, u32[]{:S(2)}) collective-permute-start(bf16[16,4096]{1,0:T(8,128)(2,1)S(1)} %get-tuple-element.22), channel_id=1, source_target_pairs={{2,0},{4,2},{6,4},{7,6},{5,7},{3,5},{1,3},{0,1},{10,8},{12,10},{14... | collective-permute-start | bytes 393224 | tf_op jit(solution)/shard_map/ppermute | solution.py:35
  13.7 7.2 %collective-permute-start.5 = (bf16[16,4096]{1,0:T(8,128)(2,1)S(1)}, bf16[16,4096]{1,0:T(8,128)(2,1)S(1)}, u32[]{:S(2)}, u32[]{:S(2)}) collective-permute-start(bf16[16,4096]{1,0:T(8,128)(2,1)S(1)} %get-tuple-element.20), channel_id=1, source_target_pairs={{2,0},{4,2},{6,4},{7,6},{5,7},{3,5},{1,3},{0,1},{10,8},{12,10},{14... | collective-permute-start | bytes 393224 | tf_op jit(solution)/shard_map/ppermute | solution.py:35
  15.3 6.9 %collective-permute-start.6 = (bf16[16,4096]{1,0:T(8,128)(2,1)S(1)}, bf16[16,4096]{1,0:T(8,128)(2,1)S(1)}, u32[]{:S(2)}, u32[]{:S(2)}) collective-permute-start(bf16[16,4096]{1,0:T(8,128)(2,1)S(1)} %get-tuple-element.21), channel_id=1, source_target_pairs={{0,2},{2,4},{4,6},{6,7},{7,5},{5,3},{3,1},{1,0},{8,10},{10,12},{12... | collective-permute-start | bytes 393224 | tf_op jit(solution)/shard_map/ppermute | solution.py:35
  17.5 6.4 %collective-permute-start.8 = (bf16[16,4096]{1,0:T(8,128)(2,1)S(1)}, bf16[16,4096]{1,0:T(8,128)(2,1)S(1)}, u32[]{:S(2)}, u32[]{:S(2)}) collective-permute-start(bf16[16,4096]{1,0:T(8,128)(2,1)S(1)} %collective-permute-done.4.refs_3_), channel_id=1, source_target_pairs={{0,2},{2,4},{4,6},{6,7},{7,5},{5,3},{3,1},{1,0},{8,10},{10,12},{12... | collective-permute-start | bytes 393224 | tf_op jit(solution)/shard_map/ppermute | solution.py:35
  18.2 6.3 %collective-permute-start.11 = (bf16[16,4096]{1,0:T(8,128)(2,1)S(1)}, bf16[16,4096]{1,0:T(8,128)(2,1)S(1)}, u32[]{:S(2)}, u32[]{:S(2)}) collective-permute-start(bf16[16,4096]{1,0:T(8,128)(2,1)S(1)} %collective-permute-done.7.refs_6_), channel_id=1, source_target_pairs={{2,0},{4,2},{6,4},{7,6},{5,7},{3,5},{1,3},{0,1},{10,8},{12,10},{14... | collective-permute-start | bytes 393224 | tf_op jit(solution)/shard_map/ppermute | solution.py:35
  21.0 5.4 %collective-permute-start.9 = (bf16[16,4096]{1,0:T(8,128)(2,1)S(1)}, bf16[16,4096]{1,0:T(8,128)(2,1)S(1)}, u32[]{:S(2)}, u32[]{:S(2)}) collective-permute-start(bf16[16,4096]{1,0:T(8,128)(2,1)S(1)} %collective-permute-done.5.refs_4_), channel_id=1, source_target_pairs={{2,0},{4,2},{6,4},{7,6},{5,7},{3,5},{1,3},{0,1},{10,8},{12,10},{14... | collective-permute-start | bytes 393224 | tf_op jit(solution)/shard_map/ppermute | solution.py:35
  22.2 5.0 %collective-permute-start.10 = (bf16[16,4096]{1,0:T(8,128)(2,1)S(1)}, bf16[16,4096]{1,0:T(8,128)(2,1)S(1)}, u32[]{:S(2)}, u32[]{:S(2)}) collective-permute-start(bf16[16,4096]{1,0:T(8,128)(2,1)S(1)} %collective-permute-done.6.refs_5_), channel_id=1, source_target_pairs={{0,2},{2,4},{4,6},{6,7},{7,5},{5,3},{3,1},{1,0},{8,10},{10,12},{12... | collective-permute-start | bytes 393224 | tf_op jit(solution)/shard_map/ppermute | solution.py:35
  23.9 5.0 %collective-permute-start.12 = (bf16[16,4096]{1,0:T(8,128)(2,1)S(1)}, bf16[16,4096]{1,0:T(8,128)(2,1)S(1)}, u32[]{:S(2)}, u32[]{:S(2)}) collective-permute-start(bf16[16,4096]{1,0:T(8,128)(2,1)S(1)} %collective-permute-done.8.refs_7_), channel_id=1, source_target_pairs={{0,2},{2,4},{4,6},{6,7},{7,5},{5,3},{3,1},{1,0},{8,10},{10,12},{12... | collective-permute-start | bytes 393224 | tf_op jit(solution)/shard_map/ppermute | solution.py:37
  24.4 5.0 %collective-permute-start.13 = (bf16[16,4096]{1,0:T(8,128)(2,1)S(1)}, bf16[16,4096]{1,0:T(8,128)(2,1)S(1)}, u32[]{:S(2)}, u32[]{:S(2)}) collective-permute-start(bf16[16,4096]{1,0:T(8,128)(2,1)S(1)} %collective-permute-done.11.refs_10_), channel_id=1, source_target_pairs={{2,0},{4,2},{6,4},{7,6},{5,7},{3,5},{1,3},{0,1},{10,8},{12,10},{14... | collective-permute-start | bytes 393224 | tf_op jit(solution)/shard_map/ppermute | solution.py:37
  31.8 18.6 %all-to-all-start = ((bf16[8,32,1280]{2,1,0:T(8,128)(2,1)}), bf16[8,32,1280]{2,1,0:T(8,128)(2,1)S(1)}, u32[]{:S(2)}, u32[]{:S(2)}) async-start(bf16[8,32,1280]{2,1,0:T(8,128)(2,1)} %get-tuple-element.24), calls=%async_computation | async-start | bytes 1310720 | tf_op jit(solution)/shard_map/all_to_all | solution.py:196

commit v18 on v17

--- a/solution.py
+++ b/solution.py
@@ -54,6 +54,14 @@
     )(*arrays, *values)
 
 
+def listed(n):
+    return [i // 2 + i % 2 * (n // 2) for i in range(n)]
+
+
+def listed_place(i, n):
+    return jnp.where(i < n // 2, 2 * i, 2 * i - n + 1)
+
+
 def ring_place(i, n):
     return jnp.where(lax.rem(i, 2) == 0, i // 2, n - 1 - i // 2)
 
@@ -91,7 +99,7 @@
         slot = slots_ref[ids_ref[group, request]]
         end = start + lengths_ref[0, request]
         panel = lax.rem(slot // tp - group + groups, groups)
-        first = (ring_place(lax.rem(slot, tp), tp) * groups + panel) * longest - start
+        first = (listed_place(lax.rem(slot, tp), tp) * groups + panel) * longest - start
         row = jnp.where((along >= start) & (along < end), first + along, row)
         column = jnp.where((down >= start) & (down < end), first + down, column)
         return end, row, column
@@ -110,14 +118,14 @@
         start = pl.multiple_of(source * rows, rows)
         tokens_ref[pl.ds(start, rows), column : column + piece.shape[1]] = piece[...]
     low = jnp.dot(tokens_ref[...], down_ref[...], preferred_element_type=jnp.float32)
-    place = ring_place(lax.axis_index("tp"), parts)
+    place = listed_place(lax.axis_index("tp"), parts)
     here = lax.broadcasted_iota(jnp.int32, (slots, tok_all), 0) + place * slots
     chosen = (here == place_ref[...]).astype(jnp.bfloat16)
     picked = jnp.dot(chosen, low.astype(jnp.bfloat16), preferred_element_type=jnp.float32)
     row_panel = lax.broadcasted_iota(jnp.int32, picked.shape, 0) // (slots // groups)
     rank_panel = lax.broadcasted_iota(jnp.int32, picked.shape, 1) // rank
     picked = jnp.where(row_panel == rank_panel, picked, 0.0).astype(jnp.bfloat16)
-    for part, owner in enumerate(ring_of(parts)):
+    for part, owner in enumerate(listed(parts)):
         out_ref[part] = jnp.dot(
             picked,
             up_ref[:, owner * columns : (owner + 1) * columns],
@@ -194,7 +202,7 @@
         name="lift",
     )(row, down, up, *pieces)
     lifts = lax.all_to_all(
-        lifts, "tp", split_axis=0, concat_axis=0, axis_index_groups=[ring_of(tp)], tiled=True
+        lifts, "tp", split_axis=0, concat_axis=0, axis_index_groups=[listed(tp)], tiled=True
     )
 
     base = jnp.dot(gathered, base_projection_weight, preferred_element_type=jnp.float32)

time: 51.7 us -> 53.1 us (1.027)
  waiting for transfers between devices: 14.2 us -> 15.6 us
    all_to_all x1, waiting for transfers between devices: 4.42 us -> 5.87 us  [on_device(): lax.all_to_all(lifts, 'tp', split_axis=0, concat_axis=0, axis_index_group...]
  transfers between devices with their start and end apart: 15 -> 15, of which waited for: 11 -> 11; matrix products, arithmetic and copies ran while one was open for 17% -> 16% of each run, Pallas kernels for 3% -> 3%
where the time goes in v18:
time: 53.1 us; the launch traced here: 52.8 us
  starting transfers between devices  19 us (36%)
  waiting for transfers between devices  15.6 us (29%)
  matrix products  8.53 us (16%)
  Pallas kernels  5.09 us (10%)
  local copies, waits for them, and re-layouts  4.53 us (9%)
    dot_general x1, matrix products, on_device(): jnp.dot(gathered, base_projection_weight, preferred_element_type=jnp.floa...  8.53 us
    ppermute x8, starting transfers between devices, ring_gather(): lax.ppermute(x, axis, way)  7.8 us
    all_to_all x1, waiting for transfers between devices, on_device(): lax.all_to_all(lifts, 'tp', split_axis=0, concat_axis=0, axis_index_group...  5.87 us
    ppermute x8, waiting for transfers between devices, ring_gather(): lax.ppermute(x, axis, way)  5.71 us
    all_to_all x1, starting transfers between devices, on_device(): lax.all_to_all(lifts, 'tp', split_axis=0, concat_axis=0, axis_index_group...  5.63 us
    unnamed x12, local copies, waits for them, and re-layouts  4.53 us
    ppermute x1, starting transfers between devices, ring_gather(): lax.ppermute(block, axis, down)  2.97 us
    pallas_call x1, Pallas kernels, on_device(): pl.pallas_call(functools.partial(lift_kernel, groups), out_shape=[jax.Sha...  2.35 us
  transfers between devices with their start and end apart: 15, of which 11 were waited for; matrix products, arithmetic and copies ran while one was open for 16% of the time, Pallas kernels for 3%

profile of v18, /device:TPU:0, one launch (start us, length us, event | category | flops | bytes accessed | tf_op | source)
XLA Modules:
  0.0 52.8 jit_solution(15768375105806426048)
XLA Ops:
  0.5 3.0 %collective-permute-start.3 = (bf16[16,8192]{1,0:T(8,128)(2,1)}, bf16[16,8192]{1,0:T(8,128)(2,1)S(1)}, u32[]{:S(2)}, u32[]{:S(2)}) collective-permute-start(bf16[16,8192]{1,0:T(8,128)(2,1)} %bitcast.14), channel_id=1, source_target_pairs={{2,0},{4,2},{6,4},{7,6},{5,7},{3,5},{1,3},{0,1},{10,8},{12,10},{14... | collective-permute-start | bytes 786440 | tf_op jit(solution)/shard_map/ppermute | solution.py:30
  3.5 0.7 %copy-done.3 = s32[2,12]{1,0:T(2,128)S(1)} copy-done((s32[2,12]{1,0:T(2,128)S(1)}, s32[2,12]{1,0:T(2,128)}, u32[]{:S(2)}) %copy-start.3) | copy-done | bytes 120
  4.2 0.7 %copy-done.4 = s32[1,12]{1,0:T(1,128)S(1)} copy-done((s32[1,12]{1,0:T(1,128)S(1)}, s32[1,12]{1,0:T(1,128)}, u32[]{:S(2)}) %copy-start.4) | copy-done | bytes 72
  5.5 1.0 %place.1 = (s32[1,128]{1,0:T(1,128)S(1)}, s32[128,1]{1,0:T(8,128)S(1)}) custom-call(s32[2,12]{1,0:T(2,128)S(1)} %copy-done.3, s32[1,12]{1,0:T(1,128)S(1)} %copy-done.4, s32[16]{0:T(128)S(1)} %copy-done.5), custom_call_target="tpu_custom_call" | custom-call | tf_op jit(solution)/shard_map/place/pallas_call | solution.py:175
  6.5 1.3 %copy-done = bf16[1,64,10240]{2,1,0:T(8,128)(2,1)S(1)} copy-done((bf16[1,64,10240]{2,1,0:T(8,128)(2,1)S(1)}, bf16[1,64,10240]{2,1,0:T(8,128)(2,1)}, u32[]{:S(2)}) %copy-start) | copy-done | bytes 1310744
  7.8 1.2 %copy-done.1 = bf16[1,8192,64]{1,2,0:T(8,128)(2,1)S(1)} copy-done((bf16[1,8192,64]{1,2,0:T(8,128)(2,1)S(1)}, bf16[1,8192,64]{1,2,0:T(8,128)(2,1)}, u32[]{:S(2)}) %copy-start.1) | copy-done | bytes 1048600
  9.1 0.7 %stack.1 = (bf16[8192,128]{1,0:T(8,128)(2,1)S(1)}, bf16[128,10240]{1,0:T(8,128)(2,1)S(1)}) custom-call(bf16[64,8192]{1,0:T(8,128)(2,1)S(1)} %bitcast.13, bf16[64,8192]{1,0:T(8,128)(2,1)S(1)} %collective-permute-done.refs_1_, bf16[64,10240]{1,0:T(8,128)(2,1)S(1)} %bitcast.11, bf16[64,10240]{1,0:T(8,128)(2,1)S(1)} %collective-permute-done.1.refs_3_), custom_call_target="tpu_custom_call" | custom-call | tf_op jit(solution)/shard_map/stack/pallas_call | solution.py:164
  10.2 1.4 %collective-permute-done.2.refs_0_.refs_1_ = bf16[16,8192]{1,0:T(8,128)(2,1)S(1)} collective-permute-done((bf16[16,8192]{1,0:T(8,128)(2,1)}, bf16[16,8192]{1,0:T(8,128)(2,1)S(1)}, u32[]{:S(2)}, u32[]{:S(2)}) %collective-permute-start.2) | collective-permute-done | bytes 262176 | tf_op jit(solution)/shard_map/ppermute | solution.py:30
  12.1 1.7 %collective-permute-start.7 = (bf16[16,4096]{1,0:T(8,128)(2,1)S(1)}, bf16[16,4096]{1,0:T(8,128)(2,1)S(1)}, u32[]{:S(2)}, u32[]{:S(2)}) collective-permute-start(bf16[16,4096]{1,0:T(8,128)(2,1)S(1)} %get-tuple-element.22), channel_id=1, source_target_pairs={{2,0},{4,2},{6,4},{7,6},{5,7},{3,5},{1,3},{0,1},{10,8},{12,10},{14... | collective-permute-start | bytes 393224 | tf_op jit(solution)/shard_map/ppermute | solution.py:35
  13.7 1.6 %collective-permute-start.5 = (bf16[16,4096]{1,0:T(8,128)(2,1)S(1)}, bf16[16,4096]{1,0:T(8,128)(2,1)S(1)}, u32[]{:S(2)}, u32[]{:S(2)}) collective-permute-start(bf16[16,4096]{1,0:T(8,128)(2,1)S(1)} %get-tuple-element.20), channel_id=1, source_target_pairs={{2,0},{4,2},{6,4},{7,6},{5,7},{3,5},{1,3},{0,1},{10,8},{12,10},{14... | collective-permute-start | bytes 393224 | tf_op jit(solution)/shard_map/ppermute | solution.py:35
  15.8 1.7 %collective-permute-done.4.refs_3_ = bf16[16,4096]{1,0:T(8,128)(2,1)S(1)} collective-permute-done((bf16[16,4096]{1,0:T(8,128)(2,1)S(1)}, bf16[16,4096]{1,0:T(8,128)(2,1)S(1)}, u32[]{:S(2)}, u32[]{:S(2)}) %collective-permute-start.4) | collective-permute-done | bytes 131104 | tf_op jit(solution)/shard_map/ppermute | solution.py:35
  18.1 1.4 %collective-permute-start.11 = (bf16[16,4096]{1,0:T(8,128)(2,1)S(1)}, bf16[16,4096]{1,0:T(8,128)(2,1)S(1)}, u32[]{:S(2)}, u32[]{:S(2)}) collective-permute-start(bf16[16,4096]{1,0:T(8,128)(2,1)S(1)} %collective-permute-done.7.refs_6_), channel_id=1, source_target_pairs={{2,0},{4,2},{6,4},{7,6},{5,7},{3,5},{1,3},{0,1},{10,8},{12,10},{14... | collective-permute-start | bytes 393224 | tf_op jit(solution)/shard_map/ppermute | solution.py:35
  19.5 1.4 %collective-permute-done.5.refs_4_ = bf16[16,4096]{1,0:T(8,128)(2,1)S(1)} collective-permute-done((bf16[16,4096]{1,0:T(8,128)(2,1)S(1)}, bf16[16,4096]{1,0:T(8,128)(2,1)S(1)}, u32[]{:S(2)}, u32[]{:S(2)}) %collective-permute-start.5) | collective-permute-done | bytes 131104 | tf_op jit(solution)/shard_map/ppermute | solution.py:35
  20.9 1.3 %collective-permute-start.9 = (bf16[16,4096]{1,0:T(8,128)(2,1)S(1)}, bf16[16,4096]{1,0:T(8,128)(2,1)S(1)}, u32[]{:S(2)}, u32[]{:S(2)}) collective-permute-start(bf16[16,4096]{1,0:T(8,128)(2,1)S(1)} %collective-permute-done.5.refs_4_), channel_id=1, source_target_pairs={{2,0},{4,2},{6,4},{7,6},{5,7},{3,5},{1,3},{0,1},{10,8},{12,10},{14... | collective-permute-start | bytes 393224 | tf_op jit(solution)/shard_map/ppermute | solution.py:35
  22.2 0.7 %collective-permute-start.10 = (bf16[16,4096]{1,0:T(8,128)(2,1)S(1)}, bf16[16,4096]{1,0:T(8,128)(2,1)S(1)}, u32[]{:S(2)}, u32[]{:S(2)}) collective-permute-start(bf16[16,4096]{1,0:T(8,128)(2,1)S(1)} %collective-permute-done.6.refs_5_), channel_id=1, source_target_pairs={{0,2},{2,4},{4,6},{6,7},{7,5},{5,3},{3,1},{1,0},{8,10},{10,12},{12... | collective-permute-start | bytes 393224 | tf_op jit(solution)/shard_map/ppermute | solution.py:35
  23.0 0.9 %collective-permute-done.8.refs_7_ = bf16[16,4096]{1,0:T(8,128)(2,1)S(1)} collective-permute-done((bf16[16,4096]{1,0:T(8,128)(2,1)S(1)}, bf16[16,4096]{1,0:T(8,128)(2,1)S(1)}, u32[]{:S(2)}, u32[]{:S(2)}) %collective-permute-start.8) | collective-permute-done | bytes 131104 | tf_op jit(solution)/shard_map/ppermute | solution.py:35
  24.4 1.5 %collective-permute-start.13 = (bf16[16,4096]{1,0:T(8,128)(2,1)S(1)}, bf16[16,4096]{1,0:T(8,128)(2,1)S(1)}, u32[]{:S(2)}, u32[]{:S(2)}) collective-permute-start(bf16[16,4096]{1,0:T(8,128)(2,1)S(1)} %collective-permute-done.11.refs_10_), channel_id=1, source_target_pairs={{2,0},{4,2},{6,4},{7,6},{5,7},{3,5},{1,3},{0,1},{10,8},{12,10},{14... | collective-permute-start | bytes 393224 | tf_op jit(solution)/shard_map/ppermute | solution.py:37
  26.3 0.9 %collective-permute-done.10.refs_9_ = bf16[16,4096]{1,0:T(8,128)(2,1)S(1)} collective-permute-done((bf16[16,4096]{1,0:T(8,128)(2,1)S(1)}, bf16[16,4096]{1,0:T(8,128)(2,1)S(1)}, u32[]{:S(2)}, u32[]{:S(2)}) %collective-permute-start.10) | collective-permute-done | bytes 131104 | tf_op jit(solution)/shard_map/ppermute | solution.py:35
  27.2 1.6 %collective-permute-done.12.refs_11_ = bf16[16,4096]{1,0:T(8,128)(2,1)S(1)} collective-permute-done((bf16[16,4096]{1,0:T(8,128)(2,1)S(1)}, bf16[16,4096]{1,0:T(8,128)(2,1)S(1)}, u32[]{:S(2)}, u32[]{:S(2)}) %collective-permute-start.12) | collective-permute-done | bytes 131104 | tf_op jit(solution)/shard_map/ppermute | solution.py:37
  29.4 2.4 %lift.1 = (bf16[128,8192]{1,0:T(8,128)(2,1)S(1)}, bf16[8,32,1280]{2,1,0:T(8,128)(2,1)}) custom-call(s32[1,128]{1,0:T(1,128)S(1)} %get-tuple-element.16.refs_4_.place_ref, bf16[8192,128]{1,0:T(8,128)(2,1)S(1)} %get-tuple-element.17.refs_2_.down_ref, bf16[128,10240]{1,0:T(8,128)(2,1)S(1)} %get-tuple-element.18.refs_3_.up_ref, bf16[16,8192]{1,0:T(8,128)(2,1)S(1)} %bitcast.16, ...), custom_call_target="tpu_custom_call" | custom-call | flops 352321536 | bytes 4718592 | tf_op jit(solution)/shard_map/lift/pallas_call | solution.py:188
  31.8 5.6 %all-to-all-start = ((bf16[8,32,1280]{2,1,0:T(8,128)(2,1)}), bf16[8,32,1280]{2,1,0:T(8,128)(2,1)S(1)}, u32[]{:S(2)}, u32[]{:S(2)}) async-start(bf16[8,32,1280]{2,1,0:T(8,128)(2,1)} %get-tuple-element.24), calls=%async_computation | async-start | bytes 1310720 | tf_op jit(solution)/shard_map/all_to_all | solution.py:204
  37.4 8.5 %fusion.base_ref = f32[128,1280]{1,0:T(8,128)S(1)} fusion(bf16[128,8192]{1,0:T(8,128)(2,1)S(1)} %get-tuple-element.23, bf16[8192,1280]{1,0:T(8,128)(2,1)} %param.8), kind=kOutput, calls=%fused_computation | convolution fusion | flops 2684354560 | bytes 23724032 | tf_op jit(solution)/shard_map/dot_general | solution.py:208
  45.9 5.9 %all-to-all-done = bf16[8,32,1280]{2,1,0:T(8,128)(2,1)S(1)} async-done(((bf16[8,32,1280]{2,1,0:T(8,128)(2,1)}), bf16[8,32,1280]{2,1,0:T(8,128)(2,1)S(1)}, u32[]{:S(2)}, u32[]{:S(2)}) %all-to-all-start) | async-done | bytes 655392 | tf_op jit(solution)/shard_map/all_to_all | solution.py:204
  51.8 1.0 %add.1 = bf16[128,1280]{1,0:T(8,128)(2,1)} custom-call(s32[128,1]{1,0:T(8,128)S(1)} %get-tuple-element.15.refs_5_.place_ref, f32[128,1280]{1,0:T(8,128)S(1)} %fusion.base_ref, bf16[256,1280]{1,0:T(8,128)(2,1)S(1)} %bitcast.9), custom_call_target="tpu_custom_call" | custom-call | tf_op jit(solution)/shard_map/add/pallas_call | solution.py:209
  (24 shorter events, 4.6 us)
Async XLA Ops:
  0.0 6.5 %collective-permute-start.1 = (bf16[64,10240]{1,0:T(8,128)(2,1)}, bf16[64,10240]{1,0:T(8,128)(2,1)S(1)}, u32[]{:S(2)}, u32[]{:S(2)}) collective-permute-start(bf16[64,10240]{1,0:T(8,128)(2,1)} %bitcast.10), channel_id=1, source_target_pairs={{8,0},{0,8},{9,1},{1,9},{10,2},{2,10},{11,3},{3,11},{12,4},{4,12},... | collective-permute-start | bytes 3932168 | tf_op jit(solution)/shard_map/ppermute | solution.py:16
  0.5 6.1 %collective-permute-start = (bf16[64,8192]{1,0:T(8,128)(2,1)}, bf16[64,8192]{1,0:T(8,128)(2,1)S(1)}, u32[]{:S(2)}, u32[]{:S(2)}) collective-permute-start(bf16[64,8192]{1,0:T(8,128)(2,1)} %bitcast.12), channel_id=1, source_target_pairs={{8,0},{0,8},{9,1},{1,9},{10,2},{2,10},{11,3},{3,11},{12,4},{4,12},... | collective-permute-start | bytes 3145736 | tf_op jit(solution)/shard_map/ppermute | solution.py:16
  0.5 9.7 %collective-permute-start.3 = (bf16[16,8192]{1,0:T(8,128)(2,1)}, bf16[16,8192]{1,0:T(8,128)(2,1)S(1)}, u32[]{:S(2)}, u32[]{:S(2)}) collective-permute-start(bf16[16,8192]{1,0:T(8,128)(2,1)} %bitcast.14), channel_id=1, source_target_pairs={{2,0},{4,2},{6,4},{7,6},{5,7},{3,5},{1,3},{0,1},{10,8},{12,10},{14... | collective-permute-start | bytes 786440 | tf_op jit(solution)/shard_map/ppermute | solution.py:30
  3.5 8.1 %collective-permute-start.2 = (bf16[16,8192]{1,0:T(8,128)(2,1)}, bf16[16,8192]{1,0:T(8,128)(2,1)S(1)}, u32[]{:S(2)}, u32[]{:S(2)}) collective-permute-start(bf16[16,8192]{1,0:T(8,128)(2,1)} %bitcast.15), channel_id=1, source_target_pairs={{0,2},{2,4},{4,6},{6,7},{7,5},{5,3},{3,1},{1,0},{8,10},{10,12},{12... | collective-permute-start | bytes 786440 | tf_op jit(solution)/shard_map/ppermute | solution.py:30
  3.5 0.7 %copy-start.3 = (s32[2,12]{1,0:T(2,128)S(1)}, s32[2,12]{1,0:T(2,128)}, u32[]{:S(2)}) copy-start(s32[2,12]{1,0:T(2,128)} %ids_ref.1) | copy-start | bytes 292
  4.2 0.7 %copy-start.4 = (s32[1,12]{1,0:T(1,128)S(1)}, s32[1,12]{1,0:T(1,128)}, u32[]{:S(2)}) copy-start(s32[1,12]{1,0:T(1,128)} %lengths_ref.1) | copy-start | bytes 148
  4.9 0.7 %copy-start.5 = (s32[16]{0:T(128)S(1)}, s32[16]{0:T(128)}, u32[]{:S(2)}) copy-start(s32[16]{0:T(128)} %slots_ref.1) | copy-start | bytes 196
  6.5 1.3 %copy-start = (bf16[1,64,10240]{2,1,0:T(8,128)(2,1)S(1)}, bf16[1,64,10240]{2,1,0:T(8,128)(2,1)}, u32[]{:S(2)}) copy-start(bf16[1,64,10240]{2,1,0:T(8,128)(2,1)} %param.10) | copy-start | bytes 3932164
  7.8 1.2 %copy-start.1 = (bf16[1,8192,64]{1,2,0:T(8,128)(2,1)S(1)}, bf16[1,8192,64]{1,2,0:T(8,128)(2,1)}, u32[]{:S(2)}) copy-start(bf16[1,8192,64]{1,2,0:T(8,128)(2,1)} %param.9) | copy-start | bytes 3145732
  11.6 17.8 %copy-start.2 = (bf16[1,16,8192]{2,1,0:T(8,128)(2,1)S(1)}, bf16[1,16,8192]{2,1,0:T(8,128)(2,1)}, u32[]{:S(2)}) copy-start(bf16[1,16,8192]{2,1,0:T(8,128)(2,1)} %param.7) | copy-start | bytes 786436
  11.7 5.9 %collective-permute-start.4 = (bf16[16,4096]{1,0:T(8,128)(2,1)S(1)}, bf16[16,4096]{1,0:T(8,128)(2,1)S(1)}, u32[]{:S(2)}, u32[]{:S(2)}) collective-permute-start(bf16[16,4096]{1,0:T(8,128)(2,1)S(1)} %get-tuple-element.19), channel_id=1, source_target_pairs={{0,2},{2,4},{4,6},{6,7},{7,5},{5,3},{3,1},{1,0},{8,10},{10,12},{12... | collective-permute-start | bytes 393224 | tf_op jit(solution)/shard_map/ppermute | solution.py:35
  12.1 6.0 %collective-permute-start.7 = (bf16[16,4096]{1,0:T(8,128)(2,1)S(1)}, bf16[16,4096]{1,0:T(8,128)(2,1)S(1)}, u32[]{:S(2)}, u32[]{:S(2)}) collective-permute-start(bf16[16,4096]{1,0:T(8,128)(2,1)S(1)} %get-tuple-element.22), channel_id=1, source_target_pairs={{2,0},{4,2},{6,4},{7,6},{5,7},{3,5},{1,3},{0,1},{10,8},{12,10},{14... | collective-permute-start | bytes 393224 | tf_op jit(solution)/shard_map/ppermute | solution.py:35
  13.7 7.2 %collective-permute-start.5 = (bf16[16,4096]{1,0:T(8,128)(2,1)S(1)}, bf16[16,4096]{1,0:T(8,128)(2,1)S(1)}, u32[]{:S(2)}, u32[]{:S(2)}) collective-permute-start(bf16[16,4096]{1,0:T(8,128)(2,1)S(1)} %get-tuple-element.20), channel_id=1, source_target_pairs={{2,0},{4,2},{6,4},{7,6},{5,7},{3,5},{1,3},{0,1},{10,8},{12,10},{14... | collective-permute-start | bytes 393224 | tf_op jit(solution)/shard_map/ppermute | solution.py:35
  15.3 6.9 %collective-permute-start.6 = (bf16[16,4096]{1,0:T(8,128)(2,1)S(1)}, bf16[16,4096]{1,0:T(8,128)(2,1)S(1)}, u32[]{:S(2)}, u32[]{:S(2)}) collective-permute-start(bf16[16,4096]{1,0:T(8,128)(2,1)S(1)} %get-tuple-element.21), channel_id=1, source_target_pairs={{0,2},{2,4},{4,6},{6,7},{7,5},{5,3},{3,1},{1,0},{8,10},{10,12},{12... | collective-permute-start | bytes 393224 | tf_op jit(solution)/shard_map/ppermute | solution.py:35
  17.5 6.4 %collective-permute-start.8 = (bf16[16,4096]{1,0:T(8,128)(2,1)S(1)}, bf16[16,4096]{1,0:T(8,128)(2,1)S(1)}, u32[]{:S(2)}, u32[]{:S(2)}) collective-permute-start(bf16[16,4096]{1,0:T(8,128)(2,1)S(1)} %collective-permute-done.4.refs_3_), channel_id=1, source_target_pairs={{0,2},{2,4},{4,6},{6,7},{7,5},{5,3},{3,1},{1,0},{8,10},{10,12},{12... | collective-permute-start | bytes 393224 | tf_op jit(solution)/shard_map/ppermute | solution.py:35
  18.1 6.3 %collective-permute-start.11 = (bf16[16,4096]{1,0:T(8,128)(2,1)S(1)}, bf16[16,4096]{1,0:T(8,128)(2,1)S(1)}, u32[]{:S(2)}, u32[]{:S(2)}) collective-permute-start(bf16[16,4096]{1,0:T(8,128)(2,1)S(1)} %collective-permute-done.7.refs_6_), channel_id=1, source_target_pairs={{2,0},{4,2},{6,4},{7,6},{5,7},{3,5},{1,3},{0,1},{10,8},{12,10},{14... | collective-permute-start | bytes 393224 | tf_op jit(solution)/shard_map/ppermute | solution.py:35
  20.9 5.4 %collective-permute-start.9 = (bf16[16,4096]{1,0:T(8,128)(2,1)S(1)}, bf16[16,4096]{1,0:T(8,128)(2,1)S(1)}, u32[]{:S(2)}, u32[]{:S(2)}) collective-permute-start(bf16[16,4096]{1,0:T(8,128)(2,1)S(1)} %collective-permute-done.5.refs_4_), channel_id=1, source_target_pairs={{2,0},{4,2},{6,4},{7,6},{5,7},{3,5},{1,3},{0,1},{10,8},{12,10},{14... | collective-permute-start | bytes 393224 | tf_op jit(solution)/shard_map/ppermute | solution.py:35
  22.2 5.0 %collective-permute-start.10 = (bf16[16,4096]{1,0:T(8,128)(2,1)S(1)}, bf16[16,4096]{1,0:T(8,128)(2,1)S(1)}, u32[]{:S(2)}, u32[]{:S(2)}) collective-permute-start(bf16[16,4096]{1,0:T(8,128)(2,1)S(1)} %collective-permute-done.6.refs_5_), channel_id=1, source_target_pairs={{0,2},{2,4},{4,6},{6,7},{7,5},{5,3},{3,1},{1,0},{8,10},{10,12},{12... | collective-permute-start | bytes 393224 | tf_op jit(solution)/shard_map/ppermute | solution.py:35
  23.9 5.0 %collective-permute-start.12 = (bf16[16,4096]{1,0:T(8,128)(2,1)S(1)}, bf16[16,4096]{1,0:T(8,128)(2,1)S(1)}, u32[]{:S(2)}, u32[]{:S(2)}) collective-permute-start(bf16[16,4096]{1,0:T(8,128)(2,1)S(1)} %collective-permute-done.8.refs_7_), channel_id=1, source_target_pairs={{0,2},{2,4},{4,6},{6,7},{7,5},{5,3},{3,1},{1,0},{8,10},{10,12},{12... | collective-permute-start | bytes 393224 | tf_op jit(solution)/shard_map/ppermute | solution.py:37
  24.4 5.0 %collective-permute-start.13 = (bf16[16,4096]{1,0:T(8,128)(2,1)S(1)}, bf16[16,4096]{1,0:T(8,128)(2,1)S(1)}, u32[]{:S(2)}, u32[]{:S(2)}) collective-permute-start(bf16[16,4096]{1,0:T(8,128)(2,1)S(1)} %collective-permute-done.11.refs_10_), channel_id=1, source_target_pairs={{2,0},{4,2},{6,4},{7,6},{5,7},{3,5},{1,3},{0,1},{10,8},{12,10},{14... | collective-permute-start | bytes 393224 | tf_op jit(solution)/shard_map/ppermute | solution.py:37
  31.8 20.0 %all-to-all-start = ((bf16[8,32,1280]{2,1,0:T(8,128)(2,1)}), bf16[8,32,1280]{2,1,0:T(8,128)(2,1)S(1)}, u32[]{:S(2)}, u32[]{:S(2)}) async-start(bf16[8,32,1280]{2,1,0:T(8,128)(2,1)} %get-tuple-element.24), calls=%async_computation | async-start | bytes 1310720 | tf_op jit(solution)/shard_map/all_to_all | solution.py:204

commit v19 on v17

--- a/solution.py
+++ b/solution.py
@@ -58,6 +58,16 @@
     return jnp.where(lax.rem(i, 2) == 0, i // 2, n - 1 - i // 2)
 
 
+def exchange_groups(groups, n):
+    ring = ring_of(n)
+    return [[g * n + ring[-p if g % 2 else p] for p in range(n)] for g in range(groups)]
+
+
+def exchange_place(i, n):
+    place = ring_place(i, n)
+    return jnp.where(lax.rem(lax.axis_index("grp"), 2) == 0, place, lax.rem(n - place, n))
+
+
 def ring_sources(axis, half):
     n = lax.axis_size(axis)
     place = ring_place(lax.axis_index(axis), n)
@@ -91,7 +101,7 @@
         slot = slots_ref[ids_ref[group, request]]
         end = start + lengths_ref[0, request]
         panel = lax.rem(slot // tp - group + groups, groups)
-        first = (ring_place(lax.rem(slot, tp), tp) * groups + panel) * longest - start
+        first = (exchange_place(lax.rem(slot, tp), tp) * groups + panel) * longest - start
         row = jnp.where((along >= start) & (along < end), first + along, row)
         column = jnp.where((down >= start) & (down < end), first + down, column)
         return end, row, column
@@ -110,15 +120,15 @@
         start = pl.multiple_of(source * rows, rows)
         tokens_ref[pl.ds(start, rows), column : column + piece.shape[1]] = piece[...]
     low = jnp.dot(tokens_ref[...], down_ref[...], preferred_element_type=jnp.float32)
-    place = ring_place(lax.axis_index("tp"), parts)
+    place = exchange_place(lax.axis_index("tp"), parts)
     here = lax.broadcasted_iota(jnp.int32, (slots, tok_all), 0) + place * slots
     chosen = (here == place_ref[...]).astype(jnp.bfloat16)
     picked = jnp.dot(chosen, low.astype(jnp.bfloat16), preferred_element_type=jnp.float32)
     row_panel = lax.broadcasted_iota(jnp.int32, picked.shape, 0) // (slots // groups)
     rank_panel = lax.broadcasted_iota(jnp.int32, picked.shape, 1) // rank
     picked = jnp.where(row_panel == rank_panel, picked, 0.0).astype(jnp.bfloat16)
-    for part, owner in enumerate(ring_of(parts)):
-        out_ref[part] = jnp.dot(
+    for owner in range(parts):
+        out_ref[exchange_place(jnp.int32(owner), parts)] = jnp.dot(
             picked,
             up_ref[:, owner * columns : (owner + 1) * columns],
             preferred_element_type=jnp.float32,
@@ -194,7 +204,12 @@
         name="lift",
     )(row, down, up, *pieces)
     lifts = lax.all_to_all(
-        lifts, "tp", split_axis=0, concat_axis=0, axis_index_groups=[ring_of(tp)], tiled=True
+        lifts,
+        ("grp", "tp"),
+        split_axis=0,
+        concat_axis=0,
+        axis_index_groups=exchange_groups(groups, tp),
+        tiled=True,
     )
 
     base = jnp.dot(gathered, base_projection_weight, preferred_element_type=jnp.float32)

time: 51.7 us -> 51.7 us (level)
  no operation moved by 1% of the time
where the time goes in v19:
time: 51.7 us; the launch traced here: 51.4 us
  starting transfers between devices  18.9 us (37%)
  waiting for transfers between devices  14.2 us (27%)
  matrix products  8.53 us (16%)
  Pallas kernels  5.16 us (10%)
  local copies, waits for them, and re-layouts  4.53 us (9%)
    dot_general x1, matrix products, on_device(): jnp.dot(gathered, base_projection_weight, preferred_element_type=jnp.floa...  8.53 us
    ppermute x8, starting transfers between devices, ring_gather(): lax.ppermute(x, axis, way)  7.73 us
    ppermute x8, waiting for transfers between devices, ring_gather(): lax.ppermute(x, axis, way)  5.78 us
    all_to_all x1, starting transfers between devices, on_device(): lax.all_to_all(lifts, ('grp', 'tp'), split_axis=0, concat_axis=0, axis_in...  5.64 us
    unnamed x12, local copies, waits for them, and re-layouts  4.53 us
    all_to_all x1, waiting for transfers between devices, on_device(): lax.all_to_all(lifts, ('grp', 'tp'), split_axis=0, concat_axis=0, axis_in...  4.46 us
    ppermute x1, starting transfers between devices, ring_gather(): lax.ppermute(block, axis, down)  2.97 us
    pallas_call x1, Pallas kernels, on_device(): pl.pallas_call(functools.partial(lift_kernel, groups), out_shape=[jax.Sha...  2.35 us
  transfers between devices with their start and end apart: 15, of which 11 were waited for; matrix products, arithmetic and copies ran while one was open for 17% of the time, Pallas kernels for 3%

profile of v19, /device:TPU:0, one launch (start us, length us, event | category | flops | bytes accessed | tf_op | source)
XLA Modules:
  0.0 51.4 jit_solution(11567117011214798300)
XLA Ops:
  0.5 3.0 %collective-permute-start.3 = (bf16[16,8192]{1,0:T(8,128)(2,1)}, bf16[16,8192]{1,0:T(8,128)(2,1)S(1)}, u32[]{:S(2)}, u32[]{:S(2)}) collective-permute-start(bf16[16,8192]{1,0:T(8,128)(2,1)} %bitcast.14), channel_id=1, source_target_pairs={{2,0},{4,2},{6,4},{7,6},{5,7},{3,5},{1,3},{0,1},{10,8},{12,10},{14... | collective-permute-start | bytes 786440 | tf_op jit(solution)/shard_map/ppermute | solution.py:30
  3.5 0.7 %copy-done.3 = s32[2,12]{1,0:T(2,128)S(1)} copy-done((s32[2,12]{1,0:T(2,128)S(1)}, s32[2,12]{1,0:T(2,128)}, u32[]{:S(2)}) %copy-start.3) | copy-done | bytes 120
  4.2 0.7 %copy-done.4 = s32[1,12]{1,0:T(1,128)S(1)} copy-done((s32[1,12]{1,0:T(1,128)S(1)}, s32[1,12]{1,0:T(1,128)}, u32[]{:S(2)}) %copy-start.4) | copy-done | bytes 72
  5.5 1.0 %place.1 = (s32[1,128]{1,0:T(1,128)S(1)}, s32[128,1]{1,0:T(8,128)S(1)}) custom-call(s32[2,12]{1,0:T(2,128)S(1)} %copy-done.3, s32[1,12]{1,0:T(1,128)S(1)} %copy-done.4, s32[16]{0:T(128)S(1)} %copy-done.5), custom_call_target="tpu_custom_call" | custom-call | tf_op jit(solution)/shard_map/place/pallas_call | solution.py:177
  6.6 1.3 %copy-done = bf16[1,64,10240]{2,1,0:T(8,128)(2,1)S(1)} copy-done((bf16[1,64,10240]{2,1,0:T(8,128)(2,1)S(1)}, bf16[1,64,10240]{2,1,0:T(8,128)(2,1)}, u32[]{:S(2)}) %copy-start) | copy-done | bytes 1310744
  7.9 1.2 %copy-done.1 = bf16[1,8192,64]{1,2,0:T(8,128)(2,1)S(1)} copy-done((bf16[1,8192,64]{1,2,0:T(8,128)(2,1)S(1)}, bf16[1,8192,64]{1,2,0:T(8,128)(2,1)}, u32[]{:S(2)}) %copy-start.1) | copy-done | bytes 1048600
  9.1 0.7 %stack.1 = (bf16[8192,128]{1,0:T(8,128)(2,1)S(1)}, bf16[128,10240]{1,0:T(8,128)(2,1)S(1)}) custom-call(bf16[64,8192]{1,0:T(8,128)(2,1)S(1)} %bitcast.13, bf16[64,8192]{1,0:T(8,128)(2,1)S(1)} %collective-permute-done.refs_1_, bf16[64,10240]{1,0:T(8,128)(2,1)S(1)} %bitcast.11, bf16[64,10240]{1,0:T(8,128)(2,1)S(1)} %collective-permute-done.1.refs_3_), custom_call_target="tpu_custom_call" | custom-call | tf_op jit(solution)/shard_map/stack/pallas_call | solution.py:166
  10.2 1.4 %collective-permute-done.2.refs_0_.refs_1_ = bf16[16,8192]{1,0:T(8,128)(2,1)S(1)} collective-permute-done((bf16[16,8192]{1,0:T(8,128)(2,1)}, bf16[16,8192]{1,0:T(8,128)(2,1)S(1)}, u32[]{:S(2)}, u32[]{:S(2)}) %collective-permute-start.2) | collective-permute-done | bytes 262176 | tf_op jit(solution)/shard_map/ppermute | solution.py:30
  12.1 1.7 %collective-permute-start.7 = (bf16[16,4096]{1,0:T(8,128)(2,1)S(1)}, bf16[16,4096]{1,0:T(8,128)(2,1)S(1)}, u32[]{:S(2)}, u32[]{:S(2)}) collective-permute-start(bf16[16,4096]{1,0:T(8,128)(2,1)S(1)} %get-tuple-element.22), channel_id=1, source_target_pairs={{2,0},{4,2},{6,4},{7,6},{5,7},{3,5},{1,3},{0,1},{10,8},{12,10},{14... | collective-permute-start | bytes 393224 | tf_op jit(solution)/shard_map/ppermute | solution.py:35
  13.7 1.6 %collective-permute-start.5 = (bf16[16,4096]{1,0:T(8,128)(2,1)S(1)}, bf16[16,4096]{1,0:T(8,128)(2,1)S(1)}, u32[]{:S(2)}, u32[]{:S(2)}) collective-permute-start(bf16[16,4096]{1,0:T(8,128)(2,1)S(1)} %get-tuple-element.20), channel_id=1, source_target_pairs={{2,0},{4,2},{6,4},{7,6},{5,7},{3,5},{1,3},{0,1},{10,8},{12,10},{14... | collective-permute-start | bytes 393224 | tf_op jit(solution)/shard_map/ppermute | solution.py:35
  15.8 1.7 %collective-permute-done.4.refs_3_ = bf16[16,4096]{1,0:T(8,128)(2,1)S(1)} collective-permute-done((bf16[16,4096]{1,0:T(8,128)(2,1)S(1)}, bf16[16,4096]{1,0:T(8,128)(2,1)S(1)}, u32[]{:S(2)}, u32[]{:S(2)}) %collective-permute-start.4) | collective-permute-done | bytes 131104 | tf_op jit(solution)/shard_map/ppermute | solution.py:35
  18.2 1.4 %collective-permute-start.11 = (bf16[16,4096]{1,0:T(8,128)(2,1)S(1)}, bf16[16,4096]{1,0:T(8,128)(2,1)S(1)}, u32[]{:S(2)}, u32[]{:S(2)}) collective-permute-start(bf16[16,4096]{1,0:T(8,128)(2,1)S(1)} %collective-permute-done.7.refs_6_), channel_id=1, source_target_pairs={{2,0},{4,2},{6,4},{7,6},{5,7},{3,5},{1,3},{0,1},{10,8},{12,10},{14... | collective-permute-start | bytes 393224 | tf_op jit(solution)/shard_map/ppermute | solution.py:35
  19.5 1.4 %collective-permute-done.5.refs_4_ = bf16[16,4096]{1,0:T(8,128)(2,1)S(1)} collective-permute-done((bf16[16,4096]{1,0:T(8,128)(2,1)S(1)}, bf16[16,4096]{1,0:T(8,128)(2,1)S(1)}, u32[]{:S(2)}, u32[]{:S(2)}) %collective-permute-start.5) | collective-permute-done | bytes 131104 | tf_op jit(solution)/shard_map/ppermute | solution.py:35
  21.0 1.2 %collective-permute-start.9 = (bf16[16,4096]{1,0:T(8,128)(2,1)S(1)}, bf16[16,4096]{1,0:T(8,128)(2,1)S(1)}, u32[]{:S(2)}, u32[]{:S(2)}) collective-permute-start(bf16[16,4096]{1,0:T(8,128)(2,1)S(1)} %collective-permute-done.5.refs_4_), channel_id=1, source_target_pairs={{2,0},{4,2},{6,4},{7,6},{5,7},{3,5},{1,3},{0,1},{10,8},{12,10},{14... | collective-permute-start | bytes 393224 | tf_op jit(solution)/shard_map/ppermute | solution.py:35
  22.2 0.8 %collective-permute-start.10 = (bf16[16,4096]{1,0:T(8,128)(2,1)S(1)}, bf16[16,4096]{1,0:T(8,128)(2,1)S(1)}, u32[]{:S(2)}, u32[]{:S(2)}) collective-permute-start(bf16[16,4096]{1,0:T(8,128)(2,1)S(1)} %collective-permute-done.6.refs_5_), channel_id=1, source_target_pairs={{0,2},{2,4},{4,6},{6,7},{7,5},{5,3},{3,1},{1,0},{8,10},{10,12},{12... | collective-permute-start | bytes 393224 | tf_op jit(solution)/shard_map/ppermute | solution.py:35
  23.0 0.9 %collective-permute-done.8.refs_7_ = bf16[16,4096]{1,0:T(8,128)(2,1)S(1)} collective-permute-done((bf16[16,4096]{1,0:T(8,128)(2,1)S(1)}, bf16[16,4096]{1,0:T(8,128)(2,1)S(1)}, u32[]{:S(2)}, u32[]{:S(2)}) %collective-permute-start.8) | collective-permute-done | bytes 131104 | tf_op jit(solution)/shard_map/ppermute | solution.py:35
  24.4 1.5 %collective-permute-start.13 = (bf16[16,4096]{1,0:T(8,128)(2,1)S(1)}, bf16[16,4096]{1,0:T(8,128)(2,1)S(1)}, u32[]{:S(2)}, u32[]{:S(2)}) collective-permute-start(bf16[16,4096]{1,0:T(8,128)(2,1)S(1)} %collective-permute-done.11.refs_10_), channel_id=1, source_target_pairs={{2,0},{4,2},{6,4},{7,6},{5,7},{3,5},{1,3},{0,1},{10,8},{12,10},{14... | collective-permute-start | bytes 393224 | tf_op jit(solution)/shard_map/ppermute | solution.py:37
  26.4 0.8 %collective-permute-done.10.refs_9_ = bf16[16,4096]{1,0:T(8,128)(2,1)S(1)} collective-permute-done((bf16[16,4096]{1,0:T(8,128)(2,1)S(1)}, bf16[16,4096]{1,0:T(8,128)(2,1)S(1)}, u32[]{:S(2)}, u32[]{:S(2)}) %collective-permute-start.10) | collective-permute-done | bytes 131104 | tf_op jit(solution)/shard_map/ppermute | solution.py:35
  27.2 1.6 %collective-permute-done.12.refs_11_ = bf16[16,4096]{1,0:T(8,128)(2,1)S(1)} collective-permute-done((bf16[16,4096]{1,0:T(8,128)(2,1)S(1)}, bf16[16,4096]{1,0:T(8,128)(2,1)S(1)}, u32[]{:S(2)}, u32[]{:S(2)}) %collective-permute-start.12) | collective-permute-done | bytes 131104 | tf_op jit(solution)/shard_map/ppermute | solution.py:37
  29.4 2.4 %lift.1 = (bf16[128,8192]{1,0:T(8,128)(2,1)S(1)}, bf16[8,32,1280]{2,1,0:T(8,128)(2,1)}) custom-call(s32[1,128]{1,0:T(1,128)S(1)} %get-tuple-element.16.refs_4_.place_ref, bf16[8192,128]{1,0:T(8,128)(2,1)S(1)} %get-tuple-element.17.refs_2_.down_ref, bf16[128,10240]{1,0:T(8,128)(2,1)S(1)} %get-tuple-element.18.refs_3_.up_ref, bf16[16,8192]{1,0:T(8,128)(2,1)S(1)} %bitcast.16, ...), custom_call_target="tpu_custom_call" | custom-call | flops 352321536 | bytes 4718592 | tf_op jit(solution)/shard_map/lift/pallas_call | solution.py:190
  31.8 5.6 %all-to-all-start = ((bf16[8,32,1280]{2,1,0:T(8,128)(2,1)}), bf16[8,32,1280]{2,1,0:T(8,128)(2,1)S(1)}, u32[]{:S(2)}, u32[]{:S(2)}) async-start(bf16[8,32,1280]{2,1,0:T(8,128)(2,1)} %get-tuple-element.24), calls=%async_computation | async-start | bytes 1310720 | tf_op jit(solution)/shard_map/all_to_all | solution.py:206
  37.4 8.5 %fusion.base_ref = f32[128,1280]{1,0:T(8,128)S(1)} fusion(bf16[128,8192]{1,0:T(8,128)(2,1)S(1)} %get-tuple-element.23, bf16[8192,1280]{1,0:T(8,128)(2,1)} %param.8), kind=kOutput, calls=%fused_computation | convolution fusion | flops 2684354560 | bytes 23724032 | tf_op jit(solution)/shard_map/dot_general | solution.py:215
  45.9 4.5 %all-to-all-done = bf16[8,32,1280]{2,1,0:T(8,128)(2,1)S(1)} async-done(((bf16[8,32,1280]{2,1,0:T(8,128)(2,1)}), bf16[8,32,1280]{2,1,0:T(8,128)(2,1)S(1)}, u32[]{:S(2)}, u32[]{:S(2)}) %all-to-all-start) | async-done | bytes 655392 | tf_op jit(solution)/shard_map/all_to_all | solution.py:206
  50.4 1.0 %add.1 = bf16[128,1280]{1,0:T(8,128)(2,1)} custom-call(s32[128,1]{1,0:T(8,128)S(1)} %get-tuple-element.15.refs_5_.place_ref, f32[128,1280]{1,0:T(8,128)S(1)} %fusion.base_ref, bf16[256,1280]{1,0:T(8,128)(2,1)S(1)} %bitcast.9), custom_call_target="tpu_custom_call" | custom-call | tf_op jit(solution)/shard_map/add/pallas_call | solution.py:216
  (24 shorter events, 4.8 us)
Async XLA Ops:
  0.0 6.6 %collective-permute-start.1 = (bf16[64,10240]{1,0:T(8,128)(2,1)}, bf16[64,10240]{1,0:T(8,128)(2,1)S(1)}, u32[]{:S(2)}, u32[]{:S(2)}) collective-permute-start(bf16[64,10240]{1,0:T(8,128)(2,1)} %bitcast.10), channel_id=1, source_target_pairs={{8,0},{0,8},{9,1},{1,9},{10,2},{2,10},{11,3},{3,11},{12,4},{4,12},... | collective-permute-start | bytes 3932168 | tf_op jit(solution)/shard_map/ppermute | solution.py:16
  0.5 6.1 %collective-permute-start = (bf16[64,8192]{1,0:T(8,128)(2,1)}, bf16[64,8192]{1,0:T(8,128)(2,1)S(1)}, u32[]{:S(2)}, u32[]{:S(2)}) collective-permute-start(bf16[64,8192]{1,0:T(8,128)(2,1)} %bitcast.12), channel_id=1, source_target_pairs={{8,0},{0,8},{9,1},{1,9},{10,2},{2,10},{11,3},{3,11},{12,4},{4,12},... | collective-permute-start | bytes 3145736 | tf_op jit(solution)/shard_map/ppermute | solution.py:16
  0.5 9.7 %collective-permute-start.3 = (bf16[16,8192]{1,0:T(8,128)(2,1)}, bf16[16,8192]{1,0:T(8,128)(2,1)S(1)}, u32[]{:S(2)}, u32[]{:S(2)}) collective-permute-start(bf16[16,8192]{1,0:T(8,128)(2,1)} %bitcast.14), channel_id=1, source_target_pairs={{2,0},{4,2},{6,4},{7,6},{5,7},{3,5},{1,3},{0,1},{10,8},{12,10},{14... | collective-permute-start | bytes 786440 | tf_op jit(solution)/shard_map/ppermute | solution.py:30
  3.5 8.1 %collective-permute-start.2 = (bf16[16,8192]{1,0:T(8,128)(2,1)}, bf16[16,8192]{1,0:T(8,128)(2,1)S(1)}, u32[]{:S(2)}, u32[]{:S(2)}) collective-permute-start(bf16[16,8192]{1,0:T(8,128)(2,1)} %bitcast.15), channel_id=1, source_target_pairs={{0,2},{2,4},{4,6},{6,7},{7,5},{5,3},{3,1},{1,0},{8,10},{10,12},{12... | collective-permute-start | bytes 786440 | tf_op jit(solution)/shard_map/ppermute | solution.py:30
  3.5 0.7 %copy-start.3 = (s32[2,12]{1,0:T(2,128)S(1)}, s32[2,12]{1,0:T(2,128)}, u32[]{:S(2)}) copy-start(s32[2,12]{1,0:T(2,128)} %ids_ref.1) | copy-start | bytes 292
  4.2 0.7 %copy-start.4 = (s32[1,12]{1,0:T(1,128)S(1)}, s32[1,12]{1,0:T(1,128)}, u32[]{:S(2)}) copy-start(s32[1,12]{1,0:T(1,128)} %lengths_ref.1) | copy-start | bytes 148
  4.9 0.7 %copy-start.5 = (s32[16]{0:T(128)S(1)}, s32[16]{0:T(128)}, u32[]{:S(2)}) copy-start(s32[16]{0:T(128)} %slots_ref.1) | copy-start | bytes 196
  6.6 1.3 %copy-start = (bf16[1,64,10240]{2,1,0:T(8,128)(2,1)S(1)}, bf16[1,64,10240]{2,1,0:T(8,128)(2,1)}, u32[]{:S(2)}) copy-start(bf16[1,64,10240]{2,1,0:T(8,128)(2,1)} %param.10) | copy-start | bytes 3932164
  7.9 1.2 %copy-start.1 = (bf16[1,8192,64]{1,2,0:T(8,128)(2,1)S(1)}, bf16[1,8192,64]{1,2,0:T(8,128)(2,1)}, u32[]{:S(2)}) copy-start(bf16[1,8192,64]{1,2,0:T(8,128)(2,1)} %param.9) | copy-start | bytes 3145732
  11.6 17.8 %copy-start.2 = (bf16[1,16,8192]{2,1,0:T(8,128)(2,1)S(1)}, bf16[1,16,8192]{2,1,0:T(8,128)(2,1)}, u32[]{:S(2)}) copy-start(bf16[1,16,8192]{2,1,0:T(8,128)(2,1)} %param.7) | copy-start | bytes 786436
  11.7 5.9 %collective-permute-start.4 = (bf16[16,4096]{1,0:T(8,128)(2,1)S(1)}, bf16[16,4096]{1,0:T(8,128)(2,1)S(1)}, u32[]{:S(2)}, u32[]{:S(2)}) collective-permute-start(bf16[16,4096]{1,0:T(8,128)(2,1)S(1)} %get-tuple-element.19), channel_id=1, source_target_pairs={{0,2},{2,4},{4,6},{6,7},{7,5},{5,3},{3,1},{1,0},{8,10},{10,12},{12... | collective-permute-start | bytes 393224 | tf_op jit(solution)/shard_map/ppermute | solution.py:35
  12.1 6.1 %collective-permute-start.7 = (bf16[16,4096]{1,0:T(8,128)(2,1)S(1)}, bf16[16,4096]{1,0:T(8,128)(2,1)S(1)}, u32[]{:S(2)}, u32[]{:S(2)}) collective-permute-start(bf16[16,4096]{1,0:T(8,128)(2,1)S(1)} %get-tuple-element.22), channel_id=1, source_target_pairs={{2,0},{4,2},{6,4},{7,6},{5,7},{3,5},{1,3},{0,1},{10,8},{12,10},{14... | collective-permute-start | bytes 393224 | tf_op jit(solution)/shard_map/ppermute | solution.py:35
  13.7 7.3 %collective-permute-start.5 = (bf16[16,4096]{1,0:T(8,128)(2,1)S(1)}, bf16[16,4096]{1,0:T(8,128)(2,1)S(1)}, u32[]{:S(2)}, u32[]{:S(2)}) collective-permute-start(bf16[16,4096]{1,0:T(8,128)(2,1)S(1)} %get-tuple-element.20), channel_id=1, source_target_pairs={{2,0},{4,2},{6,4},{7,6},{5,7},{3,5},{1,3},{0,1},{10,8},{12,10},{14... | collective-permute-start | bytes 393224 | tf_op jit(solution)/shard_map/ppermute | solution.py:35
  15.3 6.9 %collective-permute-start.6 = (bf16[16,4096]{1,0:T(8,128)(2,1)S(1)}, bf16[16,4096]{1,0:T(8,128)(2,1)S(1)}, u32[]{:S(2)}, u32[]{:S(2)}) collective-permute-start(bf16[16,4096]{1,0:T(8,128)(2,1)S(1)} %get-tuple-element.21), channel_id=1, source_target_pairs={{0,2},{2,4},{4,6},{6,7},{7,5},{5,3},{3,1},{1,0},{8,10},{10,12},{12... | collective-permute-start | bytes 393224 | tf_op jit(solution)/shard_map/ppermute | solution.py:35
  17.5 6.4 %collective-permute-start.8 = (bf16[16,4096]{1,0:T(8,128)(2,1)S(1)}, bf16[16,4096]{1,0:T(8,128)(2,1)S(1)}, u32[]{:S(2)}, u32[]{:S(2)}) collective-permute-start(bf16[16,4096]{1,0:T(8,128)(2,1)S(1)} %collective-permute-done.4.refs_3_), channel_id=1, source_target_pairs={{0,2},{2,4},{4,6},{6,7},{7,5},{5,3},{3,1},{1,0},{8,10},{10,12},{12... | collective-permute-start | bytes 393224 | tf_op jit(solution)/shard_map/ppermute | solution.py:35
  18.2 6.3 %collective-permute-start.11 = (bf16[16,4096]{1,0:T(8,128)(2,1)S(1)}, bf16[16,4096]{1,0:T(8,128)(2,1)S(1)}, u32[]{:S(2)}, u32[]{:S(2)}) collective-permute-start(bf16[16,4096]{1,0:T(8,128)(2,1)S(1)} %collective-permute-done.7.refs_6_), channel_id=1, source_target_pairs={{2,0},{4,2},{6,4},{7,6},{5,7},{3,5},{1,3},{0,1},{10,8},{12,10},{14... | collective-permute-start | bytes 393224 | tf_op jit(solution)/shard_map/ppermute | solution.py:35
  21.0 5.4 %collective-permute-start.9 = (bf16[16,4096]{1,0:T(8,128)(2,1)S(1)}, bf16[16,4096]{1,0:T(8,128)(2,1)S(1)}, u32[]{:S(2)}, u32[]{:S(2)}) collective-permute-start(bf16[16,4096]{1,0:T(8,128)(2,1)S(1)} %collective-permute-done.5.refs_4_), channel_id=1, source_target_pairs={{2,0},{4,2},{6,4},{7,6},{5,7},{3,5},{1,3},{0,1},{10,8},{12,10},{14... | collective-permute-start | bytes 393224 | tf_op jit(solution)/shard_map/ppermute | solution.py:35
  22.2 5.0 %collective-permute-start.10 = (bf16[16,4096]{1,0:T(8,128)(2,1)S(1)}, bf16[16,4096]{1,0:T(8,128)(2,1)S(1)}, u32[]{:S(2)}, u32[]{:S(2)}) collective-permute-start(bf16[16,4096]{1,0:T(8,128)(2,1)S(1)} %collective-permute-done.6.refs_5_), channel_id=1, source_target_pairs={{0,2},{2,4},{4,6},{6,7},{7,5},{5,3},{3,1},{1,0},{8,10},{10,12},{12... | collective-permute-start | bytes 393224 | tf_op jit(solution)/shard_map/ppermute | solution.py:35
  23.9 5.0 %collective-permute-start.12 = (bf16[16,4096]{1,0:T(8,128)(2,1)S(1)}, bf16[16,4096]{1,0:T(8,128)(2,1)S(1)}, u32[]{:S(2)}, u32[]{:S(2)}) collective-permute-start(bf16[16,4096]{1,0:T(8,128)(2,1)S(1)} %collective-permute-done.8.refs_7_), channel_id=1, source_target_pairs={{0,2},{2,4},{4,6},{6,7},{7,5},{5,3},{3,1},{1,0},{8,10},{10,12},{12... | collective-permute-start | bytes 393224 | tf_op jit(solution)/shard_map/ppermute | solution.py:37
  24.4 5.0 %collective-permute-start.13 = (bf16[16,4096]{1,0:T(8,128)(2,1)S(1)}, bf16[16,4096]{1,0:T(8,128)(2,1)S(1)}, u32[]{:S(2)}, u32[]{:S(2)}) collective-permute-start(bf16[16,4096]{1,0:T(8,128)(2,1)S(1)} %collective-permute-done.11.refs_10_), channel_id=1, source_target_pairs={{2,0},{4,2},{6,4},{7,6},{5,7},{3,5},{1,3},{0,1},{10,8},{12,10},{14... | collective-permute-start | bytes 393224 | tf_op jit(solution)/shard_map/ppermute | solution.py:37
  31.8 18.6 %all-to-all-start = ((bf16[8,32,1280]{2,1,0:T(8,128)(2,1)}), bf16[8,32,1280]{2,1,0:T(8,128)(2,1)S(1)}, u32[]{:S(2)}, u32[]{:S(2)}) async-start(bf16[8,32,1280]{2,1,0:T(8,128)(2,1)} %get-tuple-element.24), calls=%async_computation | async-start | bytes 1310720 | tf_op jit(solution)/shard_map/all_to_all | solution.py:206

commit v20 on v16

--- a/solution.py
+++ b/solution.py
@@ -88,7 +88,10 @@
         slot = slots_ref[ids_ref[group, request]]
         end = start + lengths_ref[0, request]
         panel = lax.rem(slot // tp - group + groups, groups)
-        first = (lax.rem(slot, tp) * groups + panel) * longest - start
+        chip = lax.rem(slot, tp)
+        other_row = lax.rem(chip + lax.axis_index("tp"), 2)
+        chip = other_row * (tp // 2) + chip // 2
+        first = (chip * groups + panel) * longest - start
         row = jnp.where((along >= start) & (along < end), first + along, row)
         column = jnp.where((down >= start) & (down < end), first + down, column)
         return end, row, column
@@ -98,30 +101,40 @@
 
 
 def lift_kernel(groups, place_ref, down_ref, up_ref, *refs):
-    pieces, (tokens_ref, out_ref) = refs[:-2], refs[-2:]
+    pieces, (tokens_ref, *out_refs) = refs[:-3], refs[-3:]
     rank = up_ref.shape[0] // groups
     rows = pieces[0].shape[0]
     tok_all = tokens_ref.shape[0]
-    parts, slots, columns = out_ref.shape
+    parts, slots, columns = out_refs[0].shape
     for piece, (source, column) in zip(pieces, ring_sources("tp", pieces[-1].shape[1])):
         start = pl.multiple_of(source * rows, rows)
         tokens_ref[pl.ds(start, rows), column : column + piece.shape[1]] = piece[...]
     low = jnp.dot(tokens_ref[...], down_ref[...], preferred_element_type=jnp.float32)
-    here = lax.broadcasted_iota(jnp.int32, (slots, tok_all), 0) + lax.axis_index("tp") * slots
+    me = lax.axis_index("tp")
+    here = lax.broadcasted_iota(jnp.int32, (slots, tok_all), 0) + me // 2 * slots
     chosen = (here == place_ref[...]).astype(jnp.bfloat16)
     picked = jnp.dot(chosen, low.astype(jnp.bfloat16), preferred_element_type=jnp.float32)
     row_panel = lax.broadcasted_iota(jnp.int32, picked.shape, 0) // (slots // groups)
     rank_panel = lax.broadcasted_iota(jnp.int32, picked.shape, 1) // rank
     picked = jnp.where(row_panel == rank_panel, picked, 0.0).astype(jnp.bfloat16)
-    for part in range(parts):
-        out_ref[part] = jnp.dot(
+    for owner in range(2 * parts):
+        lifts = jnp.dot(
             picked,
-            up_ref[:, part * columns : (part + 1) * columns],
+            up_ref[:, owner * columns : (owner + 1) * columns],
             preferred_element_type=jnp.float32,
-        ).astype(out_ref.dtype)
-
-
-def add_kernel(place_ref, base_ref, lifts_ref, out_ref):
+        ).astype(out_refs[0].dtype)
+        for other_row, out_ref in enumerate(out_refs):
+
+            @pl.when(lax.rem(me + owner, 2) == other_row)
+            def _():
+                out_ref[owner // 2] = lifts
+
+
+def add_kernel(place_ref, base_ref, *refs):
+    parts, (out_ref, lifts_ref) = refs[:-2], refs[-2:]
+    rows = parts[0].shape[0]
+    for i, part in enumerate(parts):
+        lifts_ref[i * rows : (i + 1) * rows, :] = part[...]
     place = lax.broadcasted_iota(jnp.int32, (base_ref.shape[0], lifts_ref.shape[0]), 1)
     chosen = (place == place_ref[...]).astype(jnp.bfloat16)
     lift = jnp.dot(chosen, lifts_ref[...], preferred_element_type=jnp.float32)
@@ -173,14 +186,15 @@
     )(request_adapter_ids, request_token_lengths, adapter_store_slot)
     pieces = ring_gather(tokens[0], "tp", (down, up, row, column))
 
-    gathered, lifts = pl.pallas_call(
+    gathered, *lifts = pl.pallas_call(
         functools.partial(lift_kernel, groups),
         out_shape=[
             jax.ShapeDtypeStruct((tok_all, width), jnp.bfloat16),
-            jax.ShapeDtypeStruct((tp, here, columns), jnp.bfloat16),
+            jax.ShapeDtypeStruct((tp // 2, here, columns), jnp.bfloat16),
+            jax.ShapeDtypeStruct((tp // 2, here, columns), jnp.bfloat16),
         ],
         in_specs=[in_vmem] * (3 + len(pieces)),
-        out_specs=[in_vmem] * 2,
+        out_specs=[in_vmem] * 3,
         compiler_params=pltpu.CompilerParams(vmem_limit_bytes=24 * 2**20),
         cost_estimate=pl.CostEstimate(
             flops=2 * groups * rank * (tok_all * width + here * tp * columns),
@@ -189,17 +203,25 @@
         ),
         name="lift",
     )(row, down, up, *pieces)
-    lifts = lax.all_to_all(lifts, "tp", split_axis=0, concat_axis=0, tiled=True)
+    lifts[1] = lax.ppermute(lifts[1], "tp", [(i, i ^ 1) for i in range(tp)])
+    rows = [list(range(row, tp, 2)) for row in range(2)]
+    lifts = [
+        lax.all_to_all(
+            x, "tp", split_axis=0, concat_axis=0, axis_index_groups=rows, tiled=True
+        ).reshape(tp // 2 * here, columns)
+        for x in lifts
+    ]
 
     base = jnp.dot(gathered, base_projection_weight, preferred_element_type=jnp.float32)
     out = pl.pallas_call(
         add_kernel,
         out_shape=jax.ShapeDtypeStruct((tok_all, columns), jnp.bfloat16),
-        in_specs=[in_vmem] * 3,
+        in_specs=[in_vmem] * 4,
         out_specs=in_vmem,
+        scratch_shapes=[pltpu.VMEM((tp * here, columns), jnp.bfloat16)],
         compiler_params=small,
         name="add",
-    )(column, base, lifts.reshape(tp * here, columns))
+    )(column, base, *lifts)
     return out[None]
 
 

time: 53.1 us -> 60.2 us (1.13)
  starting transfers between devices: 19 us -> 24.5 us
  Pallas kernels: 5.08 us -> 6.05 us
    ppermute x0 -> x1, waiting for transfers between devices: none -> 6.3 us  [on_device(): lifts[1] = lax.ppermute(lifts[1], 'tp', [(i, i ^ 1) for i in range(tp)])]
    all_to_all x1 -> x2, waiting for transfers between devices: 5.83 us -> 0.13 us  [on_device(): lax.all_to_all(x, 'tp', split_axis=0, concat_axis=0, axis_index_groups=ro...]
    all_to_all x1 -> x2, starting transfers between devices: 5.64 us -> 10.3 us  [on_device(): lax.all_to_all(x, 'tp', split_axis=0, concat_axis=0, axis_index_groups=ro...]
    pallas_call x1, Pallas kernels: 2.35 us -> 3.25 us  [on_device(): pl.pallas_call(functools.partial(lift_kernel, groups), out_shape=[jax.Sha...]
    ppermute x0 -> x1, starting transfers between devices: none -> 0.88 us  [on_device(): lifts[1] = lax.ppermute(lifts[1], 'tp', [(i, i ^ 1) for i in range(tp)])]
  transfers between devices with their start and end apart: 15 -> 17, of which waited for: 11 -> 12; matrix products, arithmetic and copies ran while one was open for 16% -> 14% of each run, Pallas kernels for 3% -> 3%
where the time goes in v20:
time: 60.2 us; the launch traced here: 59.8 us
  starting transfers between devices  24.5 us (41%)
  waiting for transfers between devices  16.2 us (27%)
  matrix products  8.52 us (14%)
  Pallas kernels  6.05 us (10%)
  local copies, waits for them, and re-layouts  4.53 us (8%)
    all_to_all x2, starting transfers between devices, on_device(): lax.all_to_all(x, 'tp', split_axis=0, concat_axis=0, axis_index_groups=ro...  10.3 us
    dot_general x1, matrix products, on_device(): jnp.dot(gathered, base_projection_weight, preferred_element_type=jnp.floa...  8.52 us
    ppermute x8, starting transfers between devices, ring_gather(): lax.ppermute(x, axis, way)  7.74 us
    ppermute x1, waiting for transfers between devices, on_device(): lifts[1] = lax.ppermute(lifts[1], 'tp', [(i, i ^ 1) for i in range(tp)])  6.3 us
    ppermute x8, waiting for transfers between devices, ring_gather(): lax.ppermute(x, axis, way)  5.78 us
    unnamed x12, local copies, waits for them, and re-layouts  4.53 us
    pallas_call x1, Pallas kernels, on_device(): pl.pallas_call(functools.partial(lift_kernel, groups), out_shape=[jax.Sha...  3.25 us
    ppermute x1, starting transfers between devices, ring_gather(): lax.ppermute(block, axis, down)  2.97 us
  transfers between devices with their start and end apart: 17, of which 12 were waited for; matrix products, arithmetic and copies ran while one was open for 14% of the time, Pallas kernels for 3%

profile of v20, /device:TPU:0, one launch (start us, length us, event | category | flops | bytes accessed | tf_op | source)
XLA Modules:
  0.0 59.8 jit_solution(1532133120475277212)
XLA Ops:
  0.5 3.0 %collective-permute-start.3 = (bf16[16,8192]{1,0:T(8,128)(2,1)}, bf16[16,8192]{1,0:T(8,128)(2,1)S(1)}, u32[]{:S(2)}, u32[]{:S(2)}) collective-permute-start(bf16[16,8192]{1,0:T(8,128)(2,1)} %bitcast.16), channel_id=1, source_target_pairs={{2,0},{4,2},{6,4},{7,6},{5,7},{3,5},{1,3},{0,1},{10,8},{12,10},{14... | collective-permute-start | bytes 786440 | tf_op jit(solution)/shard_map/ppermute | solution.py:30
  5.5 1.0 %place.1 = (s32[1,128]{1,0:T(1,128)S(1)}, s32[128,1]{1,0:T(8,128)S(1)}) custom-call(s32[2,12]{1,0:T(2,128)S(1)} %copy-done.3, s32[1,12]{1,0:T(1,128)S(1)} %copy-done.4, s32[16]{0:T(128)S(1)} %copy-done.5), custom_call_target="tpu_custom_call" | custom-call | tf_op jit(solution)/shard_map/place/pallas_call | solution.py:176
  6.6 1.3 %copy-done = bf16[1,64,10240]{2,1,0:T(8,128)(2,1)S(1)} copy-done((bf16[1,64,10240]{2,1,0:T(8,128)(2,1)S(1)}, bf16[1,64,10240]{2,1,0:T(8,128)(2,1)}, u32[]{:S(2)}) %copy-start) | copy-done | bytes 1310744
  7.9 1.2 %copy-done.1 = bf16[1,8192,64]{1,2,0:T(8,128)(2,1)S(1)} copy-done((bf16[1,8192,64]{1,2,0:T(8,128)(2,1)S(1)}, bf16[1,8192,64]{1,2,0:T(8,128)(2,1)}, u32[]{:S(2)}) %copy-start.1) | copy-done | bytes 1048600
  9.1 0.7 %stack.1 = (bf16[8192,128]{1,0:T(8,128)(2,1)S(1)}, bf16[128,10240]{1,0:T(8,128)(2,1)S(1)}) custom-call(bf16[64,8192]{1,0:T(8,128)(2,1)S(1)} %bitcast.15, bf16[64,8192]{1,0:T(8,128)(2,1)S(1)} %collective-permute-done.refs_1_, bf16[64,10240]{1,0:T(8,128)(2,1)S(1)} %bitcast.11, bf16[64,10240]{1,0:T(8,128)(2,1)S(1)} %collective-permute-done.1.refs_3_), custom_call_target="tpu_custom_call" | custom-call | tf_op jit(solution)/shard_map/stack/pallas_call | solution.py:165
  10.2 1.4 %collective-permute-done.2.refs_0_.refs_1_ = bf16[16,8192]{1,0:T(8,128)(2,1)S(1)} collective-permute-done((bf16[16,8192]{1,0:T(8,128)(2,1)}, bf16[16,8192]{1,0:T(8,128)(2,1)S(1)}, u32[]{:S(2)}, u32[]{:S(2)}) %collective-permute-start.2) | collective-permute-done | bytes 262176 | tf_op jit(solution)/shard_map/ppermute | solution.py:30
  12.1 1.7 %collective-permute-start.7 = (bf16[16,4096]{1,0:T(8,128)(2,1)S(1)}, bf16[16,4096]{1,0:T(8,128)(2,1)S(1)}, u32[]{:S(2)}, u32[]{:S(2)}) collective-permute-start(bf16[16,4096]{1,0:T(8,128)(2,1)S(1)} %get-tuple-element.23), channel_id=1, source_target_pairs={{2,0},{4,2},{6,4},{7,6},{5,7},{3,5},{1,3},{0,1},{10,8},{12,10},{14... | collective-permute-start | bytes 393224 | tf_op jit(solution)/shard_map/ppermute | solution.py:35
  13.7 1.6 %collective-permute-start.5 = (bf16[16,4096]{1,0:T(8,128)(2,1)S(1)}, bf16[16,4096]{1,0:T(8,128)(2,1)S(1)}, u32[]{:S(2)}, u32[]{:S(2)}) collective-permute-start(bf16[16,4096]{1,0:T(8,128)(2,1)S(1)} %get-tuple-element.21), channel_id=1, source_target_pairs={{2,0},{4,2},{6,4},{7,6},{5,7},{3,5},{1,3},{0,1},{10,8},{12,10},{14... | collective-permute-start | bytes 393224 | tf_op jit(solution)/shard_map/ppermute | solution.py:35
  15.8 1.7 %collective-permute-done.4.refs_3_ = bf16[16,4096]{1,0:T(8,128)(2,1)S(1)} collective-permute-done((bf16[16,4096]{1,0:T(8,128)(2,1)S(1)}, bf16[16,4096]{1,0:T(8,128)(2,1)S(1)}, u32[]{:S(2)}, u32[]{:S(2)}) %collective-permute-start.4) | collective-permute-done | bytes 131104 | tf_op jit(solution)/shard_map/ppermute | solution.py:35
  18.2 1.4 %collective-permute-start.11 = (bf16[16,4096]{1,0:T(8,128)(2,1)S(1)}, bf16[16,4096]{1,0:T(8,128)(2,1)S(1)}, u32[]{:S(2)}, u32[]{:S(2)}) collective-permute-start(bf16[16,4096]{1,0:T(8,128)(2,1)S(1)} %collective-permute-done.7.refs_6_), channel_id=1, source_target_pairs={{2,0},{4,2},{6,4},{7,6},{5,7},{3,5},{1,3},{0,1},{10,8},{12,10},{14... | collective-permute-start | bytes 393224 | tf_op jit(solution)/shard_map/ppermute | solution.py:35
  19.5 1.4 %collective-permute-done.5.refs_4_ = bf16[16,4096]{1,0:T(8,128)(2,1)S(1)} collective-permute-done((bf16[16,4096]{1,0:T(8,128)(2,1)S(1)}, bf16[16,4096]{1,0:T(8,128)(2,1)S(1)}, u32[]{:S(2)}, u32[]{:S(2)}) %collective-permute-start.5) | collective-permute-done | bytes 131104 | tf_op jit(solution)/shard_map/ppermute | solution.py:35
  21.0 1.3 %collective-permute-start.9 = (bf16[16,4096]{1,0:T(8,128)(2,1)S(1)}, bf16[16,4096]{1,0:T(8,128)(2,1)S(1)}, u32[]{:S(2)}, u32[]{:S(2)}) collective-permute-start(bf16[16,4096]{1,0:T(8,128)(2,1)S(1)} %collective-permute-done.5.refs_4_), channel_id=1, source_target_pairs={{2,0},{4,2},{6,4},{7,6},{5,7},{3,5},{1,3},{0,1},{10,8},{12,10},{14... | collective-permute-start | bytes 393224 | tf_op jit(solution)/shard_map/ppermute | solution.py:35
  22.2 0.8 %collective-permute-start.10 = (bf16[16,4096]{1,0:T(8,128)(2,1)S(1)}, bf16[16,4096]{1,0:T(8,128)(2,1)S(1)}, u32[]{:S(2)}, u32[]{:S(2)}) collective-permute-start(bf16[16,4096]{1,0:T(8,128)(2,1)S(1)} %collective-permute-done.6.refs_5_), channel_id=1, source_target_pairs={{0,2},{2,4},{4,6},{6,7},{7,5},{5,3},{3,1},{1,0},{8,10},{10,12},{12... | collective-permute-start | bytes 393224 | tf_op jit(solution)/shard_map/ppermute | solution.py:35
  23.0 0.9 %collective-permute-done.8.refs_7_ = bf16[16,4096]{1,0:T(8,128)(2,1)S(1)} collective-permute-done((bf16[16,4096]{1,0:T(8,128)(2,1)S(1)}, bf16[16,4096]{1,0:T(8,128)(2,1)S(1)}, u32[]{:S(2)}, u32[]{:S(2)}) %collective-permute-start.8) | collective-permute-done | bytes 131104 | tf_op jit(solution)/shard_map/ppermute | solution.py:35
  24.4 1.5 %collective-permute-start.13 = (bf16[16,4096]{1,0:T(8,128)(2,1)S(1)}, bf16[16,4096]{1,0:T(8,128)(2,1)S(1)}, u32[]{:S(2)}, u32[]{:S(2)}) collective-permute-start(bf16[16,4096]{1,0:T(8,128)(2,1)S(1)} %collective-permute-done.11.refs_10_), channel_id=1, source_target_pairs={{2,0},{4,2},{6,4},{7,6},{5,7},{3,5},{1,3},{0,1},{10,8},{12,10},{14... | collective-permute-start | bytes 393224 | tf_op jit(solution)/shard_map/ppermute | solution.py:37
  26.4 0.8 %collective-permute-done.10.refs_9_ = bf16[16,4096]{1,0:T(8,128)(2,1)S(1)} collective-permute-done((bf16[16,4096]{1,0:T(8,128)(2,1)S(1)}, bf16[16,4096]{1,0:T(8,128)(2,1)S(1)}, u32[]{:S(2)}, u32[]{:S(2)}) %collective-permute-start.10) | collective-permute-done | bytes 131104 | tf_op jit(solution)/shard_map/ppermute | solution.py:35
  27.2 1.6 %collective-permute-done.12.refs_11_ = bf16[16,4096]{1,0:T(8,128)(2,1)S(1)} collective-permute-done((bf16[16,4096]{1,0:T(8,128)(2,1)S(1)}, bf16[16,4096]{1,0:T(8,128)(2,1)S(1)}, u32[]{:S(2)}, u32[]{:S(2)}) %collective-permute-start.12) | collective-permute-done | bytes 131104 | tf_op jit(solution)/shard_map/ppermute | solution.py:37
  29.4 3.2 %lift.1 = (bf16[128,8192]{1,0:T(8,128)(2,1)S(1)}, bf16[4,32,1280]{2,1,0:T(8,128)(2,1)}, bf16[4,32,1280]{2,1,0:T(8,128)(2,1)S(1)}) custom-call(s32[1,128]{1,0:T(1,128)S(1)} %get-tuple-element.17.refs_4_.place_ref, bf16[8192,128]{1,0:T(8,128)(2,1)S(1)} %get-tuple-element.18.refs_2_.down_ref, bf16[128,10240]{1,0:T(8,128)(2,1)S(1)} %get-tuple-element.19.refs_3_.up_ref, ...), custom_call_target="tpu_custom_call" | custom-call | flops 352321536 | bytes 4718592 | tf_op jit(solution)/shard_map/lift/pallas_call | solution.py:189
  32.7 5.3 %all-to-all-start = ((bf16[4,32,1280]{2,1,0:T(8,128)(2,1)}), bf16[4,32,1280]{2,1,0:T(8,128)(2,1)S(1)}, u32[]{:S(2)}, u32[]{:S(2)}) async-start(bf16[4,32,1280]{2,1,0:T(8,128)(2,1)} %get-tuple-element.25), calls=%async_computation | async-start | bytes 655360 | tf_op jit(solution)/shard_map/all_to_all | solution.py:209
  38.0 0.9 %collective-permute-start.14 = (bf16[4,32,1280]{2,1,0:T(8,128)(2,1)S(1)}, bf16[4,32,1280]{2,1,0:T(8,128)(2,1)}, u32[]{:S(2)}, u32[]{:S(2)}) collective-permute-start(bf16[4,32,1280]{2,1,0:T(8,128)(2,1)S(1)} %get-tuple-element.26), channel_id=1, source_target_pairs={{0,1},{1,0},{2,3},{3,2},{4,5},{5,4},{6,7},{7,6},{8,9},{9,8},{10,11... | collective-permute-start | bytes 983048 | tf_op jit(solution)/shard_map/ppermute | solution.py:206
  38.9 6.3 %collective-permute-done.14 = bf16[4,32,1280]{2,1,0:T(8,128)(2,1)} collective-permute-done((bf16[4,32,1280]{2,1,0:T(8,128)(2,1)S(1)}, bf16[4,32,1280]{2,1,0:T(8,128)(2,1)}, u32[]{:S(2)}, u32[]{:S(2)}) %collective-permute-start.14) | collective-permute-done | bytes 327712 | tf_op jit(solution)/shard_map/ppermute | solution.py:206
  45.3 5.0 %all-to-all-start.1 = ((bf16[4,32,1280]{2,1,0:T(8,128)(2,1)}), bf16[4,32,1280]{2,1,0:T(8,128)(2,1)S(1)}, u32[]{:S(2)}, u32[]{:S(2)}) async-start(bf16[4,32,1280]{2,1,0:T(8,128)(2,1)} %collective-permute-done.14), calls=%async_computation.1 | async-start | bytes 655360 | tf_op jit(solution)/shard_map/all_to_all | solution.py:209
  50.3 8.5 %fusion.base_ref = f32[128,1280]{1,0:T(8,128)S(1)} fusion(bf16[128,8192]{1,0:T(8,128)(2,1)S(1)} %get-tuple-element.24, bf16[8192,1280]{1,0:T(8,128)(2,1)} %param.8), kind=kOutput, calls=%fused_computation | convolution fusion | flops 2684354560 | bytes 23724032 | tf_op jit(solution)/shard_map/dot_general | solution.py:215
  58.8 1.0 %add.1 = bf16[128,1280]{1,0:T(8,128)(2,1)} custom-call(s32[128,1]{1,0:T(8,128)S(1)} %get-tuple-element.16.refs_5_.place_ref, f32[128,1280]{1,0:T(8,128)S(1)} %fusion.base_ref, bf16[128,1280]{1,0:T(8,128)(2,1)S(1)} %bitcast.12, bf16[128,1280]{1,0:T(8,128)(2,1)S(1)} %bitcast.13), custom_call_target="tpu_custom_call" | custom-call | tf_op jit(solution)/shard_map/add/pallas_call | solution.py:216
  (28 shorter events, 6.2 us)
Async XLA Ops:
  0.0 6.6 %collective-permute-start.1 = (bf16[64,10240]{1,0:T(8,128)(2,1)}, bf16[64,10240]{1,0:T(8,128)(2,1)S(1)}, u32[]{:S(2)}, u32[]{:S(2)}) collective-permute-start(bf16[64,10240]{1,0:T(8,128)(2,1)} %bitcast.10), channel_id=1, source_target_pairs={{8,0},{0,8},{9,1},{1,9},{10,2},{2,10},{11,3},{3,11},{12,4},{4,12},... | collective-permute-start | bytes 3932168 | tf_op jit(solution)/shard_map/ppermute | solution.py:16
  0.5 6.1 %collective-permute-start = (bf16[64,8192]{1,0:T(8,128)(2,1)}, bf16[64,8192]{1,0:T(8,128)(2,1)S(1)}, u32[]{:S(2)}, u32[]{:S(2)}) collective-permute-start(bf16[64,8192]{1,0:T(8,128)(2,1)} %bitcast.14), channel_id=1, source_target_pairs={{8,0},{0,8},{9,1},{1,9},{10,2},{2,10},{11,3},{3,11},{12,4},{4,12},... | collective-permute-start | bytes 3145736 | tf_op jit(solution)/shard_map/ppermute | solution.py:16
  0.5 9.7 %collective-permute-start.3 = (bf16[16,8192]{1,0:T(8,128)(2,1)}, bf16[16,8192]{1,0:T(8,128)(2,1)S(1)}, u32[]{:S(2)}, u32[]{:S(2)}) collective-permute-start(bf16[16,8192]{1,0:T(8,128)(2,1)} %bitcast.16), channel_id=1, source_target_pairs={{2,0},{4,2},{6,4},{7,6},{5,7},{3,5},{1,3},{0,1},{10,8},{12,10},{14... | collective-permute-start | bytes 786440 | tf_op jit(solution)/shard_map/ppermute | solution.py:30
  3.5 8.1 %collective-permute-start.2 = (bf16[16,8192]{1,0:T(8,128)(2,1)}, bf16[16,8192]{1,0:T(8,128)(2,1)S(1)}, u32[]{:S(2)}, u32[]{:S(2)}) collective-permute-start(bf16[16,8192]{1,0:T(8,128)(2,1)} %bitcast.17), channel_id=1, source_target_pairs={{0,2},{2,4},{4,6},{6,7},{7,5},{5,3},{3,1},{1,0},{8,10},{10,12},{12... | collective-permute-start | bytes 786440 | tf_op jit(solution)/shard_map/ppermute | solution.py:30
  3.5 0.7 %copy-start.3 = (s32[2,12]{1,0:T(2,128)S(1)}, s32[2,12]{1,0:T(2,128)}, u32[]{:S(2)}) copy-start(s32[2,12]{1,0:T(2,128)} %ids_ref.1) | copy-start | bytes 292
  4.2 0.7 %copy-start.4 = (s32[1,12]{1,0:T(1,128)S(1)}, s32[1,12]{1,0:T(1,128)}, u32[]{:S(2)}) copy-start(s32[1,12]{1,0:T(1,128)} %lengths_ref.1) | copy-start | bytes 148
  4.9 0.7 %copy-start.5 = (s32[16]{0:T(128)S(1)}, s32[16]{0:T(128)}, u32[]{:S(2)}) copy-start(s32[16]{0:T(128)} %slots_ref.1) | copy-start | bytes 196
  6.6 1.3 %copy-start = (bf16[1,64,10240]{2,1,0:T(8,128)(2,1)S(1)}, bf16[1,64,10240]{2,1,0:T(8,128)(2,1)}, u32[]{:S(2)}) copy-start(bf16[1,64,10240]{2,1,0:T(8,128)(2,1)} %param.10) | copy-start | bytes 3932164
  7.9 1.2 %copy-start.1 = (bf16[1,8192,64]{1,2,0:T(8,128)(2,1)S(1)}, bf16[1,8192,64]{1,2,0:T(8,128)(2,1)}, u32[]{:S(2)}) copy-start(bf16[1,8192,64]{1,2,0:T(8,128)(2,1)} %param.9) | copy-start | bytes 3145732
  11.6 17.8 %copy-start.2 = (bf16[1,16,8192]{2,1,0:T(8,128)(2,1)S(1)}, bf16[1,16,8192]{2,1,0:T(8,128)(2,1)}, u32[]{:S(2)}) copy-start(bf16[1,16,8192]{2,1,0:T(8,128)(2,1)} %param.7) | copy-start | bytes 786436
  11.7 5.9 %collective-permute-start.4 = (bf16[16,4096]{1,0:T(8,128)(2,1)S(1)}, bf16[16,4096]{1,0:T(8,128)(2,1)S(1)}, u32[]{:S(2)}, u32[]{:S(2)}) collective-permute-start(bf16[16,4096]{1,0:T(8,128)(2,1)S(1)} %get-tuple-element.20), channel_id=1, source_target_pairs={{0,2},{2,4},{4,6},{6,7},{7,5},{5,3},{3,1},{1,0},{8,10},{10,12},{12... | collective-permute-start | bytes 393224 | tf_op jit(solution)/shard_map/ppermute | solution.py:35
  12.1 6.1 %collective-permute-start.7 = (bf16[16,4096]{1,0:T(8,128)(2,1)S(1)}, bf16[16,4096]{1,0:T(8,128)(2,1)S(1)}, u32[]{:S(2)}, u32[]{:S(2)}) collective-permute-start(bf16[16,4096]{1,0:T(8,128)(2,1)S(1)} %get-tuple-element.23), channel_id=1, source_target_pairs={{2,0},{4,2},{6,4},{7,6},{5,7},{3,5},{1,3},{0,1},{10,8},{12,10},{14... | collective-permute-start | bytes 393224 | tf_op jit(solution)/shard_map/ppermute | solution.py:35
  13.7 7.2 %collective-permute-start.5 = (bf16[16,4096]{1,0:T(8,128)(2,1)S(1)}, bf16[16,4096]{1,0:T(8,128)(2,1)S(1)}, u32[]{:S(2)}, u32[]{:S(2)}) collective-permute-start(bf16[16,4096]{1,0:T(8,128)(2,1)S(1)} %get-tuple-element.21), channel_id=1, source_target_pairs={{2,0},{4,2},{6,4},{7,6},{5,7},{3,5},{1,3},{0,1},{10,8},{12,10},{14... | collective-permute-start | bytes 393224 | tf_op jit(solution)/shard_map/ppermute | solution.py:35
  15.3 6.9 %collective-permute-start.6 = (bf16[16,4096]{1,0:T(8,128)(2,1)S(1)}, bf16[16,4096]{1,0:T(8,128)(2,1)S(1)}, u32[]{:S(2)}, u32[]{:S(2)}) collective-permute-start(bf16[16,4096]{1,0:T(8,128)(2,1)S(1)} %get-tuple-element.22), channel_id=1, source_target_pairs={{0,2},{2,4},{4,6},{6,7},{7,5},{5,3},{3,1},{1,0},{8,10},{10,12},{12... | collective-permute-start | bytes 393224 | tf_op jit(solution)/shard_map/ppermute | solution.py:35
  17.5 6.4 %collective-permute-start.8 = (bf16[16,4096]{1,0:T(8,128)(2,1)S(1)}, bf16[16,4096]{1,0:T(8,128)(2,1)S(1)}, u32[]{:S(2)}, u32[]{:S(2)}) collective-permute-start(bf16[16,4096]{1,0:T(8,128)(2,1)S(1)} %collective-permute-done.4.refs_3_), channel_id=1, source_target_pairs={{0,2},{2,4},{4,6},{6,7},{7,5},{5,3},{3,1},{1,0},{8,10},{10,12},{12... | collective-permute-start | bytes 393224 | tf_op jit(solution)/shard_map/ppermute | solution.py:35
  18.2 6.3 %collective-permute-start.11 = (bf16[16,4096]{1,0:T(8,128)(2,1)S(1)}, bf16[16,4096]{1,0:T(8,128)(2,1)S(1)}, u32[]{:S(2)}, u32[]{:S(2)}) collective-permute-start(bf16[16,4096]{1,0:T(8,128)(2,1)S(1)} %collective-permute-done.7.refs_6_), channel_id=1, source_target_pairs={{2,0},{4,2},{6,4},{7,6},{5,7},{3,5},{1,3},{0,1},{10,8},{12,10},{14... | collective-permute-start | bytes 393224 | tf_op jit(solution)/shard_map/ppermute | solution.py:35
  21.0 5.4 %collective-permute-start.9 = (bf16[16,4096]{1,0:T(8,128)(2,1)S(1)}, bf16[16,4096]{1,0:T(8,128)(2,1)S(1)}, u32[]{:S(2)}, u32[]{:S(2)}) collective-permute-start(bf16[16,4096]{1,0:T(8,128)(2,1)S(1)} %collective-permute-done.5.refs_4_), channel_id=1, source_target_pairs={{2,0},{4,2},{6,4},{7,6},{5,7},{3,5},{1,3},{0,1},{10,8},{12,10},{14... | collective-permute-start | bytes 393224 | tf_op jit(solution)/shard_map/ppermute | solution.py:35
  22.2 5.0 %collective-permute-start.10 = (bf16[16,4096]{1,0:T(8,128)(2,1)S(1)}, bf16[16,4096]{1,0:T(8,128)(2,1)S(1)}, u32[]{:S(2)}, u32[]{:S(2)}) collective-permute-start(bf16[16,4096]{1,0:T(8,128)(2,1)S(1)} %collective-permute-done.6.refs_5_), channel_id=1, source_target_pairs={{0,2},{2,4},{4,6},{6,7},{7,5},{5,3},{3,1},{1,0},{8,10},{10,12},{12... | collective-permute-start | bytes 393224 | tf_op jit(solution)/shard_map/ppermute | solution.py:35
  23.9 5.0 %collective-permute-start.12 = (bf16[16,4096]{1,0:T(8,128)(2,1)S(1)}, bf16[16,4096]{1,0:T(8,128)(2,1)S(1)}, u32[]{:S(2)}, u32[]{:S(2)}) collective-permute-start(bf16[16,4096]{1,0:T(8,128)(2,1)S(1)} %collective-permute-done.8.refs_7_), channel_id=1, source_target_pairs={{0,2},{2,4},{4,6},{6,7},{7,5},{5,3},{3,1},{1,0},{8,10},{10,12},{12... | collective-permute-start | bytes 393224 | tf_op jit(solution)/shard_map/ppermute | solution.py:37
  24.4 5.0 %collective-permute-start.13 = (bf16[16,4096]{1,0:T(8,128)(2,1)S(1)}, bf16[16,4096]{1,0:T(8,128)(2,1)S(1)}, u32[]{:S(2)}, u32[]{:S(2)}) collective-permute-start(bf16[16,4096]{1,0:T(8,128)(2,1)S(1)} %collective-permute-done.11.refs_10_), channel_id=1, source_target_pairs={{2,0},{4,2},{6,4},{7,6},{5,7},{3,5},{1,3},{0,1},{10,8},{12,10},{14... | collective-permute-start | bytes 393224 | tf_op jit(solution)/shard_map/ppermute | solution.py:37
  32.7 12.6 %all-to-all-start = ((bf16[4,32,1280]{2,1,0:T(8,128)(2,1)}), bf16[4,32,1280]{2,1,0:T(8,128)(2,1)S(1)}, u32[]{:S(2)}, u32[]{:S(2)}) async-start(bf16[4,32,1280]{2,1,0:T(8,128)(2,1)} %get-tuple-element.25), calls=%async_computation | async-start | bytes 655360 | tf_op jit(solution)/shard_map/all_to_all | solution.py:209
  38.0 7.2 %collective-permute-start.14 = (bf16[4,32,1280]{2,1,0:T(8,128)(2,1)S(1)}, bf16[4,32,1280]{2,1,0:T(8,128)(2,1)}, u32[]{:S(2)}, u32[]{:S(2)}) collective-permute-start(bf16[4,32,1280]{2,1,0:T(8,128)(2,1)S(1)} %get-tuple-element.26), channel_id=1, source_target_pairs={{0,1},{1,0},{2,3},{3,2},{4,5},{5,4},{6,7},{7,6},{8,9},{9,8},{10,11... | collective-permute-start | bytes 983048 | tf_op jit(solution)/shard_map/ppermute | solution.py:206
  45.3 13.5 %all-to-all-start.1 = ((bf16[4,32,1280]{2,1,0:T(8,128)(2,1)}), bf16[4,32,1280]{2,1,0:T(8,128)(2,1)S(1)}, u32[]{:S(2)}, u32[]{:S(2)}) async-start(bf16[4,32,1280]{2,1,0:T(8,128)(2,1)} %collective-permute-done.14), calls=%async_computation.1 | async-start | bytes 655360 | tf_op jit(solution)/shard_map/all_to_all | solution.py:209

commit v21 on v17

--- a/solution.py
+++ b/solution.py
@@ -58,6 +58,15 @@
     return jnp.where(lax.rem(i, 2) == 0, i // 2, n - 1 - i // 2)
 
 
+def exchange_order(n):
+    ring = ring_of(n)
+    return ring[n // 2 :] + ring[: n // 2]
+
+
+def exchange_place(i, n):
+    return lax.rem(ring_place(i, n) + n // 2, n)
+
+
 def ring_sources(axis, half):
     n = lax.axis_size(axis)
     place = ring_place(lax.axis_index(axis), n)
@@ -91,7 +100,7 @@
         slot = slots_ref[ids_ref[group, request]]
         end = start + lengths_ref[0, request]
         panel = lax.rem(slot // tp - group + groups, groups)
-        first = (ring_place(lax.rem(slot, tp), tp) * groups + panel) * longest - start
+        first = (exchange_place(lax.rem(slot, tp), tp) * groups + panel) * longest - start
         row = jnp.where((along >= start) & (along < end), first + along, row)
         column = jnp.where((down >= start) & (down < end), first + down, column)
         return end, row, column
@@ -101,7 +110,7 @@
 
 
 def lift_kernel(groups, place_ref, down_ref, up_ref, *refs):
-    pieces, (tokens_ref, out_ref) = refs[:-2], refs[-2:]
+    pieces, (tokens_ref, out_ref, made_ref, sems) = refs[:-4], refs[-4:]
     rank = up_ref.shape[0] // groups
     rows = pieces[0].shape[0]
     tok_all = tokens_ref.shape[0]
@@ -110,19 +119,26 @@
         start = pl.multiple_of(source * rows, rows)
         tokens_ref[pl.ds(start, rows), column : column + piece.shape[1]] = piece[...]
     low = jnp.dot(tokens_ref[...], down_ref[...], preferred_element_type=jnp.float32)
-    place = ring_place(lax.axis_index("tp"), parts)
+    place = exchange_place(lax.axis_index("tp"), parts)
     here = lax.broadcasted_iota(jnp.int32, (slots, tok_all), 0) + place * slots
     chosen = (here == place_ref[...]).astype(jnp.bfloat16)
     picked = jnp.dot(chosen, low.astype(jnp.bfloat16), preferred_element_type=jnp.float32)
     row_panel = lax.broadcasted_iota(jnp.int32, picked.shape, 0) // (slots // groups)
     rank_panel = lax.broadcasted_iota(jnp.int32, picked.shape, 1) // rank
     picked = jnp.where(row_panel == rank_panel, picked, 0.0).astype(jnp.bfloat16)
-    for part, owner in enumerate(ring_of(parts)):
-        out_ref[part] = jnp.dot(
+    copies = []
+    for part, owner in enumerate(exchange_order(parts)):
+        made_ref[part] = jnp.dot(
             picked,
             up_ref[:, owner * columns : (owner + 1) * columns],
             preferred_element_type=jnp.float32,
-        ).astype(out_ref.dtype)
+        ).astype(made_ref.dtype)
+        copies.append(
+            pltpu.make_async_copy(made_ref.at[part], out_ref.at[part], sems.at[part])
+        )
+        copies[-1].start()
+    for copy in copies:
+        copy.wait()
 
 
 def add_kernel(place_ref, base_ref, lifts_ref, out_ref):
@@ -184,7 +200,11 @@
             jax.ShapeDtypeStruct((tp, here, columns), jnp.bfloat16),
         ],
         in_specs=[in_vmem] * (3 + len(pieces)),
-        out_specs=[in_vmem] * 2,
+        out_specs=[in_vmem, pl.BlockSpec(memory_space=pl.ANY)],
+        scratch_shapes=[
+            pltpu.VMEM((tp, here, columns), jnp.bfloat16),
+            pltpu.SemaphoreType.DMA((tp,)),
+        ],
         compiler_params=pltpu.CompilerParams(vmem_limit_bytes=24 * 2**20),
         cost_estimate=pl.CostEstimate(
             flops=2 * groups * rank * (tok_all * width + here * tp * columns),
@@ -194,7 +214,7 @@
         name="lift",
     )(row, down, up, *pieces)
     lifts = lax.all_to_all(
-        lifts, "tp", split_axis=0, concat_axis=0, axis_index_groups=[ring_of(tp)], tiled=True
+        lifts, "tp", split_axis=0, concat_axis=0, axis_index_groups=[exchange_order(tp)], tiled=True
     )
 
     base = jnp.dot(gathered, base_projection_weight, preferred_element_type=jnp.float32)

time: 51.7 us -> 51.4 us (level)
  waiting for transfers between devices: 14.2 us -> 11.9 us
  starting transfers between devices: 19 us -> 21.1 us
    all_to_all x1, waiting for transfers between devices: 4.42 us -> 2.14 us  [on_device(): lax.all_to_all(lifts, 'tp', split_axis=0, concat_axis=0, axis_index_group...]
    all_to_all x1, starting transfers between devices: 5.64 us -> 7.83 us  [on_device(): lax.all_to_all(lifts, 'tp', split_axis=0, concat_axis=0, axis_index_group...]
where the time goes in v21:
time: 51.4 us; the launch traced here: 51.2 us
  starting transfers between devices  21.1 us (41%)
  waiting for transfers between devices  11.9 us (23%)
  matrix products  8.53 us (17%)
  Pallas kernels  5.01 us (10%)
  local copies, waits for them, and re-layouts  4.53 us (9%)
    dot_general x1, matrix products, on_device(): jnp.dot(gathered, base_projection_weight, preferred_element_type=jnp.floa...  8.53 us
    all_to_all x1, starting transfers between devices, on_device(): lax.all_to_all(lifts, 'tp', split_axis=0, concat_axis=0, axis_index_group...  7.83 us
    ppermute x8, starting transfers between devices, ring_gather(): lax.ppermute(x, axis, way)  7.73 us
    ppermute x8, waiting for transfers between devices, ring_gather(): lax.ppermute(x, axis, way)  5.78 us
    unnamed x12, local copies, waits for them, and re-layouts  4.53 us
    ppermute x1, starting transfers between devices, ring_gather(): lax.ppermute(block, axis, down)  2.97 us
    pallas_call x1, Pallas kernels, on_device(): pl.pallas_call(functools.partial(lift_kernel, groups), out_shape=[jax.Sha...  2.19 us
    all_to_all x1, waiting for transfers between devices, on_device(): lax.all_to_all(lifts, 'tp', split_axis=0, concat_axis=0, axis_index_group...  2.14 us
  transfers between devices with their start and end apart: 15, of which 11 were waited for; matrix products, arithmetic and copies ran while one was open for 17% of the time, Pallas kernels for 3%

profile of v21, /device:TPU:0, one launch (start us, length us, event | category | flops | bytes accessed | tf_op | source)
XLA Modules:
  0.0 51.2 jit_solution(7049599134853564929)
XLA Ops:
  0.5 3.0 %collective-permute-start.3 = (bf16[16,8192]{1,0:T(8,128)(2,1)}, bf16[16,8192]{1,0:T(8,128)(2,1)S(1)}, u32[]{:S(2)}, u32[]{:S(2)}) collective-permute-start(bf16[16,8192]{1,0:T(8,128)(2,1)} %bitcast.14), channel_id=1, source_target_pairs={{2,0},{4,2},{6,4},{7,6},{5,7},{3,5},{1,3},{0,1},{10,8},{12,10},{14... | collective-permute-start | bytes 786440 | tf_op jit(solution)/shard_map/ppermute | solution.py:30
  3.5 0.7 %copy-done.3 = s32[2,12]{1,0:T(2,128)S(1)} copy-done((s32[2,12]{1,0:T(2,128)S(1)}, s32[2,12]{1,0:T(2,128)}, u32[]{:S(2)}) %copy-start.3) | copy-done | bytes 120
  4.2 0.7 %copy-done.4 = s32[1,12]{1,0:T(1,128)S(1)} copy-done((s32[1,12]{1,0:T(1,128)S(1)}, s32[1,12]{1,0:T(1,128)}, u32[]{:S(2)}) %copy-start.4) | copy-done | bytes 72
  5.5 1.0 %place.1 = (s32[1,128]{1,0:T(1,128)S(1)}, s32[128,1]{1,0:T(8,128)S(1)}) custom-call(s32[2,12]{1,0:T(2,128)S(1)} %copy-done.3, s32[1,12]{1,0:T(1,128)S(1)} %copy-done.4, s32[16]{0:T(128)S(1)} %copy-done.5), custom_call_target="tpu_custom_call" | custom-call | tf_op jit(solution)/shard_map/place/pallas_call | solution.py:183
  6.6 1.3 %copy-done = bf16[1,64,10240]{2,1,0:T(8,128)(2,1)S(1)} copy-done((bf16[1,64,10240]{2,1,0:T(8,128)(2,1)S(1)}, bf16[1,64,10240]{2,1,0:T(8,128)(2,1)}, u32[]{:S(2)}) %copy-start) | copy-done | bytes 1310744
  7.9 1.2 %copy-done.1 = bf16[1,8192,64]{1,2,0:T(8,128)(2,1)S(1)} copy-done((bf16[1,8192,64]{1,2,0:T(8,128)(2,1)S(1)}, bf16[1,8192,64]{1,2,0:T(8,128)(2,1)}, u32[]{:S(2)}) %copy-start.1) | copy-done | bytes 1048600
  9.1 0.7 %stack.1 = (bf16[8192,128]{1,0:T(8,128)(2,1)S(1)}, bf16[128,10240]{1,0:T(8,128)(2,1)S(1)}) custom-call(bf16[64,8192]{1,0:T(8,128)(2,1)S(1)} %bitcast.13, bf16[64,8192]{1,0:T(8,128)(2,1)S(1)} %collective-permute-done.refs_1_, bf16[64,10240]{1,0:T(8,128)(2,1)S(1)} %bitcast.11, bf16[64,10240]{1,0:T(8,128)(2,1)S(1)} %collective-permute-done.1.refs_3_), custom_call_target="tpu_custom_call" | custom-call | tf_op jit(solution)/shard_map/stack/pallas_call | solution.py:172
  10.2 1.4 %collective-permute-done.2.refs_0_.refs_1_ = bf16[16,8192]{1,0:T(8,128)(2,1)S(1)} collective-permute-done((bf16[16,8192]{1,0:T(8,128)(2,1)}, bf16[16,8192]{1,0:T(8,128)(2,1)S(1)}, u32[]{:S(2)}, u32[]{:S(2)}) %collective-permute-start.2) | collective-permute-done | bytes 262176 | tf_op jit(solution)/shard_map/ppermute | solution.py:30
  12.1 1.7 %collective-permute-start.7 = (bf16[16,4096]{1,0:T(8,128)(2,1)S(1)}, bf16[16,4096]{1,0:T(8,128)(2,1)S(1)}, u32[]{:S(2)}, u32[]{:S(2)}) collective-permute-start(bf16[16,4096]{1,0:T(8,128)(2,1)S(1)} %get-tuple-element.22), channel_id=1, source_target_pairs={{2,0},{4,2},{6,4},{7,6},{5,7},{3,5},{1,3},{0,1},{10,8},{12,10},{14... | collective-permute-start | bytes 393224 | tf_op jit(solution)/shard_map/ppermute | solution.py:35
  13.7 1.6 %collective-permute-start.5 = (bf16[16,4096]{1,0:T(8,128)(2,1)S(1)}, bf16[16,4096]{1,0:T(8,128)(2,1)S(1)}, u32[]{:S(2)}, u32[]{:S(2)}) collective-permute-start(bf16[16,4096]{1,0:T(8,128)(2,1)S(1)} %get-tuple-element.20), channel_id=1, source_target_pairs={{2,0},{4,2},{6,4},{7,6},{5,7},{3,5},{1,3},{0,1},{10,8},{12,10},{14... | collective-permute-start | bytes 393224 | tf_op jit(solution)/shard_map/ppermute | solution.py:35
  15.8 1.7 %collective-permute-done.4.refs_3_ = bf16[16,4096]{1,0:T(8,128)(2,1)S(1)} collective-permute-done((bf16[16,4096]{1,0:T(8,128)(2,1)S(1)}, bf16[16,4096]{1,0:T(8,128)(2,1)S(1)}, u32[]{:S(2)}, u32[]{:S(2)}) %collective-permute-start.4) | collective-permute-done | bytes 131104 | tf_op jit(solution)/shard_map/ppermute | solution.py:35
  18.2 1.4 %collective-permute-start.11 = (bf16[16,4096]{1,0:T(8,128)(2,1)S(1)}, bf16[16,4096]{1,0:T(8,128)(2,1)S(1)}, u32[]{:S(2)}, u32[]{:S(2)}) collective-permute-start(bf16[16,4096]{1,0:T(8,128)(2,1)S(1)} %collective-permute-done.7.refs_6_), channel_id=1, source_target_pairs={{2,0},{4,2},{6,4},{7,6},{5,7},{3,5},{1,3},{0,1},{10,8},{12,10},{14... | collective-permute-start | bytes 393224 | tf_op jit(solution)/shard_map/ppermute | solution.py:35
  19.5 1.4 %collective-permute-done.5.refs_4_ = bf16[16,4096]{1,0:T(8,128)(2,1)S(1)} collective-permute-done((bf16[16,4096]{1,0:T(8,128)(2,1)S(1)}, bf16[16,4096]{1,0:T(8,128)(2,1)S(1)}, u32[]{:S(2)}, u32[]{:S(2)}) %collective-permute-start.5) | collective-permute-done | bytes 131104 | tf_op jit(solution)/shard_map/ppermute | solution.py:35
  21.0 1.2 %collective-permute-start.9 = (bf16[16,4096]{1,0:T(8,128)(2,1)S(1)}, bf16[16,4096]{1,0:T(8,128)(2,1)S(1)}, u32[]{:S(2)}, u32[]{:S(2)}) collective-permute-start(bf16[16,4096]{1,0:T(8,128)(2,1)S(1)} %collective-permute-done.5.refs_4_), channel_id=1, source_target_pairs={{2,0},{4,2},{6,4},{7,6},{5,7},{3,5},{1,3},{0,1},{10,8},{12,10},{14... | collective-permute-start | bytes 393224 | tf_op jit(solution)/shard_map/ppermute | solution.py:35
  22.2 0.8 %collective-permute-start.10 = (bf16[16,4096]{1,0:T(8,128)(2,1)S(1)}, bf16[16,4096]{1,0:T(8,128)(2,1)S(1)}, u32[]{:S(2)}, u32[]{:S(2)}) collective-permute-start(bf16[16,4096]{1,0:T(8,128)(2,1)S(1)} %collective-permute-done.6.refs_5_), channel_id=1, source_target_pairs={{0,2},{2,4},{4,6},{6,7},{7,5},{5,3},{3,1},{1,0},{8,10},{10,12},{12... | collective-permute-start | bytes 393224 | tf_op jit(solution)/shard_map/ppermute | solution.py:35
  23.0 0.9 %collective-permute-done.8.refs_7_ = bf16[16,4096]{1,0:T(8,128)(2,1)S(1)} collective-permute-done((bf16[16,4096]{1,0:T(8,128)(2,1)S(1)}, bf16[16,4096]{1,0:T(8,128)(2,1)S(1)}, u32[]{:S(2)}, u32[]{:S(2)}) %collective-permute-start.8) | collective-permute-done | bytes 131104 | tf_op jit(solution)/shard_map/ppermute | solution.py:35
  24.4 1.5 %collective-permute-start.13 = (bf16[16,4096]{1,0:T(8,128)(2,1)S(1)}, bf16[16,4096]{1,0:T(8,128)(2,1)S(1)}, u32[]{:S(2)}, u32[]{:S(2)}) collective-permute-start(bf16[16,4096]{1,0:T(8,128)(2,1)S(1)} %collective-permute-done.11.refs_10_), channel_id=1, source_target_pairs={{2,0},{4,2},{6,4},{7,6},{5,7},{3,5},{1,3},{0,1},{10,8},{12,10},{14... | collective-permute-start | bytes 393224 | tf_op jit(solution)/shard_map/ppermute | solution.py:37
  26.4 0.8 %collective-permute-done.10.refs_9_ = bf16[16,4096]{1,0:T(8,128)(2,1)S(1)} collective-permute-done((bf16[16,4096]{1,0:T(8,128)(2,1)S(1)}, bf16[16,4096]{1,0:T(8,128)(2,1)S(1)}, u32[]{:S(2)}, u32[]{:S(2)}) %collective-permute-start.10) | collective-permute-done | bytes 131104 | tf_op jit(solution)/shard_map/ppermute | solution.py:35
  27.2 1.6 %collective-permute-done.12.refs_11_ = bf16[16,4096]{1,0:T(8,128)(2,1)S(1)} collective-permute-done((bf16[16,4096]{1,0:T(8,128)(2,1)S(1)}, bf16[16,4096]{1,0:T(8,128)(2,1)S(1)}, u32[]{:S(2)}, u32[]{:S(2)}) %collective-permute-start.12) | collective-permute-done | bytes 131104 | tf_op jit(solution)/shard_map/ppermute | solution.py:37
  29.4 2.2 %lift.1 = (bf16[128,8192]{1,0:T(8,128)(2,1)S(1)}, bf16[8,32,1280]{2,1,0:T(8,128)(2,1)}) custom-call(s32[1,128]{1,0:T(1,128)S(1)} %get-tuple-element.16.refs_4_.place_ref, bf16[8192,128]{1,0:T(8,128)(2,1)S(1)} %get-tuple-element.17.refs_2_.down_ref, bf16[128,10240]{1,0:T(8,128)(2,1)S(1)} %get-tuple-element.18.refs_3_.up_ref, bf16[16,8192]{1,0:T(8,128)(2,1)S(1)} %bitcast.16, ...), custom_call_target="tpu_custom_call" | custom-call | flops 352321536 | bytes 4718592 | tf_op jit(solution)/shard_map/lift/pallas_call | solution.py:196
  31.6 7.8 %all-to-all-start = ((bf16[8,32,1280]{2,1,0:T(8,128)(2,1)}), bf16[8,32,1280]{2,1,0:T(8,128)(2,1)S(1)}, u32[]{:S(2)}, u32[]{:S(2)}) async-start(bf16[8,32,1280]{2,1,0:T(8,128)(2,1)} %get-tuple-element.24), calls=%async_computation | async-start | bytes 1310720 | tf_op jit(solution)/shard_map/all_to_all | solution.py:216
  39.5 8.5 %fusion.base_ref = f32[128,1280]{1,0:T(8,128)S(1)} fusion(bf16[128,8192]{1,0:T(8,128)(2,1)S(1)} %get-tuple-element.23, bf16[8192,1280]{1,0:T(8,128)(2,1)} %param.8), kind=kOutput, calls=%fused_computation | convolution fusion | flops 2684354560 | bytes 23724032 | tf_op jit(solution)/shard_map/dot_general | solution.py:220
  48.0 2.1 %all-to-all-done = bf16[8,32,1280]{2,1,0:T(8,128)(2,1)S(1)} async-done(((bf16[8,32,1280]{2,1,0:T(8,128)(2,1)}), bf16[8,32,1280]{2,1,0:T(8,128)(2,1)S(1)}, u32[]{:S(2)}, u32[]{:S(2)}) %all-to-all-start) | async-done | bytes 655392 | tf_op jit(solution)/shard_map/all_to_all | solution.py:216
  50.1 1.0 %add.1 = bf16[128,1280]{1,0:T(8,128)(2,1)} custom-call(s32[128,1]{1,0:T(8,128)S(1)} %get-tuple-element.15.refs_5_.place_ref, f32[128,1280]{1,0:T(8,128)S(1)} %fusion.base_ref, bf16[256,1280]{1,0:T(8,128)(2,1)S(1)} %bitcast.9), custom_call_target="tpu_custom_call" | custom-call | tf_op jit(solution)/shard_map/add/pallas_call | solution.py:221
  (24 shorter events, 4.8 us)
Async XLA Ops:
  0.0 6.6 %collective-permute-start.1 = (bf16[64,10240]{1,0:T(8,128)(2,1)}, bf16[64,10240]{1,0:T(8,128)(2,1)S(1)}, u32[]{:S(2)}, u32[]{:S(2)}) collective-permute-start(bf16[64,10240]{1,0:T(8,128)(2,1)} %bitcast.10), channel_id=1, source_target_pairs={{8,0},{0,8},{9,1},{1,9},{10,2},{2,10},{11,3},{3,11},{12,4},{4,12},... | collective-permute-start | bytes 3932168 | tf_op jit(solution)/shard_map/ppermute | solution.py:16
  0.5 6.1 %collective-permute-start = (bf16[64,8192]{1,0:T(8,128)(2,1)}, bf16[64,8192]{1,0:T(8,128)(2,1)S(1)}, u32[]{:S(2)}, u32[]{:S(2)}) collective-permute-start(bf16[64,8192]{1,0:T(8,128)(2,1)} %bitcast.12), channel_id=1, source_target_pairs={{8,0},{0,8},{9,1},{1,9},{10,2},{2,10},{11,3},{3,11},{12,4},{4,12},... | collective-permute-start | bytes 3145736 | tf_op jit(solution)/shard_map/ppermute | solution.py:16
  0.5 9.7 %collective-permute-start.3 = (bf16[16,8192]{1,0:T(8,128)(2,1)}, bf16[16,8192]{1,0:T(8,128)(2,1)S(1)}, u32[]{:S(2)}, u32[]{:S(2)}) collective-permute-start(bf16[16,8192]{1,0:T(8,128)(2,1)} %bitcast.14), channel_id=1, source_target_pairs={{2,0},{4,2},{6,4},{7,6},{5,7},{3,5},{1,3},{0,1},{10,8},{12,10},{14... | collective-permute-start | bytes 786440 | tf_op jit(solution)/shard_map/ppermute | solution.py:30
  3.5 8.1 %collective-permute-start.2 = (bf16[16,8192]{1,0:T(8,128)(2,1)}, bf16[16,8192]{1,0:T(8,128)(2,1)S(1)}, u32[]{:S(2)}, u32[]{:S(2)}) collective-permute-start(bf16[16,8192]{1,0:T(8,128)(2,1)} %bitcast.15), channel_id=1, source_target_pairs={{0,2},{2,4},{4,6},{6,7},{7,5},{5,3},{3,1},{1,0},{8,10},{10,12},{12... | collective-permute-start | bytes 786440 | tf_op jit(solution)/shard_map/ppermute | solution.py:30
  3.5 0.7 %copy-start.3 = (s32[2,12]{1,0:T(2,128)S(1)}, s32[2,12]{1,0:T(2,128)}, u32[]{:S(2)}) copy-start(s32[2,12]{1,0:T(2,128)} %ids_ref.1) | copy-start | bytes 292
  4.2 0.7 %copy-start.4 = (s32[1,12]{1,0:T(1,128)S(1)}, s32[1,12]{1,0:T(1,128)}, u32[]{:S(2)}) copy-start(s32[1,12]{1,0:T(1,128)} %lengths_ref.1) | copy-start | bytes 148
  4.9 0.7 %copy-start.5 = (s32[16]{0:T(128)S(1)}, s32[16]{0:T(128)}, u32[]{:S(2)}) copy-start(s32[16]{0:T(128)} %slots_ref.1) | copy-start | bytes 196
  6.6 1.3 %copy-start = (bf16[1,64,10240]{2,1,0:T(8,128)(2,1)S(1)}, bf16[1,64,10240]{2,1,0:T(8,128)(2,1)}, u32[]{:S(2)}) copy-start(bf16[1,64,10240]{2,1,0:T(8,128)(2,1)} %param.10) | copy-start | bytes 3932164
  7.9 1.2 %copy-start.1 = (bf16[1,8192,64]{1,2,0:T(8,128)(2,1)S(1)}, bf16[1,8192,64]{1,2,0:T(8,128)(2,1)}, u32[]{:S(2)}) copy-start(bf16[1,8192,64]{1,2,0:T(8,128)(2,1)} %param.9) | copy-start | bytes 3145732
  11.6 17.8 %copy-start.2 = (bf16[1,16,8192]{2,1,0:T(8,128)(2,1)S(1)}, bf16[1,16,8192]{2,1,0:T(8,128)(2,1)}, u32[]{:S(2)}) copy-start(bf16[1,16,8192]{2,1,0:T(8,128)(2,1)} %param.7) | copy-start | bytes 786436
  11.7 5.9 %collective-permute-start.4 = (bf16[16,4096]{1,0:T(8,128)(2,1)S(1)}, bf16[16,4096]{1,0:T(8,128)(2,1)S(1)}, u32[]{:S(2)}, u32[]{:S(2)}) collective-permute-start(bf16[16,4096]{1,0:T(8,128)(2,1)S(1)} %get-tuple-element.19), channel_id=1, source_target_pairs={{0,2},{2,4},{4,6},{6,7},{7,5},{5,3},{3,1},{1,0},{8,10},{10,12},{12... | collective-permute-start | bytes 393224 | tf_op jit(solution)/shard_map/ppermute | solution.py:35
  12.1 6.1 %collective-permute-start.7 = (bf16[16,4096]{1,0:T(8,128)(2,1)S(1)}, bf16[16,4096]{1,0:T(8,128)(2,1)S(1)}, u32[]{:S(2)}, u32[]{:S(2)}) collective-permute-start(bf16[16,4096]{1,0:T(8,128)(2,1)S(1)} %get-tuple-element.22), channel_id=1, source_target_pairs={{2,0},{4,2},{6,4},{7,6},{5,7},{3,5},{1,3},{0,1},{10,8},{12,10},{14... | collective-permute-start | bytes 393224 | tf_op jit(solution)/shard_map/ppermute | solution.py:35
  13.7 7.3 %collective-permute-start.5 = (bf16[16,4096]{1,0:T(8,128)(2,1)S(1)}, bf16[16,4096]{1,0:T(8,128)(2,1)S(1)}, u32[]{:S(2)}, u32[]{:S(2)}) collective-permute-start(bf16[16,4096]{1,0:T(8,128)(2,1)S(1)} %get-tuple-element.20), channel_id=1, source_target_pairs={{2,0},{4,2},{6,4},{7,6},{5,7},{3,5},{1,3},{0,1},{10,8},{12,10},{14... | collective-permute-start | bytes 393224 | tf_op jit(solution)/shard_map/ppermute | solution.py:35
  15.3 6.9 %collective-permute-start.6 = (bf16[16,4096]{1,0:T(8,128)(2,1)S(1)}, bf16[16,4096]{1,0:T(8,128)(2,1)S(1)}, u32[]{:S(2)}, u32[]{:S(2)}) collective-permute-start(bf16[16,4096]{1,0:T(8,128)(2,1)S(1)} %get-tuple-element.21), channel_id=1, source_target_pairs={{0,2},{2,4},{4,6},{6,7},{7,5},{5,3},{3,1},{1,0},{8,10},{10,12},{12... | collective-permute-start | bytes 393224 | tf_op jit(solution)/shard_map/ppermute | solution.py:35
  17.5 6.4 %collective-permute-start.8 = (bf16[16,4096]{1,0:T(8,128)(2,1)S(1)}, bf16[16,4096]{1,0:T(8,128)(2,1)S(1)}, u32[]{:S(2)}, u32[]{:S(2)}) collective-permute-start(bf16[16,4096]{1,0:T(8,128)(2,1)S(1)} %collective-permute-done.4.refs_3_), channel_id=1, source_target_pairs={{0,2},{2,4},{4,6},{6,7},{7,5},{5,3},{3,1},{1,0},{8,10},{10,12},{12... | collective-permute-start | bytes 393224 | tf_op jit(solution)/shard_map/ppermute | solution.py:35
  18.2 6.3 %collective-permute-start.11 = (bf16[16,4096]{1,0:T(8,128)(2,1)S(1)}, bf16[16,4096]{1,0:T(8,128)(2,1)S(1)}, u32[]{:S(2)}, u32[]{:S(2)}) collective-permute-start(bf16[16,4096]{1,0:T(8,128)(2,1)S(1)} %collective-permute-done.7.refs_6_), channel_id=1, source_target_pairs={{2,0},{4,2},{6,4},{7,6},{5,7},{3,5},{1,3},{0,1},{10,8},{12,10},{14... | collective-permute-start | bytes 393224 | tf_op jit(solution)/shard_map/ppermute | solution.py:35
  21.0 5.4 %collective-permute-start.9 = (bf16[16,4096]{1,0:T(8,128)(2,1)S(1)}, bf16[16,4096]{1,0:T(8,128)(2,1)S(1)}, u32[]{:S(2)}, u32[]{:S(2)}) collective-permute-start(bf16[16,4096]{1,0:T(8,128)(2,1)S(1)} %collective-permute-done.5.refs_4_), channel_id=1, source_target_pairs={{2,0},{4,2},{6,4},{7,6},{5,7},{3,5},{1,3},{0,1},{10,8},{12,10},{14... | collective-permute-start | bytes 393224 | tf_op jit(solution)/shard_map/ppermute | solution.py:35
  22.2 5.0 %collective-permute-start.10 = (bf16[16,4096]{1,0:T(8,128)(2,1)S(1)}, bf16[16,4096]{1,0:T(8,128)(2,1)S(1)}, u32[]{:S(2)}, u32[]{:S(2)}) collective-permute-start(bf16[16,4096]{1,0:T(8,128)(2,1)S(1)} %collective-permute-done.6.refs_5_), channel_id=1, source_target_pairs={{0,2},{2,4},{4,6},{6,7},{7,5},{5,3},{3,1},{1,0},{8,10},{10,12},{12... | collective-permute-start | bytes 393224 | tf_op jit(solution)/shard_map/ppermute | solution.py:35
  23.9 5.0 %collective-permute-start.12 = (bf16[16,4096]{1,0:T(8,128)(2,1)S(1)}, bf16[16,4096]{1,0:T(8,128)(2,1)S(1)}, u32[]{:S(2)}, u32[]{:S(2)}) collective-permute-start(bf16[16,4096]{1,0:T(8,128)(2,1)S(1)} %collective-permute-done.8.refs_7_), channel_id=1, source_target_pairs={{0,2},{2,4},{4,6},{6,7},{7,5},{5,3},{3,1},{1,0},{8,10},{10,12},{12... | collective-permute-start | bytes 393224 | tf_op jit(solution)/shard_map/ppermute | solution.py:37
  24.4 5.0 %collective-permute-start.13 = (bf16[16,4096]{1,0:T(8,128)(2,1)S(1)}, bf16[16,4096]{1,0:T(8,128)(2,1)S(1)}, u32[]{:S(2)}, u32[]{:S(2)}) collective-permute-start(bf16[16,4096]{1,0:T(8,128)(2,1)S(1)} %collective-permute-done.11.refs_10_), channel_id=1, source_target_pairs={{2,0},{4,2},{6,4},{7,6},{5,7},{3,5},{1,3},{0,1},{10,8},{12,10},{14... | collective-permute-start | bytes 393224 | tf_op jit(solution)/shard_map/ppermute | solution.py:37
  31.6 18.5 %all-to-all-start = ((bf16[8,32,1280]{2,1,0:T(8,128)(2,1)}), bf16[8,32,1280]{2,1,0:T(8,128)(2,1)S(1)}, u32[]{:S(2)}, u32[]{:S(2)}) async-start(bf16[8,32,1280]{2,1,0:T(8,128)(2,1)} %get-tuple-element.24), calls=%async_computation | async-start | bytes 1310720 | tf_op jit(solution)/shard_map/all_to_all | solution.py:216

commit v22 on v21

--- a/solution.py
+++ b/solution.py
@@ -60,11 +60,11 @@
 
 def exchange_order(n):
     ring = ring_of(n)
-    return ring[n // 2 :] + ring[: n // 2]
+    return ring[1:] + ring[:1]
 
 
 def exchange_place(i, n):
-    return lax.rem(ring_place(i, n) + n // 2, n)
+    return lax.rem(ring_place(i, n) + n - 1, n)
 
 
 def ring_sources(axis, half):
@@ -89,7 +89,7 @@
         up_ref[s * rank : (s + 1) * rank, :] = up[...]
 
 
-def place_kernel(groups, tp, ids_ref, lengths_ref, slots_ref, row_ref, column_ref):
+def place_kernel(groups, tp, segs, lists_ref, row_ref, column_ref):
     group = lax.axis_index("grp")
     longest = row_ref.shape[1] // 8
     along = lax.broadcasted_iota(jnp.int32, row_ref.shape, 1)
@@ -97,8 +97,9 @@
 
     def add(request, carry):
         start, row, column = carry
-        slot = slots_ref[ids_ref[group, request]]
-        end = start + lengths_ref[0, request]
+        adapter = lists_ref[group * segs + request]
+        slot = lists_ref[(groups + 1) * segs + adapter]
+        end = start + lists_ref[groups * segs + request]
         panel = lax.rem(slot // tp - group + groups, groups)
         first = (exchange_place(lax.rem(slot, tp), tp) * groups + panel) * longest - start
         row = jnp.where((along >= start) & (along < end), first + along, row)
@@ -106,7 +107,7 @@
         return end, row, column
 
     carry = (jnp.int32(0), jnp.zeros_like(along), jnp.zeros_like(down))
-    _, row_ref[...], column_ref[...] = lax.fori_loop(0, ids_ref.shape[1], add, carry)
+    _, row_ref[...], column_ref[...] = lax.fori_loop(0, segs, add, carry)
 
 
 def lift_kernel(groups, place_ref, down_ref, up_ref, *refs):
@@ -180,17 +181,20 @@
         compiler_params=small,
         name="stack",
     )(*panels)
+    lists = jnp.concatenate(
+        [request_adapter_ids.reshape(-1), request_token_lengths.reshape(-1), adapter_store_slot]
+    )
     row, column = pl.pallas_call(
-        functools.partial(place_kernel, groups, tp),
+        functools.partial(place_kernel, groups, tp, request_adapter_ids.shape[1]),
         out_shape=[
             jax.ShapeDtypeStruct((1, tok_all), jnp.int32),
             jax.ShapeDtypeStruct((tok_all, 1), jnp.int32),
         ],
-        in_specs=[in_smem] * 3,
+        in_specs=[in_smem],
         out_specs=[in_vmem] * 2,
         compiler_params=small,
         name="place",
-    )(request_adapter_ids, request_token_lengths, adapter_store_slot)
+    )(lists)
     pieces = ring_gather(tokens[0], "tp", (down, up, row, column))
 
     gathered, lifts = pl.pallas_call(

time: 51.4 us -> 50.8 us (0.988)
  starting transfers between devices: 21.1 us -> 19.3 us
  Pallas kernels: 5.01 us -> 6.26 us
  local copies, waits for them, and re-layouts: 4.53 us -> 3.3 us
  other arithmetic: 0 us -> 0.75 us
    all_to_all x1, starting transfers between devices: 7.83 us -> 5.08 us  [on_device(): lax.all_to_all(lifts, 'tp', split_axis=0, concat_axis=0, axis_index_group...]
    unnamed x12 -> x6, local copies, waits for them, and re-layouts: 4.53 us -> 2.54 us
    pallas_call x1, Pallas kernels: 0.72 us -> 1.98 us  [on_device(): pl.pallas_call(functools.partial(stack_kernel, groups), out_shape=[jax.Sh...]
    all_to_all x1, waiting for transfers between devices: 2.14 us -> 3.3 us  [on_device(): lax.all_to_all(lifts, 'tp', split_axis=0, concat_axis=0, axis_index_group...]
    ppermute x1, starting transfers between devices: 0.56 us -> 1.58 us  [ring_gather(): lax.ppermute(streams[0], axis, up)]
    ppermute x1, starting transfers between devices: 1.47 us -> 0.45 us  [ring_gather(): lax.ppermute(streams[3], axis, down)]
    ppermute x1, waiting for transfers between devices: 0.56 us -> 1.58 us  [ring_gather(): lax.ppermute(streams[3], axis, down)]
    ppermute x8, starting transfers between devices: 7.73 us -> 8.69 us  [ring_gather(): lax.ppermute(x, axis, way)]
  transfers between devices with their start and end apart: 15 -> 15, of which waited for: 11 -> 7; matrix products, arithmetic and copies ran while one was open for 17% -> 20% of each run, Pallas kernels for 3% -> 6%
where the time goes in v22:
time: 50.8 us; the launch traced here: 50.5 us
  starting transfers between devices  19.3 us (38%)
  waiting for transfers between devices  12.2 us (24%)
  matrix products  8.53 us (17%)
  Pallas kernels  6.26 us (12%)
  local copies, waits for them, and re-layouts  3.3 us (6%)
  other arithmetic  0.75 us (1%)
    ppermute x8, starting transfers between devices, ring_gather(): lax.ppermute(x, axis, way)  8.69 us
    dot_general x1, matrix products, on_device(): jnp.dot(gathered, base_projection_weight, preferred_element_type=jnp.floa...  8.53 us
    ppermute x8, waiting for transfers between devices, ring_gather(): lax.ppermute(x, axis, way)  5.27 us
    all_to_all x1, starting transfers between devices, on_device(): lax.all_to_all(lifts, 'tp', split_axis=0, concat_axis=0, axis_index_group...  5.08 us
    all_to_all x1, waiting for transfers between devices, on_device(): lax.all_to_all(lifts, 'tp', split_axis=0, concat_axis=0, axis_index_group...  3.3 us
    ppermute x1, starting transfers between devices, ring_gather(): lax.ppermute(block, axis, down)  2.97 us
    unnamed x6, local copies, waits for them, and re-layouts  2.54 us
    pallas_call x1, Pallas kernels, on_device(): pl.pallas_call(functools.partial(lift_kernel, groups), out_shape=[jax.Sha...  2.2 us
  transfers between devices with their start and end apart: 15, of which 7 were waited for; matrix products, arithmetic and copies ran while one was open for 20% of the time, Pallas kernels for 6%

profile of v22, /device:TPU:0, one launch (start us, length us, event | category | flops | bytes accessed | tf_op | source)
XLA Modules:
  0.0 50.5 jit_solution(15696206609896197159)
XLA Ops:
  0.5 3.0 %collective-permute-start.3 = (bf16[16,8192]{1,0:T(8,128)(2,1)}, bf16[16,8192]{1,0:T(8,128)(2,1)S(1)}, u32[]{:S(2)}, u32[]{:S(2)}) collective-permute-start(bf16[16,8192]{1,0:T(8,128)(2,1)} %bitcast.15), channel_id=1, source_target_pairs={{2,0},{4,2},{6,4},{7,6},{5,7},{3,5},{1,3},{0,1},{10,8},{12,10},{14... | collective-permute-start | bytes 786440 | tf_op jit(solution)/shard_map/ppermute | solution.py:30
  3.5 0.8 %reshape.9 = s32[24]{0:T(128)S(1)} reshape(s32[2,12]{1,0:T(2,128)} %param.11) | data formatting | bytes 192 | tf_op jit(solution)/shard_map/reshape | solution.py:185
  4.3 0.7 %pad_add_fusion.lists_ref = s32[52]{0:T(128)S(1)} fusion(s32[16]{0:T(128)} %param.13, s32[12]{0:T(128)} %bitcast.18, s32[24]{0:T(128)S(1)} %reshape.9), kind=kLoop, calls=%fused_computation | loop fusion | flops 104 | bytes 416 | tf_op jit(solution)/shard_map/concatenate | solution.py:184
  5.0 1.0 %place.1 = (s32[1,128]{1,0:T(1,128)S(1)}, s32[128,1]{1,0:T(8,128)S(1)}) custom-call(s32[52]{0:T(128)S(1)} %pad_add_fusion.lists_ref), custom_call_target="tpu_custom_call" | custom-call | tf_op jit(solution)/shard_map/place/pallas_call | solution.py:187
  6.1 1.3 %copy-done = bf16[1,64,10240]{2,1,0:T(8,128)(2,1)S(1)} copy-done((bf16[1,64,10240]{2,1,0:T(8,128)(2,1)S(1)}, bf16[1,64,10240]{2,1,0:T(8,128)(2,1)}, u32[]{:S(2)}) %copy-start) | copy-done | bytes 1310744
  7.4 1.2 %copy-done.1 = bf16[1,8192,64]{1,2,0:T(8,128)(2,1)S(1)} copy-done((bf16[1,8192,64]{1,2,0:T(8,128)(2,1)S(1)}, bf16[1,8192,64]{1,2,0:T(8,128)(2,1)}, u32[]{:S(2)}) %copy-start.1) | copy-done | bytes 1048600
  8.6 2.0 %stack.1 = (bf16[8192,128]{1,0:T(8,128)(2,1)S(1)}, bf16[128,10240]{1,0:T(8,128)(2,1)S(1)}) custom-call(bf16[64,8192]{1,0:T(8,128)(2,1)S(1)} %bitcast.14, bf16[64,8192]{1,0:T(8,128)(2,1)} %collective-permute-done.refs_1_, bf16[64,10240]{1,0:T(8,128)(2,1)S(1)} %bitcast.12, bf16[64,10240]{1,0:T(8,128)(2,1)S(1)} %collective-permute-done.1.refs_3_), custom_call_target="tpu_custom_call" | custom-call | tf_op jit(solution)/shard_map/stack/pallas_call | solution.py:173
  10.6 1.0 %collective-permute-done.2.refs_0_.refs_1_ = bf16[16,8192]{1,0:T(8,128)(2,1)S(1)} collective-permute-done((bf16[16,8192]{1,0:T(8,128)(2,1)}, bf16[16,8192]{1,0:T(8,128)(2,1)S(1)}, u32[]{:S(2)}, u32[]{:S(2)}) %collective-permute-start.2) | collective-permute-done | bytes 262176 | tf_op jit(solution)/shard_map/ppermute | solution.py:30
  11.7 1.1 %collective-permute-start.4 = (bf16[16,4096]{1,0:T(8,128)(2,1)S(1)}, bf16[16,4096]{1,0:T(8,128)(2,1)S(1)}, u32[]{:S(2)}, u32[]{:S(2)}) collective-permute-start(bf16[16,4096]{1,0:T(8,128)(2,1)S(1)} %get-tuple-element.19), channel_id=1, source_target_pairs={{0,2},{2,4},{4,6},{6,7},{7,5},{5,3},{3,1},{1,0},{8,10},{10,12},{12... | collective-permute-start | bytes 393224 | tf_op jit(solution)/shard_map/ppermute | solution.py:35
  12.8 1.0 %collective-permute-start.7 = (bf16[16,4096]{1,0:T(8,128)(2,1)S(1)}, bf16[16,4096]{1,0:T(8,128)(2,1)S(1)}, u32[]{:S(2)}, u32[]{:S(2)}) collective-permute-start(bf16[16,4096]{1,0:T(8,128)(2,1)S(1)} %get-tuple-element.22), channel_id=1, source_target_pairs={{2,0},{4,2},{6,4},{7,6},{5,7},{3,5},{1,3},{0,1},{10,8},{12,10},{14... | collective-permute-start | bytes 393224 | tf_op jit(solution)/shard_map/ppermute | solution.py:35
  13.8 1.6 %collective-permute-start.5 = (bf16[16,4096]{1,0:T(8,128)(2,1)S(1)}, bf16[16,4096]{1,0:T(8,128)(2,1)S(1)}, u32[]{:S(2)}, u32[]{:S(2)}) collective-permute-start(bf16[16,4096]{1,0:T(8,128)(2,1)S(1)} %get-tuple-element.20), channel_id=1, source_target_pairs={{2,0},{4,2},{6,4},{7,6},{5,7},{3,5},{1,3},{0,1},{10,8},{12,10},{14... | collective-permute-start | bytes 393224 | tf_op jit(solution)/shard_map/ppermute | solution.py:35
  15.8 1.1 %collective-permute-done.4.refs_3_ = bf16[16,4096]{1,0:T(8,128)(2,1)S(1)} collective-permute-done((bf16[16,4096]{1,0:T(8,128)(2,1)S(1)}, bf16[16,4096]{1,0:T(8,128)(2,1)S(1)}, u32[]{:S(2)}, u32[]{:S(2)}) %collective-permute-start.4) | collective-permute-done | bytes 131104 | tf_op jit(solution)/shard_map/ppermute | solution.py:35
  16.9 2.2 %collective-permute-start.8 = (bf16[16,4096]{1,0:T(8,128)(2,1)S(1)}, bf16[16,4096]{1,0:T(8,128)(2,1)S(1)}, u32[]{:S(2)}, u32[]{:S(2)}) collective-permute-start(bf16[16,4096]{1,0:T(8,128)(2,1)S(1)} %collective-permute-done.4.refs_3_), channel_id=1, source_target_pairs={{0,2},{2,4},{4,6},{6,7},{7,5},{5,3},{3,1},{1,0},{8,10},{10,12},{12... | collective-permute-start | bytes 393224 | tf_op jit(solution)/shard_map/ppermute | solution.py:35
  19.5 2.2 %collective-permute-done.5.refs_4_ = bf16[16,4096]{1,0:T(8,128)(2,1)S(1)} collective-permute-done((bf16[16,4096]{1,0:T(8,128)(2,1)S(1)}, bf16[16,4096]{1,0:T(8,128)(2,1)S(1)}, u32[]{:S(2)}, u32[]{:S(2)}) %collective-permute-start.5) | collective-permute-done | bytes 131104 | tf_op jit(solution)/shard_map/ppermute | solution.py:35
  22.0 1.7 %collective-permute-start.10 = (bf16[16,4096]{1,0:T(8,128)(2,1)S(1)}, bf16[16,4096]{1,0:T(8,128)(2,1)S(1)}, u32[]{:S(2)}, u32[]{:S(2)}) collective-permute-start(bf16[16,4096]{1,0:T(8,128)(2,1)S(1)} %collective-permute-done.6.refs_5_), channel_id=1, source_target_pairs={{0,2},{2,4},{4,6},{6,7},{7,5},{5,3},{3,1},{1,0},{8,10},{10,12},{12... | collective-permute-start | bytes 393224 | tf_op jit(solution)/shard_map/ppermute | solution.py:35
  23.7 1.6 %collective-permute-start.12 = (bf16[16,4096]{1,0:T(8,128)(2,1)S(1)}, bf16[16,4096]{1,0:T(8,128)(2,1)S(1)}, u32[]{:S(2)}, u32[]{:S(2)}) collective-permute-start(bf16[16,4096]{1,0:T(8,128)(2,1)S(1)} %collective-permute-done.8.refs_7_), channel_id=1, source_target_pairs={{0,2},{2,4},{4,6},{6,7},{7,5},{5,3},{3,1},{1,0},{8,10},{10,12},{12... | collective-permute-start | bytes 393224 | tf_op jit(solution)/shard_map/ppermute | solution.py:37
  25.8 1.9 %collective-permute-done.9.refs_8_ = bf16[16,4096]{1,0:T(8,128)(2,1)S(1)} collective-permute-done((bf16[16,4096]{1,0:T(8,128)(2,1)S(1)}, bf16[16,4096]{1,0:T(8,128)(2,1)S(1)}, u32[]{:S(2)}, u32[]{:S(2)}) %collective-permute-start.9) | collective-permute-done | bytes 131104 | tf_op jit(solution)/shard_map/ppermute | solution.py:35
  27.7 1.1 %collective-permute-done.12.refs_11_ = bf16[16,4096]{1,0:T(8,128)(2,1)S(1)} collective-permute-done((bf16[16,4096]{1,0:T(8,128)(2,1)S(1)}, bf16[16,4096]{1,0:T(8,128)(2,1)S(1)}, u32[]{:S(2)}, u32[]{:S(2)}) %collective-permute-start.12) | collective-permute-done | bytes 131104 | tf_op jit(solution)/shard_map/ppermute | solution.py:37
  28.7 1.6 %collective-permute-done.13.refs_12_ = bf16[16,4096]{1,0:T(8,128)(2,1)S(1)} collective-permute-done((bf16[16,4096]{1,0:T(8,128)(2,1)S(1)}, bf16[16,4096]{1,0:T(8,128)(2,1)S(1)}, u32[]{:S(2)}, u32[]{:S(2)}) %collective-permute-start.13) | collective-permute-done | bytes 131104 | tf_op jit(solution)/shard_map/ppermute | solution.py:37
  30.3 2.2 %lift.1 = (bf16[128,8192]{1,0:T(8,128)(2,1)S(1)}, bf16[8,32,1280]{2,1,0:T(8,128)(2,1)}) custom-call(s32[1,128]{1,0:T(1,128)S(1)} %get-tuple-element.16.refs_4_.place_ref, bf16[8192,128]{1,0:T(8,128)(2,1)S(1)} %get-tuple-element.17.refs_2_.down_ref, bf16[128,10240]{1,0:T(8,128)(2,1)S(1)} %get-tuple-element.18.refs_3_.up_ref, bf16[16,8192]{1,0:T(8,128)(2,1)S(1)} %bitcast.17, ...), custom_call_target="tpu_custom_call" | custom-call | flops 352321536 | bytes 4718592 | tf_op jit(solution)/shard_map/lift/pallas_call | solution.py:200
  32.5 5.1 %all-to-all-start = ((bf16[8,32,1280]{2,1,0:T(8,128)(2,1)}), bf16[8,32,1280]{2,1,0:T(8,128)(2,1)S(1)}, u32[]{:S(2)}, u32[]{:S(2)}) async-start(bf16[8,32,1280]{2,1,0:T(8,128)(2,1)} %get-tuple-element.24), calls=%async_computation | async-start | bytes 1310720 | tf_op jit(solution)/shard_map/all_to_all | solution.py:220
  37.6 8.5 %fusion.base_ref = f32[128,1280]{1,0:T(8,128)S(1)} fusion(bf16[128,8192]{1,0:T(8,128)(2,1)S(1)} %get-tuple-element.23, bf16[8192,1280]{1,0:T(8,128)(2,1)} %param.8), kind=kOutput, calls=%fused_computation.1 | convolution fusion | flops 2684354560 | bytes 23724032 | tf_op jit(solution)/shard_map/dot_general | solution.py:224
  46.1 3.3 %all-to-all-done = bf16[8,32,1280]{2,1,0:T(8,128)(2,1)S(1)} async-done(((bf16[8,32,1280]{2,1,0:T(8,128)(2,1)}), bf16[8,32,1280]{2,1,0:T(8,128)(2,1)S(1)}, u32[]{:S(2)}, u32[]{:S(2)}) %all-to-all-start) | async-done | bytes 655392 | tf_op jit(solution)/shard_map/all_to_all | solution.py:220
  49.4 1.0 %add.5 = bf16[128,1280]{1,0:T(8,128)(2,1)} custom-call(s32[128,1]{1,0:T(8,128)S(1)} %get-tuple-element.15.refs_5_.place_ref, f32[128,1280]{1,0:T(8,128)S(1)} %fusion.base_ref, bf16[256,1280]{1,0:T(8,128)(2,1)S(1)} %bitcast.10), custom_call_target="tpu_custom_call" | custom-call | tf_op jit(solution)/shard_map/add/pallas_call | solution.py:225
  (20 shorter events, 2.2 us)
Async XLA Ops:
  0.0 6.1 %collective-permute-start.1 = (bf16[64,10240]{1,0:T(8,128)(2,1)}, bf16[64,10240]{1,0:T(8,128)(2,1)S(1)}, u32[]{:S(2)}, u32[]{:S(2)}) collective-permute-start(bf16[64,10240]{1,0:T(8,128)(2,1)} %bitcast.11), channel_id=1, source_target_pairs={{8,0},{0,8},{9,1},{1,9},{10,2},{2,10},{11,3},{3,11},{12,4},{4,12},... | collective-permute-start | bytes 3932168 | tf_op jit(solution)/shard_map/ppermute | solution.py:16
  0.5 5.6 %collective-permute-start = (bf16[64,8192]{1,0:T(8,128)(2,1)}, bf16[64,8192]{1,0:T(8,128)(2,1)}, u32[]{:S(2)}, u32[]{:S(2)}) collective-permute-start(bf16[64,8192]{1,0:T(8,128)(2,1)} %bitcast.13), channel_id=1, source_target_pairs={{8,0},{0,8},{9,1},{1,9},{10,2},{2,10},{11,3},{3,11},{12,4},{4,12},... | collective-permute-start | bytes 3145736 | tf_op jit(solution)/shard_map/ppermute | solution.py:16
  0.5 10.1 %collective-permute-start.3 = (bf16[16,8192]{1,0:T(8,128)(2,1)}, bf16[16,8192]{1,0:T(8,128)(2,1)S(1)}, u32[]{:S(2)}, u32[]{:S(2)}) collective-permute-start(bf16[16,8192]{1,0:T(8,128)(2,1)} %bitcast.15), channel_id=1, source_target_pairs={{2,0},{4,2},{6,4},{7,6},{5,7},{3,5},{1,3},{0,1},{10,8},{12,10},{14... | collective-permute-start | bytes 786440 | tf_op jit(solution)/shard_map/ppermute | solution.py:30
  3.5 8.1 %collective-permute-start.2 = (bf16[16,8192]{1,0:T(8,128)(2,1)}, bf16[16,8192]{1,0:T(8,128)(2,1)S(1)}, u32[]{:S(2)}, u32[]{:S(2)}) collective-permute-start(bf16[16,8192]{1,0:T(8,128)(2,1)} %bitcast.16), channel_id=1, source_target_pairs={{0,2},{2,4},{4,6},{6,7},{7,5},{5,3},{3,1},{1,0},{8,10},{10,12},{12... | collective-permute-start | bytes 786440 | tf_op jit(solution)/shard_map/ppermute | solution.py:30
  6.1 1.3 %copy-start = (bf16[1,64,10240]{2,1,0:T(8,128)(2,1)S(1)}, bf16[1,64,10240]{2,1,0:T(8,128)(2,1)}, u32[]{:S(2)}) copy-start(bf16[1,64,10240]{2,1,0:T(8,128)(2,1)} %param.10) | copy-start | bytes 3932164
  7.4 1.2 %copy-start.1 = (bf16[1,8192,64]{1,2,0:T(8,128)(2,1)S(1)}, bf16[1,8192,64]{1,2,0:T(8,128)(2,1)}, u32[]{:S(2)}) copy-start(bf16[1,8192,64]{1,2,0:T(8,128)(2,1)} %param.9) | copy-start | bytes 3145732
  11.6 18.7 %copy-start.2 = (bf16[1,16,8192]{2,1,0:T(8,128)(2,1)S(1)}, bf16[1,16,8192]{2,1,0:T(8,128)(2,1)}, u32[]{:S(2)}) copy-start(bf16[1,16,8192]{2,1,0:T(8,128)(2,1)} %param.7) | copy-start | bytes 786436
  11.7 5.3 %collective-permute-start.4 = (bf16[16,4096]{1,0:T(8,128)(2,1)S(1)}, bf16[16,4096]{1,0:T(8,128)(2,1)S(1)}, u32[]{:S(2)}, u32[]{:S(2)}) collective-permute-start(bf16[16,4096]{1,0:T(8,128)(2,1)S(1)} %get-tuple-element.19), channel_id=1, source_target_pairs={{0,2},{2,4},{4,6},{6,7},{7,5},{5,3},{3,1},{1,0},{8,10},{10,12},{12... | collective-permute-start | bytes 393224 | tf_op jit(solution)/shard_map/ppermute | solution.py:35
  12.8 6.4 %collective-permute-start.7 = (bf16[16,4096]{1,0:T(8,128)(2,1)S(1)}, bf16[16,4096]{1,0:T(8,128)(2,1)S(1)}, u32[]{:S(2)}, u32[]{:S(2)}) collective-permute-start(bf16[16,4096]{1,0:T(8,128)(2,1)S(1)} %get-tuple-element.22), channel_id=1, source_target_pairs={{2,0},{4,2},{6,4},{7,6},{5,7},{3,5},{1,3},{0,1},{10,8},{12,10},{14... | collective-permute-start | bytes 393224 | tf_op jit(solution)/shard_map/ppermute | solution.py:35
  13.8 8.0 %collective-permute-start.5 = (bf16[16,4096]{1,0:T(8,128)(2,1)S(1)}, bf16[16,4096]{1,0:T(8,128)(2,1)S(1)}, u32[]{:S(2)}, u32[]{:S(2)}) collective-permute-start(bf16[16,4096]{1,0:T(8,128)(2,1)S(1)} %get-tuple-element.20), channel_id=1, source_target_pairs={{2,0},{4,2},{6,4},{7,6},{5,7},{3,5},{1,3},{0,1},{10,8},{12,10},{14... | collective-permute-start | bytes 393224 | tf_op jit(solution)/shard_map/ppermute | solution.py:35
  15.3 6.7 %collective-permute-start.6 = (bf16[16,4096]{1,0:T(8,128)(2,1)S(1)}, bf16[16,4096]{1,0:T(8,128)(2,1)S(1)}, u32[]{:S(2)}, u32[]{:S(2)}) collective-permute-start(bf16[16,4096]{1,0:T(8,128)(2,1)S(1)} %get-tuple-element.21), channel_id=1, source_target_pairs={{0,2},{2,4},{4,6},{6,7},{7,5},{5,3},{3,1},{1,0},{8,10},{10,12},{12... | collective-permute-start | bytes 393224 | tf_op jit(solution)/shard_map/ppermute | solution.py:35
  16.9 6.8 %collective-permute-start.8 = (bf16[16,4096]{1,0:T(8,128)(2,1)S(1)}, bf16[16,4096]{1,0:T(8,128)(2,1)S(1)}, u32[]{:S(2)}, u32[]{:S(2)}) collective-permute-start(bf16[16,4096]{1,0:T(8,128)(2,1)S(1)} %collective-permute-done.4.refs_3_), channel_id=1, source_target_pairs={{0,2},{2,4},{4,6},{6,7},{7,5},{5,3},{3,1},{1,0},{8,10},{10,12},{12... | collective-permute-start | bytes 393224 | tf_op jit(solution)/shard_map/ppermute | solution.py:35
  19.2 6.1 %collective-permute-start.11 = (bf16[16,4096]{1,0:T(8,128)(2,1)S(1)}, bf16[16,4096]{1,0:T(8,128)(2,1)S(1)}, u32[]{:S(2)}, u32[]{:S(2)}) collective-permute-start(bf16[16,4096]{1,0:T(8,128)(2,1)S(1)} %collective-permute-done.7.refs_6_), channel_id=1, source_target_pairs={{2,0},{4,2},{6,4},{7,6},{5,7},{3,5},{1,3},{0,1},{10,8},{12,10},{14... | collective-permute-start | bytes 393224 | tf_op jit(solution)/shard_map/ppermute | solution.py:35
  21.7 5.9 %collective-permute-start.9 = (bf16[16,4096]{1,0:T(8,128)(2,1)S(1)}, bf16[16,4096]{1,0:T(8,128)(2,1)S(1)}, u32[]{:S(2)}, u32[]{:S(2)}) collective-permute-start(bf16[16,4096]{1,0:T(8,128)(2,1)S(1)} %collective-permute-done.5.refs_4_), channel_id=1, source_target_pairs={{2,0},{4,2},{6,4},{7,6},{5,7},{3,5},{1,3},{0,1},{10,8},{12,10},{14... | collective-permute-start | bytes 393224 | tf_op jit(solution)/shard_map/ppermute | solution.py:35
  22.0 5.6 %collective-permute-start.10 = (bf16[16,4096]{1,0:T(8,128)(2,1)S(1)}, bf16[16,4096]{1,0:T(8,128)(2,1)S(1)}, u32[]{:S(2)}, u32[]{:S(2)}) collective-permute-start(bf16[16,4096]{1,0:T(8,128)(2,1)S(1)} %collective-permute-done.6.refs_5_), channel_id=1, source_target_pairs={{0,2},{2,4},{4,6},{6,7},{7,5},{5,3},{3,1},{1,0},{8,10},{10,12},{12... | collective-permute-start | bytes 393224 | tf_op jit(solution)/shard_map/ppermute | solution.py:35
  23.7 5.0 %collective-permute-start.12 = (bf16[16,4096]{1,0:T(8,128)(2,1)S(1)}, bf16[16,4096]{1,0:T(8,128)(2,1)S(1)}, u32[]{:S(2)}, u32[]{:S(2)}) collective-permute-start(bf16[16,4096]{1,0:T(8,128)(2,1)S(1)} %collective-permute-done.8.refs_7_), channel_id=1, source_target_pairs={{0,2},{2,4},{4,6},{6,7},{7,5},{5,3},{3,1},{1,0},{8,10},{10,12},{12... | collective-permute-start | bytes 393224 | tf_op jit(solution)/shard_map/ppermute | solution.py:37
  25.3 5.0 %collective-permute-start.13 = (bf16[16,4096]{1,0:T(8,128)(2,1)S(1)}, bf16[16,4096]{1,0:T(8,128)(2,1)S(1)}, u32[]{:S(2)}, u32[]{:S(2)}) collective-permute-start(bf16[16,4096]{1,0:T(8,128)(2,1)S(1)} %collective-permute-done.11.refs_10_), channel_id=1, source_target_pairs={{2,0},{4,2},{6,4},{7,6},{5,7},{3,5},{1,3},{0,1},{10,8},{12,10},{14... | collective-permute-start | bytes 393224 | tf_op jit(solution)/shard_map/ppermute | solution.py:37
  32.5 16.9 %all-to-all-start = ((bf16[8,32,1280]{2,1,0:T(8,128)(2,1)}), bf16[8,32,1280]{2,1,0:T(8,128)(2,1)S(1)}, u32[]{:S(2)}, u32[]{:S(2)}) async-start(bf16[8,32,1280]{2,1,0:T(8,128)(2,1)} %get-tuple-element.24), calls=%async_computation | async-start | bytes 1310720 | tf_op jit(solution)/shard_map/all_to_all | solution.py:220

commit v23 on v21

--- a/solution.py
+++ b/solution.py
@@ -60,11 +60,11 @@
 
 def exchange_order(n):
     ring = ring_of(n)
-    return ring[n // 2 :] + ring[: n // 2]
+    return ring[1:] + ring[:1]
 
 
 def exchange_place(i, n):
-    return lax.rem(ring_place(i, n) + n // 2, n)
+    return lax.rem(ring_place(i, n) + n - 1, n)
 
 
 def ring_sources(axis, half):

time: 51.4 us -> 50.7 us (0.986)
  starting transfers between devices: 21.1 us -> 19.5 us
  waiting for transfers between devices: 11.9 us -> 12.8 us
    all_to_all x1, starting transfers between devices: 7.83 us -> 6.21 us  [on_device(): lax.all_to_all(lifts, 'tp', split_axis=0, concat_axis=0, axis_index_group...]
    all_to_all x1, waiting for transfers between devices: 2.14 us -> 3.02 us  [on_device(): lax.all_to_all(lifts, 'tp', split_axis=0, concat_axis=0, axis_index_group...]
where the time goes in v23:
time: 50.7 us; the launch traced here: 50.4 us
  starting transfers between devices  19.5 us (38%)
  waiting for transfers between devices  12.8 us (25%)
  matrix products  8.53 us (17%)
  Pallas kernels  5 us (10%)
  local copies, waits for them, and re-layouts  4.53 us (9%)
    dot_general x1, matrix products, on_device(): jnp.dot(gathered, base_projection_weight, preferred_element_type=jnp.floa...  8.53 us
    ppermute x8, starting transfers between devices, ring_gather(): lax.ppermute(x, axis, way)  7.73 us
    all_to_all x1, starting transfers between devices, on_device(): lax.all_to_all(lifts, 'tp', split_axis=0, concat_axis=0, axis_index_group...  6.21 us
    ppermute x8, waiting for transfers between devices, ring_gather(): lax.ppermute(x, axis, way)  5.78 us
    unnamed x12, local copies, waits for them, and re-layouts  4.53 us
    all_to_all x1, waiting for transfers between devices, on_device(): lax.all_to_all(lifts, 'tp', split_axis=0, concat_axis=0, axis_index_group...  3.02 us
    ppermute x1, starting transfers between devices, ring_gather(): lax.ppermute(block, axis, down)  2.97 us
    pallas_call x1, Pallas kernels, on_device(): pl.pallas_call(functools.partial(lift_kernel, groups), out_shape=[jax.Sha...  2.19 us
  transfers between devices with their start and end apart: 15, of which 11 were waited for; matrix products, arithmetic and copies ran while one was open for 17% of the time, Pallas kernels for 3%

profile of v23, /device:TPU:0, one launch (start us, length us, event | category | flops | bytes accessed | tf_op | source)
XLA Modules:
  0.0 50.4 jit_solution(14903624938156491152)
XLA Ops:
  0.5 3.0 %collective-permute-start.3 = (bf16[16,8192]{1,0:T(8,128)(2,1)}, bf16[16,8192]{1,0:T(8,128)(2,1)S(1)}, u32[]{:S(2)}, u32[]{:S(2)}) collective-permute-start(bf16[16,8192]{1,0:T(8,128)(2,1)} %bitcast.14), channel_id=1, source_target_pairs={{2,0},{4,2},{6,4},{7,6},{5,7},{3,5},{1,3},{0,1},{10,8},{12,10},{14... | collective-permute-start | bytes 786440 | tf_op jit(solution)/shard_map/ppermute | solution.py:30
  3.5 0.7 %copy-done.3 = s32[2,12]{1,0:T(2,128)S(1)} copy-done((s32[2,12]{1,0:T(2,128)S(1)}, s32[2,12]{1,0:T(2,128)}, u32[]{:S(2)}) %copy-start.3) | copy-done | bytes 120
  4.2 0.7 %copy-done.4 = s32[1,12]{1,0:T(1,128)S(1)} copy-done((s32[1,12]{1,0:T(1,128)S(1)}, s32[1,12]{1,0:T(1,128)}, u32[]{:S(2)}) %copy-start.4) | copy-done | bytes 72
  5.5 1.0 %place.1 = (s32[1,128]{1,0:T(1,128)S(1)}, s32[128,1]{1,0:T(8,128)S(1)}) custom-call(s32[2,12]{1,0:T(2,128)S(1)} %copy-done.3, s32[1,12]{1,0:T(1,128)S(1)} %copy-done.4, s32[16]{0:T(128)S(1)} %copy-done.5), custom_call_target="tpu_custom_call" | custom-call | tf_op jit(solution)/shard_map/place/pallas_call | solution.py:183
  6.6 1.3 %copy-done = bf16[1,64,10240]{2,1,0:T(8,128)(2,1)S(1)} copy-done((bf16[1,64,10240]{2,1,0:T(8,128)(2,1)S(1)}, bf16[1,64,10240]{2,1,0:T(8,128)(2,1)}, u32[]{:S(2)}) %copy-start) | copy-done | bytes 1310744
  7.9 1.2 %copy-done.1 = bf16[1,8192,64]{1,2,0:T(8,128)(2,1)S(1)} copy-done((bf16[1,8192,64]{1,2,0:T(8,128)(2,1)S(1)}, bf16[1,8192,64]{1,2,0:T(8,128)(2,1)}, u32[]{:S(2)}) %copy-start.1) | copy-done | bytes 1048600
  9.1 0.7 %stack.1 = (bf16[8192,128]{1,0:T(8,128)(2,1)S(1)}, bf16[128,10240]{1,0:T(8,128)(2,1)S(1)}) custom-call(bf16[64,8192]{1,0:T(8,128)(2,1)S(1)} %bitcast.13, bf16[64,8192]{1,0:T(8,128)(2,1)S(1)} %collective-permute-done.refs_1_, bf16[64,10240]{1,0:T(8,128)(2,1)S(1)} %bitcast.11, bf16[64,10240]{1,0:T(8,128)(2,1)S(1)} %collective-permute-done.1.refs_3_), custom_call_target="tpu_custom_call" | custom-call | tf_op jit(solution)/shard_map/stack/pallas_call | solution.py:172
  10.2 1.4 %collective-permute-done.2.refs_0_.refs_1_ = bf16[16,8192]{1,0:T(8,128)(2,1)S(1)} collective-permute-done((bf16[16,8192]{1,0:T(8,128)(2,1)}, bf16[16,8192]{1,0:T(8,128)(2,1)S(1)}, u32[]{:S(2)}, u32[]{:S(2)}) %collective-permute-start.2) | collective-permute-done | bytes 262176 | tf_op jit(solution)/shard_map/ppermute | solution.py:30
  12.1 1.7 %collective-permute-start.7 = (bf16[16,4096]{1,0:T(8,128)(2,1)S(1)}, bf16[16,4096]{1,0:T(8,128)(2,1)S(1)}, u32[]{:S(2)}, u32[]{:S(2)}) collective-permute-start(bf16[16,4096]{1,0:T(8,128)(2,1)S(1)} %get-tuple-element.22), channel_id=1, source_target_pairs={{2,0},{4,2},{6,4},{7,6},{5,7},{3,5},{1,3},{0,1},{10,8},{12,10},{14... | collective-permute-start | bytes 393224 | tf_op jit(solution)/shard_map/ppermute | solution.py:35
  13.7 1.6 %collective-permute-start.5 = (bf16[16,4096]{1,0:T(8,128)(2,1)S(1)}, bf16[16,4096]{1,0:T(8,128)(2,1)S(1)}, u32[]{:S(2)}, u32[]{:S(2)}) collective-permute-start(bf16[16,4096]{1,0:T(8,128)(2,1)S(1)} %get-tuple-element.20), channel_id=1, source_target_pairs={{2,0},{4,2},{6,4},{7,6},{5,7},{3,5},{1,3},{0,1},{10,8},{12,10},{14... | collective-permute-start | bytes 393224 | tf_op jit(solution)/shard_map/ppermute | solution.py:35
  15.8 1.7 %collective-permute-done.4.refs_3_ = bf16[16,4096]{1,0:T(8,128)(2,1)S(1)} collective-permute-done((bf16[16,4096]{1,0:T(8,128)(2,1)S(1)}, bf16[16,4096]{1,0:T(8,128)(2,1)S(1)}, u32[]{:S(2)}, u32[]{:S(2)}) %collective-permute-start.4) | collective-permute-done | bytes 131104 | tf_op jit(solution)/shard_map/ppermute | solution.py:35
  18.2 1.4 %collective-permute-start.11 = (bf16[16,4096]{1,0:T(8,128)(2,1)S(1)}, bf16[16,4096]{1,0:T(8,128)(2,1)S(1)}, u32[]{:S(2)}, u32[]{:S(2)}) collective-permute-start(bf16[16,4096]{1,0:T(8,128)(2,1)S(1)} %collective-permute-done.7.refs_6_), channel_id=1, source_target_pairs={{2,0},{4,2},{6,4},{7,6},{5,7},{3,5},{1,3},{0,1},{10,8},{12,10},{14... | collective-permute-start | bytes 393224 | tf_op jit(solution)/shard_map/ppermute | solution.py:35
  19.5 1.4 %collective-permute-done.5.refs_4_ = bf16[16,4096]{1,0:T(8,128)(2,1)S(1)} collective-permute-done((bf16[16,4096]{1,0:T(8,128)(2,1)S(1)}, bf16[16,4096]{1,0:T(8,128)(2,1)S(1)}, u32[]{:S(2)}, u32[]{:S(2)}) %collective-permute-start.5) | collective-permute-done | bytes 131104 | tf_op jit(solution)/shard_map/ppermute | solution.py:35
  21.0 1.2 %collective-permute-start.9 = (bf16[16,4096]{1,0:T(8,128)(2,1)S(1)}, bf16[16,4096]{1,0:T(8,128)(2,1)S(1)}, u32[]{:S(2)}, u32[]{:S(2)}) collective-permute-start(bf16[16,4096]{1,0:T(8,128)(2,1)S(1)} %collective-permute-done.5.refs_4_), channel_id=1, source_target_pairs={{2,0},{4,2},{6,4},{7,6},{5,7},{3,5},{1,3},{0,1},{10,8},{12,10},{14... | collective-permute-start | bytes 393224 | tf_op jit(solution)/shard_map/ppermute | solution.py:35
  22.2 0.8 %collective-permute-start.10 = (bf16[16,4096]{1,0:T(8,128)(2,1)S(1)}, bf16[16,4096]{1,0:T(8,128)(2,1)S(1)}, u32[]{:S(2)}, u32[]{:S(2)}) collective-permute-start(bf16[16,4096]{1,0:T(8,128)(2,1)S(1)} %collective-permute-done.6.refs_5_), channel_id=1, source_target_pairs={{0,2},{2,4},{4,6},{6,7},{7,5},{5,3},{3,1},{1,0},{8,10},{10,12},{12... | collective-permute-start | bytes 393224 | tf_op jit(solution)/shard_map/ppermute | solution.py:35
  23.0 0.9 %collective-permute-done.8.refs_7_ = bf16[16,4096]{1,0:T(8,128)(2,1)S(1)} collective-permute-done((bf16[16,4096]{1,0:T(8,128)(2,1)S(1)}, bf16[16,4096]{1,0:T(8,128)(2,1)S(1)}, u32[]{:S(2)}, u32[]{:S(2)}) %collective-permute-start.8) | collective-permute-done | bytes 131104 | tf_op jit(solution)/shard_map/ppermute | solution.py:35
  24.4 1.5 %collective-permute-start.13 = (bf16[16,4096]{1,0:T(8,128)(2,1)S(1)}, bf16[16,4096]{1,0:T(8,128)(2,1)S(1)}, u32[]{:S(2)}, u32[]{:S(2)}) collective-permute-start(bf16[16,4096]{1,0:T(8,128)(2,1)S(1)} %collective-permute-done.11.refs_10_), channel_id=1, source_target_pairs={{2,0},{4,2},{6,4},{7,6},{5,7},{3,5},{1,3},{0,1},{10,8},{12,10},{14... | collective-permute-start | bytes 393224 | tf_op jit(solution)/shard_map/ppermute | solution.py:37
  26.4 0.8 %collective-permute-done.10.refs_9_ = bf16[16,4096]{1,0:T(8,128)(2,1)S(1)} collective-permute-done((bf16[16,4096]{1,0:T(8,128)(2,1)S(1)}, bf16[16,4096]{1,0:T(8,128)(2,1)S(1)}, u32[]{:S(2)}, u32[]{:S(2)}) %collective-permute-start.10) | collective-permute-done | bytes 131104 | tf_op jit(solution)/shard_map/ppermute | solution.py:35
  27.2 1.6 %collective-permute-done.12.refs_11_ = bf16[16,4096]{1,0:T(8,128)(2,1)S(1)} collective-permute-done((bf16[16,4096]{1,0:T(8,128)(2,1)S(1)}, bf16[16,4096]{1,0:T(8,128)(2,1)S(1)}, u32[]{:S(2)}, u32[]{:S(2)}) %collective-permute-start.12) | collective-permute-done | bytes 131104 | tf_op jit(solution)/shard_map/ppermute | solution.py:37
  29.4 2.2 %lift.1 = (bf16[128,8192]{1,0:T(8,128)(2,1)S(1)}, bf16[8,32,1280]{2,1,0:T(8,128)(2,1)}) custom-call(s32[1,128]{1,0:T(1,128)S(1)} %get-tuple-element.16.refs_4_.place_ref, bf16[8192,128]{1,0:T(8,128)(2,1)S(1)} %get-tuple-element.17.refs_2_.down_ref, bf16[128,10240]{1,0:T(8,128)(2,1)S(1)} %get-tuple-element.18.refs_3_.up_ref, bf16[16,8192]{1,0:T(8,128)(2,1)S(1)} %bitcast.16, ...), custom_call_target="tpu_custom_call" | custom-call | flops 352321536 | bytes 4718592 | tf_op jit(solution)/shard_map/lift/pallas_call | solution.py:196
  31.6 6.2 %all-to-all-start = ((bf16[8,32,1280]{2,1,0:T(8,128)(2,1)}), bf16[8,32,1280]{2,1,0:T(8,128)(2,1)S(1)}, u32[]{:S(2)}, u32[]{:S(2)}) async-start(bf16[8,32,1280]{2,1,0:T(8,128)(2,1)} %get-tuple-element.24), calls=%async_computation | async-start | bytes 1310720 | tf_op jit(solution)/shard_map/all_to_all | solution.py:216
  37.8 8.5 %fusion.base_ref = f32[128,1280]{1,0:T(8,128)S(1)} fusion(bf16[128,8192]{1,0:T(8,128)(2,1)S(1)} %get-tuple-element.23, bf16[8192,1280]{1,0:T(8,128)(2,1)} %param.8), kind=kOutput, calls=%fused_computation | convolution fusion | flops 2684354560 | bytes 23724032 | tf_op jit(solution)/shard_map/dot_general | solution.py:220
  46.4 3.0 %all-to-all-done = bf16[8,32,1280]{2,1,0:T(8,128)(2,1)S(1)} async-done(((bf16[8,32,1280]{2,1,0:T(8,128)(2,1)}), bf16[8,32,1280]{2,1,0:T(8,128)(2,1)S(1)}, u32[]{:S(2)}, u32[]{:S(2)}) %all-to-all-start) | async-done | bytes 655392 | tf_op jit(solution)/shard_map/all_to_all | solution.py:216
  49.4 1.0 %add.1 = bf16[128,1280]{1,0:T(8,128)(2,1)} custom-call(s32[128,1]{1,0:T(8,128)S(1)} %get-tuple-element.15.refs_5_.place_ref, f32[128,1280]{1,0:T(8,128)S(1)} %fusion.base_ref, bf16[256,1280]{1,0:T(8,128)(2,1)S(1)} %bitcast.9), custom_call_target="tpu_custom_call" | custom-call | tf_op jit(solution)/shard_map/add/pallas_call | solution.py:221
  (24 shorter events, 4.8 us)
Async XLA Ops:
  0.0 6.6 %collective-permute-start.1 = (bf16[64,10240]{1,0:T(8,128)(2,1)}, bf16[64,10240]{1,0:T(8,128)(2,1)S(1)}, u32[]{:S(2)}, u32[]{:S(2)}) collective-permute-start(bf16[64,10240]{1,0:T(8,128)(2,1)} %bitcast.10), channel_id=1, source_target_pairs={{8,0},{0,8},{9,1},{1,9},{10,2},{2,10},{11,3},{3,11},{12,4},{4,12},... | collective-permute-start | bytes 3932168 | tf_op jit(solution)/shard_map/ppermute | solution.py:16
  0.5 6.1 %collective-permute-start = (bf16[64,8192]{1,0:T(8,128)(2,1)}, bf16[64,8192]{1,0:T(8,128)(2,1)S(1)}, u32[]{:S(2)}, u32[]{:S(2)}) collective-permute-start(bf16[64,8192]{1,0:T(8,128)(2,1)} %bitcast.12), channel_id=1, source_target_pairs={{8,0},{0,8},{9,1},{1,9},{10,2},{2,10},{11,3},{3,11},{12,4},{4,12},... | collective-permute-start | bytes 3145736 | tf_op jit(solution)/shard_map/ppermute | solution.py:16
  0.5 9.7 %collective-permute-start.3 = (bf16[16,8192]{1,0:T(8,128)(2,1)}, bf16[16,8192]{1,0:T(8,128)(2,1)S(1)}, u32[]{:S(2)}, u32[]{:S(2)}) collective-permute-start(bf16[16,8192]{1,0:T(8,128)(2,1)} %bitcast.14), channel_id=1, source_target_pairs={{2,0},{4,2},{6,4},{7,6},{5,7},{3,5},{1,3},{0,1},{10,8},{12,10},{14... | collective-permute-start | bytes 786440 | tf_op jit(solution)/shard_map/ppermute | solution.py:30
  3.5 8.1 %collective-permute-start.2 = (bf16[16,8192]{1,0:T(8,128)(2,1)}, bf16[16,8192]{1,0:T(8,128)(2,1)S(1)}, u32[]{:S(2)}, u32[]{:S(2)}) collective-permute-start(bf16[16,8192]{1,0:T(8,128)(2,1)} %bitcast.15), channel_id=1, source_target_pairs={{0,2},{2,4},{4,6},{6,7},{7,5},{5,3},{3,1},{1,0},{8,10},{10,12},{12... | collective-permute-start | bytes 786440 | tf_op jit(solution)/shard_map/ppermute | solution.py:30
  3.5 0.7 %copy-start.3 = (s32[2,12]{1,0:T(2,128)S(1)}, s32[2,12]{1,0:T(2,128)}, u32[]{:S(2)}) copy-start(s32[2,12]{1,0:T(2,128)} %ids_ref.1) | copy-start | bytes 292
  4.2 0.7 %copy-start.4 = (s32[1,12]{1,0:T(1,128)S(1)}, s32[1,12]{1,0:T(1,128)}, u32[]{:S(2)}) copy-start(s32[1,12]{1,0:T(1,128)} %lengths_ref.1) | copy-start | bytes 148
  4.9 0.7 %copy-start.5 = (s32[16]{0:T(128)S(1)}, s32[16]{0:T(128)}, u32[]{:S(2)}) copy-start(s32[16]{0:T(128)} %slots_ref.1) | copy-start | bytes 196
  6.6 1.3 %copy-start = (bf16[1,64,10240]{2,1,0:T(8,128)(2,1)S(1)}, bf16[1,64,10240]{2,1,0:T(8,128)(2,1)}, u32[]{:S(2)}) copy-start(bf16[1,64,10240]{2,1,0:T(8,128)(2,1)} %param.10) | copy-start | bytes 3932164
  7.9 1.2 %copy-start.1 = (bf16[1,8192,64]{1,2,0:T(8,128)(2,1)S(1)}, bf16[1,8192,64]{1,2,0:T(8,128)(2,1)}, u32[]{:S(2)}) copy-start(bf16[1,8192,64]{1,2,0:T(8,128)(2,1)} %param.9) | copy-start | bytes 3145732
  11.6 17.8 %copy-start.2 = (bf16[1,16,8192]{2,1,0:T(8,128)(2,1)S(1)}, bf16[1,16,8192]{2,1,0:T(8,128)(2,1)}, u32[]{:S(2)}) copy-start(bf16[1,16,8192]{2,1,0:T(8,128)(2,1)} %param.7) | copy-start | bytes 786436
  11.7 5.9 %collective-permute-start.4 = (bf16[16,4096]{1,0:T(8,128)(2,1)S(1)}, bf16[16,4096]{1,0:T(8,128)(2,1)S(1)}, u32[]{:S(2)}, u32[]{:S(2)}) collective-permute-start(bf16[16,4096]{1,0:T(8,128)(2,1)S(1)} %get-tuple-element.19), channel_id=1, source_target_pairs={{0,2},{2,4},{4,6},{6,7},{7,5},{5,3},{3,1},{1,0},{8,10},{10,12},{12... | collective-permute-start | bytes 393224 | tf_op jit(solution)/shard_map/ppermute | solution.py:35
  12.1 6.1 %collective-permute-start.7 = (bf16[16,4096]{1,0:T(8,128)(2,1)S(1)}, bf16[16,4096]{1,0:T(8,128)(2,1)S(1)}, u32[]{:S(2)}, u32[]{:S(2)}) collective-permute-start(bf16[16,4096]{1,0:T(8,128)(2,1)S(1)} %get-tuple-element.22), channel_id=1, source_target_pairs={{2,0},{4,2},{6,4},{7,6},{5,7},{3,5},{1,3},{0,1},{10,8},{12,10},{14... | collective-permute-start | bytes 393224 | tf_op jit(solution)/shard_map/ppermute | solution.py:35
  13.7 7.3 %collective-permute-start.5 = (bf16[16,4096]{1,0:T(8,128)(2,1)S(1)}, bf16[16,4096]{1,0:T(8,128)(2,1)S(1)}, u32[]{:S(2)}, u32[]{:S(2)}) collective-permute-start(bf16[16,4096]{1,0:T(8,128)(2,1)S(1)} %get-tuple-element.20), channel_id=1, source_target_pairs={{2,0},{4,2},{6,4},{7,6},{5,7},{3,5},{1,3},{0,1},{10,8},{12,10},{14... | collective-permute-start | bytes 393224 | tf_op jit(solution)/shard_map/ppermute | solution.py:35
  15.3 6.9 %collective-permute-start.6 = (bf16[16,4096]{1,0:T(8,128)(2,1)S(1)}, bf16[16,4096]{1,0:T(8,128)(2,1)S(1)}, u32[]{:S(2)}, u32[]{:S(2)}) collective-permute-start(bf16[16,4096]{1,0:T(8,128)(2,1)S(1)} %get-tuple-element.21), channel_id=1, source_target_pairs={{0,2},{2,4},{4,6},{6,7},{7,5},{5,3},{3,1},{1,0},{8,10},{10,12},{12... | collective-permute-start | bytes 393224 | tf_op jit(solution)/shard_map/ppermute | solution.py:35
  17.5 6.4 %collective-permute-start.8 = (bf16[16,4096]{1,0:T(8,128)(2,1)S(1)}, bf16[16,4096]{1,0:T(8,128)(2,1)S(1)}, u32[]{:S(2)}, u32[]{:S(2)}) collective-permute-start(bf16[16,4096]{1,0:T(8,128)(2,1)S(1)} %collective-permute-done.4.refs_3_), channel_id=1, source_target_pairs={{0,2},{2,4},{4,6},{6,7},{7,5},{5,3},{3,1},{1,0},{8,10},{10,12},{12... | collective-permute-start | bytes 393224 | tf_op jit(solution)/shard_map/ppermute | solution.py:35
  18.2 6.3 %collective-permute-start.11 = (bf16[16,4096]{1,0:T(8,128)(2,1)S(1)}, bf16[16,4096]{1,0:T(8,128)(2,1)S(1)}, u32[]{:S(2)}, u32[]{:S(2)}) collective-permute-start(bf16[16,4096]{1,0:T(8,128)(2,1)S(1)} %collective-permute-done.7.refs_6_), channel_id=1, source_target_pairs={{2,0},{4,2},{6,4},{7,6},{5,7},{3,5},{1,3},{0,1},{10,8},{12,10},{14... | collective-permute-start | bytes 393224 | tf_op jit(solution)/shard_map/ppermute | solution.py:35
  21.0 5.4 %collective-permute-start.9 = (bf16[16,4096]{1,0:T(8,128)(2,1)S(1)}, bf16[16,4096]{1,0:T(8,128)(2,1)S(1)}, u32[]{:S(2)}, u32[]{:S(2)}) collective-permute-start(bf16[16,4096]{1,0:T(8,128)(2,1)S(1)} %collective-permute-done.5.refs_4_), channel_id=1, source_target_pairs={{2,0},{4,2},{6,4},{7,6},{5,7},{3,5},{1,3},{0,1},{10,8},{12,10},{14... | collective-permute-start | bytes 393224 | tf_op jit(solution)/shard_map/ppermute | solution.py:35
  22.2 5.0 %collective-permute-start.10 = (bf16[16,4096]{1,0:T(8,128)(2,1)S(1)}, bf16[16,4096]{1,0:T(8,128)(2,1)S(1)}, u32[]{:S(2)}, u32[]{:S(2)}) collective-permute-start(bf16[16,4096]{1,0:T(8,128)(2,1)S(1)} %collective-permute-done.6.refs_5_), channel_id=1, source_target_pairs={{0,2},{2,4},{4,6},{6,7},{7,5},{5,3},{3,1},{1,0},{8,10},{10,12},{12... | collective-permute-start | bytes 393224 | tf_op jit(solution)/shard_map/ppermute | solution.py:35
  23.9 5.0 %collective-permute-start.12 = (bf16[16,4096]{1,0:T(8,128)(2,1)S(1)}, bf16[16,4096]{1,0:T(8,128)(2,1)S(1)}, u32[]{:S(2)}, u32[]{:S(2)}) collective-permute-start(bf16[16,4096]{1,0:T(8,128)(2,1)S(1)} %collective-permute-done.8.refs_7_), channel_id=1, source_target_pairs={{0,2},{2,4},{4,6},{6,7},{7,5},{5,3},{3,1},{1,0},{8,10},{10,12},{12... | collective-permute-start | bytes 393224 | tf_op jit(solution)/shard_map/ppermute | solution.py:37
  24.4 5.0 %collective-permute-start.13 = (bf16[16,4096]{1,0:T(8,128)(2,1)S(1)}, bf16[16,4096]{1,0:T(8,128)(2,1)S(1)}, u32[]{:S(2)}, u32[]{:S(2)}) collective-permute-start(bf16[16,4096]{1,0:T(8,128)(2,1)S(1)} %collective-permute-done.11.refs_10_), channel_id=1, source_target_pairs={{2,0},{4,2},{6,4},{7,6},{5,7},{3,5},{1,3},{0,1},{10,8},{12,10},{14... | collective-permute-start | bytes 393224 | tf_op jit(solution)/shard_map/ppermute | solution.py:37
  31.6 17.8 %all-to-all-start = ((bf16[8,32,1280]{2,1,0:T(8,128)(2,1)}), bf16[8,32,1280]{2,1,0:T(8,128)(2,1)S(1)}, u32[]{:S(2)}, u32[]{:S(2)}) async-start(bf16[8,32,1280]{2,1,0:T(8,128)(2,1)} %get-tuple-element.24), calls=%async_computation | async-start | bytes 1310720 | tf_op jit(solution)/shard_map/all_to_all | solution.py:216

commit v24 on v23

--- a/solution.py
+++ b/solution.py
@@ -81,15 +81,13 @@
     return sources
 
 
-def stack_kernel(groups, *refs):
-    downs, ups, (down_ref, up_ref) = refs[:groups], refs[groups:-2], refs[-2:]
+def prepare_kernel(groups, tp, ids_ref, lengths_ref, slots_ref, *refs):
+    downs, ups = refs[:groups], refs[groups:-4]
+    down_ref, up_ref, row_ref, column_ref = refs[-4:]
     rank = ups[0].shape[0]
     down_ref[...] = jnp.concatenate([down[...] for down in downs], axis=0).T
     for s, up in enumerate(ups):
         up_ref[s * rank : (s + 1) * rank, :] = up[...]
-
-
-def place_kernel(groups, tp, ids_ref, lengths_ref, slots_ref, row_ref, column_ref):
     group = lax.axis_index("grp")
     longest = row_ref.shape[1] // 8
     along = lax.broadcasted_iota(jnp.int32, row_ref.shape, 1)
@@ -141,11 +139,21 @@
         copy.wait()
 
 
-def add_kernel(place_ref, base_ref, lifts_ref, out_ref):
+def add_kernel(place_ref, base_ref, lifts_ref, out_ref, made_ref, sems):
     place = lax.broadcasted_iota(jnp.int32, (base_ref.shape[0], lifts_ref.shape[0]), 1)
     chosen = (place == place_ref[...]).astype(jnp.bfloat16)
-    lift = jnp.dot(chosen, lifts_ref[...], preferred_element_type=jnp.float32)
-    out_ref[...] = (base_ref[...] + adapter_scale * lift).astype(out_ref.dtype)
+    size = base_ref.shape[1] // sems.shape[0]
+    copies = []
+    for i in range(sems.shape[0]):
+        part = pl.ds(i * size, size)
+        lift = jnp.dot(chosen, lifts_ref[:, part], preferred_element_type=jnp.float32)
+        made_ref[:, part] = (base_ref[:, part] + adapter_scale * lift).astype(made_ref.dtype)
+        copies.append(
+            pltpu.make_async_copy(made_ref.at[:, part], out_ref.at[:, part], sems.at[i])
+        )
+        copies[-1].start()
+    for copy in copies:
+        copy.wait()
 
 
 def on_device(
@@ -169,28 +177,19 @@
     small = pltpu.CompilerParams(vmem_limit_bytes=16 * 2**20)
 
     panels = swapped(adapter_down_panels[0].T, "grp") + swapped(adapter_up_panels[0], "grp")
-    down, up = pl.pallas_call(
-        functools.partial(stack_kernel, groups),
+    down, up, row, column = pl.pallas_call(
+        functools.partial(prepare_kernel, groups, tp),
         out_shape=[
             jax.ShapeDtypeStruct((width, groups * rank), jnp.bfloat16),
             jax.ShapeDtypeStruct((groups * rank, tp * columns), jnp.bfloat16),
-        ],
-        in_specs=[in_vmem] * len(panels),
-        out_specs=[in_vmem] * 2,
-        compiler_params=small,
-        name="stack",
-    )(*panels)
-    row, column = pl.pallas_call(
-        functools.partial(place_kernel, groups, tp),
-        out_shape=[
             jax.ShapeDtypeStruct((1, tok_all), jnp.int32),
             jax.ShapeDtypeStruct((tok_all, 1), jnp.int32),
         ],
-        in_specs=[in_smem] * 3,
-        out_specs=[in_vmem] * 2,
+        in_specs=[in_smem] * 3 + [in_vmem] * len(panels),
+        out_specs=[in_vmem] * 4,
         compiler_params=small,
-        name="place",
-    )(request_adapter_ids, request_token_lengths, adapter_store_slot)
+        name="prepare",
+    )(request_adapter_ids, request_token_lengths, adapter_store_slot, *panels)
     pieces = ring_gather(tokens[0], "tp", (down, up, row, column))
 
     gathered, lifts = pl.pallas_call(
@@ -222,7 +221,11 @@
         add_kernel,
         out_shape=jax.ShapeDtypeStruct((tok_all, columns), jnp.bfloat16),
         in_specs=[in_vmem] * 3,
-        out_specs=in_vmem,
+        out_specs=pl.BlockSpec(memory_space=pl.ANY),
+        scratch_shapes=[
+            pltpu.VMEM((tok_all, columns), jnp.bfloat16),
+            pltpu.SemaphoreType.DMA((columns // 256 if columns % 256 == 0 else 1,)),
+        ],
         compiler_params=small,
         name="add",
     )(column, base, lifts.reshape(tp * here, columns))

time: 50.7 us -> 52.9 us (1.043)
  waiting for transfers between devices: 12.8 us -> 14.2 us
  starting transfers between devices: 19.5 us -> 20.2 us
    ppermute x8, starting transfers between devices: 7.73 us -> 9.09 us  [ring_gather(): lax.ppermute(x, axis, way)]
    ppermute x2, waiting for transfers between devices: 0.01 us -> 1.29 us  [swapped(): lax.ppermute(x, axis, [((i + s) % n, i) for i in range(n)])]
    ppermute x1, starting transfers between devices: 0.56 us -> 1.58 us  [ring_gather(): lax.ppermute(streams[0], axis, up)]
    ppermute x1, starting transfers between devices: 1.47 us -> 0.45 us  [ring_gather(): lax.ppermute(streams[3], axis, down)]
    ppermute x1, waiting for transfers between devices: 0.56 us -> 1.58 us  [ring_gather(): lax.ppermute(streams[3], axis, down)]
    ppermute x1, waiting for transfers between devices: 1.64 us -> 0.64 us  [ring_gather(): lax.ppermute(streams[0], axis, up)]
    ppermute x1, waiting for transfers between devices: 1.41 us -> 0.5 us  [ring_gather(): lax.ppermute(block, axis, up)]
    ppermute x8, waiting for transfers between devices: 5.78 us -> 6.66 us  [ring_gather(): lax.ppermute(x, axis, way)]
  transfers between devices with their start and end apart: 15 -> 15, of which waited for: 11 -> 8; matrix products, arithmetic and copies ran while one was open for 17% -> 16% of each run, Pallas kernels for 3% -> 3%
where the time goes in v24:
time: 52.9 us; the launch traced here: 52.5 us
  starting transfers between devices  20.2 us (38%)
  waiting for transfers between devices  14.2 us (27%)
  matrix products  8.53 us (16%)
  Pallas kernels  4.94 us (9%)
  local copies, waits for them, and re-layouts  4.53 us (9%)
    ppermute x8, starting transfers between devices, ring_gather(): lax.ppermute(x, axis, way)  9.09 us
    dot_general x1, matrix products, on_device(): jnp.dot(gathered, base_projection_weight, preferred_element_type=jnp.floa...  8.53 us
    ppermute x8, waiting for transfers between devices, ring_gather(): lax.ppermute(x, axis, way)  6.66 us
    all_to_all x1, starting transfers between devices, on_device(): lax.all_to_all(lifts, 'tp', split_axis=0, concat_axis=0, axis_index_group...  5.54 us
    unnamed x12, local copies, waits for them, and re-layouts  4.53 us
    all_to_all x1, waiting for transfers between devices, on_device(): lax.all_to_all(lifts, 'tp', split_axis=0, concat_axis=0, axis_index_group...  3.57 us
    ppermute x1, starting transfers between devices, ring_gather(): lax.ppermute(block, axis, down)  2.97 us
    pallas_call x1, Pallas kernels, on_device(): pl.pallas_call(functools.partial(lift_kernel, groups), out_shape=[jax.Sha...  2.17 us
  transfers between devices with their start and end apart: 15, of which 8 were waited for; matrix products, arithmetic and copies ran while one was open for 16% of the time, Pallas kernels for 3%

profile of v24, /device:TPU:0, one launch (start us, length us, event | category | flops | bytes accessed | tf_op | source)
XLA Modules:
  0.0 52.5 jit_solution(8148959443559062351)
XLA Ops:
  0.5 3.0 %collective-permute-start.3 = (bf16[16,8192]{1,0:T(8,128)(2,1)}, bf16[16,8192]{1,0:T(8,128)(2,1)S(1)}, u32[]{:S(2)}, u32[]{:S(2)}) collective-permute-start(bf16[16,8192]{1,0:T(8,128)(2,1)} %bitcast.14), channel_id=1, source_target_pairs={{2,0},{4,2},{6,4},{7,6},{5,7},{3,5},{1,3},{0,1},{10,8},{12,10},{14... | collective-permute-start | bytes 786440 | tf_op jit(solution)/shard_map/ppermute | solution.py:30
  3.5 1.3 %collective-permute-done.refs_1_ = bf16[64,8192]{1,0:T(8,128)(2,1)S(1)} collective-permute-done((bf16[64,8192]{1,0:T(8,128)(2,1)}, bf16[64,8192]{1,0:T(8,128)(2,1)S(1)}, u32[]{:S(2)}, u32[]{:S(2)}) %collective-permute-start) | collective-permute-done | bytes 1048608 | tf_op jit(solution)/shard_map/ppermute | solution.py:16
  4.8 1.3 %copy-done = bf16[1,64,10240]{2,1,0:T(8,128)(2,1)S(1)} copy-done((bf16[1,64,10240]{2,1,0:T(8,128)(2,1)S(1)}, bf16[1,64,10240]{2,1,0:T(8,128)(2,1)}, u32[]{:S(2)}) %copy-start) | copy-done | bytes 1310744
  6.1 1.2 %copy-done.1 = bf16[1,8192,64]{1,2,0:T(8,128)(2,1)S(1)} copy-done((bf16[1,8192,64]{1,2,0:T(8,128)(2,1)S(1)}, bf16[1,8192,64]{1,2,0:T(8,128)(2,1)}, u32[]{:S(2)}) %copy-start.1) | copy-done | bytes 1048600
  7.4 0.7 %copy-done.3 = s32[2,12]{1,0:T(2,128)S(1)} copy-done((s32[2,12]{1,0:T(2,128)S(1)}, s32[2,12]{1,0:T(2,128)}, u32[]{:S(2)}) %copy-start.3) | copy-done | bytes 120
  8.1 0.7 %copy-done.4 = s32[1,12]{1,0:T(1,128)S(1)} copy-done((s32[1,12]{1,0:T(1,128)S(1)}, s32[1,12]{1,0:T(1,128)}, u32[]{:S(2)}) %copy-start.4) | copy-done | bytes 72
  8.7 0.7 %copy-done.5 = s32[16]{0:T(128)S(1)} copy-done((s32[16]{0:T(128)S(1)}, s32[16]{0:T(128)}, u32[]{:S(2)}) %copy-start.5) | copy-done | bytes 88
  9.4 1.7 %prepare.1 = (bf16[8192,128]{1,0:T(8,128)(2,1)S(1)}, bf16[128,10240]{1,0:T(8,128)(2,1)S(1)}, s32[1,128]{1,0:T(1,128)S(1)}, s32[128,1]{1,0:T(8,128)S(1)}) custom-call(s32[2,12]{1,0:T(2,128)S(1)} %copy-done.3, s32[1,12]{1,0:T(1,128)S(1)} %copy-done.4, s32[16]{0:T(128)S(1)} %copy-done.5, bf16[64,8192]{1,0:T(8,128)(2,1)S(1)} %bitcast.13, ...), custom_call_target="tpu_custom_call" | custom-call | tf_op jit(solution)/shard_map/prepare/pallas_call | solution.py:180
  11.1 0.5 collective-permute-done.2.refs_0_.refs_1_
  11.7 2.5 %collective-permute-start.4 = (bf16[16,4096]{1,0:T(8,128)(2,1)S(1)}, bf16[16,4096]{1,0:T(8,128)(2,1)S(1)}, u32[]{:S(2)}, u32[]{:S(2)}) collective-permute-start(bf16[16,4096]{1,0:T(8,128)(2,1)S(1)} %get-tuple-element.19), channel_id=1, source_target_pairs={{0,2},{2,4},{4,6},{6,7},{7,5},{5,3},{3,1},{1,0},{8,10},{10,12},{12... | collective-permute-start | bytes 393224 | tf_op jit(solution)/shard_map/ppermute | solution.py:35
  14.2 2.0 %collective-permute-start.5 = (bf16[16,4096]{1,0:T(8,128)(2,1)S(1)}, bf16[16,4096]{1,0:T(8,128)(2,1)S(1)}, u32[]{:S(2)}, u32[]{:S(2)}) collective-permute-start(bf16[16,4096]{1,0:T(8,128)(2,1)S(1)} %get-tuple-element.20), channel_id=1, source_target_pairs={{2,0},{4,2},{6,4},{7,6},{5,7},{3,5},{1,3},{0,1},{10,8},{12,10},{14... | collective-permute-start | bytes 393224 | tf_op jit(solution)/shard_map/ppermute | solution.py:35
  16.3 1.8 %collective-permute-done.4.refs_3_ = bf16[16,4096]{1,0:T(8,128)(2,1)S(1)} collective-permute-done((bf16[16,4096]{1,0:T(8,128)(2,1)S(1)}, bf16[16,4096]{1,0:T(8,128)(2,1)S(1)}, u32[]{:S(2)}, u32[]{:S(2)}) %collective-permute-start.4) | collective-permute-done | bytes 131104 | tf_op jit(solution)/shard_map/ppermute | solution.py:35
  18.0 2.5 %collective-permute-start.8 = (bf16[16,4096]{1,0:T(8,128)(2,1)S(1)}, bf16[16,4096]{1,0:T(8,128)(2,1)S(1)}, u32[]{:S(2)}, u32[]{:S(2)}) collective-permute-start(bf16[16,4096]{1,0:T(8,128)(2,1)S(1)} %collective-permute-done.4.refs_3_), channel_id=1, source_target_pairs={{0,2},{2,4},{4,6},{6,7},{7,5},{5,3},{3,1},{1,0},{8,10},{10,12},{12... | collective-permute-start | bytes 393224 | tf_op jit(solution)/shard_map/ppermute | solution.py:35
  20.6 2.5 %collective-permute-done.5.refs_4_ = bf16[16,4096]{1,0:T(8,128)(2,1)S(1)} collective-permute-done((bf16[16,4096]{1,0:T(8,128)(2,1)S(1)}, bf16[16,4096]{1,0:T(8,128)(2,1)S(1)}, u32[]{:S(2)}, u32[]{:S(2)}) %collective-permute-start.5) | collective-permute-done | bytes 131104 | tf_op jit(solution)/shard_map/ppermute | solution.py:35
  23.1 2.0 %collective-permute-start.10 = (bf16[16,4096]{1,0:T(8,128)(2,1)S(1)}, bf16[16,4096]{1,0:T(8,128)(2,1)S(1)}, u32[]{:S(2)}, u32[]{:S(2)}) collective-permute-start(bf16[16,4096]{1,0:T(8,128)(2,1)S(1)} %collective-permute-done.6.refs_5_), channel_id=1, source_target_pairs={{0,2},{2,4},{4,6},{6,7},{7,5},{5,3},{3,1},{1,0},{8,10},{10,12},{12... | collective-permute-start | bytes 393224 | tf_op jit(solution)/shard_map/ppermute | solution.py:35
  25.1 1.6 %collective-permute-start.12 = (bf16[16,4096]{1,0:T(8,128)(2,1)S(1)}, bf16[16,4096]{1,0:T(8,128)(2,1)S(1)}, u32[]{:S(2)}, u32[]{:S(2)}) collective-permute-start(bf16[16,4096]{1,0:T(8,128)(2,1)S(1)} %collective-permute-done.8.refs_7_), channel_id=1, source_target_pairs={{0,2},{2,4},{4,6},{6,7},{7,5},{5,3},{3,1},{1,0},{8,10},{10,12},{12... | collective-permute-start | bytes 393224 | tf_op jit(solution)/shard_map/ppermute | solution.py:37
  27.2 2.3 %collective-permute-done.9.refs_8_ = bf16[16,4096]{1,0:T(8,128)(2,1)S(1)} collective-permute-done((bf16[16,4096]{1,0:T(8,128)(2,1)S(1)}, bf16[16,4096]{1,0:T(8,128)(2,1)S(1)}, u32[]{:S(2)}, u32[]{:S(2)}) %collective-permute-start.9) | collective-permute-done | bytes 131104 | tf_op jit(solution)/shard_map/ppermute | solution.py:35
  29.5 0.6 %collective-permute-done.12.refs_11_ = bf16[16,4096]{1,0:T(8,128)(2,1)S(1)} collective-permute-done((bf16[16,4096]{1,0:T(8,128)(2,1)S(1)}, bf16[16,4096]{1,0:T(8,128)(2,1)S(1)}, u32[]{:S(2)}, u32[]{:S(2)}) %collective-permute-start.12) | collective-permute-done | bytes 131104 | tf_op jit(solution)/shard_map/ppermute | solution.py:37
  30.1 1.6 %collective-permute-done.13.refs_12_ = bf16[16,4096]{1,0:T(8,128)(2,1)S(1)} collective-permute-done((bf16[16,4096]{1,0:T(8,128)(2,1)S(1)}, bf16[16,4096]{1,0:T(8,128)(2,1)S(1)}, u32[]{:S(2)}, u32[]{:S(2)}) %collective-permute-start.13) | collective-permute-done | bytes 131104 | tf_op jit(solution)/shard_map/ppermute | solution.py:37
  31.7 2.2 %lift.1 = (bf16[128,8192]{1,0:T(8,128)(2,1)S(1)}, bf16[8,32,1280]{2,1,0:T(8,128)(2,1)}) custom-call(s32[1,128]{1,0:T(1,128)S(1)} %get-tuple-element.16.refs_4_.place_ref, bf16[8192,128]{1,0:T(8,128)(2,1)S(1)} %get-tuple-element.17.refs_2_.down_ref, bf16[128,10240]{1,0:T(8,128)(2,1)S(1)} %get-tuple-element.18.refs_3_.up_ref, bf16[16,8192]{1,0:T(8,128)(2,1)S(1)} %bitcast.16, ...), custom_call_target="tpu_custom_call" | custom-call | flops 352321536 | bytes 4718592 | tf_op jit(solution)/shard_map/lift/pallas_call | solution.py:195
  33.9 5.5 %all-to-all-start = ((bf16[8,32,1280]{2,1,0:T(8,128)(2,1)}), bf16[8,32,1280]{2,1,0:T(8,128)(2,1)S(1)}, u32[]{:S(2)}, u32[]{:S(2)}) async-start(bf16[8,32,1280]{2,1,0:T(8,128)(2,1)} %get-tuple-element.24), calls=%async_computation | async-start | bytes 1310720 | tf_op jit(solution)/shard_map/all_to_all | solution.py:215
  39.4 8.5 %fusion.base_ref = f32[128,1280]{1,0:T(8,128)S(1)} fusion(bf16[128,8192]{1,0:T(8,128)(2,1)S(1)} %get-tuple-element.23, bf16[8192,1280]{1,0:T(8,128)(2,1)} %param.8), kind=kOutput, calls=%fused_computation | convolution fusion | flops 2684354560 | bytes 23724032 | tf_op jit(solution)/shard_map/dot_general | solution.py:219
  47.9 3.6 %all-to-all-done = bf16[8,32,1280]{2,1,0:T(8,128)(2,1)S(1)} async-done(((bf16[8,32,1280]{2,1,0:T(8,128)(2,1)}), bf16[8,32,1280]{2,1,0:T(8,128)(2,1)S(1)}, u32[]{:S(2)}, u32[]{:S(2)}) %all-to-all-start) | async-done | bytes 655392 | tf_op jit(solution)/shard_map/all_to_all | solution.py:215
  51.5 1.0 %add.1 = bf16[128,1280]{1,0:T(8,128)(2,1)} custom-call(s32[128,1]{1,0:T(8,128)S(1)} %get-tuple-element.15.refs_5_.place_ref, f32[128,1280]{1,0:T(8,128)S(1)} %fusion.base_ref, bf16[256,1280]{1,0:T(8,128)(2,1)S(1)} %bitcast.9), custom_call_target="tpu_custom_call" | custom-call | tf_op jit(solution)/shard_map/add/pallas_call | solution.py:220
  (23 shorter events, 1.3 us)
Async XLA Ops:
  0.0 4.8 %collective-permute-start.1 = (bf16[64,10240]{1,0:T(8,128)(2,1)}, bf16[64,10240]{1,0:T(8,128)(2,1)S(1)}, u32[]{:S(2)}, u32[]{:S(2)}) collective-permute-start(bf16[64,10240]{1,0:T(8,128)(2,1)} %bitcast.10), channel_id=1, source_target_pairs={{8,0},{0,8},{9,1},{1,9},{10,2},{2,10},{11,3},{3,11},{12,4},{4,12},... | collective-permute-start | bytes 3932168 | tf_op jit(solution)/shard_map/ppermute | solution.py:16
  0.5 4.4 %collective-permute-start = (bf16[64,8192]{1,0:T(8,128)(2,1)}, bf16[64,8192]{1,0:T(8,128)(2,1)S(1)}, u32[]{:S(2)}, u32[]{:S(2)}) collective-permute-start(bf16[64,8192]{1,0:T(8,128)(2,1)} %bitcast.12), channel_id=1, source_target_pairs={{8,0},{0,8},{9,1},{1,9},{10,2},{2,10},{11,3},{3,11},{12,4},{4,12},... | collective-permute-start | bytes 3145736 | tf_op jit(solution)/shard_map/ppermute | solution.py:16
  0.5 10.6 %collective-permute-start.3 = (bf16[16,8192]{1,0:T(8,128)(2,1)}, bf16[16,8192]{1,0:T(8,128)(2,1)S(1)}, u32[]{:S(2)}, u32[]{:S(2)}) collective-permute-start(bf16[16,8192]{1,0:T(8,128)(2,1)} %bitcast.14), channel_id=1, source_target_pairs={{2,0},{4,2},{6,4},{7,6},{5,7},{3,5},{1,3},{0,1},{10,8},{12,10},{14... | collective-permute-start | bytes 786440 | tf_op jit(solution)/shard_map/ppermute | solution.py:30
  3.5 8.1 %collective-permute-start.2 = (bf16[16,8192]{1,0:T(8,128)(2,1)}, bf16[16,8192]{1,0:T(8,128)(2,1)S(1)}, u32[]{:S(2)}, u32[]{:S(2)}) collective-permute-start(bf16[16,8192]{1,0:T(8,128)(2,1)} %bitcast.15), channel_id=1, source_target_pairs={{0,2},{2,4},{4,6},{6,7},{7,5},{5,3},{3,1},{1,0},{8,10},{10,12},{12... | collective-permute-start | bytes 786440 | tf_op jit(solution)/shard_map/ppermute | solution.py:30
  4.8 1.3 %copy-start = (bf16[1,64,10240]{2,1,0:T(8,128)(2,1)S(1)}, bf16[1,64,10240]{2,1,0:T(8,128)(2,1)}, u32[]{:S(2)}) copy-start(bf16[1,64,10240]{2,1,0:T(8,128)(2,1)} %param.10) | copy-start | bytes 3932164
  6.1 1.2 %copy-start.1 = (bf16[1,8192,64]{1,2,0:T(8,128)(2,1)S(1)}, bf16[1,8192,64]{1,2,0:T(8,128)(2,1)}, u32[]{:S(2)}) copy-start(bf16[1,8192,64]{1,2,0:T(8,128)(2,1)} %param.9) | copy-start | bytes 3145732
  7.4 0.7 %copy-start.3 = (s32[2,12]{1,0:T(2,128)S(1)}, s32[2,12]{1,0:T(2,128)}, u32[]{:S(2)}) copy-start(s32[2,12]{1,0:T(2,128)} %ids_ref.1) | copy-start | bytes 292
  8.1 0.7 %copy-start.4 = (s32[1,12]{1,0:T(1,128)S(1)}, s32[1,12]{1,0:T(1,128)}, u32[]{:S(2)}) copy-start(s32[1,12]{1,0:T(1,128)} %lengths_ref.1) | copy-start | bytes 148
  8.7 0.7 %copy-start.5 = (s32[16]{0:T(128)S(1)}, s32[16]{0:T(128)}, u32[]{:S(2)}) copy-start(s32[16]{0:T(128)} %slots_ref.1) | copy-start | bytes 196
  11.6 20.1 %copy-start.2 = (bf16[1,16,8192]{2,1,0:T(8,128)(2,1)S(1)}, bf16[1,16,8192]{2,1,0:T(8,128)(2,1)}, u32[]{:S(2)}) copy-start(bf16[1,16,8192]{2,1,0:T(8,128)(2,1)} %param.7) | copy-start | bytes 786436
  11.7 6.4 %collective-permute-start.4 = (bf16[16,4096]{1,0:T(8,128)(2,1)S(1)}, bf16[16,4096]{1,0:T(8,128)(2,1)S(1)}, u32[]{:S(2)}, u32[]{:S(2)}) collective-permute-start(bf16[16,4096]{1,0:T(8,128)(2,1)S(1)} %get-tuple-element.19), channel_id=1, source_target_pairs={{0,2},{2,4},{4,6},{6,7},{7,5},{5,3},{3,1},{1,0},{8,10},{10,12},{12... | collective-permute-start | bytes 393224 | tf_op jit(solution)/shard_map/ppermute | solution.py:35
  14.2 6.4 %collective-permute-start.7 = (bf16[16,4096]{1,0:T(8,128)(2,1)S(1)}, bf16[16,4096]{1,0:T(8,128)(2,1)S(1)}, u32[]{:S(2)}, u32[]{:S(2)}) collective-permute-start(bf16[16,4096]{1,0:T(8,128)(2,1)S(1)} %get-tuple-element.22), channel_id=1, source_target_pairs={{2,0},{4,2},{6,4},{7,6},{5,7},{3,5},{1,3},{0,1},{10,8},{12,10},{14... | collective-permute-start | bytes 393224 | tf_op jit(solution)/shard_map/ppermute | solution.py:35
  14.2 8.9 %collective-permute-start.5 = (bf16[16,4096]{1,0:T(8,128)(2,1)S(1)}, bf16[16,4096]{1,0:T(8,128)(2,1)S(1)}, u32[]{:S(2)}, u32[]{:S(2)}) collective-permute-start(bf16[16,4096]{1,0:T(8,128)(2,1)S(1)} %get-tuple-element.20), channel_id=1, source_target_pairs={{2,0},{4,2},{6,4},{7,6},{5,7},{3,5},{1,3},{0,1},{10,8},{12,10},{14... | collective-permute-start | bytes 393224 | tf_op jit(solution)/shard_map/ppermute | solution.py:35
  16.2 7.0 %collective-permute-start.6 = (bf16[16,4096]{1,0:T(8,128)(2,1)S(1)}, bf16[16,4096]{1,0:T(8,128)(2,1)S(1)}, u32[]{:S(2)}, u32[]{:S(2)}) collective-permute-start(bf16[16,4096]{1,0:T(8,128)(2,1)S(1)} %get-tuple-element.21), channel_id=1, source_target_pairs={{0,2},{2,4},{4,6},{6,7},{7,5},{5,3},{3,1},{1,0},{8,10},{10,12},{12... | collective-permute-start | bytes 393224 | tf_op jit(solution)/shard_map/ppermute | solution.py:35
  18.0 7.1 %collective-permute-start.8 = (bf16[16,4096]{1,0:T(8,128)(2,1)S(1)}, bf16[16,4096]{1,0:T(8,128)(2,1)S(1)}, u32[]{:S(2)}, u32[]{:S(2)}) collective-permute-start(bf16[16,4096]{1,0:T(8,128)(2,1)S(1)} %collective-permute-done.4.refs_3_), channel_id=1, source_target_pairs={{0,2},{2,4},{4,6},{6,7},{7,5},{5,3},{3,1},{1,0},{8,10},{10,12},{12... | collective-permute-start | bytes 393224 | tf_op jit(solution)/shard_map/ppermute | solution.py:35
  20.6 6.1 %collective-permute-start.11 = (bf16[16,4096]{1,0:T(8,128)(2,1)S(1)}, bf16[16,4096]{1,0:T(8,128)(2,1)S(1)}, u32[]{:S(2)}, u32[]{:S(2)}) collective-permute-start(bf16[16,4096]{1,0:T(8,128)(2,1)S(1)} %collective-permute-done.7.refs_6_), channel_id=1, source_target_pairs={{2,0},{4,2},{6,4},{7,6},{5,7},{3,5},{1,3},{0,1},{10,8},{12,10},{14... | collective-permute-start | bytes 393224 | tf_op jit(solution)/shard_map/ppermute | solution.py:35
  23.1 6.4 %collective-permute-start.9 = (bf16[16,4096]{1,0:T(8,128)(2,1)S(1)}, bf16[16,4096]{1,0:T(8,128)(2,1)S(1)}, u32[]{:S(2)}, u32[]{:S(2)}) collective-permute-start(bf16[16,4096]{1,0:T(8,128)(2,1)S(1)} %collective-permute-done.5.refs_4_), channel_id=1, source_target_pairs={{2,0},{4,2},{6,4},{7,6},{5,7},{3,5},{1,3},{0,1},{10,8},{12,10},{14... | collective-permute-start | bytes 393224 | tf_op jit(solution)/shard_map/ppermute | solution.py:35
  23.1 6.3 %collective-permute-start.10 = (bf16[16,4096]{1,0:T(8,128)(2,1)S(1)}, bf16[16,4096]{1,0:T(8,128)(2,1)S(1)}, u32[]{:S(2)}, u32[]{:S(2)}) collective-permute-start(bf16[16,4096]{1,0:T(8,128)(2,1)S(1)} %collective-permute-done.6.refs_5_), channel_id=1, source_target_pairs={{0,2},{2,4},{4,6},{6,7},{7,5},{5,3},{3,1},{1,0},{8,10},{10,12},{12... | collective-permute-start | bytes 393224 | tf_op jit(solution)/shard_map/ppermute | solution.py:35
  25.1 5.0 %collective-permute-start.12 = (bf16[16,4096]{1,0:T(8,128)(2,1)S(1)}, bf16[16,4096]{1,0:T(8,128)(2,1)S(1)}, u32[]{:S(2)}, u32[]{:S(2)}) collective-permute-start(bf16[16,4096]{1,0:T(8,128)(2,1)S(1)} %collective-permute-done.8.refs_7_), channel_id=1, source_target_pairs={{0,2},{2,4},{4,6},{6,7},{7,5},{5,3},{3,1},{1,0},{8,10},{10,12},{12... | collective-permute-start | bytes 393224 | tf_op jit(solution)/shard_map/ppermute | solution.py:37
  26.7 5.0 %collective-permute-start.13 = (bf16[16,4096]{1,0:T(8,128)(2,1)S(1)}, bf16[16,4096]{1,0:T(8,128)(2,1)S(1)}, u32[]{:S(2)}, u32[]{:S(2)}) collective-permute-start(bf16[16,4096]{1,0:T(8,128)(2,1)S(1)} %collective-permute-done.11.refs_10_), channel_id=1, source_target_pairs={{2,0},{4,2},{6,4},{7,6},{5,7},{3,5},{1,3},{0,1},{10,8},{12,10},{14... | collective-permute-start | bytes 393224 | tf_op jit(solution)/shard_map/ppermute | solution.py:37
  33.9 17.6 %all-to-all-start = ((bf16[8,32,1280]{2,1,0:T(8,128)(2,1)}), bf16[8,32,1280]{2,1,0:T(8,128)(2,1)S(1)}, u32[]{:S(2)}, u32[]{:S(2)}) async-start(bf16[8,32,1280]{2,1,0:T(8,128)(2,1)} %get-tuple-element.24), calls=%async_computation | async-start | bytes 1310720 | tf_op jit(solution)/shard_map/all_to_all | solution.py:215

commit v25 on v23

--- a/solution.py
+++ b/solution.py
@@ -59,12 +59,12 @@
 
 
 def exchange_order(n):
-    ring = ring_of(n)
-    return ring[1:] + ring[:1]
+    rows = list(range(0, n, 2)) + list(range(1, n, 2))
+    return rows[1:] + rows[:1]
 
 
 def exchange_place(i, n):
-    return lax.rem(ring_place(i, n) + n - 1, n)
+    return lax.rem(i // 2 + lax.rem(i, 2) * (n // 2) + n - 1, n)
 
 
 def ring_sources(axis, half):

time: 50.7 us -> 53.1 us (1.047)
  waiting for transfers between devices: 12.8 us -> 15.2 us
    all_to_all x1, waiting for transfers between devices: 3.02 us -> 5.42 us  [on_device(): lax.all_to_all(lifts, 'tp', split_axis=0, concat_axis=0, axis_index_group...]
  transfers between devices with their start and end apart: 15 -> 15, of which waited for: 11 -> 11; matrix products, arithmetic and copies ran while one was open for 17% -> 16% of each run, Pallas kernels for 3% -> 3%
where the time goes in v25:
time: 53.1 us; the launch traced here: 52.8 us
  starting transfers between devices  19.5 us (37%)
  waiting for transfers between devices  15.2 us (29%)
  matrix products  8.53 us (16%)
  Pallas kernels  5 us (9%)
  local copies, waits for them, and re-layouts  4.53 us (9%)
    dot_general x1, matrix products, on_device(): jnp.dot(gathered, base_projection_weight, preferred_element_type=jnp.floa...  8.53 us
    ppermute x8, starting transfers between devices, ring_gather(): lax.ppermute(x, axis, way)  7.73 us
    all_to_all x1, starting transfers between devices, on_device(): lax.all_to_all(lifts, 'tp', split_axis=0, concat_axis=0, axis_index_group...  6.21 us
    ppermute x8, waiting for transfers between devices, ring_gather(): lax.ppermute(x, axis, way)  5.78 us
    all_to_all x1, waiting for transfers between devices, on_device(): lax.all_to_all(lifts, 'tp', split_axis=0, concat_axis=0, axis_index_group...  5.42 us
    unnamed x12, local copies, waits for them, and re-layouts  4.53 us
    ppermute x1, starting transfers between devices, ring_gather(): lax.ppermute(block, axis, down)  2.97 us
    pallas_call x1, Pallas kernels, on_device(): pl.pallas_call(functools.partial(lift_kernel, groups), out_shape=[jax.Sha...  2.2 us
  transfers between devices with their start and end apart: 15, of which 11 were waited for; matrix products, arithmetic and copies ran while one was open for 16% of the time, Pallas kernels for 3%

profile of v25, /device:TPU:0, one launch (start us, length us, event | category | flops | bytes accessed | tf_op | source)
XLA Modules:
  0.0 52.8 jit_solution(3288575241749989373)
XLA Ops:
  0.5 3.0 %collective-permute-start.3 = (bf16[16,8192]{1,0:T(8,128)(2,1)}, bf16[16,8192]{1,0:T(8,128)(2,1)S(1)}, u32[]{:S(2)}, u32[]{:S(2)}) collective-permute-start(bf16[16,8192]{1,0:T(8,128)(2,1)} %bitcast.14), channel_id=1, source_target_pairs={{2,0},{4,2},{6,4},{7,6},{5,7},{3,5},{1,3},{0,1},{10,8},{12,10},{14... | collective-permute-start | bytes 786440 | tf_op jit(solution)/shard_map/ppermute | solution.py:30
  3.5 0.7 %copy-done.3 = s32[2,12]{1,0:T(2,128)S(1)} copy-done((s32[2,12]{1,0:T(2,128)S(1)}, s32[2,12]{1,0:T(2,128)}, u32[]{:S(2)}) %copy-start.3) | copy-done | bytes 120
  4.2 0.7 %copy-done.4 = s32[1,12]{1,0:T(1,128)S(1)} copy-done((s32[1,12]{1,0:T(1,128)S(1)}, s32[1,12]{1,0:T(1,128)}, u32[]{:S(2)}) %copy-start.4) | copy-done | bytes 72
  5.5 1.0 %place.1 = (s32[1,128]{1,0:T(1,128)S(1)}, s32[128,1]{1,0:T(8,128)S(1)}) custom-call(s32[2,12]{1,0:T(2,128)S(1)} %copy-done.3, s32[1,12]{1,0:T(1,128)S(1)} %copy-done.4, s32[16]{0:T(128)S(1)} %copy-done.5), custom_call_target="tpu_custom_call" | custom-call | tf_op jit(solution)/shard_map/place/pallas_call | solution.py:183
  6.6 1.3 %copy-done = bf16[1,64,10240]{2,1,0:T(8,128)(2,1)S(1)} copy-done((bf16[1,64,10240]{2,1,0:T(8,128)(2,1)S(1)}, bf16[1,64,10240]{2,1,0:T(8,128)(2,1)}, u32[]{:S(2)}) %copy-start) | copy-done | bytes 1310744
  7.9 1.2 %copy-done.1 = bf16[1,8192,64]{1,2,0:T(8,128)(2,1)S(1)} copy-done((bf16[1,8192,64]{1,2,0:T(8,128)(2,1)S(1)}, bf16[1,8192,64]{1,2,0:T(8,128)(2,1)}, u32[]{:S(2)}) %copy-start.1) | copy-done | bytes 1048600
  9.1 0.7 %stack.1 = (bf16[8192,128]{1,0:T(8,128)(2,1)S(1)}, bf16[128,10240]{1,0:T(8,128)(2,1)S(1)}) custom-call(bf16[64,8192]{1,0:T(8,128)(2,1)S(1)} %bitcast.13, bf16[64,8192]{1,0:T(8,128)(2,1)S(1)} %collective-permute-done.refs_1_, bf16[64,10240]{1,0:T(8,128)(2,1)S(1)} %bitcast.11, bf16[64,10240]{1,0:T(8,128)(2,1)S(1)} %collective-permute-done.1.refs_3_), custom_call_target="tpu_custom_call" | custom-call | tf_op jit(solution)/shard_map/stack/pallas_call | solution.py:172
  10.2 1.4 %collective-permute-done.2.refs_0_.refs_1_ = bf16[16,8192]{1,0:T(8,128)(2,1)S(1)} collective-permute-done((bf16[16,8192]{1,0:T(8,128)(2,1)}, bf16[16,8192]{1,0:T(8,128)(2,1)S(1)}, u32[]{:S(2)}, u32[]{:S(2)}) %collective-permute-start.2) | collective-permute-done | bytes 262176 | tf_op jit(solution)/shard_map/ppermute | solution.py:30
  12.1 1.7 %collective-permute-start.7 = (bf16[16,4096]{1,0:T(8,128)(2,1)S(1)}, bf16[16,4096]{1,0:T(8,128)(2,1)S(1)}, u32[]{:S(2)}, u32[]{:S(2)}) collective-permute-start(bf16[16,4096]{1,0:T(8,128)(2,1)S(1)} %get-tuple-element.22), channel_id=1, source_target_pairs={{2,0},{4,2},{6,4},{7,6},{5,7},{3,5},{1,3},{0,1},{10,8},{12,10},{14... | collective-permute-start | bytes 393224 | tf_op jit(solution)/shard_map/ppermute | solution.py:35
  13.7 1.6 %collective-permute-start.5 = (bf16[16,4096]{1,0:T(8,128)(2,1)S(1)}, bf16[16,4096]{1,0:T(8,128)(2,1)S(1)}, u32[]{:S(2)}, u32[]{:S(2)}) collective-permute-start(bf16[16,4096]{1,0:T(8,128)(2,1)S(1)} %get-tuple-element.20), channel_id=1, source_target_pairs={{2,0},{4,2},{6,4},{7,6},{5,7},{3,5},{1,3},{0,1},{10,8},{12,10},{14... | collective-permute-start | bytes 393224 | tf_op jit(solution)/shard_map/ppermute | solution.py:35
  15.8 1.7 %collective-permute-done.4.refs_3_ = bf16[16,4096]{1,0:T(8,128)(2,1)S(1)} collective-permute-done((bf16[16,4096]{1,0:T(8,128)(2,1)S(1)}, bf16[16,4096]{1,0:T(8,128)(2,1)S(1)}, u32[]{:S(2)}, u32[]{:S(2)}) %collective-permute-start.4) | collective-permute-done | bytes 131104 | tf_op jit(solution)/shard_map/ppermute | solution.py:35
  18.2 1.4 %collective-permute-start.11 = (bf16[16,4096]{1,0:T(8,128)(2,1)S(1)}, bf16[16,4096]{1,0:T(8,128)(2,1)S(1)}, u32[]{:S(2)}, u32[]{:S(2)}) collective-permute-start(bf16[16,4096]{1,0:T(8,128)(2,1)S(1)} %collective-permute-done.7.refs_6_), channel_id=1, source_target_pairs={{2,0},{4,2},{6,4},{7,6},{5,7},{3,5},{1,3},{0,1},{10,8},{12,10},{14... | collective-permute-start | bytes 393224 | tf_op jit(solution)/shard_map/ppermute | solution.py:35
  19.5 1.4 %collective-permute-done.5.refs_4_ = bf16[16,4096]{1,0:T(8,128)(2,1)S(1)} collective-permute-done((bf16[16,4096]{1,0:T(8,128)(2,1)S(1)}, bf16[16,4096]{1,0:T(8,128)(2,1)S(1)}, u32[]{:S(2)}, u32[]{:S(2)}) %collective-permute-start.5) | collective-permute-done | bytes 131104 | tf_op jit(solution)/shard_map/ppermute | solution.py:35
  21.0 1.2 %collective-permute-start.9 = (bf16[16,4096]{1,0:T(8,128)(2,1)S(1)}, bf16[16,4096]{1,0:T(8,128)(2,1)S(1)}, u32[]{:S(2)}, u32[]{:S(2)}) collective-permute-start(bf16[16,4096]{1,0:T(8,128)(2,1)S(1)} %collective-permute-done.5.refs_4_), channel_id=1, source_target_pairs={{2,0},{4,2},{6,4},{7,6},{5,7},{3,5},{1,3},{0,1},{10,8},{12,10},{14... | collective-permute-start | bytes 393224 | tf_op jit(solution)/shard_map/ppermute | solution.py:35
  22.2 0.8 %collective-permute-start.10 = (bf16[16,4096]{1,0:T(8,128)(2,1)S(1)}, bf16[16,4096]{1,0:T(8,128)(2,1)S(1)}, u32[]{:S(2)}, u32[]{:S(2)}) collective-permute-start(bf16[16,4096]{1,0:T(8,128)(2,1)S(1)} %collective-permute-done.6.refs_5_), channel_id=1, source_target_pairs={{0,2},{2,4},{4,6},{6,7},{7,5},{5,3},{3,1},{1,0},{8,10},{10,12},{12... | collective-permute-start | bytes 393224 | tf_op jit(solution)/shard_map/ppermute | solution.py:35
  23.0 0.9 %collective-permute-done.8.refs_7_ = bf16[16,4096]{1,0:T(8,128)(2,1)S(1)} collective-permute-done((bf16[16,4096]{1,0:T(8,128)(2,1)S(1)}, bf16[16,4096]{1,0:T(8,128)(2,1)S(1)}, u32[]{:S(2)}, u32[]{:S(2)}) %collective-permute-start.8) | collective-permute-done | bytes 131104 | tf_op jit(solution)/shard_map/ppermute | solution.py:35
  24.4 1.5 %collective-permute-start.13 = (bf16[16,4096]{1,0:T(8,128)(2,1)S(1)}, bf16[16,4096]{1,0:T(8,128)(2,1)S(1)}, u32[]{:S(2)}, u32[]{:S(2)}) collective-permute-start(bf16[16,4096]{1,0:T(8,128)(2,1)S(1)} %collective-permute-done.11.refs_10_), channel_id=1, source_target_pairs={{2,0},{4,2},{6,4},{7,6},{5,7},{3,5},{1,3},{0,1},{10,8},{12,10},{14... | collective-permute-start | bytes 393224 | tf_op jit(solution)/shard_map/ppermute | solution.py:37
  26.4 0.8 %collective-permute-done.10.refs_9_ = bf16[16,4096]{1,0:T(8,128)(2,1)S(1)} collective-permute-done((bf16[16,4096]{1,0:T(8,128)(2,1)S(1)}, bf16[16,4096]{1,0:T(8,128)(2,1)S(1)}, u32[]{:S(2)}, u32[]{:S(2)}) %collective-permute-start.10) | collective-permute-done | bytes 131104 | tf_op jit(solution)/shard_map/ppermute | solution.py:35
  27.2 1.6 %collective-permute-done.12.refs_11_ = bf16[16,4096]{1,0:T(8,128)(2,1)S(1)} collective-permute-done((bf16[16,4096]{1,0:T(8,128)(2,1)S(1)}, bf16[16,4096]{1,0:T(8,128)(2,1)S(1)}, u32[]{:S(2)}, u32[]{:S(2)}) %collective-permute-start.12) | collective-permute-done | bytes 131104 | tf_op jit(solution)/shard_map/ppermute | solution.py:37
  29.4 2.2 %lift.1 = (bf16[128,8192]{1,0:T(8,128)(2,1)S(1)}, bf16[8,32,1280]{2,1,0:T(8,128)(2,1)}) custom-call(s32[1,128]{1,0:T(1,128)S(1)} %get-tuple-element.16.refs_4_.place_ref, bf16[8192,128]{1,0:T(8,128)(2,1)S(1)} %get-tuple-element.17.refs_2_.down_ref, bf16[128,10240]{1,0:T(8,128)(2,1)S(1)} %get-tuple-element.18.refs_3_.up_ref, bf16[16,8192]{1,0:T(8,128)(2,1)S(1)} %bitcast.16, ...), custom_call_target="tpu_custom_call" | custom-call | flops 352321536 | bytes 4718592 | tf_op jit(solution)/shard_map/lift/pallas_call | solution.py:196
  31.6 6.2 %all-to-all-start = ((bf16[8,32,1280]{2,1,0:T(8,128)(2,1)}), bf16[8,32,1280]{2,1,0:T(8,128)(2,1)S(1)}, u32[]{:S(2)}, u32[]{:S(2)}) async-start(bf16[8,32,1280]{2,1,0:T(8,128)(2,1)} %get-tuple-element.24), calls=%async_computation | async-start | bytes 1310720 | tf_op jit(solution)/shard_map/all_to_all | solution.py:216
  37.8 8.5 %fusion.base_ref = f32[128,1280]{1,0:T(8,128)S(1)} fusion(bf16[128,8192]{1,0:T(8,128)(2,1)S(1)} %get-tuple-element.23, bf16[8192,1280]{1,0:T(8,128)(2,1)} %param.8), kind=kOutput, calls=%fused_computation | convolution fusion | flops 2684354560 | bytes 23724032 | tf_op jit(solution)/shard_map/dot_general | solution.py:220
  46.4 5.4 %all-to-all-done = bf16[8,32,1280]{2,1,0:T(8,128)(2,1)S(1)} async-done(((bf16[8,32,1280]{2,1,0:T(8,128)(2,1)}), bf16[8,32,1280]{2,1,0:T(8,128)(2,1)S(1)}, u32[]{:S(2)}, u32[]{:S(2)}) %all-to-all-start) | async-done | bytes 655392 | tf_op jit(solution)/shard_map/all_to_all | solution.py:216
  51.8 1.0 %add.1 = bf16[128,1280]{1,0:T(8,128)(2,1)} custom-call(s32[128,1]{1,0:T(8,128)S(1)} %get-tuple-element.15.refs_5_.place_ref, f32[128,1280]{1,0:T(8,128)S(1)} %fusion.base_ref, bf16[256,1280]{1,0:T(8,128)(2,1)S(1)} %bitcast.9), custom_call_target="tpu_custom_call" | custom-call | tf_op jit(solution)/shard_map/add/pallas_call | solution.py:221
  (24 shorter events, 4.8 us)
Async XLA Ops:
  0.0 6.6 %collective-permute-start.1 = (bf16[64,10240]{1,0:T(8,128)(2,1)}, bf16[64,10240]{1,0:T(8,128)(2,1)S(1)}, u32[]{:S(2)}, u32[]{:S(2)}) collective-permute-start(bf16[64,10240]{1,0:T(8,128)(2,1)} %bitcast.10), channel_id=1, source_target_pairs={{8,0},{0,8},{9,1},{1,9},{10,2},{2,10},{11,3},{3,11},{12,4},{4,12},... | collective-permute-start | bytes 3932168 | tf_op jit(solution)/shard_map/ppermute | solution.py:16
  0.5 6.1 %collective-permute-start = (bf16[64,8192]{1,0:T(8,128)(2,1)}, bf16[64,8192]{1,0:T(8,128)(2,1)S(1)}, u32[]{:S(2)}, u32[]{:S(2)}) collective-permute-start(bf16[64,8192]{1,0:T(8,128)(2,1)} %bitcast.12), channel_id=1, source_target_pairs={{8,0},{0,8},{9,1},{1,9},{10,2},{2,10},{11,3},{3,11},{12,4},{4,12},... | collective-permute-start | bytes 3145736 | tf_op jit(solution)/shard_map/ppermute | solution.py:16
  0.5 9.7 %collective-permute-start.3 = (bf16[16,8192]{1,0:T(8,128)(2,1)}, bf16[16,8192]{1,0:T(8,128)(2,1)S(1)}, u32[]{:S(2)}, u32[]{:S(2)}) collective-permute-start(bf16[16,8192]{1,0:T(8,128)(2,1)} %bitcast.14), channel_id=1, source_target_pairs={{2,0},{4,2},{6,4},{7,6},{5,7},{3,5},{1,3},{0,1},{10,8},{12,10},{14... | collective-permute-start | bytes 786440 | tf_op jit(solution)/shard_map/ppermute | solution.py:30
  3.5 8.1 %collective-permute-start.2 = (bf16[16,8192]{1,0:T(8,128)(2,1)}, bf16[16,8192]{1,0:T(8,128)(2,1)S(1)}, u32[]{:S(2)}, u32[]{:S(2)}) collective-permute-start(bf16[16,8192]{1,0:T(8,128)(2,1)} %bitcast.15), channel_id=1, source_target_pairs={{0,2},{2,4},{4,6},{6,7},{7,5},{5,3},{3,1},{1,0},{8,10},{10,12},{12... | collective-permute-start | bytes 786440 | tf_op jit(solution)/shard_map/ppermute | solution.py:30
  3.5 0.7 %copy-start.3 = (s32[2,12]{1,0:T(2,128)S(1)}, s32[2,12]{1,0:T(2,128)}, u32[]{:S(2)}) copy-start(s32[2,12]{1,0:T(2,128)} %ids_ref.1) | copy-start | bytes 292
  4.2 0.7 %copy-start.4 = (s32[1,12]{1,0:T(1,128)S(1)}, s32[1,12]{1,0:T(1,128)}, u32[]{:S(2)}) copy-start(s32[1,12]{1,0:T(1,128)} %lengths_ref.1) | copy-start | bytes 148
  4.9 0.7 %copy-start.5 = (s32[16]{0:T(128)S(1)}, s32[16]{0:T(128)}, u32[]{:S(2)}) copy-start(s32[16]{0:T(128)} %slots_ref.1) | copy-start | bytes 196
  6.6 1.3 %copy-start = (bf16[1,64,10240]{2,1,0:T(8,128)(2,1)S(1)}, bf16[1,64,10240]{2,1,0:T(8,128)(2,1)}, u32[]{:S(2)}) copy-start(bf16[1,64,10240]{2,1,0:T(8,128)(2,1)} %param.10) | copy-start | bytes 3932164
  7.9 1.2 %copy-start.1 = (bf16[1,8192,64]{1,2,0:T(8,128)(2,1)S(1)}, bf16[1,8192,64]{1,2,0:T(8,128)(2,1)}, u32[]{:S(2)}) copy-start(bf16[1,8192,64]{1,2,0:T(8,128)(2,1)} %param.9) | copy-start | bytes 3145732
  11.6 17.8 %copy-start.2 = (bf16[1,16,8192]{2,1,0:T(8,128)(2,1)S(1)}, bf16[1,16,8192]{2,1,0:T(8,128)(2,1)}, u32[]{:S(2)}) copy-start(bf16[1,16,8192]{2,1,0:T(8,128)(2,1)} %param.7) | copy-start | bytes 786436
  11.7 5.9 %collective-permute-start.4 = (bf16[16,4096]{1,0:T(8,128)(2,1)S(1)}, bf16[16,4096]{1,0:T(8,128)(2,1)S(1)}, u32[]{:S(2)}, u32[]{:S(2)}) collective-permute-start(bf16[16,4096]{1,0:T(8,128)(2,1)S(1)} %get-tuple-element.19), channel_id=1, source_target_pairs={{0,2},{2,4},{4,6},{6,7},{7,5},{5,3},{3,1},{1,0},{8,10},{10,12},{12... | collective-permute-start | bytes 393224 | tf_op jit(solution)/shard_map/ppermute | solution.py:35
  12.1 6.1 %collective-permute-start.7 = (bf16[16,4096]{1,0:T(8,128)(2,1)S(1)}, bf16[16,4096]{1,0:T(8,128)(2,1)S(1)}, u32[]{:S(2)}, u32[]{:S(2)}) collective-permute-start(bf16[16,4096]{1,0:T(8,128)(2,1)S(1)} %get-tuple-element.22), channel_id=1, source_target_pairs={{2,0},{4,2},{6,4},{7,6},{5,7},{3,5},{1,3},{0,1},{10,8},{12,10},{14... | collective-permute-start | bytes 393224 | tf_op jit(solution)/shard_map/ppermute | solution.py:35
  13.7 7.3 %collective-permute-start.5 = (bf16[16,4096]{1,0:T(8,128)(2,1)S(1)}, bf16[16,4096]{1,0:T(8,128)(2,1)S(1)}, u32[]{:S(2)}, u32[]{:S(2)}) collective-permute-start(bf16[16,4096]{1,0:T(8,128)(2,1)S(1)} %get-tuple-element.20), channel_id=1, source_target_pairs={{2,0},{4,2},{6,4},{7,6},{5,7},{3,5},{1,3},{0,1},{10,8},{12,10},{14... | collective-permute-start | bytes 393224 | tf_op jit(solution)/shard_map/ppermute | solution.py:35
  15.3 6.9 %collective-permute-start.6 = (bf16[16,4096]{1,0:T(8,128)(2,1)S(1)}, bf16[16,4096]{1,0:T(8,128)(2,1)S(1)}, u32[]{:S(2)}, u32[]{:S(2)}) collective-permute-start(bf16[16,4096]{1,0:T(8,128)(2,1)S(1)} %get-tuple-element.21), channel_id=1, source_target_pairs={{0,2},{2,4},{4,6},{6,7},{7,5},{5,3},{3,1},{1,0},{8,10},{10,12},{12... | collective-permute-start | bytes 393224 | tf_op jit(solution)/shard_map/ppermute | solution.py:35
  17.5 6.4 %collective-permute-start.8 = (bf16[16,4096]{1,0:T(8,128)(2,1)S(1)}, bf16[16,4096]{1,0:T(8,128)(2,1)S(1)}, u32[]{:S(2)}, u32[]{:S(2)}) collective-permute-start(bf16[16,4096]{1,0:T(8,128)(2,1)S(1)} %collective-permute-done.4.refs_3_), channel_id=1, source_target_pairs={{0,2},{2,4},{4,6},{6,7},{7,5},{5,3},{3,1},{1,0},{8,10},{10,12},{12... | collective-permute-start | bytes 393224 | tf_op jit(solution)/shard_map/ppermute | solution.py:35
  18.2 6.3 %collective-permute-start.11 = (bf16[16,4096]{1,0:T(8,128)(2,1)S(1)}, bf16[16,4096]{1,0:T(8,128)(2,1)S(1)}, u32[]{:S(2)}, u32[]{:S(2)}) collective-permute-start(bf16[16,4096]{1,0:T(8,128)(2,1)S(1)} %collective-permute-done.7.refs_6_), channel_id=1, source_target_pairs={{2,0},{4,2},{6,4},{7,6},{5,7},{3,5},{1,3},{0,1},{10,8},{12,10},{14... | collective-permute-start | bytes 393224 | tf_op jit(solution)/shard_map/ppermute | solution.py:35
  21.0 5.4 %collective-permute-start.9 = (bf16[16,4096]{1,0:T(8,128)(2,1)S(1)}, bf16[16,4096]{1,0:T(8,128)(2,1)S(1)}, u32[]{:S(2)}, u32[]{:S(2)}) collective-permute-start(bf16[16,4096]{1,0:T(8,128)(2,1)S(1)} %collective-permute-done.5.refs_4_), channel_id=1, source_target_pairs={{2,0},{4,2},{6,4},{7,6},{5,7},{3,5},{1,3},{0,1},{10,8},{12,10},{14... | collective-permute-start | bytes 393224 | tf_op jit(solution)/shard_map/ppermute | solution.py:35
  22.2 5.0 %collective-permute-start.10 = (bf16[16,4096]{1,0:T(8,128)(2,1)S(1)}, bf16[16,4096]{1,0:T(8,128)(2,1)S(1)}, u32[]{:S(2)}, u32[]{:S(2)}) collective-permute-start(bf16[16,4096]{1,0:T(8,128)(2,1)S(1)} %collective-permute-done.6.refs_5_), channel_id=1, source_target_pairs={{0,2},{2,4},{4,6},{6,7},{7,5},{5,3},{3,1},{1,0},{8,10},{10,12},{12... | collective-permute-start | bytes 393224 | tf_op jit(solution)/shard_map/ppermute | solution.py:35
  23.9 5.0 %collective-permute-start.12 = (bf16[16,4096]{1,0:T(8,128)(2,1)S(1)}, bf16[16,4096]{1,0:T(8,128)(2,1)S(1)}, u32[]{:S(2)}, u32[]{:S(2)}) collective-permute-start(bf16[16,4096]{1,0:T(8,128)(2,1)S(1)} %collective-permute-done.8.refs_7_), channel_id=1, source_target_pairs={{0,2},{2,4},{4,6},{6,7},{7,5},{5,3},{3,1},{1,0},{8,10},{10,12},{12... | collective-permute-start | bytes 393224 | tf_op jit(solution)/shard_map/ppermute | solution.py:37
  24.4 5.0 %collective-permute-start.13 = (bf16[16,4096]{1,0:T(8,128)(2,1)S(1)}, bf16[16,4096]{1,0:T(8,128)(2,1)S(1)}, u32[]{:S(2)}, u32[]{:S(2)}) collective-permute-start(bf16[16,4096]{1,0:T(8,128)(2,1)S(1)} %collective-permute-done.11.refs_10_), channel_id=1, source_target_pairs={{2,0},{4,2},{6,4},{7,6},{5,7},{3,5},{1,3},{0,1},{10,8},{12,10},{14... | collective-permute-start | bytes 393224 | tf_op jit(solution)/shard_map/ppermute | solution.py:37
  31.6 20.2 %all-to-all-start = ((bf16[8,32,1280]{2,1,0:T(8,128)(2,1)}), bf16[8,32,1280]{2,1,0:T(8,128)(2,1)S(1)}, u32[]{:S(2)}, u32[]{:S(2)}) async-start(bf16[8,32,1280]{2,1,0:T(8,128)(2,1)} %get-tuple-element.24), calls=%async_computation | async-start | bytes 1310720 | tf_op jit(solution)/shard_map/all_to_all | solution.py:216

commit v26 on v23

--- a/solution.py
+++ b/solution.py
@@ -60,11 +60,11 @@
 
 def exchange_order(n):
     ring = ring_of(n)
-    return ring[1:] + ring[:1]
+    return [ring[1 - p] for p in range(n)]
 
 
 def exchange_place(i, n):
-    return lax.rem(ring_place(i, n) + n - 1, n)
+    return lax.rem(n + 1 - ring_place(i, n), n)
 
 
 def ring_sources(axis, half):

time: 50.7 us -> 52.2 us (1.030)
  waiting for transfers between devices: 12.8 us -> 14.3 us
    all_to_all x1, waiting for transfers between devices: 3.02 us -> 4.52 us  [on_device(): lax.all_to_all(lifts, 'tp', split_axis=0, concat_axis=0, axis_index_group...]
  transfers between devices with their start and end apart: 15 -> 15, of which waited for: 11 -> 11; matrix products, arithmetic and copies ran while one was open for 17% -> 16% of each run, Pallas kernels for 3% -> 3%
where the time goes in v26:
time: 52.2 us; the launch traced here: 51.9 us
  starting transfers between devices  19.5 us (37%)
  waiting for transfers between devices  14.3 us (27%)
  matrix products  8.52 us (16%)
  Pallas kernels  5 us (10%)
  local copies, waits for them, and re-layouts  4.53 us (9%)
    dot_general x1, matrix products, on_device(): jnp.dot(gathered, base_projection_weight, preferred_element_type=jnp.floa...  8.52 us
    ppermute x8, starting transfers between devices, ring_gather(): lax.ppermute(x, axis, way)  7.73 us
    all_to_all x1, starting transfers between devices, on_device(): lax.all_to_all(lifts, 'tp', split_axis=0, concat_axis=0, axis_index_group...  6.21 us
    ppermute x8, waiting for transfers between devices, ring_gather(): lax.ppermute(x, axis, way)  5.78 us
    unnamed x12, local copies, waits for them, and re-layouts  4.53 us
    all_to_all x1, waiting for transfers between devices, on_device(): lax.all_to_all(lifts, 'tp', split_axis=0, concat_axis=0, axis_index_group...  4.52 us
    ppermute x1, starting transfers between devices, ring_gather(): lax.ppermute(block, axis, down)  2.97 us
    pallas_call x1, Pallas kernels, on_device(): pl.pallas_call(functools.partial(lift_kernel, groups), out_shape=[jax.Sha...  2.19 us
  transfers between devices with their start and end apart: 15, of which 11 were waited for; matrix products, arithmetic and copies ran while one was open for 16% of the time, Pallas kernels for 3%

profile of v26, /device:TPU:0, one launch (start us, length us, event | category | flops | bytes accessed | tf_op | source)
XLA Modules:
  0.0 51.9 jit_solution(13355521189609119408)
XLA Ops:
  0.5 3.0 %collective-permute-start.3 = (bf16[16,8192]{1,0:T(8,128)(2,1)}, bf16[16,8192]{1,0:T(8,128)(2,1)S(1)}, u32[]{:S(2)}, u32[]{:S(2)}) collective-permute-start(bf16[16,8192]{1,0:T(8,128)(2,1)} %bitcast.14), channel_id=1, source_target_pairs={{2,0},{4,2},{6,4},{7,6},{5,7},{3,5},{1,3},{0,1},{10,8},{12,10},{14... | collective-permute-start | bytes 786440 | tf_op jit(solution)/shard_map/ppermute | solution.py:30
  3.5 0.7 %copy-done.3 = s32[2,12]{1,0:T(2,128)S(1)} copy-done((s32[2,12]{1,0:T(2,128)S(1)}, s32[2,12]{1,0:T(2,128)}, u32[]{:S(2)}) %copy-start.3) | copy-done | bytes 120
  4.2 0.7 %copy-done.4 = s32[1,12]{1,0:T(1,128)S(1)} copy-done((s32[1,12]{1,0:T(1,128)S(1)}, s32[1,12]{1,0:T(1,128)}, u32[]{:S(2)}) %copy-start.4) | copy-done | bytes 72
  5.5 1.0 %place.1 = (s32[1,128]{1,0:T(1,128)S(1)}, s32[128,1]{1,0:T(8,128)S(1)}) custom-call(s32[2,12]{1,0:T(2,128)S(1)} %copy-done.3, s32[1,12]{1,0:T(1,128)S(1)} %copy-done.4, s32[16]{0:T(128)S(1)} %copy-done.5), custom_call_target="tpu_custom_call" | custom-call | tf_op jit(solution)/shard_map/place/pallas_call | solution.py:183
  6.6 1.3 %copy-done = bf16[1,64,10240]{2,1,0:T(8,128)(2,1)S(1)} copy-done((bf16[1,64,10240]{2,1,0:T(8,128)(2,1)S(1)}, bf16[1,64,10240]{2,1,0:T(8,128)(2,1)}, u32[]{:S(2)}) %copy-start) | copy-done | bytes 1310744
  7.9 1.2 %copy-done.1 = bf16[1,8192,64]{1,2,0:T(8,128)(2,1)S(1)} copy-done((bf16[1,8192,64]{1,2,0:T(8,128)(2,1)S(1)}, bf16[1,8192,64]{1,2,0:T(8,128)(2,1)}, u32[]{:S(2)}) %copy-start.1) | copy-done | bytes 1048600
  9.1 0.7 %stack.1 = (bf16[8192,128]{1,0:T(8,128)(2,1)S(1)}, bf16[128,10240]{1,0:T(8,128)(2,1)S(1)}) custom-call(bf16[64,8192]{1,0:T(8,128)(2,1)S(1)} %bitcast.13, bf16[64,8192]{1,0:T(8,128)(2,1)S(1)} %collective-permute-done.refs_1_, bf16[64,10240]{1,0:T(8,128)(2,1)S(1)} %bitcast.11, bf16[64,10240]{1,0:T(8,128)(2,1)S(1)} %collective-permute-done.1.refs_3_), custom_call_target="tpu_custom_call" | custom-call | tf_op jit(solution)/shard_map/stack/pallas_call | solution.py:172
  10.2 1.4 %collective-permute-done.2.refs_0_.refs_1_ = bf16[16,8192]{1,0:T(8,128)(2,1)S(1)} collective-permute-done((bf16[16,8192]{1,0:T(8,128)(2,1)}, bf16[16,8192]{1,0:T(8,128)(2,1)S(1)}, u32[]{:S(2)}, u32[]{:S(2)}) %collective-permute-start.2) | collective-permute-done | bytes 262176 | tf_op jit(solution)/shard_map/ppermute | solution.py:30
  12.1 1.7 %collective-permute-start.7 = (bf16[16,4096]{1,0:T(8,128)(2,1)S(1)}, bf16[16,4096]{1,0:T(8,128)(2,1)S(1)}, u32[]{:S(2)}, u32[]{:S(2)}) collective-permute-start(bf16[16,4096]{1,0:T(8,128)(2,1)S(1)} %get-tuple-element.22), channel_id=1, source_target_pairs={{2,0},{4,2},{6,4},{7,6},{5,7},{3,5},{1,3},{0,1},{10,8},{12,10},{14... | collective-permute-start | bytes 393224 | tf_op jit(solution)/shard_map/ppermute | solution.py:35
  13.7 1.6 %collective-permute-start.5 = (bf16[16,4096]{1,0:T(8,128)(2,1)S(1)}, bf16[16,4096]{1,0:T(8,128)(2,1)S(1)}, u32[]{:S(2)}, u32[]{:S(2)}) collective-permute-start(bf16[16,4096]{1,0:T(8,128)(2,1)S(1)} %get-tuple-element.20), channel_id=1, source_target_pairs={{2,0},{4,2},{6,4},{7,6},{5,7},{3,5},{1,3},{0,1},{10,8},{12,10},{14... | collective-permute-start | bytes 393224 | tf_op jit(solution)/shard_map/ppermute | solution.py:35
  15.8 1.7 %collective-permute-done.4.refs_3_ = bf16[16,4096]{1,0:T(8,128)(2,1)S(1)} collective-permute-done((bf16[16,4096]{1,0:T(8,128)(2,1)S(1)}, bf16[16,4096]{1,0:T(8,128)(2,1)S(1)}, u32[]{:S(2)}, u32[]{:S(2)}) %collective-permute-start.4) | collective-permute-done | bytes 131104 | tf_op jit(solution)/shard_map/ppermute | solution.py:35
  18.2 1.4 %collective-permute-start.11 = (bf16[16,4096]{1,0:T(8,128)(2,1)S(1)}, bf16[16,4096]{1,0:T(8,128)(2,1)S(1)}, u32[]{:S(2)}, u32[]{:S(2)}) collective-permute-start(bf16[16,4096]{1,0:T(8,128)(2,1)S(1)} %collective-permute-done.7.refs_6_), channel_id=1, source_target_pairs={{2,0},{4,2},{6,4},{7,6},{5,7},{3,5},{1,3},{0,1},{10,8},{12,10},{14... | collective-permute-start | bytes 393224 | tf_op jit(solution)/shard_map/ppermute | solution.py:35
  19.5 1.4 %collective-permute-done.5.refs_4_ = bf16[16,4096]{1,0:T(8,128)(2,1)S(1)} collective-permute-done((bf16[16,4096]{1,0:T(8,128)(2,1)S(1)}, bf16[16,4096]{1,0:T(8,128)(2,1)S(1)}, u32[]{:S(2)}, u32[]{:S(2)}) %collective-permute-start.5) | collective-permute-done | bytes 131104 | tf_op jit(solution)/shard_map/ppermute | solution.py:35
  21.0 1.2 %collective-permute-start.9 = (bf16[16,4096]{1,0:T(8,128)(2,1)S(1)}, bf16[16,4096]{1,0:T(8,128)(2,1)S(1)}, u32[]{:S(2)}, u32[]{:S(2)}) collective-permute-start(bf16[16,4096]{1,0:T(8,128)(2,1)S(1)} %collective-permute-done.5.refs_4_), channel_id=1, source_target_pairs={{2,0},{4,2},{6,4},{7,6},{5,7},{3,5},{1,3},{0,1},{10,8},{12,10},{14... | collective-permute-start | bytes 393224 | tf_op jit(solution)/shard_map/ppermute | solution.py:35
  22.2 0.8 %collective-permute-start.10 = (bf16[16,4096]{1,0:T(8,128)(2,1)S(1)}, bf16[16,4096]{1,0:T(8,128)(2,1)S(1)}, u32[]{:S(2)}, u32[]{:S(2)}) collective-permute-start(bf16[16,4096]{1,0:T(8,128)(2,1)S(1)} %collective-permute-done.6.refs_5_), channel_id=1, source_target_pairs={{0,2},{2,4},{4,6},{6,7},{7,5},{5,3},{3,1},{1,0},{8,10},{10,12},{12... | collective-permute-start | bytes 393224 | tf_op jit(solution)/shard_map/ppermute | solution.py:35
  23.0 0.9 %collective-permute-done.8.refs_7_ = bf16[16,4096]{1,0:T(8,128)(2,1)S(1)} collective-permute-done((bf16[16,4096]{1,0:T(8,128)(2,1)S(1)}, bf16[16,4096]{1,0:T(8,128)(2,1)S(1)}, u32[]{:S(2)}, u32[]{:S(2)}) %collective-permute-start.8) | collective-permute-done | bytes 131104 | tf_op jit(solution)/shard_map/ppermute | solution.py:35
  24.4 1.5 %collective-permute-start.13 = (bf16[16,4096]{1,0:T(8,128)(2,1)S(1)}, bf16[16,4096]{1,0:T(8,128)(2,1)S(1)}, u32[]{:S(2)}, u32[]{:S(2)}) collective-permute-start(bf16[16,4096]{1,0:T(8,128)(2,1)S(1)} %collective-permute-done.11.refs_10_), channel_id=1, source_target_pairs={{2,0},{4,2},{6,4},{7,6},{5,7},{3,5},{1,3},{0,1},{10,8},{12,10},{14... | collective-permute-start | bytes 393224 | tf_op jit(solution)/shard_map/ppermute | solution.py:37
  26.4 0.8 %collective-permute-done.10.refs_9_ = bf16[16,4096]{1,0:T(8,128)(2,1)S(1)} collective-permute-done((bf16[16,4096]{1,0:T(8,128)(2,1)S(1)}, bf16[16,4096]{1,0:T(8,128)(2,1)S(1)}, u32[]{:S(2)}, u32[]{:S(2)}) %collective-permute-start.10) | collective-permute-done | bytes 131104 | tf_op jit(solution)/shard_map/ppermute | solution.py:35
  27.2 1.6 %collective-permute-done.12.refs_11_ = bf16[16,4096]{1,0:T(8,128)(2,1)S(1)} collective-permute-done((bf16[16,4096]{1,0:T(8,128)(2,1)S(1)}, bf16[16,4096]{1,0:T(8,128)(2,1)S(1)}, u32[]{:S(2)}, u32[]{:S(2)}) %collective-permute-start.12) | collective-permute-done | bytes 131104 | tf_op jit(solution)/shard_map/ppermute | solution.py:37
  29.4 2.2 %lift.1 = (bf16[128,8192]{1,0:T(8,128)(2,1)S(1)}, bf16[8,32,1280]{2,1,0:T(8,128)(2,1)}) custom-call(s32[1,128]{1,0:T(1,128)S(1)} %get-tuple-element.16.refs_4_.place_ref, bf16[8192,128]{1,0:T(8,128)(2,1)S(1)} %get-tuple-element.17.refs_2_.down_ref, bf16[128,10240]{1,0:T(8,128)(2,1)S(1)} %get-tuple-element.18.refs_3_.up_ref, bf16[16,8192]{1,0:T(8,128)(2,1)S(1)} %bitcast.16, ...), custom_call_target="tpu_custom_call" | custom-call | flops 352321536 | bytes 4718592 | tf_op jit(solution)/shard_map/lift/pallas_call | solution.py:196
  31.6 6.2 %all-to-all-start = ((bf16[8,32,1280]{2,1,0:T(8,128)(2,1)}), bf16[8,32,1280]{2,1,0:T(8,128)(2,1)S(1)}, u32[]{:S(2)}, u32[]{:S(2)}) async-start(bf16[8,32,1280]{2,1,0:T(8,128)(2,1)} %get-tuple-element.24), calls=%async_computation | async-start | bytes 1310720 | tf_op jit(solution)/shard_map/all_to_all | solution.py:216
  37.8 8.5 %fusion.base_ref = f32[128,1280]{1,0:T(8,128)S(1)} fusion(bf16[128,8192]{1,0:T(8,128)(2,1)S(1)} %get-tuple-element.23, bf16[8192,1280]{1,0:T(8,128)(2,1)} %param.8), kind=kOutput, calls=%fused_computation | convolution fusion | flops 2684354560 | bytes 23724032 | tf_op jit(solution)/shard_map/dot_general | solution.py:220
  46.4 4.5 %all-to-all-done = bf16[8,32,1280]{2,1,0:T(8,128)(2,1)S(1)} async-done(((bf16[8,32,1280]{2,1,0:T(8,128)(2,1)}), bf16[8,32,1280]{2,1,0:T(8,128)(2,1)S(1)}, u32[]{:S(2)}, u32[]{:S(2)}) %all-to-all-start) | async-done | bytes 655392 | tf_op jit(solution)/shard_map/all_to_all | solution.py:216
  50.9 1.0 %add.1 = bf16[128,1280]{1,0:T(8,128)(2,1)} custom-call(s32[128,1]{1,0:T(8,128)S(1)} %get-tuple-element.15.refs_5_.place_ref, f32[128,1280]{1,0:T(8,128)S(1)} %fusion.base_ref, bf16[256,1280]{1,0:T(8,128)(2,1)S(1)} %bitcast.9), custom_call_target="tpu_custom_call" | custom-call | tf_op jit(solution)/shard_map/add/pallas_call | solution.py:221
  (24 shorter events, 4.8 us)
Async XLA Ops:
  0.0 6.6 %collective-permute-start.1 = (bf16[64,10240]{1,0:T(8,128)(2,1)}, bf16[64,10240]{1,0:T(8,128)(2,1)S(1)}, u32[]{:S(2)}, u32[]{:S(2)}) collective-permute-start(bf16[64,10240]{1,0:T(8,128)(2,1)} %bitcast.10), channel_id=1, source_target_pairs={{8,0},{0,8},{9,1},{1,9},{10,2},{2,10},{11,3},{3,11},{12,4},{4,12},... | collective-permute-start | bytes 3932168 | tf_op jit(solution)/shard_map/ppermute | solution.py:16
  0.5 6.1 %collective-permute-start = (bf16[64,8192]{1,0:T(8,128)(2,1)}, bf16[64,8192]{1,0:T(8,128)(2,1)S(1)}, u32[]{:S(2)}, u32[]{:S(2)}) collective-permute-start(bf16[64,8192]{1,0:T(8,128)(2,1)} %bitcast.12), channel_id=1, source_target_pairs={{8,0},{0,8},{9,1},{1,9},{10,2},{2,10},{11,3},{3,11},{12,4},{4,12},... | collective-permute-start | bytes 3145736 | tf_op jit(solution)/shard_map/ppermute | solution.py:16
  0.5 9.7 %collective-permute-start.3 = (bf16[16,8192]{1,0:T(8,128)(2,1)}, bf16[16,8192]{1,0:T(8,128)(2,1)S(1)}, u32[]{:S(2)}, u32[]{:S(2)}) collective-permute-start(bf16[16,8192]{1,0:T(8,128)(2,1)} %bitcast.14), channel_id=1, source_target_pairs={{2,0},{4,2},{6,4},{7,6},{5,7},{3,5},{1,3},{0,1},{10,8},{12,10},{14... | collective-permute-start | bytes 786440 | tf_op jit(solution)/shard_map/ppermute | solution.py:30
  3.5 8.1 %collective-permute-start.2 = (bf16[16,8192]{1,0:T(8,128)(2,1)}, bf16[16,8192]{1,0:T(8,128)(2,1)S(1)}, u32[]{:S(2)}, u32[]{:S(2)}) collective-permute-start(bf16[16,8192]{1,0:T(8,128)(2,1)} %bitcast.15), channel_id=1, source_target_pairs={{0,2},{2,4},{4,6},{6,7},{7,5},{5,3},{3,1},{1,0},{8,10},{10,12},{12... | collective-permute-start | bytes 786440 | tf_op jit(solution)/shard_map/ppermute | solution.py:30
  3.5 0.7 %copy-start.3 = (s32[2,12]{1,0:T(2,128)S(1)}, s32[2,12]{1,0:T(2,128)}, u32[]{:S(2)}) copy-start(s32[2,12]{1,0:T(2,128)} %ids_ref.1) | copy-start | bytes 292
  4.2 0.7 %copy-start.4 = (s32[1,12]{1,0:T(1,128)S(1)}, s32[1,12]{1,0:T(1,128)}, u32[]{:S(2)}) copy-start(s32[1,12]{1,0:T(1,128)} %lengths_ref.1) | copy-start | bytes 148
  4.9 0.7 %copy-start.5 = (s32[16]{0:T(128)S(1)}, s32[16]{0:T(128)}, u32[]{:S(2)}) copy-start(s32[16]{0:T(128)} %slots_ref.1) | copy-start | bytes 196
  6.6 1.3 %copy-start = (bf16[1,64,10240]{2,1,0:T(8,128)(2,1)S(1)}, bf16[1,64,10240]{2,1,0:T(8,128)(2,1)}, u32[]{:S(2)}) copy-start(bf16[1,64,10240]{2,1,0:T(8,128)(2,1)} %param.10) | copy-start | bytes 3932164
  7.9 1.2 %copy-start.1 = (bf16[1,8192,64]{1,2,0:T(8,128)(2,1)S(1)}, bf16[1,8192,64]{1,2,0:T(8,128)(2,1)}, u32[]{:S(2)}) copy-start(bf16[1,8192,64]{1,2,0:T(8,128)(2,1)} %param.9) | copy-start | bytes 3145732
  11.6 17.8 %copy-start.2 = (bf16[1,16,8192]{2,1,0:T(8,128)(2,1)S(1)}, bf16[1,16,8192]{2,1,0:T(8,128)(2,1)}, u32[]{:S(2)}) copy-start(bf16[1,16,8192]{2,1,0:T(8,128)(2,1)} %param.7) | copy-start | bytes 786436
  11.7 5.9 %collective-permute-start.4 = (bf16[16,4096]{1,0:T(8,128)(2,1)S(1)}, bf16[16,4096]{1,0:T(8,128)(2,1)S(1)}, u32[]{:S(2)}, u32[]{:S(2)}) collective-permute-start(bf16[16,4096]{1,0:T(8,128)(2,1)S(1)} %get-tuple-element.19), channel_id=1, source_target_pairs={{0,2},{2,4},{4,6},{6,7},{7,5},{5,3},{3,1},{1,0},{8,10},{10,12},{12... | collective-permute-start | bytes 393224 | tf_op jit(solution)/shard_map/ppermute | solution.py:35
  12.1 6.1 %collective-permute-start.7 = (bf16[16,4096]{1,0:T(8,128)(2,1)S(1)}, bf16[16,4096]{1,0:T(8,128)(2,1)S(1)}, u32[]{:S(2)}, u32[]{:S(2)}) collective-permute-start(bf16[16,4096]{1,0:T(8,128)(2,1)S(1)} %get-tuple-element.22), channel_id=1, source_target_pairs={{2,0},{4,2},{6,4},{7,6},{5,7},{3,5},{1,3},{0,1},{10,8},{12,10},{14... | collective-permute-start | bytes 393224 | tf_op jit(solution)/shard_map/ppermute | solution.py:35
  13.7 7.3 %collective-permute-start.5 = (bf16[16,4096]{1,0:T(8,128)(2,1)S(1)}, bf16[16,4096]{1,0:T(8,128)(2,1)S(1)}, u32[]{:S(2)}, u32[]{:S(2)}) collective-permute-start(bf16[16,4096]{1,0:T(8,128)(2,1)S(1)} %get-tuple-element.20), channel_id=1, source_target_pairs={{2,0},{4,2},{6,4},{7,6},{5,7},{3,5},{1,3},{0,1},{10,8},{12,10},{14... | collective-permute-start | bytes 393224 | tf_op jit(solution)/shard_map/ppermute | solution.py:35
  15.3 6.9 %collective-permute-start.6 = (bf16[16,4096]{1,0:T(8,128)(2,1)S(1)}, bf16[16,4096]{1,0:T(8,128)(2,1)S(1)}, u32[]{:S(2)}, u32[]{:S(2)}) collective-permute-start(bf16[16,4096]{1,0:T(8,128)(2,1)S(1)} %get-tuple-element.21), channel_id=1, source_target_pairs={{0,2},{2,4},{4,6},{6,7},{7,5},{5,3},{3,1},{1,0},{8,10},{10,12},{12... | collective-permute-start | bytes 393224 | tf_op jit(solution)/shard_map/ppermute | solution.py:35
  17.5 6.4 %collective-permute-start.8 = (bf16[16,4096]{1,0:T(8,128)(2,1)S(1)}, bf16[16,4096]{1,0:T(8,128)(2,1)S(1)}, u32[]{:S(2)}, u32[]{:S(2)}) collective-permute-start(bf16[16,4096]{1,0:T(8,128)(2,1)S(1)} %collective-permute-done.4.refs_3_), channel_id=1, source_target_pairs={{0,2},{2,4},{4,6},{6,7},{7,5},{5,3},{3,1},{1,0},{8,10},{10,12},{12... | collective-permute-start | bytes 393224 | tf_op jit(solution)/shard_map/ppermute | solution.py:35
  18.2 6.3 %collective-permute-start.11 = (bf16[16,4096]{1,0:T(8,128)(2,1)S(1)}, bf16[16,4096]{1,0:T(8,128)(2,1)S(1)}, u32[]{:S(2)}, u32[]{:S(2)}) collective-permute-start(bf16[16,4096]{1,0:T(8,128)(2,1)S(1)} %collective-permute-done.7.refs_6_), channel_id=1, source_target_pairs={{2,0},{4,2},{6,4},{7,6},{5,7},{3,5},{1,3},{0,1},{10,8},{12,10},{14... | collective-permute-start | bytes 393224 | tf_op jit(solution)/shard_map/ppermute | solution.py:35
  21.0 5.4 %collective-permute-start.9 = (bf16[16,4096]{1,0:T(8,128)(2,1)S(1)}, bf16[16,4096]{1,0:T(8,128)(2,1)S(1)}, u32[]{:S(2)}, u32[]{:S(2)}) collective-permute-start(bf16[16,4096]{1,0:T(8,128)(2,1)S(1)} %collective-permute-done.5.refs_4_), channel_id=1, source_target_pairs={{2,0},{4,2},{6,4},{7,6},{5,7},{3,5},{1,3},{0,1},{10,8},{12,10},{14... | collective-permute-start | bytes 393224 | tf_op jit(solution)/shard_map/ppermute | solution.py:35
  22.2 5.0 %collective-permute-start.10 = (bf16[16,4096]{1,0:T(8,128)(2,1)S(1)}, bf16[16,4096]{1,0:T(8,128)(2,1)S(1)}, u32[]{:S(2)}, u32[]{:S(2)}) collective-permute-start(bf16[16,4096]{1,0:T(8,128)(2,1)S(1)} %collective-permute-done.6.refs_5_), channel_id=1, source_target_pairs={{0,2},{2,4},{4,6},{6,7},{7,5},{5,3},{3,1},{1,0},{8,10},{10,12},{12... | collective-permute-start | bytes 393224 | tf_op jit(solution)/shard_map/ppermute | solution.py:35
  23.9 5.0 %collective-permute-start.12 = (bf16[16,4096]{1,0:T(8,128)(2,1)S(1)}, bf16[16,4096]{1,0:T(8,128)(2,1)S(1)}, u32[]{:S(2)}, u32[]{:S(2)}) collective-permute-start(bf16[16,4096]{1,0:T(8,128)(2,1)S(1)} %collective-permute-done.8.refs_7_), channel_id=1, source_target_pairs={{0,2},{2,4},{4,6},{6,7},{7,5},{5,3},{3,1},{1,0},{8,10},{10,12},{12... | collective-permute-start | bytes 393224 | tf_op jit(solution)/shard_map/ppermute | solution.py:37
  24.4 5.0 %collective-permute-start.13 = (bf16[16,4096]{1,0:T(8,128)(2,1)S(1)}, bf16[16,4096]{1,0:T(8,128)(2,1)S(1)}, u32[]{:S(2)}, u32[]{:S(2)}) collective-permute-start(bf16[16,4096]{1,0:T(8,128)(2,1)S(1)} %collective-permute-done.11.refs_10_), channel_id=1, source_target_pairs={{2,0},{4,2},{6,4},{7,6},{5,7},{3,5},{1,3},{0,1},{10,8},{12,10},{14... | collective-permute-start | bytes 393224 | tf_op jit(solution)/shard_map/ppermute | solution.py:37
  31.6 19.3 %all-to-all-start = ((bf16[8,32,1280]{2,1,0:T(8,128)(2,1)}), bf16[8,32,1280]{2,1,0:T(8,128)(2,1)S(1)}, u32[]{:S(2)}, u32[]{:S(2)}) async-start(bf16[8,32,1280]{2,1,0:T(8,128)(2,1)} %get-tuple-element.24), calls=%async_computation | async-start | bytes 1310720 | tf_op jit(solution)/shard_map/all_to_all | solution.py:216

commit v27 on v26

--- a/solution.py
+++ b/solution.py
@@ -60,11 +60,11 @@
 
 def exchange_order(n):
     ring = ring_of(n)
-    return [ring[1 - p] for p in range(n)]
+    return ring[2:] + ring[:2]
 
 
 def exchange_place(i, n):
-    return lax.rem(n + 1 - ring_place(i, n), n)
+    return lax.rem(ring_place(i, n) + n - 2, n)
 
 
 def ring_sources(axis, half):

time: 52.2 us -> 49.8 us (0.954)
  waiting for transfers between devices: 14.3 us -> 11.6 us
    all_to_all x1, waiting for transfers between devices: 4.52 us -> 1.82 us  [on_device(): lax.all_to_all(lifts, 'tp', split_axis=0, concat_axis=0, axis_index_group...]
  transfers between devices with their start and end apart: 15 -> 15, of which waited for: 11 -> 11; matrix products, arithmetic and copies ran while one was open for 16% -> 17% of each run, Pallas kernels for 3% -> 4%
where the time goes in v27:
time: 49.8 us; the launch traced here: 49.5 us
  starting transfers between devices  19.8 us (40%)
  waiting for transfers between devices  11.6 us (23%)
  matrix products  8.53 us (17%)
  Pallas kernels  5 us (10%)
  local copies, waits for them, and re-layouts  4.53 us (9%)
    dot_general x1, matrix products, on_device(): jnp.dot(gathered, base_projection_weight, preferred_element_type=jnp.floa...  8.53 us
    ppermute x8, starting transfers between devices, ring_gather(): lax.ppermute(x, axis, way)  7.73 us
    all_to_all x1, starting transfers between devices, on_device(): lax.all_to_all(lifts, 'tp', split_axis=0, concat_axis=0, axis_index_group...  6.51 us
    ppermute x8, waiting for transfers between devices, ring_gather(): lax.ppermute(x, axis, way)  5.78 us
    unnamed x12, local copies, waits for them, and re-layouts  4.53 us
    ppermute x1, starting transfers between devices, ring_gather(): lax.ppermute(block, axis, down)  2.97 us
    pallas_call x1, Pallas kernels, on_device(): pl.pallas_call(functools.partial(lift_kernel, groups), out_shape=[jax.Sha...  2.19 us
    all_to_all x1, waiting for transfers between devices, on_device(): lax.all_to_all(lifts, 'tp', split_axis=0, concat_axis=0, axis_index_group...  1.82 us
  transfers between devices with their start and end apart: 15, of which 11 were waited for; matrix products, arithmetic and copies ran while one was open for 17% of the time, Pallas kernels for 4%

profile of v27, /device:TPU:0, one launch (start us, length us, event | category | flops | bytes accessed | tf_op | source)
XLA Modules:
  0.0 49.5 jit_solution(3152985110694578179)
XLA Ops:
  0.5 3.0 %collective-permute-start.3 = (bf16[16,8192]{1,0:T(8,128)(2,1)}, bf16[16,8192]{1,0:T(8,128)(2,1)S(1)}, u32[]{:S(2)}, u32[]{:S(2)}) collective-permute-start(bf16[16,8192]{1,0:T(8,128)(2,1)} %bitcast.14), channel_id=1, source_target_pairs={{2,0},{4,2},{6,4},{7,6},{5,7},{3,5},{1,3},{0,1},{10,8},{12,10},{14... | collective-permute-start | bytes 786440 | tf_op jit(solution)/shard_map/ppermute | solution.py:30
  3.5 0.7 %copy-done.3 = s32[2,12]{1,0:T(2,128)S(1)} copy-done((s32[2,12]{1,0:T(2,128)S(1)}, s32[2,12]{1,0:T(2,128)}, u32[]{:S(2)}) %copy-start.3) | copy-done | bytes 120
  4.2 0.7 %copy-done.4 = s32[1,12]{1,0:T(1,128)S(1)} copy-done((s32[1,12]{1,0:T(1,128)S(1)}, s32[1,12]{1,0:T(1,128)}, u32[]{:S(2)}) %copy-start.4) | copy-done | bytes 72
  5.5 1.0 %place.1 = (s32[1,128]{1,0:T(1,128)S(1)}, s32[128,1]{1,0:T(8,128)S(1)}) custom-call(s32[2,12]{1,0:T(2,128)S(1)} %copy-done.3, s32[1,12]{1,0:T(1,128)S(1)} %copy-done.4, s32[16]{0:T(128)S(1)} %copy-done.5), custom_call_target="tpu_custom_call" | custom-call | tf_op jit(solution)/shard_map/place/pallas_call | solution.py:183
  6.6 1.3 %copy-done = bf16[1,64,10240]{2,1,0:T(8,128)(2,1)S(1)} copy-done((bf16[1,64,10240]{2,1,0:T(8,128)(2,1)S(1)}, bf16[1,64,10240]{2,1,0:T(8,128)(2,1)}, u32[]{:S(2)}) %copy-start) | copy-done | bytes 1310744
  7.9 1.2 %copy-done.1 = bf16[1,8192,64]{1,2,0:T(8,128)(2,1)S(1)} copy-done((bf16[1,8192,64]{1,2,0:T(8,128)(2,1)S(1)}, bf16[1,8192,64]{1,2,0:T(8,128)(2,1)}, u32[]{:S(2)}) %copy-start.1) | copy-done | bytes 1048600
  9.1 0.7 %stack.1 = (bf16[8192,128]{1,0:T(8,128)(2,1)S(1)}, bf16[128,10240]{1,0:T(8,128)(2,1)S(1)}) custom-call(bf16[64,8192]{1,0:T(8,128)(2,1)S(1)} %bitcast.13, bf16[64,8192]{1,0:T(8,128)(2,1)S(1)} %collective-permute-done.refs_1_, bf16[64,10240]{1,0:T(8,128)(2,1)S(1)} %bitcast.11, bf16[64,10240]{1,0:T(8,128)(2,1)S(1)} %collective-permute-done.1.refs_3_), custom_call_target="tpu_custom_call" | custom-call | tf_op jit(solution)/shard_map/stack/pallas_call | solution.py:172
  10.2 1.4 %collective-permute-done.2.refs_0_.refs_1_ = bf16[16,8192]{1,0:T(8,128)(2,1)S(1)} collective-permute-done((bf16[16,8192]{1,0:T(8,128)(2,1)}, bf16[16,8192]{1,0:T(8,128)(2,1)S(1)}, u32[]{:S(2)}, u32[]{:S(2)}) %collective-permute-start.2) | collective-permute-done | bytes 262176 | tf_op jit(solution)/shard_map/ppermute | solution.py:30
  12.1 1.7 %collective-permute-start.7 = (bf16[16,4096]{1,0:T(8,128)(2,1)S(1)}, bf16[16,4096]{1,0:T(8,128)(2,1)S(1)}, u32[]{:S(2)}, u32[]{:S(2)}) collective-permute-start(bf16[16,4096]{1,0:T(8,128)(2,1)S(1)} %get-tuple-element.22), channel_id=1, source_target_pairs={{2,0},{4,2},{6,4},{7,6},{5,7},{3,5},{1,3},{0,1},{10,8},{12,10},{14... | collective-permute-start | bytes 393224 | tf_op jit(solution)/shard_map/ppermute | solution.py:35
  13.7 1.6 %collective-permute-start.5 = (bf16[16,4096]{1,0:T(8,128)(2,1)S(1)}, bf16[16,4096]{1,0:T(8,128)(2,1)S(1)}, u32[]{:S(2)}, u32[]{:S(2)}) collective-permute-start(bf16[16,4096]{1,0:T(8,128)(2,1)S(1)} %get-tuple-element.20), channel_id=1, source_target_pairs={{2,0},{4,2},{6,4},{7,6},{5,7},{3,5},{1,3},{0,1},{10,8},{12,10},{14... | collective-permute-start | bytes 393224 | tf_op jit(solution)/shard_map/ppermute | solution.py:35
  15.8 1.7 %collective-permute-done.4.refs_3_ = bf16[16,4096]{1,0:T(8,128)(2,1)S(1)} collective-permute-done((bf16[16,4096]{1,0:T(8,128)(2,1)S(1)}, bf16[16,4096]{1,0:T(8,128)(2,1)S(1)}, u32[]{:S(2)}, u32[]{:S(2)}) %collective-permute-start.4) | collective-permute-done | bytes 131104 | tf_op jit(solution)/shard_map/ppermute | solution.py:35
  18.2 1.4 %collective-permute-start.11 = (bf16[16,4096]{1,0:T(8,128)(2,1)S(1)}, bf16[16,4096]{1,0:T(8,128)(2,1)S(1)}, u32[]{:S(2)}, u32[]{:S(2)}) collective-permute-start(bf16[16,4096]{1,0:T(8,128)(2,1)S(1)} %collective-permute-done.7.refs_6_), channel_id=1, source_target_pairs={{2,0},{4,2},{6,4},{7,6},{5,7},{3,5},{1,3},{0,1},{10,8},{12,10},{14... | collective-permute-start | bytes 393224 | tf_op jit(solution)/shard_map/ppermute | solution.py:35
  19.5 1.4 %collective-permute-done.5.refs_4_ = bf16[16,4096]{1,0:T(8,128)(2,1)S(1)} collective-permute-done((bf16[16,4096]{1,0:T(8,128)(2,1)S(1)}, bf16[16,4096]{1,0:T(8,128)(2,1)S(1)}, u32[]{:S(2)}, u32[]{:S(2)}) %collective-permute-start.5) | collective-permute-done | bytes 131104 | tf_op jit(solution)/shard_map/ppermute | solution.py:35
  21.0 1.2 %collective-permute-start.9 = (bf16[16,4096]{1,0:T(8,128)(2,1)S(1)}, bf16[16,4096]{1,0:T(8,128)(2,1)S(1)}, u32[]{:S(2)}, u32[]{:S(2)}) collective-permute-start(bf16[16,4096]{1,0:T(8,128)(2,1)S(1)} %collective-permute-done.5.refs_4_), channel_id=1, source_target_pairs={{2,0},{4,2},{6,4},{7,6},{5,7},{3,5},{1,3},{0,1},{10,8},{12,10},{14... | collective-permute-start | bytes 393224 | tf_op jit(solution)/shard_map/ppermute | solution.py:35
  22.2 0.8 %collective-permute-start.10 = (bf16[16,4096]{1,0:T(8,128)(2,1)S(1)}, bf16[16,4096]{1,0:T(8,128)(2,1)S(1)}, u32[]{:S(2)}, u32[]{:S(2)}) collective-permute-start(bf16[16,4096]{1,0:T(8,128)(2,1)S(1)} %collective-permute-done.6.refs_5_), channel_id=1, source_target_pairs={{0,2},{2,4},{4,6},{6,7},{7,5},{5,3},{3,1},{1,0},{8,10},{10,12},{12... | collective-permute-start | bytes 393224 | tf_op jit(solution)/shard_map/ppermute | solution.py:35
  23.0 0.9 %collective-permute-done.8.refs_7_ = bf16[16,4096]{1,0:T(8,128)(2,1)S(1)} collective-permute-done((bf16[16,4096]{1,0:T(8,128)(2,1)S(1)}, bf16[16,4096]{1,0:T(8,128)(2,1)S(1)}, u32[]{:S(2)}, u32[]{:S(2)}) %collective-permute-start.8) | collective-permute-done | bytes 131104 | tf_op jit(solution)/shard_map/ppermute | solution.py:35
  24.4 1.5 %collective-permute-start.13 = (bf16[16,4096]{1,0:T(8,128)(2,1)S(1)}, bf16[16,4096]{1,0:T(8,128)(2,1)S(1)}, u32[]{:S(2)}, u32[]{:S(2)}) collective-permute-start(bf16[16,4096]{1,0:T(8,128)(2,1)S(1)} %collective-permute-done.11.refs_10_), channel_id=1, source_target_pairs={{2,0},{4,2},{6,4},{7,6},{5,7},{3,5},{1,3},{0,1},{10,8},{12,10},{14... | collective-permute-start | bytes 393224 | tf_op jit(solution)/shard_map/ppermute | solution.py:37
  26.4 0.8 %collective-permute-done.10.refs_9_ = bf16[16,4096]{1,0:T(8,128)(2,1)S(1)} collective-permute-done((bf16[16,4096]{1,0:T(8,128)(2,1)S(1)}, bf16[16,4096]{1,0:T(8,128)(2,1)S(1)}, u32[]{:S(2)}, u32[]{:S(2)}) %collective-permute-start.10) | collective-permute-done | bytes 131104 | tf_op jit(solution)/shard_map/ppermute | solution.py:35
  27.2 1.6 %collective-permute-done.12.refs_11_ = bf16[16,4096]{1,0:T(8,128)(2,1)S(1)} collective-permute-done((bf16[16,4096]{1,0:T(8,128)(2,1)S(1)}, bf16[16,4096]{1,0:T(8,128)(2,1)S(1)}, u32[]{:S(2)}, u32[]{:S(2)}) %collective-permute-start.12) | collective-permute-done | bytes 131104 | tf_op jit(solution)/shard_map/ppermute | solution.py:37
  29.4 2.2 %lift.1 = (bf16[128,8192]{1,0:T(8,128)(2,1)S(1)}, bf16[8,32,1280]{2,1,0:T(8,128)(2,1)}) custom-call(s32[1,128]{1,0:T(1,128)S(1)} %get-tuple-element.16.refs_4_.place_ref, bf16[8192,128]{1,0:T(8,128)(2,1)S(1)} %get-tuple-element.17.refs_2_.down_ref, bf16[128,10240]{1,0:T(8,128)(2,1)S(1)} %get-tuple-element.18.refs_3_.up_ref, bf16[16,8192]{1,0:T(8,128)(2,1)S(1)} %bitcast.16, ...), custom_call_target="tpu_custom_call" | custom-call | flops 352321536 | bytes 4718592 | tf_op jit(solution)/shard_map/lift/pallas_call | solution.py:196
  31.6 6.5 %all-to-all-start = ((bf16[8,32,1280]{2,1,0:T(8,128)(2,1)}), bf16[8,32,1280]{2,1,0:T(8,128)(2,1)S(1)}, u32[]{:S(2)}, u32[]{:S(2)}) async-start(bf16[8,32,1280]{2,1,0:T(8,128)(2,1)} %get-tuple-element.24), calls=%async_computation | async-start | bytes 1310720 | tf_op jit(solution)/shard_map/all_to_all | solution.py:216
  38.1 8.5 %fusion.base_ref = f32[128,1280]{1,0:T(8,128)S(1)} fusion(bf16[128,8192]{1,0:T(8,128)(2,1)S(1)} %get-tuple-element.23, bf16[8192,1280]{1,0:T(8,128)(2,1)} %param.8), kind=kOutput, calls=%fused_computation | convolution fusion | flops 2684354560 | bytes 23724032 | tf_op jit(solution)/shard_map/dot_general | solution.py:220
  46.7 1.8 %all-to-all-done = bf16[8,32,1280]{2,1,0:T(8,128)(2,1)S(1)} async-done(((bf16[8,32,1280]{2,1,0:T(8,128)(2,1)}), bf16[8,32,1280]{2,1,0:T(8,128)(2,1)S(1)}, u32[]{:S(2)}, u32[]{:S(2)}) %all-to-all-start) | async-done | bytes 655392 | tf_op jit(solution)/shard_map/all_to_all | solution.py:216
  48.5 1.0 %add.1 = bf16[128,1280]{1,0:T(8,128)(2,1)} custom-call(s32[128,1]{1,0:T(8,128)S(1)} %get-tuple-element.15.refs_5_.place_ref, f32[128,1280]{1,0:T(8,128)S(1)} %fusion.base_ref, bf16[256,1280]{1,0:T(8,128)(2,1)S(1)} %bitcast.9), custom_call_target="tpu_custom_call" | custom-call | tf_op jit(solution)/shard_map/add/pallas_call | solution.py:221
  (24 shorter events, 4.8 us)
Async XLA Ops:
  0.0 6.6 %collective-permute-start.1 = (bf16[64,10240]{1,0:T(8,128)(2,1)}, bf16[64,10240]{1,0:T(8,128)(2,1)S(1)}, u32[]{:S(2)}, u32[]{:S(2)}) collective-permute-start(bf16[64,10240]{1,0:T(8,128)(2,1)} %bitcast.10), channel_id=1, source_target_pairs={{8,0},{0,8},{9,1},{1,9},{10,2},{2,10},{11,3},{3,11},{12,4},{4,12},... | collective-permute-start | bytes 3932168 | tf_op jit(solution)/shard_map/ppermute | solution.py:16
  0.5 6.1 %collective-permute-start = (bf16[64,8192]{1,0:T(8,128)(2,1)}, bf16[64,8192]{1,0:T(8,128)(2,1)S(1)}, u32[]{:S(2)}, u32[]{:S(2)}) collective-permute-start(bf16[64,8192]{1,0:T(8,128)(2,1)} %bitcast.12), channel_id=1, source_target_pairs={{8,0},{0,8},{9,1},{1,9},{10,2},{2,10},{11,3},{3,11},{12,4},{4,12},... | collective-permute-start | bytes 3145736 | tf_op jit(solution)/shard_map/ppermute | solution.py:16
  0.5 9.7 %collective-permute-start.3 = (bf16[16,8192]{1,0:T(8,128)(2,1)}, bf16[16,8192]{1,0:T(8,128)(2,1)S(1)}, u32[]{:S(2)}, u32[]{:S(2)}) collective-permute-start(bf16[16,8192]{1,0:T(8,128)(2,1)} %bitcast.14), channel_id=1, source_target_pairs={{2,0},{4,2},{6,4},{7,6},{5,7},{3,5},{1,3},{0,1},{10,8},{12,10},{14... | collective-permute-start | bytes 786440 | tf_op jit(solution)/shard_map/ppermute | solution.py:30
  3.5 8.1 %collective-permute-start.2 = (bf16[16,8192]{1,0:T(8,128)(2,1)}, bf16[16,8192]{1,0:T(8,128)(2,1)S(1)}, u32[]{:S(2)}, u32[]{:S(2)}) collective-permute-start(bf16[16,8192]{1,0:T(8,128)(2,1)} %bitcast.15), channel_id=1, source_target_pairs={{0,2},{2,4},{4,6},{6,7},{7,5},{5,3},{3,1},{1,0},{8,10},{10,12},{12... | collective-permute-start | bytes 786440 | tf_op jit(solution)/shard_map/ppermute | solution.py:30
  3.5 0.7 %copy-start.3 = (s32[2,12]{1,0:T(2,128)S(1)}, s32[2,12]{1,0:T(2,128)}, u32[]{:S(2)}) copy-start(s32[2,12]{1,0:T(2,128)} %ids_ref.1) | copy-start | bytes 292
  4.2 0.7 %copy-start.4 = (s32[1,12]{1,0:T(1,128)S(1)}, s32[1,12]{1,0:T(1,128)}, u32[]{:S(2)}) copy-start(s32[1,12]{1,0:T(1,128)} %lengths_ref.1) | copy-start | bytes 148
  4.9 0.7 %copy-start.5 = (s32[16]{0:T(128)S(1)}, s32[16]{0:T(128)}, u32[]{:S(2)}) copy-start(s32[16]{0:T(128)} %slots_ref.1) | copy-start | bytes 196
  6.6 1.3 %copy-start = (bf16[1,64,10240]{2,1,0:T(8,128)(2,1)S(1)}, bf16[1,64,10240]{2,1,0:T(8,128)(2,1)}, u32[]{:S(2)}) copy-start(bf16[1,64,10240]{2,1,0:T(8,128)(2,1)} %param.10) | copy-start | bytes 3932164
  7.9 1.2 %copy-start.1 = (bf16[1,8192,64]{1,2,0:T(8,128)(2,1)S(1)}, bf16[1,8192,64]{1,2,0:T(8,128)(2,1)}, u32[]{:S(2)}) copy-start(bf16[1,8192,64]{1,2,0:T(8,128)(2,1)} %param.9) | copy-start | bytes 3145732
  11.6 17.8 %copy-start.2 = (bf16[1,16,8192]{2,1,0:T(8,128)(2,1)S(1)}, bf16[1,16,8192]{2,1,0:T(8,128)(2,1)}, u32[]{:S(2)}) copy-start(bf16[1,16,8192]{2,1,0:T(8,128)(2,1)} %param.7) | copy-start | bytes 786436
  11.7 5.9 %collective-permute-start.4 = (bf16[16,4096]{1,0:T(8,128)(2,1)S(1)}, bf16[16,4096]{1,0:T(8,128)(2,1)S(1)}, u32[]{:S(2)}, u32[]{:S(2)}) collective-permute-start(bf16[16,4096]{1,0:T(8,128)(2,1)S(1)} %get-tuple-element.19), channel_id=1, source_target_pairs={{0,2},{2,4},{4,6},{6,7},{7,5},{5,3},{3,1},{1,0},{8,10},{10,12},{12... | collective-permute-start | bytes 393224 | tf_op jit(solution)/shard_map/ppermute | solution.py:35
  12.1 6.1 %collective-permute-start.7 = (bf16[16,4096]{1,0:T(8,128)(2,1)S(1)}, bf16[16,4096]{1,0:T(8,128)(2,1)S(1)}, u32[]{:S(2)}, u32[]{:S(2)}) collective-permute-start(bf16[16,4096]{1,0:T(8,128)(2,1)S(1)} %get-tuple-element.22), channel_id=1, source_target_pairs={{2,0},{4,2},{6,4},{7,6},{5,7},{3,5},{1,3},{0,1},{10,8},{12,10},{14... | collective-permute-start | bytes 393224 | tf_op jit(solution)/shard_map/ppermute | solution.py:35
  13.7 7.3 %collective-permute-start.5 = (bf16[16,4096]{1,0:T(8,128)(2,1)S(1)}, bf16[16,4096]{1,0:T(8,128)(2,1)S(1)}, u32[]{:S(2)}, u32[]{:S(2)}) collective-permute-start(bf16[16,4096]{1,0:T(8,128)(2,1)S(1)} %get-tuple-element.20), channel_id=1, source_target_pairs={{2,0},{4,2},{6,4},{7,6},{5,7},{3,5},{1,3},{0,1},{10,8},{12,10},{14... | collective-permute-start | bytes 393224 | tf_op jit(solution)/shard_map/ppermute | solution.py:35
  15.3 6.9 %collective-permute-start.6 = (bf16[16,4096]{1,0:T(8,128)(2,1)S(1)}, bf16[16,4096]{1,0:T(8,128)(2,1)S(1)}, u32[]{:S(2)}, u32[]{:S(2)}) collective-permute-start(bf16[16,4096]{1,0:T(8,128)(2,1)S(1)} %get-tuple-element.21), channel_id=1, source_target_pairs={{0,2},{2,4},{4,6},{6,7},{7,5},{5,3},{3,1},{1,0},{8,10},{10,12},{12... | collective-permute-start | bytes 393224 | tf_op jit(solution)/shard_map/ppermute | solution.py:35
  17.5 6.4 %collective-permute-start.8 = (bf16[16,4096]{1,0:T(8,128)(2,1)S(1)}, bf16[16,4096]{1,0:T(8,128)(2,1)S(1)}, u32[]{:S(2)}, u32[]{:S(2)}) collective-permute-start(bf16[16,4096]{1,0:T(8,128)(2,1)S(1)} %collective-permute-done.4.refs_3_), channel_id=1, source_target_pairs={{0,2},{2,4},{4,6},{6,7},{7,5},{5,3},{3,1},{1,0},{8,10},{10,12},{12... | collective-permute-start | bytes 393224 | tf_op jit(solution)/shard_map/ppermute | solution.py:35
  18.2 6.3 %collective-permute-start.11 = (bf16[16,4096]{1,0:T(8,128)(2,1)S(1)}, bf16[16,4096]{1,0:T(8,128)(2,1)S(1)}, u32[]{:S(2)}, u32[]{:S(2)}) collective-permute-start(bf16[16,4096]{1,0:T(8,128)(2,1)S(1)} %collective-permute-done.7.refs_6_), channel_id=1, source_target_pairs={{2,0},{4,2},{6,4},{7,6},{5,7},{3,5},{1,3},{0,1},{10,8},{12,10},{14... | collective-permute-start | bytes 393224 | tf_op jit(solution)/shard_map/ppermute | solution.py:35
  21.0 5.4 %collective-permute-start.9 = (bf16[16,4096]{1,0:T(8,128)(2,1)S(1)}, bf16[16,4096]{1,0:T(8,128)(2,1)S(1)}, u32[]{:S(2)}, u32[]{:S(2)}) collective-permute-start(bf16[16,4096]{1,0:T(8,128)(2,1)S(1)} %collective-permute-done.5.refs_4_), channel_id=1, source_target_pairs={{2,0},{4,2},{6,4},{7,6},{5,7},{3,5},{1,3},{0,1},{10,8},{12,10},{14... | collective-permute-start | bytes 393224 | tf_op jit(solution)/shard_map/ppermute | solution.py:35
  22.2 5.0 %collective-permute-start.10 = (bf16[16,4096]{1,0:T(8,128)(2,1)S(1)}, bf16[16,4096]{1,0:T(8,128)(2,1)S(1)}, u32[]{:S(2)}, u32[]{:S(2)}) collective-permute-start(bf16[16,4096]{1,0:T(8,128)(2,1)S(1)} %collective-permute-done.6.refs_5_), channel_id=1, source_target_pairs={{0,2},{2,4},{4,6},{6,7},{7,5},{5,3},{3,1},{1,0},{8,10},{10,12},{12... | collective-permute-start | bytes 393224 | tf_op jit(solution)/shard_map/ppermute | solution.py:35
  23.9 5.0 %collective-permute-start.12 = (bf16[16,4096]{1,0:T(8,128)(2,1)S(1)}, bf16[16,4096]{1,0:T(8,128)(2,1)S(1)}, u32[]{:S(2)}, u32[]{:S(2)}) collective-permute-start(bf16[16,4096]{1,0:T(8,128)(2,1)S(1)} %collective-permute-done.8.refs_7_), channel_id=1, source_target_pairs={{0,2},{2,4},{4,6},{6,7},{7,5},{5,3},{3,1},{1,0},{8,10},{10,12},{12... | collective-permute-start | bytes 393224 | tf_op jit(solution)/shard_map/ppermute | solution.py:37
  24.4 5.0 %collective-permute-start.13 = (bf16[16,4096]{1,0:T(8,128)(2,1)S(1)}, bf16[16,4096]{1,0:T(8,128)(2,1)S(1)}, u32[]{:S(2)}, u32[]{:S(2)}) collective-permute-start(bf16[16,4096]{1,0:T(8,128)(2,1)S(1)} %collective-permute-done.11.refs_10_), channel_id=1, source_target_pairs={{2,0},{4,2},{6,4},{7,6},{5,7},{3,5},{1,3},{0,1},{10,8},{12,10},{14... | collective-permute-start | bytes 393224 | tf_op jit(solution)/shard_map/ppermute | solution.py:37
  31.6 16.9 %all-to-all-start = ((bf16[8,32,1280]{2,1,0:T(8,128)(2,1)}), bf16[8,32,1280]{2,1,0:T(8,128)(2,1)S(1)}, u32[]{:S(2)}, u32[]{:S(2)}) async-start(bf16[8,32,1280]{2,1,0:T(8,128)(2,1)} %get-tuple-element.24), calls=%async_computation | async-start | bytes 1310720 | tf_op jit(solution)/shard_map/all_to_all | solution.py:216

commit v28 on v27

--- a/solution.py
+++ b/solution.py
@@ -60,11 +60,11 @@
 
 def exchange_order(n):
     ring = ring_of(n)
-    return ring[2:] + ring[:2]
+    return ring[3:] + ring[:3]
 
 
 def exchange_place(i, n):
-    return lax.rem(ring_place(i, n) + n - 2, n)
+    return lax.rem(ring_place(i, n) + n - 3, n)
 
 
 def ring_sources(axis, half):

time: 49.8 us -> 50.4 us (1.012)
  starting transfers between devices: 19.8 us -> 20.8 us
  waiting for transfers between devices: 11.6 us -> 10.9 us
    all_to_all x1, starting transfers between devices: 6.51 us -> 7.54 us  [on_device(): lax.all_to_all(lifts, 'tp', split_axis=0, concat_axis=0, axis_index_group...]
    all_to_all x1, waiting for transfers between devices: 1.82 us -> 1.16 us  [on_device(): lax.all_to_all(lifts, 'tp', split_axis=0, concat_axis=0, axis_index_group...]
where the time goes in v28:
time: 50.4 us; the launch traced here: 49.9 us
  starting transfers between devices  20.8 us (41%)
  waiting for transfers between devices  10.9 us (22%)
  matrix products  8.53 us (17%)
  Pallas kernels  5 us (10%)
  local copies, waits for them, and re-layouts  4.53 us (9%)
    dot_general x1, matrix products, on_device(): jnp.dot(gathered, base_projection_weight, preferred_element_type=jnp.floa...  8.53 us
    ppermute x8, starting transfers between devices, ring_gather(): lax.ppermute(x, axis, way)  7.73 us
    all_to_all x1, starting transfers between devices, on_device(): lax.all_to_all(lifts, 'tp', split_axis=0, concat_axis=0, axis_index_group...  7.54 us
    ppermute x8, waiting for transfers between devices, ring_gather(): lax.ppermute(x, axis, way)  5.78 us
    unnamed x12, local copies, waits for them, and re-layouts  4.53 us
    ppermute x1, starting transfers between devices, ring_gather(): lax.ppermute(block, axis, down)  2.97 us
    pallas_call x1, Pallas kernels, on_device(): pl.pallas_call(functools.partial(lift_kernel, groups), out_shape=[jax.Sha...  2.19 us
    ppermute x1, waiting for transfers between devices, ring_gather(): lax.ppermute(streams[0], axis, up)  1.64 us
  transfers between devices with their start and end apart: 15, of which 11 were waited for; matrix products, arithmetic and copies ran while one was open for 17% of the time, Pallas kernels for 4%

profile of v28, /device:TPU:0, one launch (start us, length us, event | category | flops | bytes accessed | tf_op | source)
XLA Modules:
  0.0 49.9 jit_solution(7728859490850781211)
XLA Ops:
  0.5 3.0 %collective-permute-start.3 = (bf16[16,8192]{1,0:T(8,128)(2,1)}, bf16[16,8192]{1,0:T(8,128)(2,1)S(1)}, u32[]{:S(2)}, u32[]{:S(2)}) collective-permute-start(bf16[16,8192]{1,0:T(8,128)(2,1)} %bitcast.14), channel_id=1, source_target_pairs={{2,0},{4,2},{6,4},{7,6},{5,7},{3,5},{1,3},{0,1},{10,8},{12,10},{14... | collective-permute-start | bytes 786440 | tf_op jit(solution)/shard_map/ppermute | solution.py:30
  3.5 0.7 %copy-done.3 = s32[2,12]{1,0:T(2,128)S(1)} copy-done((s32[2,12]{1,0:T(2,128)S(1)}, s32[2,12]{1,0:T(2,128)}, u32[]{:S(2)}) %copy-start.3) | copy-done | bytes 120
  4.2 0.7 %copy-done.4 = s32[1,12]{1,0:T(1,128)S(1)} copy-done((s32[1,12]{1,0:T(1,128)S(1)}, s32[1,12]{1,0:T(1,128)}, u32[]{:S(2)}) %copy-start.4) | copy-done | bytes 72
  5.5 1.0 %place.1 = (s32[1,128]{1,0:T(1,128)S(1)}, s32[128,1]{1,0:T(8,128)S(1)}) custom-call(s32[2,12]{1,0:T(2,128)S(1)} %copy-done.3, s32[1,12]{1,0:T(1,128)S(1)} %copy-done.4, s32[16]{0:T(128)S(1)} %copy-done.5), custom_call_target="tpu_custom_call" | custom-call | tf_op jit(solution)/shard_map/place/pallas_call | solution.py:183
  6.6 1.3 %copy-done = bf16[1,64,10240]{2,1,0:T(8,128)(2,1)S(1)} copy-done((bf16[1,64,10240]{2,1,0:T(8,128)(2,1)S(1)}, bf16[1,64,10240]{2,1,0:T(8,128)(2,1)}, u32[]{:S(2)}) %copy-start) | copy-done | bytes 1310744
  7.9 1.2 %copy-done.1 = bf16[1,8192,64]{1,2,0:T(8,128)(2,1)S(1)} copy-done((bf16[1,8192,64]{1,2,0:T(8,128)(2,1)S(1)}, bf16[1,8192,64]{1,2,0:T(8,128)(2,1)}, u32[]{:S(2)}) %copy-start.1) | copy-done | bytes 1048600
  9.1 0.7 %stack.1 = (bf16[8192,128]{1,0:T(8,128)(2,1)S(1)}, bf16[128,10240]{1,0:T(8,128)(2,1)S(1)}) custom-call(bf16[64,8192]{1,0:T(8,128)(2,1)S(1)} %bitcast.13, bf16[64,8192]{1,0:T(8,128)(2,1)S(1)} %collective-permute-done.refs_1_, bf16[64,10240]{1,0:T(8,128)(2,1)S(1)} %bitcast.11, bf16[64,10240]{1,0:T(8,128)(2,1)S(1)} %collective-permute-done.1.refs_3_), custom_call_target="tpu_custom_call" | custom-call | tf_op jit(solution)/shard_map/stack/pallas_call | solution.py:172
  10.2 1.4 %collective-permute-done.2.refs_0_.refs_1_ = bf16[16,8192]{1,0:T(8,128)(2,1)S(1)} collective-permute-done((bf16[16,8192]{1,0:T(8,128)(2,1)}, bf16[16,8192]{1,0:T(8,128)(2,1)S(1)}, u32[]{:S(2)}, u32[]{:S(2)}) %collective-permute-start.2) | collective-permute-done | bytes 262176 | tf_op jit(solution)/shard_map/ppermute | solution.py:30
  12.1 1.7 %collective-permute-start.7 = (bf16[16,4096]{1,0:T(8,128)(2,1)S(1)}, bf16[16,4096]{1,0:T(8,128)(2,1)S(1)}, u32[]{:S(2)}, u32[]{:S(2)}) collective-permute-start(bf16[16,4096]{1,0:T(8,128)(2,1)S(1)} %get-tuple-element.22), channel_id=1, source_target_pairs={{2,0},{4,2},{6,4},{7,6},{5,7},{3,5},{1,3},{0,1},{10,8},{12,10},{14... | collective-permute-start | bytes 393224 | tf_op jit(solution)/shard_map/ppermute | solution.py:35
  13.7 1.6 %collective-permute-start.5 = (bf16[16,4096]{1,0:T(8,128)(2,1)S(1)}, bf16[16,4096]{1,0:T(8,128)(2,1)S(1)}, u32[]{:S(2)}, u32[]{:S(2)}) collective-permute-start(bf16[16,4096]{1,0:T(8,128)(2,1)S(1)} %get-tuple-element.20), channel_id=1, source_target_pairs={{2,0},{4,2},{6,4},{7,6},{5,7},{3,5},{1,3},{0,1},{10,8},{12,10},{14... | collective-permute-start | bytes 393224 | tf_op jit(solution)/shard_map/ppermute | solution.py:35
  15.8 1.7 %collective-permute-done.4.refs_3_ = bf16[16,4096]{1,0:T(8,128)(2,1)S(1)} collective-permute-done((bf16[16,4096]{1,0:T(8,128)(2,1)S(1)}, bf16[16,4096]{1,0:T(8,128)(2,1)S(1)}, u32[]{:S(2)}, u32[]{:S(2)}) %collective-permute-start.4) | collective-permute-done | bytes 131104 | tf_op jit(solution)/shard_map/ppermute | solution.py:35
  18.2 1.4 %collective-permute-start.11 = (bf16[16,4096]{1,0:T(8,128)(2,1)S(1)}, bf16[16,4096]{1,0:T(8,128)(2,1)S(1)}, u32[]{:S(2)}, u32[]{:S(2)}) collective-permute-start(bf16[16,4096]{1,0:T(8,128)(2,1)S(1)} %collective-permute-done.7.refs_6_), channel_id=1, source_target_pairs={{2,0},{4,2},{6,4},{7,6},{5,7},{3,5},{1,3},{0,1},{10,8},{12,10},{14... | collective-permute-start | bytes 393224 | tf_op jit(solution)/shard_map/ppermute | solution.py:35
  19.5 1.4 %collective-permute-done.5.refs_4_ = bf16[16,4096]{1,0:T(8,128)(2,1)S(1)} collective-permute-done((bf16[16,4096]{1,0:T(8,128)(2,1)S(1)}, bf16[16,4096]{1,0:T(8,128)(2,1)S(1)}, u32[]{:S(2)}, u32[]{:S(2)}) %collective-permute-start.5) | collective-permute-done | bytes 131104 | tf_op jit(solution)/shard_map/ppermute | solution.py:35
  21.0 1.2 %collective-permute-start.9 = (bf16[16,4096]{1,0:T(8,128)(2,1)S(1)}, bf16[16,4096]{1,0:T(8,128)(2,1)S(1)}, u32[]{:S(2)}, u32[]{:S(2)}) collective-permute-start(bf16[16,4096]{1,0:T(8,128)(2,1)S(1)} %collective-permute-done.5.refs_4_), channel_id=1, source_target_pairs={{2,0},{4,2},{6,4},{7,6},{5,7},{3,5},{1,3},{0,1},{10,8},{12,10},{14... | collective-permute-start | bytes 393224 | tf_op jit(solution)/shard_map/ppermute | solution.py:35
  22.2 0.8 %collective-permute-start.10 = (bf16[16,4096]{1,0:T(8,128)(2,1)S(1)}, bf16[16,4096]{1,0:T(8,128)(2,1)S(1)}, u32[]{:S(2)}, u32[]{:S(2)}) collective-permute-start(bf16[16,4096]{1,0:T(8,128)(2,1)S(1)} %collective-permute-done.6.refs_5_), channel_id=1, source_target_pairs={{0,2},{2,4},{4,6},{6,7},{7,5},{5,3},{3,1},{1,0},{8,10},{10,12},{12... | collective-permute-start | bytes 393224 | tf_op jit(solution)/shard_map/ppermute | solution.py:35
  23.0 0.9 %collective-permute-done.8.refs_7_ = bf16[16,4096]{1,0:T(8,128)(2,1)S(1)} collective-permute-done((bf16[16,4096]{1,0:T(8,128)(2,1)S(1)}, bf16[16,4096]{1,0:T(8,128)(2,1)S(1)}, u32[]{:S(2)}, u32[]{:S(2)}) %collective-permute-start.8) | collective-permute-done | bytes 131104 | tf_op jit(solution)/shard_map/ppermute | solution.py:35
  24.4 1.5 %collective-permute-start.13 = (bf16[16,4096]{1,0:T(8,128)(2,1)S(1)}, bf16[16,4096]{1,0:T(8,128)(2,1)S(1)}, u32[]{:S(2)}, u32[]{:S(2)}) collective-permute-start(bf16[16,4096]{1,0:T(8,128)(2,1)S(1)} %collective-permute-done.11.refs_10_), channel_id=1, source_target_pairs={{2,0},{4,2},{6,4},{7,6},{5,7},{3,5},{1,3},{0,1},{10,8},{12,10},{14... | collective-permute-start | bytes 393224 | tf_op jit(solution)/shard_map/ppermute | solution.py:37
  26.4 0.8 %collective-permute-done.10.refs_9_ = bf16[16,4096]{1,0:T(8,128)(2,1)S(1)} collective-permute-done((bf16[16,4096]{1,0:T(8,128)(2,1)S(1)}, bf16[16,4096]{1,0:T(8,128)(2,1)S(1)}, u32[]{:S(2)}, u32[]{:S(2)}) %collective-permute-start.10) | collective-permute-done | bytes 131104 | tf_op jit(solution)/shard_map/ppermute | solution.py:35
  27.2 1.6 %collective-permute-done.12.refs_11_ = bf16[16,4096]{1,0:T(8,128)(2,1)S(1)} collective-permute-done((bf16[16,4096]{1,0:T(8,128)(2,1)S(1)}, bf16[16,4096]{1,0:T(8,128)(2,1)S(1)}, u32[]{:S(2)}, u32[]{:S(2)}) %collective-permute-start.12) | collective-permute-done | bytes 131104 | tf_op jit(solution)/shard_map/ppermute | solution.py:37
  29.4 2.2 %lift.1 = (bf16[128,8192]{1,0:T(8,128)(2,1)S(1)}, bf16[8,32,1280]{2,1,0:T(8,128)(2,1)}) custom-call(s32[1,128]{1,0:T(1,128)S(1)} %get-tuple-element.16.refs_4_.place_ref, bf16[8192,128]{1,0:T(8,128)(2,1)S(1)} %get-tuple-element.17.refs_2_.down_ref, bf16[128,10240]{1,0:T(8,128)(2,1)S(1)} %get-tuple-element.18.refs_3_.up_ref, bf16[16,8192]{1,0:T(8,128)(2,1)S(1)} %bitcast.16, ...), custom_call_target="tpu_custom_call" | custom-call | flops 352321536 | bytes 4718592 | tf_op jit(solution)/shard_map/lift/pallas_call | solution.py:196
  31.6 7.5 %all-to-all-start = ((bf16[8,32,1280]{2,1,0:T(8,128)(2,1)}), bf16[8,32,1280]{2,1,0:T(8,128)(2,1)S(1)}, u32[]{:S(2)}, u32[]{:S(2)}) async-start(bf16[8,32,1280]{2,1,0:T(8,128)(2,1)} %get-tuple-element.24), calls=%async_computation | async-start | bytes 1310720 | tf_op jit(solution)/shard_map/all_to_all | solution.py:216
  39.2 8.5 %fusion.base_ref = f32[128,1280]{1,0:T(8,128)S(1)} fusion(bf16[128,8192]{1,0:T(8,128)(2,1)S(1)} %get-tuple-element.23, bf16[8192,1280]{1,0:T(8,128)(2,1)} %param.8), kind=kOutput, calls=%fused_computation | convolution fusion | flops 2684354560 | bytes 23724032 | tf_op jit(solution)/shard_map/dot_general | solution.py:220
  47.7 1.2 %all-to-all-done = bf16[8,32,1280]{2,1,0:T(8,128)(2,1)S(1)} async-done(((bf16[8,32,1280]{2,1,0:T(8,128)(2,1)}), bf16[8,32,1280]{2,1,0:T(8,128)(2,1)S(1)}, u32[]{:S(2)}, u32[]{:S(2)}) %all-to-all-start) | async-done | bytes 655392 | tf_op jit(solution)/shard_map/all_to_all | solution.py:216
  48.9 1.0 %add.1 = bf16[128,1280]{1,0:T(8,128)(2,1)} custom-call(s32[128,1]{1,0:T(8,128)S(1)} %get-tuple-element.15.refs_5_.place_ref, f32[128,1280]{1,0:T(8,128)S(1)} %fusion.base_ref, bf16[256,1280]{1,0:T(8,128)(2,1)S(1)} %bitcast.9), custom_call_target="tpu_custom_call" | custom-call | tf_op jit(solution)/shard_map/add/pallas_call | solution.py:221
  (24 shorter events, 4.8 us)
Async XLA Ops:
  0.0 6.6 %collective-permute-start.1 = (bf16[64,10240]{1,0:T(8,128)(2,1)}, bf16[64,10240]{1,0:T(8,128)(2,1)S(1)}, u32[]{:S(2)}, u32[]{:S(2)}) collective-permute-start(bf16[64,10240]{1,0:T(8,128)(2,1)} %bitcast.10), channel_id=1, source_target_pairs={{8,0},{0,8},{9,1},{1,9},{10,2},{2,10},{11,3},{3,11},{12,4},{4,12},... | collective-permute-start | bytes 3932168 | tf_op jit(solution)/shard_map/ppermute | solution.py:16
  0.5 6.1 %collective-permute-start = (bf16[64,8192]{1,0:T(8,128)(2,1)}, bf16[64,8192]{1,0:T(8,128)(2,1)S(1)}, u32[]{:S(2)}, u32[]{:S(2)}) collective-permute-start(bf16[64,8192]{1,0:T(8,128)(2,1)} %bitcast.12), channel_id=1, source_target_pairs={{8,0},{0,8},{9,1},{1,9},{10,2},{2,10},{11,3},{3,11},{12,4},{4,12},... | collective-permute-start | bytes 3145736 | tf_op jit(solution)/shard_map/ppermute | solution.py:16
  0.5 9.7 %collective-permute-start.3 = (bf16[16,8192]{1,0:T(8,128)(2,1)}, bf16[16,8192]{1,0:T(8,128)(2,1)S(1)}, u32[]{:S(2)}, u32[]{:S(2)}) collective-permute-start(bf16[16,8192]{1,0:T(8,128)(2,1)} %bitcast.14), channel_id=1, source_target_pairs={{2,0},{4,2},{6,4},{7,6},{5,7},{3,5},{1,3},{0,1},{10,8},{12,10},{14... | collective-permute-start | bytes 786440 | tf_op jit(solution)/shard_map/ppermute | solution.py:30
  3.5 8.1 %collective-permute-start.2 = (bf16[16,8192]{1,0:T(8,128)(2,1)}, bf16[16,8192]{1,0:T(8,128)(2,1)S(1)}, u32[]{:S(2)}, u32[]{:S(2)}) collective-permute-start(bf16[16,8192]{1,0:T(8,128)(2,1)} %bitcast.15), channel_id=1, source_target_pairs={{0,2},{2,4},{4,6},{6,7},{7,5},{5,3},{3,1},{1,0},{8,10},{10,12},{12... | collective-permute-start | bytes 786440 | tf_op jit(solution)/shard_map/ppermute | solution.py:30
  3.5 0.7 %copy-start.3 = (s32[2,12]{1,0:T(2,128)S(1)}, s32[2,12]{1,0:T(2,128)}, u32[]{:S(2)}) copy-start(s32[2,12]{1,0:T(2,128)} %ids_ref.1) | copy-start | bytes 292
  4.2 0.7 %copy-start.4 = (s32[1,12]{1,0:T(1,128)S(1)}, s32[1,12]{1,0:T(1,128)}, u32[]{:S(2)}) copy-start(s32[1,12]{1,0:T(1,128)} %lengths_ref.1) | copy-start | bytes 148
  4.9 0.7 %copy-start.5 = (s32[16]{0:T(128)S(1)}, s32[16]{0:T(128)}, u32[]{:S(2)}) copy-start(s32[16]{0:T(128)} %slots_ref.1) | copy-start | bytes 196
  6.6 1.3 %copy-start = (bf16[1,64,10240]{2,1,0:T(8,128)(2,1)S(1)}, bf16[1,64,10240]{2,1,0:T(8,128)(2,1)}, u32[]{:S(2)}) copy-start(bf16[1,64,10240]{2,1,0:T(8,128)(2,1)} %param.10) | copy-start | bytes 3932164
  7.9 1.2 %copy-start.1 = (bf16[1,8192,64]{1,2,0:T(8,128)(2,1)S(1)}, bf16[1,8192,64]{1,2,0:T(8,128)(2,1)}, u32[]{:S(2)}) copy-start(bf16[1,8192,64]{1,2,0:T(8,128)(2,1)} %param.9) | copy-start | bytes 3145732
  11.6 17.8 %copy-start.2 = (bf16[1,16,8192]{2,1,0:T(8,128)(2,1)S(1)}, bf16[1,16,8192]{2,1,0:T(8,128)(2,1)}, u32[]{:S(2)}) copy-start(bf16[1,16,8192]{2,1,0:T(8,128)(2,1)} %param.7) | copy-start | bytes 786436
  11.7 5.9 %collective-permute-start.4 = (bf16[16,4096]{1,0:T(8,128)(2,1)S(1)}, bf16[16,4096]{1,0:T(8,128)(2,1)S(1)}, u32[]{:S(2)}, u32[]{:S(2)}) collective-permute-start(bf16[16,4096]{1,0:T(8,128)(2,1)S(1)} %get-tuple-element.19), channel_id=1, source_target_pairs={{0,2},{2,4},{4,6},{6,7},{7,5},{5,3},{3,1},{1,0},{8,10},{10,12},{12... | collective-permute-start | bytes 393224 | tf_op jit(solution)/shard_map/ppermute | solution.py:35
  12.1 6.1 %collective-permute-start.7 = (bf16[16,4096]{1,0:T(8,128)(2,1)S(1)}, bf16[16,4096]{1,0:T(8,128)(2,1)S(1)}, u32[]{:S(2)}, u32[]{:S(2)}) collective-permute-start(bf16[16,4096]{1,0:T(8,128)(2,1)S(1)} %get-tuple-element.22), channel_id=1, source_target_pairs={{2,0},{4,2},{6,4},{7,6},{5,7},{3,5},{1,3},{0,1},{10,8},{12,10},{14... | collective-permute-start | bytes 393224 | tf_op jit(solution)/shard_map/ppermute | solution.py:35
  13.7 7.3 %collective-permute-start.5 = (bf16[16,4096]{1,0:T(8,128)(2,1)S(1)}, bf16[16,4096]{1,0:T(8,128)(2,1)S(1)}, u32[]{:S(2)}, u32[]{:S(2)}) collective-permute-start(bf16[16,4096]{1,0:T(8,128)(2,1)S(1)} %get-tuple-element.20), channel_id=1, source_target_pairs={{2,0},{4,2},{6,4},{7,6},{5,7},{3,5},{1,3},{0,1},{10,8},{12,10},{14... | collective-permute-start | bytes 393224 | tf_op jit(solution)/shard_map/ppermute | solution.py:35
  15.3 6.9 %collective-permute-start.6 = (bf16[16,4096]{1,0:T(8,128)(2,1)S(1)}, bf16[16,4096]{1,0:T(8,128)(2,1)S(1)}, u32[]{:S(2)}, u32[]{:S(2)}) collective-permute-start(bf16[16,4096]{1,0:T(8,128)(2,1)S(1)} %get-tuple-element.21), channel_id=1, source_target_pairs={{0,2},{2,4},{4,6},{6,7},{7,5},{5,3},{3,1},{1,0},{8,10},{10,12},{12... | collective-permute-start | bytes 393224 | tf_op jit(solution)/shard_map/ppermute | solution.py:35
  17.5 6.4 %collective-permute-start.8 = (bf16[16,4096]{1,0:T(8,128)(2,1)S(1)}, bf16[16,4096]{1,0:T(8,128)(2,1)S(1)}, u32[]{:S(2)}, u32[]{:S(2)}) collective-permute-start(bf16[16,4096]{1,0:T(8,128)(2,1)S(1)} %collective-permute-done.4.refs_3_), channel_id=1, source_target_pairs={{0,2},{2,4},{4,6},{6,7},{7,5},{5,3},{3,1},{1,0},{8,10},{10,12},{12... | collective-permute-start | bytes 393224 | tf_op jit(solution)/shard_map/ppermute | solution.py:35
  18.2 6.3 %collective-permute-start.11 = (bf16[16,4096]{1,0:T(8,128)(2,1)S(1)}, bf16[16,4096]{1,0:T(8,128)(2,1)S(1)}, u32[]{:S(2)}, u32[]{:S(2)}) collective-permute-start(bf16[16,4096]{1,0:T(8,128)(2,1)S(1)} %collective-permute-done.7.refs_6_), channel_id=1, source_target_pairs={{2,0},{4,2},{6,4},{7,6},{5,7},{3,5},{1,3},{0,1},{10,8},{12,10},{14... | collective-permute-start | bytes 393224 | tf_op jit(solution)/shard_map/ppermute | solution.py:35
  21.0 5.4 %collective-permute-start.9 = (bf16[16,4096]{1,0:T(8,128)(2,1)S(1)}, bf16[16,4096]{1,0:T(8,128)(2,1)S(1)}, u32[]{:S(2)}, u32[]{:S(2)}) collective-permute-start(bf16[16,4096]{1,0:T(8,128)(2,1)S(1)} %collective-permute-done.5.refs_4_), channel_id=1, source_target_pairs={{2,0},{4,2},{6,4},{7,6},{5,7},{3,5},{1,3},{0,1},{10,8},{12,10},{14... | collective-permute-start | bytes 393224 | tf_op jit(solution)/shard_map/ppermute | solution.py:35
  22.2 5.0 %collective-permute-start.10 = (bf16[16,4096]{1,0:T(8,128)(2,1)S(1)}, bf16[16,4096]{1,0:T(8,128)(2,1)S(1)}, u32[]{:S(2)}, u32[]{:S(2)}) collective-permute-start(bf16[16,4096]{1,0:T(8,128)(2,1)S(1)} %collective-permute-done.6.refs_5_), channel_id=1, source_target_pairs={{0,2},{2,4},{4,6},{6,7},{7,5},{5,3},{3,1},{1,0},{8,10},{10,12},{12... | collective-permute-start | bytes 393224 | tf_op jit(solution)/shard_map/ppermute | solution.py:35
  23.9 5.0 %collective-permute-start.12 = (bf16[16,4096]{1,0:T(8,128)(2,1)S(1)}, bf16[16,4096]{1,0:T(8,128)(2,1)S(1)}, u32[]{:S(2)}, u32[]{:S(2)}) collective-permute-start(bf16[16,4096]{1,0:T(8,128)(2,1)S(1)} %collective-permute-done.8.refs_7_), channel_id=1, source_target_pairs={{0,2},{2,4},{4,6},{6,7},{7,5},{5,3},{3,1},{1,0},{8,10},{10,12},{12... | collective-permute-start | bytes 393224 | tf_op jit(solution)/shard_map/ppermute | solution.py:37
  24.4 5.0 %collective-permute-start.13 = (bf16[16,4096]{1,0:T(8,128)(2,1)S(1)}, bf16[16,4096]{1,0:T(8,128)(2,1)S(1)}, u32[]{:S(2)}, u32[]{:S(2)}) collective-permute-start(bf16[16,4096]{1,0:T(8,128)(2,1)S(1)} %collective-permute-done.11.refs_10_), channel_id=1, source_target_pairs={{2,0},{4,2},{6,4},{7,6},{5,7},{3,5},{1,3},{0,1},{10,8},{12,10},{14... | collective-permute-start | bytes 393224 | tf_op jit(solution)/shard_map/ppermute | solution.py:37
  31.6 17.2 %all-to-all-start = ((bf16[8,32,1280]{2,1,0:T(8,128)(2,1)}), bf16[8,32,1280]{2,1,0:T(8,128)(2,1)S(1)}, u32[]{:S(2)}, u32[]{:S(2)}) async-start(bf16[8,32,1280]{2,1,0:T(8,128)(2,1)} %get-tuple-element.24), calls=%async_computation | async-start | bytes 1310720 | tf_op jit(solution)/shard_map/all_to_all | solution.py:216

commit v29 on v28

--- a/solution.py
+++ b/solution.py
@@ -58,13 +58,14 @@
     return jnp.where(lax.rem(i, 2) == 0, i // 2, n - 1 - i // 2)
 
 
-def exchange_order(n):
+def exchange_groups(groups, n):
     ring = ring_of(n)
-    return ring[3:] + ring[:3]
+    return [[g * n + ring[(2 - p if g % 2 else 2 + p) % n] for p in range(n)] for g in range(groups)]
 
 
 def exchange_place(i, n):
-    return lax.rem(ring_place(i, n) + n - 3, n)
+    ahead = ring_place(i, n) + n - 2
+    return lax.rem(jnp.where(lax.rem(lax.axis_index("grp"), 2) == 0, ahead, 2 * n - ahead), n)
 
 
 def ring_sources(axis, half):
@@ -127,14 +128,15 @@
     rank_panel = lax.broadcasted_iota(jnp.int32, picked.shape, 1) // rank
     picked = jnp.where(row_panel == rank_panel, picked, 0.0).astype(jnp.bfloat16)
     copies = []
-    for part, owner in enumerate(exchange_order(parts)):
-        made_ref[part] = jnp.dot(
+    for owner in range(parts):
+        part = exchange_place(jnp.int32(owner), parts)
+        made_ref[owner] = jnp.dot(
             picked,
             up_ref[:, owner * columns : (owner + 1) * columns],
             preferred_element_type=jnp.float32,
         ).astype(made_ref.dtype)
         copies.append(
-            pltpu.make_async_copy(made_ref.at[part], out_ref.at[part], sems.at[part])
+            pltpu.make_async_copy(made_ref.at[owner], out_ref.at[part], sems.at[owner])
         )
         copies[-1].start()
     for copy in copies:
@@ -214,7 +216,12 @@
         name="lift",
     )(row, down, up, *pieces)
     lifts = lax.all_to_all(
-        lifts, "tp", split_axis=0, concat_axis=0, axis_index_groups=[exchange_order(tp)], tiled=True
+        lifts,
+        ("grp", "tp"),
+        split_axis=0,
+        concat_axis=0,
+        axis_index_groups=exchange_groups(groups, tp),
+        tiled=True,
     )
 
     base = jnp.dot(gathered, base_projection_weight, preferred_element_type=jnp.float32)

time: 50.4 us -> 49.8 us (0.988)
  starting transfers between devices: 20.8 us -> 19.8 us
  waiting for transfers between devices: 10.9 us -> 11.6 us
    all_to_all x1, starting transfers between devices: 7.54 us -> 6.48 us  [on_device(): lax.all_to_all(lifts, ('grp', 'tp'), split_axis=0, concat_axis=0, axis_in...]
    all_to_all x1, waiting for transfers between devices: 1.16 us -> 1.88 us  [on_device(): lax.all_to_all(lifts, ('grp', 'tp'), split_axis=0, concat_axis=0, axis_in...]
where the time goes in v29:
time: 49.8 us; the launch traced here: 49.6 us
  starting transfers between devices  19.8 us (40%)
  waiting for transfers between devices  11.6 us (23%)
  matrix products  8.52 us (17%)
  Pallas kernels  5.02 us (10%)
  local copies, waits for them, and re-layouts  4.53 us (9%)
    dot_general x1, matrix products, on_device(): jnp.dot(gathered, base_projection_weight, preferred_element_type=jnp.floa...  8.52 us
    ppermute x8, starting transfers between devices, ring_gather(): lax.ppermute(x, axis, way)  7.73 us
    all_to_all x1, starting transfers between devices, on_device(): lax.all_to_all(lifts, ('grp', 'tp'), split_axis=0, concat_axis=0, axis_in...  6.48 us
    ppermute x8, waiting for transfers between devices, ring_gather(): lax.ppermute(x, axis, way)  5.79 us
    unnamed x12, local copies, waits for them, and re-layouts  4.53 us
    ppermute x1, starting transfers between devices, ring_gather(): lax.ppermute(block, axis, down)  2.97 us
    pallas_call x1, Pallas kernels, on_device(): pl.pallas_call(functools.partial(lift_kernel, groups), out_shape=[jax.Sha...  2.21 us
    all_to_all x1, waiting for transfers between devices, on_device(): lax.all_to_all(lifts, ('grp', 'tp'), split_axis=0, concat_axis=0, axis_in...  1.88 us
  transfers between devices with their start and end apart: 15, of which 11 were waited for; matrix products, arithmetic and copies ran while one was open for 17% of the time, Pallas kernels for 4%

profile of v29, /device:TPU:0, one launch (start us, length us, event | category | flops | bytes accessed | tf_op | source)
XLA Modules:
  0.0 49.6 jit_solution(6144059745458953181)
XLA Ops:
  0.5 3.0 %collective-permute-start.3 = (bf16[16,8192]{1,0:T(8,128)(2,1)}, bf16[16,8192]{1,0:T(8,128)(2,1)S(1)}, u32[]{:S(2)}, u32[]{:S(2)}) collective-permute-start(bf16[16,8192]{1,0:T(8,128)(2,1)} %bitcast.14), channel_id=1, source_target_pairs={{2,0},{4,2},{6,4},{7,6},{5,7},{3,5},{1,3},{0,1},{10,8},{12,10},{14... | collective-permute-start | bytes 786440 | tf_op jit(solution)/shard_map/ppermute | solution.py:30
  3.5 0.7 %copy-done.3 = s32[2,12]{1,0:T(2,128)S(1)} copy-done((s32[2,12]{1,0:T(2,128)S(1)}, s32[2,12]{1,0:T(2,128)}, u32[]{:S(2)}) %copy-start.3) | copy-done | bytes 120
  4.2 0.7 %copy-done.4 = s32[1,12]{1,0:T(1,128)S(1)} copy-done((s32[1,12]{1,0:T(1,128)S(1)}, s32[1,12]{1,0:T(1,128)}, u32[]{:S(2)}) %copy-start.4) | copy-done | bytes 72
  5.5 1.0 %place.1 = (s32[1,128]{1,0:T(1,128)S(1)}, s32[128,1]{1,0:T(8,128)S(1)}) custom-call(s32[2,12]{1,0:T(2,128)S(1)} %copy-done.3, s32[1,12]{1,0:T(1,128)S(1)} %copy-done.4, s32[16]{0:T(128)S(1)} %copy-done.5), custom_call_target="tpu_custom_call" | custom-call | tf_op jit(solution)/shard_map/place/pallas_call | solution.py:185
  6.6 1.3 %copy-done = bf16[1,64,10240]{2,1,0:T(8,128)(2,1)S(1)} copy-done((bf16[1,64,10240]{2,1,0:T(8,128)(2,1)S(1)}, bf16[1,64,10240]{2,1,0:T(8,128)(2,1)}, u32[]{:S(2)}) %copy-start) | copy-done | bytes 1310744
  7.9 1.2 %copy-done.1 = bf16[1,8192,64]{1,2,0:T(8,128)(2,1)S(1)} copy-done((bf16[1,8192,64]{1,2,0:T(8,128)(2,1)S(1)}, bf16[1,8192,64]{1,2,0:T(8,128)(2,1)}, u32[]{:S(2)}) %copy-start.1) | copy-done | bytes 1048600
  9.1 0.7 %stack.1 = (bf16[8192,128]{1,0:T(8,128)(2,1)S(1)}, bf16[128,10240]{1,0:T(8,128)(2,1)S(1)}) custom-call(bf16[64,8192]{1,0:T(8,128)(2,1)S(1)} %bitcast.13, bf16[64,8192]{1,0:T(8,128)(2,1)S(1)} %collective-permute-done.refs_1_, bf16[64,10240]{1,0:T(8,128)(2,1)S(1)} %bitcast.11, bf16[64,10240]{1,0:T(8,128)(2,1)S(1)} %collective-permute-done.1.refs_3_), custom_call_target="tpu_custom_call" | custom-call | tf_op jit(solution)/shard_map/stack/pallas_call | solution.py:174
  10.2 1.4 %collective-permute-done.2.refs_0_.refs_1_ = bf16[16,8192]{1,0:T(8,128)(2,1)S(1)} collective-permute-done((bf16[16,8192]{1,0:T(8,128)(2,1)}, bf16[16,8192]{1,0:T(8,128)(2,1)S(1)}, u32[]{:S(2)}, u32[]{:S(2)}) %collective-permute-start.2) | collective-permute-done | bytes 262176 | tf_op jit(solution)/shard_map/ppermute | solution.py:30
  12.1 1.7 %collective-permute-start.7 = (bf16[16,4096]{1,0:T(8,128)(2,1)S(1)}, bf16[16,4096]{1,0:T(8,128)(2,1)S(1)}, u32[]{:S(2)}, u32[]{:S(2)}) collective-permute-start(bf16[16,4096]{1,0:T(8,128)(2,1)S(1)} %get-tuple-element.22), channel_id=1, source_target_pairs={{2,0},{4,2},{6,4},{7,6},{5,7},{3,5},{1,3},{0,1},{10,8},{12,10},{14... | collective-permute-start | bytes 393224 | tf_op jit(solution)/shard_map/ppermute | solution.py:35
  13.7 1.6 %collective-permute-start.5 = (bf16[16,4096]{1,0:T(8,128)(2,1)S(1)}, bf16[16,4096]{1,0:T(8,128)(2,1)S(1)}, u32[]{:S(2)}, u32[]{:S(2)}) collective-permute-start(bf16[16,4096]{1,0:T(8,128)(2,1)S(1)} %get-tuple-element.20), channel_id=1, source_target_pairs={{2,0},{4,2},{6,4},{7,6},{5,7},{3,5},{1,3},{0,1},{10,8},{12,10},{14... | collective-permute-start | bytes 393224 | tf_op jit(solution)/shard_map/ppermute | solution.py:35
  15.8 1.7 %collective-permute-done.4.refs_3_ = bf16[16,4096]{1,0:T(8,128)(2,1)S(1)} collective-permute-done((bf16[16,4096]{1,0:T(8,128)(2,1)S(1)}, bf16[16,4096]{1,0:T(8,128)(2,1)S(1)}, u32[]{:S(2)}, u32[]{:S(2)}) %collective-permute-start.4) | collective-permute-done | bytes 131104 | tf_op jit(solution)/shard_map/ppermute | solution.py:35
  18.2 1.4 %collective-permute-start.11 = (bf16[16,4096]{1,0:T(8,128)(2,1)S(1)}, bf16[16,4096]{1,0:T(8,128)(2,1)S(1)}, u32[]{:S(2)}, u32[]{:S(2)}) collective-permute-start(bf16[16,4096]{1,0:T(8,128)(2,1)S(1)} %collective-permute-done.7.refs_6_), channel_id=1, source_target_pairs={{2,0},{4,2},{6,4},{7,6},{5,7},{3,5},{1,3},{0,1},{10,8},{12,10},{14... | collective-permute-start | bytes 393224 | tf_op jit(solution)/shard_map/ppermute | solution.py:35
  19.5 1.5 %collective-permute-done.5.refs_4_ = bf16[16,4096]{1,0:T(8,128)(2,1)S(1)} collective-permute-done((bf16[16,4096]{1,0:T(8,128)(2,1)S(1)}, bf16[16,4096]{1,0:T(8,128)(2,1)S(1)}, u32[]{:S(2)}, u32[]{:S(2)}) %collective-permute-start.5) | collective-permute-done | bytes 131104 | tf_op jit(solution)/shard_map/ppermute | solution.py:35
  21.0 1.2 %collective-permute-start.9 = (bf16[16,4096]{1,0:T(8,128)(2,1)S(1)}, bf16[16,4096]{1,0:T(8,128)(2,1)S(1)}, u32[]{:S(2)}, u32[]{:S(2)}) collective-permute-start(bf16[16,4096]{1,0:T(8,128)(2,1)S(1)} %collective-permute-done.5.refs_4_), channel_id=1, source_target_pairs={{2,0},{4,2},{6,4},{7,6},{5,7},{3,5},{1,3},{0,1},{10,8},{12,10},{14... | collective-permute-start | bytes 393224 | tf_op jit(solution)/shard_map/ppermute | solution.py:35
  22.2 0.8 %collective-permute-start.10 = (bf16[16,4096]{1,0:T(8,128)(2,1)S(1)}, bf16[16,4096]{1,0:T(8,128)(2,1)S(1)}, u32[]{:S(2)}, u32[]{:S(2)}) collective-permute-start(bf16[16,4096]{1,0:T(8,128)(2,1)S(1)} %collective-permute-done.6.refs_5_), channel_id=1, source_target_pairs={{0,2},{2,4},{4,6},{6,7},{7,5},{5,3},{3,1},{1,0},{8,10},{10,12},{12... | collective-permute-start | bytes 393224 | tf_op jit(solution)/shard_map/ppermute | solution.py:35
  23.0 0.9 %collective-permute-done.8.refs_7_ = bf16[16,4096]{1,0:T(8,128)(2,1)S(1)} collective-permute-done((bf16[16,4096]{1,0:T(8,128)(2,1)S(1)}, bf16[16,4096]{1,0:T(8,128)(2,1)S(1)}, u32[]{:S(2)}, u32[]{:S(2)}) %collective-permute-start.8) | collective-permute-done | bytes 131104 | tf_op jit(solution)/shard_map/ppermute | solution.py:35
  24.5 1.5 %collective-permute-start.13 = (bf16[16,4096]{1,0:T(8,128)(2,1)S(1)}, bf16[16,4096]{1,0:T(8,128)(2,1)S(1)}, u32[]{:S(2)}, u32[]{:S(2)}) collective-permute-start(bf16[16,4096]{1,0:T(8,128)(2,1)S(1)} %collective-permute-done.11.refs_10_), channel_id=1, source_target_pairs={{2,0},{4,2},{6,4},{7,6},{5,7},{3,5},{1,3},{0,1},{10,8},{12,10},{14... | collective-permute-start | bytes 393224 | tf_op jit(solution)/shard_map/ppermute | solution.py:37
  26.4 0.8 %collective-permute-done.10.refs_9_ = bf16[16,4096]{1,0:T(8,128)(2,1)S(1)} collective-permute-done((bf16[16,4096]{1,0:T(8,128)(2,1)S(1)}, bf16[16,4096]{1,0:T(8,128)(2,1)S(1)}, u32[]{:S(2)}, u32[]{:S(2)}) %collective-permute-start.10) | collective-permute-done | bytes 131104 | tf_op jit(solution)/shard_map/ppermute | solution.py:35
  27.2 1.6 %collective-permute-done.12.refs_11_ = bf16[16,4096]{1,0:T(8,128)(2,1)S(1)} collective-permute-done((bf16[16,4096]{1,0:T(8,128)(2,1)S(1)}, bf16[16,4096]{1,0:T(8,128)(2,1)S(1)}, u32[]{:S(2)}, u32[]{:S(2)}) %collective-permute-start.12) | collective-permute-done | bytes 131104 | tf_op jit(solution)/shard_map/ppermute | solution.py:37
  29.4 2.2 %lift.1 = (bf16[128,8192]{1,0:T(8,128)(2,1)S(1)}, bf16[8,32,1280]{2,1,0:T(8,128)(2,1)}) custom-call(s32[1,128]{1,0:T(1,128)S(1)} %get-tuple-element.16.refs_4_.place_ref, bf16[8192,128]{1,0:T(8,128)(2,1)S(1)} %get-tuple-element.17.refs_2_.down_ref, bf16[128,10240]{1,0:T(8,128)(2,1)S(1)} %get-tuple-element.18.refs_3_.up_ref, bf16[16,8192]{1,0:T(8,128)(2,1)S(1)} %bitcast.16, ...), custom_call_target="tpu_custom_call" | custom-call | flops 352321536 | bytes 4718592 | tf_op jit(solution)/shard_map/lift/pallas_call | solution.py:198
  31.6 6.5 %all-to-all-start = ((bf16[8,32,1280]{2,1,0:T(8,128)(2,1)}), bf16[8,32,1280]{2,1,0:T(8,128)(2,1)S(1)}, u32[]{:S(2)}, u32[]{:S(2)}) async-start(bf16[8,32,1280]{2,1,0:T(8,128)(2,1)} %get-tuple-element.24), calls=%async_computation | async-start | bytes 1310720 | tf_op jit(solution)/shard_map/all_to_all | solution.py:218
  38.1 8.5 %fusion.base_ref = f32[128,1280]{1,0:T(8,128)S(1)} fusion(bf16[128,8192]{1,0:T(8,128)(2,1)S(1)} %get-tuple-element.23, bf16[8192,1280]{1,0:T(8,128)(2,1)} %param.8), kind=kOutput, calls=%fused_computation | convolution fusion | flops 2684354560 | bytes 23724032 | tf_op jit(solution)/shard_map/dot_general | solution.py:227
  46.7 1.9 %all-to-all-done = bf16[8,32,1280]{2,1,0:T(8,128)(2,1)S(1)} async-done(((bf16[8,32,1280]{2,1,0:T(8,128)(2,1)}), bf16[8,32,1280]{2,1,0:T(8,128)(2,1)S(1)}, u32[]{:S(2)}, u32[]{:S(2)}) %all-to-all-start) | async-done | bytes 655392 | tf_op jit(solution)/shard_map/all_to_all | solution.py:218
  48.5 1.0 %add.1 = bf16[128,1280]{1,0:T(8,128)(2,1)} custom-call(s32[128,1]{1,0:T(8,128)S(1)} %get-tuple-element.15.refs_5_.place_ref, f32[128,1280]{1,0:T(8,128)S(1)} %fusion.base_ref, bf16[256,1280]{1,0:T(8,128)(2,1)S(1)} %bitcast.9), custom_call_target="tpu_custom_call" | custom-call | tf_op jit(solution)/shard_map/add/pallas_call | solution.py:228
  (24 shorter events, 4.8 us)
Async XLA Ops:
  0.0 6.6 %collective-permute-start.1 = (bf16[64,10240]{1,0:T(8,128)(2,1)}, bf16[64,10240]{1,0:T(8,128)(2,1)S(1)}, u32[]{:S(2)}, u32[]{:S(2)}) collective-permute-start(bf16[64,10240]{1,0:T(8,128)(2,1)} %bitcast.10), channel_id=1, source_target_pairs={{8,0},{0,8},{9,1},{1,9},{10,2},{2,10},{11,3},{3,11},{12,4},{4,12},... | collective-permute-start | bytes 3932168 | tf_op jit(solution)/shard_map/ppermute | solution.py:16
  0.5 6.1 %collective-permute-start = (bf16[64,8192]{1,0:T(8,128)(2,1)}, bf16[64,8192]{1,0:T(8,128)(2,1)S(1)}, u32[]{:S(2)}, u32[]{:S(2)}) collective-permute-start(bf16[64,8192]{1,0:T(8,128)(2,1)} %bitcast.12), channel_id=1, source_target_pairs={{8,0},{0,8},{9,1},{1,9},{10,2},{2,10},{11,3},{3,11},{12,4},{4,12},... | collective-permute-start | bytes 3145736 | tf_op jit(solution)/shard_map/ppermute | solution.py:16
  0.5 9.7 %collective-permute-start.3 = (bf16[16,8192]{1,0:T(8,128)(2,1)}, bf16[16,8192]{1,0:T(8,128)(2,1)S(1)}, u32[]{:S(2)}, u32[]{:S(2)}) collective-permute-start(bf16[16,8192]{1,0:T(8,128)(2,1)} %bitcast.14), channel_id=1, source_target_pairs={{2,0},{4,2},{6,4},{7,6},{5,7},{3,5},{1,3},{0,1},{10,8},{12,10},{14... | collective-permute-start | bytes 786440 | tf_op jit(solution)/shard_map/ppermute | solution.py:30
  3.5 8.1 %collective-permute-start.2 = (bf16[16,8192]{1,0:T(8,128)(2,1)}, bf16[16,8192]{1,0:T(8,128)(2,1)S(1)}, u32[]{:S(2)}, u32[]{:S(2)}) collective-permute-start(bf16[16,8192]{1,0:T(8,128)(2,1)} %bitcast.15), channel_id=1, source_target_pairs={{0,2},{2,4},{4,6},{6,7},{7,5},{5,3},{3,1},{1,0},{8,10},{10,12},{12... | collective-permute-start | bytes 786440 | tf_op jit(solution)/shard_map/ppermute | solution.py:30
  3.5 0.7 %copy-start.3 = (s32[2,12]{1,0:T(2,128)S(1)}, s32[2,12]{1,0:T(2,128)}, u32[]{:S(2)}) copy-start(s32[2,12]{1,0:T(2,128)} %ids_ref.1) | copy-start | bytes 292
  4.2 0.7 %copy-start.4 = (s32[1,12]{1,0:T(1,128)S(1)}, s32[1,12]{1,0:T(1,128)}, u32[]{:S(2)}) copy-start(s32[1,12]{1,0:T(1,128)} %lengths_ref.1) | copy-start | bytes 148
  4.9 0.7 %copy-start.5 = (s32[16]{0:T(128)S(1)}, s32[16]{0:T(128)}, u32[]{:S(2)}) copy-start(s32[16]{0:T(128)} %slots_ref.1) | copy-start | bytes 196
  6.6 1.3 %copy-start = (bf16[1,64,10240]{2,1,0:T(8,128)(2,1)S(1)}, bf16[1,64,10240]{2,1,0:T(8,128)(2,1)}, u32[]{:S(2)}) copy-start(bf16[1,64,10240]{2,1,0:T(8,128)(2,1)} %param.10) | copy-start | bytes 3932164
  7.9 1.2 %copy-start.1 = (bf16[1,8192,64]{1,2,0:T(8,128)(2,1)S(1)}, bf16[1,8192,64]{1,2,0:T(8,128)(2,1)}, u32[]{:S(2)}) copy-start(bf16[1,8192,64]{1,2,0:T(8,128)(2,1)} %param.9) | copy-start | bytes 3145732
  11.6 17.8 %copy-start.2 = (bf16[1,16,8192]{2,1,0:T(8,128)(2,1)S(1)}, bf16[1,16,8192]{2,1,0:T(8,128)(2,1)}, u32[]{:S(2)}) copy-start(bf16[1,16,8192]{2,1,0:T(8,128)(2,1)} %param.7) | copy-start | bytes 786436
  11.7 5.9 %collective-permute-start.4 = (bf16[16,4096]{1,0:T(8,128)(2,1)S(1)}, bf16[16,4096]{1,0:T(8,128)(2,1)S(1)}, u32[]{:S(2)}, u32[]{:S(2)}) collective-permute-start(bf16[16,4096]{1,0:T(8,128)(2,1)S(1)} %get-tuple-element.19), channel_id=1, source_target_pairs={{0,2},{2,4},{4,6},{6,7},{7,5},{5,3},{3,1},{1,0},{8,10},{10,12},{12... | collective-permute-start | bytes 393224 | tf_op jit(solution)/shard_map/ppermute | solution.py:35
  12.1 6.1 %collective-permute-start.7 = (bf16[16,4096]{1,0:T(8,128)(2,1)S(1)}, bf16[16,4096]{1,0:T(8,128)(2,1)S(1)}, u32[]{:S(2)}, u32[]{:S(2)}) collective-permute-start(bf16[16,4096]{1,0:T(8,128)(2,1)S(1)} %get-tuple-element.22), channel_id=1, source_target_pairs={{2,0},{4,2},{6,4},{7,6},{5,7},{3,5},{1,3},{0,1},{10,8},{12,10},{14... | collective-permute-start | bytes 393224 | tf_op jit(solution)/shard_map/ppermute | solution.py:35
  13.7 7.3 %collective-permute-start.5 = (bf16[16,4096]{1,0:T(8,128)(2,1)S(1)}, bf16[16,4096]{1,0:T(8,128)(2,1)S(1)}, u32[]{:S(2)}, u32[]{:S(2)}) collective-permute-start(bf16[16,4096]{1,0:T(8,128)(2,1)S(1)} %get-tuple-element.20), channel_id=1, source_target_pairs={{2,0},{4,2},{6,4},{7,6},{5,7},{3,5},{1,3},{0,1},{10,8},{12,10},{14... | collective-permute-start | bytes 393224 | tf_op jit(solution)/shard_map/ppermute | solution.py:35
  15.3 6.9 %collective-permute-start.6 = (bf16[16,4096]{1,0:T(8,128)(2,1)S(1)}, bf16[16,4096]{1,0:T(8,128)(2,1)S(1)}, u32[]{:S(2)}, u32[]{:S(2)}) collective-permute-start(bf16[16,4096]{1,0:T(8,128)(2,1)S(1)} %get-tuple-element.21), channel_id=1, source_target_pairs={{0,2},{2,4},{4,6},{6,7},{7,5},{5,3},{3,1},{1,0},{8,10},{10,12},{12... | collective-permute-start | bytes 393224 | tf_op jit(solution)/shard_map/ppermute | solution.py:35
  17.5 6.4 %collective-permute-start.8 = (bf16[16,4096]{1,0:T(8,128)(2,1)S(1)}, bf16[16,4096]{1,0:T(8,128)(2,1)S(1)}, u32[]{:S(2)}, u32[]{:S(2)}) collective-permute-start(bf16[16,4096]{1,0:T(8,128)(2,1)S(1)} %collective-permute-done.4.refs_3_), channel_id=1, source_target_pairs={{0,2},{2,4},{4,6},{6,7},{7,5},{5,3},{3,1},{1,0},{8,10},{10,12},{12... | collective-permute-start | bytes 393224 | tf_op jit(solution)/shard_map/ppermute | solution.py:35
  18.2 6.3 %collective-permute-start.11 = (bf16[16,4096]{1,0:T(8,128)(2,1)S(1)}, bf16[16,4096]{1,0:T(8,128)(2,1)S(1)}, u32[]{:S(2)}, u32[]{:S(2)}) collective-permute-start(bf16[16,4096]{1,0:T(8,128)(2,1)S(1)} %collective-permute-done.7.refs_6_), channel_id=1, source_target_pairs={{2,0},{4,2},{6,4},{7,6},{5,7},{3,5},{1,3},{0,1},{10,8},{12,10},{14... | collective-permute-start | bytes 393224 | tf_op jit(solution)/shard_map/ppermute | solution.py:35
  21.0 5.4 %collective-permute-start.9 = (bf16[16,4096]{1,0:T(8,128)(2,1)S(1)}, bf16[16,4096]{1,0:T(8,128)(2,1)S(1)}, u32[]{:S(2)}, u32[]{:S(2)}) collective-permute-start(bf16[16,4096]{1,0:T(8,128)(2,1)S(1)} %collective-permute-done.5.refs_4_), channel_id=1, source_target_pairs={{2,0},{4,2},{6,4},{7,6},{5,7},{3,5},{1,3},{0,1},{10,8},{12,10},{14... | collective-permute-start | bytes 393224 | tf_op jit(solution)/shard_map/ppermute | solution.py:35
  22.2 5.0 %collective-permute-start.10 = (bf16[16,4096]{1,0:T(8,128)(2,1)S(1)}, bf16[16,4096]{1,0:T(8,128)(2,1)S(1)}, u32[]{:S(2)}, u32[]{:S(2)}) collective-permute-start(bf16[16,4096]{1,0:T(8,128)(2,1)S(1)} %collective-permute-done.6.refs_5_), channel_id=1, source_target_pairs={{0,2},{2,4},{4,6},{6,7},{7,5},{5,3},{3,1},{1,0},{8,10},{10,12},{12... | collective-permute-start | bytes 393224 | tf_op jit(solution)/shard_map/ppermute | solution.py:35
  23.9 5.0 %collective-permute-start.12 = (bf16[16,4096]{1,0:T(8,128)(2,1)S(1)}, bf16[16,4096]{1,0:T(8,128)(2,1)S(1)}, u32[]{:S(2)}, u32[]{:S(2)}) collective-permute-start(bf16[16,4096]{1,0:T(8,128)(2,1)S(1)} %collective-permute-done.8.refs_7_), channel_id=1, source_target_pairs={{0,2},{2,4},{4,6},{6,7},{7,5},{5,3},{3,1},{1,0},{8,10},{10,12},{12... | collective-permute-start | bytes 393224 | tf_op jit(solution)/shard_map/ppermute | solution.py:37
  24.5 5.0 %collective-permute-start.13 = (bf16[16,4096]{1,0:T(8,128)(2,1)S(1)}, bf16[16,4096]{1,0:T(8,128)(2,1)S(1)}, u32[]{:S(2)}, u32[]{:S(2)}) collective-permute-start(bf16[16,4096]{1,0:T(8,128)(2,1)S(1)} %collective-permute-done.11.refs_10_), channel_id=1, source_target_pairs={{2,0},{4,2},{6,4},{7,6},{5,7},{3,5},{1,3},{0,1},{10,8},{12,10},{14... | collective-permute-start | bytes 393224 | tf_op jit(solution)/shard_map/ppermute | solution.py:37
  31.6 16.9 %all-to-all-start = ((bf16[8,32,1280]{2,1,0:T(8,128)(2,1)}), bf16[8,32,1280]{2,1,0:T(8,128)(2,1)S(1)}, u32[]{:S(2)}, u32[]{:S(2)}) async-start(bf16[8,32,1280]{2,1,0:T(8,128)(2,1)} %get-tuple-element.24), calls=%async_computation | async-start | bytes 1310720 | tf_op jit(solution)/shard_map/all_to_all | solution.py:218
